TPU v7x, 32 devices: a whole 2x2x4 slice. The times are simulated.
32 devices in a mesh: group: 2 (over y), rows: 4 (over z), layer: 4 (over x, core).
Axes of the slice: x: 2, y: 2, z: 4, core: 2. Of those that a mesh axis runs over, the one named last changes fastest.
Arguments:
- train_grads: bfloat16 [1024, 8192], P(('group', 'rows'), 'layer'), parts along dimension 0, may hold values from -0.0625 to 0.0625
- query_grads: bfloat16 [4096, 8192], P(('group', 'rows'), 'layer'), parts along dimension 0, may hold values from -6 to 6
- eigenbases: bfloat16 [16, 512, 512], P('layer'), may hold values from -0.25 to 0.25
- eigenvalues: float32 [16, 512], P('layer'), may hold values from 0.05 to 5
- layer_offsets: int32 [16], P('layer'), may hold values from 0 to 7680, as said below
- query_doc_ids: int32 [4096], P(('group', 'rows')), parts along dimension 0, may hold values from 0 to 511
Outputs:
- scores: float32 [4, 512, 1024], P(None, 'layer', ('group', 'rows')), parts along dimension 2
There are 2 independent parts, one for each index of `group`. A program takes and returns all parts, laid end to end along the dimension named above; an argument that names none is the same for every part. Nothing has to cross between parts.
Inputs may be any that keep to these rules, and one draw needn't show every extreme that they name: `layer_offsets`: the layers l with equal l // 4 take the 4 column blocks of width 512 starting at 512 * 4 * (l // 4), in some order.
All inputs are finite; a program needn't handle non-finite values.
Results may differ from a plain program's by a relative error of at most 0.0037.
Values may be sent and summed in bfloat16 or wider, within the bound.
No kernel may reach another device: no remote copies, remote signals or barrier semaphores. Data moves between devices by JAX's collectives and lax.ppermute only.
A program may use at most 64 MiB of HBM per device.

v0:
```python
import jax
import jax.numpy as jnp
from jax import lax
from jax.sharding import PartitionSpec as P

LDIM = 512
LAY_DEV = 4
STEPS = 4


DAMPING = 0.05


def from_behind(value, axis, steps):
    count = lax.axis_size(axis)
    pairs = [(source, (source + steps) % count) for source in range(count)]
    return lax.ppermute(value, axis, pairs)


def precondition(block, basis, values):
    projected = jnp.dot(block, basis, preferred_element_type=jnp.float32)
    scaled = (projected / (values + DAMPING)).astype(jnp.bfloat16)
    return jnp.dot(scaled, basis.T, preferred_element_type=jnp.float32).astype(jnp.bfloat16)


def contract(queries, documents):
    return lax.dot_general(
        queries, documents, (((1,), (1,)), ((), ())), preferred_element_type=jnp.float32
    )


def masked(tile, query_ids, doc_ids):
    return jnp.where(query_ids[:, None] == doc_ids[None, :], jnp.zeros_like(tile), tile)


def layer_tiles(pairs, share_rows):
    tile_list = []
    for queries, documents in pairs:

        def partial_value(first_row, row_count, queries=queries, documents=documents):
            return contract(queries, documents)

        tile_list.append(
            lax.psum_scatter(
                partial_value(jnp.int32(0), lax.axis_size("layer") * share_rows),
                "layer",
                scatter_dimension=0,
                tiled=True,
            )
        )
    return tile_list


def local(train_grads, query_grads, eigenbases, eigenvalues, layer_offsets, query_doc_ids):
    row_index = lax.axis_index("rows")
    layer_index = lax.axis_index("layer")
    share_rows = query_grads.shape[0] // lax.axis_size("layer")
    doc_rows = train_grads.shape[0]
    base_column = layer_index * (LAY_DEV * LDIM)
    ordered = jnp.concatenate(
        [
            lax.dynamic_slice_in_dim(train_grads, layer_offsets[layer] - base_column, LDIM, 1)
            for layer in range(LAY_DEV)
        ],
        axis=1,
    )
    conditioned = jnp.concatenate(
        [
            precondition(
                query_grads[:, layer * LDIM : (layer + 1) * LDIM],
                eigenbases[layer],
                eigenvalues[layer],
            )
            for layer in range(LAY_DEV)
        ],
        axis=1,
    )
    positions = jnp.arange(doc_rows, dtype=jnp.int32)
    result = []
    current = (conditioned, query_doc_ids)
    pairs = []
    id_list = []
    for step in range(STEPS):
        if step > 0:
            current = from_behind((current[0], current[1]), "rows", 1)
        pairs.append((current[0], ordered))
        id_list.append(current[1])
    doc_ids = row_index * doc_rows + positions
    tile_list = layer_tiles(pairs, share_rows)
    for step in range(STEPS):
        query_ids = lax.dynamic_slice_in_dim(id_list[step], layer_index * share_rows, share_rows, 0)
        result.append(masked(tile_list[step], query_ids, doc_ids))
    return jnp.stack(result, axis=0)


def solution(mesh):
    in_specs = (
        P(("group", "rows"), "layer"),
        P(("group", "rows"), "layer"),
        P("layer", None, None),
        P("layer", None),
        P("layer"),
        P(("group", "rows")),
    )
    out_specs = P(None, "layer", ("group", "rows"))
    return jax.shard_map(local, mesh=mesh, in_specs=in_specs, out_specs=out_specs, check_vma=False)
```

profile of v0, /device:TPU:0, one launch (start us, length us, event | category | flops | bytes accessed | tf_op | source)
XLA Modules:
  0.0 223.4 jit_solution(17923631746103274185)
XLA Ops:
  6.5 0.0 reduce-scatter.5.cloned.1.call-start
  6.5 0.9 slice_add_fusion.3
  7.4 2.2 %convolution_convert_fusion.2 = bf16[512,512]{0,1:T(8,128)(2,1)S(1)} fusion(f32[512]{0:T(512)S(1)} %bitcast.39, bf16[4,512,512]{2,1,0:T(8,128)(2,1)} %param.8, bf16[512,2048]{1,0:T(8,128)(2,1)} %param.7), kind=kOutput, calls=%fused_computation.7 | convolution fusion | flops 537657344 | bytes 2099200 | tf_op jit(solution)/shard_map/dot_general | solution.py:23
  9.6 3.0 %convolution_convert_fusion.3 = bf16[512,512]{0,1:T(8,128)(2,1)} fusion(f32[512]{0:T(512)S(1)} %bitcast.38, bf16[4,512,512]{2,1,0:T(8,128)(2,1)} %param.8, bf16[512,2048]{1,0:T(8,128)(2,1)} %param.7), kind=kOutput, calls=%fused_computation.8 | convolution fusion | flops 537657344 | bytes 2099200 | tf_op jit(solution)/shard_map/dot_general | solution.py:23
  12.7 3.0 %convolution_convert_fusion = bf16[512,512]{0,1:T(8,128)(2,1)} fusion(f32[512]{0:T(512)S(1)} %bitcast.37, bf16[4,512,512]{2,1,0:T(8,128)(2,1)} %param.8, bf16[512,2048]{1,0:T(8,128)(2,1)} %param.7), kind=kOutput, calls=%fused_computation.5 | convolution fusion | flops 537657344 | bytes 2099200 | tf_op jit(solution)/shard_map/dot_general | solution.py:23
  15.7 3.0 %convolution_convert_fusion.1 = bf16[512,512]{0,1:T(8,128)(2,1)} fusion(f32[512]{0:T(512)S(1)} %bitcast.36, bf16[4,512,512]{2,1,0:T(8,128)(2,1)} %param.8, bf16[512,2048]{1,0:T(8,128)(2,1)} %param.7), kind=kOutput, calls=%fused_computation.6 | convolution fusion | flops 537657344 | bytes 2099200 | tf_op jit(solution)/shard_map/dot_general | solution.py:23
  18.7 0.0 copy-start.1
  18.7 1.6 pad_maximum_fusion
  20.2 3.1 %collective-permute-start.1 = (bf16[512,2048]{0,1:T(8,128)(2,1)S(1)}, bf16[512,2048]{0,1:T(8,128)(2,1)S(1)}, u32[]{:S(2)}, u32[]{:S(2)}) collective-permute-start(bf16[512,2048]{0,1:T(8,128)(2,1)S(1)} %pad_maximum_fusion), channel_id=1, source_target_pairs={{0,4},{4,8},{8,12},{12,0},{1,5},{5,9},{9,13},{13,1},{2,6},{6,10},{... | collective-permute-start | bytes 6291464 | tf_op jit(solution)/shard_map/ppermute | solution.py:17
  23.3 47.7 %collective-permute-done.1 = bf16[512,2048]{0,1:T(8,128)(2,1)S(1)} collective-permute-done((bf16[512,2048]{0,1:T(8,128)(2,1)S(1)}, bf16[512,2048]{0,1:T(8,128)(2,1)S(1)}, u32[]{:S(2)}, u32[]{:S(2)}) %collective-permute-start.1) | collective-permute-done | bytes 2097184 | tf_op jit(solution)/shard_map/ppermute | solution.py:17
  71.0 0.0 copy-start.2
  71.0 1.3 copy-done.2
  72.3 0.0 collective-permute-start.3
  72.3 48.7 %collective-permute-done.3 = bf16[512,2048]{0,1:T(8,128)(2,1)} collective-permute-done((bf16[512,2048]{0,1:T(8,128)(2,1)S(1)}, bf16[512,2048]{0,1:T(8,128)(2,1)}, u32[]{:S(2)}, u32[]{:S(2)}) %collective-permute-start.3) | collective-permute-done | bytes 2097184 | tf_op jit(solution)/shard_map/ppermute | solution.py:17
  121.0 0.0 collective-permute-start.5
  121.0 0.0 copy-done.1
  121.0 0.6 fusion.36
  124.2 0.0 copy-done
  124.2 0.3 constant_dynamic-slice_fusion.3
  124.5 1.4 fusion.35
  125.9 0.0 reduce-scatter.5.cloned.1.call-update
  126.0 0.0 reduce-scatter.7.cloned.1.call-start
  126.0 3.0 %fusion.34 = f32[512,128]{1,0:T(8,128)} fusion(bf16[512,2048]{0,1:T(8,128)(2,1)} %copy-done.2, bf16[128,512]{1,0:T(8,128)(2,1)S(1)} %get-tuple-element.7, bf16[128,512]{1,0:T(8,128)(2,1)S(1)} %get-tuple-element.8, bf16[128,512]{1,0:T(8,128)(2,1)S(1)} %get-tuple-element.6, bf16[128,512]{1,0:T(8,128)(2,1)S(1)} %get-tuple-element.5), kind=kOutput, calls=%fused_computation.46 | convolution fusion | flops 270532608 | bytes 2883584 | tf_op jit(solution)/shard_map/dot_general | solution.py:27
  129.0 0.0 reduce-scatter.7.cloned.1.call-update
  129.1 0.0 reduce-scatter.9.cloned.1.call-start
  129.1 3.0 %fusion.33 = f32[512,128]{1,0:T(8,128)} fusion(bf16[512,2048]{0,1:T(8,128)(2,1)} %collective-permute-done.3, bf16[128,512]{1,0:T(8,128)(2,1)S(1)} %get-tuple-element.7, bf16[128,512]{1,0:T(8,128)(2,1)S(1)} %get-tuple-element.8, bf16[128,512]{1,0:T(8,128)(2,1)S(1)} %get-tuple-element.6, bf16[128,512]{1,0:T(8,128)(2,1)S(1)} %get-tuple-element.5), kind=kOutput, calls=%fused_computation.45 | convolution fusion | flops 270532608 | bytes 2883584 | tf_op jit(solution)/shard_map/dot_general | solution.py:27
  132.2 0.0 reduce-scatter.9.cloned.1.call-update
  132.2 0.0 copy-start.3
  132.2 0.0 reduce-scatter.11.cloned.1.call-start
  132.3 36.8 %collective-permute-done.5 = bf16[512,2048]{0,1:T(8,128)(2,1)} collective-permute-done((bf16[512,2048]{0,1:T(8,128)(2,1)}, bf16[512,2048]{0,1:T(8,128)(2,1)}, u32[]{:S(2)}, u32[]{:S(2)}) %collective-permute-start.5) | collective-permute-done | bytes 2097184 | tf_op jit(solution)/shard_map/ppermute | solution.py:17
  169.0 3.1 %fusion.32 = f32[512,128]{1,0:T(8,128)} fusion(bf16[512,2048]{0,1:T(8,128)(2,1)} %collective-permute-done.5, bf16[128,512]{1,0:T(8,128)(2,1)S(1)} %get-tuple-element.7, bf16[128,512]{1,0:T(8,128)(2,1)S(1)} %get-tuple-element.8, bf16[128,512]{1,0:T(8,128)(2,1)S(1)} %get-tuple-element.6, bf16[128,512]{1,0:T(8,128)(2,1)S(1)} %get-tuple-element.5), kind=kOutput, calls=%fused_computation.44 | convolution fusion | flops 270532608 | bytes 2883584 | tf_op jit(solution)/shard_map/dot_general | solution.py:27
  172.1 0.0 reduce-scatter.11.cloned.1.call-update
  172.1 0.0 copy-done.3
  172.1 0.1 collective-permute-start
  172.2 5.4 %collective-permute-done = s32[512]{0:T(512)S(1)} collective-permute-done((s32[512]{0:T(512)S(1)}, s32[512]{0:T(512)S(1)}, u32[]{:S(2)}, u32[]{:S(2)}) %collective-permute-start) | collective-permute-done | bytes 2080 | tf_op jit(solution)/shard_map/ppermute | solution.py:17
  177.6 0.0 collective-permute-start.2
  177.6 5.4 %collective-permute-done.2 = s32[512]{0:T(512)S(1)} collective-permute-done((s32[512]{0:T(512)S(1)}, s32[512]{0:T(512)S(1)}, u32[]{:S(2)}, u32[]{:S(2)}) %collective-permute-start.2) | collective-permute-done | bytes 2080 | tf_op jit(solution)/shard_map/ppermute | solution.py:17
  183.0 0.0 collective-permute-start.4
  183.0 0.1 dynamic_slice.24
  183.0 0.1 dynamic_slice.29
  183.1 0.1 dynamic_slice.30
  183.2 5.2 %collective-permute-done.4 = s32[512]{0:T(512)S(1)} collective-permute-done((s32[512]{0:T(512)S(1)}, s32[512]{0:T(512)S(1)}, u32[]{:S(2)}, u32[]{:S(2)}) %collective-permute-start.4) | collective-permute-done | bytes 2080 | tf_op jit(solution)/shard_map/ppermute | solution.py:17
  188.3 0.1 dynamic_slice.31
  188.4 0.0 reduce-scatter.5.cloned.1.call-done
  188.4 4.1 %reduce-scatter.9.cloned.1.call-done = f32[128,128]{1,0:T(8,128)} async-done(((f32[512,128]{1,0:T(8,128)}), f32[128,128]{1,0:T(8,128)}) %reduce-scatter.9.cloned.1.call-update) | async-done | bytes 65552 | tf_op jit(solution)/shard_map/reduce_scatter | solution.py:44
  192.5 22.5 %reduce-scatter.11.cloned.1.call-done = f32[128,128]{1,0:T(8,128)} async-done(((f32[512,128]{1,0:T(8,128)}), f32[128,128]{1,0:T(8,128)}) %reduce-scatter.11.cloned.1.call-update) | async-done | bytes 65552 | tf_op jit(solution)/shard_map/reduce_scatter | solution.py:44
  215.1 1.1 select_bitcast_fusion.3
  216.1 0.7 pad_maximum_fusion.2
  (3 shorter events, 0.0 us)
Async XLA Ops:
  6.5 181.9 %reduce-scatter.5.cloned.1.call-start = ((), (), s32[]{:S(2)}) async-start(), calls=%async_computation.4 | async-start | bytes 327680 | tf_op jit(solution)/shard_map/reduce_scatter | solution.py:44
  18.7 102.4 %copy-start.1 = (s32[4]{0:T(128)S(1)}, s32[4]{0:T(128)}, u32[]{:S(2)}) copy-start(s32[4]{0:T(128)} %param.10) | copy-start | bytes 52
  18.7 105.5 %copy-start = (bf16[128,2048]{1,0:T(8,128)(2,1)S(1)}, bf16[128,2048]{1,0:T(8,128)(2,1)}, u32[]{:S(2)}) copy-start(bf16[128,2048]{1,0:T(8,128)(2,1)} %param.6) | copy-start | bytes 1572868
  20.2 50.7 %collective-permute-start.1 = (bf16[512,2048]{0,1:T(8,128)(2,1)S(1)}, bf16[512,2048]{0,1:T(8,128)(2,1)S(1)}, u32[]{:S(2)}, u32[]{:S(2)}) collective-permute-start(bf16[512,2048]{0,1:T(8,128)(2,1)S(1)} %pad_maximum_fusion), channel_id=1, source_target_pairs={{0,4},{4,8},{8,12},{12,0},{1,5},{5,9},{9,13},{13,1},{2,6},{6,10},{... | collective-permute-start | bytes 6291464 | tf_op jit(solution)/shard_map/ppermute | solution.py:17
  71.0 1.3 copy-start.2
  72.3 48.7 %collective-permute-start.3 = (bf16[512,2048]{0,1:T(8,128)(2,1)S(1)}, bf16[512,2048]{0,1:T(8,128)(2,1)}, u32[]{:S(2)}, u32[]{:S(2)}) collective-permute-start(bf16[512,2048]{0,1:T(8,128)(2,1)S(1)} %collective-permute-done.1), channel_id=1, source_target_pairs={{0,4},{4,8},{8,12},{12,0},{1,5},{5,9},{9,13},{13,1},{2,6},{6,10},{... | collective-permute-start | bytes 6291464 | tf_op jit(solution)/shard_map/ppermute | solution.py:17
  121.0 48.0 %collective-permute-start.5 = (bf16[512,2048]{0,1:T(8,128)(2,1)}, bf16[512,2048]{0,1:T(8,128)(2,1)}, u32[]{:S(2)}, u32[]{:S(2)}) collective-permute-start(bf16[512,2048]{0,1:T(8,128)(2,1)} %collective-permute-done.3), channel_id=1, source_target_pairs={{0,4},{4,8},{8,12},{12,0},{1,5},{5,9},{9,13},{13,1},{2,6},{6,10},{... | collective-permute-start | bytes 6291464 | tf_op jit(solution)/shard_map/ppermute | solution.py:17
  126.0 62.5 %reduce-scatter.7.cloned.1.call-start = ((), (), s32[]{:S(2)}) async-start(), calls=%async_computation.5 | async-start | bytes 327680 | tf_op jit(solution)/shard_map/reduce_scatter | solution.py:44
  129.1 63.5 %reduce-scatter.9.cloned.1.call-start = ((), (), s32[]{:S(2)}) async-start(), calls=%async_computation.6 | async-start | bytes 327680 | tf_op jit(solution)/shard_map/reduce_scatter | solution.py:44
  132.2 39.9 %copy-start.3 = (s32[512]{0:T(512)S(1)}, s32[512]{0:T(512)}, u32[]{:S(2)}) copy-start(s32[512]{0:T(512)} %param.11) | copy-start | bytes 6148
  132.2 82.9 %reduce-scatter.11.cloned.1.call-start = ((), (), s32[]{:S(2)}) async-start(), calls=%async_computation.7 | async-start | bytes 327680 | tf_op jit(solution)/shard_map/reduce_scatter | solution.py:44
  172.1 5.4 %collective-permute-start = (s32[512]{0:T(512)S(1)}, s32[512]{0:T(512)S(1)}, u32[]{:S(2)}, u32[]{:S(2)}) collective-permute-start(s32[512]{0:T(512)S(1)} %copy-done.3), channel_id=1, source_target_pairs={{0,4},{4,8},{8,12},{12,0},{1,5},{5,9},{9,13},{13,1},{2,6},{6,10},{... | collective-permute-start | bytes 6152 | tf_op jit(solution)/shard_map/ppermute | solution.py:17
  177.6 5.4 %collective-permute-start.2 = (s32[512]{0:T(512)S(1)}, s32[512]{0:T(512)S(1)}, u32[]{:S(2)}, u32[]{:S(2)}) collective-permute-start(s32[512]{0:T(512)S(1)} %collective-permute-done), channel_id=1, source_target_pairs={{0,4},{4,8},{8,12},{12,0},{1,5},{5,9},{9,13},{13,1},{2,6},{6,10},{... | collective-permute-start | bytes 6152 | tf_op jit(solution)/shard_map/ppermute | solution.py:17
  183.0 5.4 %collective-permute-start.4 = (s32[512]{0:T(512)S(1)}, s32[512]{0:T(512)S(1)}, u32[]{:S(2)}, u32[]{:S(2)}) collective-permute-start(s32[512]{0:T(512)S(1)} %collective-permute-done.2), channel_id=1, source_target_pairs={{0,4},{4,8},{8,12},{12,0},{1,5},{5,9},{9,13},{13,1},{2,6},{6,10},{... | collective-permute-start | bytes 6152 | tf_op jit(solution)/shard_map/ppermute | solution.py:17
Sparse Core Ops, SparseCore 0:
  126.1 21.2 reduce-scatter.4
  149.9 20.0 reduce-scatter.6
  172.5 19.9 reduce-scatter.8
  195.0 20.0 reduce-scatter.10
where the time goes:
time: 224 us; the launch traced here: 223 us
  waiting for transfers between devices  176 us (79%)
  matrix products  21.9 us (10%)
  between operations  15.7 us (7%)
  other arithmetic  4.2 us (2%)
  starting transfers between devices  3.27 us (1%)
  local copies, waits for them, and re-layouts  2.6 us (1%)
    ppermute x6, waiting for transfers between devices, from_behind(): return lax.ppermute(value, axis, pairs)  149 us
    reduce_scatter x4, waiting for transfers between devices, layer_tiles(): lax.psum_scatter(partial_value(jnp.int32(0), lax.axis_size('layer') * sha...  26.6 us
    dot_general x4, matrix products, precondition(): jnp.dot(scaled, basis.T, preferred_element_type=jnp.float32)  11.3 us
    dot_general x4, matrix products, contract(): lax.dot_general(queries, documents, (((1,), (1,)), ((), ())), preferred_e...  10.6 us
  transfers between devices with their start and end apart: 10, of which 8 were waited for; matrix products, arithmetic and copies ran while one was open for 5% of the time, Pallas kernels for 0%

commit v1 on v0

v1 whole, which is shorter than its diff:
```python
import functools

import jax
import jax.numpy as jnp
from jax import lax
from jax.experimental import pallas as pl
from jax.experimental.pallas import tpu as pltpu
from jax.sharding import PartitionSpec as P

LDIM = 512
LAY_DEV = 4
STEPS = 4
DAMPING = 0.05
NT = (((1,), (1,)), ((), ()))
VMEM_LIMIT = 40 * 1024 * 1024


def precondition_kernel(slots, query_ref, basis_ref, values_ref, out_ref):
    layer = pl.program_id(0)
    basis = basis_ref[0]
    projected = jnp.dot(query_ref[...], basis, preferred_element_type=jnp.float32)
    scaled = (projected / (values_ref[pl.ds(layer, 1), :] + DAMPING)).astype(jnp.bfloat16)
    out_ref[...] = lax.dot_general(scaled, basis, NT, preferred_element_type=jnp.float32).astype(jnp.bfloat16)


def precondition(query_grads, eigenbases, eigenvalues, slots):
    rows = query_grads.shape[0]
    return pl.pallas_call(
        precondition_kernel,
        out_shape=jax.ShapeDtypeStruct((rows, LAY_DEV * LDIM), jnp.bfloat16),
        grid_spec=pltpu.PrefetchScalarGridSpec(
            num_scalar_prefetch=1,
            grid=(LAY_DEV,),
            in_specs=[
                pl.BlockSpec((rows, LDIM), lambda layer, slots: (0, layer)),
                pl.BlockSpec((1, LDIM, LDIM), lambda layer, slots: (layer, 0, 0)),
                pl.BlockSpec((LAY_DEV, LDIM), lambda layer, slots: (0, 0)),
            ],
            out_specs=pl.BlockSpec((rows, LDIM), lambda layer, slots: (0, slots[layer])),
        ),
        compiler_params=pltpu.CompilerParams(vmem_limit_bytes=VMEM_LIMIT),
        cost_estimate=pl.CostEstimate(
            flops=4 * rows * LAY_DEV * LDIM * LDIM, bytes_accessed=6 * 1024 * 1024, transcendentals=0
        ),
    )(slots, query_grads, eigenbases, eigenvalues)


def score_kernel(shares, place, queries_ref, documents_ref, ids_ref, *refs):
    *out_refs, held = refs
    tile = lax.dot_general(queries_ref[...], documents_ref[...], NT, preferred_element_type=jnp.float32)
    doc_ids = place[1] + lax.broadcasted_iota(jnp.int32, tile.shape, 1)
    held[...] = jnp.where(ids_ref[...] == doc_ids, 0.0, tile)
    share_rows = tile.shape[0] // shares
    for turn in range(shares):
        share = lax.rem(place[0] + turn, shares)
        first = pl.multiple_of(share * share_rows, share_rows)
        out_refs[turn][...] = held[pl.ds(first, share_rows), :].astype(jnp.bfloat16)


def partial_scores(conditioned, documents, query_ids, place, shares):
    rows, dims = conditioned.shape
    docs = documents.shape[0]
    vmem = pl.BlockSpec(memory_space=pltpu.VMEM)
    return pl.pallas_call(
        functools.partial(score_kernel, shares),
        out_shape=[jax.ShapeDtypeStruct((rows // shares, docs), jnp.bfloat16)] * shares,
        in_specs=[pl.BlockSpec(memory_space=pltpu.SMEM), vmem, vmem, vmem],
        out_specs=[vmem] * shares,
        scratch_shapes=[pltpu.VMEM((rows, docs), jnp.float32)],
        compiler_params=pltpu.CompilerParams(vmem_limit_bytes=VMEM_LIMIT),
        cost_estimate=pl.CostEstimate(
            flops=2 * rows * docs * dims, bytes_accessed=2 * dims * (rows + docs), transcendentals=0
        ),
    )(place, conditioned, documents, query_ids)


def sum_kernel(shares, *refs):
    *in_refs, out_ref = refs
    for step in range(STEPS):
        total = in_refs[step * shares][...].astype(jnp.float32)
        for turn in range(1, shares):
            total += in_refs[step * shares + turn][...].astype(jnp.float32)
        out_ref[step] = total


def sum_shares(blocks, shares):
    vmem = pl.BlockSpec(memory_space=pltpu.VMEM)
    return pl.pallas_call(
        functools.partial(sum_kernel, shares),
        out_shape=jax.ShapeDtypeStruct((STEPS,) + blocks[0].shape, jnp.float32),
        in_specs=[vmem] * len(blocks),
        out_specs=vmem,
    )(*blocks)


def local(train_grads, query_grads, eigenbases, eigenvalues, layer_offsets, query_doc_ids):
    n_rows = lax.axis_size("rows")
    shares = lax.axis_size("layer")
    row_index = lax.axis_index("rows")
    layer_index = lax.axis_index("layer")
    doc_rows = train_grads.shape[0]

    documents = [train_grads]
    for step in range(1, STEPS):
        pairs = [(source, (source - step) % n_rows) for source in range(n_rows)]
        documents.append(lax.ppermute(train_grads, "rows", pairs))

    slots = layer_offsets // LDIM - layer_index * LAY_DEV
    conditioned = precondition(query_grads, eigenbases, eigenvalues, slots)
    query_ids = query_doc_ids[:, None]

    blocks = [None] * (STEPS * shares)
    for step in range(STEPS):
        doc_base = (row_index + step) % n_rows * doc_rows
        place = jnp.stack([layer_index, doc_base]).astype(jnp.int32)
        tiles = partial_scores(conditioned, documents[step], query_ids, place, shares)
        for turn in range(shares):
            pairs = [
                (row * shares + lay, (row + step) % n_rows * shares + (lay + turn) % shares)
                for row in range(n_rows)
                for lay in range(shares)
            ]
            tile = tiles[turn]
            if step or turn:
                tile = lax.ppermute(tile, ("rows", "layer"), pairs)
            blocks[step * shares + turn] = tile
    return sum_shares(blocks, shares)


def solution(mesh):
    in_specs = (
        P(("group", "rows"), "layer"),
        P(("group", "rows"), "layer"),
        P("layer", None, None),
        P("layer", None),
        P("layer"),
        P(("group", "rows")),
    )
    out_specs = P(None, "layer", ("group", "rows"))
    return jax.shard_map(local, mesh=mesh, in_specs=in_specs, out_specs=out_specs, check_vma=False)
```

time: 224 us -> 76.9 us (0.34)
  waiting for transfers between devices: 176 us -> 22.2 us
  starting transfers between devices: 3.27 us -> 35.6 us
  matrix products: 21.9 us -> 0 us
  between operations: 15.7 us -> 0.29 us
  Pallas kernels: 0 us -> 11.6 us
  other arithmetic: 4.2 us -> 0.96 us
  local copies, waits for them, and re-layouts: 2.6 us -> 5.84 us
    ppermute x6 -> x18, waiting for transfers between devices: 149 us -> 22.2 us  [the longest x3 19.4 us: local(): documents.append(lax.ppermute(train_grads, 'rows', pairs))]
    ppermute x6 -> x18, starting transfers between devices: 3.15 us -> 35.6 us  [the longest x15 27.8 us: local(): tile = lax.ppermute(tile, ('rows', 'layer'), pairs)]
    reduce_scatter x4 -> x0, waiting for transfers between devices: 26.6 us -> none  [layer_tiles(): lax.psum_scatter(partial_value(jnp.int32(0), lax.axis_size('layer') * sha...]
    dot_general x8 -> x0, matrix products: 21.9 us -> none  [the longest x4 11.3 us: precondition(): jnp.dot(scaled, basis.T, preferred_element_type=jnp.float32)]
    pallas_call x0 -> x6, Pallas kernels: none -> 11.6 us  [the longest x4 6.12 us: partial_scores(): pl.pallas_call(functools.partial(score_kernel, shares), out_shape=[jax.Sh...]
    unnamed x8 -> x40, local copies, waits for them, and re-layouts: 1.35 us -> 5.02 us
  transfers between devices with their start and end apart: 10 -> 18, of which waited for: 8 -> 4; matrix products, arithmetic and copies ran while one was open for 5% -> 2% of each run, Pallas kernels for 0% -> 13%
where the time goes in v1:
time: 76.9 us; the launch traced here: 76.5 us
  starting transfers between devices  35.6 us (46%)
  waiting for transfers between devices  22.2 us (29%)
  Pallas kernels  11.6 us (15%)
  local copies, waits for them, and re-layouts  5.84 us (8%)
  other arithmetic  0.96 us (1%)
    ppermute x15, starting transfers between devices, local(): tile = lax.ppermute(tile, ('rows', 'layer'), pairs)  27.8 us
    ppermute x3, waiting for transfers between devices, local(): documents.append(lax.ppermute(train_grads, 'rows', pairs))  19.4 us
    ppermute x3, starting transfers between devices, local(): documents.append(lax.ppermute(train_grads, 'rows', pairs))  7.86 us
    pallas_call x4, Pallas kernels, partial_scores(): pl.pallas_call(functools.partial(score_kernel, shares), out_shape=[jax.Sh...  6.12 us
    unnamed x40, local copies, waits for them, and re-layouts  5.02 us
    pallas_call x1, Pallas kernels, precondition(): pl.pallas_call(precondition_kernel, out_shape=jax.ShapeDtypeStruct((rows,...  3.72 us
    ppermute x15, waiting for transfers between devices, local(): tile = lax.ppermute(tile, ('rows', 'layer'), pairs)  2.75 us
    pallas_call x1, Pallas kernels, sum_shares(): pl.pallas_call(functools.partial(sum_kernel, shares), out_shape=jax.Shape...  1.77 us
  transfers between devices with their start and end apart: 18, of which 4 were waited for; matrix products, arithmetic and copies ran while one was open for 2% of the time, Pallas kernels for 13%

profile of v1, /device:TPU:0, one launch (start us, length us, event | category | flops | bytes accessed | tf_op | source)
XLA Modules:
  0.0 76.5 jit_solution(12299260103111642202)
XLA Ops:
  0.0 4.0 %collective-permute-start.8 = (bf16[128,2048]{1,0:T(8,128)(2,1)}, bf16[128,2048]{1,0:T(8,128)(2,1)}, u32[]{:S(2)}, u32[]{:S(2)}) collective-permute-start(bf16[128,2048]{1,0:T(8,128)(2,1)} %documents_ref.1), channel_id=1, source_target_pairs={{0,8},{4,12},{8,0},{12,4},{1,9},{5,13},{9,1},{13,5},{2,10},{6,14},... | collective-permute-start | bytes 1572872 | tf_op jit(solution)/shard_map/ppermute | solution.py:106
  4.0 1.6 %collective-permute-start.13 = (bf16[128,2048]{1,0:T(8,128)(2,1)}, bf16[128,2048]{1,0:T(8,128)(2,1)}, u32[]{:S(2)}, u32[]{:S(2)}) collective-permute-start(bf16[128,2048]{1,0:T(8,128)(2,1)} %documents_ref.1), channel_id=1, source_target_pairs={{0,4},{4,8},{8,12},{12,0},{1,5},{5,9},{9,13},{13,1},{2,6},{6,10},{... | collective-permute-start | bytes 1572872 | tf_op jit(solution)/shard_map/ppermute | solution.py:106
  5.6 2.2 %collective-permute-start.3 = (bf16[128,2048]{1,0:T(8,128)(2,1)}, bf16[128,2048]{1,0:T(8,128)(2,1)S(1)}, u32[]{:S(2)}, u32[]{:S(2)}) collective-permute-start(bf16[128,2048]{1,0:T(8,128)(2,1)} %documents_ref.1), channel_id=1, source_target_pairs={{0,12},{4,0},{8,4},{12,8},{1,13},{5,1},{9,5},{13,9},{2,14},{6,2},{... | collective-permute-start | bytes 1572872 | tf_op jit(solution)/shard_map/ppermute | solution.py:106
  7.9 0.7 fusion.slots
  8.5 0.1 pad_add_fusion.place
  8.6 0.8 %copy.7.ids_ref = s32[512,1]{1,0:T(8,128)S(1)} copy(s32[512,1]{0,1:T(1,128)} %bitcast.6) | data formatting | bytes 4096 | tf_op jit(solution)/shard_map/broadcast_in_dim | solution.py:110
  9.4 0.0 copy-start.2
  9.4 1.6 %copy-done.2 = bf16[512,2048]{1,0:T(8,128)(2,1)S(1)} copy-done((bf16[512,2048]{1,0:T(8,128)(2,1)S(1)}, bf16[512,2048]{1,0:T(8,128)(2,1)}, u32[]{:S(2)}) %copy-start.2) | copy-done | bytes 2097176
  11.0 1.6 %copy-done.3 = bf16[4,512,512]{2,1,0:T(8,128)(2,1)S(1)} copy-done((bf16[4,512,512]{2,1,0:T(8,128)(2,1)S(1)}, bf16[4,512,512]{2,1,0:T(8,128)(2,1)}, u32[]{:S(2)}) %copy-start.3) | copy-done | bytes 2097176
  12.6 0.7 copy-done.4
  13.3 3.7 %shard_map.64.queries_ref = bf16[512,2048]{1,0:T(8,128)(2,1)S(1)} custom-call(s32[4]{0:T(128)S(1)} %fusion.slots, bf16[512,2048]{1,0:T(8,128)(2,1)S(1)} %copy-done.2, bf16[4,512,512]{2,1,0:T(8,128)(2,1)S(1)} %copy-done.3, f32[4,512]{1,0:T(4,128)S(1)} %copy-done.4), custom_call_target="tpu_custom_call" | custom-call | flops 2147483648 | bytes 6291456 | tf_op jit(solution)/shard_map/pallas_call | solution.py:28
  17.1 1.3 %shard_map.65 = (bf16[128,128]{1,0:T(8,128)(2,1)S(1)}, bf16[128,128]{1,0:T(8,128)(2,1)S(1)}, bf16[128,128]{1,0:T(8,128)(2,1)S(1)}, bf16[128,128]{1,0:T(8,128)(2,1)S(1)}) custom-call(s32[2]{0:T(128)S(1)} %pad_add_fusion.place, bf16[512,2048]{1,0:T(8,128)(2,1)S(1)} %shard_map.64.queries_ref, bf16[128,2048]{1,0:T(8,128)(2,1)S(1)} %copy-done, ...), custom_call_target="tpu_custom_call" | custom-call | flops 268435456 | bytes 2621440 | tf_op jit(solution)/shard_map/pallas_call | solution.py:64
  18.3 0.6 copy-done.1
  18.9 0.0 collective-permute-start
  18.9 1.5 %collective-permute-start.1 = (bf16[128,128]{1,0:T(8,128)(2,1)S(1)}, bf16[128,128]{1,0:T(8,128)(2,1)S(1)}, u32[]{:S(2)}, u32[]{:S(2)}) collective-permute-start(bf16[128,128]{1,0:T(8,128)(2,1)S(1)} %get-tuple-element.23), channel_id=1, source_target_pairs={{0,2},{1,3},{2,0},{3,1},{4,6},{5,7},{6,4},{7,5},{8,10},{9,11},{10,... | collective-permute-start | bytes 98312 | tf_op jit(solution)/shard_map/ppermute | solution.py:125
  20.5 0.1 pad_add_fusion.2.place
  20.5 19.4 %collective-permute-done.8.documents_ref = bf16[128,2048]{1,0:T(8,128)(2,1)} collective-permute-done((bf16[128,2048]{1,0:T(8,128)(2,1)}, bf16[128,2048]{1,0:T(8,128)(2,1)}, u32[]{:S(2)}, u32[]{:S(2)}) %collective-permute-start.8) | collective-permute-done | bytes 524320 | tf_op jit(solution)/shard_map/ppermute | solution.py:106
  40.0 0.0 collective-permute-start.2
  40.0 1.8 %shard_map.67 = (bf16[128,128]{1,0:T(8,128)(2,1)S(1)}, bf16[128,128]{1,0:T(8,128)(2,1)S(1)}, bf16[128,128]{1,0:T(8,128)(2,1)S(1)}, bf16[128,128]{1,0:T(8,128)(2,1)S(1)}) custom-call(s32[2]{0:T(128)S(1)} %pad_add_fusion.2.place, bf16[512,2048]{1,0:T(8,128)(2,1)S(1)} %shard_map.64.queries_ref, bf16[128,2048]{1,0:T(8,128)(2,1)} %collective-permute-done.8.documents_ref, ...), custom_call_target="tpu_custom_call" | custom-call | flops 268435456 | bytes 2621440 | tf_op jit(solution)/shard_map/pallas_call | solution.py:64
  41.8 0.1 collective-permute-start.10
  41.9 0.0 collective-permute-done.13.documents_ref
  41.9 12.5 %collective-permute-start.11 = (bf16[128,128]{1,0:T(8,128)(2,1)S(1)}, bf16[128,128]{1,0:T(8,128)(2,1)S(1)}, u32[]{:S(2)}, u32[]{:S(2)}) collective-permute-start(bf16[128,128]{1,0:T(8,128)(2,1)S(1)} %get-tuple-element.31), channel_id=1, source_target_pairs={{0,10},{1,11},{2,8},{3,9},{4,14},{5,15},{6,12},{7,13},{8,2},{9,3},... | collective-permute-start | bytes 98312 | tf_op jit(solution)/shard_map/ppermute | solution.py:125
  54.3 0.1 pad_add_fusion.3.place
  54.4 1.8 %shard_map.68 = (bf16[128,128]{1,0:T(8,128)(2,1)S(1)}, bf16[128,128]{1,0:T(8,128)(2,1)S(1)}, bf16[128,128]{1,0:T(8,128)(2,1)S(1)}, bf16[128,128]{1,0:T(8,128)(2,1)S(1)}) custom-call(s32[2]{0:T(128)S(1)} %pad_add_fusion.3.place, bf16[512,2048]{1,0:T(8,128)(2,1)S(1)} %shard_map.64.queries_ref, bf16[128,2048]{1,0:T(8,128)(2,1)} %collective-permute-done.13.documents_ref, ...), custom_call_target="tpu_custom_call" | custom-call | flops 268435456 | bytes 2621440 | tf_op jit(solution)/shard_map/pallas_call | solution.py:64
  56.2 0.0 collective-permute-done.1.refs_2_
  56.2 0.1 collective-permute-start.12
  56.3 0.0 collective-permute-done.2.refs_3_
  56.3 0.5 collective-permute-start.14
  56.8 3.3 %collective-permute-start.15 = (bf16[128,128]{1,0:T(8,128)(2,1)S(1)}, bf16[128,128]{1,0:T(8,128)(2,1)S(1)}, u32[]{:S(2)}, u32[]{:S(2)}) collective-permute-start(bf16[128,128]{1,0:T(8,128)(2,1)S(1)} %get-tuple-element.34), channel_id=1, source_target_pairs={{0,13},{1,14},{2,15},{3,12},{4,1},{5,2},{6,3},{7,0},{8,5},{9,6},{1... | collective-permute-start | bytes 98312 | tf_op jit(solution)/shard_map/ppermute | solution.py:125
  60.1 0.8 %collective-permute-start.16 = (bf16[128,128]{1,0:T(8,128)(2,1)S(1)}, bf16[128,128]{1,0:T(8,128)(2,1)S(1)}, u32[]{:S(2)}, u32[]{:S(2)}) collective-permute-start(bf16[128,128]{1,0:T(8,128)(2,1)S(1)} %get-tuple-element.35), channel_id=1, source_target_pairs={{0,14},{1,15},{2,12},{3,13},{4,2},{5,3},{6,0},{7,1},{8,6},{9,7},{1... | collective-permute-start | bytes 98312 | tf_op jit(solution)/shard_map/ppermute | solution.py:125
  60.9 0.7 collective-permute-start.17
  61.6 0.1 pad_add_fusion.1.place
  61.7 1.3 %shard_map.66 = (bf16[128,128]{1,0:T(8,128)(2,1)S(1)}, bf16[128,128]{1,0:T(8,128)(2,1)S(1)}, bf16[128,128]{1,0:T(8,128)(2,1)S(1)}, bf16[128,128]{1,0:T(8,128)(2,1)S(1)}) custom-call(s32[2]{0:T(128)S(1)} %pad_add_fusion.1.place, bf16[512,2048]{1,0:T(8,128)(2,1)S(1)} %shard_map.64.queries_ref, bf16[128,2048]{1,0:T(8,128)(2,1)S(1)} %collective-permute-done.3.documents_ref, ...), custom_call_target="tpu_custom_call" | custom-call | flops 268435456 | bytes 2621440 | tf_op jit(solution)/shard_map/pallas_call | solution.py:64
  63.0 0.0 collective-permute-done.12.refs_11_
  63.0 1.7 %collective-permute-start.4 = (bf16[128,128]{1,0:T(8,128)(2,1)S(1)}, bf16[128,128]{1,0:T(8,128)(2,1)S(1)}, u32[]{:S(2)}, u32[]{:S(2)}) collective-permute-start(bf16[128,128]{1,0:T(8,128)(2,1)S(1)} %get-tuple-element.25), channel_id=1, source_target_pairs={{0,4},{1,5},{2,6},{3,7},{4,8},{5,9},{6,10},{7,11},{8,12},{9,13},{1... | collective-permute-start | bytes 98312 | tf_op jit(solution)/shard_map/ppermute | solution.py:125
  64.7 0.0 collective-permute-done.14.refs_12_
  64.7 0.3 collective-permute-start.5
  65.0 1.7 %collective-permute-start.6 = (bf16[128,128]{1,0:T(8,128)(2,1)S(1)}, bf16[128,128]{1,0:T(8,128)(2,1)S(1)}, u32[]{:S(2)}, u32[]{:S(2)}) collective-permute-start(bf16[128,128]{1,0:T(8,128)(2,1)S(1)} %get-tuple-element.27), channel_id=1, source_target_pairs={{0,6},{1,7},{2,4},{3,5},{4,10},{5,11},{6,8},{7,9},{8,14},{9,15},{1... | collective-permute-start | bytes 98312 | tf_op jit(solution)/shard_map/ppermute | solution.py:125
  66.7 2.6 %collective-permute-start.7 = (bf16[128,128]{1,0:T(8,128)(2,1)S(1)}, bf16[128,128]{1,0:T(8,128)(2,1)S(1)}, u32[]{:S(2)}, u32[]{:S(2)}) collective-permute-start(bf16[128,128]{1,0:T(8,128)(2,1)S(1)} %get-tuple-element.28), channel_id=1, source_target_pairs={{0,7},{1,4},{2,5},{3,6},{4,11},{5,8},{6,9},{7,10},{8,15},{9,12},{1... | collective-permute-start | bytes 98312 | tf_op jit(solution)/shard_map/ppermute | solution.py:125
  69.3 0.0 collective-permute-done.17.refs_15_
  69.3 2.1 %collective-permute-start.9 = (bf16[128,128]{1,0:T(8,128)(2,1)S(1)}, bf16[128,128]{1,0:T(8,128)(2,1)S(1)}, u32[]{:S(2)}, u32[]{:S(2)}) collective-permute-start(bf16[128,128]{1,0:T(8,128)(2,1)S(1)} %get-tuple-element.29), channel_id=1, source_target_pairs={{0,8},{1,9},{2,10},{3,11},{4,12},{5,13},{6,14},{7,15},{8,0},{9,1},... | collective-permute-start | bytes 98312 | tf_op jit(solution)/shard_map/ppermute | solution.py:125
  71.4 0.0 collective-permute-done.4.refs_4_
  71.4 0.0 collective-permute-done.5.refs_5_
  71.4 0.3 collective-permute-done.6.refs_6_
  71.7 1.2 %collective-permute-done.7.refs_7_ = bf16[128,128]{1,0:T(8,128)(2,1)S(1)} collective-permute-done((bf16[128,128]{1,0:T(8,128)(2,1)S(1)}, bf16[128,128]{1,0:T(8,128)(2,1)S(1)}, u32[]{:S(2)}, u32[]{:S(2)}) %collective-permute-start.7) | collective-permute-done | bytes 32800 | tf_op jit(solution)/shard_map/ppermute | solution.py:125
  72.9 1.2 %collective-permute-done.9.refs_8_ = bf16[128,128]{1,0:T(8,128)(2,1)S(1)} collective-permute-done((bf16[128,128]{1,0:T(8,128)(2,1)S(1)}, bf16[128,128]{1,0:T(8,128)(2,1)S(1)}, u32[]{:S(2)}, u32[]{:S(2)}) %collective-permute-start.9) | collective-permute-done | bytes 32800 | tf_op jit(solution)/shard_map/ppermute | solution.py:125
  74.3 0.5 copy-done.19
  74.8 1.8 %shard_map.69 = f32[4,128,128]{2,1,0:T(8,128)} custom-call(bf16[128,128]{1,0:T(8,128)(2,1)} %copy-done.1, bf16[128,128]{1,0:T(8,128)(2,1)} %copy-done.5, bf16[128,128]{1,0:T(8,128)(2,1)} %copy-done.6, bf16[128,128]{1,0:T(8,128)(2,1)} %copy-done.7, bf16[128,128]{1,0:T(8,128)(2,1)} %copy-done.15, bf16[128,128]{1,0:T(8,128)(2,1)} %copy-done.16, ...), custom_call_target="tpu_custom_call" | custom-call | tf_op jit(solution)/shard_map/pallas_call | solution.py:88
  (40 shorter events, 0.1 us)
Async XLA Ops:
  0.0 40.0 %collective-permute-start.8 = (bf16[128,2048]{1,0:T(8,128)(2,1)}, bf16[128,2048]{1,0:T(8,128)(2,1)}, u32[]{:S(2)}, u32[]{:S(2)}) collective-permute-start(bf16[128,2048]{1,0:T(8,128)(2,1)} %documents_ref.1), channel_id=1, source_target_pairs={{0,8},{4,12},{8,0},{12,4},{1,9},{5,13},{9,1},{13,5},{2,10},{6,14},... | collective-permute-start | bytes 1572872 | tf_op jit(solution)/shard_map/ppermute | solution.py:106
  4.0 37.8 %collective-permute-start.13 = (bf16[128,2048]{1,0:T(8,128)(2,1)}, bf16[128,2048]{1,0:T(8,128)(2,1)}, u32[]{:S(2)}, u32[]{:S(2)}) collective-permute-start(bf16[128,2048]{1,0:T(8,128)(2,1)} %documents_ref.1), channel_id=1, source_target_pairs={{0,4},{4,8},{8,12},{12,0},{1,5},{5,9},{9,13},{13,1},{2,6},{6,10},{... | collective-permute-start | bytes 1572872 | tf_op jit(solution)/shard_map/ppermute | solution.py:106
  5.6 51.2 %collective-permute-start.3 = (bf16[128,2048]{1,0:T(8,128)(2,1)}, bf16[128,2048]{1,0:T(8,128)(2,1)S(1)}, u32[]{:S(2)}, u32[]{:S(2)}) collective-permute-start(bf16[128,2048]{1,0:T(8,128)(2,1)} %documents_ref.1), channel_id=1, source_target_pairs={{0,12},{4,0},{8,4},{12,8},{1,13},{5,1},{9,5},{13,9},{2,14},{6,2},{... | collective-permute-start | bytes 1572872 | tf_op jit(solution)/shard_map/ppermute | solution.py:106
  9.4 1.6 %copy-start.2 = (bf16[512,2048]{1,0:T(8,128)(2,1)S(1)}, bf16[512,2048]{1,0:T(8,128)(2,1)}, u32[]{:S(2)}) copy-start(bf16[512,2048]{1,0:T(8,128)(2,1)} %query_ref.1) | copy-start | bytes 6291460
  11.0 1.6 %copy-start.3 = (bf16[4,512,512]{2,1,0:T(8,128)(2,1)S(1)}, bf16[4,512,512]{2,1,0:T(8,128)(2,1)}, u32[]{:S(2)}) copy-start(bf16[4,512,512]{2,1,0:T(8,128)(2,1)} %basis_ref.1) | copy-start | bytes 6291460
  12.6 0.7 copy-start.4
  13.3 3.7 %copy-start = (bf16[128,2048]{1,0:T(8,128)(2,1)S(1)}, bf16[128,2048]{1,0:T(8,128)(2,1)}, u32[]{:S(2)}) copy-start(bf16[128,2048]{1,0:T(8,128)(2,1)} %documents_ref.1) | copy-start | bytes 1572868
  18.3 0.6 copy-start.1
  18.9 22.8 %collective-permute-start = (bf16[128,128]{1,0:T(8,128)(2,1)S(1)}, bf16[128,128]{1,0:T(8,128)(2,1)S(1)}, u32[]{:S(2)}, u32[]{:S(2)}) collective-permute-start(bf16[128,128]{1,0:T(8,128)(2,1)S(1)} %get-tuple-element.22), channel_id=1, source_target_pairs={{0,1},{1,2},{2,3},{3,0},{4,5},{5,6},{6,7},{7,4},{8,9},{9,10},{10,1... | collective-permute-start | bytes 98312 | tf_op jit(solution)/shard_map/ppermute | solution.py:125
  18.9 37.3 %collective-permute-start.1 = (bf16[128,128]{1,0:T(8,128)(2,1)S(1)}, bf16[128,128]{1,0:T(8,128)(2,1)S(1)}, u32[]{:S(2)}, u32[]{:S(2)}) collective-permute-start(bf16[128,128]{1,0:T(8,128)(2,1)S(1)} %get-tuple-element.23), channel_id=1, source_target_pairs={{0,2},{1,3},{2,0},{3,1},{4,6},{5,7},{6,4},{7,5},{8,10},{9,11},{10,... | collective-permute-start | bytes 98312 | tf_op jit(solution)/shard_map/ppermute | solution.py:125
  40.0 16.3 %collective-permute-start.2 = (bf16[128,128]{1,0:T(8,128)(2,1)S(1)}, bf16[128,128]{1,0:T(8,128)(2,1)S(1)}, u32[]{:S(2)}, u32[]{:S(2)}) collective-permute-start(bf16[128,128]{1,0:T(8,128)(2,1)S(1)} %get-tuple-element.24), channel_id=1, source_target_pairs={{0,3},{1,0},{2,1},{3,2},{4,7},{5,4},{6,5},{7,6},{8,11},{9,8},{10,9... | collective-permute-start | bytes 98312 | tf_op jit(solution)/shard_map/ppermute | solution.py:125
  41.8 21.2 %copy-start.5 = (bf16[128,128]{1,0:T(8,128)(2,1)}, bf16[128,128]{1,0:T(8,128)(2,1)S(1)}, u32[]{:S(2)}) copy-start(bf16[128,128]{1,0:T(8,128)(2,1)S(1)} %collective-permute-done.refs_1_) | copy-start | bytes 98308
  41.8 18.3 %collective-permute-start.10 = (bf16[128,128]{1,0:T(8,128)(2,1)S(1)}, bf16[128,128]{1,0:T(8,128)(2,1)S(1)}, u32[]{:S(2)}, u32[]{:S(2)}) collective-permute-start(bf16[128,128]{1,0:T(8,128)(2,1)S(1)} %get-tuple-element.30), channel_id=1, source_target_pairs={{0,9},{1,10},{2,11},{3,8},{4,13},{5,14},{6,15},{7,12},{8,1},{9,2},... | collective-permute-start | bytes 98312 | tf_op jit(solution)/shard_map/ppermute | solution.py:125
  41.9 19.0 %collective-permute-start.11 = (bf16[128,128]{1,0:T(8,128)(2,1)S(1)}, bf16[128,128]{1,0:T(8,128)(2,1)S(1)}, u32[]{:S(2)}, u32[]{:S(2)}) collective-permute-start(bf16[128,128]{1,0:T(8,128)(2,1)S(1)} %get-tuple-element.31), channel_id=1, source_target_pairs={{0,10},{1,11},{2,8},{3,9},{4,14},{5,15},{6,12},{7,13},{8,2},{9,3},... | collective-permute-start | bytes 98312 | tf_op jit(solution)/shard_map/ppermute | solution.py:125
  56.2 17.9 %copy-start.6 = (bf16[128,128]{1,0:T(8,128)(2,1)}, bf16[128,128]{1,0:T(8,128)(2,1)S(1)}, u32[]{:S(2)}) copy-start(bf16[128,128]{1,0:T(8,128)(2,1)S(1)} %collective-permute-done.1.refs_2_) | copy-start | bytes 98308
  56.2 6.8 %collective-permute-start.12 = (bf16[128,128]{1,0:T(8,128)(2,1)S(1)}, bf16[128,128]{1,0:T(8,128)(2,1)S(1)}, u32[]{:S(2)}, u32[]{:S(2)}) collective-permute-start(bf16[128,128]{1,0:T(8,128)(2,1)S(1)} %get-tuple-element.32), channel_id=1, source_target_pairs={{0,11},{1,8},{2,9},{3,10},{4,15},{5,12},{6,13},{7,14},{8,3},{9,0},... | collective-permute-start | bytes 98312 | tf_op jit(solution)/shard_map/ppermute | solution.py:125
  56.3 17.8 %copy-start.7 = (bf16[128,128]{1,0:T(8,128)(2,1)}, bf16[128,128]{1,0:T(8,128)(2,1)S(1)}, u32[]{:S(2)}) copy-start(bf16[128,128]{1,0:T(8,128)(2,1)S(1)} %collective-permute-done.2.refs_3_) | copy-start | bytes 98308
  56.3 8.4 %collective-permute-start.14 = (bf16[128,128]{1,0:T(8,128)(2,1)S(1)}, bf16[128,128]{1,0:T(8,128)(2,1)S(1)}, u32[]{:S(2)}, u32[]{:S(2)}) collective-permute-start(bf16[128,128]{1,0:T(8,128)(2,1)S(1)} %get-tuple-element.33), channel_id=1, source_target_pairs={{0,12},{1,13},{2,14},{3,15},{4,0},{5,1},{6,2},{7,3},{8,4},{9,5},{1... | collective-permute-start | bytes 98312 | tf_op jit(solution)/shard_map/ppermute | solution.py:125
  56.8 8.2 %collective-permute-start.15 = (bf16[128,128]{1,0:T(8,128)(2,1)S(1)}, bf16[128,128]{1,0:T(8,128)(2,1)S(1)}, u32[]{:S(2)}, u32[]{:S(2)}) collective-permute-start(bf16[128,128]{1,0:T(8,128)(2,1)S(1)} %get-tuple-element.34), channel_id=1, source_target_pairs={{0,13},{1,14},{2,15},{3,12},{4,1},{5,2},{6,3},{7,0},{8,5},{9,6},{1... | collective-permute-start | bytes 98312 | tf_op jit(solution)/shard_map/ppermute | solution.py:125
  60.1 14.0 %copy-start.8 = (bf16[128,128]{1,0:T(8,128)(2,1)}, bf16[128,128]{1,0:T(8,128)(2,1)S(1)}, u32[]{:S(2)}) copy-start(bf16[128,128]{1,0:T(8,128)(2,1)S(1)} %collective-permute-done.10.refs_9_) | copy-start | bytes 98308
  60.1 6.6 %collective-permute-start.16 = (bf16[128,128]{1,0:T(8,128)(2,1)S(1)}, bf16[128,128]{1,0:T(8,128)(2,1)S(1)}, u32[]{:S(2)}, u32[]{:S(2)}) collective-permute-start(bf16[128,128]{1,0:T(8,128)(2,1)S(1)} %get-tuple-element.35), channel_id=1, source_target_pairs={{0,14},{1,15},{2,12},{3,13},{4,2},{5,3},{6,0},{7,1},{8,6},{9,7},{1... | collective-permute-start | bytes 98312 | tf_op jit(solution)/shard_map/ppermute | solution.py:125
  60.9 13.3 %copy-start.9 = (bf16[128,128]{1,0:T(8,128)(2,1)}, bf16[128,128]{1,0:T(8,128)(2,1)S(1)}, u32[]{:S(2)}) copy-start(bf16[128,128]{1,0:T(8,128)(2,1)S(1)} %collective-permute-done.11.refs_10_) | copy-start | bytes 98308
  60.9 8.4 %collective-permute-start.17 = (bf16[128,128]{1,0:T(8,128)(2,1)S(1)}, bf16[128,128]{1,0:T(8,128)(2,1)S(1)}, u32[]{:S(2)}, u32[]{:S(2)}) collective-permute-start(bf16[128,128]{1,0:T(8,128)(2,1)S(1)} %get-tuple-element.36), channel_id=1, source_target_pairs={{0,15},{1,12},{2,13},{3,14},{4,3},{5,0},{6,1},{7,2},{8,7},{9,4},{1... | collective-permute-start | bytes 98312 | tf_op jit(solution)/shard_map/ppermute | solution.py:125
  63.0 11.2 %copy-start.10 = (bf16[128,128]{1,0:T(8,128)(2,1)}, bf16[128,128]{1,0:T(8,128)(2,1)S(1)}, u32[]{:S(2)}) copy-start(bf16[128,128]{1,0:T(8,128)(2,1)S(1)} %collective-permute-done.12.refs_11_) | copy-start | bytes 98308
  63.0 8.4 %collective-permute-start.4 = (bf16[128,128]{1,0:T(8,128)(2,1)S(1)}, bf16[128,128]{1,0:T(8,128)(2,1)S(1)}, u32[]{:S(2)}, u32[]{:S(2)}) collective-permute-start(bf16[128,128]{1,0:T(8,128)(2,1)S(1)} %get-tuple-element.25), channel_id=1, source_target_pairs={{0,4},{1,5},{2,6},{3,7},{4,8},{5,9},{6,10},{7,11},{8,12},{9,13},{1... | collective-permute-start | bytes 98312 | tf_op jit(solution)/shard_map/ppermute | solution.py:125
  64.7 9.5 %copy-start.11 = (bf16[128,128]{1,0:T(8,128)(2,1)}, bf16[128,128]{1,0:T(8,128)(2,1)S(1)}, u32[]{:S(2)}) copy-start(bf16[128,128]{1,0:T(8,128)(2,1)S(1)} %collective-permute-done.14.refs_12_) | copy-start | bytes 98308
  64.7 6.7 %collective-permute-start.5 = (bf16[128,128]{1,0:T(8,128)(2,1)S(1)}, bf16[128,128]{1,0:T(8,128)(2,1)S(1)}, u32[]{:S(2)}, u32[]{:S(2)}) collective-permute-start(bf16[128,128]{1,0:T(8,128)(2,1)S(1)} %get-tuple-element.26), channel_id=1, source_target_pairs={{0,5},{1,6},{2,7},{3,4},{4,9},{5,10},{6,11},{7,8},{8,13},{9,14},{1... | collective-permute-start | bytes 98312 | tf_op jit(solution)/shard_map/ppermute | solution.py:125
  65.0 9.2 %copy-start.12 = (bf16[128,128]{1,0:T(8,128)(2,1)}, bf16[128,128]{1,0:T(8,128)(2,1)S(1)}, u32[]{:S(2)}) copy-start(bf16[128,128]{1,0:T(8,128)(2,1)S(1)} %collective-permute-done.15.refs_13_) | copy-start | bytes 98308
  65.0 6.6 %collective-permute-start.6 = (bf16[128,128]{1,0:T(8,128)(2,1)S(1)}, bf16[128,128]{1,0:T(8,128)(2,1)S(1)}, u32[]{:S(2)}, u32[]{:S(2)}) collective-permute-start(bf16[128,128]{1,0:T(8,128)(2,1)S(1)} %get-tuple-element.27), channel_id=1, source_target_pairs={{0,6},{1,7},{2,4},{3,5},{4,10},{5,11},{6,8},{7,9},{8,14},{9,15},{1... | collective-permute-start | bytes 98312 | tf_op jit(solution)/shard_map/ppermute | solution.py:125
  66.7 7.5 %copy-start.13 = (bf16[128,128]{1,0:T(8,128)(2,1)}, bf16[128,128]{1,0:T(8,128)(2,1)S(1)}, u32[]{:S(2)}) copy-start(bf16[128,128]{1,0:T(8,128)(2,1)S(1)} %collective-permute-done.16.refs_14_) | copy-start | bytes 98308
  66.7 6.2 %collective-permute-start.7 = (bf16[128,128]{1,0:T(8,128)(2,1)S(1)}, bf16[128,128]{1,0:T(8,128)(2,1)S(1)}, u32[]{:S(2)}, u32[]{:S(2)}) collective-permute-start(bf16[128,128]{1,0:T(8,128)(2,1)S(1)} %get-tuple-element.28), channel_id=1, source_target_pairs={{0,7},{1,4},{2,5},{3,6},{4,11},{5,8},{6,9},{7,10},{8,15},{9,12},{1... | collective-permute-start | bytes 98312 | tf_op jit(solution)/shard_map/ppermute | solution.py:125
  69.3 4.8 %copy-start.14 = (bf16[128,128]{1,0:T(8,128)(2,1)}, bf16[128,128]{1,0:T(8,128)(2,1)S(1)}, u32[]{:S(2)}) copy-start(bf16[128,128]{1,0:T(8,128)(2,1)S(1)} %collective-permute-done.17.refs_15_) | copy-start | bytes 98308
  69.3 4.8 %collective-permute-start.9 = (bf16[128,128]{1,0:T(8,128)(2,1)S(1)}, bf16[128,128]{1,0:T(8,128)(2,1)S(1)}, u32[]{:S(2)}, u32[]{:S(2)}) collective-permute-start(bf16[128,128]{1,0:T(8,128)(2,1)S(1)} %get-tuple-element.29), channel_id=1, source_target_pairs={{0,8},{1,9},{2,10},{3,11},{4,12},{5,13},{6,14},{7,15},{8,0},{9,1},... | collective-permute-start | bytes 98312 | tf_op jit(solution)/shard_map/ppermute | solution.py:125
  71.4 2.8 %copy-start.15 = (bf16[128,128]{1,0:T(8,128)(2,1)}, bf16[128,128]{1,0:T(8,128)(2,1)S(1)}, u32[]{:S(2)}) copy-start(bf16[128,128]{1,0:T(8,128)(2,1)S(1)} %collective-permute-done.4.refs_4_) | copy-start | bytes 98308
  71.4 2.8 %copy-start.16 = (bf16[128,128]{1,0:T(8,128)(2,1)}, bf16[128,128]{1,0:T(8,128)(2,1)S(1)}, u32[]{:S(2)}) copy-start(bf16[128,128]{1,0:T(8,128)(2,1)S(1)} %collective-permute-done.5.refs_5_) | copy-start | bytes 98308
  71.7 2.6 %copy-start.17 = (bf16[128,128]{1,0:T(8,128)(2,1)}, bf16[128,128]{1,0:T(8,128)(2,1)S(1)}, u32[]{:S(2)}) copy-start(bf16[128,128]{1,0:T(8,128)(2,1)S(1)} %collective-permute-done.6.refs_6_) | copy-start | bytes 98308
  72.9 1.4 %copy-start.18 = (bf16[128,128]{1,0:T(8,128)(2,1)}, bf16[128,128]{1,0:T(8,128)(2,1)S(1)}, u32[]{:S(2)}) copy-start(bf16[128,128]{1,0:T(8,128)(2,1)S(1)} %collective-permute-done.7.refs_7_) | copy-start | bytes 98308
  74.2 0.6 copy-start.19

commit v2 on v1

v2 whole, which is shorter than its diff:
```python
import functools

import jax
import jax.numpy as jnp
from jax import lax
from jax.experimental import pallas as pl
from jax.experimental.pallas import tpu as pltpu
from jax.sharding import PartitionSpec as P

LDIM = 512
LAY_DEV = 4
STEPS = 4
DAMPING = 0.05
NT = (((1,), (1,)), ((), ()))
VMEM_LIMIT = 40 * 1024 * 1024


def precondition_kernel(slots, query_ref, basis_ref, values_ref, out_ref):
    layer = pl.program_id(0)
    basis = basis_ref[0]
    projected = jnp.dot(query_ref[...], basis, preferred_element_type=jnp.float32)
    scaled = (projected / (values_ref[pl.ds(layer, 1), :] + DAMPING)).astype(jnp.bfloat16)
    out_ref[...] = lax.dot_general(scaled, basis, NT, preferred_element_type=jnp.float32).astype(jnp.bfloat16)


def precondition(query_grads, eigenbases, eigenvalues, slots):
    rows = query_grads.shape[0]
    return pl.pallas_call(
        precondition_kernel,
        out_shape=jax.ShapeDtypeStruct((rows, LAY_DEV * LDIM), jnp.bfloat16),
        grid_spec=pltpu.PrefetchScalarGridSpec(
            num_scalar_prefetch=1,
            grid=(LAY_DEV,),
            in_specs=[
                pl.BlockSpec((rows, LDIM), lambda layer, slots: (0, layer)),
                pl.BlockSpec((1, LDIM, LDIM), lambda layer, slots: (layer, 0, 0)),
                pl.BlockSpec((LAY_DEV, LDIM), lambda layer, slots: (0, 0)),
            ],
            out_specs=pl.BlockSpec((rows, LDIM), lambda layer, slots: (0, slots[layer])),
        ),
        compiler_params=pltpu.CompilerParams(vmem_limit_bytes=VMEM_LIMIT),
        cost_estimate=pl.CostEstimate(
            flops=4 * rows * LAY_DEV * LDIM * LDIM, bytes_accessed=6 * 1024 * 1024, transcendentals=0
        ),
    )(slots, query_grads, eigenbases, eigenvalues)


def score_kernel(shares, row, queries_ref, documents_ref, ids_ref, out_ref):
    tile = lax.dot_general(queries_ref[...], documents_ref[...], NT, preferred_element_type=jnp.float32)
    doc_rows = out_ref.shape[3]
    share_rows = out_ref.shape[2]
    doc_ids = row[0] + lax.broadcasted_iota(jnp.int32, tile.shape, 1)
    tile = jnp.where(ids_ref[...] == doc_ids, 0.0, tile).astype(jnp.bfloat16)
    for owner in range(out_ref.shape[0]):
        for share in range(shares):
            out_ref[owner, share] = tile[
                share * share_rows : (share + 1) * share_rows, owner * doc_rows : (owner + 1) * doc_rows
            ]


def partial_scores(conditioned, documents, query_ids, first_doc, doc_rows, shares):
    rows, dims = conditioned.shape
    docs = documents.shape[0]
    vmem = pl.BlockSpec(memory_space=pltpu.VMEM)
    return pl.pallas_call(
        functools.partial(score_kernel, shares),
        out_shape=jax.ShapeDtypeStruct((docs // doc_rows, shares, rows // shares, doc_rows), jnp.bfloat16),
        in_specs=[pl.BlockSpec(memory_space=pltpu.SMEM), vmem, vmem, vmem],
        out_specs=vmem,
        compiler_params=pltpu.CompilerParams(vmem_limit_bytes=VMEM_LIMIT),
        cost_estimate=pl.CostEstimate(
            flops=2 * rows * docs * dims, bytes_accessed=2 * dims * (rows + docs), transcendentals=0
        ),
    )(first_doc, conditioned, documents, query_ids)


def sum_kernel(row, in_ref, out_ref):
    steps, shares = in_ref.shape[:2]
    for step in range(steps):
        source = lax.rem(row[0] - step + steps, steps)
        total = in_ref[source, 0].astype(jnp.float32)
        for share in range(1, shares):
            total += in_ref[source, share].astype(jnp.float32)
        out_ref[step] = total


def sum_shares(blocks, row):
    vmem = pl.BlockSpec(memory_space=pltpu.VMEM)
    return pl.pallas_call(
        sum_kernel,
        out_shape=jax.ShapeDtypeStruct(blocks.shape[:1] + blocks.shape[2:], jnp.float32),
        in_specs=[pl.BlockSpec(memory_space=pltpu.SMEM), vmem],
        out_specs=vmem,
    )(row, blocks)


def local(train_grads, query_grads, eigenbases, eigenvalues, layer_offsets, query_doc_ids):
    n_rows = lax.axis_size("rows")
    shares = lax.axis_size("layer")
    row = lax.axis_index("rows").astype(jnp.int32)
    layer_index = lax.axis_index("layer")
    doc_rows = train_grads.shape[0]
    query_ids = query_doc_ids[:, None]
    slots = layer_offsets // LDIM - layer_index * LAY_DEV

    if n_rows == STEPS:
        documents = lax.all_gather(train_grads, "rows", tiled=True)
        conditioned = precondition(query_grads, eigenbases, eigenvalues, slots)
        tiles = partial_scores(conditioned, documents, query_ids, jnp.zeros((1,), jnp.int32), doc_rows, shares)
        blocks = tiles.reshape((n_rows * shares,) + tiles.shape[2:])
        blocks = lax.all_to_all(blocks, ("rows", "layer"), 0, 0, tiled=True)
        return sum_shares(blocks.reshape(tiles.shape), row[None])

    conditioned = precondition(query_grads, eigenbases, eigenvalues, slots)
    blocks = []
    for step in range(STEPS):
        back = [(source, (source - step) % n_rows) for source in range(n_rows)]
        documents = lax.ppermute(train_grads, "rows", back) if step else train_grads
        first_doc = (row + step) % n_rows * doc_rows
        tiles = partial_scores(conditioned, documents, query_ids, first_doc[None], doc_rows, shares)
        shared = lax.all_to_all(tiles[0], "layer", 0, 0, tiled=True)
        onward = [(source, (source + step) % n_rows) for source in range(n_rows)]
        blocks.append(lax.ppermute(shared, "rows", onward) if step else shared)
    return jnp.sum(jnp.stack(blocks).astype(jnp.float32), axis=1)


def solution(mesh):
    in_specs = (
        P(("group", "rows"), "layer"),
        P(("group", "rows"), "layer"),
        P("layer", None, None),
        P("layer", None),
        P("layer"),
        P(("group", "rows")),
    )
    out_specs = P(None, "layer", ("group", "rows"))
    return jax.shard_map(local, mesh=mesh, in_specs=in_specs, out_specs=out_specs, check_vma=False)
```

time: 76.9 us -> 89.2 us (1.16)
  waiting for transfers between devices: 22.2 us -> 56.4 us
  starting transfers between devices: 35.6 us -> 3.57 us
  between operations: 0.29 us -> 13.4 us
  Pallas kernels: 11.6 us -> 7.6 us
  local copies, waits for them, and re-layouts: 5.84 us -> 7.09 us
    all_gather x0 -> x1, waiting for transfers between devices: none -> 41.2 us  [local(): documents = lax.all_gather(train_grads, 'rows', tiled=True)]
    ppermute x18 -> x0, starting transfers between devices: 35.6 us -> none  [the longest x15 27.8 us: local(): tile = lax.ppermute(tile, ('rows', 'layer'), pairs)]
    ppermute x18 -> x0, waiting for transfers between devices: 22.2 us -> none  [the longest x3 19.4 us: local(): documents.append(lax.ppermute(train_grads, 'rows', pairs))]
    all_to_all x0 -> x1, waiting for transfers between devices: none -> 14.4 us  [local(): blocks = lax.all_to_all(blocks, ('rows', 'layer'), 0, 0, tiled=True)]
    pallas_call x5 -> x2, Pallas kernels: 7.89 us -> 3.89 us  [the longest x1 2.08 us: partial_scores(): pl.pallas_call(functools.partial(score_kernel, shares), out_shape=jax.Sha...]
    all_to_all x0 -> x1, starting transfers between devices: none -> 3.57 us  [local(): blocks = lax.all_to_all(blocks, ('rows', 'layer'), 0, 0, tiled=True)]
    unnamed x40 -> x10, local copies, waits for them, and re-layouts: 5.02 us -> 6.27 us
  transfers between devices with their start and end apart: 18 -> 2, of which waited for: 4 -> 2; matrix products, arithmetic and copies ran while one was open for 2% -> 2% of each run, Pallas kernels for 13% -> 4%
where the time goes in v2:
time: 89.2 us; the launch traced here: 88.7 us
  waiting for transfers between devices  56.4 us (63%)
  between operations  13.4 us (15%)
  Pallas kernels  7.6 us (9%)
  local copies, waits for them, and re-layouts  7.09 us (8%)
  starting transfers between devices  3.57 us (4%)
    all_gather x1, waiting for transfers between devices, local(): documents = lax.all_gather(train_grads, 'rows', tiled=True)  41.2 us
    all_to_all x1, waiting for transfers between devices, local(): blocks = lax.all_to_all(blocks, ('rows', 'layer'), 0, 0, tiled=True)  14.4 us
    unnamed x10, local copies, waits for them, and re-layouts  6.27 us
    pallas_call x1, Pallas kernels, precondition(): pl.pallas_call(precondition_kernel, out_shape=jax.ShapeDtypeStruct((rows,...  3.72 us
    all_to_all x1, starting transfers between devices, local(): blocks = lax.all_to_all(blocks, ('rows', 'layer'), 0, 0, tiled=True)  3.57 us
    pallas_call x1, Pallas kernels, partial_scores(): pl.pallas_call(functools.partial(score_kernel, shares), out_shape=jax.Sha...  2.08 us
    pallas_call x1, Pallas kernels, sum_shares(): pl.pallas_call(sum_kernel, out_shape=jax.ShapeDtypeStruct(blocks.shape[:1...  1.81 us
  transfers between devices with their start and end apart: 2, of which 2 were waited for; matrix products, arithmetic and copies ran while one was open for 2% of the time, Pallas kernels for 4%

profile of v2, /device:TPU:0, one launch (start us, length us, event | category | flops | bytes accessed | tf_op | source)
XLA Modules:
  0.0 88.7 jit_solution(1715742221091331273)
XLA Ops:
  6.5 0.0 all-gather.2.cloned.1.call-start
  6.5 0.7 all-gather.2.cloned.1.call-update
  7.3 0.8 copy.7.ids_ref
  8.1 0.7 fusion.slots
  8.8 0.0 copy-start.1
  8.8 1.6 %copy-done.1 = bf16[512,2048]{1,0:T(8,128)(2,1)S(1)} copy-done((bf16[512,2048]{1,0:T(8,128)(2,1)S(1)}, bf16[512,2048]{1,0:T(8,128)(2,1)}, u32[]{:S(2)}) %copy-start.1) | copy-done | bytes 2097176
  10.4 0.0 copy-start.2
  10.4 1.6 %copy-done.2 = bf16[4,512,512]{2,1,0:T(8,128)(2,1)S(1)} copy-done((bf16[4,512,512]{2,1,0:T(8,128)(2,1)S(1)}, bf16[4,512,512]{2,1,0:T(8,128)(2,1)}, u32[]{:S(2)}) %copy-start.2) | copy-done | bytes 2097176
  11.9 0.0 copy-start.3
  11.9 0.7 copy-done.3
  12.6 3.7 %shard_map.64.queries_ref = bf16[512,2048]{1,0:T(8,128)(2,1)S(1)} custom-call(s32[4]{0:T(128)S(1)} %fusion.slots, bf16[512,2048]{1,0:T(8,128)(2,1)S(1)} %copy-done.1, bf16[4,512,512]{2,1,0:T(8,128)(2,1)S(1)} %copy-done.2, f32[4,512]{1,0:T(4,128)S(1)} %copy-done.3), custom_call_target="tpu_custom_call" | custom-call | flops 2147483648 | bytes 6291456 | tf_op jit(solution)/shard_map/pallas_call | solution.py:28
  16.4 41.2 %all-gather.2.cloned.1.call-done.documents_ref = bf16[512,2048]{1,0:T(8,128)(2,1)} async-done(((bf16[128,2048]{1,0:T(8,128)(2,1)}), bf16[512,2048]{1,0:T(8,128)(2,1)}) %all-gather.2.cloned.1.call-update) | async-done | bytes 2097168 | tf_op jit(solution)/shard_map/all_gather | solution.py:107
  57.6 0.0 copy-start
  57.6 1.6 %copy-done = bf16[512,2048]{1,0:T(8,128)(2,1)S(1)} copy-done((bf16[512,2048]{1,0:T(8,128)(2,1)S(1)}, bf16[512,2048]{1,0:T(8,128)(2,1)}, u32[]{:S(2)}) %copy-start) | copy-done | bytes 2097176
  59.2 2.1 %shard_map.65 = bf16[4,4,128,128]{3,2,1,0:T(8,128)(2,1)} custom-call(s32[1]{0:T(128)} %constant.20.clone.1.row, bf16[512,2048]{1,0:T(8,128)(2,1)S(1)} %shard_map.64.queries_ref, bf16[512,2048]{1,0:T(8,128)(2,1)S(1)} %copy-done, s32[512,1]{1,0:T(8,128)S(1)} %copy.7.ids_ref), custom_call_target="tpu_custom_call" | custom-call | flops 1073741824 | bytes 4194304 | tf_op jit(solution)/shard_map/pallas_call | solution.py:65
  61.3 3.6 %all-to-all-start = ((bf16[16,128,128]{2,1,0:T(8,128)(2,1)}), bf16[16,128,128]{2,1,0:T(8,128)(2,1)S(1)}, u32[]{:S(2)}, u32[]{:S(2)}) async-start(bf16[16,128,128]{2,1,0:T(8,128)(2,1)} %bitcast.2), calls=%async_computation | async-start | bytes 1048576 | tf_op jit(solution)/shard_map/all_to_all | solution.py:111
  64.9 14.4 %all-to-all-done = bf16[16,128,128]{2,1,0:T(8,128)(2,1)S(1)} async-done(((bf16[16,128,128]{2,1,0:T(8,128)(2,1)}), bf16[16,128,128]{2,1,0:T(8,128)(2,1)S(1)}, u32[]{:S(2)}, u32[]{:S(2)}) %all-to-all-start) | async-done | bytes 524320 | tf_op jit(solution)/shard_map/all_to_all | solution.py:111
  79.3 0.0 copy-start.4
  79.3 0.8 copy-done.4
  80.1 1.8 %shard_map.66 = f32[4,128,128]{2,1,0:T(8,128)} custom-call(s32[1]{0:T(128)} %bitcast.row, bf16[4,4,128,128]{3,2,1,0:T(8,128)(2,1)} %bitcast.4), custom_call_target="tpu_custom_call" | custom-call | tf_op jit(solution)/shard_map/pallas_call | solution.py:89
Async XLA Ops:
  6.5 51.1 %all-gather.2.cloned.1.call-start = ((), (), s32[]{:S(2)}) async-start(), calls=%async_computation.1 | async-start | bytes 2621440 | tf_op jit(solution)/shard_map/all_gather | solution.py:107
  8.8 1.6 %copy-start.1 = (bf16[512,2048]{1,0:T(8,128)(2,1)S(1)}, bf16[512,2048]{1,0:T(8,128)(2,1)}, u32[]{:S(2)}) copy-start(bf16[512,2048]{1,0:T(8,128)(2,1)} %query_ref.1) | copy-start | bytes 6291460
  10.4 1.6 %copy-start.2 = (bf16[4,512,512]{2,1,0:T(8,128)(2,1)S(1)}, bf16[4,512,512]{2,1,0:T(8,128)(2,1)}, u32[]{:S(2)}) copy-start(bf16[4,512,512]{2,1,0:T(8,128)(2,1)} %basis_ref.1) | copy-start | bytes 6291460
  11.9 0.7 copy-start.3
  57.6 1.6 %copy-start = (bf16[512,2048]{1,0:T(8,128)(2,1)S(1)}, bf16[512,2048]{1,0:T(8,128)(2,1)}, u32[]{:S(2)}) copy-start(bf16[512,2048]{1,0:T(8,128)(2,1)} %all-gather.2.cloned.1.call-done.documents_ref) | copy-start | bytes 6291460
  61.3 18.0 %all-to-all-start = ((bf16[16,128,128]{2,1,0:T(8,128)(2,1)}), bf16[16,128,128]{2,1,0:T(8,128)(2,1)S(1)}, u32[]{:S(2)}, u32[]{:S(2)}) async-start(bf16[16,128,128]{2,1,0:T(8,128)(2,1)} %bitcast.2), calls=%async_computation | async-start | bytes 1048576 | tf_op jit(solution)/shard_map/all_to_all | solution.py:111
  79.3 0.8 copy-start.4
Sparse Core Ops, SparseCore 0:
  8.9 48.6 all-gather.1

commit v3 on v2

v3 whole, which is shorter than its diff:
```python
import functools

import jax
import jax.numpy as jnp
from jax import lax
from jax.experimental import pallas as pl
from jax.experimental.pallas import tpu as pltpu
from jax.sharding import PartitionSpec as P

LDIM = 512
LAY_DEV = 4
STEPS = 4
DAMPING = 0.05
NT = (((1,), (1,)), ((), ()))
VMEM_LIMIT = 40 * 1024 * 1024


def precondition_kernel(slots, query_ref, basis_ref, values_ref, out_ref):
    layer = pl.program_id(0)
    basis = basis_ref[0]
    projected = jnp.dot(query_ref[...], basis, preferred_element_type=jnp.float32)
    scaled = (projected / (values_ref[pl.ds(layer, 1), :] + DAMPING)).astype(jnp.bfloat16)
    out_ref[...] = lax.dot_general(scaled, basis, NT, preferred_element_type=jnp.float32).astype(jnp.bfloat16)


def precondition(query_grads, eigenbases, eigenvalues, slots):
    rows = query_grads.shape[0]
    return pl.pallas_call(
        precondition_kernel,
        out_shape=jax.ShapeDtypeStruct((rows, LAY_DEV * LDIM), jnp.bfloat16),
        grid_spec=pltpu.PrefetchScalarGridSpec(
            num_scalar_prefetch=1,
            grid=(LAY_DEV,),
            in_specs=[
                pl.BlockSpec((rows, LDIM), lambda layer, slots: (0, layer)),
                pl.BlockSpec((1, LDIM, LDIM), lambda layer, slots: (layer, 0, 0)),
                pl.BlockSpec((LAY_DEV, LDIM), lambda layer, slots: (0, 0)),
            ],
            out_specs=pl.BlockSpec((rows, LDIM), lambda layer, slots: (0, slots[layer])),
        ),
        compiler_params=pltpu.CompilerParams(vmem_limit_bytes=VMEM_LIMIT),
        cost_estimate=pl.CostEstimate(
            flops=4 * rows * LAY_DEV * LDIM * LDIM, bytes_accessed=6 * 1024 * 1024, transcendentals=0
        ),
    )(slots, query_grads, eigenbases, eigenvalues)


def score_kernel(shares, turned, place, queries_ref, ids_ref, *refs):
    if turned:
        document_refs, out_refs, held = refs[: -1 - shares], refs[-1 - shares : -1], refs[-1]
    else:
        document_refs, out_refs = refs[:-1], refs[-1:]
    doc_rows = document_refs[0].shape[0]
    for spot, document_ref in enumerate(document_refs):
        tile = lax.dot_general(queries_ref[...], document_ref[...], NT, preferred_element_type=jnp.float32)
        doc_ids = place[1 + spot] + lax.broadcasted_iota(jnp.int32, tile.shape, 1)
        tile = jnp.where(ids_ref[...] == doc_ids, 0.0, tile)
        share_rows = tile.shape[0] // shares
        if turned:
            held[...] = tile
            for turn in range(shares):
                first = pl.multiple_of(lax.rem(place[0] + turn, shares) * share_rows, share_rows)
                out_refs[turn][...] = held[pl.ds(first, share_rows), :].astype(jnp.bfloat16)
        else:
            columns = slice(spot * doc_rows, (spot + 1) * doc_rows)
            for share in range(shares):
                part = tile[share * share_rows : (share + 1) * share_rows]
                out_refs[0][share, :, columns] = part.astype(jnp.bfloat16)


def partial_scores(conditioned, query_ids, documents, place, shares, turned=False):
    rows, dims = conditioned.shape
    doc_rows = documents[0].shape[0]
    docs = doc_rows * len(documents)
    vmem = pl.BlockSpec(memory_space=pltpu.VMEM)
    if turned:
        out_shape = [jax.ShapeDtypeStruct((rows // shares, docs), jnp.bfloat16)] * shares
        scratch = [pltpu.VMEM((rows, docs), jnp.float32)]
    else:
        out_shape = jax.ShapeDtypeStruct((shares, rows // shares, docs), jnp.bfloat16)
        scratch = []
    return pl.pallas_call(
        functools.partial(score_kernel, shares, turned),
        out_shape=out_shape,
        in_specs=[pl.BlockSpec(memory_space=pltpu.SMEM)] + [vmem] * (2 + len(documents)),
        out_specs=[vmem] * shares if turned else vmem,
        scratch_shapes=scratch,
        compiler_params=pltpu.CompilerParams(vmem_limit_bytes=VMEM_LIMIT),
        cost_estimate=pl.CostEstimate(
            flops=2 * rows * docs * dims, bytes_accessed=2 * dims * (rows + docs), transcendentals=0
        ),
    )(place, conditioned, query_ids, *documents)


def sum_kernel(in_ref, *out_refs):
    doc_rows = out_refs[0].shape[1]
    for spot, out_ref in enumerate(out_refs):
        columns = slice(spot * doc_rows, (spot + 1) * doc_rows)
        total = in_ref[0, :, columns].astype(jnp.float32)
        for share in range(1, in_ref.shape[0]):
            total += in_ref[share, :, columns].astype(jnp.float32)
        out_ref[...] = total


def sum_shares(tiles, doc_rows):
    tiles = lax.all_to_all(tiles, "layer", 0, 0, tiled=True)
    shares, share_rows, docs = tiles.shape
    vmem = pl.BlockSpec(memory_space=pltpu.VMEM)
    return pl.pallas_call(
        sum_kernel,
        out_shape=[jax.ShapeDtypeStruct((share_rows, doc_rows), jnp.float32)] * (docs // doc_rows),
        in_specs=[vmem],
        out_specs=[vmem] * (docs // doc_rows),
    )(tiles)


def final_kernel(row, own_ref, ahead_ref, behind_ref, across_ref, *refs):
    *last_refs, out_ref = refs
    last = last_refs[0][...].astype(jnp.float32)
    for last_ref in last_refs[1:]:
        last += last_ref[...].astype(jnp.float32)
    out_ref[0] = own_ref[...]
    out_ref[1] = jnp.where(row[0] == 0, last, ahead_ref[...])
    out_ref[2] = across_ref[...]
    out_ref[3] = jnp.where(row[0] == STEPS - 1, last, behind_ref[...])


def final_scores(row, own, ahead, behind, across, last):
    vmem = pl.BlockSpec(memory_space=pltpu.VMEM)
    return pl.pallas_call(
        final_kernel,
        out_shape=jax.ShapeDtypeStruct((STEPS,) + own.shape, jnp.float32),
        in_specs=[pl.BlockSpec(memory_space=pltpu.SMEM)] + [vmem] * (4 + len(last)),
        out_specs=vmem,
    )(row[None], own, ahead, behind, across, *last)


def along_line(documents, conditioned, query_ids, row, layer_index, shares):
    doc_rows = documents.shape[0]

    def hop(value, *pairs):
        return lax.ppermute(value, "rows", pairs)

    def scores(blocks, sources, turned=False):
        place = jnp.stack([layer_index] + [source * doc_rows for source in sources]).astype(jnp.int32)
        return partial_scores(conditioned, query_ids, blocks, place, shares, turned)

    below = hop(documents, (0, 1), (1, 2), (2, 3))
    above = hop(documents, (3, 2), (2, 1), (1, 0))
    below, above, conditioned = lax.optimization_barrier((below, above, conditioned))
    below2 = hop(below, (1, 2), (2, 3))
    above2 = hop(above, (2, 1), (1, 0))

    tiles = scores([documents, below, above], [row, row - 1, row + 1])
    own, lower, upper = sum_shares(tiles, doc_rows)
    behind = hop(lower, (1, 0), (2, 1), (3, 2))
    ahead = hop(upper, (0, 1), (1, 2), (2, 3))

    opposite = below2 + above2
    final = hop(opposite, (2, 3), (1, 0))
    tiles = scores([opposite], [(row + 2) % STEPS])
    (across,) = sum_shares(tiles, doc_rows)
    across = hop(across, (0, 2), (1, 3), (2, 0), (3, 1))

    tiles = scores([final], [STEPS - 1 - row], turned=True)
    last = []
    for turn, tile in enumerate(tiles):
        pairs = [
            (here * shares + lay, there * shares + (lay + turn) % shares)
            for here, there in ((0, 3), (3, 0))
            for lay in range(shares)
        ]
        last.append(lax.ppermute(tile, ("rows", "layer"), pairs))
    return final_scores(row, own, ahead, behind, across, last)


def around_ring(documents, conditioned, query_ids, row, layer_index, shares):
    n_rows = lax.axis_size("rows")
    doc_rows = documents.shape[0]
    result = []
    for step in range(STEPS):
        back = [(source, (source - step) % n_rows) for source in range(n_rows)]
        block = lax.ppermute(documents, "rows", back) if step else documents
        place = jnp.stack([layer_index, (row + step) % n_rows * doc_rows]).astype(jnp.int32)
        (total,) = sum_shares(partial_scores(conditioned, query_ids, [block], place, shares), doc_rows)
        onward = [(source, (source + step) % n_rows) for source in range(n_rows)]
        result.append(lax.ppermute(total, "rows", onward) if step else total)
    return jnp.stack(result)


def local(train_grads, query_grads, eigenbases, eigenvalues, layer_offsets, query_doc_ids):
    row = lax.axis_index("rows").astype(jnp.int32)
    layer_index = lax.axis_index("layer").astype(jnp.int32)
    slots = layer_offsets // LDIM - layer_index * LAY_DEV
    conditioned = precondition(query_grads, eigenbases, eigenvalues, slots)
    plan = along_line if lax.axis_size("rows") == STEPS else around_ring
    return plan(train_grads, conditioned, query_doc_ids[:, None], row, layer_index, lax.axis_size("layer"))


def solution(mesh):
    in_specs = (
        P(("group", "rows"), "layer"),
        P(("group", "rows"), "layer"),
        P("layer", None, None),
        P("layer", None),
        P("layer"),
        P(("group", "rows")),
    )
    out_specs = P(None, "layer", ("group", "rows"))
    return jax.shard_map(local, mesh=mesh, in_specs=in_specs, out_specs=out_specs, check_vma=False)
```

time: 89.2 us -> 99.8 us (1.12)
  the two profiles are of different devices: /device:TPU:0 before, /device:TPU:1 now
where the time goes in v3:
time: 99.8 us; the launch traced here: 98.9 us
  starting transfers between devices  43.9 us (44%)
  waiting for transfers between devices  29.4 us (29%)
  Pallas kernels  15.9 us (16%)
  local copies, waits for them, and re-layouts  7.1 us (7%)
  other arithmetic  2.22 us (2%)
    ppermute x8, waiting for transfers between devices, hop(): return lax.ppermute(value, 'rows', pairs)  19.7 us
    ppermute x8, starting transfers between devices, hop(): return lax.ppermute(value, 'rows', pairs)  17.5 us
    ppermute x4, starting transfers between devices, along_line(): last.append(lax.ppermute(tile, ('rows', 'layer'), pairs))  16 us
    all_to_all x2, starting transfers between devices, sum_shares(): tiles = lax.all_to_all(tiles, 'layer', 0, 0, tiled=True)  10.4 us
    pallas_call x3, Pallas kernels, partial_scores(): pl.pallas_call(functools.partial(score_kernel, shares, turned), out_shape...  7.28 us
    unnamed x32, local copies, waits for them, and re-layouts  6.96 us
    ppermute x4, waiting for transfers between devices, along_line(): last.append(lax.ppermute(tile, ('rows', 'layer'), pairs))  5.15 us
    all_to_all x2, waiting for transfers between devices, sum_shares(): tiles = lax.all_to_all(tiles, 'layer', 0, 0, tiled=True)  4.6 us
  transfers between devices with their start and end apart: 14, of which 6 were waited for; matrix products, arithmetic and copies ran while one was open for 1% of the time, Pallas kernels for 14%

profile of v3, /device:TPU:1, one launch (start us, length us, event | category | flops | bytes accessed | tf_op | source)
XLA Modules:
  0.0 98.9 jit_solution(13883572677761782983)
XLA Ops:
  0.0 4.1 %collective-permute-start = (bf16[128,2048]{1,0:T(8,128)(2,1)}, bf16[128,2048]{1,0:T(8,128)(2,1)S(1)}, u32[]{:S(2)}, u32[]{:S(2)}) collective-permute-start(bf16[128,2048]{1,0:T(8,128)(2,1)} %refs_0_.1), channel_id=1, source_target_pairs={{0,4},{4,8},{8,12},{1,5},{5,9},{9,13},{2,6},{6,10},{10,14},{3,7},{... | collective-permute-start | bytes 1572872 | tf_op jit(solution)/shard_map/ppermute | solution.py:142
  4.1 1.3 %collective-permute-start.1 = (bf16[128,2048]{1,0:T(8,128)(2,1)}, bf16[128,2048]{1,0:T(8,128)(2,1)}, u32[]{:S(2)}, u32[]{:S(2)}) collective-permute-start(bf16[128,2048]{1,0:T(8,128)(2,1)} %refs_0_.1), channel_id=1, source_target_pairs={{12,8},{8,4},{4,0},{13,9},{9,5},{5,1},{14,10},{10,6},{6,2},{15,11}... | collective-permute-start | bytes 1572872 | tf_op jit(solution)/shard_map/ppermute | solution.py:142
  5.4 0.7 fusion.slots
  6.0 1.6 %copy-done.3 = bf16[512,2048]{1,0:T(8,128)(2,1)S(1)} copy-done((bf16[512,2048]{1,0:T(8,128)(2,1)S(1)}, bf16[512,2048]{1,0:T(8,128)(2,1)}, u32[]{:S(2)}) %copy-start.3) | copy-done | bytes 2097176
  7.6 1.6 %copy-done.4 = bf16[4,512,512]{2,1,0:T(8,128)(2,1)S(1)} copy-done((bf16[4,512,512]{2,1,0:T(8,128)(2,1)S(1)}, bf16[4,512,512]{2,1,0:T(8,128)(2,1)}, u32[]{:S(2)}) %copy-start.4) | copy-done | bytes 2097176
  9.2 0.7 copy-done.5
  9.9 3.7 %shard_map.64.queries_ref = bf16[512,2048]{1,0:T(8,128)(2,1)S(1)} custom-call(s32[4]{0:T(128)S(1)} %fusion.slots, bf16[512,2048]{1,0:T(8,128)(2,1)S(1)} %copy-done.3, bf16[4,512,512]{2,1,0:T(8,128)(2,1)S(1)} %copy-done.4, f32[4,512]{1,0:T(4,128)S(1)} %copy-done.5), custom_call_target="tpu_custom_call" | custom-call | flops 2147483648 | bytes 6291456 | tf_op jit(solution)/shard_map/pallas_call | solution.py:28
  13.6 0.0 copy-start
  13.7 1.3 %collective-permute-done.refs_1_ = bf16[128,2048]{1,0:T(8,128)(2,1)S(1)} collective-permute-done((bf16[128,2048]{1,0:T(8,128)(2,1)}, bf16[128,2048]{1,0:T(8,128)(2,1)S(1)}, u32[]{:S(2)}, u32[]{:S(2)}) %collective-permute-start) | collective-permute-done | bytes 524320 | tf_op jit(solution)/shard_map/ppermute | solution.py:142
  14.9 3.8 %collective-permute-done.1.refs_2_ = bf16[128,2048]{1,0:T(8,128)(2,1)} collective-permute-done((bf16[128,2048]{1,0:T(8,128)(2,1)}, bf16[128,2048]{1,0:T(8,128)(2,1)}, u32[]{:S(2)}, u32[]{:S(2)}) %collective-permute-start.1) | collective-permute-done | bytes 524320 | tf_op jit(solution)/shard_map/ppermute | solution.py:142
  18.7 1.5 %collective-permute-start.4 = (bf16[128,2048]{1,0:T(8,128)(2,1)S(1)}, bf16[128,2048]{1,0:T(8,128)(2,1)}, u32[]{:S(2)}, u32[]{:S(2)}) collective-permute-start(bf16[128,2048]{1,0:T(8,128)(2,1)S(1)} %collective-permute-done.refs_1_), channel_id=1, source_target_pairs={{4,8},{8,12},{5,9},{9,13},{6,10},{10,14},{7,11},{11,15},{20,24},{2... | collective-permute-start | bytes 1572872 | tf_op jit(solution)/shard_map/ppermute | solution.py:142
  20.2 0.8 copy-done.1
  21.0 1.3 %collective-permute-start.5 = (bf16[128,2048]{1,0:T(8,128)(2,1)}, bf16[128,2048]{1,0:T(8,128)(2,1)}, u32[]{:S(2)}, u32[]{:S(2)}) collective-permute-start(bf16[128,2048]{1,0:T(8,128)(2,1)} %collective-permute-done.1.refs_2_), channel_id=1, source_target_pairs={{8,4},{4,0},{9,5},{5,1},{10,6},{6,2},{11,7},{7,3},{24,20},{20,16},... | collective-permute-start | bytes 1572872 | tf_op jit(solution)/shard_map/ppermute | solution.py:142
  22.3 0.1 copy.7.ids_ref
  22.5 0.1 pad_add_fusion.place
  22.6 0.0 collective-permute-done.4
  22.6 14.6 %collective-permute-done.5 = bf16[128,2048]{1,0:T(8,128)(2,1)} collective-permute-done((bf16[128,2048]{1,0:T(8,128)(2,1)}, bf16[128,2048]{1,0:T(8,128)(2,1)}, u32[]{:S(2)}, u32[]{:S(2)}) %collective-permute-start.5) | collective-permute-done | bytes 524320 | tf_op jit(solution)/shard_map/ppermute | solution.py:142
  37.1 1.3 %add.18.refs_0_ = bf16[128,2048]{1,0:T(8,128)(2,1)S(1)} add(bf16[128,2048]{1,0:T(8,128)(2,1)} %collective-permute-done.4, bf16[128,2048]{1,0:T(8,128)(2,1)} %collective-permute-done.5) | non-fusion elementwise | flops 262144 | bytes 1572864 | tf_op jit(solution)/shard_map/add | solution.py:159
  38.5 1.3 %collective-permute-start.7 = (bf16[128,2048]{1,0:T(8,128)(2,1)S(1)}, bf16[128,2048]{1,0:T(8,128)(2,1)}, u32[]{:S(2)}, u32[]{:S(2)}) collective-permute-start(bf16[128,2048]{1,0:T(8,128)(2,1)S(1)} %add.18.refs_0_), channel_id=1, source_target_pairs={{8,12},{4,0},{9,13},{5,1},{10,14},{6,2},{11,15},{7,3},{24,28},{20,... | collective-permute-start | bytes 1572872 | tf_op jit(solution)/shard_map/ppermute | solution.py:142
  39.8 1.0 %copy-done.2 = bf16[128,2048]{1,0:T(8,128)(2,1)S(1)} copy-done((bf16[128,2048]{1,0:T(8,128)(2,1)S(1)}, bf16[128,2048]{1,0:T(8,128)(2,1)}, u32[]{:S(2)}) %copy-start.2) | copy-done | bytes 524312
  40.8 3.6 %shard_map.65 = bf16[4,128,384]{2,1,0:T(8,128)(2,1)} custom-call(s32[4]{0:T(128)S(1)} %pad_add_fusion.place, bf16[512,2048]{1,0:T(8,128)(2,1)S(1)} %shard_map.64.queries_ref, s32[512,1]{1,0:T(8,128)S(1)} %copy.7.ids_ref, bf16[128,2048]{1,0:T(8,128)(2,1)S(1)} %copy-done, bf16[128,2048]{1,0:T(8,128)(2,1)S(1)} %copy-done.2, ...), custom_call_target="tpu_custom_call" | custom-call | flops 805306368 | bytes 3670016 | tf_op jit(solution)/shard_map/pallas_call | solution.py:82
  44.4 6.2 %all-to-all-start = ((bf16[4,128,384]{2,1,0:T(8,128)(2,1)}), bf16[4,128,384]{2,1,0:T(8,128)(2,1)S(1)}, u32[]{:S(2)}, u32[]{:S(2)}) async-start(bf16[4,128,384]{2,1,0:T(8,128)(2,1)} %shard_map.65), calls=%async_computation | async-start | bytes 786432 | tf_op jit(solution)/shard_map/all_to_all | solution.py:106
  50.6 0.1 pad_add_fusion.1.place
  50.7 1.9 %shard_map.67 = bf16[4,128,128]{2,1,0:T(8,128)(2,1)} custom-call(s32[2]{0:T(128)S(1)} %pad_add_fusion.1.place, bf16[512,2048]{1,0:T(8,128)(2,1)S(1)} %shard_map.64.queries_ref, s32[512,1]{1,0:T(8,128)S(1)} %copy.7.ids_ref, bf16[128,2048]{1,0:T(8,128)(2,1)S(1)} %add.18.refs_0_), custom_call_target="tpu_custom_call" | custom-call | flops 268435456 | bytes 2621440 | tf_op jit(solution)/shard_map/pallas_call | solution.py:82
  52.6 4.6 %all-to-all-done.in_ref = bf16[4,128,384]{2,1,0:T(8,128)(2,1)S(1)} async-done(((bf16[4,128,384]{2,1,0:T(8,128)(2,1)}), bf16[4,128,384]{2,1,0:T(8,128)(2,1)S(1)}, u32[]{:S(2)}, u32[]{:S(2)}) %all-to-all-start) | async-done | bytes 393248 | tf_op jit(solution)/shard_map/all_to_all | solution.py:106
  57.2 4.2 %all-to-all-start.1 = ((bf16[4,128,128]{2,1,0:T(8,128)(2,1)}), bf16[4,128,128]{2,1,0:T(8,128)(2,1)S(1)}, u32[]{:S(2)}, u32[]{:S(2)}) async-start(bf16[4,128,128]{2,1,0:T(8,128)(2,1)} %shard_map.67), calls=%async_computation.1 | async-start | bytes 262144 | tf_op jit(solution)/shard_map/all_to_all | solution.py:106
  61.4 1.7 %shard_map.66 = (f32[128,128]{1,0:T(8,128)}, f32[128,128]{1,0:T(8,128)}, f32[128,128]{1,0:T(8,128)}) custom-call(bf16[4,128,384]{2,1,0:T(8,128)(2,1)} %copy-done.6), custom_call_target="tpu_custom_call" | custom-call | tf_op jit(solution)/shard_map/pallas_call | solution.py:109
  63.0 5.1 %collective-permute-start.2 = (f32[128,128]{1,0:T(8,128)}, f32[128,128]{1,0:T(8,128)S(1)}, u32[]{:S(2)}, u32[]{:S(2)}) collective-permute-start(f32[128,128]{1,0:T(8,128)} %get-tuple-element.19), channel_id=1, source_target_pairs={{0,4},{4,8},{8,12},{1,5},{5,9},{9,13},{2,6},{6,10},{10,14},{3,7},{... | collective-permute-start | bytes 196616 | tf_op jit(solution)/shard_map/ppermute | solution.py:142
  68.1 1.3 %collective-permute-start.3 = (f32[128,128]{1,0:T(8,128)}, f32[128,128]{1,0:T(8,128)S(1)}, u32[]{:S(2)}, u32[]{:S(2)}) collective-permute-start(f32[128,128]{1,0:T(8,128)} %get-tuple-element.20), channel_id=1, source_target_pairs={{4,0},{8,4},{12,8},{5,1},{9,5},{13,9},{6,2},{10,6},{14,10},{7,3},{... | collective-permute-start | bytes 196616 | tf_op jit(solution)/shard_map/ppermute | solution.py:142
  69.4 0.0 all-to-all-done.1.in_ref
  69.4 0.0 copy-start.7
  69.4 0.6 copy-done.7
  70.1 1.5 %shard_map.68 = f32[128,128]{1,0:T(8,128)} custom-call(bf16[4,128,128]{2,1,0:T(8,128)(2,1)} %copy-done.7), custom_call_target="tpu_custom_call" | custom-call | tf_op jit(solution)/shard_map/pallas_call | solution.py:109
  71.6 1.8 %collective-permute-start.6 = (f32[128,128]{1,0:T(8,128)}, f32[128,128]{1,0:T(8,128)S(1)}, u32[]{:S(2)}, u32[]{:S(2)}) collective-permute-start(f32[128,128]{1,0:T(8,128)} %shard_map.68), channel_id=1, source_target_pairs={{0,8},{4,12},{8,0},{12,4},{1,9},{5,13},{9,1},{13,5},{2,10},{6,14},... | collective-permute-start | bytes 196616 | tf_op jit(solution)/shard_map/ppermute | solution.py:142
  73.4 0.1 pad_add_fusion.2.place
  73.5 0.0 collective-permute-done.7.refs_0_
  73.5 1.8 %shard_map.69 = (bf16[128,128]{1,0:T(8,128)(2,1)S(1)}, bf16[128,128]{1,0:T(8,128)(2,1)S(1)}, bf16[128,128]{1,0:T(8,128)(2,1)S(1)}, bf16[128,128]{1,0:T(8,128)(2,1)S(1)}) custom-call(s32[2]{0:T(128)S(1)} %pad_add_fusion.2.place, bf16[512,2048]{1,0:T(8,128)(2,1)S(1)} %shard_map.64.queries_ref, s32[512,1]{1,0:T(8,128)S(1)} %copy.7.ids_ref, ...), custom_call_target="tpu_custom_call" | custom-call | flops 268435456 | bytes 2621440 | tf_op jit(solution)/shard_map/pallas_call | solution.py:82
  75.3 4.3 %collective-permute-start.8 = (bf16[128,128]{1,0:T(8,128)(2,1)S(1)}, bf16[128,128]{1,0:T(8,128)(2,1)S(1)}, u32[]{:S(2)}, u32[]{:S(2)}) collective-permute-start(bf16[128,128]{1,0:T(8,128)(2,1)S(1)} %get-tuple-element.21), channel_id=1, source_target_pairs={{0,12},{1,13},{2,14},{3,15},{12,0},{13,1},{14,2},{15,3},{16,28},{1... | collective-permute-start | bytes 98312 | tf_op jit(solution)/shard_map/ppermute | solution.py:173
  79.5 5.0 %collective-permute-start.9 = (bf16[128,128]{1,0:T(8,128)(2,1)S(1)}, bf16[128,128]{1,0:T(8,128)(2,1)S(1)}, u32[]{:S(2)}, u32[]{:S(2)}) collective-permute-start(bf16[128,128]{1,0:T(8,128)(2,1)S(1)} %get-tuple-element.22), channel_id=1, source_target_pairs={{0,13},{1,14},{2,15},{3,12},{12,1},{13,2},{14,3},{15,0},{16,29},{1... | collective-permute-start | bytes 98312 | tf_op jit(solution)/shard_map/ppermute | solution.py:173
  84.6 0.0 collective-permute-done.2.ahead_ref
  84.6 4.0 %collective-permute-start.10 = (bf16[128,128]{1,0:T(8,128)(2,1)S(1)}, bf16[128,128]{1,0:T(8,128)(2,1)S(1)}, u32[]{:S(2)}, u32[]{:S(2)}) collective-permute-start(bf16[128,128]{1,0:T(8,128)(2,1)S(1)} %get-tuple-element.23), channel_id=1, source_target_pairs={{0,14},{1,15},{2,12},{3,13},{12,2},{13,3},{14,0},{15,1},{16,30},{1... | collective-permute-start | bytes 98312 | tf_op jit(solution)/shard_map/ppermute | solution.py:173
  88.6 2.7 %collective-permute-start.11 = (bf16[128,128]{1,0:T(8,128)(2,1)S(1)}, bf16[128,128]{1,0:T(8,128)(2,1)S(1)}, u32[]{:S(2)}, u32[]{:S(2)}) collective-permute-start(bf16[128,128]{1,0:T(8,128)(2,1)S(1)} %get-tuple-element.24), channel_id=1, source_target_pairs={{0,15},{1,12},{2,13},{3,14},{12,3},{13,0},{14,1},{15,2},{16,31},{1... | collective-permute-start | bytes 98312 | tf_op jit(solution)/shard_map/ppermute | solution.py:173
  91.4 0.0 collective-permute-done.8.refs_0_
  91.4 0.0 collective-permute-done.9.refs_1_
  91.4 0.5 collective-permute-done.10.refs_2_
  91.9 4.6 %collective-permute-done.11.refs_3_ = bf16[128,128]{1,0:T(8,128)(2,1)S(1)} collective-permute-done((bf16[128,128]{1,0:T(8,128)(2,1)S(1)}, bf16[128,128]{1,0:T(8,128)(2,1)S(1)}, u32[]{:S(2)}, u32[]{:S(2)}) %collective-permute-start.11) | collective-permute-done | bytes 32800 | tf_op jit(solution)/shard_map/ppermute | solution.py:173
  96.6 0.6 copy-done.14
  97.2 1.7 %shard_map.70 = f32[4,128,128]{2,1,0:T(8,128)} custom-call(s32[1]{0:T(128)} %bitcast.row, f32[128,128]{1,0:T(8,128)} %get-tuple-element.18.own_ref, f32[128,128]{1,0:T(8,128)} %copy-done.8, f32[128,128]{1,0:T(8,128)} %copy-done.9, f32[128,128]{1,0:T(8,128)} %copy-done.10, bf16[128,128]{1,0:T(8,128)(2,1)} %copy-done.11, bf16[128,128]{1,0:T(8,128)(2,1)} %copy-done.12, ...), custom_call_target="tpu_custom_call" | custom-call | tf_op jit(solution)/shard_map/pallas_call | solution.py:130
  (25 shorter events, 0.0 us)
Async XLA Ops:
  0.0 14.9 %collective-permute-start = (bf16[128,2048]{1,0:T(8,128)(2,1)}, bf16[128,2048]{1,0:T(8,128)(2,1)S(1)}, u32[]{:S(2)}, u32[]{:S(2)}) collective-permute-start(bf16[128,2048]{1,0:T(8,128)(2,1)} %refs_0_.1), channel_id=1, source_target_pairs={{0,4},{4,8},{8,12},{1,5},{5,9},{9,13},{2,6},{6,10},{10,14},{3,7},{... | collective-permute-start | bytes 1572872 | tf_op jit(solution)/shard_map/ppermute | solution.py:142
  4.1 14.7 %collective-permute-start.1 = (bf16[128,2048]{1,0:T(8,128)(2,1)}, bf16[128,2048]{1,0:T(8,128)(2,1)}, u32[]{:S(2)}, u32[]{:S(2)}) collective-permute-start(bf16[128,2048]{1,0:T(8,128)(2,1)} %refs_0_.1), channel_id=1, source_target_pairs={{12,8},{8,4},{4,0},{13,9},{9,5},{5,1},{14,10},{10,6},{6,2},{15,11}... | collective-permute-start | bytes 1572872 | tf_op jit(solution)/shard_map/ppermute | solution.py:142
  6.0 1.6 %copy-start.3 = (bf16[512,2048]{1,0:T(8,128)(2,1)S(1)}, bf16[512,2048]{1,0:T(8,128)(2,1)}, u32[]{:S(2)}) copy-start(bf16[512,2048]{1,0:T(8,128)(2,1)} %query_ref.1) | copy-start | bytes 6291460
  7.6 1.6 %copy-start.4 = (bf16[4,512,512]{2,1,0:T(8,128)(2,1)S(1)}, bf16[4,512,512]{2,1,0:T(8,128)(2,1)}, u32[]{:S(2)}) copy-start(bf16[4,512,512]{2,1,0:T(8,128)(2,1)} %basis_ref.1) | copy-start | bytes 6291460
  9.2 0.7 copy-start.5
  9.9 12.4 %copy-start.15 = (s32[512]{0:T(512)S(1)}, s32[512]{0:T(512)}, u32[]{:S(2)}) copy-start(s32[512]{0:T(512)} %param.11) | copy-start | bytes 6148
  13.6 26.1 %copy-start = (bf16[128,2048]{1,0:T(8,128)(2,1)S(1)}, bf16[128,2048]{1,0:T(8,128)(2,1)}, u32[]{:S(2)}) copy-start(bf16[128,2048]{1,0:T(8,128)(2,1)} %refs_0_.1) | copy-start | bytes 1572868
  18.7 3.8 %collective-permute-start.4 = (bf16[128,2048]{1,0:T(8,128)(2,1)S(1)}, bf16[128,2048]{1,0:T(8,128)(2,1)}, u32[]{:S(2)}, u32[]{:S(2)}) collective-permute-start(bf16[128,2048]{1,0:T(8,128)(2,1)S(1)} %collective-permute-done.refs_1_), channel_id=1, source_target_pairs={{4,8},{8,12},{5,9},{9,13},{6,10},{10,14},{7,11},{11,15},{20,24},{2... | collective-permute-start | bytes 1572872 | tf_op jit(solution)/shard_map/ppermute | solution.py:142
  20.2 0.8 copy-start.1
  21.0 16.1 %collective-permute-start.5 = (bf16[128,2048]{1,0:T(8,128)(2,1)}, bf16[128,2048]{1,0:T(8,128)(2,1)}, u32[]{:S(2)}, u32[]{:S(2)}) collective-permute-start(bf16[128,2048]{1,0:T(8,128)(2,1)} %collective-permute-done.1.refs_2_), channel_id=1, source_target_pairs={{8,4},{4,0},{9,5},{5,1},{10,6},{6,2},{11,7},{7,3},{24,20},{20,16},... | collective-permute-start | bytes 1572872 | tf_op jit(solution)/shard_map/ppermute | solution.py:142
  38.5 35.0 %collective-permute-start.7 = (bf16[128,2048]{1,0:T(8,128)(2,1)S(1)}, bf16[128,2048]{1,0:T(8,128)(2,1)}, u32[]{:S(2)}, u32[]{:S(2)}) collective-permute-start(bf16[128,2048]{1,0:T(8,128)(2,1)S(1)} %add.18.refs_0_), channel_id=1, source_target_pairs={{8,12},{4,0},{9,13},{5,1},{10,14},{6,2},{11,15},{7,3},{24,28},{20,... | collective-permute-start | bytes 1572872 | tf_op jit(solution)/shard_map/ppermute | solution.py:142
  39.8 1.0 %copy-start.2 = (bf16[128,2048]{1,0:T(8,128)(2,1)S(1)}, bf16[128,2048]{1,0:T(8,128)(2,1)}, u32[]{:S(2)}) copy-start(bf16[128,2048]{1,0:T(8,128)(2,1)} %copy-done.1) | copy-start | bytes 1572868
  44.4 12.8 %all-to-all-start = ((bf16[4,128,384]{2,1,0:T(8,128)(2,1)}), bf16[4,128,384]{2,1,0:T(8,128)(2,1)S(1)}, u32[]{:S(2)}, u32[]{:S(2)}) async-start(bf16[4,128,384]{2,1,0:T(8,128)(2,1)} %shard_map.65), calls=%async_computation | async-start | bytes 786432 | tf_op jit(solution)/shard_map/all_to_all | solution.py:106
  57.2 4.2 %copy-start.6 = (bf16[4,128,384]{2,1,0:T(8,128)(2,1)}, bf16[4,128,384]{2,1,0:T(8,128)(2,1)S(1)}, u32[]{:S(2)}) copy-start(bf16[4,128,384]{2,1,0:T(8,128)(2,1)S(1)} %all-to-all-done.in_ref) | copy-start | bytes 1179652
  57.2 12.2 %all-to-all-start.1 = ((bf16[4,128,128]{2,1,0:T(8,128)(2,1)}), bf16[4,128,128]{2,1,0:T(8,128)(2,1)S(1)}, u32[]{:S(2)}, u32[]{:S(2)}) async-start(bf16[4,128,128]{2,1,0:T(8,128)(2,1)} %shard_map.67), calls=%async_computation.1 | async-start | bytes 262144 | tf_op jit(solution)/shard_map/all_to_all | solution.py:106
  63.0 21.5 %collective-permute-start.2 = (f32[128,128]{1,0:T(8,128)}, f32[128,128]{1,0:T(8,128)S(1)}, u32[]{:S(2)}, u32[]{:S(2)}) collective-permute-start(f32[128,128]{1,0:T(8,128)} %get-tuple-element.19), channel_id=1, source_target_pairs={{0,4},{4,8},{8,12},{1,5},{5,9},{9,13},{2,6},{6,10},{10,14},{3,7},{... | collective-permute-start | bytes 196616 | tf_op jit(solution)/shard_map/ppermute | solution.py:142
  68.1 20.5 %collective-permute-start.3 = (f32[128,128]{1,0:T(8,128)}, f32[128,128]{1,0:T(8,128)S(1)}, u32[]{:S(2)}, u32[]{:S(2)}) collective-permute-start(f32[128,128]{1,0:T(8,128)} %get-tuple-element.20), channel_id=1, source_target_pairs={{4,0},{8,4},{12,8},{5,1},{9,5},{13,9},{6,2},{10,6},{14,10},{7,3},{... | collective-permute-start | bytes 196616 | tf_op jit(solution)/shard_map/ppermute | solution.py:142
  69.4 0.7 copy-start.7
  71.6 19.8 %collective-permute-start.6 = (f32[128,128]{1,0:T(8,128)}, f32[128,128]{1,0:T(8,128)S(1)}, u32[]{:S(2)}, u32[]{:S(2)}) collective-permute-start(f32[128,128]{1,0:T(8,128)} %shard_map.68), channel_id=1, source_target_pairs={{0,8},{4,12},{8,0},{12,4},{1,9},{5,13},{9,1},{13,5},{2,10},{6,14},... | collective-permute-start | bytes 196616 | tf_op jit(solution)/shard_map/ppermute | solution.py:142
  75.3 16.1 %collective-permute-start.8 = (bf16[128,128]{1,0:T(8,128)(2,1)S(1)}, bf16[128,128]{1,0:T(8,128)(2,1)S(1)}, u32[]{:S(2)}, u32[]{:S(2)}) collective-permute-start(bf16[128,128]{1,0:T(8,128)(2,1)S(1)} %get-tuple-element.21), channel_id=1, source_target_pairs={{0,12},{1,13},{2,14},{3,15},{12,0},{13,1},{14,2},{15,3},{16,28},{1... | collective-permute-start | bytes 98312 | tf_op jit(solution)/shard_map/ppermute | solution.py:173
  79.5 11.9 %collective-permute-start.9 = (bf16[128,128]{1,0:T(8,128)(2,1)S(1)}, bf16[128,128]{1,0:T(8,128)(2,1)S(1)}, u32[]{:S(2)}, u32[]{:S(2)}) collective-permute-start(bf16[128,128]{1,0:T(8,128)(2,1)S(1)} %get-tuple-element.22), channel_id=1, source_target_pairs={{0,13},{1,14},{2,15},{3,12},{12,1},{13,2},{14,3},{15,0},{16,29},{1... | collective-permute-start | bytes 98312 | tf_op jit(solution)/shard_map/ppermute | solution.py:173
  84.6 12.0 %copy-start.8 = (f32[128,128]{1,0:T(8,128)}, f32[128,128]{1,0:T(8,128)S(1)}, u32[]{:S(2)}) copy-start(f32[128,128]{1,0:T(8,128)S(1)} %collective-permute-done.2.ahead_ref) | copy-start | bytes 196612
  84.6 7.4 %collective-permute-start.10 = (bf16[128,128]{1,0:T(8,128)(2,1)S(1)}, bf16[128,128]{1,0:T(8,128)(2,1)S(1)}, u32[]{:S(2)}, u32[]{:S(2)}) collective-permute-start(bf16[128,128]{1,0:T(8,128)(2,1)S(1)} %get-tuple-element.23), channel_id=1, source_target_pairs={{0,14},{1,15},{2,12},{3,13},{12,2},{13,3},{14,0},{15,1},{16,30},{1... | collective-permute-start | bytes 98312 | tf_op jit(solution)/shard_map/ppermute | solution.py:173
  88.6 7.9 %copy-start.9 = (f32[128,128]{1,0:T(8,128)}, f32[128,128]{1,0:T(8,128)S(1)}, u32[]{:S(2)}) copy-start(f32[128,128]{1,0:T(8,128)S(1)} %collective-permute-done.3.behind_ref) | copy-start | bytes 196612
  88.6 7.9 %collective-permute-start.11 = (bf16[128,128]{1,0:T(8,128)(2,1)S(1)}, bf16[128,128]{1,0:T(8,128)(2,1)S(1)}, u32[]{:S(2)}, u32[]{:S(2)}) collective-permute-start(bf16[128,128]{1,0:T(8,128)(2,1)S(1)} %get-tuple-element.24), channel_id=1, source_target_pairs={{0,15},{1,12},{2,13},{3,14},{12,3},{13,0},{14,1},{15,2},{16,31},{1... | collective-permute-start | bytes 98312 | tf_op jit(solution)/shard_map/ppermute | solution.py:173
  91.4 5.2 %copy-start.10 = (f32[128,128]{1,0:T(8,128)}, f32[128,128]{1,0:T(8,128)S(1)}, u32[]{:S(2)}) copy-start(f32[128,128]{1,0:T(8,128)S(1)} %collective-permute-done.6.across_ref) | copy-start | bytes 196612
  91.4 5.2 %copy-start.11 = (bf16[128,128]{1,0:T(8,128)(2,1)}, bf16[128,128]{1,0:T(8,128)(2,1)S(1)}, u32[]{:S(2)}) copy-start(bf16[128,128]{1,0:T(8,128)(2,1)S(1)} %collective-permute-done.8.refs_0_) | copy-start | bytes 98308
  91.4 5.2 %copy-start.12 = (bf16[128,128]{1,0:T(8,128)(2,1)}, bf16[128,128]{1,0:T(8,128)(2,1)S(1)}, u32[]{:S(2)}) copy-start(bf16[128,128]{1,0:T(8,128)(2,1)S(1)} %collective-permute-done.9.refs_1_) | copy-start | bytes 98308
  91.9 4.7 %copy-start.13 = (bf16[128,128]{1,0:T(8,128)(2,1)}, bf16[128,128]{1,0:T(8,128)(2,1)S(1)}, u32[]{:S(2)}) copy-start(bf16[128,128]{1,0:T(8,128)(2,1)S(1)} %collective-permute-done.10.refs_2_) | copy-start | bytes 98308
  96.6 0.6 copy-start.14

commit v4 on v3

--- a/solution.py
+++ b/solution.py
@@ -45,7 +45,7 @@
     )(slots, query_grads, eigenbases, eigenvalues)
 
 
-def score_kernel(shares, turned, place, queries_ref, ids_ref, *refs):
+def score_kernel(shares, block_of, turned, place, queries_ref, ids_ref, *refs):
     if turned:
         document_refs, out_refs, held = refs[: -1 - shares], refs[-1 - shares : -1], refs[-1]
     else:
@@ -53,7 +53,7 @@
     doc_rows = document_refs[0].shape[0]
     for spot, document_ref in enumerate(document_refs):
         tile = lax.dot_general(queries_ref[...], document_ref[...], NT, preferred_element_type=jnp.float32)
-        doc_ids = place[1 + spot] + lax.broadcasted_iota(jnp.int32, tile.shape, 1)
+        doc_ids = block_of[spot](place[1]) * doc_rows + lax.broadcasted_iota(jnp.int32, tile.shape, 1)
         tile = jnp.where(ids_ref[...] == doc_ids, 0.0, tile)
         share_rows = tile.shape[0] // shares
         if turned:
@@ -68,7 +68,7 @@
                 out_refs[0][share, :, columns] = part.astype(jnp.bfloat16)
 
 
-def partial_scores(conditioned, query_ids, documents, place, shares, turned=False):
+def partial_scores(conditioned, query_ids, documents, block_of, place, shares, turned=False):
     rows, dims = conditioned.shape
     doc_rows = documents[0].shape[0]
     docs = doc_rows * len(documents)
@@ -80,7 +80,7 @@
         out_shape = jax.ShapeDtypeStruct((shares, rows // shares, docs), jnp.bfloat16)
         scratch = []
     return pl.pallas_call(
-        functools.partial(score_kernel, shares, turned),
+        functools.partial(score_kernel, shares, block_of, turned),
         out_shape=out_shape,
         in_specs=[pl.BlockSpec(memory_space=pltpu.SMEM)] + [vmem] * (2 + len(documents)),
         out_specs=[vmem] * shares if turned else vmem,
@@ -114,87 +114,103 @@
     )(tiles)
 
 
-def final_kernel(row, own_ref, ahead_ref, behind_ref, across_ref, *refs):
-    *last_refs, out_ref = refs
-    last = last_refs[0][...].astype(jnp.float32)
-    for last_ref in last_refs[1:]:
-        last += last_ref[...].astype(jnp.float32)
+ROUND_ONE = ((0, 2), (3, 1), (2, 3), (1, 0))
+ROUND_TWO = ((0, 1), (3, 2), (1, 3), (2, 0))
+ROUND_INNER = ((1, 2), (2, 1))
+ROUND_OUTER = ((2, 3), (1, 0))
+BLOCK_ONE = (1, 3, 0, 2)
+BLOCK_TWO = (2, 0, 3, 1)
+BLOCK_LAST = (3, 2, 1, 0)
+
+
+def pick(table):
+    def entry(row):
+        value = jnp.int32(table[0])
+        for index in range(1, len(table)):
+            value = jnp.where(row == index, jnp.int32(table[index]), value)
+        return value
+
+    return entry
+
+
+def step_of(table):
+    return pick([(block - table.index(block)) % STEPS for block in range(STEPS)])
+
+
+def final_kernel(place, own_ref, first_ref, *refs):
+    *late_refs, out_ref = refs
     out_ref[0] = own_ref[...]
-    out_ref[1] = jnp.where(row[0] == 0, last, ahead_ref[...])
-    out_ref[2] = across_ref[...]
-    out_ref[3] = jnp.where(row[0] == STEPS - 1, last, behind_ref[...])
-
-
-def final_scores(row, own, ahead, behind, across, last):
+    out_ref[step_of(BLOCK_ONE)(place[1])] = first_ref[...]
+    count = len(late_refs) // 2
+    for spot, table in enumerate((BLOCK_TWO, BLOCK_LAST)):
+        total = late_refs[spot * count][...].astype(jnp.float32)
+        for late_ref in late_refs[spot * count + 1 : (spot + 1) * count]:
+            total += late_ref[...].astype(jnp.float32)
+        out_ref[step_of(table)(place[1])] = total
+
+
+def final_scores(place, own, first, late):
     vmem = pl.BlockSpec(memory_space=pltpu.VMEM)
     return pl.pallas_call(
         final_kernel,
         out_shape=jax.ShapeDtypeStruct((STEPS,) + own.shape, jnp.float32),
-        in_specs=[pl.BlockSpec(memory_space=pltpu.SMEM)] + [vmem] * (4 + len(last)),
+        in_specs=[pl.BlockSpec(memory_space=pltpu.SMEM)] + [vmem] * (2 + len(late)),
         out_specs=vmem,
-    )(row[None], own, ahead, behind, across, *last)
-
-
-def along_line(documents, conditioned, query_ids, row, layer_index, shares):
+    )(place, own, first, *late)
+
+
+def along_line(documents, conditioned, query_ids, place, shares):
     doc_rows = documents.shape[0]
 
-    def hop(value, *pairs):
-        return lax.ppermute(value, "rows", pairs)
-
-    def scores(blocks, sources, turned=False):
-        place = jnp.stack([layer_index] + [source * doc_rows for source in sources]).astype(jnp.int32)
-        return partial_scores(conditioned, query_ids, blocks, place, shares, turned)
-
-    below = hop(documents, (0, 1), (1, 2), (2, 3))
-    above = hop(documents, (3, 2), (2, 1), (1, 0))
-    below, above, conditioned = lax.optimization_barrier((below, above, conditioned))
-    below2 = hop(below, (1, 2), (2, 3))
-    above2 = hop(above, (2, 1), (1, 0))
-
-    tiles = scores([documents, below, above], [row, row - 1, row + 1])
-    own, lower, upper = sum_shares(tiles, doc_rows)
-    behind = hop(lower, (1, 0), (2, 1), (3, 2))
-    ahead = hop(upper, (0, 1), (1, 2), (2, 3))
-
-    opposite = below2 + above2
-    final = hop(opposite, (2, 3), (1, 0))
-    tiles = scores([opposite], [(row + 2) % STEPS])
-    (across,) = sum_shares(tiles, doc_rows)
-    across = hop(across, (0, 2), (1, 3), (2, 0), (3, 1))
-
-    tiles = scores([final], [STEPS - 1 - row], turned=True)
-    last = []
-    for turn, tile in enumerate(tiles):
-        pairs = [
-            (here * shares + lay, there * shares + (lay + turn) % shares)
-            for here, there in ((0, 3), (3, 0))
-            for lay in range(shares)
-        ]
-        last.append(lax.ppermute(tile, ("rows", "layer"), pairs))
-    return final_scores(row, own, ahead, behind, across, last)
-
-
-def around_ring(documents, conditioned, query_ids, row, layer_index, shares):
+    def straight(block, table):
+        tiles = partial_scores(conditioned, query_ids, [block], [pick(table)], place, shares, turned=True)
+        arrived = []
+        for turn, tile in enumerate(tiles):
+            pairs = [
+                (here * shares + lay, there * shares + (lay + turn) % shares)
+                for here, there in enumerate(table)
+                for lay in range(shares)
+            ]
+            arrived.append(lax.ppermute(tile, ("rows", "layer"), pairs))
+        return arrived
+
+    one = lax.ppermute(documents, "rows", ROUND_ONE)
+    later, conditioned = lax.optimization_barrier((documents, conditioned))
+    two = lax.ppermute(later, "rows", ROUND_TWO)
+    later, one = lax.optimization_barrier((later, one))
+    outer = lax.ppermute(one, "rows", ROUND_OUTER)
+    inner = lax.ppermute(later, "rows", ROUND_INNER)
+
+    both = [lambda row: row, pick(BLOCK_ONE)]
+    tiles = partial_scores(conditioned, query_ids, [documents, one], both, place, shares)
+    two, tiles = lax.optimization_barrier((two, tiles))
+    own, first = sum_shares(tiles, doc_rows)
+    first = lax.ppermute(first, "rows", tuple(enumerate(BLOCK_ONE)))
+    second = straight(two, BLOCK_TWO)
+    last = straight(outer + inner, BLOCK_LAST)
+    return final_scores(place, own, first, second + last)
+
+
+def around_ring(documents, conditioned, query_ids, place, shares):
     n_rows = lax.axis_size("rows")
-    doc_rows = documents.shape[0]
     result = []
     for step in range(STEPS):
         back = [(source, (source - step) % n_rows) for source in range(n_rows)]
         block = lax.ppermute(documents, "rows", back) if step else documents
-        place = jnp.stack([layer_index, (row + step) % n_rows * doc_rows]).astype(jnp.int32)
-        (total,) = sum_shares(partial_scores(conditioned, query_ids, [block], place, shares), doc_rows)
+        block_of = [lambda row, step=step: lax.rem(row + step, n_rows)]
+        tiles = partial_scores(conditioned, query_ids, [block], block_of, place, shares)
+        (total,) = sum_shares(tiles, documents.shape[0])
         onward = [(source, (source + step) % n_rows) for source in range(n_rows)]
         result.append(lax.ppermute(total, "rows", onward) if step else total)
     return jnp.stack(result)
 
 
 def local(train_grads, query_grads, eigenbases, eigenvalues, layer_offsets, query_doc_ids):
-    row = lax.axis_index("rows").astype(jnp.int32)
-    layer_index = lax.axis_index("layer").astype(jnp.int32)
-    slots = layer_offsets // LDIM - layer_index * LAY_DEV
+    place = jnp.stack([lax.axis_index("layer"), lax.axis_index("rows")]).astype(jnp.int32)
+    slots = layer_offsets // LDIM - place[0] * LAY_DEV
     conditioned = precondition(query_grads, eigenbases, eigenvalues, slots)
     plan = along_line if lax.axis_size("rows") == STEPS else around_ring
-    return plan(train_grads, conditioned, query_doc_ids[:, None], row, layer_index, lax.axis_size("layer"))
+    return plan(train_grads, conditioned, query_doc_ids[:, None], place, lax.axis_size("layer"))
 
 
 def solution(mesh):

time: 99.8 us -> 61.1 us (0.61)
  starting transfers between devices: 43.9 us -> 25.6 us
  waiting for transfers between devices: 29.4 us -> 15.6 us
  Pallas kernels: 15.9 us -> 12.6 us
  local copies, waits for them, and re-layouts: 7.1 us -> 4.63 us
    ppermute x12 -> x13, starting transfers between devices: 33.6 us -> 20.4 us  [the longest x8 13.4 us: straight(): arrived.append(lax.ppermute(tile, ('rows', 'layer'), pairs))]
    ppermute x12 -> x13, waiting for transfers between devices: 24.8 us -> 15.6 us  [the longest x1 8.26 us: along_line(): two = lax.ppermute(later, 'rows', ROUND_TWO)]
    all_to_all x2 -> x1, starting transfers between devices: 10.4 us -> 5.25 us  [sum_shares(): tiles = lax.all_to_all(tiles, 'layer', 0, 0, tiled=True)]
    all_to_all x2 -> x1, waiting for transfers between devices: 4.6 us -> 0.01 us  [sum_shares(): tiles = lax.all_to_all(tiles, 'layer', 0, 0, tiled=True)]
    unnamed x32 -> x24, local copies, waits for them, and re-layouts: 6.96 us -> 4.48 us
    pallas_call x3, Pallas kernels: 7.28 us -> 5.57 us  [partial_scores(): pl.pallas_call(functools.partial(score_kernel, shares, block_of, turned),...]
    pallas_call x2 -> x1, Pallas kernels: 3.22 us -> 1.62 us  [sum_shares(): pl.pallas_call(sum_kernel, out_shape=[jax.ShapeDtypeStruct((share_rows, d...]
  transfers between devices with their start and end apart: 14 -> 14, of which waited for: 6 -> 4; matrix products, arithmetic and copies ran while one was open for 1% -> 4% of each run, Pallas kernels for 14% -> 18%
where the time goes in v4:
time: 61.1 us; the launch traced here: 60.6 us
  starting transfers between devices  25.6 us (42%)
  waiting for transfers between devices  15.6 us (26%)
  Pallas kernels  12.6 us (21%)
  local copies, waits for them, and re-layouts  4.63 us (8%)
  other arithmetic  2.07 us (3%)
    ppermute x8, starting transfers between devices, straight(): arrived.append(lax.ppermute(tile, ('rows', 'layer'), pairs))  13.4 us
    ppermute x1, waiting for transfers between devices, along_line(): two = lax.ppermute(later, 'rows', ROUND_TWO)  8.26 us
    pallas_call x3, Pallas kernels, partial_scores(): pl.pallas_call(functools.partial(score_kernel, shares, block_of, turned),...  5.57 us
    all_to_all x1, starting transfers between devices, sum_shares(): tiles = lax.all_to_all(tiles, 'layer', 0, 0, tiled=True)  5.25 us
    ppermute x8, waiting for transfers between devices, straight(): arrived.append(lax.ppermute(tile, ('rows', 'layer'), pairs))  4.74 us
    unnamed x24, local copies, waits for them, and re-layouts  4.48 us
    pallas_call x1, Pallas kernels, precondition(): pl.pallas_call(precondition_kernel, out_shape=jax.ShapeDtypeStruct((rows,...  3.72 us
    ppermute x1, starting transfers between devices, along_line(): one = lax.ppermute(documents, 'rows', ROUND_ONE)  3.14 us
  transfers between devices with their start and end apart: 14, of which 4 were waited for; matrix products, arithmetic and copies ran while one was open for 4% of the time, Pallas kernels for 18%

profile of v4, /device:TPU:1, one launch (start us, length us, event | category | flops | bytes accessed | tf_op | source)
XLA Modules:
  0.0 60.6 jit_solution(4392537555791304863)
XLA Ops:
  0.0 3.1 %collective-permute-start.1 = (bf16[128,2048]{1,0:T(8,128)(2,1)}, bf16[128,2048]{1,0:T(8,128)(2,1)S(1)}, u32[]{:S(2)}, u32[]{:S(2)}) collective-permute-start(bf16[128,2048]{1,0:T(8,128)(2,1)} %refs_0_.1), channel_id=1, source_target_pairs={{0,8},{12,4},{8,12},{4,0},{1,9},{13,5},{9,13},{5,1},{2,10},{14,6},... | collective-permute-start | bytes 1572872 | tf_op jit(solution)/shard_map/ppermute | solution.py:177
  3.1 0.7 %fusion.slots = s32[4]{0:T(128)S(1)} fusion(s32[4]{0:T(128)} %param.10, s32[]{:T(128)S(6)} %mul.3), kind=kLoop, calls=%fused_computation.5 | loop fusion | flops 64 | bytes 36 | tf_op jit(solution)/shard_map/sub | solution.py:210
  3.8 1.6 %copy-done.2 = bf16[512,2048]{1,0:T(8,128)(2,1)S(1)} copy-done((bf16[512,2048]{1,0:T(8,128)(2,1)S(1)}, bf16[512,2048]{1,0:T(8,128)(2,1)}, u32[]{:S(2)}) %copy-start.2) | copy-done | bytes 2097176
  5.4 1.6 %copy-done.3 = bf16[4,512,512]{2,1,0:T(8,128)(2,1)S(1)} copy-done((bf16[4,512,512]{2,1,0:T(8,128)(2,1)S(1)}, bf16[4,512,512]{2,1,0:T(8,128)(2,1)}, u32[]{:S(2)}) %copy-start.3) | copy-done | bytes 2097176
  7.0 0.7 %copy-done.4 = f32[4,512]{1,0:T(4,128)S(1)} copy-done((f32[4,512]{1,0:T(4,128)S(1)}, f32[4,512]{1,0:T(4,128)}, u32[]{:S(2)}) %copy-start.4) | copy-done | bytes 8216
  7.7 3.7 %shard_map.64.queries_ref = bf16[512,2048]{1,0:T(8,128)(2,1)S(1)} custom-call(s32[4]{0:T(128)S(1)} %fusion.slots, bf16[512,2048]{1,0:T(8,128)(2,1)S(1)} %copy-done.2, bf16[4,512,512]{2,1,0:T(8,128)(2,1)S(1)} %copy-done.3, f32[4,512]{1,0:T(4,128)S(1)} %copy-done.4), custom_call_target="tpu_custom_call" | custom-call | flops 2147483648 | bytes 6291456 | tf_op jit(solution)/shard_map/pallas_call | solution.py:28
  11.4 0.0 copy-done
  11.4 0.1 collective-permute-start
  11.5 2.6 %collective-permute-done.1.refs_1_ = bf16[128,2048]{1,0:T(8,128)(2,1)S(1)} collective-permute-done((bf16[128,2048]{1,0:T(8,128)(2,1)}, bf16[128,2048]{1,0:T(8,128)(2,1)S(1)}, u32[]{:S(2)}, u32[]{:S(2)}) %collective-permute-start.1) | collective-permute-done | bytes 524320 | tf_op jit(solution)/shard_map/ppermute | solution.py:177
  14.1 1.3 %collective-permute-start.7 = (bf16[128,2048]{1,0:T(8,128)(2,1)S(1)}, bf16[128,2048]{1,0:T(8,128)(2,1)}, u32[]{:S(2)}, u32[]{:S(2)}) collective-permute-start(bf16[128,2048]{1,0:T(8,128)(2,1)S(1)} %collective-permute-done.1.refs_1_), channel_id=1, source_target_pairs={{8,12},{4,0},{9,13},{5,1},{10,14},{6,2},{11,15},{7,3},{24,28},{20,... | collective-permute-start | bytes 1572872 | tf_op jit(solution)/shard_map/ppermute | solution.py:181
  15.4 1.5 %collective-permute-start.8 = (bf16[128,2048]{1,0:T(8,128)(2,1)S(1)}, bf16[128,2048]{1,0:T(8,128)(2,1)}, u32[]{:S(2)}, u32[]{:S(2)}) collective-permute-start(bf16[128,2048]{1,0:T(8,128)(2,1)S(1)} %copy-done), channel_id=1, source_target_pairs={{4,8},{8,4},{5,9},{9,5},{6,10},{10,6},{7,11},{11,7},{20,24},{24,20... | collective-permute-start | bytes 1572872 | tf_op jit(solution)/shard_map/ppermute | solution.py:182
  16.9 0.0 copy-done.11
  16.9 0.1 copy.7.ids_ref
  17.0 0.1 pad_add_fusion.place
  17.1 2.5 %shard_map.65 = bf16[4,128,256]{2,1,0:T(8,128)(2,1)} custom-call(s32[2]{0:T(128)S(1)} %pad_add_fusion.place, bf16[512,2048]{1,0:T(8,128)(2,1)S(1)} %shard_map.64.queries_ref, s32[512,1]{1,0:T(8,128)S(1)} %copy.7.ids_ref, bf16[128,2048]{1,0:T(8,128)(2,1)S(1)} %copy-done, bf16[128,2048]{1,0:T(8,128)(2,1)S(1)} %collective-permute-done.1.refs_1_), custom_call_target="tpu_custom_call" | custom-call | flops 536870912 | bytes 3145728 | tf_op jit(solution)/shard_map/pallas_call | solution.py:82
  19.6 8.3 %collective-permute-done.refs_0_ = bf16[128,2048]{1,0:T(8,128)(2,1)} collective-permute-done((bf16[128,2048]{1,0:T(8,128)(2,1)S(1)}, bf16[128,2048]{1,0:T(8,128)(2,1)}, u32[]{:S(2)}, u32[]{:S(2)}) %collective-permute-start) | collective-permute-done | bytes 524320 | tf_op jit(solution)/shard_map/ppermute | solution.py:179
  27.8 5.3 %all-to-all-start = ((bf16[4,128,256]{2,1,0:T(8,128)(2,1)}), bf16[4,128,256]{2,1,0:T(8,128)(2,1)}, u32[]{:S(2)}, u32[]{:S(2)}) async-start(bf16[4,128,256]{2,1,0:T(8,128)(2,1)} %shard_map.65), calls=%async_computation | async-start | bytes 524288 | tf_op jit(solution)/shard_map/all_to_all | solution.py:106
  33.1 1.8 %shard_map.67 = (bf16[128,128]{1,0:T(8,128)(2,1)S(1)}, bf16[128,128]{1,0:T(8,128)(2,1)S(1)}, bf16[128,128]{1,0:T(8,128)(2,1)S(1)}, bf16[128,128]{1,0:T(8,128)(2,1)S(1)}) custom-call(s32[2]{0:T(128)S(1)} %pad_add_fusion.place, bf16[512,2048]{1,0:T(8,128)(2,1)S(1)} %shard_map.64.queries_ref, s32[512,1]{1,0:T(8,128)S(1)} %copy.7.ids_ref, ...), custom_call_target="tpu_custom_call" | custom-call | flops 268435456 | bytes 2621440 | tf_op jit(solution)/shard_map/pallas_call | solution.py:82
  34.9 0.1 collective-permute-start.3
  35.0 3.8 %collective-permute-start.4 = (bf16[128,128]{1,0:T(8,128)(2,1)S(1)}, bf16[128,128]{1,0:T(8,128)(2,1)}, u32[]{:S(2)}, u32[]{:S(2)}) collective-permute-start(bf16[128,128]{1,0:T(8,128)(2,1)S(1)} %get-tuple-element.29), channel_id=1, source_target_pairs={{0,9},{1,10},{2,11},{3,8},{4,1},{5,2},{6,3},{7,0},{8,13},{9,14},{1... | collective-permute-start | bytes 98312 | tf_op jit(solution)/shard_map/ppermute | solution.py:174
  38.7 0.0 collective-permute-start.5
  38.7 0.0 all-to-all-done.in_ref
  38.7 1.6 %shard_map.66 = (f32[128,128]{1,0:T(8,128)}, f32[128,128]{1,0:T(8,128)}) custom-call(bf16[4,128,256]{2,1,0:T(8,128)(2,1)} %all-to-all-done.in_ref), custom_call_target="tpu_custom_call" | custom-call | tf_op jit(solution)/shard_map/pallas_call | solution.py:109
  40.3 0.0 collective-permute-done.7
  40.3 1.0 %collective-permute-start.2 = (f32[128,128]{1,0:T(8,128)}, f32[128,128]{1,0:T(8,128)S(1)}, u32[]{:S(2)}, u32[]{:S(2)}) collective-permute-start(f32[128,128]{1,0:T(8,128)} %get-tuple-element.26), channel_id=1, source_target_pairs={{0,4},{4,12},{8,0},{12,8},{1,5},{5,13},{9,1},{13,9},{2,6},{6,14},{... | collective-permute-start | bytes 196616 | tf_op jit(solution)/shard_map/ppermute | solution.py:188
  41.3 0.0 collective-permute-done.8
  41.3 2.1 %collective-permute-start.6 = (bf16[128,128]{1,0:T(8,128)(2,1)S(1)}, bf16[128,128]{1,0:T(8,128)(2,1)S(1)}, u32[]{:S(2)}, u32[]{:S(2)}) collective-permute-start(bf16[128,128]{1,0:T(8,128)(2,1)S(1)} %get-tuple-element.31), channel_id=1, source_target_pairs={{0,11},{1,8},{2,9},{3,10},{4,3},{5,0},{6,1},{7,2},{8,15},{9,12},{1... | collective-permute-start | bytes 98312 | tf_op jit(solution)/shard_map/ppermute | solution.py:174
  43.4 1.3 %add.4.refs_0_ = bf16[128,2048]{1,0:T(8,128)(2,1)S(1)} add(bf16[128,2048]{1,0:T(8,128)(2,1)} %collective-permute-done.7, bf16[128,2048]{1,0:T(8,128)(2,1)} %collective-permute-done.8) | non-fusion elementwise | flops 262144 | bytes 1572864 | tf_op jit(solution)/shard_map/add | solution.py:190
  44.7 0.0 copy-done.1
  44.7 1.3 %shard_map.68 = (bf16[128,128]{1,0:T(8,128)(2,1)S(1)}, bf16[128,128]{1,0:T(8,128)(2,1)S(1)}, bf16[128,128]{1,0:T(8,128)(2,1)S(1)}, bf16[128,128]{1,0:T(8,128)(2,1)S(1)}) custom-call(s32[2]{0:T(128)S(1)} %pad_add_fusion.place, bf16[512,2048]{1,0:T(8,128)(2,1)S(1)} %shard_map.64.queries_ref, s32[512,1]{1,0:T(8,128)S(1)} %copy.7.ids_ref, ...), custom_call_target="tpu_custom_call" | custom-call | flops 268435456 | bytes 2621440 | tf_op jit(solution)/shard_map/pallas_call | solution.py:82
  46.0 0.0 collective-permute-done.3.refs_0_
  46.0 1.9 %collective-permute-start.9 = (bf16[128,128]{1,0:T(8,128)(2,1)S(1)}, bf16[128,128]{1,0:T(8,128)(2,1)S(1)}, u32[]{:S(2)}, u32[]{:S(2)}) collective-permute-start(bf16[128,128]{1,0:T(8,128)(2,1)S(1)} %get-tuple-element.33), channel_id=1, source_target_pairs={{0,12},{1,13},{2,14},{3,15},{4,8},{5,9},{6,10},{7,11},{8,4},{9,5},... | collective-permute-start | bytes 98312 | tf_op jit(solution)/shard_map/ppermute | solution.py:174
  48.0 0.0 collective-permute-done.4.refs_1_
  48.0 2.2 %collective-permute-start.10 = (bf16[128,128]{1,0:T(8,128)(2,1)S(1)}, bf16[128,128]{1,0:T(8,128)(2,1)S(1)}, u32[]{:S(2)}, u32[]{:S(2)}) collective-permute-start(bf16[128,128]{1,0:T(8,128)(2,1)S(1)} %get-tuple-element.34), channel_id=1, source_target_pairs={{0,13},{1,14},{2,15},{3,12},{4,9},{5,10},{6,11},{7,8},{8,5},{9,6},... | collective-permute-start | bytes 98312 | tf_op jit(solution)/shard_map/ppermute | solution.py:174
  50.1 0.0 collective-permute-done.5.refs_2_
  50.1 2.1 %collective-permute-start.11 = (bf16[128,128]{1,0:T(8,128)(2,1)S(1)}, bf16[128,128]{1,0:T(8,128)(2,1)S(1)}, u32[]{:S(2)}, u32[]{:S(2)}) collective-permute-start(bf16[128,128]{1,0:T(8,128)(2,1)S(1)} %get-tuple-element.35), channel_id=1, source_target_pairs={{0,14},{1,15},{2,12},{3,13},{4,10},{5,11},{6,8},{7,9},{8,6},{9,7},... | collective-permute-start | bytes 98312 | tf_op jit(solution)/shard_map/ppermute | solution.py:174
  52.3 0.0 collective-permute-done.6.refs_3_
  52.3 1.3 %collective-permute-start.12 = (bf16[128,128]{1,0:T(8,128)(2,1)S(1)}, bf16[128,128]{1,0:T(8,128)(2,1)S(1)}, u32[]{:S(2)}, u32[]{:S(2)}) collective-permute-start(bf16[128,128]{1,0:T(8,128)(2,1)S(1)} %get-tuple-element.36), channel_id=1, source_target_pairs={{0,15},{1,12},{2,13},{3,14},{4,11},{5,8},{6,9},{7,10},{8,7},{9,4},... | collective-permute-start | bytes 98312 | tf_op jit(solution)/shard_map/ppermute | solution.py:174
  53.6 0.0 collective-permute-done.2.first_ref
  53.6 0.0 collective-permute-done.9.refs_4_
  53.6 0.0 copy-start.7
  53.6 0.0 collective-permute-done.10.refs_5_
  53.6 0.0 copy-start.8
  53.6 2.5 %collective-permute-done.11.refs_6_ = bf16[128,128]{1,0:T(8,128)(2,1)S(1)} collective-permute-done((bf16[128,128]{1,0:T(8,128)(2,1)S(1)}, bf16[128,128]{1,0:T(8,128)(2,1)S(1)}, u32[]{:S(2)}, u32[]{:S(2)}) %collective-permute-start.11) | collective-permute-done | bytes 32800 | tf_op jit(solution)/shard_map/ppermute | solution.py:174
  56.2 2.2 %collective-permute-done.12.refs_7_ = bf16[128,128]{1,0:T(8,128)(2,1)S(1)} collective-permute-done((bf16[128,128]{1,0:T(8,128)(2,1)S(1)}, bf16[128,128]{1,0:T(8,128)(2,1)S(1)}, u32[]{:S(2)}, u32[]{:S(2)}) %collective-permute-start.12) | collective-permute-done | bytes 32800 | tf_op jit(solution)/shard_map/ppermute | solution.py:174
  58.3 0.0 copy-done.6
  58.4 0.6 copy-done.10
  59.0 1.7 %shard_map.69 = f32[4,128,128]{2,1,0:T(8,128)} custom-call(s32[2]{0:T(128)} %copy-done.1, f32[128,128]{1,0:T(8,128)} %get-tuple-element.25.own_ref, f32[128,128]{1,0:T(8,128)} %copy-done.5, bf16[128,128]{1,0:T(8,128)(2,1)} %collective-permute-done.3.refs_0_, bf16[128,128]{1,0:T(8,128)(2,1)} %collective-permute-done.4.refs_1_, ...), custom_call_target="tpu_custom_call" | custom-call | tf_op jit(solution)/shard_map/pallas_call | solution.py:154
  (14 shorter events, 0.0 us)
Async XLA Ops:
  0.0 14.1 %collective-permute-start.1 = (bf16[128,2048]{1,0:T(8,128)(2,1)}, bf16[128,2048]{1,0:T(8,128)(2,1)S(1)}, u32[]{:S(2)}, u32[]{:S(2)}) collective-permute-start(bf16[128,2048]{1,0:T(8,128)(2,1)} %refs_0_.1), channel_id=1, source_target_pairs={{0,8},{12,4},{8,12},{4,0},{1,9},{13,5},{9,13},{5,1},{2,10},{14,6},... | collective-permute-start | bytes 1572872 | tf_op jit(solution)/shard_map/ppermute | solution.py:177
  3.8 1.6 %copy-start.2 = (bf16[512,2048]{1,0:T(8,128)(2,1)S(1)}, bf16[512,2048]{1,0:T(8,128)(2,1)}, u32[]{:S(2)}) copy-start(bf16[512,2048]{1,0:T(8,128)(2,1)} %query_ref.1) | copy-start | bytes 6291460
  5.4 1.6 %copy-start.3 = (bf16[4,512,512]{2,1,0:T(8,128)(2,1)S(1)}, bf16[4,512,512]{2,1,0:T(8,128)(2,1)}, u32[]{:S(2)}) copy-start(bf16[4,512,512]{2,1,0:T(8,128)(2,1)} %basis_ref.1) | copy-start | bytes 6291460
  7.0 0.7 %copy-start.4 = (f32[4,512]{1,0:T(4,128)S(1)}, f32[4,512]{1,0:T(4,128)}, u32[]{:S(2)}) copy-start(f32[4,512]{1,0:T(4,128)} %values_ref.1) | copy-start | bytes 24580
  7.7 3.7 %copy-start = (bf16[128,2048]{1,0:T(8,128)(2,1)S(1)}, bf16[128,2048]{1,0:T(8,128)(2,1)}, u32[]{:S(2)}) copy-start(bf16[128,2048]{1,0:T(8,128)(2,1)} %refs_0_.1) | copy-start | bytes 1572868
  7.7 9.2 %copy-start.11 = (s32[512]{0:T(512)S(1)}, s32[512]{0:T(512)}, u32[]{:S(2)}) copy-start(s32[512]{0:T(512)} %param.11) | copy-start | bytes 6148
  11.4 16.4 %collective-permute-start = (bf16[128,2048]{1,0:T(8,128)(2,1)S(1)}, bf16[128,2048]{1,0:T(8,128)(2,1)}, u32[]{:S(2)}, u32[]{:S(2)}) collective-permute-start(bf16[128,2048]{1,0:T(8,128)(2,1)S(1)} %copy-done), channel_id=1, source_target_pairs={{0,4},{12,8},{4,12},{8,0},{1,5},{13,9},{5,13},{9,1},{2,6},{14,10},... | collective-permute-start | bytes 1572872 | tf_op jit(solution)/shard_map/ppermute | solution.py:179
  14.1 26.3 %collective-permute-start.7 = (bf16[128,2048]{1,0:T(8,128)(2,1)S(1)}, bf16[128,2048]{1,0:T(8,128)(2,1)}, u32[]{:S(2)}, u32[]{:S(2)}) collective-permute-start(bf16[128,2048]{1,0:T(8,128)(2,1)S(1)} %collective-permute-done.1.refs_1_), channel_id=1, source_target_pairs={{8,12},{4,0},{9,13},{5,1},{10,14},{6,2},{11,15},{7,3},{24,28},{20,... | collective-permute-start | bytes 1572872 | tf_op jit(solution)/shard_map/ppermute | solution.py:181
  15.4 25.9 %collective-permute-start.8 = (bf16[128,2048]{1,0:T(8,128)(2,1)S(1)}, bf16[128,2048]{1,0:T(8,128)(2,1)}, u32[]{:S(2)}, u32[]{:S(2)}) collective-permute-start(bf16[128,2048]{1,0:T(8,128)(2,1)S(1)} %copy-done), channel_id=1, source_target_pairs={{4,8},{8,4},{5,9},{9,5},{6,10},{10,6},{7,11},{11,7},{20,24},{24,20... | collective-permute-start | bytes 1572872 | tf_op jit(solution)/shard_map/ppermute | solution.py:182
  17.1 27.7 %copy-start.1 = (s32[2]{0:T(128)}, s32[2]{0:T(128)S(1)}, u32[]{:S(2)}) copy-start(s32[2]{0:T(128)S(1)} %pad_add_fusion.place) | copy-start | bytes 28
  27.8 10.9 %all-to-all-start = ((bf16[4,128,256]{2,1,0:T(8,128)(2,1)}), bf16[4,128,256]{2,1,0:T(8,128)(2,1)}, u32[]{:S(2)}, u32[]{:S(2)}) async-start(bf16[4,128,256]{2,1,0:T(8,128)(2,1)} %shard_map.65), calls=%async_computation | async-start | bytes 524288 | tf_op jit(solution)/shard_map/all_to_all | solution.py:106
  34.9 11.1 %collective-permute-start.3 = (bf16[128,128]{1,0:T(8,128)(2,1)S(1)}, bf16[128,128]{1,0:T(8,128)(2,1)}, u32[]{:S(2)}, u32[]{:S(2)}) collective-permute-start(bf16[128,128]{1,0:T(8,128)(2,1)S(1)} %get-tuple-element.28), channel_id=1, source_target_pairs={{0,8},{1,9},{2,10},{3,11},{4,0},{5,1},{6,2},{7,3},{8,12},{9,13},{1... | collective-permute-start | bytes 98312 | tf_op jit(solution)/shard_map/ppermute | solution.py:174
  35.0 13.0 %collective-permute-start.4 = (bf16[128,128]{1,0:T(8,128)(2,1)S(1)}, bf16[128,128]{1,0:T(8,128)(2,1)}, u32[]{:S(2)}, u32[]{:S(2)}) collective-permute-start(bf16[128,128]{1,0:T(8,128)(2,1)S(1)} %get-tuple-element.29), channel_id=1, source_target_pairs={{0,9},{1,10},{2,11},{3,8},{4,1},{5,2},{6,3},{7,0},{8,13},{9,14},{1... | collective-permute-start | bytes 98312 | tf_op jit(solution)/shard_map/ppermute | solution.py:174
  38.7 11.4 %collective-permute-start.5 = (bf16[128,128]{1,0:T(8,128)(2,1)S(1)}, bf16[128,128]{1,0:T(8,128)(2,1)}, u32[]{:S(2)}, u32[]{:S(2)}) collective-permute-start(bf16[128,128]{1,0:T(8,128)(2,1)S(1)} %get-tuple-element.30), channel_id=1, source_target_pairs={{0,10},{1,11},{2,8},{3,9},{4,2},{5,3},{6,0},{7,1},{8,14},{9,15},{1... | collective-permute-start | bytes 98312 | tf_op jit(solution)/shard_map/ppermute | solution.py:174
  40.3 13.2 %collective-permute-start.2 = (f32[128,128]{1,0:T(8,128)}, f32[128,128]{1,0:T(8,128)S(1)}, u32[]{:S(2)}, u32[]{:S(2)}) collective-permute-start(f32[128,128]{1,0:T(8,128)} %get-tuple-element.26), channel_id=1, source_target_pairs={{0,4},{4,12},{8,0},{12,8},{1,5},{5,13},{9,1},{13,9},{2,6},{6,14},{... | collective-permute-start | bytes 196616 | tf_op jit(solution)/shard_map/ppermute | solution.py:188
  41.3 11.0 %collective-permute-start.6 = (bf16[128,128]{1,0:T(8,128)(2,1)S(1)}, bf16[128,128]{1,0:T(8,128)(2,1)S(1)}, u32[]{:S(2)}, u32[]{:S(2)}) collective-permute-start(bf16[128,128]{1,0:T(8,128)(2,1)S(1)} %get-tuple-element.31), channel_id=1, source_target_pairs={{0,11},{1,8},{2,9},{3,10},{4,3},{5,0},{6,1},{7,2},{8,15},{9,12},{1... | collective-permute-start | bytes 98312 | tf_op jit(solution)/shard_map/ppermute | solution.py:174
  46.0 7.5 %collective-permute-start.9 = (bf16[128,128]{1,0:T(8,128)(2,1)S(1)}, bf16[128,128]{1,0:T(8,128)(2,1)S(1)}, u32[]{:S(2)}, u32[]{:S(2)}) collective-permute-start(bf16[128,128]{1,0:T(8,128)(2,1)S(1)} %get-tuple-element.33), channel_id=1, source_target_pairs={{0,12},{1,13},{2,14},{3,15},{4,8},{5,9},{6,10},{7,11},{8,4},{9,5},... | collective-permute-start | bytes 98312 | tf_op jit(solution)/shard_map/ppermute | solution.py:174
  48.0 5.6 %collective-permute-start.10 = (bf16[128,128]{1,0:T(8,128)(2,1)S(1)}, bf16[128,128]{1,0:T(8,128)(2,1)S(1)}, u32[]{:S(2)}, u32[]{:S(2)}) collective-permute-start(bf16[128,128]{1,0:T(8,128)(2,1)S(1)} %get-tuple-element.34), channel_id=1, source_target_pairs={{0,13},{1,14},{2,15},{3,12},{4,9},{5,10},{6,11},{7,8},{8,5},{9,6},... | collective-permute-start | bytes 98312 | tf_op jit(solution)/shard_map/ppermute | solution.py:174
  50.1 6.0 %collective-permute-start.11 = (bf16[128,128]{1,0:T(8,128)(2,1)S(1)}, bf16[128,128]{1,0:T(8,128)(2,1)S(1)}, u32[]{:S(2)}, u32[]{:S(2)}) collective-permute-start(bf16[128,128]{1,0:T(8,128)(2,1)S(1)} %get-tuple-element.35), channel_id=1, source_target_pairs={{0,14},{1,15},{2,12},{3,13},{4,10},{5,11},{6,8},{7,9},{8,6},{9,7},... | collective-permute-start | bytes 98312 | tf_op jit(solution)/shard_map/ppermute | solution.py:174
  52.3 6.0 %copy-start.6 = (bf16[128,128]{1,0:T(8,128)(2,1)}, bf16[128,128]{1,0:T(8,128)(2,1)S(1)}, u32[]{:S(2)}) copy-start(bf16[128,128]{1,0:T(8,128)(2,1)S(1)} %collective-permute-done.6.refs_3_) | copy-start | bytes 98308
  52.3 6.0 %collective-permute-start.12 = (bf16[128,128]{1,0:T(8,128)(2,1)S(1)}, bf16[128,128]{1,0:T(8,128)(2,1)S(1)}, u32[]{:S(2)}, u32[]{:S(2)}) collective-permute-start(bf16[128,128]{1,0:T(8,128)(2,1)S(1)} %get-tuple-element.36), channel_id=1, source_target_pairs={{0,15},{1,12},{2,13},{3,14},{4,11},{5,8},{6,9},{7,10},{8,7},{9,4},... | collective-permute-start | bytes 98312 | tf_op jit(solution)/shard_map/ppermute | solution.py:174
  53.6 4.8 %copy-start.5 = (f32[128,128]{1,0:T(8,128)}, f32[128,128]{1,0:T(8,128)S(1)}, u32[]{:S(2)}) copy-start(f32[128,128]{1,0:T(8,128)S(1)} %collective-permute-done.2.first_ref) | copy-start | bytes 196612
  53.6 4.8 %copy-start.7 = (bf16[128,128]{1,0:T(8,128)(2,1)}, bf16[128,128]{1,0:T(8,128)(2,1)S(1)}, u32[]{:S(2)}) copy-start(bf16[128,128]{1,0:T(8,128)(2,1)S(1)} %collective-permute-done.9.refs_4_) | copy-start | bytes 98308
  53.6 4.7 %copy-start.8 = (bf16[128,128]{1,0:T(8,128)(2,1)}, bf16[128,128]{1,0:T(8,128)(2,1)S(1)}, u32[]{:S(2)}) copy-start(bf16[128,128]{1,0:T(8,128)(2,1)S(1)} %collective-permute-done.10.refs_5_) | copy-start | bytes 98308
  56.2 2.2 %copy-start.9 = (bf16[128,128]{1,0:T(8,128)(2,1)}, bf16[128,128]{1,0:T(8,128)(2,1)S(1)}, u32[]{:S(2)}) copy-start(bf16[128,128]{1,0:T(8,128)(2,1)S(1)} %collective-permute-done.11.refs_6_) | copy-start | bytes 98308
  58.3 0.6 %copy-start.10 = (bf16[128,128]{1,0:T(8,128)(2,1)}, bf16[128,128]{1,0:T(8,128)(2,1)S(1)}, u32[]{:S(2)}) copy-start(bf16[128,128]{1,0:T(8,128)(2,1)S(1)} %collective-permute-done.12.refs_7_) | copy-start | bytes 98308

commit v5 on v1

v5 whole, which is shorter than its diff:
```python
import functools

import jax
import jax.numpy as jnp
from jax import lax
from jax.experimental import pallas as pl
from jax.experimental.pallas import tpu as pltpu
from jax.sharding import PartitionSpec as P

LDIM = 512
LAY_DEV = 4
STEPS = 4
DAMPING = 0.05
NT = (((1,), (1,)), ((), ()))
MIB = 1024 * 1024


def prepare_kernel(
    place, offsets, documents_hbm, queries_hbm, bases_hbm, values_hbm, ids_ref,
    conditioned_ref, own_ref, documents, queries, bases, values, arrived,
):
    copies = [
        pltpu.make_async_copy(values_hbm, values, arrived.at[0]),
        pltpu.make_async_copy(documents_hbm, documents, arrived.at[1]),
    ]
    for layer in range(LAY_DEV):
        columns = queries_hbm.at[:, layer * LDIM : (layer + 1) * LDIM]
        copies.append(pltpu.make_async_copy(columns, queries.at[layer], arrived.at[2 + 2 * layer]))
        copies.append(pltpu.make_async_copy(bases_hbm.at[layer], bases.at[layer], arrived.at[3 + 2 * layer]))
    for copy in copies:
        copy.start()
    copies[0].wait()
    for layer in range(LAY_DEV):
        copies[2 + 2 * layer].wait()
        copies[3 + 2 * layer].wait()
        basis = bases[layer]
        projected = jnp.dot(queries[layer], basis, preferred_element_type=jnp.float32)
        scaled = (projected / (values[layer : layer + 1, :] + DAMPING)).astype(jnp.bfloat16)
        restored = lax.dot_general(scaled, basis, NT, preferred_element_type=jnp.float32)
        first = pl.multiple_of(offsets[layer] - place[0] * (LAY_DEV * LDIM), LDIM)
        conditioned_ref[:, pl.ds(first, LDIM)] = restored.astype(jnp.bfloat16)
    copies[1].wait()
    tile = masked_tile(conditioned_ref, documents, ids_ref, place[1])
    shares, share_rows = own_ref.shape[:2]
    for share in range(shares):
        own_ref[share] = tile[share * share_rows : (share + 1) * share_rows].astype(jnp.bfloat16)


def prepare(documents, queries, bases, values, offsets, query_ids, place, shares):
    rows, dims = queries.shape
    docs = documents.shape[0]
    smem = pl.BlockSpec(memory_space=pltpu.SMEM)
    hbm = pl.BlockSpec(memory_space=pltpu.HBM)
    vmem = pl.BlockSpec(memory_space=pltpu.VMEM)
    return pl.pallas_call(
        prepare_kernel,
        out_shape=[
            jax.ShapeDtypeStruct((rows, dims), jnp.bfloat16),
            jax.ShapeDtypeStruct((shares, rows // shares, docs), jnp.bfloat16),
        ],
        in_specs=[smem, smem, hbm, hbm, hbm, hbm, vmem],
        out_specs=[vmem, vmem],
        scratch_shapes=[
            pltpu.VMEM(documents.shape, jnp.bfloat16),
            pltpu.VMEM((LAY_DEV, rows, LDIM), jnp.bfloat16),
            pltpu.VMEM(bases.shape, jnp.bfloat16),
            pltpu.VMEM(values.shape, jnp.float32),
            pltpu.SemaphoreType.DMA((2 + 2 * LAY_DEV,)),
        ],
        compiler_params=pltpu.CompilerParams(vmem_limit_bytes=62 * MIB),
        cost_estimate=pl.CostEstimate(
            flops=2 * rows * dims * (2 * LDIM + docs), bytes_accessed=6 * MIB, transcendentals=0
        ),
    )(place, offsets, documents, queries, bases, values, query_ids)


def masked_tile(queries_ref, documents, ids_ref, block):
    tile = lax.dot_general(queries_ref[...], documents[...], NT, preferred_element_type=jnp.float32)
    doc_ids = block * tile.shape[1] + lax.broadcasted_iota(jnp.int32, tile.shape, 1)
    return jnp.where(ids_ref[...] == doc_ids, 0.0, tile)


def score_kernel(shares, block_of, place, queries_ref, ids_ref, *refs):
    *document_refs, held = refs[: -1 - shares] + refs[-1:]
    out_refs = refs[-1 - shares : -1]
    documents = document_refs[0][...]
    for document_ref in document_refs[1:]:
        documents = documents + document_ref[...]
    held[...] = masked_tile(queries_ref, documents, ids_ref, block_of(place[1]))
    share_rows = out_refs[0].shape[0]
    for turn in range(shares):
        first = pl.multiple_of(lax.rem(place[0] + turn, shares) * share_rows, share_rows)
        out_refs[turn][...] = held[pl.ds(first, share_rows), :].astype(jnp.bfloat16)


def partial_scores(conditioned, query_ids, documents, block_of, place, shares):
    rows, dims = conditioned.shape
    docs = documents[0].shape[0]
    vmem = pl.BlockSpec(memory_space=pltpu.VMEM)
    return pl.pallas_call(
        functools.partial(score_kernel, shares, block_of),
        out_shape=[jax.ShapeDtypeStruct((rows // shares, docs), jnp.bfloat16)] * shares,
        in_specs=[pl.BlockSpec(memory_space=pltpu.SMEM)] + [vmem] * (2 + len(documents)),
        out_specs=[vmem] * shares,
        scratch_shapes=[pltpu.VMEM((rows, docs), jnp.float32)],
        compiler_params=pltpu.CompilerParams(vmem_limit_bytes=12 * MIB),
        cost_estimate=pl.CostEstimate(
            flops=2 * rows * docs * dims, bytes_accessed=2 * dims * (rows + docs), transcendentals=0
        ),
    )(place, conditioned, query_ids, *documents)


ROUND_ONE = ((0, 2), (3, 1), (2, 3), (1, 0))
ROUND_TWO = ((0, 1), (3, 2), (1, 3), (2, 0))
ROUND_INNER = ((1, 2), (2, 1))
ROUND_OUTER = ((2, 3), (1, 0))
BLOCK_ONE = (1, 3, 0, 2)
BLOCK_TWO = (2, 0, 3, 1)
BLOCK_LAST = (3, 2, 1, 0)


def pick(table):
    def entry(row):
        value = jnp.int32(table[0])
        for index in range(1, len(table)):
            value = jnp.where(row == index, jnp.int32(table[index]), value)
        return value

    return entry


def step_of(table):
    return pick([(block - table.index(block)) % STEPS for block in range(STEPS)])


def final_kernel(tables, place, own_ref, *refs):
    *late_refs, out_ref = refs
    shares = own_ref.shape[0]
    total = own_ref[0].astype(jnp.float32)
    for share in range(1, shares):
        total += own_ref[share].astype(jnp.float32)
    out_ref[0] = total
    for spot, step_at in enumerate(tables):
        total = late_refs[spot * shares][...].astype(jnp.float32)
        for late_ref in late_refs[spot * shares + 1 : (spot + 1) * shares]:
            total += late_ref[...].astype(jnp.float32)
        out_ref[step_at(place[1])] = total


def final_scores(place, own, late, tables):
    vmem = pl.BlockSpec(memory_space=pltpu.VMEM)
    return pl.pallas_call(
        functools.partial(final_kernel, tables),
        out_shape=jax.ShapeDtypeStruct((STEPS,) + own.shape[1:], jnp.float32),
        in_specs=[pl.BlockSpec(memory_space=pltpu.SMEM)] + [vmem] * (1 + len(late)),
        out_specs=vmem,
        compiler_params=pltpu.CompilerParams(vmem_limit_bytes=4 * MIB),
    )(place, own, *late)


def exchange(tiles, target_of):
    n_rows, shares = lax.axis_size("rows"), lax.axis_size("layer")
    arrived = []
    for turn, tile in enumerate(tiles):
        pairs = [
            (row * shares + lay, target_of(row) * shares + (lay + turn) % shares)
            for row in range(n_rows)
            for lay in range(shares)
        ]
        arrived.append(lax.ppermute(tile, ("rows", "layer"), pairs))
    return arrived


def along_line(documents, conditioned, own, query_ids, place, shares):
    def scored(blocks, table):
        return partial_scores(conditioned, query_ids, blocks, pick(table), place, shares)

    one = lax.ppermute(documents, "rows", ROUND_ONE)
    later, conditioned = lax.optimization_barrier((documents, conditioned))
    two = lax.ppermute(later, "rows", ROUND_TWO)
    later, one, own = lax.optimization_barrier((later, one, own))
    outer = lax.ppermute(one, "rows", ROUND_OUTER)
    inner = lax.ppermute(later, "rows", ROUND_INNER)

    first = exchange(scored([one], BLOCK_ONE), BLOCK_ONE.__getitem__)
    second = exchange(scored([two], BLOCK_TWO), BLOCK_TWO.__getitem__)
    last = exchange(scored([outer, inner], BLOCK_LAST), BLOCK_LAST.__getitem__)
    return own, first + second + last, [step_of(table) for table in (BLOCK_ONE, BLOCK_TWO, BLOCK_LAST)]


def around_ring(documents, conditioned, own, query_ids, place, shares):
    n_rows = lax.axis_size("rows")
    late = []
    for step in range(1, STEPS):
        back = [(row, (row - step) % n_rows) for row in range(n_rows)]
        block = lax.ppermute(documents, "rows", back)

        def ahead(row, step=step):
            return lax.rem(row + step, n_rows)

        tiles = partial_scores(conditioned, query_ids, [block], ahead, place, shares)
        late += exchange(tiles, lambda row, step=step: (row + step) % n_rows)
    return own, late, [lambda row, step=step: step for step in range(1, STEPS)]


def local(train_grads, query_grads, eigenbases, eigenvalues, layer_offsets, query_doc_ids):
    shares = lax.axis_size("layer")
    place = jnp.stack([lax.axis_index("layer"), lax.axis_index("rows")]).astype(jnp.int32)
    query_ids = query_doc_ids[:, None]
    conditioned, own = prepare(
        train_grads, query_grads, eigenbases, eigenvalues, layer_offsets, query_ids, place, shares
    )
    own = lax.all_to_all(own, "layer", 0, 0, tiled=True)
    plan = along_line if lax.axis_size("rows") == STEPS else around_ring
    own, late, tables = plan(train_grads, conditioned, own, query_ids, place, shares)
    return final_scores(place, own, late, tables)


def solution(mesh):
    in_specs = (
        P(("group", "rows"), "layer"),
        P(("group", "rows"), "layer"),
        P("layer", None, None),
        P("layer", None),
        P("layer"),
        P(("group", "rows")),
    )
    out_specs = P(None, "layer", ("group", "rows"))
    return jax.shard_map(local, mesh=mesh, in_specs=in_specs, out_specs=out_specs, check_vma=False)
```

time: 76.9 us -> 66.3 us (0.86)
  the two profiles are of different devices: /device:TPU:0 before, /device:TPU:1 now
where the time goes in v5:
time: 66.3 us; the launch traced here: 66 us
  starting transfers between devices  29.5 us (44%)
  waiting for transfers between devices  19.7 us (30%)
  Pallas kernels  13 us (20%)
  local copies, waits for them, and re-layouts  3.13 us (5%)
    ppermute x12, starting transfers between devices, exchange(): arrived.append(lax.ppermute(tile, ('rows', 'layer'), pairs))  20.1 us
    ppermute x12, waiting for transfers between devices, exchange(): arrived.append(lax.ppermute(tile, ('rows', 'layer'), pairs))  15.1 us
    pallas_call x1, Pallas kernels, prepare(): pl.pallas_call(prepare_kernel, out_shape=[jax.ShapeDtypeStruct((rows, dim...  7.77 us
    all_to_all x1, starting transfers between devices, local(): own = lax.all_to_all(own, 'layer', 0, 0, tiled=True)  4.26 us
    pallas_call x3, Pallas kernels, partial_scores(): pl.pallas_call(functools.partial(score_kernel, shares, block_of), out_sha...  3.91 us
    all_to_all x1, waiting for transfers between devices, local(): own = lax.all_to_all(own, 'layer', 0, 0, tiled=True)  3.59 us
    ppermute x1, starting transfers between devices, along_line(): one = lax.ppermute(documents, 'rows', ROUND_ONE)  3.14 us
    unnamed x8, local copies, waits for them, and re-layouts  1.6 us
  transfers between devices with their start and end apart: 17, of which 7 were waited for; matrix products, arithmetic and copies ran while one was open for 3% of the time, Pallas kernels for 18%

profile of v5, /device:TPU:1, one launch (start us, length us, event | category | flops | bytes accessed | tf_op | source)
XLA Modules:
  0.0 66.0 jit_solution(10524424750080283542)
XLA Ops:
  0.0 3.1 %collective-permute-start = (bf16[128,2048]{1,0:T(8,128)(2,1)}, bf16[128,2048]{1,0:T(8,128)(2,1)S(1)}, u32[]{:S(2)}, u32[]{:S(2)}) collective-permute-start(bf16[128,2048]{1,0:T(8,128)(2,1)} %documents_hbm.1), channel_id=1, source_target_pairs={{0,8},{12,4},{8,12},{4,0},{1,9},{13,5},{9,13},{5,1},{2,10},{14,6},... | collective-permute-start | bytes 1572872 | tf_op jit(solution)/shard_map/ppermute | solution.py:178
  3.1 1.5 %copy.7.ids_ref = s32[512,1]{1,0:T(8,128)} copy(s32[512,1]{0,1:T(1,128)} %bitcast.3) | data formatting | bytes 4096 | tf_op jit(solution)/shard_map/broadcast_in_dim | solution.py:209
  4.7 0.6 pad_add_fusion.place
  5.3 0.0 copy-start.3
  5.3 0.0 copy-start.1
  5.3 7.8 %shard_map.64 = (bf16[512,2048]{1,0:T(8,128)(2,1)}, bf16[4,128,128]{2,1,0:T(8,128)(2,1)}) custom-call(s32[2]{0:T(128)} %pad_add_fusion.place, s32[4]{0:T(128)} %offsets.1, bf16[128,2048]{1,0:T(8,128)(2,1)} %documents_hbm.1, bf16[512,2048]{1,0:T(8,128)(2,1)} %queries_hbm.1, bf16[4,512,512]{2,1,0:T(8,128)(2,1)} %bases_hbm.1, f32[4,512]{1,0:T(4,128)} %values_hbm.1, ...), custom_call_target="tpu_custom_call" | custom-call | flops 2415919104 | bytes 6291456 | tf_op jit(solution)/shard_map/pallas_call | solution.py:55
  13.0 4.3 %all-to-all-start = ((bf16[4,128,128]{2,1,0:T(8,128)(2,1)}), bf16[4,128,128]{2,1,0:T(8,128)(2,1)S(1)}, u32[]{:S(2)}, u32[]{:S(2)}) async-start(bf16[4,128,128]{2,1,0:T(8,128)(2,1)} %get-tuple-element.26), calls=%async_computation | async-start | bytes 262144 | tf_op jit(solution)/shard_map/all_to_all | solution.py:213
  17.3 0.0 copy-done.3
  17.3 0.0 collective-permute-start.5
  17.3 3.6 %all-to-all-done.own_ref = bf16[4,128,128]{2,1,0:T(8,128)(2,1)S(1)} async-done(((bf16[4,128,128]{2,1,0:T(8,128)(2,1)}), bf16[4,128,128]{2,1,0:T(8,128)(2,1)S(1)}, u32[]{:S(2)}, u32[]{:S(2)}) %all-to-all-start) | async-done | bytes 131104 | tf_op jit(solution)/shard_map/all_to_all | solution.py:213
  20.9 0.0 collective-permute-done.refs_0_
  20.9 1.3 %collective-permute-start.10 = (bf16[128,2048]{1,0:T(8,128)(2,1)S(1)}, bf16[128,2048]{1,0:T(8,128)(2,1)S(1)}, u32[]{:S(2)}, u32[]{:S(2)}) collective-permute-start(bf16[128,2048]{1,0:T(8,128)(2,1)S(1)} %collective-permute-done.refs_0_), channel_id=1, source_target_pairs={{8,12},{4,0},{9,13},{5,1},{10,14},{6,2},{11,15},{7,3},{24,28},{20,... | collective-permute-start | bytes 1572872 | tf_op jit(solution)/shard_map/ppermute | solution.py:182
  22.2 0.7 %collective-permute-start.11 = (bf16[128,2048]{1,0:T(8,128)(2,1)S(1)}, bf16[128,2048]{1,0:T(8,128)(2,1)S(1)}, u32[]{:S(2)}, u32[]{:S(2)}) collective-permute-start(bf16[128,2048]{1,0:T(8,128)(2,1)S(1)} %copy-done.3), channel_id=1, source_target_pairs={{4,8},{8,4},{5,9},{9,5},{6,10},{10,6},{7,11},{11,7},{20,24},{24,20... | collective-permute-start | bytes 1572872 | tf_op jit(solution)/shard_map/ppermute | solution.py:183
  22.9 0.0 copy-done.1
  22.9 0.0 copy-done.2
  22.9 0.0 copy-start
  22.9 1.6 %copy-done = bf16[512,2048]{1,0:T(8,128)(2,1)S(1)} copy-done((bf16[512,2048]{1,0:T(8,128)(2,1)S(1)}, bf16[512,2048]{1,0:T(8,128)(2,1)}, u32[]{:S(2)}) %copy-start) | copy-done | bytes 2097176
  24.5 1.3 %shard_map.65 = (bf16[128,128]{1,0:T(8,128)(2,1)S(1)}, bf16[128,128]{1,0:T(8,128)(2,1)S(1)}, bf16[128,128]{1,0:T(8,128)(2,1)S(1)}, bf16[128,128]{1,0:T(8,128)(2,1)S(1)}) custom-call(s32[2]{0:T(128)S(1)} %copy-done.2, bf16[512,2048]{1,0:T(8,128)(2,1)S(1)} %copy-done, s32[512,1]{1,0:T(8,128)S(1)} %copy-done.1, bf16[128,2048]{1,0:T(8,128)(2,1)S(1)} %collective-permute-done.refs_0_), custom_call_target="tpu_custom_call" | custom-call | flops 268435456 | bytes 2621440 | tf_op jit(solution)/shard_map/pallas_call | solution.py:100
  25.8 3.5 %collective-permute-start.1 = (bf16[128,128]{1,0:T(8,128)(2,1)S(1)}, bf16[128,128]{1,0:T(8,128)(2,1)S(1)}, u32[]{:S(2)}, u32[]{:S(2)}) collective-permute-start(bf16[128,128]{1,0:T(8,128)(2,1)S(1)} %get-tuple-element.30), channel_id=1, source_target_pairs={{0,4},{1,5},{2,6},{3,7},{4,12},{5,13},{6,14},{7,15},{8,0},{9,1},{1... | collective-permute-start | bytes 98312 | tf_op jit(solution)/shard_map/ppermute | solution.py:170
  29.4 1.3 %collective-permute-start.2 = (bf16[128,128]{1,0:T(8,128)(2,1)S(1)}, bf16[128,128]{1,0:T(8,128)(2,1)S(1)}, u32[]{:S(2)}, u32[]{:S(2)}) collective-permute-start(bf16[128,128]{1,0:T(8,128)(2,1)S(1)} %get-tuple-element.31), channel_id=1, source_target_pairs={{0,5},{1,6},{2,7},{3,4},{4,13},{5,14},{6,15},{7,12},{8,1},{9,2},{1... | collective-permute-start | bytes 98312 | tf_op jit(solution)/shard_map/ppermute | solution.py:170
  30.7 1.0 %collective-permute-done.5.refs_0_ = bf16[128,2048]{1,0:T(8,128)(2,1)S(1)} collective-permute-done((bf16[128,2048]{1,0:T(8,128)(2,1)S(1)}, bf16[128,2048]{1,0:T(8,128)(2,1)S(1)}, u32[]{:S(2)}, u32[]{:S(2)}) %collective-permute-start.5) | collective-permute-done | bytes 524320 | tf_op jit(solution)/shard_map/ppermute | solution.py:180
  31.7 2.8 %collective-permute-start.3 = (bf16[128,128]{1,0:T(8,128)(2,1)S(1)}, bf16[128,128]{1,0:T(8,128)(2,1)S(1)}, u32[]{:S(2)}, u32[]{:S(2)}) collective-permute-start(bf16[128,128]{1,0:T(8,128)(2,1)S(1)} %get-tuple-element.32), channel_id=1, source_target_pairs={{0,6},{1,7},{2,4},{3,5},{4,14},{5,15},{6,12},{7,13},{8,2},{9,3},{1... | collective-permute-start | bytes 98312 | tf_op jit(solution)/shard_map/ppermute | solution.py:170
  34.5 1.3 %shard_map.66 = (bf16[128,128]{1,0:T(8,128)(2,1)S(1)}, bf16[128,128]{1,0:T(8,128)(2,1)S(1)}, bf16[128,128]{1,0:T(8,128)(2,1)S(1)}, bf16[128,128]{1,0:T(8,128)(2,1)S(1)}) custom-call(s32[2]{0:T(128)S(1)} %copy-done.2, bf16[512,2048]{1,0:T(8,128)(2,1)S(1)} %copy-done, s32[512,1]{1,0:T(8,128)S(1)} %copy-done.1, bf16[128,2048]{1,0:T(8,128)(2,1)S(1)} %collective-permute-done.5.refs_0_), custom_call_target="tpu_custom_call" | custom-call | flops 268435456 | bytes 2621440 | tf_op jit(solution)/shard_map/pallas_call | solution.py:100
  35.8 7.6 %collective-permute-done.1.refs_0_ = bf16[128,128]{1,0:T(8,128)(2,1)S(1)} collective-permute-done((bf16[128,128]{1,0:T(8,128)(2,1)S(1)}, bf16[128,128]{1,0:T(8,128)(2,1)S(1)}, u32[]{:S(2)}, u32[]{:S(2)}) %collective-permute-start.1) | collective-permute-done | bytes 32800 | tf_op jit(solution)/shard_map/ppermute | solution.py:170
  43.4 0.0 collective-permute-start.4
  43.4 1.8 %collective-permute-done.2.refs_1_ = bf16[128,128]{1,0:T(8,128)(2,1)S(1)} collective-permute-done((bf16[128,128]{1,0:T(8,128)(2,1)S(1)}, bf16[128,128]{1,0:T(8,128)(2,1)S(1)}, u32[]{:S(2)}, u32[]{:S(2)}) %collective-permute-start.2) | collective-permute-done | bytes 32800 | tf_op jit(solution)/shard_map/ppermute | solution.py:170
  45.1 2.1 %collective-permute-start.6 = (bf16[128,128]{1,0:T(8,128)(2,1)S(1)}, bf16[128,128]{1,0:T(8,128)(2,1)S(1)}, u32[]{:S(2)}, u32[]{:S(2)}) collective-permute-start(bf16[128,128]{1,0:T(8,128)(2,1)S(1)} %get-tuple-element.34), channel_id=1, source_target_pairs={{0,8},{1,9},{2,10},{3,11},{4,0},{5,1},{6,2},{7,3},{8,12},{9,13},{1... | collective-permute-start | bytes 98312 | tf_op jit(solution)/shard_map/ppermute | solution.py:170
  47.3 0.0 collective-permute-done.10.refs_0_
  47.3 0.6 collective-permute-start.7
  47.9 0.0 collective-permute-done.11.refs_1_
  47.9 1.5 %collective-permute-start.8 = (bf16[128,128]{1,0:T(8,128)(2,1)S(1)}, bf16[128,128]{1,0:T(8,128)(2,1)S(1)}, u32[]{:S(2)}, u32[]{:S(2)}) collective-permute-start(bf16[128,128]{1,0:T(8,128)(2,1)S(1)} %get-tuple-element.36), channel_id=1, source_target_pairs={{0,10},{1,11},{2,8},{3,9},{4,2},{5,3},{6,0},{7,1},{8,14},{9,15},{1... | collective-permute-start | bytes 98312 | tf_op jit(solution)/shard_map/ppermute | solution.py:170
  49.3 1.3 %shard_map.67 = (bf16[128,128]{1,0:T(8,128)(2,1)S(1)}, bf16[128,128]{1,0:T(8,128)(2,1)S(1)}, bf16[128,128]{1,0:T(8,128)(2,1)S(1)}, bf16[128,128]{1,0:T(8,128)(2,1)S(1)}) custom-call(s32[2]{0:T(128)S(1)} %copy-done.2, bf16[512,2048]{1,0:T(8,128)(2,1)S(1)} %copy-done, s32[512,1]{1,0:T(8,128)S(1)} %copy-done.1, ...), custom_call_target="tpu_custom_call" | custom-call | flops 268435456 | bytes 2621440 | tf_op jit(solution)/shard_map/pallas_call | solution.py:100
  50.6 0.0 collective-permute-done.3.refs_2_
  50.7 1.4 %collective-permute-start.9 = (bf16[128,128]{1,0:T(8,128)(2,1)S(1)}, bf16[128,128]{1,0:T(8,128)(2,1)S(1)}, u32[]{:S(2)}, u32[]{:S(2)}) collective-permute-start(bf16[128,128]{1,0:T(8,128)(2,1)S(1)} %get-tuple-element.37), channel_id=1, source_target_pairs={{0,11},{1,8},{2,9},{3,10},{4,3},{5,0},{6,1},{7,2},{8,15},{9,12},{1... | collective-permute-start | bytes 98312 | tf_op jit(solution)/shard_map/ppermute | solution.py:170
  52.1 0.0 collective-permute-done.4.refs_3_
  52.1 2.1 %collective-permute-start.12 = (bf16[128,128]{1,0:T(8,128)(2,1)S(1)}, bf16[128,128]{1,0:T(8,128)(2,1)S(1)}, u32[]{:S(2)}, u32[]{:S(2)}) collective-permute-start(bf16[128,128]{1,0:T(8,128)(2,1)S(1)} %get-tuple-element.39), channel_id=1, source_target_pairs={{0,12},{1,13},{2,14},{3,15},{4,8},{5,9},{6,10},{7,11},{8,4},{9,5},... | collective-permute-start | bytes 98312 | tf_op jit(solution)/shard_map/ppermute | solution.py:170
  54.1 0.0 collective-permute-done.6.refs_4_
  54.1 2.4 %collective-permute-start.13 = (bf16[128,128]{1,0:T(8,128)(2,1)S(1)}, bf16[128,128]{1,0:T(8,128)(2,1)S(1)}, u32[]{:S(2)}, u32[]{:S(2)}) collective-permute-start(bf16[128,128]{1,0:T(8,128)(2,1)S(1)} %get-tuple-element.40), channel_id=1, source_target_pairs={{0,13},{1,14},{2,15},{3,12},{4,9},{5,10},{6,11},{7,8},{8,5},{9,6},... | collective-permute-start | bytes 98312 | tf_op jit(solution)/shard_map/ppermute | solution.py:170
  56.6 0.0 collective-permute-done.7.refs_5_
  56.6 2.1 %collective-permute-start.14 = (bf16[128,128]{1,0:T(8,128)(2,1)S(1)}, bf16[128,128]{1,0:T(8,128)(2,1)S(1)}, u32[]{:S(2)}, u32[]{:S(2)}) collective-permute-start(bf16[128,128]{1,0:T(8,128)(2,1)S(1)} %get-tuple-element.41), channel_id=1, source_target_pairs={{0,14},{1,15},{2,12},{3,13},{4,10},{5,11},{6,8},{7,9},{8,6},{9,7},... | collective-permute-start | bytes 98312 | tf_op jit(solution)/shard_map/ppermute | solution.py:170
  58.6 0.0 collective-permute-done.8.refs_6_
  58.6 0.3 collective-permute-start.15
  58.9 0.0 collective-permute-done.9.refs_7_
  58.9 0.0 collective-permute-done.12.refs_8_
  58.9 0.5 collective-permute-done.13.refs_9_
  59.4 2.6 %collective-permute-done.14.refs_10_ = bf16[128,128]{1,0:T(8,128)(2,1)S(1)} collective-permute-done((bf16[128,128]{1,0:T(8,128)(2,1)S(1)}, bf16[128,128]{1,0:T(8,128)(2,1)S(1)}, u32[]{:S(2)}, u32[]{:S(2)}) %collective-permute-start.14) | collective-permute-done | bytes 32800 | tf_op jit(solution)/shard_map/ppermute | solution.py:170
  62.0 2.6 %collective-permute-done.15.refs_11_ = bf16[128,128]{1,0:T(8,128)(2,1)S(1)} collective-permute-done((bf16[128,128]{1,0:T(8,128)(2,1)S(1)}, bf16[128,128]{1,0:T(8,128)(2,1)S(1)}, u32[]{:S(2)}, u32[]{:S(2)}) %collective-permute-start.15) | collective-permute-done | bytes 32800 | tf_op jit(solution)/shard_map/ppermute | solution.py:170
  64.7 1.3 %shard_map.68 = f32[4,128,128]{2,1,0:T(8,128)} custom-call(s32[2]{0:T(128)S(1)} %copy-done.2, bf16[4,128,128]{2,1,0:T(8,128)(2,1)S(1)} %all-to-all-done.own_ref, bf16[128,128]{1,0:T(8,128)(2,1)S(1)} %collective-permute-done.1.refs_0_, bf16[128,128]{1,0:T(8,128)(2,1)S(1)} %collective-permute-done.2.refs_1_, ...), custom_call_target="tpu_custom_call" | custom-call | tf_op jit(solution)/shard_map/pallas_call | solution.py:152
  (1 shorter events, 0.0 us)
Async XLA Ops:
  0.0 20.9 %collective-permute-start = (bf16[128,2048]{1,0:T(8,128)(2,1)}, bf16[128,2048]{1,0:T(8,128)(2,1)S(1)}, u32[]{:S(2)}, u32[]{:S(2)}) collective-permute-start(bf16[128,2048]{1,0:T(8,128)(2,1)} %documents_hbm.1), channel_id=1, source_target_pairs={{0,8},{12,4},{8,12},{4,0},{1,9},{13,5},{9,13},{5,1},{2,10},{14,6},... | collective-permute-start | bytes 1572872 | tf_op jit(solution)/shard_map/ppermute | solution.py:178
  5.3 12.0 %copy-start.3 = (bf16[128,2048]{1,0:T(8,128)(2,1)S(1)}, bf16[128,2048]{1,0:T(8,128)(2,1)}, u32[]{:S(2)}) copy-start(bf16[128,2048]{1,0:T(8,128)(2,1)} %documents_hbm.1) | copy-start | bytes 1572868
  5.3 17.6 %copy-start.1 = (s32[512,1]{1,0:T(8,128)S(1)}, s32[512,1]{1,0:T(8,128)}, u32[]{:S(2)}) copy-start(s32[512,1]{1,0:T(8,128)} %copy.7.ids_ref) | copy-start | bytes 6148
  5.3 17.6 %copy-start.2 = (s32[2]{0:T(128)S(1)}, s32[2]{0:T(128)}, u32[]{:S(2)}) copy-start(s32[2]{0:T(128)} %pad_add_fusion.place) | copy-start | bytes 28
  13.0 7.9 %all-to-all-start = ((bf16[4,128,128]{2,1,0:T(8,128)(2,1)}), bf16[4,128,128]{2,1,0:T(8,128)(2,1)S(1)}, u32[]{:S(2)}, u32[]{:S(2)}) async-start(bf16[4,128,128]{2,1,0:T(8,128)(2,1)} %get-tuple-element.26), calls=%async_computation | async-start | bytes 262144 | tf_op jit(solution)/shard_map/all_to_all | solution.py:213
  17.3 14.4 %collective-permute-start.5 = (bf16[128,2048]{1,0:T(8,128)(2,1)S(1)}, bf16[128,2048]{1,0:T(8,128)(2,1)S(1)}, u32[]{:S(2)}, u32[]{:S(2)}) collective-permute-start(bf16[128,2048]{1,0:T(8,128)(2,1)S(1)} %copy-done.3), channel_id=1, source_target_pairs={{0,4},{12,8},{4,12},{8,0},{1,5},{13,9},{5,13},{9,1},{2,6},{14,10},... | collective-permute-start | bytes 1572872 | tf_op jit(solution)/shard_map/ppermute | solution.py:180
  20.9 26.4 %collective-permute-start.10 = (bf16[128,2048]{1,0:T(8,128)(2,1)S(1)}, bf16[128,2048]{1,0:T(8,128)(2,1)S(1)}, u32[]{:S(2)}, u32[]{:S(2)}) collective-permute-start(bf16[128,2048]{1,0:T(8,128)(2,1)S(1)} %collective-permute-done.refs_0_), channel_id=1, source_target_pairs={{8,12},{4,0},{9,13},{5,1},{10,14},{6,2},{11,15},{7,3},{24,28},{20,... | collective-permute-start | bytes 1572872 | tf_op jit(solution)/shard_map/ppermute | solution.py:182
  22.2 25.7 %collective-permute-start.11 = (bf16[128,2048]{1,0:T(8,128)(2,1)S(1)}, bf16[128,2048]{1,0:T(8,128)(2,1)S(1)}, u32[]{:S(2)}, u32[]{:S(2)}) collective-permute-start(bf16[128,2048]{1,0:T(8,128)(2,1)S(1)} %copy-done.3), channel_id=1, source_target_pairs={{4,8},{8,4},{5,9},{9,5},{6,10},{10,6},{7,11},{11,7},{20,24},{24,20... | collective-permute-start | bytes 1572872 | tf_op jit(solution)/shard_map/ppermute | solution.py:183
  22.9 1.6 %copy-start = (bf16[512,2048]{1,0:T(8,128)(2,1)S(1)}, bf16[512,2048]{1,0:T(8,128)(2,1)}, u32[]{:S(2)}) copy-start(bf16[512,2048]{1,0:T(8,128)(2,1)} %get-tuple-element.28.queries_ref) | copy-start | bytes 6291460
  25.8 17.6 %collective-permute-start.1 = (bf16[128,128]{1,0:T(8,128)(2,1)S(1)}, bf16[128,128]{1,0:T(8,128)(2,1)S(1)}, u32[]{:S(2)}, u32[]{:S(2)}) collective-permute-start(bf16[128,128]{1,0:T(8,128)(2,1)S(1)} %get-tuple-element.30), channel_id=1, source_target_pairs={{0,4},{1,5},{2,6},{3,7},{4,12},{5,13},{6,14},{7,15},{8,0},{9,1},{1... | collective-permute-start | bytes 98312 | tf_op jit(solution)/shard_map/ppermute | solution.py:170
  29.4 15.8 %collective-permute-start.2 = (bf16[128,128]{1,0:T(8,128)(2,1)S(1)}, bf16[128,128]{1,0:T(8,128)(2,1)S(1)}, u32[]{:S(2)}, u32[]{:S(2)}) collective-permute-start(bf16[128,128]{1,0:T(8,128)(2,1)S(1)} %get-tuple-element.31), channel_id=1, source_target_pairs={{0,5},{1,6},{2,7},{3,4},{4,13},{5,14},{6,15},{7,12},{8,1},{9,2},{1... | collective-permute-start | bytes 98312 | tf_op jit(solution)/shard_map/ppermute | solution.py:170
  31.7 18.9 %collective-permute-start.3 = (bf16[128,128]{1,0:T(8,128)(2,1)S(1)}, bf16[128,128]{1,0:T(8,128)(2,1)S(1)}, u32[]{:S(2)}, u32[]{:S(2)}) collective-permute-start(bf16[128,128]{1,0:T(8,128)(2,1)S(1)} %get-tuple-element.32), channel_id=1, source_target_pairs={{0,6},{1,7},{2,4},{3,5},{4,14},{5,15},{6,12},{7,13},{8,2},{9,3},{1... | collective-permute-start | bytes 98312 | tf_op jit(solution)/shard_map/ppermute | solution.py:170
  43.4 8.7 %collective-permute-start.4 = (bf16[128,128]{1,0:T(8,128)(2,1)S(1)}, bf16[128,128]{1,0:T(8,128)(2,1)S(1)}, u32[]{:S(2)}, u32[]{:S(2)}) collective-permute-start(bf16[128,128]{1,0:T(8,128)(2,1)S(1)} %get-tuple-element.33), channel_id=1, source_target_pairs={{0,7},{1,4},{2,5},{3,6},{4,15},{5,12},{6,13},{7,14},{8,3},{9,0},{1... | collective-permute-start | bytes 98312 | tf_op jit(solution)/shard_map/ppermute | solution.py:170
  45.1 9.0 %collective-permute-start.6 = (bf16[128,128]{1,0:T(8,128)(2,1)S(1)}, bf16[128,128]{1,0:T(8,128)(2,1)S(1)}, u32[]{:S(2)}, u32[]{:S(2)}) collective-permute-start(bf16[128,128]{1,0:T(8,128)(2,1)S(1)} %get-tuple-element.34), channel_id=1, source_target_pairs={{0,8},{1,9},{2,10},{3,11},{4,0},{5,1},{6,2},{7,3},{8,12},{9,13},{1... | collective-permute-start | bytes 98312 | tf_op jit(solution)/shard_map/ppermute | solution.py:170
  47.3 9.3 %collective-permute-start.7 = (bf16[128,128]{1,0:T(8,128)(2,1)S(1)}, bf16[128,128]{1,0:T(8,128)(2,1)S(1)}, u32[]{:S(2)}, u32[]{:S(2)}) collective-permute-start(bf16[128,128]{1,0:T(8,128)(2,1)S(1)} %get-tuple-element.35), channel_id=1, source_target_pairs={{0,9},{1,10},{2,11},{3,8},{4,1},{5,2},{6,3},{7,0},{8,13},{9,14},{1... | collective-permute-start | bytes 98312 | tf_op jit(solution)/shard_map/ppermute | solution.py:170
  47.9 10.8 %collective-permute-start.8 = (bf16[128,128]{1,0:T(8,128)(2,1)S(1)}, bf16[128,128]{1,0:T(8,128)(2,1)S(1)}, u32[]{:S(2)}, u32[]{:S(2)}) collective-permute-start(bf16[128,128]{1,0:T(8,128)(2,1)S(1)} %get-tuple-element.36), channel_id=1, source_target_pairs={{0,10},{1,11},{2,8},{3,9},{4,2},{5,3},{6,0},{7,1},{8,14},{9,15},{1... | collective-permute-start | bytes 98312 | tf_op jit(solution)/shard_map/ppermute | solution.py:170
  50.7 8.3 %collective-permute-start.9 = (bf16[128,128]{1,0:T(8,128)(2,1)S(1)}, bf16[128,128]{1,0:T(8,128)(2,1)S(1)}, u32[]{:S(2)}, u32[]{:S(2)}) collective-permute-start(bf16[128,128]{1,0:T(8,128)(2,1)S(1)} %get-tuple-element.37), channel_id=1, source_target_pairs={{0,11},{1,8},{2,9},{3,10},{4,3},{5,0},{6,1},{7,2},{8,15},{9,12},{1... | collective-permute-start | bytes 98312 | tf_op jit(solution)/shard_map/ppermute | solution.py:170
  52.1 6.9 %collective-permute-start.12 = (bf16[128,128]{1,0:T(8,128)(2,1)S(1)}, bf16[128,128]{1,0:T(8,128)(2,1)S(1)}, u32[]{:S(2)}, u32[]{:S(2)}) collective-permute-start(bf16[128,128]{1,0:T(8,128)(2,1)S(1)} %get-tuple-element.39), channel_id=1, source_target_pairs={{0,12},{1,13},{2,14},{3,15},{4,8},{5,9},{6,10},{7,11},{8,4},{9,5},... | collective-permute-start | bytes 98312 | tf_op jit(solution)/shard_map/ppermute | solution.py:170
  54.1 5.3 %collective-permute-start.13 = (bf16[128,128]{1,0:T(8,128)(2,1)S(1)}, bf16[128,128]{1,0:T(8,128)(2,1)S(1)}, u32[]{:S(2)}, u32[]{:S(2)}) collective-permute-start(bf16[128,128]{1,0:T(8,128)(2,1)S(1)} %get-tuple-element.40), channel_id=1, source_target_pairs={{0,13},{1,14},{2,15},{3,12},{4,9},{5,10},{6,11},{7,8},{8,5},{9,6},... | collective-permute-start | bytes 98312 | tf_op jit(solution)/shard_map/ppermute | solution.py:170
  56.6 5.5 %collective-permute-start.14 = (bf16[128,128]{1,0:T(8,128)(2,1)S(1)}, bf16[128,128]{1,0:T(8,128)(2,1)S(1)}, u32[]{:S(2)}, u32[]{:S(2)}) collective-permute-start(bf16[128,128]{1,0:T(8,128)(2,1)S(1)} %get-tuple-element.41), channel_id=1, source_target_pairs={{0,14},{1,15},{2,12},{3,13},{4,10},{5,11},{6,8},{7,9},{8,6},{9,7},... | collective-permute-start | bytes 98312 | tf_op jit(solution)/shard_map/ppermute | solution.py:170
  58.6 6.0 %collective-permute-start.15 = (bf16[128,128]{1,0:T(8,128)(2,1)S(1)}, bf16[128,128]{1,0:T(8,128)(2,1)S(1)}, u32[]{:S(2)}, u32[]{:S(2)}) collective-permute-start(bf16[128,128]{1,0:T(8,128)(2,1)S(1)} %get-tuple-element.42), channel_id=1, source_target_pairs={{0,15},{1,12},{2,13},{3,14},{4,11},{5,8},{6,9},{7,10},{8,7},{9,4},... | collective-permute-start | bytes 98312 | tf_op jit(solution)/shard_map/ppermute | solution.py:170

commit v6 on v5

v6 whole, which is shorter than its diff:
```python
import functools

import jax
import jax.numpy as jnp
from jax import lax
from jax.experimental import pallas as pl
from jax.experimental.pallas import tpu as pltpu
from jax.sharding import PartitionSpec as P

LDIM = 512
LAY_DEV = 4
STEPS = 4
DAMPING = 0.05
NT = (((1,), (1,)), ((), ()))
MIB = 1024 * 1024


def prepare_kernel(
    offsets, queries_hbm, bases_hbm, values_hbm, conditioned_ref, queries, bases, values, arrived
):
    copies = [pltpu.make_async_copy(values_hbm, values, arrived.at[0])]
    for layer in range(LAY_DEV):
        columns = queries_hbm.at[:, layer * LDIM : (layer + 1) * LDIM]
        copies.append(pltpu.make_async_copy(columns, queries.at[layer], arrived.at[1 + 2 * layer]))
        copies.append(pltpu.make_async_copy(bases_hbm.at[layer], bases.at[layer], arrived.at[2 + 2 * layer]))
    for copy in copies:
        copy.start()
    base_column = lax.axis_index("layer") * (LAY_DEV * LDIM)
    copies[0].wait()
    for layer in range(LAY_DEV):
        copies[1 + 2 * layer].wait()
        copies[2 + 2 * layer].wait()
        basis = bases[layer]
        projected = jnp.dot(queries[layer], basis, preferred_element_type=jnp.float32)
        scaled = (projected / (values[layer : layer + 1, :] + DAMPING)).astype(jnp.bfloat16)
        restored = lax.dot_general(scaled, basis, NT, preferred_element_type=jnp.float32)
        first = pl.multiple_of(offsets[layer] - base_column, LDIM)
        conditioned_ref[:, pl.ds(first, LDIM)] = restored.astype(jnp.bfloat16)


def prepare(queries, bases, values, offsets):
    rows, dims = queries.shape
    hbm = pl.BlockSpec(memory_space=pltpu.HBM)
    return pl.pallas_call(
        prepare_kernel,
        out_shape=jax.ShapeDtypeStruct((rows, dims), jnp.bfloat16),
        in_specs=[pl.BlockSpec(memory_space=pltpu.SMEM), hbm, hbm, hbm],
        out_specs=pl.BlockSpec(memory_space=pltpu.VMEM),
        scratch_shapes=[
            pltpu.VMEM((LAY_DEV, rows, LDIM), jnp.bfloat16),
            pltpu.VMEM(bases.shape, jnp.bfloat16),
            pltpu.VMEM(values.shape, jnp.float32),
            pltpu.SemaphoreType.DMA((1 + 2 * LAY_DEV,)),
        ],
        compiler_params=pltpu.CompilerParams(vmem_limit_bytes=62 * MIB),
        cost_estimate=pl.CostEstimate(
            flops=4 * rows * dims * LDIM, bytes_accessed=6 * MIB, transcendentals=0
        ),
    )(offsets, queries, bases, values)


def masked_tile(queries_ref, documents, ids_ref, block):
    tile = lax.dot_general(queries_ref[...], documents[...], NT, preferred_element_type=jnp.float32)
    doc_ids = block * tile.shape[1] + lax.broadcasted_iota(jnp.int32, tile.shape, 1)
    return jnp.where(ids_ref[...] == doc_ids, 0.0, tile)


def score_kernel(shares, block_of, place, queries_ref, ids_ref, documents_ref, *refs):
    front_refs, out_refs, held = refs[: -1 - shares], refs[-1 - shares : -1], refs[-1]
    held[...] = masked_tile(queries_ref, documents_ref, ids_ref, block_of(place[1]))
    docs = documents_ref.shape[0]
    for turn, out_ref in enumerate(out_refs):
        share_rows, width = out_ref.shape
        first = pl.multiple_of(lax.rem(place[0] + turn, shares) * share_rows, share_rows)
        if front_refs:
            out_ref[:, : width - docs] = front_refs[turn][...]
        out_ref[:, width - docs :] = held[pl.ds(first, share_rows), :].astype(jnp.bfloat16)


def partial_scores(conditioned, query_ids, documents, block_of, place, shares, front=()):
    rows, dims = conditioned.shape
    docs = documents.shape[0]
    width = docs + (front[0].shape[1] if front else 0)
    vmem = pl.BlockSpec(memory_space=pltpu.VMEM)
    return pl.pallas_call(
        functools.partial(score_kernel, shares, block_of),
        out_shape=[jax.ShapeDtypeStruct((rows // shares, width), jnp.bfloat16)] * shares,
        in_specs=[pl.BlockSpec(memory_space=pltpu.SMEM)] + [vmem] * (3 + len(front)),
        out_specs=[vmem] * shares,
        scratch_shapes=[pltpu.VMEM((rows, docs), jnp.float32)],
        compiler_params=pltpu.CompilerParams(vmem_limit_bytes=12 * MIB),
        cost_estimate=pl.CostEstimate(
            flops=2 * rows * docs * dims, bytes_accessed=2 * dims * (rows + docs), transcendentals=0
        ),
    )(place, conditioned, query_ids, documents, *front)


def total_of(refs):
    total = refs[0][...].astype(jnp.float32)
    for ref in refs[1:]:
        total += ref[...].astype(jnp.float32)
    return total


def sum_kernel(shares, *refs):
    in_refs, out_refs = refs[:shares], refs[shares:]
    total = total_of(in_refs)
    docs = out_refs[0].shape[1]
    for spot, out_ref in enumerate(out_refs):
        out_ref[...] = total[:, spot * docs : (spot + 1) * docs]


def row_exchange(tiles):
    shares = len(tiles)
    arrived = [tiles[0]]
    for turn in range(1, shares):
        pairs = [(lay, (lay + turn) % shares) for lay in range(shares)]
        arrived.append(lax.ppermute(tiles[turn], "layer", pairs))
    return arrived


def row_sums(tiles, docs):
    shares = len(tiles)
    rows, width = tiles[0].shape
    vmem = pl.BlockSpec(memory_space=pltpu.VMEM)
    return pl.pallas_call(
        functools.partial(sum_kernel, shares),
        out_shape=[jax.ShapeDtypeStruct((rows, docs), jnp.float32)] * (width // docs),
        in_specs=[vmem] * shares,
        out_specs=[vmem] * (width // docs),
        compiler_params=pltpu.CompilerParams(vmem_limit_bytes=4 * MIB),
    )(*tiles)


ROUND_ONE = ((0, 2), (2, 3), (3, 1), (1, 0))
ROUND_TWO = ((0, 1), (1, 3), (3, 2), (2, 0))
BLOCK_ONE = (1, 3, 0, 2)
BLOCK_TWO = (2, 0, 3, 1)
BLOCK_LAST = (3, 2, 1, 0)


def pick(table):
    def entry(row):
        value = jnp.int32(table[0])
        for index in range(1, len(table)):
            value = jnp.where(row == index, jnp.int32(table[index]), value)
        return value

    return entry


def step_of(table):
    return pick([(block - table.index(block)) % STEPS for block in range(STEPS)])


def final_kernel(tables, place, own_ref, *refs):
    *round_refs, out_ref = refs
    out_ref[0] = own_ref[...]
    for spot, step_at in enumerate(tables):
        parts = round_refs[spot:] if spot == len(tables) - 1 else round_refs[spot : spot + 1]
        out_ref[step_at(place[1])] = total_of(parts)


def final_scores(place, own, rounds, last, tables):
    vmem = pl.BlockSpec(memory_space=pltpu.VMEM)
    return pl.pallas_call(
        functools.partial(final_kernel, tables),
        out_shape=jax.ShapeDtypeStruct((STEPS,) + own.shape, jnp.float32),
        in_specs=[pl.BlockSpec(memory_space=pltpu.SMEM)] + [vmem] * (1 + len(rounds) + len(last)),
        out_specs=vmem,
        compiler_params=pltpu.CompilerParams(vmem_limit_bytes=4 * MIB),
    )(place, own, *rounds, *last)


def exchange(tiles, target_of):
    n_rows, shares = lax.axis_size("rows"), lax.axis_size("layer")
    arrived = []
    for turn, tile in enumerate(tiles):
        pairs = [
            (row * shares + lay, target_of(row) * shares + (lay + turn) % shares)
            for row in range(n_rows)
            for lay in range(shares)
        ]
        arrived.append(lax.ppermute(tile, ("rows", "layer"), pairs))
    return arrived


def along_line(documents, conditioned, query_ids, place, shares):
    docs = documents.shape[0]

    def scored(block, block_of, front=()):
        return partial_scores(conditioned, query_ids, block, block_of, place, shares, front)

    one = lax.ppermute(documents, "rows", ROUND_ONE)
    later, conditioned = lax.optimization_barrier((documents, conditioned))
    two = lax.ppermute(later, "rows", ROUND_TWO)
    tiles = scored(later, lambda row: row)
    one, tiles = lax.optimization_barrier((one, tiles))
    three = lax.ppermute(one, "rows", ROUND_ONE)

    tiles = row_exchange(scored(one, pick(BLOCK_ONE), tiles))
    two, tiles[1] = lax.optimization_barrier((two, tiles[1]))
    own, first = row_sums(tiles, docs)
    first = lax.ppermute(first, "rows", tuple(enumerate(BLOCK_ONE)))
    (second,) = row_sums(row_exchange(scored(two, pick(BLOCK_TWO))), docs)
    second = lax.ppermute(second, "rows", tuple(enumerate(BLOCK_TWO)))
    last = exchange(scored(three, pick(BLOCK_LAST)), BLOCK_LAST.__getitem__)
    tables = [step_of(table) for table in (BLOCK_ONE, BLOCK_TWO, BLOCK_LAST)]
    return final_scores(place, own, [first, second], last, tables)


def around_ring(documents, conditioned, query_ids, place, shares):
    n_rows = lax.axis_size("rows")
    docs = documents.shape[0]
    result = []
    for step in range(STEPS):
        back = [(row, (row - step) % n_rows) for row in range(n_rows)]
        block = lax.ppermute(documents, "rows", back) if step else documents

        def ahead(row, step=step):
            return lax.rem(row + step, n_rows)

        tiles = partial_scores(conditioned, query_ids, block, ahead, place, shares)
        (total,) = row_sums(row_exchange(tiles), docs)
        onward = [(row, (row + step) % n_rows) for row in range(n_rows)]
        result.append(lax.ppermute(total, "rows", onward) if step else total)
    return jnp.stack(result)


def local(train_grads, query_grads, eigenbases, eigenvalues, layer_offsets, query_doc_ids):
    place = jnp.stack([lax.axis_index("layer"), lax.axis_index("rows")]).astype(jnp.int32)
    conditioned = prepare(query_grads, eigenbases, eigenvalues, layer_offsets)
    plan = along_line if lax.axis_size("rows") == STEPS else around_ring
    return plan(train_grads, conditioned, query_doc_ids[:, None], place, lax.axis_size("layer"))


def solution(mesh):
    in_specs = (
        P(("group", "rows"), "layer"),
        P(("group", "rows"), "layer"),
        P("layer", None, None),
        P("layer", None),
        P("layer"),
        P(("group", "rows")),
    )
    out_specs = P(None, "layer", ("group", "rows"))
    return jax.shard_map(local, mesh=mesh, in_specs=in_specs, out_specs=out_specs, check_vma=False)
```

time: 66.3 us -> 56 us (0.84)
  starting transfers between devices: 29.5 us -> 22.6 us
  local copies, waits for them, and re-layouts: 3.13 us -> 1.74 us
  waiting for transfers between devices: 19.7 us -> 18.7 us
    ppermute x12 -> x4, starting transfers between devices: 20.1 us -> 8.86 us  [exchange(): arrived.append(lax.ppermute(tile, ('rows', 'layer'), pairs))]
    ppermute x12 -> x4, waiting for transfers between devices: 15.1 us -> 5.68 us  [exchange(): arrived.append(lax.ppermute(tile, ('rows', 'layer'), pairs))]
    ppermute x2 -> x9, starting transfers between devices: 1.98 us -> 10.5 us  [the longest x6 6.81 us: row_exchange(): arrived.append(lax.ppermute(tiles[turn], 'layer', pairs))]
    ppermute x2 -> x9, waiting for transfers between devices: 0.01 us -> 5.22 us  [the longest x6 2.94 us: row_exchange(): arrived.append(lax.ppermute(tiles[turn], 'layer', pairs))]
    ppermute x1, waiting for transfers between devices: 1.03 us -> 6.16 us  [along_line(): two = lax.ppermute(later, 'rows', ROUND_TWO)]
    all_to_all x1 -> x0, starting transfers between devices: 4.26 us -> none  [local(): own = lax.all_to_all(own, 'layer', 0, 0, tiled=True)]
    all_to_all x1 -> x0, waiting for transfers between devices: 3.59 us -> none  [local(): own = lax.all_to_all(own, 'layer', 0, 0, tiled=True)]
    ppermute x1, waiting for transfers between devices: 0.01 us -> 1.67 us  [along_line(): one = lax.ppermute(documents, 'rows', ROUND_ONE)]
  transfers between devices with their start and end apart: 17 -> 15, of which waited for: 7 -> 8; matrix products, arithmetic and copies ran while one was open for 3% -> 0% of each run, Pallas kernels for 18% -> 20%
where the time goes in v6:
time: 56 us; the launch traced here: 55.8 us
  starting transfers between devices  22.6 us (40%)
  waiting for transfers between devices  18.7 us (33%)
  Pallas kernels  12.6 us (22%)
  local copies, waits for them, and re-layouts  1.74 us (3%)
    ppermute x4, starting transfers between devices, exchange(): arrived.append(lax.ppermute(tile, ('rows', 'layer'), pairs))  8.86 us
    ppermute x6, starting transfers between devices, row_exchange(): arrived.append(lax.ppermute(tiles[turn], 'layer', pairs))  6.81 us
    ppermute x1, waiting for transfers between devices, along_line(): two = lax.ppermute(later, 'rows', ROUND_TWO)  6.16 us
    pallas_call x1, Pallas kernels, prepare(): pl.pallas_call(prepare_kernel, out_shape=jax.ShapeDtypeStruct((rows, dims...  6.14 us
    ppermute x4, waiting for transfers between devices, exchange(): arrived.append(lax.ppermute(tile, ('rows', 'layer'), pairs))  5.68 us
    pallas_call x4, Pallas kernels, partial_scores(): pl.pallas_call(functools.partial(score_kernel, shares, block_of), out_sha...  5.12 us
    ppermute x1, starting transfers between devices, along_line(): one = lax.ppermute(documents, 'rows', ROUND_ONE)  3.14 us
    ppermute x6, waiting for transfers between devices, row_exchange(): arrived.append(lax.ppermute(tiles[turn], 'layer', pairs))  2.94 us
  transfers between devices with their start and end apart: 15, of which 8 were waited for; matrix products, arithmetic and copies ran while one was open for 0% of the time, Pallas kernels for 20%

profile of v6, /device:TPU:1, one launch (start us, length us, event | category | flops | bytes accessed | tf_op | source)
XLA Modules:
  0.0 55.8 jit_solution(11926659709996895403)
XLA Ops:
  0.0 0.0 copy-start.1
  0.0 0.0 copy-start.2
  0.0 3.1 %collective-permute-start = (bf16[128,2048]{1,0:T(8,128)(2,1)}, bf16[128,2048]{1,0:T(8,128)(2,1)S(1)}, u32[]{:S(2)}, u32[]{:S(2)}) collective-permute-start(bf16[128,2048]{1,0:T(8,128)(2,1)} %documents_ref), channel_id=1, source_target_pairs={{0,8},{8,12},{12,4},{4,0},{1,9},{9,13},{13,5},{5,1},{2,10},{10,14}... | collective-permute-start | bytes 1572872 | tf_op jit(solution)/shard_map/ppermute | solution.py:194
  3.1 6.1 %shard_map.64.queries_ref = bf16[512,2048]{1,0:T(8,128)(2,1)} custom-call(s32[4]{0:T(128)} %offsets.1, bf16[512,2048]{1,0:T(8,128)(2,1)} %queries_hbm.1, bf16[4,512,512]{2,1,0:T(8,128)(2,1)} %bases_hbm.1, f32[4,512]{1,0:T(4,128)} %values_hbm.1), custom_call_target="tpu_custom_call" | custom-call | flops 2147483648 | bytes 6291456 | tf_op jit(solution)/shard_map/pallas_call | solution.py:44
  9.3 0.0 copy-done.1
  9.3 0.1 collective-permute-start.1
  9.4 0.1 pad_add_fusion.place
  9.4 0.0 copy-done.2
  9.5 0.1 copy.8.ids_ref
  9.6 0.0 copy-start
  9.6 1.6 %copy-done = bf16[512,2048]{1,0:T(8,128)(2,1)S(1)} copy-done((bf16[512,2048]{1,0:T(8,128)(2,1)S(1)}, bf16[512,2048]{1,0:T(8,128)(2,1)}, u32[]{:S(2)}) %copy-start) | copy-done | bytes 2097176
  11.2 1.3 %shard_map.65 = (bf16[128,128]{1,0:T(8,128)(2,1)S(1)}, bf16[128,128]{1,0:T(8,128)(2,1)S(1)}, bf16[128,128]{1,0:T(8,128)(2,1)S(1)}, bf16[128,128]{1,0:T(8,128)(2,1)S(1)}) custom-call(s32[2]{0:T(128)S(1)} %pad_add_fusion.place, bf16[512,2048]{1,0:T(8,128)(2,1)S(1)} %copy-done, s32[512,1]{1,0:T(8,128)S(1)} %copy.8.ids_ref, bf16[128,2048]{1,0:T(8,128)(2,1)S(1)} %copy-done.1), custom_call_target="tpu_custom_call" | custom-call | flops 268435456 | bytes 2621440 | tf_op jit(solution)/shard_map/pallas_call | solution.py:85
  12.5 1.7 %collective-permute-done.documents_ref = bf16[128,2048]{1,0:T(8,128)(2,1)S(1)} collective-permute-done((bf16[128,2048]{1,0:T(8,128)(2,1)}, bf16[128,2048]{1,0:T(8,128)(2,1)S(1)}, u32[]{:S(2)}, u32[]{:S(2)}) %collective-permute-start) | collective-permute-done | bytes 524320 | tf_op jit(solution)/shard_map/ppermute | solution.py:194
  14.2 2.9 %collective-permute-start.10 = (bf16[128,2048]{1,0:T(8,128)(2,1)S(1)}, bf16[128,2048]{1,0:T(8,128)(2,1)S(1)}, u32[]{:S(2)}, u32[]{:S(2)}) collective-permute-start(bf16[128,2048]{1,0:T(8,128)(2,1)S(1)} %collective-permute-done.documents_ref), channel_id=1, source_target_pairs={{0,8},{8,12},{12,4},{4,0},{1,9},{9,13},{13,5},{5,1},{2,10},{10,14}... | collective-permute-start | bytes 1572872 | tf_op jit(solution)/shard_map/ppermute | solution.py:199
  17.1 1.3 %shard_map.66 = (bf16[128,256]{1,0:T(8,128)(2,1)S(1)}, bf16[128,256]{1,0:T(8,128)(2,1)S(1)}, bf16[128,256]{1,0:T(8,128)(2,1)S(1)}, bf16[128,256]{1,0:T(8,128)(2,1)S(1)}) custom-call(s32[2]{0:T(128)S(1)} %pad_add_fusion.place, bf16[512,2048]{1,0:T(8,128)(2,1)S(1)} %copy-done, s32[512,1]{1,0:T(8,128)S(1)} %copy.8.ids_ref, ...), custom_call_target="tpu_custom_call" | custom-call | flops 268435456 | bytes 2621440 | tf_op jit(solution)/shard_map/pallas_call | solution.py:85
  18.4 4.1 %collective-permute-start.2 = (bf16[128,256]{1,0:T(8,128)(2,1)S(1)}, bf16[128,256]{1,0:T(8,128)(2,1)S(1)}, u32[]{:S(2)}, u32[]{:S(2)}) collective-permute-start(bf16[128,256]{1,0:T(8,128)(2,1)S(1)} %get-tuple-element.44), channel_id=1, source_target_pairs={{0,1},{1,2},{2,3},{3,0},{4,5},{5,6},{6,7},{7,4},{8,9},{9,10},{10,1... | collective-permute-start | bytes 196616 | tf_op jit(solution)/shard_map/ppermute | solution.py:118
  22.5 0.3 collective-permute-start.3
  22.8 0.2 collective-permute-start.4
  23.0 6.2 %collective-permute-done.1.documents_ref = bf16[128,2048]{1,0:T(8,128)(2,1)S(1)} collective-permute-done((bf16[128,2048]{1,0:T(8,128)(2,1)S(1)}, bf16[128,2048]{1,0:T(8,128)(2,1)S(1)}, u32[]{:S(2)}, u32[]{:S(2)}) %collective-permute-start.1) | collective-permute-done | bytes 524320 | tf_op jit(solution)/shard_map/ppermute | solution.py:196
  29.1 0.0 collective-permute-done.2.refs_1_
  29.1 1.3 %shard_map.68 = (bf16[128,128]{1,0:T(8,128)(2,1)S(1)}, bf16[128,128]{1,0:T(8,128)(2,1)S(1)}, bf16[128,128]{1,0:T(8,128)(2,1)S(1)}, bf16[128,128]{1,0:T(8,128)(2,1)S(1)}) custom-call(s32[2]{0:T(128)S(1)} %pad_add_fusion.place, bf16[512,2048]{1,0:T(8,128)(2,1)S(1)} %copy-done, s32[512,1]{1,0:T(8,128)S(1)} %copy.8.ids_ref, ...), custom_call_target="tpu_custom_call" | custom-call | flops 268435456 | bytes 2621440 | tf_op jit(solution)/shard_map/pallas_call | solution.py:85
  30.4 1.7 %collective-permute-start.6 = (bf16[128,128]{1,0:T(8,128)(2,1)S(1)}, bf16[128,128]{1,0:T(8,128)(2,1)S(1)}, u32[]{:S(2)}, u32[]{:S(2)}) collective-permute-start(bf16[128,128]{1,0:T(8,128)(2,1)S(1)} %get-tuple-element.52), channel_id=1, source_target_pairs={{0,1},{1,2},{2,3},{3,0},{4,5},{5,6},{6,7},{7,4},{8,9},{9,10},{10,1... | collective-permute-start | bytes 98312 | tf_op jit(solution)/shard_map/ppermute | solution.py:118
  32.2 0.3 collective-permute-start.7
  32.4 0.0 collective-permute-done.3.refs_2_
  32.4 0.2 collective-permute-start.8
  32.6 0.0 collective-permute-done.4.refs_3_
  32.7 0.4 collective-permute-start.5
  33.1 0.1 collective-permute-done.6.refs_1_
  33.2 2.0 %collective-permute-done.7.refs_2_ = bf16[128,128]{1,0:T(8,128)(2,1)S(1)} collective-permute-done((bf16[128,128]{1,0:T(8,128)(2,1)S(1)}, bf16[128,128]{1,0:T(8,128)(2,1)S(1)}, u32[]{:S(2)}, u32[]{:S(2)}) %collective-permute-start.7) | collective-permute-done | bytes 32800 | tf_op jit(solution)/shard_map/ppermute | solution.py:118
  35.2 0.8 %collective-permute-done.8.refs_3_ = bf16[128,128]{1,0:T(8,128)(2,1)S(1)} collective-permute-done((bf16[128,128]{1,0:T(8,128)(2,1)S(1)}, bf16[128,128]{1,0:T(8,128)(2,1)S(1)}, u32[]{:S(2)}, u32[]{:S(2)}) %collective-permute-start.8) | collective-permute-done | bytes 32800 | tf_op jit(solution)/shard_map/ppermute | solution.py:118
  36.1 0.3 collective-permute-start.9
  36.4 2.3 %collective-permute-done.10.documents_ref = bf16[128,2048]{1,0:T(8,128)(2,1)S(1)} collective-permute-done((bf16[128,2048]{1,0:T(8,128)(2,1)S(1)}, bf16[128,2048]{1,0:T(8,128)(2,1)S(1)}, u32[]{:S(2)}, u32[]{:S(2)}) %collective-permute-start.10) | collective-permute-done | bytes 524320 | tf_op jit(solution)/shard_map/ppermute | solution.py:199
  38.7 1.3 %shard_map.70 = (bf16[128,128]{1,0:T(8,128)(2,1)S(1)}, bf16[128,128]{1,0:T(8,128)(2,1)S(1)}, bf16[128,128]{1,0:T(8,128)(2,1)S(1)}, bf16[128,128]{1,0:T(8,128)(2,1)S(1)}) custom-call(s32[2]{0:T(128)S(1)} %pad_add_fusion.place, bf16[512,2048]{1,0:T(8,128)(2,1)S(1)} %copy-done, s32[512,1]{1,0:T(8,128)S(1)} %copy.8.ids_ref, ...), custom_call_target="tpu_custom_call" | custom-call | flops 268435456 | bytes 2621440 | tf_op jit(solution)/shard_map/pallas_call | solution.py:85
  40.0 3.2 %collective-permute-start.11 = (bf16[128,128]{1,0:T(8,128)(2,1)S(1)}, bf16[128,128]{1,0:T(8,128)(2,1)S(1)}, u32[]{:S(2)}, u32[]{:S(2)}) collective-permute-start(bf16[128,128]{1,0:T(8,128)(2,1)S(1)} %get-tuple-element.55), channel_id=1, source_target_pairs={{0,12},{1,13},{2,14},{3,15},{4,8},{5,9},{6,10},{7,11},{8,4},{9,5},... | collective-permute-start | bytes 98312 | tf_op jit(solution)/shard_map/ppermute | solution.py:184
  43.2 3.0 %collective-permute-start.12 = (bf16[128,128]{1,0:T(8,128)(2,1)S(1)}, bf16[128,128]{1,0:T(8,128)(2,1)S(1)}, u32[]{:S(2)}, u32[]{:S(2)}) collective-permute-start(bf16[128,128]{1,0:T(8,128)(2,1)S(1)} %get-tuple-element.56), channel_id=1, source_target_pairs={{0,13},{1,14},{2,15},{3,12},{4,9},{5,10},{6,11},{7,8},{8,5},{9,6},... | collective-permute-start | bytes 98312 | tf_op jit(solution)/shard_map/ppermute | solution.py:184
  46.3 2.2 %collective-permute-start.13 = (bf16[128,128]{1,0:T(8,128)(2,1)S(1)}, bf16[128,128]{1,0:T(8,128)(2,1)S(1)}, u32[]{:S(2)}, u32[]{:S(2)}) collective-permute-start(bf16[128,128]{1,0:T(8,128)(2,1)S(1)} %get-tuple-element.57), channel_id=1, source_target_pairs={{0,14},{1,15},{2,12},{3,13},{4,10},{5,11},{6,8},{7,9},{8,6},{9,7},... | collective-permute-start | bytes 98312 | tf_op jit(solution)/shard_map/ppermute | solution.py:184
  48.5 0.0 collective-permute-done.5.refs_0_
  48.5 0.3 collective-permute-start.14
  48.8 0.0 collective-permute-done.9.refs_1_
  48.8 0.0 collective-permute-done.11.refs_2_
  48.8 0.0 collective-permute-done.12.refs_3_
  48.8 2.9 %collective-permute-done.13.refs_4_ = bf16[128,128]{1,0:T(8,128)(2,1)S(1)} collective-permute-done((bf16[128,128]{1,0:T(8,128)(2,1)S(1)}, bf16[128,128]{1,0:T(8,128)(2,1)S(1)}, u32[]{:S(2)}, u32[]{:S(2)}) %collective-permute-start.13) | collective-permute-done | bytes 32800 | tf_op jit(solution)/shard_map/ppermute | solution.py:184
  51.7 2.8 %collective-permute-done.14.refs_5_ = bf16[128,128]{1,0:T(8,128)(2,1)S(1)} collective-permute-done((bf16[128,128]{1,0:T(8,128)(2,1)S(1)}, bf16[128,128]{1,0:T(8,128)(2,1)S(1)}, u32[]{:S(2)}, u32[]{:S(2)}) %collective-permute-start.14) | collective-permute-done | bytes 32800 | tf_op jit(solution)/shard_map/ppermute | solution.py:184
  54.5 1.3 %shard_map.71 = f32[4,128,128]{2,1,0:T(8,128)} custom-call(s32[2]{0:T(128)S(1)} %pad_add_fusion.place, f32[128,128]{1,0:T(8,128)S(1)} %get-tuple-element.48.own_ref, f32[128,128]{1,0:T(8,128)S(1)} %collective-permute-done.5.refs_0_, f32[128,128]{1,0:T(8,128)S(1)} %collective-permute-done.9.refs_1_, bf16[128,128]{1,0:T(8,128)(2,1)S(1)} %collective-permute-done.11.refs_2_, ...), custom_call_target="tpu_custom_call" | custom-call | tf_op jit(solution)/shard_map/pallas_call | solution.py:166
  (2 shorter events, 0.1 us)
Async XLA Ops:
  0.0 9.3 %copy-start.1 = (bf16[128,2048]{1,0:T(8,128)(2,1)S(1)}, bf16[128,2048]{1,0:T(8,128)(2,1)}, u32[]{:S(2)}) copy-start(bf16[128,2048]{1,0:T(8,128)(2,1)} %documents_ref) | copy-start | bytes 1572868
  0.0 9.4 %copy-start.2 = (s32[512]{0:T(512)S(1)}, s32[512]{0:T(512)}, u32[]{:S(2)}) copy-start(s32[512]{0:T(512)} %param.11) | copy-start | bytes 6148
  0.0 14.2 %collective-permute-start = (bf16[128,2048]{1,0:T(8,128)(2,1)}, bf16[128,2048]{1,0:T(8,128)(2,1)S(1)}, u32[]{:S(2)}, u32[]{:S(2)}) collective-permute-start(bf16[128,2048]{1,0:T(8,128)(2,1)} %documents_ref), channel_id=1, source_target_pairs={{0,8},{8,12},{12,4},{4,0},{1,9},{9,13},{13,5},{5,1},{2,10},{10,14}... | collective-permute-start | bytes 1572872 | tf_op jit(solution)/shard_map/ppermute | solution.py:194
  9.3 19.8 %collective-permute-start.1 = (bf16[128,2048]{1,0:T(8,128)(2,1)S(1)}, bf16[128,2048]{1,0:T(8,128)(2,1)S(1)}, u32[]{:S(2)}, u32[]{:S(2)}) collective-permute-start(bf16[128,2048]{1,0:T(8,128)(2,1)S(1)} %copy-done.1), channel_id=1, source_target_pairs={{0,4},{4,12},{12,8},{8,0},{1,5},{5,13},{13,9},{9,1},{2,6},{6,14},{... | collective-permute-start | bytes 1572872 | tf_op jit(solution)/shard_map/ppermute | solution.py:196
  9.6 1.6 %copy-start = (bf16[512,2048]{1,0:T(8,128)(2,1)S(1)}, bf16[512,2048]{1,0:T(8,128)(2,1)}, u32[]{:S(2)}) copy-start(bf16[512,2048]{1,0:T(8,128)(2,1)} %shard_map.64.queries_ref) | copy-start | bytes 6291460
  14.2 24.5 %collective-permute-start.10 = (bf16[128,2048]{1,0:T(8,128)(2,1)S(1)}, bf16[128,2048]{1,0:T(8,128)(2,1)S(1)}, u32[]{:S(2)}, u32[]{:S(2)}) collective-permute-start(bf16[128,2048]{1,0:T(8,128)(2,1)S(1)} %collective-permute-done.documents_ref), channel_id=1, source_target_pairs={{0,8},{8,12},{12,4},{4,0},{1,9},{9,13},{13,5},{5,1},{2,10},{10,14}... | collective-permute-start | bytes 1572872 | tf_op jit(solution)/shard_map/ppermute | solution.py:199
  18.4 10.8 %collective-permute-start.2 = (bf16[128,256]{1,0:T(8,128)(2,1)S(1)}, bf16[128,256]{1,0:T(8,128)(2,1)S(1)}, u32[]{:S(2)}, u32[]{:S(2)}) collective-permute-start(bf16[128,256]{1,0:T(8,128)(2,1)S(1)} %get-tuple-element.44), channel_id=1, source_target_pairs={{0,1},{1,2},{2,3},{3,0},{4,5},{5,6},{6,7},{7,4},{8,9},{9,10},{10,1... | collective-permute-start | bytes 196616 | tf_op jit(solution)/shard_map/ppermute | solution.py:118
  22.5 9.9 %collective-permute-start.3 = (bf16[128,256]{1,0:T(8,128)(2,1)S(1)}, bf16[128,256]{1,0:T(8,128)(2,1)S(1)}, u32[]{:S(2)}, u32[]{:S(2)}) collective-permute-start(bf16[128,256]{1,0:T(8,128)(2,1)S(1)} %get-tuple-element.46), channel_id=1, source_target_pairs={{0,2},{1,3},{2,0},{3,1},{4,6},{5,7},{6,4},{7,5},{8,10},{9,11},{10,... | collective-permute-start | bytes 196616 | tf_op jit(solution)/shard_map/ppermute | solution.py:118
  22.8 9.9 %collective-permute-start.4 = (bf16[128,256]{1,0:T(8,128)(2,1)S(1)}, bf16[128,256]{1,0:T(8,128)(2,1)S(1)}, u32[]{:S(2)}, u32[]{:S(2)}) collective-permute-start(bf16[128,256]{1,0:T(8,128)(2,1)S(1)} %get-tuple-element.47), channel_id=1, source_target_pairs={{0,3},{1,0},{2,1},{3,2},{4,7},{5,4},{6,5},{7,6},{8,11},{9,8},{10,9... | collective-permute-start | bytes 196616 | tf_op jit(solution)/shard_map/ppermute | solution.py:118
  30.4 2.8 %collective-permute-start.6 = (bf16[128,128]{1,0:T(8,128)(2,1)S(1)}, bf16[128,128]{1,0:T(8,128)(2,1)S(1)}, u32[]{:S(2)}, u32[]{:S(2)}) collective-permute-start(bf16[128,128]{1,0:T(8,128)(2,1)S(1)} %get-tuple-element.52), channel_id=1, source_target_pairs={{0,1},{1,2},{2,3},{3,0},{4,5},{5,6},{6,7},{7,4},{8,9},{9,10},{10,1... | collective-permute-start | bytes 98312 | tf_op jit(solution)/shard_map/ppermute | solution.py:118
  32.2 3.1 %collective-permute-start.7 = (bf16[128,128]{1,0:T(8,128)(2,1)S(1)}, bf16[128,128]{1,0:T(8,128)(2,1)S(1)}, u32[]{:S(2)}, u32[]{:S(2)}) collective-permute-start(bf16[128,128]{1,0:T(8,128)(2,1)S(1)} %get-tuple-element.53), channel_id=1, source_target_pairs={{0,2},{1,3},{2,0},{3,1},{4,6},{5,7},{6,4},{7,5},{8,10},{9,11},{10,... | collective-permute-start | bytes 98312 | tf_op jit(solution)/shard_map/ppermute | solution.py:118
  32.4 3.6 %collective-permute-start.8 = (bf16[128,128]{1,0:T(8,128)(2,1)S(1)}, bf16[128,128]{1,0:T(8,128)(2,1)S(1)}, u32[]{:S(2)}, u32[]{:S(2)}) collective-permute-start(bf16[128,128]{1,0:T(8,128)(2,1)S(1)} %get-tuple-element.54), channel_id=1, source_target_pairs={{0,3},{1,0},{2,1},{3,2},{4,7},{5,4},{6,5},{7,6},{8,11},{9,8},{10,9... | collective-permute-start | bytes 98312 | tf_op jit(solution)/shard_map/ppermute | solution.py:118
  32.7 15.8 %collective-permute-start.5 = (f32[128,128]{1,0:T(8,128)S(1)}, f32[128,128]{1,0:T(8,128)S(1)}, u32[]{:S(2)}, u32[]{:S(2)}) collective-permute-start(f32[128,128]{1,0:T(8,128)S(1)} %get-tuple-element.49), channel_id=1, source_target_pairs={{0,4},{4,12},{8,0},{12,8},{1,5},{5,13},{9,1},{13,9},{2,6},{6,14},{... | collective-permute-start | bytes 196616 | tf_op jit(solution)/shard_map/ppermute | solution.py:204
  36.1 12.8 %collective-permute-start.9 = (f32[128,128]{1,0:T(8,128)S(1)}, f32[128,128]{1,0:T(8,128)S(1)}, u32[]{:S(2)}, u32[]{:S(2)}) collective-permute-start(f32[128,128]{1,0:T(8,128)S(1)} %shard_map.69), channel_id=1, source_target_pairs={{0,8},{4,0},{8,12},{12,4},{1,9},{5,1},{9,13},{13,5},{2,10},{6,2},{... | collective-permute-start | bytes 196616 | tf_op jit(solution)/shard_map/ppermute | solution.py:206
  40.0 8.9 %collective-permute-start.11 = (bf16[128,128]{1,0:T(8,128)(2,1)S(1)}, bf16[128,128]{1,0:T(8,128)(2,1)S(1)}, u32[]{:S(2)}, u32[]{:S(2)}) collective-permute-start(bf16[128,128]{1,0:T(8,128)(2,1)S(1)} %get-tuple-element.55), channel_id=1, source_target_pairs={{0,12},{1,13},{2,14},{3,15},{4,8},{5,9},{6,10},{7,11},{8,4},{9,5},... | collective-permute-start | bytes 98312 | tf_op jit(solution)/shard_map/ppermute | solution.py:184
  43.2 5.6 %collective-permute-start.12 = (bf16[128,128]{1,0:T(8,128)(2,1)S(1)}, bf16[128,128]{1,0:T(8,128)(2,1)S(1)}, u32[]{:S(2)}, u32[]{:S(2)}) collective-permute-start(bf16[128,128]{1,0:T(8,128)(2,1)S(1)} %get-tuple-element.56), channel_id=1, source_target_pairs={{0,13},{1,14},{2,15},{3,12},{4,9},{5,10},{6,11},{7,8},{8,5},{9,6},... | collective-permute-start | bytes 98312 | tf_op jit(solution)/shard_map/ppermute | solution.py:184
  46.3 5.5 %collective-permute-start.13 = (bf16[128,128]{1,0:T(8,128)(2,1)S(1)}, bf16[128,128]{1,0:T(8,128)(2,1)S(1)}, u32[]{:S(2)}, u32[]{:S(2)}) collective-permute-start(bf16[128,128]{1,0:T(8,128)(2,1)S(1)} %get-tuple-element.57), channel_id=1, source_target_pairs={{0,14},{1,15},{2,12},{3,13},{4,10},{5,11},{6,8},{7,9},{8,6},{9,7},... | collective-permute-start | bytes 98312 | tf_op jit(solution)/shard_map/ppermute | solution.py:184
  48.5 6.0 %collective-permute-start.14 = (bf16[128,128]{1,0:T(8,128)(2,1)S(1)}, bf16[128,128]{1,0:T(8,128)(2,1)S(1)}, u32[]{:S(2)}, u32[]{:S(2)}) collective-permute-start(bf16[128,128]{1,0:T(8,128)(2,1)S(1)} %get-tuple-element.58), channel_id=1, source_target_pairs={{0,15},{1,12},{2,13},{3,14},{4,11},{5,8},{6,9},{7,10},{8,7},{9,4},... | collective-permute-start | bytes 98312 | tf_op jit(solution)/shard_map/ppermute | solution.py:184

commit v7 on v6

--- a/solution.py
+++ b/solution.py
@@ -66,33 +66,53 @@
 
 
 def score_kernel(shares, block_of, place, queries_ref, ids_ref, documents_ref, *refs):
-    front_refs, out_refs, held = refs[: -1 - shares], refs[-1 - shares : -1], refs[-1]
+    *out_refs, held = refs
     held[...] = masked_tile(queries_ref, documents_ref, ids_ref, block_of(place[1]))
-    docs = documents_ref.shape[0]
     for turn, out_ref in enumerate(out_refs):
-        share_rows, width = out_ref.shape
+        share_rows = out_ref.shape[0]
         first = pl.multiple_of(lax.rem(place[0] + turn, shares) * share_rows, share_rows)
-        if front_refs:
-            out_ref[:, : width - docs] = front_refs[turn][...]
-        out_ref[:, width - docs :] = held[pl.ds(first, share_rows), :].astype(jnp.bfloat16)
-
-
-def partial_scores(conditioned, query_ids, documents, block_of, place, shares, front=()):
+        out_ref[...] = held[pl.ds(first, share_rows), :].astype(jnp.bfloat16)
+
+
+def own_kernel(shares, place, queries_ref, ids_ref, documents_ref, out_ref):
+    tile = masked_tile(queries_ref, documents_ref, ids_ref, place[1])
+    out_ref[...] = tile.astype(jnp.bfloat16).reshape(out_ref.shape)
+
+
+def pair_kernel(shares, place, queries_ref, ids_ref, documents_ref, own_ref, out_ref):
+    tile = masked_tile(queries_ref, documents_ref, ids_ref, STEPS - 1 - place[1])
+    spot = own_spot(place[1])
+    out_ref[spot] = own_ref[...]
+    out_ref[1 - spot] = tile.astype(jnp.bfloat16).reshape(own_ref.shape)
+
+
+def own_spot(row):
+    return jnp.where(row < STEPS - 1 - row, 0, 1)
+
+
+def partial_scores(kernel, out_shape, conditioned, query_ids, documents, place, extra=(), scratch=()):
     rows, dims = conditioned.shape
     docs = documents.shape[0]
-    width = docs + (front[0].shape[1] if front else 0)
     vmem = pl.BlockSpec(memory_space=pltpu.VMEM)
     return pl.pallas_call(
-        functools.partial(score_kernel, shares, block_of),
-        out_shape=[jax.ShapeDtypeStruct((rows // shares, width), jnp.bfloat16)] * shares,
-        in_specs=[pl.BlockSpec(memory_space=pltpu.SMEM)] + [vmem] * (3 + len(front)),
-        out_specs=[vmem] * shares,
-        scratch_shapes=[pltpu.VMEM((rows, docs), jnp.float32)],
+        kernel,
+        out_shape=out_shape,
+        in_specs=[pl.BlockSpec(memory_space=pltpu.SMEM)] + [vmem] * (3 + len(extra)),
+        out_specs=jax.tree.map(lambda _: vmem, out_shape),
+        scratch_shapes=scratch,
         compiler_params=pltpu.CompilerParams(vmem_limit_bytes=12 * MIB),
         cost_estimate=pl.CostEstimate(
             flops=2 * rows * docs * dims, bytes_accessed=2 * dims * (rows + docs), transcendentals=0
         ),
-    )(place, conditioned, query_ids, documents, *front)
+    )(place, conditioned, query_ids, documents, *extra)
+
+
+def turned_scores(conditioned, query_ids, documents, block_of, place, shares):
+    rows, docs = conditioned.shape[0], documents.shape[0]
+    out_shape = [jax.ShapeDtypeStruct((rows // shares, docs), jnp.bfloat16)] * shares
+    kernel = functools.partial(score_kernel, shares, block_of)
+    scratch = [pltpu.VMEM((rows, docs), jnp.float32)]
+    return partial_scores(kernel, out_shape, conditioned, query_ids, documents, place, (), scratch)
 
 
 def total_of(refs):
@@ -102,12 +122,8 @@
     return total
 
 
-def sum_kernel(shares, *refs):
-    in_refs, out_refs = refs[:shares], refs[shares:]
-    total = total_of(in_refs)
-    docs = out_refs[0].shape[1]
-    for spot, out_ref in enumerate(out_refs):
-        out_ref[...] = total[:, spot * docs : (spot + 1) * docs]
+def sum_kernel(*refs):
+    refs[-1][...] = total_of(refs[:-1])
 
 
 def row_exchange(tiles):
@@ -119,15 +135,13 @@
     return arrived
 
 
-def row_sums(tiles, docs):
-    shares = len(tiles)
-    rows, width = tiles[0].shape
+def row_sum(tiles):
     vmem = pl.BlockSpec(memory_space=pltpu.VMEM)
     return pl.pallas_call(
-        functools.partial(sum_kernel, shares),
-        out_shape=[jax.ShapeDtypeStruct((rows, docs), jnp.float32)] * (width // docs),
-        in_specs=[vmem] * shares,
-        out_specs=[vmem] * (width // docs),
+        sum_kernel,
+        out_shape=jax.ShapeDtypeStruct(tiles[0].shape, jnp.float32),
+        in_specs=[vmem] * len(tiles),
+        out_specs=vmem,
         compiler_params=pltpu.CompilerParams(vmem_limit_bytes=4 * MIB),
     )(*tiles)
 
@@ -153,75 +167,80 @@
     return pick([(block - table.index(block)) % STEPS for block in range(STEPS)])
 
 
-def final_kernel(tables, place, own_ref, *refs):
-    *round_refs, out_ref = refs
-    out_ref[0] = own_ref[...]
-    for spot, step_at in enumerate(tables):
-        parts = round_refs[spot:] if spot == len(tables) - 1 else round_refs[spot : spot + 1]
-        out_ref[step_at(place[1])] = total_of(parts)
-
-
-def final_scores(place, own, rounds, last, tables):
+def final_kernel(place, first_ref, second_ref, pair_ref, out_ref):
+    row = place[1]
+    spot = own_spot(row)
+    shares = pair_ref.shape[1]
+    out_ref[0] = total_of([pair_ref.at[spot, share] for share in range(shares)])
+    out_ref[step_of(BLOCK_ONE)(row)] = first_ref[...]
+    out_ref[step_of(BLOCK_TWO)(row)] = second_ref[...]
+    out_ref[step_of(BLOCK_LAST)(row)] = total_of([pair_ref.at[1 - spot, share] for share in range(shares)])
+
+
+def final_scores(place, first, second, pair):
     vmem = pl.BlockSpec(memory_space=pltpu.VMEM)
     return pl.pallas_call(
-        functools.partial(final_kernel, tables),
-        out_shape=jax.ShapeDtypeStruct((STEPS,) + own.shape, jnp.float32),
-        in_specs=[pl.BlockSpec(memory_space=pltpu.SMEM)] + [vmem] * (1 + len(rounds) + len(last)),
+        final_kernel,
+        out_shape=jax.ShapeDtypeStruct((STEPS,) + first.shape, jnp.float32),
+        in_specs=[pl.BlockSpec(memory_space=pltpu.SMEM)] + [vmem] * 3,
         out_specs=vmem,
         compiler_params=pltpu.CompilerParams(vmem_limit_bytes=4 * MIB),
-    )(place, own, *rounds, *last)
-
-
-def exchange(tiles, target_of):
-    n_rows, shares = lax.axis_size("rows"), lax.axis_size("layer")
-    arrived = []
-    for turn, tile in enumerate(tiles):
-        pairs = [
-            (row * shares + lay, target_of(row) * shares + (lay + turn) % shares)
-            for row in range(n_rows)
-            for lay in range(shares)
-        ]
-        arrived.append(lax.ppermute(tile, ("rows", "layer"), pairs))
-    return arrived
+    )(place, first, second, pair)
 
 
 def along_line(documents, conditioned, query_ids, place, shares):
     docs = documents.shape[0]
-
-    def scored(block, block_of, front=()):
-        return partial_scores(conditioned, query_ids, block, block_of, place, shares, front)
+    own_shape = (shares, conditioned.shape[0] // shares, docs)
+
+    def row_scores(block, table):
+        tiles = turned_scores(conditioned, query_ids, block, pick(table), place, shares)
+        return row_exchange(tiles)
+
+    def back(total, table):
+        return lax.ppermute(total, "rows", tuple(enumerate(table)))
 
     one = lax.ppermute(documents, "rows", ROUND_ONE)
     later, conditioned = lax.optimization_barrier((documents, conditioned))
     two = lax.ppermute(later, "rows", ROUND_TWO)
-    tiles = scored(later, lambda row: row)
-    one, tiles = lax.optimization_barrier((one, tiles))
+    own = partial_scores(
+        functools.partial(own_kernel, shares),
+        jax.ShapeDtypeStruct(own_shape, jnp.bfloat16),
+        conditioned, query_ids, later, place,
+    )
+    one, own = lax.optimization_barrier((one, own))
     three = lax.ppermute(one, "rows", ROUND_ONE)
 
-    tiles = row_exchange(scored(one, pick(BLOCK_ONE), tiles))
+    tiles = row_scores(one, BLOCK_ONE)
     two, tiles[1] = lax.optimization_barrier((two, tiles[1]))
-    own, first = row_sums(tiles, docs)
-    first = lax.ppermute(first, "rows", tuple(enumerate(BLOCK_ONE)))
-    (second,) = row_sums(row_exchange(scored(two, pick(BLOCK_TWO))), docs)
-    second = lax.ppermute(second, "rows", tuple(enumerate(BLOCK_TWO)))
-    last = exchange(scored(three, pick(BLOCK_LAST)), BLOCK_LAST.__getitem__)
-    tables = [step_of(table) for table in (BLOCK_ONE, BLOCK_TWO, BLOCK_LAST)]
-    return final_scores(place, own, [first, second], last, tables)
+    first = back(row_sum(tiles), BLOCK_ONE)
+    second = back(row_sum(row_scores(two, BLOCK_TWO)), BLOCK_TWO)
+
+    pair = partial_scores(
+        functools.partial(pair_kernel, shares),
+        jax.ShapeDtypeStruct((2,) + own_shape, jnp.bfloat16),
+        conditioned, query_ids, three, place, (own,),
+    )
+    groups = [
+        [row * shares + lay for row in (low, STEPS - 1 - low) for lay in range(shares)]
+        for low in range(STEPS // 2)
+    ]
+    blocks = pair.reshape((2 * shares,) + own_shape[1:])
+    blocks = lax.all_to_all(blocks, ("rows", "layer"), 0, 0, axis_index_groups=groups, tiled=True)
+    return final_scores(place, first, second, blocks.reshape(pair.shape))
 
 
 def around_ring(documents, conditioned, query_ids, place, shares):
     n_rows = lax.axis_size("rows")
-    docs = documents.shape[0]
     result = []
     for step in range(STEPS):
-        back = [(row, (row - step) % n_rows) for row in range(n_rows)]
-        block = lax.ppermute(documents, "rows", back) if step else documents
+        behind = [(row, (row - step) % n_rows) for row in range(n_rows)]
+        block = lax.ppermute(documents, "rows", behind) if step else documents
 
         def ahead(row, step=step):
             return lax.rem(row + step, n_rows)
 
-        tiles = partial_scores(conditioned, query_ids, block, ahead, place, shares)
-        (total,) = row_sums(row_exchange(tiles), docs)
+        tiles = turned_scores(conditioned, query_ids, block, ahead, place, shares)
+        total = row_sum(row_exchange(tiles))
         onward = [(row, (row + step) % n_rows) for row in range(n_rows)]
         result.append(lax.ppermute(total, "rows", onward) if step else total)
     return jnp.stack(result)

time: 56 us -> 56.6 us (1.011)
  the two profiles are of different devices: /device:TPU:1 before, /device:TPU:0 now
where the time goes in v7:
time: 56.6 us; the launch traced here: 56.2 us
  starting transfers between devices  22.4 us (40%)
  waiting for transfers between devices  16.8 us (30%)
  Pallas kernels  14.4 us (25%)
  local copies, waits for them, and re-layouts  2.42 us (4%)
    ppermute x1, waiting for transfers between devices, along_line(): three = lax.ppermute(one, 'rows', ROUND_ONE)  12.7 us
    pallas_call x4, Pallas kernels, partial_scores(): pl.pallas_call(kernel, out_shape=out_shape, in_specs=[pl.BlockSpec(memory...  6.77 us
    ppermute x6, starting transfers between devices, row_exchange(): arrived.append(lax.ppermute(tiles[turn], 'layer', pairs))  6.56 us
    pallas_call x1, Pallas kernels, prepare(): pl.pallas_call(prepare_kernel, out_shape=jax.ShapeDtypeStruct((rows, dims...  6.29 us
    ppermute x2, starting transfers between devices, back(): return lax.ppermute(total, 'rows', tuple(enumerate(table)))  4.86 us
    ppermute x1, starting transfers between devices, along_line(): one = lax.ppermute(documents, 'rows', ROUND_ONE)  4.04 us
    all_to_all x1, starting transfers between devices, along_line(): lax.all_to_all(blocks, ('rows', 'layer'), 0, 0, axis_index_groups=groups,...  3.59 us
    ppermute x1, starting transfers between devices, along_line(): three = lax.ppermute(one, 'rows', ROUND_ONE)  3.38 us
  transfers between devices with their start and end apart: 12, of which 5 were waited for; matrix products, arithmetic and copies ran while one was open for 2% of the time, Pallas kernels for 23%

profile of v7, /device:TPU:0, one launch (start us, length us, event | category | flops | bytes accessed | tf_op | source)
XLA Modules:
  0.0 56.2 jit_solution(18005090820163482617)
XLA Ops:
  0.0 4.0 %collective-permute-start = (bf16[128,2048]{1,0:T(8,128)(2,1)}, bf16[128,2048]{1,0:T(8,128)(2,1)}, u32[]{:S(2)}, u32[]{:S(2)}) collective-permute-start(bf16[128,2048]{1,0:T(8,128)(2,1)} %documents_ref), channel_id=1, source_target_pairs={{0,8},{8,12},{12,4},{4,0},{1,9},{9,13},{13,5},{5,1},{2,10},{10,14}... | collective-permute-start | bytes 1572872 | tf_op jit(solution)/shard_map/ppermute | solution.py:202
  4.0 0.8 %copy.8.ids_ref = s32[512,1]{1,0:T(8,128)S(1)} copy(s32[512,1]{0,1:T(1,128)} %bitcast.6) | data formatting | bytes 4096 | tf_op jit(solution)/shard_map/broadcast_in_dim | solution.py:253
  4.9 0.0 copy-start.2
  4.9 6.3 %shard_map.64.queries_ref = bf16[512,2048]{1,0:T(8,128)(2,1)} custom-call(s32[4]{0:T(128)} %offsets.1, bf16[512,2048]{1,0:T(8,128)(2,1)} %queries_hbm.1, bf16[4,512,512]{2,1,0:T(8,128)(2,1)} %bases_hbm.1, f32[4,512]{1,0:T(4,128)} %values_hbm.1), custom_call_target="tpu_custom_call" | custom-call | flops 2147483648 | bytes 6291456 | tf_op jit(solution)/shard_map/pallas_call | solution.py:44
  11.2 0.1 pad_add_fusion.place
  11.3 0.0 copy-done.2
  11.3 0.0 copy-start
  11.3 1.6 %copy-done = bf16[512,2048]{1,0:T(8,128)(2,1)S(1)} copy-done((bf16[512,2048]{1,0:T(8,128)(2,1)S(1)}, bf16[512,2048]{1,0:T(8,128)(2,1)}, u32[]{:S(2)}) %copy-start) | copy-done | bytes 2097176
  12.9 1.2 %shard_map.65.own_ref = bf16[4,128,128]{2,1,0:T(8,128)(2,1)S(1)} custom-call(s32[2]{0:T(128)S(1)} %pad_add_fusion.place, bf16[512,2048]{1,0:T(8,128)(2,1)S(1)} %copy-done, s32[512,1]{1,0:T(8,128)S(1)} %copy.8.ids_ref, bf16[128,2048]{1,0:T(8,128)(2,1)S(1)} %copy-done.2), custom_call_target="tpu_custom_call" | custom-call | flops 268435456 | bytes 2621440 | tf_op jit(solution)/shard_map/pallas_call | solution.py:97
  14.1 0.0 copy-start.1
  14.1 1.4 %collective-permute-done.documents_ref = bf16[128,2048]{1,0:T(8,128)(2,1)} collective-permute-done((bf16[128,2048]{1,0:T(8,128)(2,1)}, bf16[128,2048]{1,0:T(8,128)(2,1)}, u32[]{:S(2)}, u32[]{:S(2)}) %collective-permute-start) | collective-permute-done | bytes 524320 | tf_op jit(solution)/shard_map/ppermute | solution.py:202
  15.5 3.4 %collective-permute-start.10 = (bf16[128,2048]{1,0:T(8,128)(2,1)}, bf16[128,2048]{1,0:T(8,128)(2,1)S(1)}, u32[]{:S(2)}, u32[]{:S(2)}) collective-permute-start(bf16[128,2048]{1,0:T(8,128)(2,1)} %collective-permute-done.documents_ref), channel_id=1, source_target_pairs={{0,8},{8,12},{12,4},{4,0},{1,9},{9,13},{13,5},{5,1},{2,10},{10,14}... | collective-permute-start | bytes 1572872 | tf_op jit(solution)/shard_map/ppermute | solution.py:211
  18.9 0.0 collective-permute-start.1
  18.9 12.7 %collective-permute-done.10.documents_ref = bf16[128,2048]{1,0:T(8,128)(2,1)S(1)} collective-permute-done((bf16[128,2048]{1,0:T(8,128)(2,1)}, bf16[128,2048]{1,0:T(8,128)(2,1)S(1)}, u32[]{:S(2)}, u32[]{:S(2)}) %collective-permute-start.10) | collective-permute-done | bytes 524320 | tf_op jit(solution)/shard_map/ppermute | solution.py:211
  31.6 2.0 %shard_map.70 = bf16[2,4,128,128]{3,2,1,0:T(8,128)(2,1)} custom-call(s32[2]{0:T(128)S(1)} %pad_add_fusion.place, bf16[512,2048]{1,0:T(8,128)(2,1)S(1)} %copy-done, s32[512,1]{1,0:T(8,128)S(1)} %copy.8.ids_ref, bf16[128,2048]{1,0:T(8,128)(2,1)S(1)} %collective-permute-done.10.documents_ref, bf16[4,128,128]{2,1,0:T(8,128)(2,1)S(1)} %shard_map.65.own_ref), custom_call_target="tpu_custom_call" | custom-call | flops 268435456 | bytes 2621440 | tf_op jit(solution)/shard_map/pallas_call | solution.py:97
  33.6 3.6 %all-to-all-start = ((bf16[8,128,128]{2,1,0:T(8,128)(2,1)}), bf16[8,128,128]{2,1,0:T(8,128)(2,1)S(1)}, u32[]{:S(2)}, u32[]{:S(2)}) async-start(bf16[8,128,128]{2,1,0:T(8,128)(2,1)} %bitcast.3), calls=%async_computation | async-start | bytes 524288 | tf_op jit(solution)/shard_map/all_to_all | solution.py:228
  37.2 0.0 copy-done.1
  37.2 1.8 %shard_map.66 = (bf16[128,128]{1,0:T(8,128)(2,1)S(1)}, bf16[128,128]{1,0:T(8,128)(2,1)S(1)}, bf16[128,128]{1,0:T(8,128)(2,1)S(1)}, bf16[128,128]{1,0:T(8,128)(2,1)S(1)}) custom-call(s32[2]{0:T(128)S(1)} %pad_add_fusion.place, bf16[512,2048]{1,0:T(8,128)(2,1)S(1)} %copy-done.1, s32[512,1]{1,0:T(8,128)S(1)} %copy.8.ids_ref, ...), custom_call_target="tpu_custom_call" | custom-call | flops 268435456 | bytes 2621440 | tf_op jit(solution)/shard_map/pallas_call | solution.py:97
  39.0 0.6 collective-permute-start.2
  39.5 1.7 %collective-permute-start.3 = (bf16[128,128]{1,0:T(8,128)(2,1)S(1)}, bf16[128,128]{1,0:T(8,128)(2,1)S(1)}, u32[]{:S(2)}, u32[]{:S(2)}) collective-permute-start(bf16[128,128]{1,0:T(8,128)(2,1)S(1)} %get-tuple-element.25), channel_id=1, source_target_pairs={{0,2},{1,3},{2,0},{3,1},{4,6},{5,7},{6,4},{7,5},{8,10},{9,11},{10,... | collective-permute-start | bytes 98312 | tf_op jit(solution)/shard_map/ppermute | solution.py:134
  41.2 1.3 %collective-permute-start.4 = (bf16[128,128]{1,0:T(8,128)(2,1)S(1)}, bf16[128,128]{1,0:T(8,128)(2,1)S(1)}, u32[]{:S(2)}, u32[]{:S(2)}) collective-permute-start(bf16[128,128]{1,0:T(8,128)(2,1)S(1)} %get-tuple-element.26), channel_id=1, source_target_pairs={{0,3},{1,0},{2,1},{3,2},{4,7},{5,4},{6,5},{7,6},{8,11},{9,8},{10,9... | collective-permute-start | bytes 98312 | tf_op jit(solution)/shard_map/ppermute | solution.py:134
  42.5 0.5 collective-permute-done.1.documents_ref
  43.0 0.0 collective-permute-done.2.refs_1_
  43.0 1.8 %shard_map.68 = (bf16[128,128]{1,0:T(8,128)(2,1)S(1)}, bf16[128,128]{1,0:T(8,128)(2,1)S(1)}, bf16[128,128]{1,0:T(8,128)(2,1)S(1)}, bf16[128,128]{1,0:T(8,128)(2,1)S(1)}) custom-call(s32[2]{0:T(128)S(1)} %pad_add_fusion.place, bf16[512,2048]{1,0:T(8,128)(2,1)S(1)} %copy-done.1, s32[512,1]{1,0:T(8,128)S(1)} %copy.8.ids_ref, ...), custom_call_target="tpu_custom_call" | custom-call | flops 268435456 | bytes 2621440 | tf_op jit(solution)/shard_map/pallas_call | solution.py:97
  44.8 0.1 collective-permute-start.6
  44.8 1.6 %collective-permute-start.7 = (bf16[128,128]{1,0:T(8,128)(2,1)S(1)}, bf16[128,128]{1,0:T(8,128)(2,1)S(1)}, u32[]{:S(2)}, u32[]{:S(2)}) collective-permute-start(bf16[128,128]{1,0:T(8,128)(2,1)S(1)} %get-tuple-element.30), channel_id=1, source_target_pairs={{0,2},{1,3},{2,0},{3,1},{4,6},{5,7},{6,4},{7,5},{8,10},{9,11},{10,... | collective-permute-start | bytes 98312 | tf_op jit(solution)/shard_map/ppermute | solution.py:134
  46.4 1.4 %collective-permute-start.8 = (bf16[128,128]{1,0:T(8,128)(2,1)S(1)}, bf16[128,128]{1,0:T(8,128)(2,1)S(1)}, u32[]{:S(2)}, u32[]{:S(2)}) collective-permute-start(bf16[128,128]{1,0:T(8,128)(2,1)S(1)} %get-tuple-element.31), channel_id=1, source_target_pairs={{0,3},{1,0},{2,1},{3,2},{4,7},{5,4},{6,5},{7,6},{8,11},{9,8},{10,9... | collective-permute-start | bytes 98312 | tf_op jit(solution)/shard_map/ppermute | solution.py:134
  47.8 0.0 collective-permute-done.3.refs_2_
  47.8 0.0 collective-permute-done.4.refs_3_
  47.8 2.4 %collective-permute-start.5 = (f32[128,128]{1,0:T(8,128)S(1)}, f32[128,128]{1,0:T(8,128)S(1)}, u32[]{:S(2)}, u32[]{:S(2)}) collective-permute-start(f32[128,128]{1,0:T(8,128)S(1)} %shard_map.67), channel_id=1, source_target_pairs={{0,4},{4,12},{8,0},{12,8},{1,5},{5,13},{9,1},{13,9},{2,6},{6,14},{... | collective-permute-start | bytes 196616 | tf_op jit(solution)/shard_map/ppermute | solution.py:200
  50.2 0.0 collective-permute-done.6.refs_1_
  50.2 0.0 collective-permute-done.7.refs_2_
  50.2 0.0 collective-permute-done.8.refs_3_
  50.3 2.5 %collective-permute-start.9 = (f32[128,128]{1,0:T(8,128)S(1)}, f32[128,128]{1,0:T(8,128)S(1)}, u32[]{:S(2)}, u32[]{:S(2)}) collective-permute-start(f32[128,128]{1,0:T(8,128)S(1)} %shard_map.69), channel_id=1, source_target_pairs={{0,8},{4,0},{8,12},{12,4},{1,9},{5,1},{9,13},{13,5},{2,10},{6,2},{... | collective-permute-start | bytes 196616 | tf_op jit(solution)/shard_map/ppermute | solution.py:200
  52.7 0.7 %collective-permute-done.5.first_ref = f32[128,128]{1,0:T(8,128)S(1)} collective-permute-done((f32[128,128]{1,0:T(8,128)S(1)}, f32[128,128]{1,0:T(8,128)S(1)}, u32[]{:S(2)}, u32[]{:S(2)}) %collective-permute-start.5) | collective-permute-done | bytes 65568 | tf_op jit(solution)/shard_map/ppermute | solution.py:200
  53.4 1.5 %collective-permute-done.9.second_ref = f32[128,128]{1,0:T(8,128)S(1)} collective-permute-done((f32[128,128]{1,0:T(8,128)S(1)}, f32[128,128]{1,0:T(8,128)S(1)}, u32[]{:S(2)}, u32[]{:S(2)}) %collective-permute-start.9) | collective-permute-done | bytes 65568 | tf_op jit(solution)/shard_map/ppermute | solution.py:200
  54.9 0.0 all-to-all-done
  54.9 1.3 %shard_map.71 = f32[4,128,128]{2,1,0:T(8,128)} custom-call(s32[2]{0:T(128)S(1)} %pad_add_fusion.place, f32[128,128]{1,0:T(8,128)S(1)} %collective-permute-done.5.first_ref, f32[128,128]{1,0:T(8,128)S(1)} %collective-permute-done.9.second_ref, bf16[2,4,128,128]{3,2,1,0:T(8,128)(2,1)S(1)} %bitcast.5), custom_call_target="tpu_custom_call" | custom-call | tf_op jit(solution)/shard_map/pallas_call | solution.py:182
  (2 shorter events, 0.0 us)
Async XLA Ops:
  0.0 15.5 %collective-permute-start = (bf16[128,2048]{1,0:T(8,128)(2,1)}, bf16[128,2048]{1,0:T(8,128)(2,1)}, u32[]{:S(2)}, u32[]{:S(2)}) collective-permute-start(bf16[128,2048]{1,0:T(8,128)(2,1)} %documents_ref), channel_id=1, source_target_pairs={{0,8},{8,12},{12,4},{4,0},{1,9},{9,13},{13,5},{5,1},{2,10},{10,14}... | collective-permute-start | bytes 1572872 | tf_op jit(solution)/shard_map/ppermute | solution.py:202
  4.9 6.4 %copy-start.2 = (bf16[128,2048]{1,0:T(8,128)(2,1)S(1)}, bf16[128,2048]{1,0:T(8,128)(2,1)}, u32[]{:S(2)}) copy-start(bf16[128,2048]{1,0:T(8,128)(2,1)} %documents_ref) | copy-start | bytes 1572868
  11.3 1.6 %copy-start = (bf16[512,2048]{1,0:T(8,128)(2,1)S(1)}, bf16[512,2048]{1,0:T(8,128)(2,1)}, u32[]{:S(2)}) copy-start(bf16[512,2048]{1,0:T(8,128)(2,1)} %shard_map.64.queries_ref) | copy-start | bytes 6291460
  14.1 23.1 %copy-start.1 = (bf16[512,2048]{1,0:T(8,128)(2,1)S(1)}, bf16[512,2048]{1,0:T(8,128)(2,1)}, u32[]{:S(2)}) copy-start(bf16[512,2048]{1,0:T(8,128)(2,1)} %shard_map.64.queries_ref) | copy-start | bytes 6291460
  15.5 16.1 %collective-permute-start.10 = (bf16[128,2048]{1,0:T(8,128)(2,1)}, bf16[128,2048]{1,0:T(8,128)(2,1)S(1)}, u32[]{:S(2)}, u32[]{:S(2)}) collective-permute-start(bf16[128,2048]{1,0:T(8,128)(2,1)} %collective-permute-done.documents_ref), channel_id=1, source_target_pairs={{0,8},{8,12},{12,4},{4,0},{1,9},{9,13},{13,5},{5,1},{2,10},{10,14}... | collective-permute-start | bytes 1572872 | tf_op jit(solution)/shard_map/ppermute | solution.py:211
  18.9 24.0 %collective-permute-start.1 = (bf16[128,2048]{1,0:T(8,128)(2,1)S(1)}, bf16[128,2048]{1,0:T(8,128)(2,1)}, u32[]{:S(2)}, u32[]{:S(2)}) collective-permute-start(bf16[128,2048]{1,0:T(8,128)(2,1)S(1)} %copy-done.2), channel_id=1, source_target_pairs={{0,4},{4,12},{12,8},{8,0},{1,5},{5,13},{13,9},{9,1},{2,6},{6,14},{... | collective-permute-start | bytes 1572872 | tf_op jit(solution)/shard_map/ppermute | solution.py:204
  33.6 21.3 %all-to-all-start = ((bf16[8,128,128]{2,1,0:T(8,128)(2,1)}), bf16[8,128,128]{2,1,0:T(8,128)(2,1)S(1)}, u32[]{:S(2)}, u32[]{:S(2)}) async-start(bf16[8,128,128]{2,1,0:T(8,128)(2,1)} %bitcast.3), calls=%async_computation | async-start | bytes 524288 | tf_op jit(solution)/shard_map/all_to_all | solution.py:228
  39.0 4.0 %collective-permute-start.2 = (bf16[128,128]{1,0:T(8,128)(2,1)S(1)}, bf16[128,128]{1,0:T(8,128)(2,1)S(1)}, u32[]{:S(2)}, u32[]{:S(2)}) collective-permute-start(bf16[128,128]{1,0:T(8,128)(2,1)S(1)} %get-tuple-element.23), channel_id=1, source_target_pairs={{0,1},{1,2},{2,3},{3,0},{4,5},{5,6},{6,7},{7,4},{8,9},{9,10},{10,1... | collective-permute-start | bytes 98312 | tf_op jit(solution)/shard_map/ppermute | solution.py:134
  39.5 8.3 %collective-permute-start.3 = (bf16[128,128]{1,0:T(8,128)(2,1)S(1)}, bf16[128,128]{1,0:T(8,128)(2,1)S(1)}, u32[]{:S(2)}, u32[]{:S(2)}) collective-permute-start(bf16[128,128]{1,0:T(8,128)(2,1)S(1)} %get-tuple-element.25), channel_id=1, source_target_pairs={{0,2},{1,3},{2,0},{3,1},{4,6},{5,7},{6,4},{7,5},{8,10},{9,11},{10,... | collective-permute-start | bytes 98312 | tf_op jit(solution)/shard_map/ppermute | solution.py:134
  41.2 6.6 %collective-permute-start.4 = (bf16[128,128]{1,0:T(8,128)(2,1)S(1)}, bf16[128,128]{1,0:T(8,128)(2,1)S(1)}, u32[]{:S(2)}, u32[]{:S(2)}) collective-permute-start(bf16[128,128]{1,0:T(8,128)(2,1)S(1)} %get-tuple-element.26), channel_id=1, source_target_pairs={{0,3},{1,0},{2,1},{3,2},{4,7},{5,4},{6,5},{7,6},{8,11},{9,8},{10,9... | collective-permute-start | bytes 98312 | tf_op jit(solution)/shard_map/ppermute | solution.py:134
  44.8 5.5 %collective-permute-start.6 = (bf16[128,128]{1,0:T(8,128)(2,1)S(1)}, bf16[128,128]{1,0:T(8,128)(2,1)S(1)}, u32[]{:S(2)}, u32[]{:S(2)}) collective-permute-start(bf16[128,128]{1,0:T(8,128)(2,1)S(1)} %get-tuple-element.29), channel_id=1, source_target_pairs={{0,1},{1,2},{2,3},{3,0},{4,5},{5,6},{6,7},{7,4},{8,9},{9,10},{10,1... | collective-permute-start | bytes 98312 | tf_op jit(solution)/shard_map/ppermute | solution.py:134
  44.8 5.4 %collective-permute-start.7 = (bf16[128,128]{1,0:T(8,128)(2,1)S(1)}, bf16[128,128]{1,0:T(8,128)(2,1)S(1)}, u32[]{:S(2)}, u32[]{:S(2)}) collective-permute-start(bf16[128,128]{1,0:T(8,128)(2,1)S(1)} %get-tuple-element.30), channel_id=1, source_target_pairs={{0,2},{1,3},{2,0},{3,1},{4,6},{5,7},{6,4},{7,5},{8,10},{9,11},{10,... | collective-permute-start | bytes 98312 | tf_op jit(solution)/shard_map/ppermute | solution.py:134
  46.4 3.8 %collective-permute-start.8 = (bf16[128,128]{1,0:T(8,128)(2,1)S(1)}, bf16[128,128]{1,0:T(8,128)(2,1)S(1)}, u32[]{:S(2)}, u32[]{:S(2)}) collective-permute-start(bf16[128,128]{1,0:T(8,128)(2,1)S(1)} %get-tuple-element.31), channel_id=1, source_target_pairs={{0,3},{1,0},{2,1},{3,2},{4,7},{5,4},{6,5},{7,6},{8,11},{9,8},{10,9... | collective-permute-start | bytes 98312 | tf_op jit(solution)/shard_map/ppermute | solution.py:134
  47.8 5.6 %collective-permute-start.5 = (f32[128,128]{1,0:T(8,128)S(1)}, f32[128,128]{1,0:T(8,128)S(1)}, u32[]{:S(2)}, u32[]{:S(2)}) collective-permute-start(f32[128,128]{1,0:T(8,128)S(1)} %shard_map.67), channel_id=1, source_target_pairs={{0,4},{4,12},{8,0},{12,8},{1,5},{5,13},{9,1},{13,9},{2,6},{6,14},{... | collective-permute-start | bytes 196616 | tf_op jit(solution)/shard_map/ppermute | solution.py:200
  50.3 4.6 %collective-permute-start.9 = (f32[128,128]{1,0:T(8,128)S(1)}, f32[128,128]{1,0:T(8,128)S(1)}, u32[]{:S(2)}, u32[]{:S(2)}) collective-permute-start(f32[128,128]{1,0:T(8,128)S(1)} %shard_map.69), channel_id=1, source_target_pairs={{0,8},{4,0},{8,12},{12,4},{1,9},{5,1},{9,13},{13,5},{2,10},{6,2},{... | collective-permute-start | bytes 196616 | tf_op jit(solution)/shard_map/ppermute | solution.py:200

commit v8 on v6

--- a/solution.py
+++ b/solution.py
@@ -153,36 +153,22 @@
     return pick([(block - table.index(block)) % STEPS for block in range(STEPS)])
 
 
-def final_kernel(tables, place, own_ref, *refs):
+def final_kernel(place, own_ref, *refs):
     *round_refs, out_ref = refs
     out_ref[0] = own_ref[...]
-    for spot, step_at in enumerate(tables):
-        parts = round_refs[spot:] if spot == len(tables) - 1 else round_refs[spot : spot + 1]
-        out_ref[step_at(place[1])] = total_of(parts)
-
-
-def final_scores(place, own, rounds, last, tables):
+    for round_ref, table in zip(round_refs, (BLOCK_ONE, BLOCK_TWO, BLOCK_LAST)):
+        out_ref[step_of(table)(place[1])] = round_ref[...]
+
+
+def final_scores(place, own, rounds):
     vmem = pl.BlockSpec(memory_space=pltpu.VMEM)
     return pl.pallas_call(
-        functools.partial(final_kernel, tables),
+        final_kernel,
         out_shape=jax.ShapeDtypeStruct((STEPS,) + own.shape, jnp.float32),
-        in_specs=[pl.BlockSpec(memory_space=pltpu.SMEM)] + [vmem] * (1 + len(rounds) + len(last)),
+        in_specs=[pl.BlockSpec(memory_space=pltpu.SMEM)] + [vmem] * (1 + len(rounds)),
         out_specs=vmem,
         compiler_params=pltpu.CompilerParams(vmem_limit_bytes=4 * MIB),
-    )(place, own, *rounds, *last)
-
-
-def exchange(tiles, target_of):
-    n_rows, shares = lax.axis_size("rows"), lax.axis_size("layer")
-    arrived = []
-    for turn, tile in enumerate(tiles):
-        pairs = [
-            (row * shares + lay, target_of(row) * shares + (lay + turn) % shares)
-            for row in range(n_rows)
-            for lay in range(shares)
-        ]
-        arrived.append(lax.ppermute(tile, ("rows", "layer"), pairs))
-    return arrived
+    )(place, own, *rounds)
 
 
 def along_line(documents, conditioned, query_ids, place, shares):
@@ -190,6 +176,9 @@
 
     def scored(block, block_of, front=()):
         return partial_scores(conditioned, query_ids, block, block_of, place, shares, front)
+
+    def back(total, table):
+        return lax.ppermute(total, "rows", tuple(enumerate(table)))
 
     one = lax.ppermute(documents, "rows", ROUND_ONE)
     later, conditioned = lax.optimization_barrier((documents, conditioned))
@@ -201,12 +190,13 @@
     tiles = row_exchange(scored(one, pick(BLOCK_ONE), tiles))
     two, tiles[1] = lax.optimization_barrier((two, tiles[1]))
     own, first = row_sums(tiles, docs)
-    first = lax.ppermute(first, "rows", tuple(enumerate(BLOCK_ONE)))
+    first = back(first, BLOCK_ONE)
     (second,) = row_sums(row_exchange(scored(two, pick(BLOCK_TWO))), docs)
-    second = lax.ppermute(second, "rows", tuple(enumerate(BLOCK_TWO)))
-    last = exchange(scored(three, pick(BLOCK_LAST)), BLOCK_LAST.__getitem__)
-    tables = [step_of(table) for table in (BLOCK_ONE, BLOCK_TWO, BLOCK_LAST)]
-    return final_scores(place, own, [first, second], last, tables)
+    second = back(second, BLOCK_TWO)
+    three, first, second = lax.optimization_barrier((three, first, second))
+    (last,) = row_sums(row_exchange(scored(three, pick(BLOCK_LAST))), docs)
+    last = back(last, BLOCK_LAST)
+    return final_scores(place, own, [first, second, last])
 
 
 def around_ring(documents, conditioned, query_ids, place, shares):

time: 56 us -> 56.1 us (level)
  the two profiles are of different devices: /device:TPU:1 before, /device:TPU:0 now
where the time goes in v8:
time: 56.1 us; the launch traced here: 55.9 us
  starting transfers between devices  21.3 us (38%)
  waiting for transfers between devices  20.1 us (36%)
  Pallas kernels  12.6 us (22%)
  local copies, waits for them, and re-layouts  1.75 us (3%)
    ppermute x9, starting transfers between devices, row_exchange(): arrived.append(lax.ppermute(tiles[turn], 'layer', pairs))  9 us
    ppermute x3, waiting for transfers between devices, back(): return lax.ppermute(total, 'rows', tuple(enumerate(table)))  8.92 us
    pallas_call x1, Pallas kernels, prepare(): pl.pallas_call(prepare_kernel, out_shape=jax.ShapeDtypeStruct((rows, dims...  6.14 us
    ppermute x1, waiting for transfers between devices, along_line(): two = lax.ppermute(later, 'rows', ROUND_TWO)  5.37 us
    pallas_call x4, Pallas kernels, partial_scores(): pl.pallas_call(functools.partial(score_kernel, shares, block_of), out_sha...  5.11 us
    ppermute x3, starting transfers between devices, back(): return lax.ppermute(total, 'rows', tuple(enumerate(table)))  4.95 us
    ppermute x1, starting transfers between devices, along_line(): one = lax.ppermute(documents, 'rows', ROUND_ONE)  4.04 us
    ppermute x1, waiting for transfers between devices, along_line(): one = lax.ppermute(documents, 'rows', ROUND_ONE)  3.34 us
  transfers between devices with their start and end apart: 15, of which 10 were waited for; matrix products, arithmetic and copies ran while one was open for 0% of the time, Pallas kernels for 18%

profile of v8, /device:TPU:0, one launch (start us, length us, event | category | flops | bytes accessed | tf_op | source)
XLA Modules:
  0.0 55.9 jit_solution(4826930095408394252)
XLA Ops:
  0.0 0.0 copy-start.1
  0.0 0.0 copy-start.2
  0.0 4.0 %collective-permute-start = (bf16[128,2048]{1,0:T(8,128)(2,1)}, bf16[128,2048]{1,0:T(8,128)(2,1)S(1)}, u32[]{:S(2)}, u32[]{:S(2)}) collective-permute-start(bf16[128,2048]{1,0:T(8,128)(2,1)} %documents_ref), channel_id=1, source_target_pairs={{0,8},{8,12},{12,4},{4,0},{1,9},{9,13},{13,5},{5,1},{2,10},{10,14}... | collective-permute-start | bytes 1572872 | tf_op jit(solution)/shard_map/ppermute | solution.py:183
  4.0 6.1 %shard_map.64.queries_ref = bf16[512,2048]{1,0:T(8,128)(2,1)} custom-call(s32[4]{0:T(128)} %offsets.1, bf16[512,2048]{1,0:T(8,128)(2,1)} %queries_hbm.1, bf16[4,512,512]{2,1,0:T(8,128)(2,1)} %bases_hbm.1, f32[4,512]{1,0:T(4,128)} %values_hbm.1), custom_call_target="tpu_custom_call" | custom-call | flops 2147483648 | bytes 6291456 | tf_op jit(solution)/shard_map/pallas_call | solution.py:44
  10.2 0.0 copy-done.1
  10.2 0.1 collective-permute-start.1
  10.3 0.0 copy-done.2
  10.3 0.1 copy.8.ids_ref
  10.4 0.1 pad_add_fusion.place
  10.5 0.0 copy-start
  10.5 1.6 %copy-done = bf16[512,2048]{1,0:T(8,128)(2,1)S(1)} copy-done((bf16[512,2048]{1,0:T(8,128)(2,1)S(1)}, bf16[512,2048]{1,0:T(8,128)(2,1)}, u32[]{:S(2)}) %copy-start) | copy-done | bytes 2097176
  12.1 1.3 %shard_map.65 = (bf16[128,128]{1,0:T(8,128)(2,1)S(1)}, bf16[128,128]{1,0:T(8,128)(2,1)S(1)}, bf16[128,128]{1,0:T(8,128)(2,1)S(1)}, bf16[128,128]{1,0:T(8,128)(2,1)S(1)}) custom-call(s32[2]{0:T(128)S(1)} %pad_add_fusion.place, bf16[512,2048]{1,0:T(8,128)(2,1)S(1)} %copy-done, s32[512,1]{1,0:T(8,128)S(1)} %copy.8.ids_ref, bf16[128,2048]{1,0:T(8,128)(2,1)S(1)} %copy-done.1), custom_call_target="tpu_custom_call" | custom-call | flops 268435456 | bytes 2621440 | tf_op jit(solution)/shard_map/pallas_call | solution.py:85
  13.4 3.3 %collective-permute-done.documents_ref = bf16[128,2048]{1,0:T(8,128)(2,1)S(1)} collective-permute-done((bf16[128,2048]{1,0:T(8,128)(2,1)}, bf16[128,2048]{1,0:T(8,128)(2,1)S(1)}, u32[]{:S(2)}, u32[]{:S(2)}) %collective-permute-start) | collective-permute-done | bytes 524320 | tf_op jit(solution)/shard_map/ppermute | solution.py:183
  16.7 3.3 %collective-permute-start.5 = (bf16[128,2048]{1,0:T(8,128)(2,1)S(1)}, bf16[128,2048]{1,0:T(8,128)(2,1)S(1)}, u32[]{:S(2)}, u32[]{:S(2)}) collective-permute-start(bf16[128,2048]{1,0:T(8,128)(2,1)S(1)} %collective-permute-done.documents_ref), channel_id=1, source_target_pairs={{0,8},{8,12},{12,4},{4,0},{1,9},{9,13},{13,5},{5,1},{2,10},{10,14}... | collective-permute-start | bytes 1572872 | tf_op jit(solution)/shard_map/ppermute | solution.py:188
  20.0 1.3 %shard_map.66 = (bf16[128,256]{1,0:T(8,128)(2,1)S(1)}, bf16[128,256]{1,0:T(8,128)(2,1)S(1)}, bf16[128,256]{1,0:T(8,128)(2,1)S(1)}, bf16[128,256]{1,0:T(8,128)(2,1)S(1)}) custom-call(s32[2]{0:T(128)S(1)} %pad_add_fusion.place, bf16[512,2048]{1,0:T(8,128)(2,1)S(1)} %copy-done, s32[512,1]{1,0:T(8,128)S(1)} %copy.8.ids_ref, ...), custom_call_target="tpu_custom_call" | custom-call | flops 268435456 | bytes 2621440 | tf_op jit(solution)/shard_map/pallas_call | solution.py:85
  21.3 0.1 collective-permute-start.2
  21.4 1.6 %collective-permute-start.3 = (bf16[128,256]{1,0:T(8,128)(2,1)S(1)}, bf16[128,256]{1,0:T(8,128)(2,1)S(1)}, u32[]{:S(2)}, u32[]{:S(2)}) collective-permute-start(bf16[128,256]{1,0:T(8,128)(2,1)S(1)} %get-tuple-element.49), channel_id=1, source_target_pairs={{0,2},{1,3},{2,0},{3,1},{4,6},{5,7},{6,4},{7,5},{8,10},{9,11},{10,... | collective-permute-start | bytes 196616 | tf_op jit(solution)/shard_map/ppermute | solution.py:118
  22.9 1.4 %collective-permute-start.4 = (bf16[128,256]{1,0:T(8,128)(2,1)S(1)}, bf16[128,256]{1,0:T(8,128)(2,1)S(1)}, u32[]{:S(2)}, u32[]{:S(2)}) collective-permute-start(bf16[128,256]{1,0:T(8,128)(2,1)S(1)} %get-tuple-element.50), channel_id=1, source_target_pairs={{0,3},{1,0},{2,1},{3,2},{4,7},{5,4},{6,5},{7,6},{8,11},{9,8},{10,9... | collective-permute-start | bytes 196616 | tf_op jit(solution)/shard_map/ppermute | solution.py:118
  24.3 5.4 %collective-permute-done.1.documents_ref = bf16[128,2048]{1,0:T(8,128)(2,1)S(1)} collective-permute-done((bf16[128,2048]{1,0:T(8,128)(2,1)S(1)}, bf16[128,2048]{1,0:T(8,128)(2,1)S(1)}, u32[]{:S(2)}, u32[]{:S(2)}) %collective-permute-start.1) | collective-permute-done | bytes 524320 | tf_op jit(solution)/shard_map/ppermute | solution.py:185
  29.7 0.0 collective-permute-done.2.refs_1_
  29.7 1.3 %shard_map.68 = (bf16[128,128]{1,0:T(8,128)(2,1)S(1)}, bf16[128,128]{1,0:T(8,128)(2,1)S(1)}, bf16[128,128]{1,0:T(8,128)(2,1)S(1)}, bf16[128,128]{1,0:T(8,128)(2,1)S(1)}) custom-call(s32[2]{0:T(128)S(1)} %pad_add_fusion.place, bf16[512,2048]{1,0:T(8,128)(2,1)S(1)} %copy-done, s32[512,1]{1,0:T(8,128)S(1)} %copy.8.ids_ref, ...), custom_call_target="tpu_custom_call" | custom-call | flops 268435456 | bytes 2621440 | tf_op jit(solution)/shard_map/pallas_call | solution.py:85
  31.0 0.1 collective-permute-start.7
  31.0 1.6 %collective-permute-start.8 = (bf16[128,128]{1,0:T(8,128)(2,1)S(1)}, bf16[128,128]{1,0:T(8,128)(2,1)S(1)}, u32[]{:S(2)}, u32[]{:S(2)}) collective-permute-start(bf16[128,128]{1,0:T(8,128)(2,1)S(1)} %get-tuple-element.56), channel_id=1, source_target_pairs={{0,2},{1,3},{2,0},{3,1},{4,6},{5,7},{6,4},{7,5},{8,10},{9,11},{10,... | collective-permute-start | bytes 98312 | tf_op jit(solution)/shard_map/ppermute | solution.py:118
  32.6 0.0 collective-permute-done.3.refs_2_
  32.6 1.4 %collective-permute-start.9 = (bf16[128,128]{1,0:T(8,128)(2,1)S(1)}, bf16[128,128]{1,0:T(8,128)(2,1)S(1)}, u32[]{:S(2)}, u32[]{:S(2)}) collective-permute-start(bf16[128,128]{1,0:T(8,128)(2,1)S(1)} %get-tuple-element.57), channel_id=1, source_target_pairs={{0,3},{1,0},{2,1},{3,2},{4,7},{5,4},{6,5},{7,6},{8,11},{9,8},{10,9... | collective-permute-start | bytes 98312 | tf_op jit(solution)/shard_map/ppermute | solution.py:118
  34.0 0.0 collective-permute-done.4.refs_3_
  34.0 0.7 %collective-permute-start.6 = (f32[128,128]{1,0:T(8,128)S(1)}, f32[128,128]{1,0:T(8,128)S(1)}, u32[]{:S(2)}, u32[]{:S(2)}) collective-permute-start(f32[128,128]{1,0:T(8,128)S(1)} %get-tuple-element.52), channel_id=1, source_target_pairs={{0,4},{4,12},{8,0},{12,8},{1,5},{5,13},{9,1},{13,9},{2,6},{6,14},{... | collective-permute-start | bytes 196616 | tf_op jit(solution)/shard_map/ppermute | solution.py:181
  34.7 0.0 collective-permute-done.7.refs_1_
  34.7 0.3 collective-permute-done.8.refs_2_
  35.0 0.6 %collective-permute-done.9.refs_3_ = bf16[128,128]{1,0:T(8,128)(2,1)S(1)} collective-permute-done((bf16[128,128]{1,0:T(8,128)(2,1)S(1)}, bf16[128,128]{1,0:T(8,128)(2,1)S(1)}, u32[]{:S(2)}, u32[]{:S(2)}) %collective-permute-start.9) | collective-permute-done | bytes 32800 | tf_op jit(solution)/shard_map/ppermute | solution.py:118
  35.6 1.5 %collective-permute-start.10 = (f32[128,128]{1,0:T(8,128)S(1)}, f32[128,128]{1,0:T(8,128)S(1)}, u32[]{:S(2)}, u32[]{:S(2)}) collective-permute-start(f32[128,128]{1,0:T(8,128)S(1)} %shard_map.69), channel_id=1, source_target_pairs={{0,8},{4,0},{8,12},{12,4},{1,9},{5,1},{9,13},{13,5},{2,10},{6,2},{... | collective-permute-start | bytes 196616 | tf_op jit(solution)/shard_map/ppermute | solution.py:181
  37.1 4.9 %collective-permute-done.6.refs_0_ = f32[128,128]{1,0:T(8,128)S(1)} collective-permute-done((f32[128,128]{1,0:T(8,128)S(1)}, f32[128,128]{1,0:T(8,128)S(1)}, u32[]{:S(2)}, u32[]{:S(2)}) %collective-permute-start.6) | collective-permute-done | bytes 65568 | tf_op jit(solution)/shard_map/ppermute | solution.py:181
  42.0 0.2 collective-permute-done.10.refs_1_
  42.2 0.0 collective-permute-done.5.documents_ref
  42.2 1.3 %shard_map.70 = (bf16[128,128]{1,0:T(8,128)(2,1)S(1)}, bf16[128,128]{1,0:T(8,128)(2,1)S(1)}, bf16[128,128]{1,0:T(8,128)(2,1)S(1)}, bf16[128,128]{1,0:T(8,128)(2,1)S(1)}) custom-call(s32[2]{0:T(128)S(1)} %pad_add_fusion.place, bf16[512,2048]{1,0:T(8,128)(2,1)S(1)} %copy-done, s32[512,1]{1,0:T(8,128)S(1)} %copy.8.ids_ref, ...), custom_call_target="tpu_custom_call" | custom-call | flops 268435456 | bytes 2621440 | tf_op jit(solution)/shard_map/pallas_call | solution.py:85
  43.4 0.1 collective-permute-start.11
  43.5 1.6 %collective-permute-start.12 = (bf16[128,128]{1,0:T(8,128)(2,1)S(1)}, bf16[128,128]{1,0:T(8,128)(2,1)S(1)}, u32[]{:S(2)}, u32[]{:S(2)}) collective-permute-start(bf16[128,128]{1,0:T(8,128)(2,1)S(1)} %get-tuple-element.63), channel_id=1, source_target_pairs={{0,2},{1,3},{2,0},{3,1},{4,6},{5,7},{6,4},{7,5},{8,10},{9,11},{10,... | collective-permute-start | bytes 98312 | tf_op jit(solution)/shard_map/ppermute | solution.py:118
  45.1 1.4 %collective-permute-start.13 = (bf16[128,128]{1,0:T(8,128)(2,1)S(1)}, bf16[128,128]{1,0:T(8,128)(2,1)S(1)}, u32[]{:S(2)}, u32[]{:S(2)}) collective-permute-start(bf16[128,128]{1,0:T(8,128)(2,1)S(1)} %get-tuple-element.64), channel_id=1, source_target_pairs={{0,3},{1,0},{2,1},{3,2},{4,7},{5,4},{6,5},{7,6},{8,11},{9,8},{10,9... | collective-permute-start | bytes 98312 | tf_op jit(solution)/shard_map/ppermute | solution.py:118
  46.5 0.4 collective-permute-done.11.refs_1_
  46.8 0.7 %collective-permute-done.12.refs_2_ = bf16[128,128]{1,0:T(8,128)(2,1)S(1)} collective-permute-done((bf16[128,128]{1,0:T(8,128)(2,1)S(1)}, bf16[128,128]{1,0:T(8,128)(2,1)S(1)}, u32[]{:S(2)}, u32[]{:S(2)}) %collective-permute-start.12) | collective-permute-done | bytes 32800 | tf_op jit(solution)/shard_map/ppermute | solution.py:118
  47.5 0.6 collective-permute-done.13.refs_3_
  48.1 2.7 %collective-permute-start.14 = (f32[128,128]{1,0:T(8,128)S(1)}, f32[128,128]{1,0:T(8,128)S(1)}, u32[]{:S(2)}, u32[]{:S(2)}) collective-permute-start(f32[128,128]{1,0:T(8,128)S(1)} %shard_map.71), channel_id=1, source_target_pairs={{0,12},{4,8},{8,4},{12,0},{1,13},{5,9},{9,5},{13,1},{2,14},{6,10},... | collective-permute-start | bytes 196616 | tf_op jit(solution)/shard_map/ppermute | solution.py:181
  50.8 3.8 %collective-permute-done.14.refs_2_ = f32[128,128]{1,0:T(8,128)S(1)} collective-permute-done((f32[128,128]{1,0:T(8,128)S(1)}, f32[128,128]{1,0:T(8,128)S(1)}, u32[]{:S(2)}, u32[]{:S(2)}) %collective-permute-start.14) | collective-permute-done | bytes 65568 | tf_op jit(solution)/shard_map/ppermute | solution.py:181
  54.7 1.3 %shard_map.72 = f32[4,128,128]{2,1,0:T(8,128)} custom-call(s32[2]{0:T(128)S(1)} %pad_add_fusion.place, f32[128,128]{1,0:T(8,128)S(1)} %get-tuple-element.51.own_ref, f32[128,128]{1,0:T(8,128)S(1)} %collective-permute-done.6.refs_0_, f32[128,128]{1,0:T(8,128)S(1)} %collective-permute-done.10.refs_1_, f32[128,128]{1,0:T(8,128)S(1)} %collective-permute-done.14.refs_2_), custom_call_target="tpu_custom_call" | custom-call | tf_op jit(solution)/shard_map/pallas_call | solution.py:165
  (3 shorter events, 0.1 us)
Async XLA Ops:
  0.0 10.2 %copy-start.1 = (bf16[128,2048]{1,0:T(8,128)(2,1)S(1)}, bf16[128,2048]{1,0:T(8,128)(2,1)}, u32[]{:S(2)}) copy-start(bf16[128,2048]{1,0:T(8,128)(2,1)} %documents_ref) | copy-start | bytes 1572868
  0.0 10.3 %copy-start.2 = (s32[512]{0:T(512)S(1)}, s32[512]{0:T(512)}, u32[]{:S(2)}) copy-start(s32[512]{0:T(512)} %param.11) | copy-start | bytes 6148
  0.0 16.7 %collective-permute-start = (bf16[128,2048]{1,0:T(8,128)(2,1)}, bf16[128,2048]{1,0:T(8,128)(2,1)S(1)}, u32[]{:S(2)}, u32[]{:S(2)}) collective-permute-start(bf16[128,2048]{1,0:T(8,128)(2,1)} %documents_ref), channel_id=1, source_target_pairs={{0,8},{8,12},{12,4},{4,0},{1,9},{9,13},{13,5},{5,1},{2,10},{10,14}... | collective-permute-start | bytes 1572872 | tf_op jit(solution)/shard_map/ppermute | solution.py:183
  10.2 19.5 %collective-permute-start.1 = (bf16[128,2048]{1,0:T(8,128)(2,1)S(1)}, bf16[128,2048]{1,0:T(8,128)(2,1)S(1)}, u32[]{:S(2)}, u32[]{:S(2)}) collective-permute-start(bf16[128,2048]{1,0:T(8,128)(2,1)S(1)} %copy-done.1), channel_id=1, source_target_pairs={{0,4},{4,12},{12,8},{8,0},{1,5},{5,13},{13,9},{9,1},{2,6},{6,14},{... | collective-permute-start | bytes 1572872 | tf_op jit(solution)/shard_map/ppermute | solution.py:185
  10.5 1.6 %copy-start = (bf16[512,2048]{1,0:T(8,128)(2,1)S(1)}, bf16[512,2048]{1,0:T(8,128)(2,1)}, u32[]{:S(2)}) copy-start(bf16[512,2048]{1,0:T(8,128)(2,1)} %shard_map.64.queries_ref) | copy-start | bytes 6291460
  16.7 25.4 %collective-permute-start.5 = (bf16[128,2048]{1,0:T(8,128)(2,1)S(1)}, bf16[128,2048]{1,0:T(8,128)(2,1)S(1)}, u32[]{:S(2)}, u32[]{:S(2)}) collective-permute-start(bf16[128,2048]{1,0:T(8,128)(2,1)S(1)} %collective-permute-done.documents_ref), channel_id=1, source_target_pairs={{0,8},{8,12},{12,4},{4,0},{1,9},{9,13},{13,5},{5,1},{2,10},{10,14}... | collective-permute-start | bytes 1572872 | tf_op jit(solution)/shard_map/ppermute | solution.py:188
  21.3 8.4 %collective-permute-start.2 = (bf16[128,256]{1,0:T(8,128)(2,1)S(1)}, bf16[128,256]{1,0:T(8,128)(2,1)S(1)}, u32[]{:S(2)}, u32[]{:S(2)}) collective-permute-start(bf16[128,256]{1,0:T(8,128)(2,1)S(1)} %get-tuple-element.47), channel_id=1, source_target_pairs={{0,1},{1,2},{2,3},{3,0},{4,5},{5,6},{6,7},{7,4},{8,9},{9,10},{10,1... | collective-permute-start | bytes 196616 | tf_op jit(solution)/shard_map/ppermute | solution.py:118
  21.4 11.2 %collective-permute-start.3 = (bf16[128,256]{1,0:T(8,128)(2,1)S(1)}, bf16[128,256]{1,0:T(8,128)(2,1)S(1)}, u32[]{:S(2)}, u32[]{:S(2)}) collective-permute-start(bf16[128,256]{1,0:T(8,128)(2,1)S(1)} %get-tuple-element.49), channel_id=1, source_target_pairs={{0,2},{1,3},{2,0},{3,1},{4,6},{5,7},{6,4},{7,5},{8,10},{9,11},{10,... | collective-permute-start | bytes 196616 | tf_op jit(solution)/shard_map/ppermute | solution.py:118
  22.9 11.1 %collective-permute-start.4 = (bf16[128,256]{1,0:T(8,128)(2,1)S(1)}, bf16[128,256]{1,0:T(8,128)(2,1)S(1)}, u32[]{:S(2)}, u32[]{:S(2)}) collective-permute-start(bf16[128,256]{1,0:T(8,128)(2,1)S(1)} %get-tuple-element.50), channel_id=1, source_target_pairs={{0,3},{1,0},{2,1},{3,2},{4,7},{5,4},{6,5},{7,6},{8,11},{9,8},{10,9... | collective-permute-start | bytes 196616 | tf_op jit(solution)/shard_map/ppermute | solution.py:118
  31.0 3.8 %collective-permute-start.7 = (bf16[128,128]{1,0:T(8,128)(2,1)S(1)}, bf16[128,128]{1,0:T(8,128)(2,1)S(1)}, u32[]{:S(2)}, u32[]{:S(2)}) collective-permute-start(bf16[128,128]{1,0:T(8,128)(2,1)S(1)} %get-tuple-element.55), channel_id=1, source_target_pairs={{0,1},{1,2},{2,3},{3,0},{4,5},{5,6},{6,7},{7,4},{8,9},{9,10},{10,1... | collective-permute-start | bytes 98312 | tf_op jit(solution)/shard_map/ppermute | solution.py:118
  31.0 4.0 %collective-permute-start.8 = (bf16[128,128]{1,0:T(8,128)(2,1)S(1)}, bf16[128,128]{1,0:T(8,128)(2,1)S(1)}, u32[]{:S(2)}, u32[]{:S(2)}) collective-permute-start(bf16[128,128]{1,0:T(8,128)(2,1)S(1)} %get-tuple-element.56), channel_id=1, source_target_pairs={{0,2},{1,3},{2,0},{3,1},{4,6},{5,7},{6,4},{7,5},{8,10},{9,11},{10,... | collective-permute-start | bytes 98312 | tf_op jit(solution)/shard_map/ppermute | solution.py:118
  32.6 3.0 %collective-permute-start.9 = (bf16[128,128]{1,0:T(8,128)(2,1)S(1)}, bf16[128,128]{1,0:T(8,128)(2,1)S(1)}, u32[]{:S(2)}, u32[]{:S(2)}) collective-permute-start(bf16[128,128]{1,0:T(8,128)(2,1)S(1)} %get-tuple-element.57), channel_id=1, source_target_pairs={{0,3},{1,0},{2,1},{3,2},{4,7},{5,4},{6,5},{7,6},{8,11},{9,8},{10,9... | collective-permute-start | bytes 98312 | tf_op jit(solution)/shard_map/ppermute | solution.py:118
  34.0 8.0 %collective-permute-start.6 = (f32[128,128]{1,0:T(8,128)S(1)}, f32[128,128]{1,0:T(8,128)S(1)}, u32[]{:S(2)}, u32[]{:S(2)}) collective-permute-start(f32[128,128]{1,0:T(8,128)S(1)} %get-tuple-element.52), channel_id=1, source_target_pairs={{0,4},{4,12},{8,0},{12,8},{1,5},{5,13},{9,1},{13,9},{2,6},{6,14},{... | collective-permute-start | bytes 196616 | tf_op jit(solution)/shard_map/ppermute | solution.py:181
  35.6 6.6 %collective-permute-start.10 = (f32[128,128]{1,0:T(8,128)S(1)}, f32[128,128]{1,0:T(8,128)S(1)}, u32[]{:S(2)}, u32[]{:S(2)}) collective-permute-start(f32[128,128]{1,0:T(8,128)S(1)} %shard_map.69), channel_id=1, source_target_pairs={{0,8},{4,0},{8,12},{12,4},{1,9},{5,1},{9,13},{13,5},{2,10},{6,2},{... | collective-permute-start | bytes 196616 | tf_op jit(solution)/shard_map/ppermute | solution.py:181
  43.4 3.4 %collective-permute-start.11 = (bf16[128,128]{1,0:T(8,128)(2,1)S(1)}, bf16[128,128]{1,0:T(8,128)(2,1)S(1)}, u32[]{:S(2)}, u32[]{:S(2)}) collective-permute-start(bf16[128,128]{1,0:T(8,128)(2,1)S(1)} %get-tuple-element.62), channel_id=1, source_target_pairs={{0,1},{1,2},{2,3},{3,0},{4,5},{5,6},{6,7},{7,4},{8,9},{9,10},{10,1... | collective-permute-start | bytes 98312 | tf_op jit(solution)/shard_map/ppermute | solution.py:118
  43.5 4.0 %collective-permute-start.12 = (bf16[128,128]{1,0:T(8,128)(2,1)S(1)}, bf16[128,128]{1,0:T(8,128)(2,1)S(1)}, u32[]{:S(2)}, u32[]{:S(2)}) collective-permute-start(bf16[128,128]{1,0:T(8,128)(2,1)S(1)} %get-tuple-element.63), channel_id=1, source_target_pairs={{0,2},{1,3},{2,0},{3,1},{4,6},{5,7},{6,4},{7,5},{8,10},{9,11},{10,... | collective-permute-start | bytes 98312 | tf_op jit(solution)/shard_map/ppermute | solution.py:118
  45.1 3.0 %collective-permute-start.13 = (bf16[128,128]{1,0:T(8,128)(2,1)S(1)}, bf16[128,128]{1,0:T(8,128)(2,1)S(1)}, u32[]{:S(2)}, u32[]{:S(2)}) collective-permute-start(bf16[128,128]{1,0:T(8,128)(2,1)S(1)} %get-tuple-element.64), channel_id=1, source_target_pairs={{0,3},{1,0},{2,1},{3,2},{4,7},{5,4},{6,5},{7,6},{8,11},{9,8},{10,9... | collective-permute-start | bytes 98312 | tf_op jit(solution)/shard_map/ppermute | solution.py:118
  48.1 6.6 %collective-permute-start.14 = (f32[128,128]{1,0:T(8,128)S(1)}, f32[128,128]{1,0:T(8,128)S(1)}, u32[]{:S(2)}, u32[]{:S(2)}) collective-permute-start(f32[128,128]{1,0:T(8,128)S(1)} %shard_map.71), channel_id=1, source_target_pairs={{0,12},{4,8},{8,4},{12,0},{1,13},{5,9},{9,5},{13,1},{2,14},{6,10},... | collective-permute-start | bytes 196616 | tf_op jit(solution)/shard_map/ppermute | solution.py:181

commit v9 on v8

v9 whole, which is shorter than its diff:
```python
import functools

import jax
import jax.numpy as jnp
from jax import lax
from jax.experimental import pallas as pl
from jax.experimental.pallas import tpu as pltpu
from jax.sharding import PartitionSpec as P

LDIM = 512
LAY_DEV = 4
STEPS = 4
DAMPING = 0.05
NT = (((1,), (1,)), ((), ()))
MIB = 1024 * 1024


def prepare_kernel(
    offsets, queries_hbm, bases_hbm, values_hbm, conditioned_ref, queries, bases, values, arrived
):
    copies = [pltpu.make_async_copy(values_hbm, values, arrived.at[0])]
    for layer in range(LAY_DEV):
        columns = queries_hbm.at[:, layer * LDIM : (layer + 1) * LDIM]
        copies.append(pltpu.make_async_copy(columns, queries.at[layer], arrived.at[1 + 2 * layer]))
        copies.append(pltpu.make_async_copy(bases_hbm.at[layer], bases.at[layer], arrived.at[2 + 2 * layer]))
    for copy in copies:
        copy.start()
    base_column = lax.axis_index("layer") * (LAY_DEV * LDIM)
    copies[0].wait()
    for layer in range(LAY_DEV):
        copies[1 + 2 * layer].wait()
        copies[2 + 2 * layer].wait()
        basis = bases[layer]
        projected = jnp.dot(queries[layer], basis, preferred_element_type=jnp.float32)
        scaled = (projected / (values[layer : layer + 1, :] + DAMPING)).astype(jnp.bfloat16)
        restored = lax.dot_general(scaled, basis, NT, preferred_element_type=jnp.float32)
        first = pl.multiple_of(offsets[layer] - base_column, LDIM)
        conditioned_ref[:, pl.ds(first, LDIM)] = restored.astype(jnp.bfloat16)


def prepare(queries, bases, values, offsets):
    rows, dims = queries.shape
    hbm = pl.BlockSpec(memory_space=pltpu.HBM)
    return pl.pallas_call(
        prepare_kernel,
        out_shape=jax.ShapeDtypeStruct((rows, dims), jnp.bfloat16),
        in_specs=[pl.BlockSpec(memory_space=pltpu.SMEM), hbm, hbm, hbm],
        out_specs=pl.BlockSpec(memory_space=pltpu.VMEM),
        scratch_shapes=[
            pltpu.VMEM((LAY_DEV, rows, LDIM), jnp.bfloat16),
            pltpu.VMEM(bases.shape, jnp.bfloat16),
            pltpu.VMEM(values.shape, jnp.float32),
            pltpu.SemaphoreType.DMA((1 + 2 * LAY_DEV,)),
        ],
        compiler_params=pltpu.CompilerParams(vmem_limit_bytes=62 * MIB),
        cost_estimate=pl.CostEstimate(
            flops=4 * rows * dims * LDIM, bytes_accessed=6 * MIB, transcendentals=0
        ),
    )(offsets, queries, bases, values)


def masked_tile(queries, documents, query_ids, block):
    tile = lax.dot_general(queries, documents, NT, preferred_element_type=jnp.float32)
    doc_ids = block * tile.shape[1] + lax.broadcasted_iota(jnp.int32, tile.shape, 1)
    return jnp.where(query_ids == doc_ids, 0.0, tile)


def scoring(kernel, out_shape, place, conditioned, query_ids, documents, extra=(), scratch=()):
    dims = conditioned.shape[1]
    docs = documents.shape[0]
    rows = sum(shape.shape[0] for shape in out_shape)
    vmem = pl.BlockSpec(memory_space=pltpu.VMEM)
    return pl.pallas_call(
        kernel,
        out_shape=out_shape,
        in_specs=[pl.BlockSpec(memory_space=pltpu.SMEM)] + [vmem] * (3 + len(extra)),
        out_specs=[vmem] * len(out_shape),
        scratch_shapes=scratch,
        compiler_params=pltpu.CompilerParams(vmem_limit_bytes=12 * MIB),
        cost_estimate=pl.CostEstimate(
            flops=2 * rows * docs * dims, bytes_accessed=2 * dims * (rows + docs), transcendentals=0
        ),
    )(place, conditioned, query_ids, documents, *extra)


def turned_kernel(shares, block_of, place, queries_ref, ids_ref, documents_ref, *refs):
    *out_refs, held = refs
    held[...] = masked_tile(queries_ref[...], documents_ref[...], ids_ref[...], block_of(place[1]))
    for turn, out_ref in enumerate(out_refs):
        share_rows = out_ref.shape[0]
        first = pl.multiple_of(lax.rem(place[0] + turn, shares) * share_rows, share_rows)
        out_ref[...] = held[pl.ds(first, share_rows), :].astype(jnp.bfloat16)


def half_shares(layer, share_rows, kept):
    core = lax.rem(layer, 2)
    core = core if kept else 1 - core
    return [pl.multiple_of((2 * chip + core) * share_rows, share_rows) for chip in range(2)]


def halves_kernel(block_of, place, queries_ref, ids_ref, documents_ref, *refs):
    front_refs, out_refs, held = refs[:-3], refs[-3:-1], refs[-1]
    held[...] = masked_tile(queries_ref[...], documents_ref[...], ids_ref[...], block_of(place[1]))
    docs = documents_ref.shape[0]
    rows, width = out_refs[0].shape
    for side, kept in enumerate((True, False)):
        if front_refs:
            out_refs[side][:, : width - docs] = front_refs[side][...]
        for chip, first in enumerate(half_shares(place[0], rows // 2, kept)):
            spot = slice(chip * (rows // 2), (chip + 1) * (rows // 2))
            out_refs[side][spot, width - docs :] = held[pl.ds(first, rows // 2), :]


def half_kernel(block_of, kept, place, queries_ref, ids_ref, documents_ref, out_ref):
    share_rows = out_ref.shape[0] // 2
    firsts = half_shares(place[0], share_rows, kept)
    queries = jnp.concatenate([queries_ref[pl.ds(first, share_rows), :] for first in firsts], axis=0)
    query_ids = jnp.concatenate([ids_ref[pl.ds(first, share_rows), :] for first in firsts], axis=0)
    out_ref[...] = masked_tile(queries, documents_ref[...], query_ids, block_of(place[1]))


def total_of(refs):
    total = refs[0][...].astype(jnp.float32)
    for ref in refs[1:]:
        total += ref[...].astype(jnp.float32)
    return total


def sum_kernel(*refs):
    refs[-1][...] = total_of(refs[:-1])


def small_call(kernel, out_shape, *args, place=None):
    vmem = pl.BlockSpec(memory_space=pltpu.VMEM)
    scalars = [] if place is None else [place]
    return pl.pallas_call(
        kernel,
        out_shape=out_shape,
        in_specs=[pl.BlockSpec(memory_space=pltpu.SMEM)] * len(scalars) + [vmem] * len(args),
        out_specs=[vmem] * len(out_shape),
        compiler_params=pltpu.CompilerParams(vmem_limit_bytes=4 * MIB),
    )(*scalars, *args)


def direct_sum(tiles):
    shares = len(tiles)
    arrived = [tiles[0]]
    for turn in range(1, shares):
        pairs = [(lay, (lay + turn) % shares) for lay in range(shares)]
        arrived.append(lax.ppermute(tiles[turn], "layer", pairs))
    (total,) = small_call(sum_kernel, [jax.ShapeDtypeStruct(tiles[0].shape, jnp.float32)], *arrived)
    return total


def core_sum_kernel(place, kept_ref, arrived_ref, mine_ref, other_ref):
    rows = mine_ref.shape[0]
    chip = place[0] // 2
    mine = pl.ds(pl.multiple_of(chip * rows, rows), rows)
    other = pl.ds(pl.multiple_of((1 - chip) * rows, rows), rows)
    mine_ref[...] = kept_ref[mine, :] + arrived_ref[mine, :]
    other_ref[...] = (kept_ref[other, :] + arrived_ref[other, :]).astype(other_ref.dtype)


def chip_sum_kernel(mine_ref, arrived_ref, *out_refs):
    docs = out_refs[0].shape[1]
    for spot, out_ref in enumerate(out_refs):
        columns = slice(spot * docs, (spot + 1) * docs)
        total = mine_ref[:, columns] + arrived_ref[:, columns].astype(jnp.float32)
        out_ref[...] = total.astype(out_ref.dtype)


def swap(value, distance):
    count = lax.axis_size("layer")
    return lax.ppermute(value, "layer", [(lay, lay ^ distance) for lay in range(count)])


def layer_sum(kept, sent, place, out_types):
    rows, width = kept.shape[0] // 2, kept.shape[1]
    mine, other = small_call(
        core_sum_kernel,
        [jax.ShapeDtypeStruct((rows, width), jnp.float32), jax.ShapeDtypeStruct((rows, width), jnp.bfloat16)],
        kept, swap(sent, 1), place=place,
    )
    docs = width // len(out_types)
    out_shape = [jax.ShapeDtypeStruct((rows, docs), out_type) for out_type in out_types]
    return small_call(chip_sum_kernel, out_shape, mine, swap(other, 2))


ROUND_ONE = ((0, 2), (2, 3), (3, 1), (1, 0))
ROUND_TWO = ((0, 1), (1, 3), (3, 2), (2, 0))
BLOCK_ONE = (1, 3, 0, 2)
BLOCK_TWO = (2, 0, 3, 1)
BLOCK_LAST = (3, 2, 1, 0)


def pick(table):
    def entry(row):
        value = jnp.int32(table[0])
        for index in range(1, len(table)):
            value = jnp.where(row == index, jnp.int32(table[index]), value)
        return value

    return entry


def step_of(table):
    return pick([(block - table.index(block)) % STEPS for block in range(STEPS)])


def assemble_kernel(place, own_ref, first_ref, second_ref, out_ref):
    out_ref[0] = own_ref[...]
    for ref, table in ((first_ref, BLOCK_ONE), (second_ref, BLOCK_TWO)):
        out_ref[step_of(table)(place[1])] = ref[...].astype(jnp.float32)


def finish_kernel(place, last_ref, scores_hbm, out_hbm, wide, copied):
    del scores_hbm
    wide[...] = last_ref[...].astype(jnp.float32)
    copy = pltpu.make_async_copy(wide, out_hbm.at[step_of(BLOCK_LAST)(place[1])], copied)
    copy.start()
    copy.wait()


def finish(place, last, scores):
    hbm = pl.BlockSpec(memory_space=pltpu.HBM)
    return pl.pallas_call(
        finish_kernel,
        out_shape=jax.ShapeDtypeStruct(scores.shape, scores.dtype),
        in_specs=[pl.BlockSpec(memory_space=pltpu.SMEM), pl.BlockSpec(memory_space=pltpu.VMEM), hbm],
        out_specs=hbm,
        scratch_shapes=[pltpu.VMEM(last.shape, jnp.float32), pltpu.SemaphoreType.DMA],
        input_output_aliases={2: 0},
        compiler_params=pltpu.CompilerParams(vmem_limit_bytes=4 * MIB),
    )(place, last, scores)


def along_line(documents, conditioned, query_ids, place):
    docs = documents.shape[0]
    half = (conditioned.shape[0] // 2, docs)

    def halves(block, block_of, front=()):
        width = docs * (1 + bool(front))
        out_shape = [jax.ShapeDtypeStruct((half[0], width), jnp.float32)] * 2
        scratch = [pltpu.VMEM((2 * half[0], docs), jnp.float32)]
        kernel = functools.partial(halves_kernel, block_of)
        return scoring(kernel, out_shape, place, conditioned, query_ids, block, front, scratch)

    def one_half(block, block_of, kept):
        kernel = functools.partial(half_kernel, block_of, kept)
        out_shape = [jax.ShapeDtypeStruct(half, jnp.float32)]
        return scoring(kernel, out_shape, place, conditioned, query_ids, block)[0]

    def back(total, table):
        return lax.ppermute(total, "rows", tuple(enumerate(table)))

    one = lax.ppermute(documents, "rows", ROUND_ONE)
    later, conditioned = lax.optimization_barrier((documents, conditioned))
    two = lax.ppermute(later, "rows", ROUND_TWO)
    own = halves(later, lambda row: row)
    one, own = lax.optimization_barrier((one, own))
    three = lax.ppermute(one, "rows", ROUND_ONE)

    own, first = layer_sum(*halves(one, pick(BLOCK_ONE), own), place, (jnp.float32, jnp.bfloat16))
    two, first = lax.optimization_barrier((two, first))
    first = back(first, BLOCK_ONE)
    (second,) = layer_sum(*halves(two, pick(BLOCK_TWO)), place, (jnp.bfloat16,))
    second = back(second, BLOCK_TWO)
    three, first, second = lax.optimization_barrier((three, first, second))

    sent = one_half(three, pick(BLOCK_LAST), False)
    kept = one_half(three, pick(BLOCK_LAST), True)
    (last,) = layer_sum(kept, sent, place, (jnp.bfloat16,))
    last = back(last, BLOCK_LAST)
    out_shape = [jax.ShapeDtypeStruct((STEPS,) + own.shape, jnp.float32)]
    (scores,) = small_call(assemble_kernel, out_shape, own, first, second, place=place)
    return finish(place, last, scores)


def around_ring(documents, conditioned, query_ids, place):
    n_rows, shares = lax.axis_size("rows"), lax.axis_size("layer")
    rows, docs = conditioned.shape[0], documents.shape[0]
    result = []
    for step in range(STEPS):
        behind = [(row, (row - step) % n_rows) for row in range(n_rows)]
        block = lax.ppermute(documents, "rows", behind) if step else documents

        def ahead(row, step=step):
            return lax.rem(row + step, n_rows)

        kernel = functools.partial(turned_kernel, shares, ahead)
        out_shape = [jax.ShapeDtypeStruct((rows // shares, docs), jnp.bfloat16)] * shares
        scratch = [pltpu.VMEM((rows, docs), jnp.float32)]
        total = direct_sum(scoring(kernel, out_shape, place, conditioned, query_ids, block, (), scratch))
        onward = [(row, (row + step) % n_rows) for row in range(n_rows)]
        result.append(lax.ppermute(total, "rows", onward) if step else total)
    return jnp.stack(result)


def local(train_grads, query_grads, eigenbases, eigenvalues, layer_offsets, query_doc_ids):
    place = jnp.stack([lax.axis_index("layer"), lax.axis_index("rows")]).astype(jnp.int32)
    conditioned = prepare(query_grads, eigenbases, eigenvalues, layer_offsets)
    on_line = lax.axis_size("rows") == 4 and lax.axis_size("layer") == 4
    plan = along_line if on_line else around_ring
    return plan(train_grads, conditioned, query_doc_ids[:, None], place)


def solution(mesh):
    in_specs = (
        P(("group", "rows"), "layer"),
        P(("group", "rows"), "layer"),
        P("layer", None, None),
        P("layer", None),
        P("layer"),
        P(("group", "rows")),
    )
    out_specs = P(None, "layer", ("group", "rows"))
    return jax.shard_map(local, mesh=mesh, in_specs=in_specs, out_specs=out_specs, check_vma=False)
```

time: 56.1 us -> 55.3 us (0.986)
  starting transfers between devices: 21.3 us -> 16.2 us
  Pallas kernels: 12.6 us -> 16.2 us
  waiting for transfers between devices: 20.1 us -> 20.7 us
    ppermute x9 -> x6, waiting for transfers between devices: 2.44 us -> 8.64 us  [swap(): lax.ppermute(value, 'layer', [(lay, lay ^ distance) for lay in range(coun...]
    ppermute x9 -> x6, starting transfers between devices: 9 us -> 4.88 us  [swap(): lax.ppermute(value, 'layer', [(lay, lay ^ distance) for lay in range(coun...]
    pallas_call x8 -> x13, Pallas kernels: 6.45 us -> 10 us  [the longest x5 5.85 us: scoring(): pl.pallas_call(kernel, out_shape=out_shape, in_specs=[pl.BlockSpec(memory...]
    ppermute x3, waiting for transfers between devices: 8.92 us -> 5.51 us  [back(): return lax.ppermute(total, 'rows', tuple(enumerate(table)))]
    ppermute x1, waiting for transfers between devices: 5.37 us -> 3.29 us  [along_line(): two = lax.ppermute(later, 'rows', ROUND_TWO)]
    ppermute x3, starting transfers between devices: 4.95 us -> 3.86 us  [back(): return lax.ppermute(total, 'rows', tuple(enumerate(table)))]
  transfers between devices with their start and end apart: 15 -> 12, of which waited for: 10 -> 10; matrix products, arithmetic and copies ran while one was open for 0% -> 0% of each run, Pallas kernels for 18% -> 24%
where the time goes in v9:
time: 55.3 us; the launch traced here: 55.1 us
  waiting for transfers between devices  20.7 us (37%)
  starting transfers between devices  16.2 us (29%)
  Pallas kernels  16.2 us (29%)
  local copies, waits for them, and re-layouts  1.75 us (3%)
    ppermute x6, waiting for transfers between devices, swap(): lax.ppermute(value, 'layer', [(lay, lay ^ distance) for lay in range(coun...  8.64 us
    pallas_call x1, Pallas kernels, prepare(): pl.pallas_call(prepare_kernel, out_shape=jax.ShapeDtypeStruct((rows, dims...  6.15 us
    pallas_call x5, Pallas kernels, scoring(): pl.pallas_call(kernel, out_shape=out_shape, in_specs=[pl.BlockSpec(memory...  5.85 us
    ppermute x3, waiting for transfers between devices, back(): return lax.ppermute(total, 'rows', tuple(enumerate(table)))  5.51 us
    ppermute x6, starting transfers between devices, swap(): lax.ppermute(value, 'layer', [(lay, lay ^ distance) for lay in range(coun...  4.88 us
    ppermute x1, starting transfers between devices, along_line(): one = lax.ppermute(documents, 'rows', ROUND_ONE)  4.04 us
    ppermute x3, starting transfers between devices, back(): return lax.ppermute(total, 'rows', tuple(enumerate(table)))  3.86 us
    ppermute x1, starting transfers between devices, along_line(): three = lax.ppermute(one, 'rows', ROUND_ONE)  3.33 us
  transfers between devices with their start and end apart: 12, of which 10 were waited for; matrix products, arithmetic and copies ran while one was open for 0% of the time, Pallas kernels for 24%

profile of v9, /device:TPU:0, one launch (start us, length us, event | category | flops | bytes accessed | tf_op | source)
XLA Modules:
  0.0 55.1 jit_solution(10856361993948566455)
XLA Ops:
  0.0 0.0 copy-start.1
  0.0 0.0 copy-start.2
  0.0 4.0 %collective-permute-start = (bf16[128,2048]{1,0:T(8,128)(2,1)}, bf16[128,2048]{1,0:T(8,128)(2,1)S(1)}, u32[]{:S(2)}, u32[]{:S(2)}) collective-permute-start(bf16[128,2048]{1,0:T(8,128)(2,1)} %documents_ref), channel_id=1, source_target_pairs={{0,8},{8,12},{12,4},{4,0},{1,9},{9,13},{13,5},{5,1},{2,10},{10,14}... | collective-permute-start | bytes 1572872 | tf_op jit(solution)/shard_map/ppermute | solution.py:256
  4.0 6.1 %shard_map.64.queries_ref = bf16[512,2048]{1,0:T(8,128)(2,1)} custom-call(s32[4]{0:T(128)} %offsets.1, bf16[512,2048]{1,0:T(8,128)(2,1)} %queries_hbm.1, bf16[4,512,512]{2,1,0:T(8,128)(2,1)} %bases_hbm.1, f32[4,512]{1,0:T(4,128)} %values_hbm.1), custom_call_target="tpu_custom_call" | custom-call | flops 2147483648 | bytes 6291456 | tf_op jit(solution)/shard_map/pallas_call | solution.py:44
  10.2 0.0 copy-done.1
  10.2 0.1 collective-permute-start.2
  10.3 0.0 copy-done.2
  10.3 0.1 copy.11.ids_ref
  10.4 0.1 pad_add_fusion.place
  10.5 0.0 copy-start
  10.5 1.6 %copy-done = bf16[512,2048]{1,0:T(8,128)(2,1)S(1)} copy-done((bf16[512,2048]{1,0:T(8,128)(2,1)S(1)}, bf16[512,2048]{1,0:T(8,128)(2,1)}, u32[]{:S(2)}) %copy-start) | copy-done | bytes 2097176
  12.1 1.3 %shard_map.65 = (f32[256,128]{1,0:T(8,128)S(1)}, f32[256,128]{1,0:T(8,128)S(1)}) custom-call(s32[2]{0:T(128)S(1)} %pad_add_fusion.place, bf16[512,2048]{1,0:T(8,128)(2,1)S(1)} %copy-done, s32[512,1]{1,0:T(8,128)S(1)} %copy.11.ids_ref, bf16[128,2048]{1,0:T(8,128)(2,1)S(1)} %copy-done.1), custom_call_target="tpu_custom_call" | custom-call | flops 268435456 | bytes 2621440 | tf_op jit(solution)/shard_map/pallas_call | solution.py:73
  13.4 3.3 %collective-permute-done.documents_ref = bf16[128,2048]{1,0:T(8,128)(2,1)S(1)} collective-permute-done((bf16[128,2048]{1,0:T(8,128)(2,1)}, bf16[128,2048]{1,0:T(8,128)(2,1)S(1)}, u32[]{:S(2)}, u32[]{:S(2)}) %collective-permute-start) | collective-permute-done | bytes 524320 | tf_op jit(solution)/shard_map/ppermute | solution.py:256
  16.7 1.3 %shard_map.66 = (f32[256,256]{1,0:T(8,128)S(1)}, f32[256,256]{1,0:T(8,128)S(1)}) custom-call(s32[2]{0:T(128)S(1)} %pad_add_fusion.place, bf16[512,2048]{1,0:T(8,128)(2,1)S(1)} %copy-done, s32[512,1]{1,0:T(8,128)S(1)} %copy.11.ids_ref, bf16[128,2048]{1,0:T(8,128)(2,1)S(1)} %collective-permute-done.documents_ref, f32[256,128]{1,0:T(8,128)S(1)} %get-tuple-element.34.refs_0_, ...), custom_call_target="tpu_custom_call" | custom-call | flops 268435456 | bytes 2621440 | tf_op jit(solution)/shard_map/pallas_call | solution.py:73
  18.0 0.1 collective-permute-start.3
  18.1 3.3 %collective-permute-start.1 = (bf16[128,2048]{1,0:T(8,128)(2,1)S(1)}, bf16[128,2048]{1,0:T(8,128)(2,1)S(1)}, u32[]{:S(2)}, u32[]{:S(2)}) collective-permute-start(bf16[128,2048]{1,0:T(8,128)(2,1)S(1)} %collective-permute-done.documents_ref), channel_id=1, source_target_pairs={{0,8},{8,12},{12,4},{4,0},{1,9},{9,13},{13,5},{5,1},{2,10},{10,14}... | collective-permute-start | bytes 1572872 | tf_op jit(solution)/shard_map/ppermute | solution.py:261
  21.4 0.0 collective-permute-done.3.arrived_ref
  21.4 0.6 %shard_map.67 = (f32[128,256]{1,0:T(8,128)S(1)}, bf16[128,256]{1,0:T(8,128)(2,1)S(1)}) custom-call(s32[2]{0:T(128)S(1)} %pad_add_fusion.place, f32[256,256]{1,0:T(8,128)S(1)} %get-tuple-element.36.kept_ref, f32[256,256]{1,0:T(8,128)S(1)} %collective-permute-done.3.arrived_ref), custom_call_target="tpu_custom_call" | custom-call | tf_op jit(solution)/shard_map/pallas_call | solution.py:136
  22.0 1.6 %collective-permute-start.4 = (bf16[128,256]{1,0:T(8,128)(2,1)S(1)}, bf16[128,256]{1,0:T(8,128)(2,1)S(1)}, u32[]{:S(2)}, u32[]{:S(2)}) collective-permute-start(bf16[128,256]{1,0:T(8,128)(2,1)S(1)} %get-tuple-element.39), channel_id=1, source_target_pairs={{0,2},{1,3},{2,0},{3,1},{4,6},{5,7},{6,4},{7,5},{8,10},{9,11},{10,... | collective-permute-start | bytes 196616 | tf_op jit(solution)/shard_map/ppermute | solution.py:174
  23.6 2.8 %collective-permute-done.4.arrived_ref = bf16[128,256]{1,0:T(8,128)(2,1)S(1)} collective-permute-done((bf16[128,256]{1,0:T(8,128)(2,1)S(1)}, bf16[128,256]{1,0:T(8,128)(2,1)S(1)}, u32[]{:S(2)}, u32[]{:S(2)}) %collective-permute-start.4) | collective-permute-done | bytes 65568 | tf_op jit(solution)/shard_map/ppermute | solution.py:174
  26.4 3.3 %collective-permute-done.2.documents_ref = bf16[128,2048]{1,0:T(8,128)(2,1)S(1)} collective-permute-done((bf16[128,2048]{1,0:T(8,128)(2,1)S(1)}, bf16[128,2048]{1,0:T(8,128)(2,1)S(1)}, u32[]{:S(2)}, u32[]{:S(2)}) %collective-permute-start.2) | collective-permute-done | bytes 524320 | tf_op jit(solution)/shard_map/ppermute | solution.py:258
  29.7 1.3 %shard_map.69 = (f32[256,128]{1,0:T(8,128)S(1)}, f32[256,128]{1,0:T(8,128)S(1)}) custom-call(s32[2]{0:T(128)S(1)} %pad_add_fusion.place, bf16[512,2048]{1,0:T(8,128)(2,1)S(1)} %copy-done, s32[512,1]{1,0:T(8,128)S(1)} %copy.11.ids_ref, bf16[128,2048]{1,0:T(8,128)(2,1)S(1)} %collective-permute-done.2.documents_ref), custom_call_target="tpu_custom_call" | custom-call | flops 268435456 | bytes 2621440 | tf_op jit(solution)/shard_map/pallas_call | solution.py:73
  31.0 0.1 collective-permute-start.6
  31.1 1.3 %collective-permute-done.6.arrived_ref = f32[256,128]{1,0:T(8,128)S(1)} collective-permute-done((f32[256,128]{1,0:T(8,128)S(1)}, f32[256,128]{1,0:T(8,128)S(1)}, u32[]{:S(2)}, u32[]{:S(2)}) %collective-permute-start.6) | collective-permute-done | bytes 131104 | tf_op jit(solution)/shard_map/ppermute | solution.py:174
  32.4 0.6 %shard_map.70 = (f32[128,128]{1,0:T(8,128)S(1)}, bf16[128,128]{1,0:T(8,128)(2,1)S(1)}) custom-call(s32[2]{0:T(128)S(1)} %pad_add_fusion.place, f32[256,128]{1,0:T(8,128)S(1)} %get-tuple-element.43.kept_ref, f32[256,128]{1,0:T(8,128)S(1)} %collective-permute-done.6.arrived_ref), custom_call_target="tpu_custom_call" | custom-call | tf_op jit(solution)/shard_map/pallas_call | solution.py:136
  33.0 1.6 %collective-permute-start.7 = (bf16[128,128]{1,0:T(8,128)(2,1)S(1)}, bf16[128,128]{1,0:T(8,128)(2,1)S(1)}, u32[]{:S(2)}, u32[]{:S(2)}) collective-permute-start(bf16[128,128]{1,0:T(8,128)(2,1)S(1)} %get-tuple-element.46), channel_id=1, source_target_pairs={{0,2},{1,3},{2,0},{3,1},{4,6},{5,7},{6,4},{7,5},{8,10},{9,11},{10,... | collective-permute-start | bytes 98312 | tf_op jit(solution)/shard_map/ppermute | solution.py:174
  34.5 0.7 %collective-permute-start.5 = (bf16[128,128]{1,0:T(8,128)(2,1)S(1)}, bf16[128,128]{1,0:T(8,128)(2,1)S(1)}, u32[]{:S(2)}, u32[]{:S(2)}) collective-permute-start(bf16[128,128]{1,0:T(8,128)(2,1)S(1)} %get-tuple-element.41), channel_id=1, source_target_pairs={{0,4},{4,12},{8,0},{12,8},{1,5},{5,13},{9,1},{13,9},{2,6},{6,14},{... | collective-permute-start | bytes 98312 | tf_op jit(solution)/shard_map/ppermute | solution.py:254
  35.2 1.7 %collective-permute-done.7.arrived_ref = bf16[128,128]{1,0:T(8,128)(2,1)S(1)} collective-permute-done((bf16[128,128]{1,0:T(8,128)(2,1)S(1)}, bf16[128,128]{1,0:T(8,128)(2,1)S(1)}, u32[]{:S(2)}, u32[]{:S(2)}) %collective-permute-start.7) | collective-permute-done | bytes 32800 | tf_op jit(solution)/shard_map/ppermute | solution.py:174
  37.0 0.6 %collective-permute-start.8 = (bf16[128,128]{1,0:T(8,128)(2,1)S(1)}, bf16[128,128]{1,0:T(8,128)(2,1)S(1)}, u32[]{:S(2)}, u32[]{:S(2)}) collective-permute-start(bf16[128,128]{1,0:T(8,128)(2,1)S(1)} %shard_map.71), channel_id=1, source_target_pairs={{0,8},{4,0},{8,12},{12,4},{1,9},{5,1},{9,13},{13,5},{2,10},{6,2},{... | collective-permute-start | bytes 98312 | tf_op jit(solution)/shard_map/ppermute | solution.py:254
  37.6 3.2 %collective-permute-done.5.first_ref = bf16[128,128]{1,0:T(8,128)(2,1)S(1)} collective-permute-done((bf16[128,128]{1,0:T(8,128)(2,1)S(1)}, bf16[128,128]{1,0:T(8,128)(2,1)S(1)}, u32[]{:S(2)}, u32[]{:S(2)}) %collective-permute-start.5) | collective-permute-done | bytes 32800 | tf_op jit(solution)/shard_map/ppermute | solution.py:254
  40.7 0.0 collective-permute-done.1.documents_ref
  40.7 0.4 collective-permute-done.8.second_ref
  41.1 1.0 %shard_map.73 = f32[256,128]{1,0:T(8,128)S(1)} custom-call(s32[2]{0:T(128)S(1)} %pad_add_fusion.place, bf16[512,2048]{1,0:T(8,128)(2,1)S(1)} %copy-done, s32[512,1]{1,0:T(8,128)S(1)} %copy.11.ids_ref, bf16[128,2048]{1,0:T(8,128)(2,1)S(1)} %collective-permute-done.1.documents_ref), custom_call_target="tpu_custom_call" | custom-call | flops 134217728 | bytes 1572864 | tf_op jit(solution)/shard_map/pallas_call | solution.py:73
  42.1 0.1 collective-permute-start.9
  42.2 1.0 %shard_map.72.kept_ref = f32[256,128]{1,0:T(8,128)S(1)} custom-call(s32[2]{0:T(128)S(1)} %pad_add_fusion.place, bf16[512,2048]{1,0:T(8,128)(2,1)S(1)} %copy-done, s32[512,1]{1,0:T(8,128)S(1)} %copy.11.ids_ref, bf16[128,2048]{1,0:T(8,128)(2,1)S(1)} %collective-permute-done.1.documents_ref), custom_call_target="tpu_custom_call" | custom-call | flops 134217728 | bytes 1572864 | tf_op jit(solution)/shard_map/pallas_call | solution.py:73
  43.2 0.4 collective-permute-done.9.arrived_ref
  43.5 0.6 %shard_map.74 = (f32[128,128]{1,0:T(8,128)S(1)}, bf16[128,128]{1,0:T(8,128)(2,1)S(1)}) custom-call(s32[2]{0:T(128)S(1)} %pad_add_fusion.place, f32[256,128]{1,0:T(8,128)S(1)} %shard_map.72.kept_ref, f32[256,128]{1,0:T(8,128)S(1)} %collective-permute-done.9.arrived_ref), custom_call_target="tpu_custom_call" | custom-call | tf_op jit(solution)/shard_map/pallas_call | solution.py:136
  44.1 1.6 %collective-permute-start.10 = (bf16[128,128]{1,0:T(8,128)(2,1)S(1)}, bf16[128,128]{1,0:T(8,128)(2,1)S(1)}, u32[]{:S(2)}, u32[]{:S(2)}) collective-permute-start(bf16[128,128]{1,0:T(8,128)(2,1)S(1)} %get-tuple-element.49), channel_id=1, source_target_pairs={{0,2},{1,3},{2,0},{3,1},{4,6},{5,7},{6,4},{7,5},{8,10},{9,11},{10,... | collective-permute-start | bytes 98312 | tf_op jit(solution)/shard_map/ppermute | solution.py:174
  45.7 2.4 %collective-permute-done.10.arrived_ref = bf16[128,128]{1,0:T(8,128)(2,1)S(1)} collective-permute-done((bf16[128,128]{1,0:T(8,128)(2,1)S(1)}, bf16[128,128]{1,0:T(8,128)(2,1)S(1)}, u32[]{:S(2)}, u32[]{:S(2)}) %collective-permute-start.10) | collective-permute-done | bytes 32800 | tf_op jit(solution)/shard_map/ppermute | solution.py:174
  48.1 2.6 %collective-permute-start.11 = (bf16[128,128]{1,0:T(8,128)(2,1)S(1)}, bf16[128,128]{1,0:T(8,128)(2,1)S(1)}, u32[]{:S(2)}, u32[]{:S(2)}) collective-permute-start(bf16[128,128]{1,0:T(8,128)(2,1)S(1)} %shard_map.75), channel_id=1, source_target_pairs={{0,12},{4,8},{8,4},{12,0},{1,13},{5,9},{9,5},{13,1},{2,14},{6,10},... | collective-permute-start | bytes 98312 | tf_op jit(solution)/shard_map/ppermute | solution.py:254
  50.7 1.3 %shard_map.76.scores_hbm = f32[4,128,128]{2,1,0:T(8,128)} custom-call(s32[2]{0:T(128)S(1)} %pad_add_fusion.place, f32[128,128]{1,0:T(8,128)S(1)} %get-tuple-element.50.own_ref, bf16[128,128]{1,0:T(8,128)(2,1)S(1)} %collective-permute-done.5.first_ref, bf16[128,128]{1,0:T(8,128)(2,1)S(1)} %collective-permute-done.8.second_ref), custom_call_target="tpu_custom_call" | custom-call | tf_op jit(solution)/shard_map/pallas_call | solution.py:136
  51.9 1.9 %collective-permute-done.11.last_ref = bf16[128,128]{1,0:T(8,128)(2,1)S(1)} collective-permute-done((bf16[128,128]{1,0:T(8,128)(2,1)S(1)}, bf16[128,128]{1,0:T(8,128)(2,1)S(1)}, u32[]{:S(2)}, u32[]{:S(2)}) %collective-permute-start.11) | collective-permute-done | bytes 32800 | tf_op jit(solution)/shard_map/ppermute | solution.py:254
  53.9 1.2 %shard_map.77 = f32[4,128,128]{2,1,0:T(8,128)} custom-call(s32[2]{0:T(128)S(1)} %pad_add_fusion.place, bf16[128,128]{1,0:T(8,128)(2,1)S(1)} %collective-permute-done.11.last_ref, f32[4,128,128]{2,1,0:T(8,128)} %shard_map.76.scores_hbm), custom_call_target="tpu_custom_call", output_to_operand_aliasing={{}: (2, {})} | custom-call | tf_op jit(solution)/shard_map/pallas_call | solution.py:226
  (3 shorter events, 0.0 us)
Async XLA Ops:
  0.0 10.2 %copy-start.1 = (bf16[128,2048]{1,0:T(8,128)(2,1)S(1)}, bf16[128,2048]{1,0:T(8,128)(2,1)}, u32[]{:S(2)}) copy-start(bf16[128,2048]{1,0:T(8,128)(2,1)} %documents_ref) | copy-start | bytes 1572868
  0.0 10.3 %copy-start.2 = (s32[512]{0:T(512)S(1)}, s32[512]{0:T(512)}, u32[]{:S(2)}) copy-start(s32[512]{0:T(512)} %param.11) | copy-start | bytes 6148
  0.0 16.7 %collective-permute-start = (bf16[128,2048]{1,0:T(8,128)(2,1)}, bf16[128,2048]{1,0:T(8,128)(2,1)S(1)}, u32[]{:S(2)}, u32[]{:S(2)}) collective-permute-start(bf16[128,2048]{1,0:T(8,128)(2,1)} %documents_ref), channel_id=1, source_target_pairs={{0,8},{8,12},{12,4},{4,0},{1,9},{9,13},{13,5},{5,1},{2,10},{10,14}... | collective-permute-start | bytes 1572872 | tf_op jit(solution)/shard_map/ppermute | solution.py:256
  10.2 19.5 %collective-permute-start.2 = (bf16[128,2048]{1,0:T(8,128)(2,1)S(1)}, bf16[128,2048]{1,0:T(8,128)(2,1)S(1)}, u32[]{:S(2)}, u32[]{:S(2)}) collective-permute-start(bf16[128,2048]{1,0:T(8,128)(2,1)S(1)} %copy-done.1), channel_id=1, source_target_pairs={{0,4},{4,12},{12,8},{8,0},{1,5},{5,13},{13,9},{9,1},{2,6},{6,14},{... | collective-permute-start | bytes 1572872 | tf_op jit(solution)/shard_map/ppermute | solution.py:258
  10.5 1.6 %copy-start = (bf16[512,2048]{1,0:T(8,128)(2,1)S(1)}, bf16[512,2048]{1,0:T(8,128)(2,1)}, u32[]{:S(2)}) copy-start(bf16[512,2048]{1,0:T(8,128)(2,1)} %shard_map.64.queries_ref) | copy-start | bytes 6291460
  18.0 3.4 %collective-permute-start.3 = (f32[256,256]{1,0:T(8,128)S(1)}, f32[256,256]{1,0:T(8,128)S(1)}, u32[]{:S(2)}, u32[]{:S(2)}) collective-permute-start(f32[256,256]{1,0:T(8,128)S(1)} %get-tuple-element.37), channel_id=1, source_target_pairs={{0,1},{1,0},{2,3},{3,2},{4,5},{5,4},{6,7},{7,6},{8,9},{9,8},{10,11... | collective-permute-start | bytes 786440 | tf_op jit(solution)/shard_map/ppermute | solution.py:174
  18.1 22.6 %collective-permute-start.1 = (bf16[128,2048]{1,0:T(8,128)(2,1)S(1)}, bf16[128,2048]{1,0:T(8,128)(2,1)S(1)}, u32[]{:S(2)}, u32[]{:S(2)}) collective-permute-start(bf16[128,2048]{1,0:T(8,128)(2,1)S(1)} %collective-permute-done.documents_ref), channel_id=1, source_target_pairs={{0,8},{8,12},{12,4},{4,0},{1,9},{9,13},{13,5},{5,1},{2,10},{10,14}... | collective-permute-start | bytes 1572872 | tf_op jit(solution)/shard_map/ppermute | solution.py:261
  22.0 4.3 %collective-permute-start.4 = (bf16[128,256]{1,0:T(8,128)(2,1)S(1)}, bf16[128,256]{1,0:T(8,128)(2,1)S(1)}, u32[]{:S(2)}, u32[]{:S(2)}) collective-permute-start(bf16[128,256]{1,0:T(8,128)(2,1)S(1)} %get-tuple-element.39), channel_id=1, source_target_pairs={{0,2},{1,3},{2,0},{3,1},{4,6},{5,7},{6,4},{7,5},{8,10},{9,11},{10,... | collective-permute-start | bytes 196616 | tf_op jit(solution)/shard_map/ppermute | solution.py:174
  31.0 1.4 %collective-permute-start.6 = (f32[256,128]{1,0:T(8,128)S(1)}, f32[256,128]{1,0:T(8,128)S(1)}, u32[]{:S(2)}, u32[]{:S(2)}) collective-permute-start(f32[256,128]{1,0:T(8,128)S(1)} %get-tuple-element.44), channel_id=1, source_target_pairs={{0,1},{1,0},{2,3},{3,2},{4,5},{5,4},{6,7},{7,6},{8,9},{9,8},{10,11... | collective-permute-start | bytes 393224 | tf_op jit(solution)/shard_map/ppermute | solution.py:174
  33.0 4.0 %collective-permute-start.7 = (bf16[128,128]{1,0:T(8,128)(2,1)S(1)}, bf16[128,128]{1,0:T(8,128)(2,1)S(1)}, u32[]{:S(2)}, u32[]{:S(2)}) collective-permute-start(bf16[128,128]{1,0:T(8,128)(2,1)S(1)} %get-tuple-element.46), channel_id=1, source_target_pairs={{0,2},{1,3},{2,0},{3,1},{4,6},{5,7},{6,4},{7,5},{8,10},{9,11},{10,... | collective-permute-start | bytes 98312 | tf_op jit(solution)/shard_map/ppermute | solution.py:174
  34.5 6.2 %collective-permute-start.5 = (bf16[128,128]{1,0:T(8,128)(2,1)S(1)}, bf16[128,128]{1,0:T(8,128)(2,1)S(1)}, u32[]{:S(2)}, u32[]{:S(2)}) collective-permute-start(bf16[128,128]{1,0:T(8,128)(2,1)S(1)} %get-tuple-element.41), channel_id=1, source_target_pairs={{0,4},{4,12},{8,0},{12,8},{1,5},{5,13},{9,1},{13,9},{2,6},{6,14},{... | collective-permute-start | bytes 98312 | tf_op jit(solution)/shard_map/ppermute | solution.py:254
  37.0 4.2 %collective-permute-start.8 = (bf16[128,128]{1,0:T(8,128)(2,1)S(1)}, bf16[128,128]{1,0:T(8,128)(2,1)S(1)}, u32[]{:S(2)}, u32[]{:S(2)}) collective-permute-start(bf16[128,128]{1,0:T(8,128)(2,1)S(1)} %shard_map.71), channel_id=1, source_target_pairs={{0,8},{4,0},{8,12},{12,4},{1,9},{5,1},{9,13},{13,5},{2,10},{6,2},{... | collective-permute-start | bytes 98312 | tf_op jit(solution)/shard_map/ppermute | solution.py:254
  42.1 1.4 %collective-permute-start.9 = (f32[256,128]{1,0:T(8,128)S(1)}, f32[256,128]{1,0:T(8,128)S(1)}, u32[]{:S(2)}, u32[]{:S(2)}) collective-permute-start(f32[256,128]{1,0:T(8,128)S(1)} %shard_map.73), channel_id=1, source_target_pairs={{0,1},{1,0},{2,3},{3,2},{4,5},{5,4},{6,7},{7,6},{8,9},{9,8},{10,11... | collective-permute-start | bytes 393224 | tf_op jit(solution)/shard_map/ppermute | solution.py:174
  44.1 4.0 %collective-permute-start.10 = (bf16[128,128]{1,0:T(8,128)(2,1)S(1)}, bf16[128,128]{1,0:T(8,128)(2,1)S(1)}, u32[]{:S(2)}, u32[]{:S(2)}) collective-permute-start(bf16[128,128]{1,0:T(8,128)(2,1)S(1)} %get-tuple-element.49), channel_id=1, source_target_pairs={{0,2},{1,3},{2,0},{3,1},{4,6},{5,7},{6,4},{7,5},{8,10},{9,11},{10,... | collective-permute-start | bytes 98312 | tf_op jit(solution)/shard_map/ppermute | solution.py:174
  48.1 5.8 %collective-permute-start.11 = (bf16[128,128]{1,0:T(8,128)(2,1)S(1)}, bf16[128,128]{1,0:T(8,128)(2,1)S(1)}, u32[]{:S(2)}, u32[]{:S(2)}) collective-permute-start(bf16[128,128]{1,0:T(8,128)(2,1)S(1)} %shard_map.75), channel_id=1, source_target_pairs={{0,12},{4,8},{8,4},{12,0},{1,13},{5,9},{9,5},{13,1},{2,14},{6,10},... | collective-permute-start | bytes 98312 | tf_op jit(solution)/shard_map/ppermute | solution.py:254

commit v10 on v9

--- a/solution.py
+++ b/solution.py
@@ -13,6 +13,14 @@
 DAMPING = 0.05
 NT = (((1,), (1,)), ((), ()))
 MIB = 1024 * 1024
+
+
+def layer_index():
+    return lax.axis_index("layer").astype(jnp.int32)
+
+
+def row_index():
+    return lax.axis_index("rows").astype(jnp.int32)
 
 
 def prepare_kernel(
@@ -25,7 +33,7 @@
         copies.append(pltpu.make_async_copy(bases_hbm.at[layer], bases.at[layer], arrived.at[2 + 2 * layer]))
     for copy in copies:
         copy.start()
-    base_column = lax.axis_index("layer") * (LAY_DEV * LDIM)
+    base_column = layer_index() * (LAY_DEV * LDIM)
     copies[0].wait()
     for layer in range(LAY_DEV):
         copies[1 + 2 * layer].wait()
@@ -65,7 +73,7 @@
     return jnp.where(query_ids == doc_ids, 0.0, tile)
 
 
-def scoring(kernel, out_shape, place, conditioned, query_ids, documents, extra=(), scratch=()):
+def scoring(kernel, out_shape, conditioned, query_ids, documents, extra=(), scratch=()):
     dims = conditioned.shape[1]
     docs = documents.shape[0]
     rows = sum(shape.shape[0] for shape in out_shape)
@@ -73,50 +81,50 @@
     return pl.pallas_call(
         kernel,
         out_shape=out_shape,
-        in_specs=[pl.BlockSpec(memory_space=pltpu.SMEM)] + [vmem] * (3 + len(extra)),
+        in_specs=[vmem] * (3 + len(extra)),
         out_specs=[vmem] * len(out_shape),
         scratch_shapes=scratch,
         compiler_params=pltpu.CompilerParams(vmem_limit_bytes=12 * MIB),
         cost_estimate=pl.CostEstimate(
             flops=2 * rows * docs * dims, bytes_accessed=2 * dims * (rows + docs), transcendentals=0
         ),
-    )(place, conditioned, query_ids, documents, *extra)
-
-
-def turned_kernel(shares, block_of, place, queries_ref, ids_ref, documents_ref, *refs):
+    )(conditioned, query_ids, documents, *extra)
+
+
+def turned_kernel(shares, block_of, queries_ref, ids_ref, documents_ref, *refs):
     *out_refs, held = refs
-    held[...] = masked_tile(queries_ref[...], documents_ref[...], ids_ref[...], block_of(place[1]))
+    held[...] = masked_tile(queries_ref[...], documents_ref[...], ids_ref[...], block_of(row_index()))
     for turn, out_ref in enumerate(out_refs):
         share_rows = out_ref.shape[0]
-        first = pl.multiple_of(lax.rem(place[0] + turn, shares) * share_rows, share_rows)
+        first = pl.multiple_of(lax.rem(layer_index() + turn, shares) * share_rows, share_rows)
         out_ref[...] = held[pl.ds(first, share_rows), :].astype(jnp.bfloat16)
 
 
-def half_shares(layer, share_rows, kept):
-    core = lax.rem(layer, 2)
+def half_shares(share_rows, kept):
+    core = lax.rem(layer_index(), 2)
     core = core if kept else 1 - core
     return [pl.multiple_of((2 * chip + core) * share_rows, share_rows) for chip in range(2)]
 
 
-def halves_kernel(block_of, place, queries_ref, ids_ref, documents_ref, *refs):
+def halves_kernel(block_of, queries_ref, ids_ref, documents_ref, *refs):
     front_refs, out_refs, held = refs[:-3], refs[-3:-1], refs[-1]
-    held[...] = masked_tile(queries_ref[...], documents_ref[...], ids_ref[...], block_of(place[1]))
+    held[...] = masked_tile(queries_ref[...], documents_ref[...], ids_ref[...], block_of(row_index()))
     docs = documents_ref.shape[0]
     rows, width = out_refs[0].shape
     for side, kept in enumerate((True, False)):
         if front_refs:
             out_refs[side][:, : width - docs] = front_refs[side][...]
-        for chip, first in enumerate(half_shares(place[0], rows // 2, kept)):
+        for chip, first in enumerate(half_shares(rows // 2, kept)):
             spot = slice(chip * (rows // 2), (chip + 1) * (rows // 2))
             out_refs[side][spot, width - docs :] = held[pl.ds(first, rows // 2), :]
 
 
-def half_kernel(block_of, kept, place, queries_ref, ids_ref, documents_ref, out_ref):
+def half_kernel(block_of, kept, queries_ref, ids_ref, documents_ref, out_ref):
     share_rows = out_ref.shape[0] // 2
-    firsts = half_shares(place[0], share_rows, kept)
+    firsts = half_shares(share_rows, kept)
     queries = jnp.concatenate([queries_ref[pl.ds(first, share_rows), :] for first in firsts], axis=0)
     query_ids = jnp.concatenate([ids_ref[pl.ds(first, share_rows), :] for first in firsts], axis=0)
-    out_ref[...] = masked_tile(queries, documents_ref[...], query_ids, block_of(place[1]))
+    out_ref[...] = masked_tile(queries, documents_ref[...], query_ids, block_of(row_index()))
 
 
 def total_of(refs):
@@ -130,16 +138,15 @@
     refs[-1][...] = total_of(refs[:-1])
 
 
-def small_call(kernel, out_shape, *args, place=None):
+def small_call(kernel, out_shape, *args):
     vmem = pl.BlockSpec(memory_space=pltpu.VMEM)
-    scalars = [] if place is None else [place]
     return pl.pallas_call(
         kernel,
         out_shape=out_shape,
-        in_specs=[pl.BlockSpec(memory_space=pltpu.SMEM)] * len(scalars) + [vmem] * len(args),
+        in_specs=[vmem] * len(args),
         out_specs=[vmem] * len(out_shape),
         compiler_params=pltpu.CompilerParams(vmem_limit_bytes=4 * MIB),
-    )(*scalars, *args)
+    )(*args)
 
 
 def direct_sum(tiles):
@@ -152,12 +159,12 @@
     return total
 
 
-def core_sum_kernel(place, kept_ref, arrived_ref, mine_ref, other_ref):
+def core_sum_kernel(kept_ref, arrived_ref, mine_ref, other_ref):
     rows = mine_ref.shape[0]
-    chip = place[0] // 2
+    chip = lax.div(layer_index(), 2)
     mine = pl.ds(pl.multiple_of(chip * rows, rows), rows)
     other = pl.ds(pl.multiple_of((1 - chip) * rows, rows), rows)
-    mine_ref[...] = kept_ref[mine, :] + arrived_ref[mine, :]
+    mine_ref[...] = (kept_ref[mine, :] + arrived_ref[mine, :]).astype(mine_ref.dtype)
     other_ref[...] = (kept_ref[other, :] + arrived_ref[other, :]).astype(other_ref.dtype)
 
 
@@ -174,14 +181,15 @@
     return lax.ppermute(value, "layer", [(lay, lay ^ distance) for lay in range(count)])
 
 
-def layer_sum(kept, sent, place, out_types):
+def core_sum(kept, arrived, mine_type):
     rows, width = kept.shape[0] // 2, kept.shape[1]
-    mine, other = small_call(
-        core_sum_kernel,
-        [jax.ShapeDtypeStruct((rows, width), jnp.float32), jax.ShapeDtypeStruct((rows, width), jnp.bfloat16)],
-        kept, swap(sent, 1), place=place,
-    )
-    docs = width // len(out_types)
+    out_shape = [jax.ShapeDtypeStruct((rows, width), out_type) for out_type in (mine_type, jnp.bfloat16)]
+    return small_call(core_sum_kernel, out_shape, kept, arrived)
+
+
+def layer_sum(kept, sent, out_types):
+    mine, other = core_sum(kept, swap(sent, 1), jnp.float32)
+    rows, docs = mine.shape[0], mine.shape[1] // len(out_types)
     out_shape = [jax.ShapeDtypeStruct((rows, docs), out_type) for out_type in out_types]
     return small_call(chip_sum_kernel, out_shape, mine, swap(other, 2))
 
@@ -207,34 +215,35 @@
     return pick([(block - table.index(block)) % STEPS for block in range(STEPS)])
 
 
-def assemble_kernel(place, own_ref, first_ref, second_ref, out_ref):
+def assemble_kernel(own_ref, first_ref, second_ref, out_ref):
     out_ref[0] = own_ref[...]
     for ref, table in ((first_ref, BLOCK_ONE), (second_ref, BLOCK_TWO)):
-        out_ref[step_of(table)(place[1])] = ref[...].astype(jnp.float32)
-
-
-def finish_kernel(place, last_ref, scores_hbm, out_hbm, wide, copied):
+        out_ref[step_of(table)(row_index())] = ref[...].astype(jnp.float32)
+
+
+def finish_kernel(mine_ref, other_ref, scores_hbm, out_hbm, total, copied):
     del scores_hbm
-    wide[...] = last_ref[...].astype(jnp.float32)
-    copy = pltpu.make_async_copy(wide, out_hbm.at[step_of(BLOCK_LAST)(place[1])], copied)
+    total[...] = total_of([mine_ref, other_ref])
+    copy = pltpu.make_async_copy(total, out_hbm.at[step_of(BLOCK_LAST)(row_index())], copied)
     copy.start()
     copy.wait()
 
 
-def finish(place, last, scores):
+def finish(mine, other, scores):
     hbm = pl.BlockSpec(memory_space=pltpu.HBM)
+    vmem = pl.BlockSpec(memory_space=pltpu.VMEM)
     return pl.pallas_call(
         finish_kernel,
         out_shape=jax.ShapeDtypeStruct(scores.shape, scores.dtype),
-        in_specs=[pl.BlockSpec(memory_space=pltpu.SMEM), pl.BlockSpec(memory_space=pltpu.VMEM), hbm],
+        in_specs=[vmem, vmem, hbm],
         out_specs=hbm,
-        scratch_shapes=[pltpu.VMEM(last.shape, jnp.float32), pltpu.SemaphoreType.DMA],
+        scratch_shapes=[pltpu.VMEM(mine.shape, jnp.float32), pltpu.SemaphoreType.DMA],
         input_output_aliases={2: 0},
         compiler_params=pltpu.CompilerParams(vmem_limit_bytes=4 * MIB),
-    )(place, last, scores)
-
-
-def along_line(documents, conditioned, query_ids, place):
+    )(mine, other, scores)
+
+
+def along_line(documents, conditioned, query_ids):
     docs = documents.shape[0]
     half = (conditioned.shape[0] // 2, docs)
 
@@ -243,12 +252,12 @@
         out_shape = [jax.ShapeDtypeStruct((half[0], width), jnp.float32)] * 2
         scratch = [pltpu.VMEM((2 * half[0], docs), jnp.float32)]
         kernel = functools.partial(halves_kernel, block_of)
-        return scoring(kernel, out_shape, place, conditioned, query_ids, block, front, scratch)
+        return scoring(kernel, out_shape, conditioned, query_ids, block, front, scratch)
 
     def one_half(block, block_of, kept):
         kernel = functools.partial(half_kernel, block_of, kept)
         out_shape = [jax.ShapeDtypeStruct(half, jnp.float32)]
-        return scoring(kernel, out_shape, place, conditioned, query_ids, block)[0]
+        return scoring(kernel, out_shape, conditioned, query_ids, block)[0]
 
     def back(total, table):
         return lax.ppermute(total, "rows", tuple(enumerate(table)))
@@ -260,23 +269,30 @@
     one, own = lax.optimization_barrier((one, own))
     three = lax.ppermute(one, "rows", ROUND_ONE)
 
-    own, first = layer_sum(*halves(one, pick(BLOCK_ONE), own), place, (jnp.float32, jnp.bfloat16))
+    own, first = layer_sum(*halves(one, pick(BLOCK_ONE), own), (jnp.float32, jnp.bfloat16))
     two, first = lax.optimization_barrier((two, first))
     first = back(first, BLOCK_ONE)
-    (second,) = layer_sum(*halves(two, pick(BLOCK_TWO)), place, (jnp.bfloat16,))
+    (second,) = layer_sum(*halves(two, pick(BLOCK_TWO)), (jnp.bfloat16,))
     second = back(second, BLOCK_TWO)
     three, first, second = lax.optimization_barrier((three, first, second))
 
-    sent = one_half(three, pick(BLOCK_LAST), False)
+    arrived = swap(one_half(three, pick(BLOCK_LAST), False), 1)
     kept = one_half(three, pick(BLOCK_LAST), True)
-    (last,) = layer_sum(kept, sent, place, (jnp.bfloat16,))
-    last = back(last, BLOCK_LAST)
+    mine, other = core_sum(kept, arrived, jnp.bfloat16)
+    mine = back(mine, BLOCK_LAST)
+    shares = lax.axis_size("layer")
+    pairs = [
+        (row * shares + lay, BLOCK_LAST[row] * shares + (lay ^ 2))
+        for row in range(len(BLOCK_LAST))
+        for lay in range(shares)
+    ]
+    other = lax.ppermute(other, ("rows", "layer"), pairs)
     out_shape = [jax.ShapeDtypeStruct((STEPS,) + own.shape, jnp.float32)]
-    (scores,) = small_call(assemble_kernel, out_shape, own, first, second, place=place)
-    return finish(place, last, scores)
-
-
-def around_ring(documents, conditioned, query_ids, place):
+    (scores,) = small_call(assemble_kernel, out_shape, own, first, second)
+    return finish(mine, other, scores)
+
+
+def around_ring(documents, conditioned, query_ids):
     n_rows, shares = lax.axis_size("rows"), lax.axis_size("layer")
     rows, docs = conditioned.shape[0], documents.shape[0]
     result = []
@@ -290,18 +306,17 @@
         kernel = functools.partial(turned_kernel, shares, ahead)
         out_shape = [jax.ShapeDtypeStruct((rows // shares, docs), jnp.bfloat16)] * shares
         scratch = [pltpu.VMEM((rows, docs), jnp.float32)]
-        total = direct_sum(scoring(kernel, out_shape, place, conditioned, query_ids, block, (), scratch))
+        total = direct_sum(scoring(kernel, out_shape, conditioned, query_ids, block, (), scratch))
         onward = [(row, (row + step) % n_rows) for row in range(n_rows)]
         result.append(lax.ppermute(total, "rows", onward) if step else total)
     return jnp.stack(result)
 
 
 def local(train_grads, query_grads, eigenbases, eigenvalues, layer_offsets, query_doc_ids):
-    place = jnp.stack([lax.axis_index("layer"), lax.axis_index("rows")]).astype(jnp.int32)
     conditioned = prepare(query_grads, eigenbases, eigenvalues, layer_offsets)
     on_line = lax.axis_size("rows") == 4 and lax.axis_size("layer") == 4
     plan = along_line if on_line else around_ring
-    return plan(train_grads, conditioned, query_doc_ids[:, None], place)
+    return plan(train_grads, conditioned, query_doc_ids[:, None])
 
 
 def solution(mesh):

time: 55.3 us -> 53 us (0.958)
  Pallas kernels: 16.2 us -> 10.7 us
  waiting for transfers between devices: 20.7 us -> 23.2 us
  starting transfers between devices: 16.2 us -> 16.9 us
    pallas_call x12 -> x11, Pallas kernels: 8.86 us -> 3.96 us  [the longest x5 3.15 us: scoring(): pl.pallas_call(kernel, out_shape=out_shape, in_specs=[vmem] * (3 + len(ex...]
    ppermute x0 -> x1, waiting for transfers between devices: none -> 3.33 us  [along_line(): other = lax.ppermute(other, ('rows', 'layer'), pairs)]
    ppermute x0 -> x1, starting transfers between devices: none -> 2.29 us  [along_line(): other = lax.ppermute(other, ('rows', 'layer'), pairs)]
    ppermute x6 -> x5, waiting for transfers between devices: 8.64 us -> 6.68 us  [swap(): lax.ppermute(value, 'layer', [(lay, lay ^ distance) for lay in range(coun...]
    ppermute x6 -> x5, starting transfers between devices: 4.88 us -> 3.41 us  [swap(): lax.ppermute(value, 'layer', [(lay, lay ^ distance) for lay in range(coun...]
    ppermute x1, waiting for transfers between devices: 3.29 us -> 4.39 us  [along_line(): two = lax.ppermute(later, 'rows', ROUND_TWO)]
    ppermute x1, waiting for transfers between devices: 3.31 us -> 3.93 us  [along_line(): one = lax.ppermute(documents, 'rows', ROUND_ONE)]
    ppermute x3, waiting for transfers between devices: 5.51 us -> 4.92 us  [back(): return lax.ppermute(total, 'rows', tuple(enumerate(table)))]
  transfers between devices with their start and end apart: 12 -> 12, of which waited for: 10 -> 10; matrix products, arithmetic and copies ran while one was open for 0% -> 0% of each run, Pallas kernels for 24% -> 18%
where the time goes in v10:
time: 53 us; the launch traced here: 52.8 us
  waiting for transfers between devices  23.2 us (44%)
  starting transfers between devices  16.9 us (32%)
  Pallas kernels  10.7 us (20%)
  local copies, waits for them, and re-layouts  1.74 us (3%)
    ppermute x5, waiting for transfers between devices, swap(): lax.ppermute(value, 'layer', [(lay, lay ^ distance) for lay in range(coun...  6.68 us
    pallas_call x1, Pallas kernels, prepare(): pl.pallas_call(prepare_kernel, out_shape=jax.ShapeDtypeStruct((rows, dims...  6.15 us
    ppermute x3, waiting for transfers between devices, back(): return lax.ppermute(total, 'rows', tuple(enumerate(table)))  4.92 us
    ppermute x1, waiting for transfers between devices, along_line(): two = lax.ppermute(later, 'rows', ROUND_TWO)  4.39 us
    ppermute x1, starting transfers between devices, along_line(): one = lax.ppermute(documents, 'rows', ROUND_ONE)  4.04 us
    ppermute x1, waiting for transfers between devices, along_line(): one = lax.ppermute(documents, 'rows', ROUND_ONE)  3.93 us
    ppermute x3, starting transfers between devices, back(): return lax.ppermute(total, 'rows', tuple(enumerate(table)))  3.82 us
    ppermute x5, starting transfers between devices, swap(): lax.ppermute(value, 'layer', [(lay, lay ^ distance) for lay in range(coun...  3.41 us
  transfers between devices with their start and end apart: 12, of which 10 were waited for; matrix products, arithmetic and copies ran while one was open for 0% of the time, Pallas kernels for 18%

profile of v10, /device:TPU:0, one launch (start us, length us, event | category | flops | bytes accessed | tf_op | source)
XLA Modules:
  0.0 52.8 jit_solution(4991514414209198536)
XLA Ops:
  0.0 0.0 copy-start.1
  0.0 0.0 copy-start.2
  0.0 4.0 %collective-permute-start = (bf16[128,2048]{1,0:T(8,128)(2,1)}, bf16[128,2048]{1,0:T(8,128)(2,1)S(1)}, u32[]{:S(2)}, u32[]{:S(2)}) collective-permute-start(bf16[128,2048]{1,0:T(8,128)(2,1)} %documents_ref), channel_id=1, source_target_pairs={{0,8},{8,12},{12,4},{4,0},{1,9},{9,13},{13,5},{5,1},{2,10},{10,14}... | collective-permute-start | bytes 1572872 | tf_op jit(solution)/shard_map/ppermute | solution.py:265
  4.0 6.1 %shard_map.64.queries_ref = bf16[512,2048]{1,0:T(8,128)(2,1)} custom-call(s32[4]{0:T(128)} %offsets.1, bf16[512,2048]{1,0:T(8,128)(2,1)} %queries_hbm.1, bf16[4,512,512]{2,1,0:T(8,128)(2,1)} %bases_hbm.1, f32[4,512]{1,0:T(4,128)} %values_hbm.1), custom_call_target="tpu_custom_call" | custom-call | flops 2147483648 | bytes 6291456 | tf_op jit(solution)/shard_map/pallas_call | solution.py:52
  10.2 0.0 copy-done.1
  10.2 0.1 collective-permute-start.2
  10.3 0.0 copy-done.2
  10.3 0.1 copy.11.ids_ref
  10.4 0.0 copy-start
  10.4 1.6 %copy-done = bf16[512,2048]{1,0:T(8,128)(2,1)S(1)} copy-done((bf16[512,2048]{1,0:T(8,128)(2,1)S(1)}, bf16[512,2048]{1,0:T(8,128)(2,1)}, u32[]{:S(2)}) %copy-start) | copy-done | bytes 2097176
  12.0 0.8 %shard_map.65 = (f32[256,128]{1,0:T(8,128)S(1)}, f32[256,128]{1,0:T(8,128)S(1)}) custom-call(bf16[512,2048]{1,0:T(8,128)(2,1)S(1)} %copy-done, s32[512,1]{1,0:T(8,128)S(1)} %copy.11.ids_ref, bf16[128,2048]{1,0:T(8,128)(2,1)S(1)} %copy-done.1), custom_call_target="tpu_custom_call" | custom-call | flops 268435456 | bytes 2621440 | tf_op jit(solution)/shard_map/pallas_call | solution.py:81
  12.8 3.9 %collective-permute-done.documents_ref = bf16[128,2048]{1,0:T(8,128)(2,1)S(1)} collective-permute-done((bf16[128,2048]{1,0:T(8,128)(2,1)}, bf16[128,2048]{1,0:T(8,128)(2,1)S(1)}, u32[]{:S(2)}, u32[]{:S(2)}) %collective-permute-start) | collective-permute-done | bytes 524320 | tf_op jit(solution)/shard_map/ppermute | solution.py:265
  16.7 0.8 %shard_map.66 = (f32[256,256]{1,0:T(8,128)S(1)}, f32[256,256]{1,0:T(8,128)S(1)}) custom-call(bf16[512,2048]{1,0:T(8,128)(2,1)S(1)} %copy-done, s32[512,1]{1,0:T(8,128)S(1)} %copy.11.ids_ref, bf16[128,2048]{1,0:T(8,128)(2,1)S(1)} %collective-permute-done.documents_ref, f32[256,128]{1,0:T(8,128)S(1)} %get-tuple-element.34.refs_0_, ...), custom_call_target="tpu_custom_call" | custom-call | flops 268435456 | bytes 2621440 | tf_op jit(solution)/shard_map/pallas_call | solution.py:81
  17.5 0.1 collective-permute-start.3
  17.6 3.3 %collective-permute-start.1 = (bf16[128,2048]{1,0:T(8,128)(2,1)S(1)}, bf16[128,2048]{1,0:T(8,128)(2,1)S(1)}, u32[]{:S(2)}, u32[]{:S(2)}) collective-permute-start(bf16[128,2048]{1,0:T(8,128)(2,1)S(1)} %collective-permute-done.documents_ref), channel_id=1, source_target_pairs={{0,8},{8,12},{12,4},{4,0},{1,9},{9,13},{13,5},{5,1},{2,10},{10,14}... | collective-permute-start | bytes 1572872 | tf_op jit(solution)/shard_map/ppermute | solution.py:270
  20.9 0.0 collective-permute-done.3.arrived_ref
  20.9 1.6 %collective-permute-start.4 = (bf16[128,256]{1,0:T(8,128)(2,1)S(1)}, bf16[128,256]{1,0:T(8,128)(2,1)S(1)}, u32[]{:S(2)}, u32[]{:S(2)}) collective-permute-start(bf16[128,256]{1,0:T(8,128)(2,1)S(1)} %get-tuple-element.39), channel_id=1, source_target_pairs={{0,2},{1,3},{2,0},{3,1},{4,6},{5,7},{6,4},{7,5},{8,10},{9,11},{10,... | collective-permute-start | bytes 196616 | tf_op jit(solution)/shard_map/ppermute | solution.py:181
  22.5 2.8 %collective-permute-done.4.arrived_ref = bf16[128,256]{1,0:T(8,128)(2,1)S(1)} collective-permute-done((bf16[128,256]{1,0:T(8,128)(2,1)S(1)}, bf16[128,256]{1,0:T(8,128)(2,1)S(1)}, u32[]{:S(2)}, u32[]{:S(2)}) %collective-permute-start.4) | collective-permute-done | bytes 65568 | tf_op jit(solution)/shard_map/ppermute | solution.py:181
  25.3 4.4 %collective-permute-done.2.documents_ref = bf16[128,2048]{1,0:T(8,128)(2,1)S(1)} collective-permute-done((bf16[128,2048]{1,0:T(8,128)(2,1)S(1)}, bf16[128,2048]{1,0:T(8,128)(2,1)S(1)}, u32[]{:S(2)}, u32[]{:S(2)}) %collective-permute-start.2) | collective-permute-done | bytes 524320 | tf_op jit(solution)/shard_map/ppermute | solution.py:267
  29.7 0.8 %shard_map.69 = (f32[256,128]{1,0:T(8,128)S(1)}, f32[256,128]{1,0:T(8,128)S(1)}) custom-call(bf16[512,2048]{1,0:T(8,128)(2,1)S(1)} %copy-done, s32[512,1]{1,0:T(8,128)S(1)} %copy.11.ids_ref, bf16[128,2048]{1,0:T(8,128)(2,1)S(1)} %collective-permute-done.2.documents_ref), custom_call_target="tpu_custom_call" | custom-call | flops 268435456 | bytes 2621440 | tf_op jit(solution)/shard_map/pallas_call | solution.py:81
  30.4 0.1 collective-permute-start.6
  30.5 1.3 %collective-permute-done.6.arrived_ref = f32[256,128]{1,0:T(8,128)S(1)} collective-permute-done((f32[256,128]{1,0:T(8,128)S(1)}, f32[256,128]{1,0:T(8,128)S(1)}, u32[]{:S(2)}, u32[]{:S(2)}) %collective-permute-start.6) | collective-permute-done | bytes 131104 | tf_op jit(solution)/shard_map/ppermute | solution.py:181
  31.9 1.6 %collective-permute-start.7 = (bf16[128,128]{1,0:T(8,128)(2,1)S(1)}, bf16[128,128]{1,0:T(8,128)(2,1)S(1)}, u32[]{:S(2)}, u32[]{:S(2)}) collective-permute-start(bf16[128,128]{1,0:T(8,128)(2,1)S(1)} %get-tuple-element.46), channel_id=1, source_target_pairs={{0,2},{1,3},{2,0},{3,1},{4,6},{5,7},{6,4},{7,5},{8,10},{9,11},{10,... | collective-permute-start | bytes 98312 | tf_op jit(solution)/shard_map/ppermute | solution.py:181
  33.4 0.7 %collective-permute-start.5 = (bf16[128,128]{1,0:T(8,128)(2,1)S(1)}, bf16[128,128]{1,0:T(8,128)(2,1)S(1)}, u32[]{:S(2)}, u32[]{:S(2)}) collective-permute-start(bf16[128,128]{1,0:T(8,128)(2,1)S(1)} %get-tuple-element.41), channel_id=1, source_target_pairs={{0,4},{4,12},{8,0},{12,8},{1,5},{5,13},{9,1},{13,9},{2,6},{6,14},{... | collective-permute-start | bytes 98312 | tf_op jit(solution)/shard_map/ppermute | solution.py:263
  34.1 1.7 %collective-permute-done.7.arrived_ref = bf16[128,128]{1,0:T(8,128)(2,1)S(1)} collective-permute-done((bf16[128,128]{1,0:T(8,128)(2,1)S(1)}, bf16[128,128]{1,0:T(8,128)(2,1)S(1)}, u32[]{:S(2)}, u32[]{:S(2)}) %collective-permute-start.7) | collective-permute-done | bytes 32800 | tf_op jit(solution)/shard_map/ppermute | solution.py:181
  35.9 0.6 %collective-permute-start.8 = (bf16[128,128]{1,0:T(8,128)(2,1)S(1)}, bf16[128,128]{1,0:T(8,128)(2,1)S(1)}, u32[]{:S(2)}, u32[]{:S(2)}) collective-permute-start(bf16[128,128]{1,0:T(8,128)(2,1)S(1)} %shard_map.71), channel_id=1, source_target_pairs={{0,8},{4,0},{8,12},{12,4},{1,9},{5,1},{9,13},{13,5},{2,10},{6,2},{... | collective-permute-start | bytes 98312 | tf_op jit(solution)/shard_map/ppermute | solution.py:263
  36.5 4.5 %collective-permute-done.5.first_ref = bf16[128,128]{1,0:T(8,128)(2,1)S(1)} collective-permute-done((bf16[128,128]{1,0:T(8,128)(2,1)S(1)}, bf16[128,128]{1,0:T(8,128)(2,1)S(1)}, u32[]{:S(2)}, u32[]{:S(2)}) %collective-permute-start.5) | collective-permute-done | bytes 32800 | tf_op jit(solution)/shard_map/ppermute | solution.py:263
  40.9 0.0 collective-permute-done.1.documents_ref
  40.9 0.2 collective-permute-done.8.second_ref
  41.1 0.4 shard_map.73
  41.6 0.2 collective-permute-start.9
  41.7 0.4 shard_map.72.kept_ref
  42.2 0.8 %collective-permute-done.9.arrived_ref = f32[256,128]{1,0:T(8,128)S(1)} collective-permute-done((f32[256,128]{1,0:T(8,128)S(1)}, f32[256,128]{1,0:T(8,128)S(1)}, u32[]{:S(2)}, u32[]{:S(2)}) %collective-permute-start.9) | collective-permute-done | bytes 131104 | tf_op jit(solution)/shard_map/ppermute | solution.py:181
  43.0 2.5 %collective-permute-start.10 = (bf16[128,128]{1,0:T(8,128)(2,1)S(1)}, bf16[128,128]{1,0:T(8,128)(2,1)S(1)}, u32[]{:S(2)}, u32[]{:S(2)}) collective-permute-start(bf16[128,128]{1,0:T(8,128)(2,1)S(1)} %get-tuple-element.48), channel_id=1, source_target_pairs={{0,12},{4,8},{8,4},{12,0},{1,13},{5,9},{9,5},{13,1},{2,14},{6,10},... | collective-permute-start | bytes 98312 | tf_op jit(solution)/shard_map/ppermute | solution.py:263
  45.5 2.3 %collective-permute-start.11 = (bf16[128,128]{1,0:T(8,128)(2,1)S(1)}, bf16[128,128]{1,0:T(8,128)(2,1)S(1)}, u32[]{:S(2)}, u32[]{:S(2)}) collective-permute-start(bf16[128,128]{1,0:T(8,128)(2,1)S(1)} %get-tuple-element.49), channel_id=1, source_target_pairs={{0,14},{1,15},{2,12},{3,13},{4,10},{5,11},{6,8},{7,9},{8,6},{9,7},... | collective-permute-start | bytes 98312 | tf_op jit(solution)/shard_map/ppermute | solution.py:289
  47.8 0.7 %shard_map.75.scores_hbm = f32[4,128,128]{2,1,0:T(8,128)} custom-call(f32[128,128]{1,0:T(8,128)S(1)} %get-tuple-element.50.own_ref, bf16[128,128]{1,0:T(8,128)(2,1)S(1)} %collective-permute-done.5.first_ref, bf16[128,128]{1,0:T(8,128)(2,1)S(1)} %collective-permute-done.8.second_ref), custom_call_target="tpu_custom_call" | custom-call | tf_op jit(solution)/shard_map/pallas_call | solution.py:143
  48.5 0.3 collective-permute-done.10.mine_ref
  48.8 3.3 %collective-permute-done.11.other_ref = bf16[128,128]{1,0:T(8,128)(2,1)S(1)} collective-permute-done((bf16[128,128]{1,0:T(8,128)(2,1)S(1)}, bf16[128,128]{1,0:T(8,128)(2,1)S(1)}, u32[]{:S(2)}, u32[]{:S(2)}) %collective-permute-start.11) | collective-permute-done | bytes 32800 | tf_op jit(solution)/shard_map/ppermute | solution.py:289
  52.1 0.6 %shard_map.76 = f32[4,128,128]{2,1,0:T(8,128)} custom-call(bf16[128,128]{1,0:T(8,128)(2,1)S(1)} %collective-permute-done.10.mine_ref, bf16[128,128]{1,0:T(8,128)(2,1)S(1)} %collective-permute-done.11.other_ref, f32[4,128,128]{2,1,0:T(8,128)} %shard_map.75.scores_hbm), custom_call_target="tpu_custom_call", output_to_operand_aliasing={{}: (2, {})} | custom-call | tf_op jit(solution)/shard_map/pallas_call | solution.py:235
  (5 shorter events, 0.1 us)
Async XLA Ops:
  0.0 10.2 %copy-start.1 = (bf16[128,2048]{1,0:T(8,128)(2,1)S(1)}, bf16[128,2048]{1,0:T(8,128)(2,1)}, u32[]{:S(2)}) copy-start(bf16[128,2048]{1,0:T(8,128)(2,1)} %documents_ref) | copy-start | bytes 1572868
  0.0 10.3 %copy-start.2 = (s32[512]{0:T(512)S(1)}, s32[512]{0:T(512)}, u32[]{:S(2)}) copy-start(s32[512]{0:T(512)} %param.11) | copy-start | bytes 6148
  0.0 16.7 %collective-permute-start = (bf16[128,2048]{1,0:T(8,128)(2,1)}, bf16[128,2048]{1,0:T(8,128)(2,1)S(1)}, u32[]{:S(2)}, u32[]{:S(2)}) collective-permute-start(bf16[128,2048]{1,0:T(8,128)(2,1)} %documents_ref), channel_id=1, source_target_pairs={{0,8},{8,12},{12,4},{4,0},{1,9},{9,13},{13,5},{5,1},{2,10},{10,14}... | collective-permute-start | bytes 1572872 | tf_op jit(solution)/shard_map/ppermute | solution.py:265
  10.2 19.5 %collective-permute-start.2 = (bf16[128,2048]{1,0:T(8,128)(2,1)S(1)}, bf16[128,2048]{1,0:T(8,128)(2,1)S(1)}, u32[]{:S(2)}, u32[]{:S(2)}) collective-permute-start(bf16[128,2048]{1,0:T(8,128)(2,1)S(1)} %copy-done.1), channel_id=1, source_target_pairs={{0,4},{4,12},{12,8},{8,0},{1,5},{5,13},{13,9},{9,1},{2,6},{6,14},{... | collective-permute-start | bytes 1572872 | tf_op jit(solution)/shard_map/ppermute | solution.py:267
  10.4 1.6 %copy-start = (bf16[512,2048]{1,0:T(8,128)(2,1)S(1)}, bf16[512,2048]{1,0:T(8,128)(2,1)}, u32[]{:S(2)}) copy-start(bf16[512,2048]{1,0:T(8,128)(2,1)} %shard_map.64.queries_ref) | copy-start | bytes 6291460
  17.5 3.4 %collective-permute-start.3 = (f32[256,256]{1,0:T(8,128)S(1)}, f32[256,256]{1,0:T(8,128)S(1)}, u32[]{:S(2)}, u32[]{:S(2)}) collective-permute-start(f32[256,256]{1,0:T(8,128)S(1)} %get-tuple-element.37), channel_id=1, source_target_pairs={{0,1},{1,0},{2,3},{3,2},{4,5},{5,4},{6,7},{7,6},{8,9},{9,8},{10,11... | collective-permute-start | bytes 786440 | tf_op jit(solution)/shard_map/ppermute | solution.py:181
  17.6 23.4 %collective-permute-start.1 = (bf16[128,2048]{1,0:T(8,128)(2,1)S(1)}, bf16[128,2048]{1,0:T(8,128)(2,1)S(1)}, u32[]{:S(2)}, u32[]{:S(2)}) collective-permute-start(bf16[128,2048]{1,0:T(8,128)(2,1)S(1)} %collective-permute-done.documents_ref), channel_id=1, source_target_pairs={{0,8},{8,12},{12,4},{4,0},{1,9},{9,13},{13,5},{5,1},{2,10},{10,14}... | collective-permute-start | bytes 1572872 | tf_op jit(solution)/shard_map/ppermute | solution.py:270
  20.9 4.3 %collective-permute-start.4 = (bf16[128,256]{1,0:T(8,128)(2,1)S(1)}, bf16[128,256]{1,0:T(8,128)(2,1)S(1)}, u32[]{:S(2)}, u32[]{:S(2)}) collective-permute-start(bf16[128,256]{1,0:T(8,128)(2,1)S(1)} %get-tuple-element.39), channel_id=1, source_target_pairs={{0,2},{1,3},{2,0},{3,1},{4,6},{5,7},{6,4},{7,5},{8,10},{9,11},{10,... | collective-permute-start | bytes 196616 | tf_op jit(solution)/shard_map/ppermute | solution.py:181
  30.4 1.4 %collective-permute-start.6 = (f32[256,128]{1,0:T(8,128)S(1)}, f32[256,128]{1,0:T(8,128)S(1)}, u32[]{:S(2)}, u32[]{:S(2)}) collective-permute-start(f32[256,128]{1,0:T(8,128)S(1)} %get-tuple-element.44), channel_id=1, source_target_pairs={{0,1},{1,0},{2,3},{3,2},{4,5},{5,4},{6,7},{7,6},{8,9},{9,8},{10,11... | collective-permute-start | bytes 393224 | tf_op jit(solution)/shard_map/ppermute | solution.py:181
  31.9 4.0 %collective-permute-start.7 = (bf16[128,128]{1,0:T(8,128)(2,1)S(1)}, bf16[128,128]{1,0:T(8,128)(2,1)S(1)}, u32[]{:S(2)}, u32[]{:S(2)}) collective-permute-start(bf16[128,128]{1,0:T(8,128)(2,1)S(1)} %get-tuple-element.46), channel_id=1, source_target_pairs={{0,2},{1,3},{2,0},{3,1},{4,6},{5,7},{6,4},{7,5},{8,10},{9,11},{10,... | collective-permute-start | bytes 98312 | tf_op jit(solution)/shard_map/ppermute | solution.py:181
  33.4 7.5 %collective-permute-start.5 = (bf16[128,128]{1,0:T(8,128)(2,1)S(1)}, bf16[128,128]{1,0:T(8,128)(2,1)S(1)}, u32[]{:S(2)}, u32[]{:S(2)}) collective-permute-start(bf16[128,128]{1,0:T(8,128)(2,1)S(1)} %get-tuple-element.41), channel_id=1, source_target_pairs={{0,4},{4,12},{8,0},{12,8},{1,5},{5,13},{9,1},{13,9},{2,6},{6,14},{... | collective-permute-start | bytes 98312 | tf_op jit(solution)/shard_map/ppermute | solution.py:263
  35.9 5.3 %collective-permute-start.8 = (bf16[128,128]{1,0:T(8,128)(2,1)S(1)}, bf16[128,128]{1,0:T(8,128)(2,1)S(1)}, u32[]{:S(2)}, u32[]{:S(2)}) collective-permute-start(bf16[128,128]{1,0:T(8,128)(2,1)S(1)} %shard_map.71), channel_id=1, source_target_pairs={{0,8},{4,0},{8,12},{12,4},{1,9},{5,1},{9,13},{13,5},{2,10},{6,2},{... | collective-permute-start | bytes 98312 | tf_op jit(solution)/shard_map/ppermute | solution.py:263
  41.6 1.4 %collective-permute-start.9 = (f32[256,128]{1,0:T(8,128)S(1)}, f32[256,128]{1,0:T(8,128)S(1)}, u32[]{:S(2)}, u32[]{:S(2)}) collective-permute-start(f32[256,128]{1,0:T(8,128)S(1)} %shard_map.73), channel_id=1, source_target_pairs={{0,1},{1,0},{2,3},{3,2},{4,5},{5,4},{6,7},{7,6},{8,9},{9,8},{10,11... | collective-permute-start | bytes 393224 | tf_op jit(solution)/shard_map/ppermute | solution.py:181
  43.0 5.8 %collective-permute-start.10 = (bf16[128,128]{1,0:T(8,128)(2,1)S(1)}, bf16[128,128]{1,0:T(8,128)(2,1)S(1)}, u32[]{:S(2)}, u32[]{:S(2)}) collective-permute-start(bf16[128,128]{1,0:T(8,128)(2,1)S(1)} %get-tuple-element.48), channel_id=1, source_target_pairs={{0,12},{4,8},{8,4},{12,0},{1,13},{5,9},{9,5},{13,1},{2,14},{6,10},... | collective-permute-start | bytes 98312 | tf_op jit(solution)/shard_map/ppermute | solution.py:263
  45.5 6.6 %collective-permute-start.11 = (bf16[128,128]{1,0:T(8,128)(2,1)S(1)}, bf16[128,128]{1,0:T(8,128)(2,1)S(1)}, u32[]{:S(2)}, u32[]{:S(2)}) collective-permute-start(bf16[128,128]{1,0:T(8,128)(2,1)S(1)} %get-tuple-element.49), channel_id=1, source_target_pairs={{0,14},{1,15},{2,12},{3,13},{4,10},{5,11},{6,8},{7,9},{8,6},{9,7},... | collective-permute-start | bytes 98312 | tf_op jit(solution)/shard_map/ppermute | solution.py:289

commit v11 on v10

--- a/solution.py
+++ b/solution.py
@@ -194,11 +194,11 @@
     return small_call(chip_sum_kernel, out_shape, mine, swap(other, 2))
 
 
-ROUND_ONE = ((0, 2), (2, 3), (3, 1), (1, 0))
-ROUND_TWO = ((0, 1), (1, 3), (3, 2), (2, 0))
-BLOCK_ONE = (1, 3, 0, 2)
-BLOCK_TWO = (2, 0, 3, 1)
-BLOCK_LAST = (3, 2, 1, 0)
+ROUND_ONE = ((0, 1), (1, 2), (2, 3), (3, 0))
+ROUND_TWO = ((0, 3), (1, 0), (2, 1), (3, 2))
+BLOCK_ONE = (3, 0, 1, 2)
+BLOCK_TWO = (1, 2, 3, 0)
+BLOCK_LAST = (2, 3, 0, 1)
 
 
 def pick(table):
@@ -279,7 +279,6 @@
     arrived = swap(one_half(three, pick(BLOCK_LAST), False), 1)
     kept = one_half(three, pick(BLOCK_LAST), True)
     mine, other = core_sum(kept, arrived, jnp.bfloat16)
-    mine = back(mine, BLOCK_LAST)
     shares = lax.axis_size("layer")
     pairs = [
         (row * shares + lay, BLOCK_LAST[row] * shares + (lay ^ 2))
@@ -287,6 +286,7 @@
         for lay in range(shares)
     ]
     other = lax.ppermute(other, ("rows", "layer"), pairs)
+    mine = back(mine, BLOCK_LAST)
     out_shape = [jax.ShapeDtypeStruct((STEPS,) + own.shape, jnp.float32)]
     (scores,) = small_call(assemble_kernel, out_shape, own, first, second)
     return finish(mine, other, scores)

time: 53 us -> 54.1 us (1.021)
  starting transfers between devices: 16.9 us -> 19.7 us
  waiting for transfers between devices: 23.2 us -> 21.6 us
    ppermute x3, starting transfers between devices: 3.82 us -> 7.97 us  [back(): return lax.ppermute(total, 'rows', tuple(enumerate(table)))]
    ppermute x1, starting transfers between devices: 3.33 us -> 0.06 us  [along_line(): three = lax.ppermute(one, 'rows', ROUND_ONE)]
    ppermute x1, waiting for transfers between devices: 3.33 us -> 1.03 us  [along_line(): other = lax.ppermute(other, ('rows', 'layer'), pairs)]
    ppermute x1, starting transfers between devices: 0.06 us -> 2.22 us  [along_line(): two = lax.ppermute(later, 'rows', ROUND_TWO)]
    ppermute x3, waiting for transfers between devices: 4.92 us -> 6.51 us  [back(): return lax.ppermute(total, 'rows', tuple(enumerate(table)))]
    ppermute x1, starting transfers between devices: 4.04 us -> 3.02 us  [along_line(): one = lax.ppermute(documents, 'rows', ROUND_ONE)]
    ppermute x1, waiting for transfers between devices: 4.39 us -> 3.62 us  [along_line(): two = lax.ppermute(later, 'rows', ROUND_TWO)]
    ppermute x1, starting transfers between devices: 2.29 us -> 2.89 us  [along_line(): other = lax.ppermute(other, ('rows', 'layer'), pairs)]
where the time goes in v11:
time: 54.1 us; the launch traced here: 53.9 us
  waiting for transfers between devices  21.6 us (40%)
  starting transfers between devices  19.7 us (36%)
  Pallas kernels  10.7 us (20%)
  local copies, waits for them, and re-layouts  1.74 us (3%)
    ppermute x3, starting transfers between devices, back(): return lax.ppermute(total, 'rows', tuple(enumerate(table)))  7.97 us
    ppermute x3, waiting for transfers between devices, back(): return lax.ppermute(total, 'rows', tuple(enumerate(table)))  6.51 us
    ppermute x5, waiting for transfers between devices, swap(): lax.ppermute(value, 'layer', [(lay, lay ^ distance) for lay in range(coun...  6.28 us
    pallas_call x1, Pallas kernels, prepare(): pl.pallas_call(prepare_kernel, out_shape=jax.ShapeDtypeStruct((rows, dims...  6.15 us
    ppermute x1, waiting for transfers between devices, along_line(): one = lax.ppermute(documents, 'rows', ROUND_ONE)  4.2 us
    ppermute x1, waiting for transfers between devices, along_line(): two = lax.ppermute(later, 'rows', ROUND_TWO)  3.62 us
    ppermute x5, starting transfers between devices, swap(): lax.ppermute(value, 'layer', [(lay, lay ^ distance) for lay in range(coun...  3.51 us
    pallas_call x5, Pallas kernels, scoring(): pl.pallas_call(kernel, out_shape=out_shape, in_specs=[vmem] * (3 + len(ex...  3.15 us
  transfers between devices with their start and end apart: 12, of which 10 were waited for; matrix products, arithmetic and copies ran while one was open for 0% of the time, Pallas kernels for 18%

profile of v11, /device:TPU:0, one launch (start us, length us, event | category | flops | bytes accessed | tf_op | source)
XLA Modules:
  0.0 53.9 jit_solution(13232285271836501177)
XLA Ops:
  0.0 0.0 copy-start.1
  0.0 0.0 copy-start.2
  0.0 3.0 %collective-permute-start = (bf16[128,2048]{1,0:T(8,128)(2,1)}, bf16[128,2048]{1,0:T(8,128)(2,1)S(1)}, u32[]{:S(2)}, u32[]{:S(2)}) collective-permute-start(bf16[128,2048]{1,0:T(8,128)(2,1)} %documents_ref), channel_id=1, source_target_pairs={{0,4},{4,8},{8,12},{12,0},{1,5},{5,9},{9,13},{13,1},{2,6},{6,10},{... | collective-permute-start | bytes 1572872 | tf_op jit(solution)/shard_map/ppermute | solution.py:265
  3.0 6.1 %shard_map.64.queries_ref = bf16[512,2048]{1,0:T(8,128)(2,1)} custom-call(s32[4]{0:T(128)} %offsets.1, bf16[512,2048]{1,0:T(8,128)(2,1)} %queries_hbm.1, bf16[4,512,512]{2,1,0:T(8,128)(2,1)} %bases_hbm.1, f32[4,512]{1,0:T(4,128)} %values_hbm.1), custom_call_target="tpu_custom_call" | custom-call | flops 2147483648 | bytes 6291456 | tf_op jit(solution)/shard_map/pallas_call | solution.py:52
  9.2 0.0 copy-done.1
  9.2 2.2 %collective-permute-start.2 = (bf16[128,2048]{1,0:T(8,128)(2,1)S(1)}, bf16[128,2048]{1,0:T(8,128)(2,1)S(1)}, u32[]{:S(2)}, u32[]{:S(2)}) collective-permute-start(bf16[128,2048]{1,0:T(8,128)(2,1)S(1)} %copy-done.1), channel_id=1, source_target_pairs={{0,12},{4,0},{8,4},{12,8},{1,13},{5,1},{9,5},{13,9},{2,14},{6,2},{... | collective-permute-start | bytes 1572872 | tf_op jit(solution)/shard_map/ppermute | solution.py:267
  11.4 0.0 copy-done.2
  11.4 0.1 copy.11.ids_ref
  11.6 0.0 copy-start
  11.6 1.6 %copy-done = bf16[512,2048]{1,0:T(8,128)(2,1)S(1)} copy-done((bf16[512,2048]{1,0:T(8,128)(2,1)S(1)}, bf16[512,2048]{1,0:T(8,128)(2,1)}, u32[]{:S(2)}) %copy-start) | copy-done | bytes 2097176
  13.2 0.8 %shard_map.65 = (f32[256,128]{1,0:T(8,128)S(1)}, f32[256,128]{1,0:T(8,128)S(1)}) custom-call(bf16[512,2048]{1,0:T(8,128)(2,1)S(1)} %copy-done, s32[512,1]{1,0:T(8,128)S(1)} %copy.11.ids_ref, bf16[128,2048]{1,0:T(8,128)(2,1)S(1)} %copy-done.1), custom_call_target="tpu_custom_call" | custom-call | flops 268435456 | bytes 2621440 | tf_op jit(solution)/shard_map/pallas_call | solution.py:81
  13.9 4.2 %collective-permute-done.documents_ref = bf16[128,2048]{1,0:T(8,128)(2,1)S(1)} collective-permute-done((bf16[128,2048]{1,0:T(8,128)(2,1)}, bf16[128,2048]{1,0:T(8,128)(2,1)S(1)}, u32[]{:S(2)}, u32[]{:S(2)}) %collective-permute-start) | collective-permute-done | bytes 524320 | tf_op jit(solution)/shard_map/ppermute | solution.py:265
  18.1 0.8 %shard_map.66 = (f32[256,256]{1,0:T(8,128)S(1)}, f32[256,256]{1,0:T(8,128)S(1)}) custom-call(bf16[512,2048]{1,0:T(8,128)(2,1)S(1)} %copy-done, s32[512,1]{1,0:T(8,128)S(1)} %copy.11.ids_ref, bf16[128,2048]{1,0:T(8,128)(2,1)S(1)} %collective-permute-done.documents_ref, f32[256,128]{1,0:T(8,128)S(1)} %get-tuple-element.34.refs_0_, ...), custom_call_target="tpu_custom_call" | custom-call | flops 268435456 | bytes 2621440 | tf_op jit(solution)/shard_map/pallas_call | solution.py:81
  18.9 0.1 collective-permute-start.3
  19.0 0.1 collective-permute-start.1
  19.0 1.5 %collective-permute-done.3.arrived_ref = f32[256,256]{1,0:T(8,128)S(1)} collective-permute-done((f32[256,256]{1,0:T(8,128)S(1)}, f32[256,256]{1,0:T(8,128)S(1)}, u32[]{:S(2)}, u32[]{:S(2)}) %collective-permute-start.3) | collective-permute-done | bytes 262176 | tf_op jit(solution)/shard_map/ppermute | solution.py:181
  20.5 1.7 %collective-permute-start.4 = (bf16[128,256]{1,0:T(8,128)(2,1)S(1)}, bf16[128,256]{1,0:T(8,128)(2,1)S(1)}, u32[]{:S(2)}, u32[]{:S(2)}) collective-permute-start(bf16[128,256]{1,0:T(8,128)(2,1)S(1)} %get-tuple-element.39), channel_id=1, source_target_pairs={{0,2},{1,3},{2,0},{3,1},{4,6},{5,7},{6,4},{7,5},{8,10},{9,11},{10,... | collective-permute-start | bytes 196616 | tf_op jit(solution)/shard_map/ppermute | solution.py:181
  22.3 2.6 %collective-permute-done.4.arrived_ref = bf16[128,256]{1,0:T(8,128)(2,1)S(1)} collective-permute-done((bf16[128,256]{1,0:T(8,128)(2,1)S(1)}, bf16[128,256]{1,0:T(8,128)(2,1)S(1)}, u32[]{:S(2)}, u32[]{:S(2)}) %collective-permute-start.4) | collective-permute-done | bytes 65568 | tf_op jit(solution)/shard_map/ppermute | solution.py:181
  24.9 3.6 %collective-permute-done.2.documents_ref = bf16[128,2048]{1,0:T(8,128)(2,1)S(1)} collective-permute-done((bf16[128,2048]{1,0:T(8,128)(2,1)S(1)}, bf16[128,2048]{1,0:T(8,128)(2,1)S(1)}, u32[]{:S(2)}, u32[]{:S(2)}) %collective-permute-start.2) | collective-permute-done | bytes 524320 | tf_op jit(solution)/shard_map/ppermute | solution.py:267
  28.5 0.8 %shard_map.69 = (f32[256,128]{1,0:T(8,128)S(1)}, f32[256,128]{1,0:T(8,128)S(1)}) custom-call(bf16[512,2048]{1,0:T(8,128)(2,1)S(1)} %copy-done, s32[512,1]{1,0:T(8,128)S(1)} %copy.11.ids_ref, bf16[128,2048]{1,0:T(8,128)(2,1)S(1)} %collective-permute-done.2.documents_ref), custom_call_target="tpu_custom_call" | custom-call | flops 268435456 | bytes 2621440 | tf_op jit(solution)/shard_map/pallas_call | solution.py:81
  29.3 0.1 collective-permute-start.6
  29.3 1.3 %collective-permute-done.6.arrived_ref = f32[256,128]{1,0:T(8,128)S(1)} collective-permute-done((f32[256,128]{1,0:T(8,128)S(1)}, f32[256,128]{1,0:T(8,128)S(1)}, u32[]{:S(2)}, u32[]{:S(2)}) %collective-permute-start.6) | collective-permute-done | bytes 131104 | tf_op jit(solution)/shard_map/ppermute | solution.py:181
  30.7 1.6 %collective-permute-start.7 = (bf16[128,128]{1,0:T(8,128)(2,1)S(1)}, bf16[128,128]{1,0:T(8,128)(2,1)S(1)}, u32[]{:S(2)}, u32[]{:S(2)}) collective-permute-start(bf16[128,128]{1,0:T(8,128)(2,1)S(1)} %get-tuple-element.46), channel_id=1, source_target_pairs={{0,2},{1,3},{2,0},{3,1},{4,6},{5,7},{6,4},{7,5},{8,10},{9,11},{10,... | collective-permute-start | bytes 98312 | tf_op jit(solution)/shard_map/ppermute | solution.py:181
  32.2 7.5 %collective-permute-start.5 = (bf16[128,128]{1,0:T(8,128)(2,1)S(1)}, bf16[128,128]{1,0:T(8,128)(2,1)S(1)}, u32[]{:S(2)}, u32[]{:S(2)}) collective-permute-start(bf16[128,128]{1,0:T(8,128)(2,1)S(1)} %get-tuple-element.41), channel_id=1, source_target_pairs={{0,12},{4,0},{8,4},{12,8},{1,13},{5,1},{9,5},{13,9},{2,14},{6,2},{... | collective-permute-start | bytes 98312 | tf_op jit(solution)/shard_map/ppermute | solution.py:263
  39.7 0.0 collective-permute-done.7.arrived_ref
  39.7 0.4 collective-permute-start.8
  40.2 3.2 %collective-permute-done.5.first_ref = bf16[128,128]{1,0:T(8,128)(2,1)S(1)} collective-permute-done((bf16[128,128]{1,0:T(8,128)(2,1)S(1)}, bf16[128,128]{1,0:T(8,128)(2,1)S(1)}, u32[]{:S(2)}, u32[]{:S(2)}) %collective-permute-start.5) | collective-permute-done | bytes 32800 | tf_op jit(solution)/shard_map/ppermute | solution.py:263
  43.3 0.0 collective-permute-done.1.documents_ref
  43.3 2.2 %collective-permute-done.8.second_ref = bf16[128,128]{1,0:T(8,128)(2,1)S(1)} collective-permute-done((bf16[128,128]{1,0:T(8,128)(2,1)S(1)}, bf16[128,128]{1,0:T(8,128)(2,1)S(1)}, u32[]{:S(2)}, u32[]{:S(2)}) %collective-permute-start.8) | collective-permute-done | bytes 32800 | tf_op jit(solution)/shard_map/ppermute | solution.py:263
  45.5 0.4 shard_map.73
  45.9 0.1 collective-permute-start.9
  46.0 0.4 shard_map.72.kept_ref
  46.4 0.9 %collective-permute-done.9.arrived_ref = f32[256,128]{1,0:T(8,128)S(1)} collective-permute-done((f32[256,128]{1,0:T(8,128)S(1)}, f32[256,128]{1,0:T(8,128)S(1)}, u32[]{:S(2)}, u32[]{:S(2)}) %collective-permute-start.9) | collective-permute-done | bytes 131104 | tf_op jit(solution)/shard_map/ppermute | solution.py:181
  47.3 0.1 collective-permute-start.10
  47.4 2.9 %collective-permute-start.11 = (bf16[128,128]{1,0:T(8,128)(2,1)S(1)}, bf16[128,128]{1,0:T(8,128)(2,1)S(1)}, u32[]{:S(2)}, u32[]{:S(2)}) collective-permute-start(bf16[128,128]{1,0:T(8,128)(2,1)S(1)} %get-tuple-element.49), channel_id=1, source_target_pairs={{0,10},{1,11},{2,8},{3,9},{4,14},{5,15},{6,12},{7,13},{8,2},{9,3},... | collective-permute-start | bytes 98312 | tf_op jit(solution)/shard_map/ppermute | solution.py:288
  50.3 0.7 %shard_map.75.scores_hbm = f32[4,128,128]{2,1,0:T(8,128)} custom-call(f32[128,128]{1,0:T(8,128)S(1)} %get-tuple-element.50.own_ref, bf16[128,128]{1,0:T(8,128)(2,1)S(1)} %collective-permute-done.5.first_ref, bf16[128,128]{1,0:T(8,128)(2,1)S(1)} %collective-permute-done.8.second_ref), custom_call_target="tpu_custom_call" | custom-call | tf_op jit(solution)/shard_map/pallas_call | solution.py:143
  51.0 1.2 %collective-permute-done.10.mine_ref = bf16[128,128]{1,0:T(8,128)(2,1)S(1)} collective-permute-done((bf16[128,128]{1,0:T(8,128)(2,1)S(1)}, bf16[128,128]{1,0:T(8,128)(2,1)S(1)}, u32[]{:S(2)}, u32[]{:S(2)}) %collective-permute-start.10) | collective-permute-done | bytes 32800 | tf_op jit(solution)/shard_map/ppermute | solution.py:263
  52.2 1.0 %collective-permute-done.11.other_ref = bf16[128,128]{1,0:T(8,128)(2,1)S(1)} collective-permute-done((bf16[128,128]{1,0:T(8,128)(2,1)S(1)}, bf16[128,128]{1,0:T(8,128)(2,1)S(1)}, u32[]{:S(2)}, u32[]{:S(2)}) %collective-permute-start.11) | collective-permute-done | bytes 32800 | tf_op jit(solution)/shard_map/ppermute | solution.py:288
  53.3 0.6 %shard_map.76 = f32[4,128,128]{2,1,0:T(8,128)} custom-call(bf16[128,128]{1,0:T(8,128)(2,1)S(1)} %collective-permute-done.10.mine_ref, bf16[128,128]{1,0:T(8,128)(2,1)S(1)} %collective-permute-done.11.other_ref, f32[4,128,128]{2,1,0:T(8,128)} %shard_map.75.scores_hbm), custom_call_target="tpu_custom_call", output_to_operand_aliasing={{}: (2, {})} | custom-call | tf_op jit(solution)/shard_map/pallas_call | solution.py:235
  (5 shorter events, 0.1 us)
Async XLA Ops:
  0.0 9.2 %copy-start.1 = (bf16[128,2048]{1,0:T(8,128)(2,1)S(1)}, bf16[128,2048]{1,0:T(8,128)(2,1)}, u32[]{:S(2)}) copy-start(bf16[128,2048]{1,0:T(8,128)(2,1)} %documents_ref) | copy-start | bytes 1572868
  0.0 11.4 %copy-start.2 = (s32[512]{0:T(512)S(1)}, s32[512]{0:T(512)}, u32[]{:S(2)}) copy-start(s32[512]{0:T(512)} %param.11) | copy-start | bytes 6148
  0.0 18.1 %collective-permute-start = (bf16[128,2048]{1,0:T(8,128)(2,1)}, bf16[128,2048]{1,0:T(8,128)(2,1)S(1)}, u32[]{:S(2)}, u32[]{:S(2)}) collective-permute-start(bf16[128,2048]{1,0:T(8,128)(2,1)} %documents_ref), channel_id=1, source_target_pairs={{0,4},{4,8},{8,12},{12,0},{1,5},{5,9},{9,13},{13,1},{2,6},{6,10},{... | collective-permute-start | bytes 1572872 | tf_op jit(solution)/shard_map/ppermute | solution.py:265
  9.2 19.3 %collective-permute-start.2 = (bf16[128,2048]{1,0:T(8,128)(2,1)S(1)}, bf16[128,2048]{1,0:T(8,128)(2,1)S(1)}, u32[]{:S(2)}, u32[]{:S(2)}) collective-permute-start(bf16[128,2048]{1,0:T(8,128)(2,1)S(1)} %copy-done.1), channel_id=1, source_target_pairs={{0,12},{4,0},{8,4},{12,8},{1,13},{5,1},{9,5},{13,9},{2,14},{6,2},{... | collective-permute-start | bytes 1572872 | tf_op jit(solution)/shard_map/ppermute | solution.py:267
  11.6 1.6 %copy-start = (bf16[512,2048]{1,0:T(8,128)(2,1)S(1)}, bf16[512,2048]{1,0:T(8,128)(2,1)}, u32[]{:S(2)}) copy-start(bf16[512,2048]{1,0:T(8,128)(2,1)} %shard_map.64.queries_ref) | copy-start | bytes 6291460
  18.9 1.6 %collective-permute-start.3 = (f32[256,256]{1,0:T(8,128)S(1)}, f32[256,256]{1,0:T(8,128)S(1)}, u32[]{:S(2)}, u32[]{:S(2)}) collective-permute-start(f32[256,256]{1,0:T(8,128)S(1)} %get-tuple-element.37), channel_id=1, source_target_pairs={{0,1},{1,0},{2,3},{3,2},{4,5},{5,4},{6,7},{7,6},{8,9},{9,8},{10,11... | collective-permute-start | bytes 786440 | tf_op jit(solution)/shard_map/ppermute | solution.py:181
  19.0 24.4 %collective-permute-start.1 = (bf16[128,2048]{1,0:T(8,128)(2,1)S(1)}, bf16[128,2048]{1,0:T(8,128)(2,1)S(1)}, u32[]{:S(2)}, u32[]{:S(2)}) collective-permute-start(bf16[128,2048]{1,0:T(8,128)(2,1)S(1)} %collective-permute-done.documents_ref), channel_id=1, source_target_pairs={{0,4},{4,8},{8,12},{12,0},{1,5},{5,9},{9,13},{13,1},{2,6},{6,10},{... | collective-permute-start | bytes 1572872 | tf_op jit(solution)/shard_map/ppermute | solution.py:270
  20.5 4.3 %collective-permute-start.4 = (bf16[128,256]{1,0:T(8,128)(2,1)S(1)}, bf16[128,256]{1,0:T(8,128)(2,1)S(1)}, u32[]{:S(2)}, u32[]{:S(2)}) collective-permute-start(bf16[128,256]{1,0:T(8,128)(2,1)S(1)} %get-tuple-element.39), channel_id=1, source_target_pairs={{0,2},{1,3},{2,0},{3,1},{4,6},{5,7},{6,4},{7,5},{8,10},{9,11},{10,... | collective-permute-start | bytes 196616 | tf_op jit(solution)/shard_map/ppermute | solution.py:181
  29.3 1.4 %collective-permute-start.6 = (f32[256,128]{1,0:T(8,128)S(1)}, f32[256,128]{1,0:T(8,128)S(1)}, u32[]{:S(2)}, u32[]{:S(2)}) collective-permute-start(f32[256,128]{1,0:T(8,128)S(1)} %get-tuple-element.44), channel_id=1, source_target_pairs={{0,1},{1,0},{2,3},{3,2},{4,5},{5,4},{6,7},{7,6},{8,9},{9,8},{10,11... | collective-permute-start | bytes 393224 | tf_op jit(solution)/shard_map/ppermute | solution.py:181
  30.7 9.0 %collective-permute-start.7 = (bf16[128,128]{1,0:T(8,128)(2,1)S(1)}, bf16[128,128]{1,0:T(8,128)(2,1)S(1)}, u32[]{:S(2)}, u32[]{:S(2)}) collective-permute-start(bf16[128,128]{1,0:T(8,128)(2,1)S(1)} %get-tuple-element.46), channel_id=1, source_target_pairs={{0,2},{1,3},{2,0},{3,1},{4,6},{5,7},{6,4},{7,5},{8,10},{9,11},{10,... | collective-permute-start | bytes 98312 | tf_op jit(solution)/shard_map/ppermute | solution.py:181
  32.2 11.1 %collective-permute-start.5 = (bf16[128,128]{1,0:T(8,128)(2,1)S(1)}, bf16[128,128]{1,0:T(8,128)(2,1)S(1)}, u32[]{:S(2)}, u32[]{:S(2)}) collective-permute-start(bf16[128,128]{1,0:T(8,128)(2,1)S(1)} %get-tuple-element.41), channel_id=1, source_target_pairs={{0,12},{4,0},{8,4},{12,8},{1,13},{5,1},{9,5},{13,9},{2,14},{6,2},{... | collective-permute-start | bytes 98312 | tf_op jit(solution)/shard_map/ppermute | solution.py:263
  39.7 5.8 %collective-permute-start.8 = (bf16[128,128]{1,0:T(8,128)(2,1)S(1)}, bf16[128,128]{1,0:T(8,128)(2,1)S(1)}, u32[]{:S(2)}, u32[]{:S(2)}) collective-permute-start(bf16[128,128]{1,0:T(8,128)(2,1)S(1)} %shard_map.71), channel_id=1, source_target_pairs={{0,4},{4,8},{8,12},{12,0},{1,5},{5,9},{9,13},{13,1},{2,6},{6,10},{... | collective-permute-start | bytes 98312 | tf_op jit(solution)/shard_map/ppermute | solution.py:263
  45.9 1.4 %collective-permute-start.9 = (f32[256,128]{1,0:T(8,128)S(1)}, f32[256,128]{1,0:T(8,128)S(1)}, u32[]{:S(2)}, u32[]{:S(2)}) collective-permute-start(f32[256,128]{1,0:T(8,128)S(1)} %shard_map.73), channel_id=1, source_target_pairs={{0,1},{1,0},{2,3},{3,2},{4,5},{5,4},{6,7},{7,6},{8,9},{9,8},{10,11... | collective-permute-start | bytes 393224 | tf_op jit(solution)/shard_map/ppermute | solution.py:181
  47.3 4.9 %collective-permute-start.10 = (bf16[128,128]{1,0:T(8,128)(2,1)S(1)}, bf16[128,128]{1,0:T(8,128)(2,1)S(1)}, u32[]{:S(2)}, u32[]{:S(2)}) collective-permute-start(bf16[128,128]{1,0:T(8,128)(2,1)S(1)} %get-tuple-element.48), channel_id=1, source_target_pairs={{0,8},{4,12},{8,0},{12,4},{1,9},{5,13},{9,1},{13,5},{2,10},{6,14},... | collective-permute-start | bytes 98312 | tf_op jit(solution)/shard_map/ppermute | solution.py:263
  47.4 5.8 %collective-permute-start.11 = (bf16[128,128]{1,0:T(8,128)(2,1)S(1)}, bf16[128,128]{1,0:T(8,128)(2,1)S(1)}, u32[]{:S(2)}, u32[]{:S(2)}) collective-permute-start(bf16[128,128]{1,0:T(8,128)(2,1)S(1)} %get-tuple-element.49), channel_id=1, source_target_pairs={{0,10},{1,11},{2,8},{3,9},{4,14},{5,15},{6,12},{7,13},{8,2},{9,3},... | collective-permute-start | bytes 98312 | tf_op jit(solution)/shard_map/ppermute | solution.py:288

commit v12 on v10

--- a/solution.py
+++ b/solution.py
@@ -263,9 +263,8 @@
         return lax.ppermute(total, "rows", tuple(enumerate(table)))
 
     one = lax.ppermute(documents, "rows", ROUND_ONE)
-    later, conditioned = lax.optimization_barrier((documents, conditioned))
-    two = lax.ppermute(later, "rows", ROUND_TWO)
-    own = halves(later, lambda row: row)
+    two = lax.ppermute(documents, "rows", ROUND_TWO)
+    own = halves(documents, lambda row: row)
     one, own = lax.optimization_barrier((one, own))
     three = lax.ppermute(one, "rows", ROUND_ONE)
 
@@ -279,7 +278,6 @@
     arrived = swap(one_half(three, pick(BLOCK_LAST), False), 1)
     kept = one_half(three, pick(BLOCK_LAST), True)
     mine, other = core_sum(kept, arrived, jnp.bfloat16)
-    mine = back(mine, BLOCK_LAST)
     shares = lax.axis_size("layer")
     pairs = [
         (row * shares + lay, BLOCK_LAST[row] * shares + (lay ^ 2))
@@ -287,6 +285,7 @@
         for lay in range(shares)
     ]
     other = lax.ppermute(other, ("rows", "layer"), pairs)
+    mine = back(mine, BLOCK_LAST)
     out_shape = [jax.ShapeDtypeStruct((STEPS,) + own.shape, jnp.float32)]
     (scores,) = small_call(assemble_kernel, out_shape, own, first, second)
     return finish(mine, other, scores)

time: 53 us -> 53 us (level)
  waiting for transfers between devices: 23.2 us -> 22.5 us
  local copies, waits for them, and re-layouts: 1.74 us -> 2.41 us
    ppermute x1, waiting for transfers between devices: 3.93 us -> 3.18 us  [along_line(): one = lax.ppermute(documents, 'rows', ROUND_ONE)]
    broadcast_in_dim x1, local copies, waits for them, and re-layouts: 0.14 us -> 0.82 us  [local(): return plan(train_grads, conditioned, query_doc_ids[:, None])]
    unnamed x6 -> x4, local copies, waits for them, and re-layouts: 1.6 us -> 1.59 us
  transfers between devices with their start and end apart: 12 -> 12, of which waited for: 10 -> 10; matrix products, arithmetic and copies ran while one was open for 0% -> 2% of each run, Pallas kernels for 18% -> 19%
where the time goes in v12:
time: 53 us; the launch traced here: 52.8 us
  waiting for transfers between devices  22.5 us (42%)
  starting transfers between devices  16.9 us (32%)
  Pallas kernels  10.9 us (21%)
  local copies, waits for them, and re-layouts  2.41 us (5%)
    ppermute x5, waiting for transfers between devices, swap(): lax.ppermute(value, 'layer', [(lay, lay ^ distance) for lay in range(coun...  6.67 us
    pallas_call x1, Pallas kernels, prepare(): pl.pallas_call(prepare_kernel, out_shape=jax.ShapeDtypeStruct((rows, dims...  6.29 us
    ppermute x3, waiting for transfers between devices, back(): return lax.ppermute(total, 'rows', tuple(enumerate(table)))  4.92 us
    ppermute x1, waiting for transfers between devices, along_line(): two = lax.ppermute(documents, 'rows', ROUND_TWO)  4.38 us
    ppermute x1, starting transfers between devices, along_line(): one = lax.ppermute(documents, 'rows', ROUND_ONE)  4.04 us
    ppermute x3, starting transfers between devices, back(): return lax.ppermute(total, 'rows', tuple(enumerate(table)))  3.83 us
    ppermute x5, starting transfers between devices, swap(): lax.ppermute(value, 'layer', [(lay, lay ^ distance) for lay in range(coun...  3.41 us
    ppermute x1, waiting for transfers between devices, along_line(): other = lax.ppermute(other, ('rows', 'layer'), pairs)  3.33 us
  transfers between devices with their start and end apart: 12, of which 10 were waited for; matrix products, arithmetic and copies ran while one was open for 2% of the time, Pallas kernels for 19%

profile of v12, /device:TPU:0, one launch (start us, length us, event | category | flops | bytes accessed | tf_op | source)
XLA Modules:
  0.0 52.8 jit_solution(8771688044730216073)
XLA Ops:
  0.0 4.0 %collective-permute-start = (bf16[128,2048]{1,0:T(8,128)(2,1)}, bf16[128,2048]{1,0:T(8,128)(2,1)S(1)}, u32[]{:S(2)}, u32[]{:S(2)}) collective-permute-start(bf16[128,2048]{1,0:T(8,128)(2,1)} %documents_ref.1), channel_id=1, source_target_pairs={{0,8},{8,12},{12,4},{4,0},{1,9},{9,13},{13,5},{5,1},{2,10},{10,14}... | collective-permute-start | bytes 1572872 | tf_op jit(solution)/shard_map/ppermute | solution.py:265
  4.0 0.0 collective-permute-start.2
  4.0 0.8 %copy.11.ids_ref = s32[512,1]{1,0:T(8,128)S(1)} copy(s32[512,1]{0,1:T(1,128)} %bitcast.1) | data formatting | bytes 4096 | tf_op jit(solution)/shard_map/broadcast_in_dim | solution.py:318
  4.9 0.0 copy-start.1
  4.9 6.3 %shard_map.64.queries_ref = bf16[512,2048]{1,0:T(8,128)(2,1)} custom-call(s32[4]{0:T(128)} %offsets.1, bf16[512,2048]{1,0:T(8,128)(2,1)} %queries_hbm.1, bf16[4,512,512]{2,1,0:T(8,128)(2,1)} %bases_hbm.1, f32[4,512]{1,0:T(4,128)} %values_hbm.1), custom_call_target="tpu_custom_call" | custom-call | flops 2147483648 | bytes 6291456 | tf_op jit(solution)/shard_map/pallas_call | solution.py:52
  11.2 0.0 copy-done.1
  11.2 0.0 copy-start
  11.2 1.6 %copy-done = bf16[512,2048]{1,0:T(8,128)(2,1)S(1)} copy-done((bf16[512,2048]{1,0:T(8,128)(2,1)S(1)}, bf16[512,2048]{1,0:T(8,128)(2,1)}, u32[]{:S(2)}) %copy-start) | copy-done | bytes 2097176
  12.8 0.8 %shard_map.65 = (f32[256,128]{1,0:T(8,128)S(1)}, f32[256,128]{1,0:T(8,128)S(1)}) custom-call(bf16[512,2048]{1,0:T(8,128)(2,1)S(1)} %copy-done, s32[512,1]{1,0:T(8,128)S(1)} %copy.11.ids_ref, bf16[128,2048]{1,0:T(8,128)(2,1)S(1)} %copy-done.1), custom_call_target="tpu_custom_call" | custom-call | flops 268435456 | bytes 2621440 | tf_op jit(solution)/shard_map/pallas_call | solution.py:81
  13.5 3.2 %collective-permute-done.documents_ref = bf16[128,2048]{1,0:T(8,128)(2,1)S(1)} collective-permute-done((bf16[128,2048]{1,0:T(8,128)(2,1)}, bf16[128,2048]{1,0:T(8,128)(2,1)S(1)}, u32[]{:S(2)}, u32[]{:S(2)}) %collective-permute-start) | collective-permute-done | bytes 524320 | tf_op jit(solution)/shard_map/ppermute | solution.py:265
  16.7 0.8 %shard_map.66 = (f32[256,256]{1,0:T(8,128)S(1)}, f32[256,256]{1,0:T(8,128)S(1)}) custom-call(bf16[512,2048]{1,0:T(8,128)(2,1)S(1)} %copy-done, s32[512,1]{1,0:T(8,128)S(1)} %copy.11.ids_ref, bf16[128,2048]{1,0:T(8,128)(2,1)S(1)} %collective-permute-done.documents_ref, f32[256,128]{1,0:T(8,128)S(1)} %get-tuple-element.30.refs_0_, ...), custom_call_target="tpu_custom_call" | custom-call | flops 268435456 | bytes 2621440 | tf_op jit(solution)/shard_map/pallas_call | solution.py:81
  17.5 0.1 collective-permute-start.3
  17.6 3.3 %collective-permute-start.1 = (bf16[128,2048]{1,0:T(8,128)(2,1)S(1)}, bf16[128,2048]{1,0:T(8,128)(2,1)S(1)}, u32[]{:S(2)}, u32[]{:S(2)}) collective-permute-start(bf16[128,2048]{1,0:T(8,128)(2,1)S(1)} %collective-permute-done.documents_ref), channel_id=1, source_target_pairs={{0,8},{8,12},{12,4},{4,0},{1,9},{9,13},{13,5},{5,1},{2,10},{10,14}... | collective-permute-start | bytes 1572872 | tf_op jit(solution)/shard_map/ppermute | solution.py:269
  20.9 0.0 collective-permute-done.3.arrived_ref
  20.9 1.6 %collective-permute-start.4 = (bf16[128,256]{1,0:T(8,128)(2,1)S(1)}, bf16[128,256]{1,0:T(8,128)(2,1)S(1)}, u32[]{:S(2)}, u32[]{:S(2)}) collective-permute-start(bf16[128,256]{1,0:T(8,128)(2,1)S(1)} %get-tuple-element.35), channel_id=1, source_target_pairs={{0,2},{1,3},{2,0},{3,1},{4,6},{5,7},{6,4},{7,5},{8,10},{9,11},{10,... | collective-permute-start | bytes 196616 | tf_op jit(solution)/shard_map/ppermute | solution.py:181
  22.5 2.8 %collective-permute-done.4.arrived_ref = bf16[128,256]{1,0:T(8,128)(2,1)S(1)} collective-permute-done((bf16[128,256]{1,0:T(8,128)(2,1)S(1)}, bf16[128,256]{1,0:T(8,128)(2,1)S(1)}, u32[]{:S(2)}, u32[]{:S(2)}) %collective-permute-start.4) | collective-permute-done | bytes 65568 | tf_op jit(solution)/shard_map/ppermute | solution.py:181
  25.3 4.4 %collective-permute-done.2.documents_ref = bf16[128,2048]{1,0:T(8,128)(2,1)S(1)} collective-permute-done((bf16[128,2048]{1,0:T(8,128)(2,1)}, bf16[128,2048]{1,0:T(8,128)(2,1)S(1)}, u32[]{:S(2)}, u32[]{:S(2)}) %collective-permute-start.2) | collective-permute-done | bytes 524320 | tf_op jit(solution)/shard_map/ppermute | solution.py:266
  29.7 0.8 %shard_map.69 = (f32[256,128]{1,0:T(8,128)S(1)}, f32[256,128]{1,0:T(8,128)S(1)}) custom-call(bf16[512,2048]{1,0:T(8,128)(2,1)S(1)} %copy-done, s32[512,1]{1,0:T(8,128)S(1)} %copy.11.ids_ref, bf16[128,2048]{1,0:T(8,128)(2,1)S(1)} %collective-permute-done.2.documents_ref), custom_call_target="tpu_custom_call" | custom-call | flops 268435456 | bytes 2621440 | tf_op jit(solution)/shard_map/pallas_call | solution.py:81
  30.4 0.1 collective-permute-start.6
  30.5 1.3 %collective-permute-done.6.arrived_ref = f32[256,128]{1,0:T(8,128)S(1)} collective-permute-done((f32[256,128]{1,0:T(8,128)S(1)}, f32[256,128]{1,0:T(8,128)S(1)}, u32[]{:S(2)}, u32[]{:S(2)}) %collective-permute-start.6) | collective-permute-done | bytes 131104 | tf_op jit(solution)/shard_map/ppermute | solution.py:181
  31.9 1.6 %collective-permute-start.7 = (bf16[128,128]{1,0:T(8,128)(2,1)S(1)}, bf16[128,128]{1,0:T(8,128)(2,1)S(1)}, u32[]{:S(2)}, u32[]{:S(2)}) collective-permute-start(bf16[128,128]{1,0:T(8,128)(2,1)S(1)} %get-tuple-element.42), channel_id=1, source_target_pairs={{0,2},{1,3},{2,0},{3,1},{4,6},{5,7},{6,4},{7,5},{8,10},{9,11},{10,... | collective-permute-start | bytes 98312 | tf_op jit(solution)/shard_map/ppermute | solution.py:181
  33.4 0.7 %collective-permute-start.5 = (bf16[128,128]{1,0:T(8,128)(2,1)S(1)}, bf16[128,128]{1,0:T(8,128)(2,1)S(1)}, u32[]{:S(2)}, u32[]{:S(2)}) collective-permute-start(bf16[128,128]{1,0:T(8,128)(2,1)S(1)} %get-tuple-element.37), channel_id=1, source_target_pairs={{0,4},{4,12},{8,0},{12,8},{1,5},{5,13},{9,1},{13,9},{2,6},{6,14},{... | collective-permute-start | bytes 98312 | tf_op jit(solution)/shard_map/ppermute | solution.py:263
  34.1 1.7 %collective-permute-done.7.arrived_ref = bf16[128,128]{1,0:T(8,128)(2,1)S(1)} collective-permute-done((bf16[128,128]{1,0:T(8,128)(2,1)S(1)}, bf16[128,128]{1,0:T(8,128)(2,1)S(1)}, u32[]{:S(2)}, u32[]{:S(2)}) %collective-permute-start.7) | collective-permute-done | bytes 32800 | tf_op jit(solution)/shard_map/ppermute | solution.py:181
  35.8 0.6 %collective-permute-start.8 = (bf16[128,128]{1,0:T(8,128)(2,1)S(1)}, bf16[128,128]{1,0:T(8,128)(2,1)S(1)}, u32[]{:S(2)}, u32[]{:S(2)}) collective-permute-start(bf16[128,128]{1,0:T(8,128)(2,1)S(1)} %shard_map.71), channel_id=1, source_target_pairs={{0,8},{4,0},{8,12},{12,4},{1,9},{5,1},{9,13},{13,5},{2,10},{6,2},{... | collective-permute-start | bytes 98312 | tf_op jit(solution)/shard_map/ppermute | solution.py:263
  36.5 4.4 %collective-permute-done.5.first_ref = bf16[128,128]{1,0:T(8,128)(2,1)S(1)} collective-permute-done((bf16[128,128]{1,0:T(8,128)(2,1)S(1)}, bf16[128,128]{1,0:T(8,128)(2,1)S(1)}, u32[]{:S(2)}, u32[]{:S(2)}) %collective-permute-start.5) | collective-permute-done | bytes 32800 | tf_op jit(solution)/shard_map/ppermute | solution.py:263
  40.9 0.2 collective-permute-done.8.second_ref
  41.1 0.0 collective-permute-done.1.documents_ref
  41.1 0.4 shard_map.73
  41.6 0.2 collective-permute-start.9
  41.7 0.4 shard_map.72.kept_ref
  42.2 0.8 %collective-permute-done.9.arrived_ref = f32[256,128]{1,0:T(8,128)S(1)} collective-permute-done((f32[256,128]{1,0:T(8,128)S(1)}, f32[256,128]{1,0:T(8,128)S(1)}, u32[]{:S(2)}, u32[]{:S(2)}) %collective-permute-start.9) | collective-permute-done | bytes 131104 | tf_op jit(solution)/shard_map/ppermute | solution.py:181
  43.0 2.5 %collective-permute-start.10 = (bf16[128,128]{1,0:T(8,128)(2,1)S(1)}, bf16[128,128]{1,0:T(8,128)(2,1)S(1)}, u32[]{:S(2)}, u32[]{:S(2)}) collective-permute-start(bf16[128,128]{1,0:T(8,128)(2,1)S(1)} %get-tuple-element.44), channel_id=1, source_target_pairs={{0,12},{4,8},{8,4},{12,0},{1,13},{5,9},{9,5},{13,1},{2,14},{6,10},... | collective-permute-start | bytes 98312 | tf_op jit(solution)/shard_map/ppermute | solution.py:263
  45.5 2.3 %collective-permute-start.11 = (bf16[128,128]{1,0:T(8,128)(2,1)S(1)}, bf16[128,128]{1,0:T(8,128)(2,1)S(1)}, u32[]{:S(2)}, u32[]{:S(2)}) collective-permute-start(bf16[128,128]{1,0:T(8,128)(2,1)S(1)} %get-tuple-element.45), channel_id=1, source_target_pairs={{0,14},{1,15},{2,12},{3,13},{4,10},{5,11},{6,8},{7,9},{8,6},{9,7},... | collective-permute-start | bytes 98312 | tf_op jit(solution)/shard_map/ppermute | solution.py:287
  47.8 0.7 %shard_map.75.scores_hbm = f32[4,128,128]{2,1,0:T(8,128)} custom-call(f32[128,128]{1,0:T(8,128)S(1)} %get-tuple-element.46.own_ref, bf16[128,128]{1,0:T(8,128)(2,1)S(1)} %collective-permute-done.5.first_ref, bf16[128,128]{1,0:T(8,128)(2,1)S(1)} %collective-permute-done.8.second_ref), custom_call_target="tpu_custom_call" | custom-call | tf_op jit(solution)/shard_map/pallas_call | solution.py:143
  48.5 0.3 collective-permute-done.10.mine_ref
  48.8 3.3 %collective-permute-done.11.other_ref = bf16[128,128]{1,0:T(8,128)(2,1)S(1)} collective-permute-done((bf16[128,128]{1,0:T(8,128)(2,1)S(1)}, bf16[128,128]{1,0:T(8,128)(2,1)S(1)}, u32[]{:S(2)}, u32[]{:S(2)}) %collective-permute-start.11) | collective-permute-done | bytes 32800 | tf_op jit(solution)/shard_map/ppermute | solution.py:287
  52.1 0.6 %shard_map.76 = f32[4,128,128]{2,1,0:T(8,128)} custom-call(bf16[128,128]{1,0:T(8,128)(2,1)S(1)} %collective-permute-done.10.mine_ref, bf16[128,128]{1,0:T(8,128)(2,1)S(1)} %collective-permute-done.11.other_ref, f32[4,128,128]{2,1,0:T(8,128)} %shard_map.75.scores_hbm), custom_call_target="tpu_custom_call", output_to_operand_aliasing={{}: (2, {})} | custom-call | tf_op jit(solution)/shard_map/pallas_call | solution.py:235
  (5 shorter events, 0.1 us)
Async XLA Ops:
  0.0 16.7 %collective-permute-start = (bf16[128,2048]{1,0:T(8,128)(2,1)}, bf16[128,2048]{1,0:T(8,128)(2,1)S(1)}, u32[]{:S(2)}, u32[]{:S(2)}) collective-permute-start(bf16[128,2048]{1,0:T(8,128)(2,1)} %documents_ref.1), channel_id=1, source_target_pairs={{0,8},{8,12},{12,4},{4,0},{1,9},{9,13},{13,5},{5,1},{2,10},{10,14}... | collective-permute-start | bytes 1572872 | tf_op jit(solution)/shard_map/ppermute | solution.py:265
  4.0 25.6 %collective-permute-start.2 = (bf16[128,2048]{1,0:T(8,128)(2,1)}, bf16[128,2048]{1,0:T(8,128)(2,1)S(1)}, u32[]{:S(2)}, u32[]{:S(2)}) collective-permute-start(bf16[128,2048]{1,0:T(8,128)(2,1)} %documents_ref.1), channel_id=1, source_target_pairs={{0,4},{4,12},{12,8},{8,0},{1,5},{5,13},{13,9},{9,1},{2,6},{6,14},{... | collective-permute-start | bytes 1572872 | tf_op jit(solution)/shard_map/ppermute | solution.py:266
  4.9 6.3 %copy-start.1 = (bf16[128,2048]{1,0:T(8,128)(2,1)S(1)}, bf16[128,2048]{1,0:T(8,128)(2,1)}, u32[]{:S(2)}) copy-start(bf16[128,2048]{1,0:T(8,128)(2,1)} %documents_ref.1) | copy-start | bytes 1572868
  11.2 1.6 %copy-start = (bf16[512,2048]{1,0:T(8,128)(2,1)S(1)}, bf16[512,2048]{1,0:T(8,128)(2,1)}, u32[]{:S(2)}) copy-start(bf16[512,2048]{1,0:T(8,128)(2,1)} %shard_map.64.queries_ref) | copy-start | bytes 6291460
  17.5 3.4 %collective-permute-start.3 = (f32[256,256]{1,0:T(8,128)S(1)}, f32[256,256]{1,0:T(8,128)S(1)}, u32[]{:S(2)}, u32[]{:S(2)}) collective-permute-start(f32[256,256]{1,0:T(8,128)S(1)} %get-tuple-element.33), channel_id=1, source_target_pairs={{0,1},{1,0},{2,3},{3,2},{4,5},{5,4},{6,7},{7,6},{8,9},{9,8},{10,11... | collective-permute-start | bytes 786440 | tf_op jit(solution)/shard_map/ppermute | solution.py:181
  17.6 23.6 %collective-permute-start.1 = (bf16[128,2048]{1,0:T(8,128)(2,1)S(1)}, bf16[128,2048]{1,0:T(8,128)(2,1)S(1)}, u32[]{:S(2)}, u32[]{:S(2)}) collective-permute-start(bf16[128,2048]{1,0:T(8,128)(2,1)S(1)} %collective-permute-done.documents_ref), channel_id=1, source_target_pairs={{0,8},{8,12},{12,4},{4,0},{1,9},{9,13},{13,5},{5,1},{2,10},{10,14}... | collective-permute-start | bytes 1572872 | tf_op jit(solution)/shard_map/ppermute | solution.py:269
  20.9 4.3 %collective-permute-start.4 = (bf16[128,256]{1,0:T(8,128)(2,1)S(1)}, bf16[128,256]{1,0:T(8,128)(2,1)S(1)}, u32[]{:S(2)}, u32[]{:S(2)}) collective-permute-start(bf16[128,256]{1,0:T(8,128)(2,1)S(1)} %get-tuple-element.35), channel_id=1, source_target_pairs={{0,2},{1,3},{2,0},{3,1},{4,6},{5,7},{6,4},{7,5},{8,10},{9,11},{10,... | collective-permute-start | bytes 196616 | tf_op jit(solution)/shard_map/ppermute | solution.py:181
  30.4 1.4 %collective-permute-start.6 = (f32[256,128]{1,0:T(8,128)S(1)}, f32[256,128]{1,0:T(8,128)S(1)}, u32[]{:S(2)}, u32[]{:S(2)}) collective-permute-start(f32[256,128]{1,0:T(8,128)S(1)} %get-tuple-element.40), channel_id=1, source_target_pairs={{0,1},{1,0},{2,3},{3,2},{4,5},{5,4},{6,7},{7,6},{8,9},{9,8},{10,11... | collective-permute-start | bytes 393224 | tf_op jit(solution)/shard_map/ppermute | solution.py:181
  31.9 4.0 %collective-permute-start.7 = (bf16[128,128]{1,0:T(8,128)(2,1)S(1)}, bf16[128,128]{1,0:T(8,128)(2,1)S(1)}, u32[]{:S(2)}, u32[]{:S(2)}) collective-permute-start(bf16[128,128]{1,0:T(8,128)(2,1)S(1)} %get-tuple-element.42), channel_id=1, source_target_pairs={{0,2},{1,3},{2,0},{3,1},{4,6},{5,7},{6,4},{7,5},{8,10},{9,11},{10,... | collective-permute-start | bytes 98312 | tf_op jit(solution)/shard_map/ppermute | solution.py:181
  33.4 7.5 %collective-permute-start.5 = (bf16[128,128]{1,0:T(8,128)(2,1)S(1)}, bf16[128,128]{1,0:T(8,128)(2,1)S(1)}, u32[]{:S(2)}, u32[]{:S(2)}) collective-permute-start(bf16[128,128]{1,0:T(8,128)(2,1)S(1)} %get-tuple-element.37), channel_id=1, source_target_pairs={{0,4},{4,12},{8,0},{12,8},{1,5},{5,13},{9,1},{13,9},{2,6},{6,14},{... | collective-permute-start | bytes 98312 | tf_op jit(solution)/shard_map/ppermute | solution.py:263
  35.8 5.3 %collective-permute-start.8 = (bf16[128,128]{1,0:T(8,128)(2,1)S(1)}, bf16[128,128]{1,0:T(8,128)(2,1)S(1)}, u32[]{:S(2)}, u32[]{:S(2)}) collective-permute-start(bf16[128,128]{1,0:T(8,128)(2,1)S(1)} %shard_map.71), channel_id=1, source_target_pairs={{0,8},{4,0},{8,12},{12,4},{1,9},{5,1},{9,13},{13,5},{2,10},{6,2},{... | collective-permute-start | bytes 98312 | tf_op jit(solution)/shard_map/ppermute | solution.py:263
  41.6 1.4 %collective-permute-start.9 = (f32[256,128]{1,0:T(8,128)S(1)}, f32[256,128]{1,0:T(8,128)S(1)}, u32[]{:S(2)}, u32[]{:S(2)}) collective-permute-start(f32[256,128]{1,0:T(8,128)S(1)} %shard_map.73), channel_id=1, source_target_pairs={{0,1},{1,0},{2,3},{3,2},{4,5},{5,4},{6,7},{7,6},{8,9},{9,8},{10,11... | collective-permute-start | bytes 393224 | tf_op jit(solution)/shard_map/ppermute | solution.py:181
  43.0 5.8 %collective-permute-start.10 = (bf16[128,128]{1,0:T(8,128)(2,1)S(1)}, bf16[128,128]{1,0:T(8,128)(2,1)S(1)}, u32[]{:S(2)}, u32[]{:S(2)}) collective-permute-start(bf16[128,128]{1,0:T(8,128)(2,1)S(1)} %get-tuple-element.44), channel_id=1, source_target_pairs={{0,12},{4,8},{8,4},{12,0},{1,13},{5,9},{9,5},{13,1},{2,14},{6,10},... | collective-permute-start | bytes 98312 | tf_op jit(solution)/shard_map/ppermute | solution.py:263
  45.5 6.6 %collective-permute-start.11 = (bf16[128,128]{1,0:T(8,128)(2,1)S(1)}, bf16[128,128]{1,0:T(8,128)(2,1)S(1)}, u32[]{:S(2)}, u32[]{:S(2)}) collective-permute-start(bf16[128,128]{1,0:T(8,128)(2,1)S(1)} %get-tuple-element.45), channel_id=1, source_target_pairs={{0,14},{1,15},{2,12},{3,13},{4,10},{5,11},{6,8},{7,9},{8,6},{9,7},... | collective-permute-start | bytes 98312 | tf_op jit(solution)/shard_map/ppermute | solution.py:287

commit v13 on v10

--- a/solution.py
+++ b/solution.py
@@ -221,26 +221,41 @@
         out_ref[step_of(table)(row_index())] = ref[...].astype(jnp.float32)
 
 
-def finish_kernel(mine_ref, other_ref, scores_hbm, out_hbm, total, copied):
+def own_side():
+    row = row_index()
+    return jnp.where(row < pick(BLOCK_LAST)(row), 0, 1)
+
+
+def pair_sum_kernel(kept_ref, arrived_ref, out_ref):
+    side = own_side()
+    rows = out_ref.shape[2]
+    out_ref[side] = jnp.zeros(out_ref.shape[1:], out_ref.dtype)
+    for chip in range(2):
+        share = slice(chip * rows, (chip + 1) * rows)
+        out_ref[1 - side, chip] = (kept_ref[share, :] + arrived_ref[share, :]).astype(out_ref.dtype)
+
+
+def finish_kernel(pair_ref, scores_hbm, out_hbm, total, copied):
     del scores_hbm
-    total[...] = total_of([mine_ref, other_ref])
+    side = 1 - own_side()
+    total[...] = total_of([pair_ref.at[side, chip] for chip in range(2)])
     copy = pltpu.make_async_copy(total, out_hbm.at[step_of(BLOCK_LAST)(row_index())], copied)
     copy.start()
     copy.wait()
 
 
-def finish(mine, other, scores):
+def finish(pair, scores):
     hbm = pl.BlockSpec(memory_space=pltpu.HBM)
     vmem = pl.BlockSpec(memory_space=pltpu.VMEM)
     return pl.pallas_call(
         finish_kernel,
         out_shape=jax.ShapeDtypeStruct(scores.shape, scores.dtype),
-        in_specs=[vmem, vmem, hbm],
+        in_specs=[vmem, hbm],
         out_specs=hbm,
-        scratch_shapes=[pltpu.VMEM(mine.shape, jnp.float32), pltpu.SemaphoreType.DMA],
-        input_output_aliases={2: 0},
+        scratch_shapes=[pltpu.VMEM(pair.shape[2:], jnp.float32), pltpu.SemaphoreType.DMA],
+        input_output_aliases={1: 0},
         compiler_params=pltpu.CompilerParams(vmem_limit_bytes=4 * MIB),
-    )(mine, other, scores)
+    )(pair, scores)
 
 
 def along_line(documents, conditioned, query_ids):
@@ -278,18 +293,19 @@
 
     arrived = swap(one_half(three, pick(BLOCK_LAST), False), 1)
     kept = one_half(three, pick(BLOCK_LAST), True)
-    mine, other = core_sum(kept, arrived, jnp.bfloat16)
-    mine = back(mine, BLOCK_LAST)
+    pair_shape = (2, 2) + own.shape
+    (pair,) = small_call(pair_sum_kernel, [jax.ShapeDtypeStruct(pair_shape, jnp.bfloat16)], kept, arrived)
     shares = lax.axis_size("layer")
-    pairs = [
-        (row * shares + lay, BLOCK_LAST[row] * shares + (lay ^ 2))
-        for row in range(len(BLOCK_LAST))
-        for lay in range(shares)
+    groups = [
+        [row * shares + 2 * chip + core for row in (low, BLOCK_LAST[low]) for chip in range(2)]
+        for low in range(STEPS // 2)
+        for core in range(2)
     ]
-    other = lax.ppermute(other, ("rows", "layer"), pairs)
+    blocks = pair.reshape((4,) + own.shape)
+    blocks = lax.all_to_all(blocks, ("rows", "layer"), 0, 0, axis_index_groups=groups, tiled=True)
     out_shape = [jax.ShapeDtypeStruct((STEPS,) + own.shape, jnp.float32)]
     (scores,) = small_call(assemble_kernel, out_shape, own, first, second)
-    return finish(mine, other, scores)
+    return finish(blocks.reshape(pair_shape), scores)
 
 
 def around_ring(documents, conditioned, query_ids):

time: 53 us -> 56 us (1.057)
  waiting for transfers between devices: 23.2 us -> 25.7 us
  Pallas kernels: 10.7 us -> 11.4 us
    all_to_all x0 -> x1, waiting for transfers between devices: none -> 6.1 us  [along_line(): lax.all_to_all(blocks, ('rows', 'layer'), 0, 0, axis_index_groups=groups,...]
    all_to_all x0 -> x1, starting transfers between devices: none -> 4.66 us  [along_line(): lax.all_to_all(blocks, ('rows', 'layer'), 0, 0, axis_index_groups=groups,...]
    ppermute x1 -> x0, waiting for transfers between devices: 3.33 us -> none  [along_line(): other = lax.ppermute(other, ('rows', 'layer'), pairs)]
    ppermute x3 -> x2, starting transfers between devices: 3.82 us -> 1.29 us  [back(): return lax.ppermute(total, 'rows', tuple(enumerate(table)))]
    ppermute x1 -> x0, starting transfers between devices: 2.29 us -> none  [along_line(): other = lax.ppermute(other, ('rows', 'layer'), pairs)]
    pallas_call x6, Pallas kernels: 0.8 us -> 1.46 us  [small_call(): pl.pallas_call(kernel, out_shape=out_shape, in_specs=[vmem] * len(args),...]
    ppermute x3 -> x2, waiting for transfers between devices: 4.92 us -> 4.65 us  [back(): return lax.ppermute(total, 'rows', tuple(enumerate(table)))]
  transfers between devices with their start and end apart: 12 -> 11, of which waited for: 10 -> 9; matrix products, arithmetic and copies ran while one was open for 0% -> 0% of each run, Pallas kernels for 18% -> 17%
where the time goes in v13:
time: 56 us; the launch traced here: 55.8 us
  waiting for transfers between devices  25.7 us (46%)
  starting transfers between devices  16.8 us (30%)
  Pallas kernels  11.4 us (20%)
  local copies, waits for them, and re-layouts  1.74 us (3%)
    ppermute x5, waiting for transfers between devices, swap(): lax.ppermute(value, 'layer', [(lay, lay ^ distance) for lay in range(coun...  6.68 us
    pallas_call x1, Pallas kernels, prepare(): pl.pallas_call(prepare_kernel, out_shape=jax.ShapeDtypeStruct((rows, dims...  6.15 us
    all_to_all x1, waiting for transfers between devices, along_line(): lax.all_to_all(blocks, ('rows', 'layer'), 0, 0, axis_index_groups=groups,...  6.1 us
    all_to_all x1, starting transfers between devices, along_line(): lax.all_to_all(blocks, ('rows', 'layer'), 0, 0, axis_index_groups=groups,...  4.66 us
    ppermute x2, waiting for transfers between devices, back(): return lax.ppermute(total, 'rows', tuple(enumerate(table)))  4.65 us
    ppermute x1, waiting for transfers between devices, along_line(): two = lax.ppermute(later, 'rows', ROUND_TWO)  4.39 us
    ppermute x1, starting transfers between devices, along_line(): one = lax.ppermute(documents, 'rows', ROUND_ONE)  4.04 us
    ppermute x1, waiting for transfers between devices, along_line(): one = lax.ppermute(documents, 'rows', ROUND_ONE)  3.93 us
  transfers between devices with their start and end apart: 11, of which 9 were waited for; matrix products, arithmetic and copies ran while one was open for 0% of the time, Pallas kernels for 17%

profile of v13, /device:TPU:0, one launch (start us, length us, event | category | flops | bytes accessed | tf_op | source)
XLA Modules:
  0.0 55.8 jit_solution(12970077961578645682)
XLA Ops:
  0.0 0.0 copy-start.1
  0.0 0.0 copy-start.2
  0.0 4.0 %collective-permute-start = (bf16[128,2048]{1,0:T(8,128)(2,1)}, bf16[128,2048]{1,0:T(8,128)(2,1)S(1)}, u32[]{:S(2)}, u32[]{:S(2)}) collective-permute-start(bf16[128,2048]{1,0:T(8,128)(2,1)} %documents_ref), channel_id=1, source_target_pairs={{0,8},{8,12},{12,4},{4,0},{1,9},{9,13},{13,5},{5,1},{2,10},{10,14}... | collective-permute-start | bytes 1572872 | tf_op jit(solution)/shard_map/ppermute | solution.py:280
  4.0 6.2 %shard_map.64.queries_ref = bf16[512,2048]{1,0:T(8,128)(2,1)} custom-call(s32[4]{0:T(128)} %offsets.1, bf16[512,2048]{1,0:T(8,128)(2,1)} %queries_hbm.1, bf16[4,512,512]{2,1,0:T(8,128)(2,1)} %bases_hbm.1, f32[4,512]{1,0:T(4,128)} %values_hbm.1), custom_call_target="tpu_custom_call" | custom-call | flops 2147483648 | bytes 6291456 | tf_op jit(solution)/shard_map/pallas_call | solution.py:52
  10.2 0.0 copy-done.1
  10.2 0.1 collective-permute-start.2
  10.3 0.0 copy-done.2
  10.3 0.1 copy.11.ids_ref
  10.4 0.0 copy-start
  10.4 1.6 %copy-done = bf16[512,2048]{1,0:T(8,128)(2,1)S(1)} copy-done((bf16[512,2048]{1,0:T(8,128)(2,1)S(1)}, bf16[512,2048]{1,0:T(8,128)(2,1)}, u32[]{:S(2)}) %copy-start) | copy-done | bytes 2097176
  12.0 0.8 %shard_map.65 = (f32[256,128]{1,0:T(8,128)S(1)}, f32[256,128]{1,0:T(8,128)S(1)}) custom-call(bf16[512,2048]{1,0:T(8,128)(2,1)S(1)} %copy-done, s32[512,1]{1,0:T(8,128)S(1)} %copy.11.ids_ref, bf16[128,2048]{1,0:T(8,128)(2,1)S(1)} %copy-done.1), custom_call_target="tpu_custom_call" | custom-call | flops 268435456 | bytes 2621440 | tf_op jit(solution)/shard_map/pallas_call | solution.py:81
  12.8 3.9 %collective-permute-done.documents_ref = bf16[128,2048]{1,0:T(8,128)(2,1)S(1)} collective-permute-done((bf16[128,2048]{1,0:T(8,128)(2,1)}, bf16[128,2048]{1,0:T(8,128)(2,1)S(1)}, u32[]{:S(2)}, u32[]{:S(2)}) %collective-permute-start) | collective-permute-done | bytes 524320 | tf_op jit(solution)/shard_map/ppermute | solution.py:280
  16.7 0.8 %shard_map.66 = (f32[256,256]{1,0:T(8,128)S(1)}, f32[256,256]{1,0:T(8,128)S(1)}) custom-call(bf16[512,2048]{1,0:T(8,128)(2,1)S(1)} %copy-done, s32[512,1]{1,0:T(8,128)S(1)} %copy.11.ids_ref, bf16[128,2048]{1,0:T(8,128)(2,1)S(1)} %collective-permute-done.documents_ref, f32[256,128]{1,0:T(8,128)S(1)} %get-tuple-element.32.refs_0_, ...), custom_call_target="tpu_custom_call" | custom-call | flops 268435456 | bytes 2621440 | tf_op jit(solution)/shard_map/pallas_call | solution.py:81
  17.5 0.1 collective-permute-start.3
  17.6 3.3 %collective-permute-start.1 = (bf16[128,2048]{1,0:T(8,128)(2,1)S(1)}, bf16[128,2048]{1,0:T(8,128)(2,1)S(1)}, u32[]{:S(2)}, u32[]{:S(2)}) collective-permute-start(bf16[128,2048]{1,0:T(8,128)(2,1)S(1)} %collective-permute-done.documents_ref), channel_id=1, source_target_pairs={{0,8},{8,12},{12,4},{4,0},{1,9},{9,13},{13,5},{5,1},{2,10},{10,14}... | collective-permute-start | bytes 1572872 | tf_op jit(solution)/shard_map/ppermute | solution.py:285
  20.9 0.0 collective-permute-done.3.arrived_ref
  20.9 1.6 %collective-permute-start.4 = (bf16[128,256]{1,0:T(8,128)(2,1)S(1)}, bf16[128,256]{1,0:T(8,128)(2,1)S(1)}, u32[]{:S(2)}, u32[]{:S(2)}) collective-permute-start(bf16[128,256]{1,0:T(8,128)(2,1)S(1)} %get-tuple-element.37), channel_id=1, source_target_pairs={{0,2},{1,3},{2,0},{3,1},{4,6},{5,7},{6,4},{7,5},{8,10},{9,11},{10,... | collective-permute-start | bytes 196616 | tf_op jit(solution)/shard_map/ppermute | solution.py:181
  22.5 2.8 %collective-permute-done.4.arrived_ref = bf16[128,256]{1,0:T(8,128)(2,1)S(1)} collective-permute-done((bf16[128,256]{1,0:T(8,128)(2,1)S(1)}, bf16[128,256]{1,0:T(8,128)(2,1)S(1)}, u32[]{:S(2)}, u32[]{:S(2)}) %collective-permute-start.4) | collective-permute-done | bytes 65568 | tf_op jit(solution)/shard_map/ppermute | solution.py:181
  25.3 4.4 %collective-permute-done.2.documents_ref = bf16[128,2048]{1,0:T(8,128)(2,1)S(1)} collective-permute-done((bf16[128,2048]{1,0:T(8,128)(2,1)S(1)}, bf16[128,2048]{1,0:T(8,128)(2,1)S(1)}, u32[]{:S(2)}, u32[]{:S(2)}) %collective-permute-start.2) | collective-permute-done | bytes 524320 | tf_op jit(solution)/shard_map/ppermute | solution.py:282
  29.7 0.8 %shard_map.69 = (f32[256,128]{1,0:T(8,128)S(1)}, f32[256,128]{1,0:T(8,128)S(1)}) custom-call(bf16[512,2048]{1,0:T(8,128)(2,1)S(1)} %copy-done, s32[512,1]{1,0:T(8,128)S(1)} %copy.11.ids_ref, bf16[128,2048]{1,0:T(8,128)(2,1)S(1)} %collective-permute-done.2.documents_ref), custom_call_target="tpu_custom_call" | custom-call | flops 268435456 | bytes 2621440 | tf_op jit(solution)/shard_map/pallas_call | solution.py:81
  30.4 0.1 collective-permute-start.6
  30.5 1.3 %collective-permute-done.6.arrived_ref = f32[256,128]{1,0:T(8,128)S(1)} collective-permute-done((f32[256,128]{1,0:T(8,128)S(1)}, f32[256,128]{1,0:T(8,128)S(1)}, u32[]{:S(2)}, u32[]{:S(2)}) %collective-permute-start.6) | collective-permute-done | bytes 131104 | tf_op jit(solution)/shard_map/ppermute | solution.py:181
  31.9 1.6 %collective-permute-start.7 = (bf16[128,128]{1,0:T(8,128)(2,1)S(1)}, bf16[128,128]{1,0:T(8,128)(2,1)S(1)}, u32[]{:S(2)}, u32[]{:S(2)}) collective-permute-start(bf16[128,128]{1,0:T(8,128)(2,1)S(1)} %get-tuple-element.44), channel_id=1, source_target_pairs={{0,2},{1,3},{2,0},{3,1},{4,6},{5,7},{6,4},{7,5},{8,10},{9,11},{10,... | collective-permute-start | bytes 98312 | tf_op jit(solution)/shard_map/ppermute | solution.py:181
  33.4 0.7 %collective-permute-start.5 = (bf16[128,128]{1,0:T(8,128)(2,1)S(1)}, bf16[128,128]{1,0:T(8,128)(2,1)S(1)}, u32[]{:S(2)}, u32[]{:S(2)}) collective-permute-start(bf16[128,128]{1,0:T(8,128)(2,1)S(1)} %get-tuple-element.39), channel_id=1, source_target_pairs={{0,4},{4,12},{8,0},{12,8},{1,5},{5,13},{9,1},{13,9},{2,6},{6,14},{... | collective-permute-start | bytes 98312 | tf_op jit(solution)/shard_map/ppermute | solution.py:278
  34.1 1.7 %collective-permute-done.7.arrived_ref = bf16[128,128]{1,0:T(8,128)(2,1)S(1)} collective-permute-done((bf16[128,128]{1,0:T(8,128)(2,1)S(1)}, bf16[128,128]{1,0:T(8,128)(2,1)S(1)}, u32[]{:S(2)}, u32[]{:S(2)}) %collective-permute-start.7) | collective-permute-done | bytes 32800 | tf_op jit(solution)/shard_map/ppermute | solution.py:181
  35.9 0.6 %collective-permute-start.8 = (bf16[128,128]{1,0:T(8,128)(2,1)S(1)}, bf16[128,128]{1,0:T(8,128)(2,1)S(1)}, u32[]{:S(2)}, u32[]{:S(2)}) collective-permute-start(bf16[128,128]{1,0:T(8,128)(2,1)S(1)} %shard_map.71), channel_id=1, source_target_pairs={{0,8},{4,0},{8,12},{12,4},{1,9},{5,1},{9,13},{13,5},{2,10},{6,2},{... | collective-permute-start | bytes 98312 | tf_op jit(solution)/shard_map/ppermute | solution.py:278
  36.5 4.5 %collective-permute-done.5.first_ref = bf16[128,128]{1,0:T(8,128)(2,1)S(1)} collective-permute-done((bf16[128,128]{1,0:T(8,128)(2,1)S(1)}, bf16[128,128]{1,0:T(8,128)(2,1)S(1)}, u32[]{:S(2)}, u32[]{:S(2)}) %collective-permute-start.5) | collective-permute-done | bytes 32800 | tf_op jit(solution)/shard_map/ppermute | solution.py:278
  40.9 0.0 collective-permute-done.1.documents_ref
  40.9 0.2 collective-permute-done.8.second_ref
  41.1 0.4 shard_map.73
  41.6 0.2 collective-permute-start.9
  41.7 0.4 shard_map.72.kept_ref
  42.2 0.8 %collective-permute-done.9.arrived_ref = f32[256,128]{1,0:T(8,128)S(1)} collective-permute-done((f32[256,128]{1,0:T(8,128)S(1)}, f32[256,128]{1,0:T(8,128)S(1)}, u32[]{:S(2)}, u32[]{:S(2)}) %collective-permute-start.9) | collective-permute-done | bytes 131104 | tf_op jit(solution)/shard_map/ppermute | solution.py:181
  43.0 0.7 %shard_map.74 = bf16[2,2,128,128]{3,2,1,0:T(8,128)(2,1)} custom-call(f32[256,128]{1,0:T(8,128)S(1)} %shard_map.72.kept_ref, f32[256,128]{1,0:T(8,128)S(1)} %collective-permute-done.9.arrived_ref), custom_call_target="tpu_custom_call" | custom-call | tf_op jit(solution)/shard_map/pallas_call | solution.py:143
  43.7 4.7 %all-to-all-start = ((bf16[4,128,128]{2,1,0:T(8,128)(2,1)}), bf16[4,128,128]{2,1,0:T(8,128)(2,1)S(1)}, u32[]{:S(2)}, u32[]{:S(2)}) async-start(bf16[4,128,128]{2,1,0:T(8,128)(2,1)} %bitcast.1), calls=%async_computation | async-start | bytes 262144 | tf_op jit(solution)/shard_map/all_to_all | solution.py:305
  48.3 0.7 %shard_map.75.scores_hbm = f32[4,128,128]{2,1,0:T(8,128)} custom-call(f32[128,128]{1,0:T(8,128)S(1)} %get-tuple-element.46.own_ref, bf16[128,128]{1,0:T(8,128)(2,1)S(1)} %collective-permute-done.5.first_ref, bf16[128,128]{1,0:T(8,128)(2,1)S(1)} %collective-permute-done.8.second_ref), custom_call_target="tpu_custom_call" | custom-call | tf_op jit(solution)/shard_map/pallas_call | solution.py:143
  49.0 6.1 %all-to-all-done = bf16[4,128,128]{2,1,0:T(8,128)(2,1)S(1)} async-done(((bf16[4,128,128]{2,1,0:T(8,128)(2,1)}), bf16[4,128,128]{2,1,0:T(8,128)(2,1)S(1)}, u32[]{:S(2)}, u32[]{:S(2)}) %all-to-all-start) | async-done | bytes 131104 | tf_op jit(solution)/shard_map/all_to_all | solution.py:305
  55.1 0.6 %shard_map.76 = f32[4,128,128]{2,1,0:T(8,128)} custom-call(bf16[2,2,128,128]{3,2,1,0:T(8,128)(2,1)S(1)} %bitcast.3, f32[4,128,128]{2,1,0:T(8,128)} %shard_map.75.scores_hbm), custom_call_target="tpu_custom_call", output_to_operand_aliasing={{}: (1, {})} | custom-call | tf_op jit(solution)/shard_map/pallas_call | solution.py:250
  (4 shorter events, 0.1 us)
Async XLA Ops:
  0.0 10.2 %copy-start.1 = (bf16[128,2048]{1,0:T(8,128)(2,1)S(1)}, bf16[128,2048]{1,0:T(8,128)(2,1)}, u32[]{:S(2)}) copy-start(bf16[128,2048]{1,0:T(8,128)(2,1)} %documents_ref) | copy-start | bytes 1572868
  0.0 10.3 %copy-start.2 = (s32[512]{0:T(512)S(1)}, s32[512]{0:T(512)}, u32[]{:S(2)}) copy-start(s32[512]{0:T(512)} %param.11) | copy-start | bytes 6148
  0.0 16.7 %collective-permute-start = (bf16[128,2048]{1,0:T(8,128)(2,1)}, bf16[128,2048]{1,0:T(8,128)(2,1)S(1)}, u32[]{:S(2)}, u32[]{:S(2)}) collective-permute-start(bf16[128,2048]{1,0:T(8,128)(2,1)} %documents_ref), channel_id=1, source_target_pairs={{0,8},{8,12},{12,4},{4,0},{1,9},{9,13},{13,5},{5,1},{2,10},{10,14}... | collective-permute-start | bytes 1572872 | tf_op jit(solution)/shard_map/ppermute | solution.py:280
  10.2 19.5 %collective-permute-start.2 = (bf16[128,2048]{1,0:T(8,128)(2,1)S(1)}, bf16[128,2048]{1,0:T(8,128)(2,1)S(1)}, u32[]{:S(2)}, u32[]{:S(2)}) collective-permute-start(bf16[128,2048]{1,0:T(8,128)(2,1)S(1)} %copy-done.1), channel_id=1, source_target_pairs={{0,4},{4,12},{12,8},{8,0},{1,5},{5,13},{13,9},{9,1},{2,6},{6,14},{... | collective-permute-start | bytes 1572872 | tf_op jit(solution)/shard_map/ppermute | solution.py:282
  10.4 1.6 %copy-start = (bf16[512,2048]{1,0:T(8,128)(2,1)S(1)}, bf16[512,2048]{1,0:T(8,128)(2,1)}, u32[]{:S(2)}) copy-start(bf16[512,2048]{1,0:T(8,128)(2,1)} %shard_map.64.queries_ref) | copy-start | bytes 6291460
  17.5 3.4 %collective-permute-start.3 = (f32[256,256]{1,0:T(8,128)S(1)}, f32[256,256]{1,0:T(8,128)S(1)}, u32[]{:S(2)}, u32[]{:S(2)}) collective-permute-start(f32[256,256]{1,0:T(8,128)S(1)} %get-tuple-element.35), channel_id=1, source_target_pairs={{0,1},{1,0},{2,3},{3,2},{4,5},{5,4},{6,7},{7,6},{8,9},{9,8},{10,11... | collective-permute-start | bytes 786440 | tf_op jit(solution)/shard_map/ppermute | solution.py:181
  17.6 23.4 %collective-permute-start.1 = (bf16[128,2048]{1,0:T(8,128)(2,1)S(1)}, bf16[128,2048]{1,0:T(8,128)(2,1)S(1)}, u32[]{:S(2)}, u32[]{:S(2)}) collective-permute-start(bf16[128,2048]{1,0:T(8,128)(2,1)S(1)} %collective-permute-done.documents_ref), channel_id=1, source_target_pairs={{0,8},{8,12},{12,4},{4,0},{1,9},{9,13},{13,5},{5,1},{2,10},{10,14}... | collective-permute-start | bytes 1572872 | tf_op jit(solution)/shard_map/ppermute | solution.py:285
  20.9 4.3 %collective-permute-start.4 = (bf16[128,256]{1,0:T(8,128)(2,1)S(1)}, bf16[128,256]{1,0:T(8,128)(2,1)S(1)}, u32[]{:S(2)}, u32[]{:S(2)}) collective-permute-start(bf16[128,256]{1,0:T(8,128)(2,1)S(1)} %get-tuple-element.37), channel_id=1, source_target_pairs={{0,2},{1,3},{2,0},{3,1},{4,6},{5,7},{6,4},{7,5},{8,10},{9,11},{10,... | collective-permute-start | bytes 196616 | tf_op jit(solution)/shard_map/ppermute | solution.py:181
  30.4 1.4 %collective-permute-start.6 = (f32[256,128]{1,0:T(8,128)S(1)}, f32[256,128]{1,0:T(8,128)S(1)}, u32[]{:S(2)}, u32[]{:S(2)}) collective-permute-start(f32[256,128]{1,0:T(8,128)S(1)} %get-tuple-element.42), channel_id=1, source_target_pairs={{0,1},{1,0},{2,3},{3,2},{4,5},{5,4},{6,7},{7,6},{8,9},{9,8},{10,11... | collective-permute-start | bytes 393224 | tf_op jit(solution)/shard_map/ppermute | solution.py:181
  31.9 4.0 %collective-permute-start.7 = (bf16[128,128]{1,0:T(8,128)(2,1)S(1)}, bf16[128,128]{1,0:T(8,128)(2,1)S(1)}, u32[]{:S(2)}, u32[]{:S(2)}) collective-permute-start(bf16[128,128]{1,0:T(8,128)(2,1)S(1)} %get-tuple-element.44), channel_id=1, source_target_pairs={{0,2},{1,3},{2,0},{3,1},{4,6},{5,7},{6,4},{7,5},{8,10},{9,11},{10,... | collective-permute-start | bytes 98312 | tf_op jit(solution)/shard_map/ppermute | solution.py:181
  33.4 7.5 %collective-permute-start.5 = (bf16[128,128]{1,0:T(8,128)(2,1)S(1)}, bf16[128,128]{1,0:T(8,128)(2,1)S(1)}, u32[]{:S(2)}, u32[]{:S(2)}) collective-permute-start(bf16[128,128]{1,0:T(8,128)(2,1)S(1)} %get-tuple-element.39), channel_id=1, source_target_pairs={{0,4},{4,12},{8,0},{12,8},{1,5},{5,13},{9,1},{13,9},{2,6},{6,14},{... | collective-permute-start | bytes 98312 | tf_op jit(solution)/shard_map/ppermute | solution.py:278
  35.9 5.3 %collective-permute-start.8 = (bf16[128,128]{1,0:T(8,128)(2,1)S(1)}, bf16[128,128]{1,0:T(8,128)(2,1)S(1)}, u32[]{:S(2)}, u32[]{:S(2)}) collective-permute-start(bf16[128,128]{1,0:T(8,128)(2,1)S(1)} %shard_map.71), channel_id=1, source_target_pairs={{0,8},{4,0},{8,12},{12,4},{1,9},{5,1},{9,13},{13,5},{2,10},{6,2},{... | collective-permute-start | bytes 98312 | tf_op jit(solution)/shard_map/ppermute | solution.py:278
  41.6 1.4 %collective-permute-start.9 = (f32[256,128]{1,0:T(8,128)S(1)}, f32[256,128]{1,0:T(8,128)S(1)}, u32[]{:S(2)}, u32[]{:S(2)}) collective-permute-start(f32[256,128]{1,0:T(8,128)S(1)} %shard_map.73), channel_id=1, source_target_pairs={{0,1},{1,0},{2,3},{3,2},{4,5},{5,4},{6,7},{7,6},{8,9},{9,8},{10,11... | collective-permute-start | bytes 393224 | tf_op jit(solution)/shard_map/ppermute | solution.py:181
  43.7 11.5 %all-to-all-start = ((bf16[4,128,128]{2,1,0:T(8,128)(2,1)}), bf16[4,128,128]{2,1,0:T(8,128)(2,1)S(1)}, u32[]{:S(2)}, u32[]{:S(2)}) async-start(bf16[4,128,128]{2,1,0:T(8,128)(2,1)} %bitcast.1), calls=%async_computation | async-start | bytes 262144 | tf_op jit(solution)/shard_map/all_to_all | solution.py:305

commit v14 on v10

--- a/solution.py
+++ b/solution.py
@@ -119,12 +119,16 @@
             out_refs[side][spot, width - docs :] = held[pl.ds(first, rows // 2), :]
 
 
+def target_chip():
+    chip, core = lax.div(layer_index(), 2), lax.rem(layer_index(), 2)
+    return jnp.where(chip == core, 0, 1)
+
+
 def half_kernel(block_of, kept, queries_ref, ids_ref, documents_ref, out_ref):
-    share_rows = out_ref.shape[0] // 2
-    firsts = half_shares(share_rows, kept)
-    queries = jnp.concatenate([queries_ref[pl.ds(first, share_rows), :] for first in firsts], axis=0)
-    query_ids = jnp.concatenate([ids_ref[pl.ds(first, share_rows), :] for first in firsts], axis=0)
-    out_ref[...] = masked_tile(queries, documents_ref[...], query_ids, block_of(row_index()))
+    rows = out_ref.shape[0]
+    chip = target_chip() if kept else 1 - target_chip()
+    spot = pl.ds(pl.multiple_of(chip * rows, rows), rows)
+    out_ref[...] = masked_tile(queries_ref[spot, :], documents_ref[...], ids_ref[spot, :], block_of(row_index()))
 
 
 def total_of(refs):
@@ -135,7 +139,7 @@
 
 
 def sum_kernel(*refs):
-    refs[-1][...] = total_of(refs[:-1])
+    refs[-1][...] = total_of(refs[:-1]).astype(refs[-1].dtype)
 
 
 def small_call(kernel, out_shape, *args):
@@ -221,15 +225,17 @@
         out_ref[step_of(table)(row_index())] = ref[...].astype(jnp.float32)
 
 
-def finish_kernel(mine_ref, other_ref, scores_hbm, out_hbm, total, copied):
+def finish_kernel(mine_ref, arrived_ref, scores_hbm, out_hbm, total, copied):
     del scores_hbm
-    total[...] = total_of([mine_ref, other_ref])
+    rows = total.shape[0]
+    share = pl.ds(pl.multiple_of(lax.rem(layer_index(), 2) * rows, rows), rows)
+    total[...] = mine_ref[share, :].astype(jnp.float32) + arrived_ref[share, :].astype(jnp.float32)
     copy = pltpu.make_async_copy(total, out_hbm.at[step_of(BLOCK_LAST)(row_index())], copied)
     copy.start()
     copy.wait()
 
 
-def finish(mine, other, scores):
+def finish(mine, arrived, scores):
     hbm = pl.BlockSpec(memory_space=pltpu.HBM)
     vmem = pl.BlockSpec(memory_space=pltpu.VMEM)
     return pl.pallas_call(
@@ -237,10 +243,10 @@
         out_shape=jax.ShapeDtypeStruct(scores.shape, scores.dtype),
         in_specs=[vmem, vmem, hbm],
         out_specs=hbm,
-        scratch_shapes=[pltpu.VMEM(mine.shape, jnp.float32), pltpu.SemaphoreType.DMA],
+        scratch_shapes=[pltpu.VMEM(scores.shape[1:], jnp.float32), pltpu.SemaphoreType.DMA],
         input_output_aliases={2: 0},
         compiler_params=pltpu.CompilerParams(vmem_limit_bytes=4 * MIB),
-    )(mine, other, scores)
+    )(mine, arrived, scores)
 
 
 def along_line(documents, conditioned, query_ids):
@@ -278,18 +284,17 @@
 
     arrived = swap(one_half(three, pick(BLOCK_LAST), False), 1)
     kept = one_half(three, pick(BLOCK_LAST), True)
-    mine, other = core_sum(kept, arrived, jnp.bfloat16)
-    mine = back(mine, BLOCK_LAST)
+    (both,) = small_call(sum_kernel, [jax.ShapeDtypeStruct(half, jnp.bfloat16)], kept, arrived)
     shares = lax.axis_size("layer")
     pairs = [
-        (row * shares + lay, BLOCK_LAST[row] * shares + (lay ^ 2))
+        (row * shares + lay, BLOCK_LAST[row] * shares + 2 * ((lay // 2) ^ (lay % 2)) + lay % 2)
         for row in range(len(BLOCK_LAST))
         for lay in range(shares)
     ]
-    other = lax.ppermute(other, ("rows", "layer"), pairs)
+    mine = lax.ppermute(both, ("rows", "layer"), pairs)
     out_shape = [jax.ShapeDtypeStruct((STEPS,) + own.shape, jnp.float32)]
     (scores,) = small_call(assemble_kernel, out_shape, own, first, second)
-    return finish(mine, other, scores)
+    return finish(mine, swap(mine, 1), scores)
 
 
 def around_ring(documents, conditioned, query_ids):

time: 53 us -> 51.8 us (0.977)
  starting transfers between devices: 16.9 us -> 14.6 us
  waiting for transfers between devices: 23.2 us -> 24.4 us
    ppermute x3 -> x2, starting transfers between devices: 3.82 us -> 1.29 us  [back(): return lax.ppermute(total, 'rows', tuple(enumerate(table)))]
    ppermute x1, waiting for transfers between devices: 3.33 us -> 4.2 us  [along_line(): mine = lax.ppermute(both, ('rows', 'layer'), pairs)]
    ppermute x5 -> x6, waiting for transfers between devices: 6.68 us -> 7.21 us  [swap(): lax.ppermute(value, 'layer', [(lay, lay ^ distance) for lay in range(coun...]
    ppermute x3 -> x2, waiting for transfers between devices: 4.92 us -> 4.65 us  [back(): return lax.ppermute(total, 'rows', tuple(enumerate(table)))]
    ppermute x5 -> x6, starting transfers between devices: 3.41 us -> 3.41 us  [swap(): lax.ppermute(value, 'layer', [(lay, lay ^ distance) for lay in range(coun...]
  transfers between devices with their start and end apart: 12 -> 12, of which waited for: 10 -> 10; matrix products, arithmetic and copies ran while one was open for 0% -> 0% of each run, Pallas kernels for 18% -> 19%
where the time goes in v14:
time: 51.8 us; the launch traced here: 51.6 us
  waiting for transfers between devices  24.4 us (47%)
  starting transfers between devices  14.6 us (28%)
  Pallas kernels  10.8 us (21%)
  local copies, waits for them, and re-layouts  1.74 us (3%)
    ppermute x6, waiting for transfers between devices, swap(): lax.ppermute(value, 'layer', [(lay, lay ^ distance) for lay in range(coun...  7.21 us
    pallas_call x1, Pallas kernels, prepare(): pl.pallas_call(prepare_kernel, out_shape=jax.ShapeDtypeStruct((rows, dims...  6.15 us
    ppermute x2, waiting for transfers between devices, back(): return lax.ppermute(total, 'rows', tuple(enumerate(table)))  4.65 us
    ppermute x1, waiting for transfers between devices, along_line(): two = lax.ppermute(later, 'rows', ROUND_TWO)  4.39 us
    ppermute x1, waiting for transfers between devices, along_line(): mine = lax.ppermute(both, ('rows', 'layer'), pairs)  4.2 us
    ppermute x1, starting transfers between devices, along_line(): one = lax.ppermute(documents, 'rows', ROUND_ONE)  4.04 us
    ppermute x1, waiting for transfers between devices, along_line(): one = lax.ppermute(documents, 'rows', ROUND_ONE)  3.93 us
    ppermute x6, starting transfers between devices, swap(): lax.ppermute(value, 'layer', [(lay, lay ^ distance) for lay in range(coun...  3.41 us
  transfers between devices with their start and end apart: 12, of which 10 were waited for; matrix products, arithmetic and copies ran while one was open for 0% of the time, Pallas kernels for 19%

profile of v14, /device:TPU:0, one launch (start us, length us, event | category | flops | bytes accessed | tf_op | source)
XLA Modules:
  0.0 51.6 jit_solution(15574807597993696758)
XLA Ops:
  0.0 0.0 copy-start.1
  0.0 0.0 copy-start.2
  0.0 4.0 %collective-permute-start = (bf16[128,2048]{1,0:T(8,128)(2,1)}, bf16[128,2048]{1,0:T(8,128)(2,1)S(1)}, u32[]{:S(2)}, u32[]{:S(2)}) collective-permute-start(bf16[128,2048]{1,0:T(8,128)(2,1)} %documents_ref), channel_id=1, source_target_pairs={{0,8},{8,12},{12,4},{4,0},{1,9},{9,13},{13,5},{5,1},{2,10},{10,14}... | collective-permute-start | bytes 1572872 | tf_op jit(solution)/shard_map/ppermute | solution.py:271
  4.0 6.2 %shard_map.64.queries_ref = bf16[512,2048]{1,0:T(8,128)(2,1)} custom-call(s32[4]{0:T(128)} %offsets.1, bf16[512,2048]{1,0:T(8,128)(2,1)} %queries_hbm.1, bf16[4,512,512]{2,1,0:T(8,128)(2,1)} %bases_hbm.1, f32[4,512]{1,0:T(4,128)} %values_hbm.1), custom_call_target="tpu_custom_call" | custom-call | flops 2147483648 | bytes 6291456 | tf_op jit(solution)/shard_map/pallas_call | solution.py:52
  10.2 0.0 copy-done.1
  10.2 0.1 collective-permute-start.2
  10.3 0.0 copy-done.2
  10.3 0.1 copy.11.ids_ref
  10.4 0.0 copy-start
  10.4 1.6 %copy-done = bf16[512,2048]{1,0:T(8,128)(2,1)S(1)} copy-done((bf16[512,2048]{1,0:T(8,128)(2,1)S(1)}, bf16[512,2048]{1,0:T(8,128)(2,1)}, u32[]{:S(2)}) %copy-start) | copy-done | bytes 2097176
  12.0 0.8 %shard_map.65 = (f32[256,128]{1,0:T(8,128)S(1)}, f32[256,128]{1,0:T(8,128)S(1)}) custom-call(bf16[512,2048]{1,0:T(8,128)(2,1)S(1)} %copy-done, s32[512,1]{1,0:T(8,128)S(1)} %copy.11.ids_ref, bf16[128,2048]{1,0:T(8,128)(2,1)S(1)} %copy-done.1), custom_call_target="tpu_custom_call" | custom-call | flops 268435456 | bytes 2621440 | tf_op jit(solution)/shard_map/pallas_call | solution.py:81
  12.8 3.9 %collective-permute-done.documents_ref = bf16[128,2048]{1,0:T(8,128)(2,1)S(1)} collective-permute-done((bf16[128,2048]{1,0:T(8,128)(2,1)}, bf16[128,2048]{1,0:T(8,128)(2,1)S(1)}, u32[]{:S(2)}, u32[]{:S(2)}) %collective-permute-start) | collective-permute-done | bytes 524320 | tf_op jit(solution)/shard_map/ppermute | solution.py:271
  16.7 0.8 %shard_map.66 = (f32[256,256]{1,0:T(8,128)S(1)}, f32[256,256]{1,0:T(8,128)S(1)}) custom-call(bf16[512,2048]{1,0:T(8,128)(2,1)S(1)} %copy-done, s32[512,1]{1,0:T(8,128)S(1)} %copy.11.ids_ref, bf16[128,2048]{1,0:T(8,128)(2,1)S(1)} %collective-permute-done.documents_ref, f32[256,128]{1,0:T(8,128)S(1)} %get-tuple-element.32.refs_0_, ...), custom_call_target="tpu_custom_call" | custom-call | flops 268435456 | bytes 2621440 | tf_op jit(solution)/shard_map/pallas_call | solution.py:81
  17.5 0.1 collective-permute-start.3
  17.6 3.3 %collective-permute-start.1 = (bf16[128,2048]{1,0:T(8,128)(2,1)S(1)}, bf16[128,2048]{1,0:T(8,128)(2,1)S(1)}, u32[]{:S(2)}, u32[]{:S(2)}) collective-permute-start(bf16[128,2048]{1,0:T(8,128)(2,1)S(1)} %collective-permute-done.documents_ref), channel_id=1, source_target_pairs={{0,8},{8,12},{12,4},{4,0},{1,9},{9,13},{13,5},{5,1},{2,10},{10,14}... | collective-permute-start | bytes 1572872 | tf_op jit(solution)/shard_map/ppermute | solution.py:276
  20.9 0.0 collective-permute-done.3.arrived_ref
  20.9 1.6 %collective-permute-start.4 = (bf16[128,256]{1,0:T(8,128)(2,1)S(1)}, bf16[128,256]{1,0:T(8,128)(2,1)S(1)}, u32[]{:S(2)}, u32[]{:S(2)}) collective-permute-start(bf16[128,256]{1,0:T(8,128)(2,1)S(1)} %get-tuple-element.37), channel_id=1, source_target_pairs={{0,2},{1,3},{2,0},{3,1},{4,6},{5,7},{6,4},{7,5},{8,10},{9,11},{10,... | collective-permute-start | bytes 196616 | tf_op jit(solution)/shard_map/ppermute | solution.py:185
  22.5 2.8 %collective-permute-done.4.arrived_ref = bf16[128,256]{1,0:T(8,128)(2,1)S(1)} collective-permute-done((bf16[128,256]{1,0:T(8,128)(2,1)S(1)}, bf16[128,256]{1,0:T(8,128)(2,1)S(1)}, u32[]{:S(2)}, u32[]{:S(2)}) %collective-permute-start.4) | collective-permute-done | bytes 65568 | tf_op jit(solution)/shard_map/ppermute | solution.py:185
  25.3 4.4 %collective-permute-done.2.documents_ref = bf16[128,2048]{1,0:T(8,128)(2,1)S(1)} collective-permute-done((bf16[128,2048]{1,0:T(8,128)(2,1)S(1)}, bf16[128,2048]{1,0:T(8,128)(2,1)S(1)}, u32[]{:S(2)}, u32[]{:S(2)}) %collective-permute-start.2) | collective-permute-done | bytes 524320 | tf_op jit(solution)/shard_map/ppermute | solution.py:273
  29.7 0.8 %shard_map.69 = (f32[256,128]{1,0:T(8,128)S(1)}, f32[256,128]{1,0:T(8,128)S(1)}) custom-call(bf16[512,2048]{1,0:T(8,128)(2,1)S(1)} %copy-done, s32[512,1]{1,0:T(8,128)S(1)} %copy.11.ids_ref, bf16[128,2048]{1,0:T(8,128)(2,1)S(1)} %collective-permute-done.2.documents_ref), custom_call_target="tpu_custom_call" | custom-call | flops 268435456 | bytes 2621440 | tf_op jit(solution)/shard_map/pallas_call | solution.py:81
  30.4 0.1 collective-permute-start.6
  30.5 1.3 %collective-permute-done.6.arrived_ref = f32[256,128]{1,0:T(8,128)S(1)} collective-permute-done((f32[256,128]{1,0:T(8,128)S(1)}, f32[256,128]{1,0:T(8,128)S(1)}, u32[]{:S(2)}, u32[]{:S(2)}) %collective-permute-start.6) | collective-permute-done | bytes 131104 | tf_op jit(solution)/shard_map/ppermute | solution.py:185
  31.9 1.6 %collective-permute-start.7 = (bf16[128,128]{1,0:T(8,128)(2,1)S(1)}, bf16[128,128]{1,0:T(8,128)(2,1)S(1)}, u32[]{:S(2)}, u32[]{:S(2)}) collective-permute-start(bf16[128,128]{1,0:T(8,128)(2,1)S(1)} %get-tuple-element.44), channel_id=1, source_target_pairs={{0,2},{1,3},{2,0},{3,1},{4,6},{5,7},{6,4},{7,5},{8,10},{9,11},{10,... | collective-permute-start | bytes 98312 | tf_op jit(solution)/shard_map/ppermute | solution.py:185
  33.4 0.7 %collective-permute-start.5 = (bf16[128,128]{1,0:T(8,128)(2,1)S(1)}, bf16[128,128]{1,0:T(8,128)(2,1)S(1)}, u32[]{:S(2)}, u32[]{:S(2)}) collective-permute-start(bf16[128,128]{1,0:T(8,128)(2,1)S(1)} %get-tuple-element.39), channel_id=1, source_target_pairs={{0,4},{4,12},{8,0},{12,8},{1,5},{5,13},{9,1},{13,9},{2,6},{6,14},{... | collective-permute-start | bytes 98312 | tf_op jit(solution)/shard_map/ppermute | solution.py:269
  34.1 1.7 %collective-permute-done.7.arrived_ref = bf16[128,128]{1,0:T(8,128)(2,1)S(1)} collective-permute-done((bf16[128,128]{1,0:T(8,128)(2,1)S(1)}, bf16[128,128]{1,0:T(8,128)(2,1)S(1)}, u32[]{:S(2)}, u32[]{:S(2)}) %collective-permute-start.7) | collective-permute-done | bytes 32800 | tf_op jit(solution)/shard_map/ppermute | solution.py:185
  35.9 0.6 %collective-permute-start.8 = (bf16[128,128]{1,0:T(8,128)(2,1)S(1)}, bf16[128,128]{1,0:T(8,128)(2,1)S(1)}, u32[]{:S(2)}, u32[]{:S(2)}) collective-permute-start(bf16[128,128]{1,0:T(8,128)(2,1)S(1)} %shard_map.71), channel_id=1, source_target_pairs={{0,8},{4,0},{8,12},{12,4},{1,9},{5,1},{9,13},{13,5},{2,10},{6,2},{... | collective-permute-start | bytes 98312 | tf_op jit(solution)/shard_map/ppermute | solution.py:269
  36.5 4.5 %collective-permute-done.5.first_ref = bf16[128,128]{1,0:T(8,128)(2,1)S(1)} collective-permute-done((bf16[128,128]{1,0:T(8,128)(2,1)S(1)}, bf16[128,128]{1,0:T(8,128)(2,1)S(1)}, u32[]{:S(2)}, u32[]{:S(2)}) %collective-permute-start.5) | collective-permute-done | bytes 32800 | tf_op jit(solution)/shard_map/ppermute | solution.py:269
  40.9 0.0 collective-permute-done.1.documents_ref
  40.9 0.2 collective-permute-done.8.second_ref
  41.1 0.4 shard_map.73
  41.6 0.2 collective-permute-start.9
  41.7 0.4 shard_map.72.refs_0_
  42.2 0.8 %collective-permute-done.9.refs_1_ = f32[256,128]{1,0:T(8,128)S(1)} collective-permute-done((f32[256,128]{1,0:T(8,128)S(1)}, f32[256,128]{1,0:T(8,128)S(1)}, u32[]{:S(2)}, u32[]{:S(2)}) %collective-permute-start.9) | collective-permute-done | bytes 131104 | tf_op jit(solution)/shard_map/ppermute | solution.py:185
  43.0 2.5 %collective-permute-start.10 = (bf16[256,128]{1,0:T(8,128)(2,1)S(1)}, bf16[256,128]{1,0:T(8,128)(2,1)S(1)}, u32[]{:S(2)}, u32[]{:S(2)}) collective-permute-start(bf16[256,128]{1,0:T(8,128)(2,1)S(1)} %shard_map.74), channel_id=1, source_target_pairs={{0,12},{1,15},{2,14},{3,13},{4,8},{5,11},{6,10},{7,9},{8,4},{9,7},... | collective-permute-start | bytes 196616 | tf_op jit(solution)/shard_map/ppermute | solution.py:294
  45.5 4.2 %collective-permute-done.10.mine_ref = bf16[256,128]{1,0:T(8,128)(2,1)S(1)} collective-permute-done((bf16[256,128]{1,0:T(8,128)(2,1)S(1)}, bf16[256,128]{1,0:T(8,128)(2,1)S(1)}, u32[]{:S(2)}, u32[]{:S(2)}) %collective-permute-start.10) | collective-permute-done | bytes 65568 | tf_op jit(solution)/shard_map/ppermute | solution.py:294
  49.7 0.0 collective-permute-start.11
  49.7 0.7 %shard_map.75.scores_hbm = f32[4,128,128]{2,1,0:T(8,128)} custom-call(f32[128,128]{1,0:T(8,128)S(1)} %get-tuple-element.46.own_ref, bf16[128,128]{1,0:T(8,128)(2,1)S(1)} %collective-permute-done.5.first_ref, bf16[128,128]{1,0:T(8,128)(2,1)S(1)} %collective-permute-done.8.second_ref), custom_call_target="tpu_custom_call" | custom-call | tf_op jit(solution)/shard_map/pallas_call | solution.py:147
  50.4 0.5 %collective-permute-done.11.arrived_ref = bf16[256,128]{1,0:T(8,128)(2,1)S(1)} collective-permute-done((bf16[256,128]{1,0:T(8,128)(2,1)S(1)}, bf16[256,128]{1,0:T(8,128)(2,1)S(1)}, u32[]{:S(2)}, u32[]{:S(2)}) %collective-permute-start.11) | collective-permute-done | bytes 65568 | tf_op jit(solution)/shard_map/ppermute | solution.py:185
  51.0 0.6 %shard_map.76 = f32[4,128,128]{2,1,0:T(8,128)} custom-call(bf16[256,128]{1,0:T(8,128)(2,1)S(1)} %collective-permute-done.10.mine_ref, bf16[256,128]{1,0:T(8,128)(2,1)S(1)} %collective-permute-done.11.arrived_ref, f32[4,128,128]{2,1,0:T(8,128)} %shard_map.75.scores_hbm), custom_call_target="tpu_custom_call", output_to_operand_aliasing={{}: (2, {})} | custom-call | tf_op jit(solution)/shard_map/pallas_call | solution.py:241
  (5 shorter events, 0.1 us)
Async XLA Ops:
  0.0 10.2 %copy-start.1 = (bf16[128,2048]{1,0:T(8,128)(2,1)S(1)}, bf16[128,2048]{1,0:T(8,128)(2,1)}, u32[]{:S(2)}) copy-start(bf16[128,2048]{1,0:T(8,128)(2,1)} %documents_ref) | copy-start | bytes 1572868
  0.0 10.3 %copy-start.2 = (s32[512]{0:T(512)S(1)}, s32[512]{0:T(512)}, u32[]{:S(2)}) copy-start(s32[512]{0:T(512)} %param.11) | copy-start | bytes 6148
  0.0 16.7 %collective-permute-start = (bf16[128,2048]{1,0:T(8,128)(2,1)}, bf16[128,2048]{1,0:T(8,128)(2,1)S(1)}, u32[]{:S(2)}, u32[]{:S(2)}) collective-permute-start(bf16[128,2048]{1,0:T(8,128)(2,1)} %documents_ref), channel_id=1, source_target_pairs={{0,8},{8,12},{12,4},{4,0},{1,9},{9,13},{13,5},{5,1},{2,10},{10,14}... | collective-permute-start | bytes 1572872 | tf_op jit(solution)/shard_map/ppermute | solution.py:271
  10.2 19.5 %collective-permute-start.2 = (bf16[128,2048]{1,0:T(8,128)(2,1)S(1)}, bf16[128,2048]{1,0:T(8,128)(2,1)S(1)}, u32[]{:S(2)}, u32[]{:S(2)}) collective-permute-start(bf16[128,2048]{1,0:T(8,128)(2,1)S(1)} %copy-done.1), channel_id=1, source_target_pairs={{0,4},{4,12},{12,8},{8,0},{1,5},{5,13},{13,9},{9,1},{2,6},{6,14},{... | collective-permute-start | bytes 1572872 | tf_op jit(solution)/shard_map/ppermute | solution.py:273
  10.4 1.6 %copy-start = (bf16[512,2048]{1,0:T(8,128)(2,1)S(1)}, bf16[512,2048]{1,0:T(8,128)(2,1)}, u32[]{:S(2)}) copy-start(bf16[512,2048]{1,0:T(8,128)(2,1)} %shard_map.64.queries_ref) | copy-start | bytes 6291460
  17.5 3.4 %collective-permute-start.3 = (f32[256,256]{1,0:T(8,128)S(1)}, f32[256,256]{1,0:T(8,128)S(1)}, u32[]{:S(2)}, u32[]{:S(2)}) collective-permute-start(f32[256,256]{1,0:T(8,128)S(1)} %get-tuple-element.35), channel_id=1, source_target_pairs={{0,1},{1,0},{2,3},{3,2},{4,5},{5,4},{6,7},{7,6},{8,9},{9,8},{10,11... | collective-permute-start | bytes 786440 | tf_op jit(solution)/shard_map/ppermute | solution.py:185
  17.6 23.4 %collective-permute-start.1 = (bf16[128,2048]{1,0:T(8,128)(2,1)S(1)}, bf16[128,2048]{1,0:T(8,128)(2,1)S(1)}, u32[]{:S(2)}, u32[]{:S(2)}) collective-permute-start(bf16[128,2048]{1,0:T(8,128)(2,1)S(1)} %collective-permute-done.documents_ref), channel_id=1, source_target_pairs={{0,8},{8,12},{12,4},{4,0},{1,9},{9,13},{13,5},{5,1},{2,10},{10,14}... | collective-permute-start | bytes 1572872 | tf_op jit(solution)/shard_map/ppermute | solution.py:276
  20.9 4.3 %collective-permute-start.4 = (bf16[128,256]{1,0:T(8,128)(2,1)S(1)}, bf16[128,256]{1,0:T(8,128)(2,1)S(1)}, u32[]{:S(2)}, u32[]{:S(2)}) collective-permute-start(bf16[128,256]{1,0:T(8,128)(2,1)S(1)} %get-tuple-element.37), channel_id=1, source_target_pairs={{0,2},{1,3},{2,0},{3,1},{4,6},{5,7},{6,4},{7,5},{8,10},{9,11},{10,... | collective-permute-start | bytes 196616 | tf_op jit(solution)/shard_map/ppermute | solution.py:185
  30.4 1.4 %collective-permute-start.6 = (f32[256,128]{1,0:T(8,128)S(1)}, f32[256,128]{1,0:T(8,128)S(1)}, u32[]{:S(2)}, u32[]{:S(2)}) collective-permute-start(f32[256,128]{1,0:T(8,128)S(1)} %get-tuple-element.42), channel_id=1, source_target_pairs={{0,1},{1,0},{2,3},{3,2},{4,5},{5,4},{6,7},{7,6},{8,9},{9,8},{10,11... | collective-permute-start | bytes 393224 | tf_op jit(solution)/shard_map/ppermute | solution.py:185
  31.9 4.0 %collective-permute-start.7 = (bf16[128,128]{1,0:T(8,128)(2,1)S(1)}, bf16[128,128]{1,0:T(8,128)(2,1)S(1)}, u32[]{:S(2)}, u32[]{:S(2)}) collective-permute-start(bf16[128,128]{1,0:T(8,128)(2,1)S(1)} %get-tuple-element.44), channel_id=1, source_target_pairs={{0,2},{1,3},{2,0},{3,1},{4,6},{5,7},{6,4},{7,5},{8,10},{9,11},{10,... | collective-permute-start | bytes 98312 | tf_op jit(solution)/shard_map/ppermute | solution.py:185
  33.4 7.5 %collective-permute-start.5 = (bf16[128,128]{1,0:T(8,128)(2,1)S(1)}, bf16[128,128]{1,0:T(8,128)(2,1)S(1)}, u32[]{:S(2)}, u32[]{:S(2)}) collective-permute-start(bf16[128,128]{1,0:T(8,128)(2,1)S(1)} %get-tuple-element.39), channel_id=1, source_target_pairs={{0,4},{4,12},{8,0},{12,8},{1,5},{5,13},{9,1},{13,9},{2,6},{6,14},{... | collective-permute-start | bytes 98312 | tf_op jit(solution)/shard_map/ppermute | solution.py:269
  35.9 5.3 %collective-permute-start.8 = (bf16[128,128]{1,0:T(8,128)(2,1)S(1)}, bf16[128,128]{1,0:T(8,128)(2,1)S(1)}, u32[]{:S(2)}, u32[]{:S(2)}) collective-permute-start(bf16[128,128]{1,0:T(8,128)(2,1)S(1)} %shard_map.71), channel_id=1, source_target_pairs={{0,8},{4,0},{8,12},{12,4},{1,9},{5,1},{9,13},{13,5},{2,10},{6,2},{... | collective-permute-start | bytes 98312 | tf_op jit(solution)/shard_map/ppermute | solution.py:269
  41.6 1.4 %collective-permute-start.9 = (f32[256,128]{1,0:T(8,128)S(1)}, f32[256,128]{1,0:T(8,128)S(1)}, u32[]{:S(2)}, u32[]{:S(2)}) collective-permute-start(f32[256,128]{1,0:T(8,128)S(1)} %shard_map.73), channel_id=1, source_target_pairs={{0,1},{1,0},{2,3},{3,2},{4,5},{5,4},{6,7},{7,6},{8,9},{9,8},{10,11... | collective-permute-start | bytes 393224 | tf_op jit(solution)/shard_map/ppermute | solution.py:185
  43.0 6.7 %collective-permute-start.10 = (bf16[256,128]{1,0:T(8,128)(2,1)S(1)}, bf16[256,128]{1,0:T(8,128)(2,1)S(1)}, u32[]{:S(2)}, u32[]{:S(2)}) collective-permute-start(bf16[256,128]{1,0:T(8,128)(2,1)S(1)} %shard_map.74), channel_id=1, source_target_pairs={{0,12},{1,15},{2,14},{3,13},{4,8},{5,11},{6,10},{7,9},{8,4},{9,7},... | collective-permute-start | bytes 196616 | tf_op jit(solution)/shard_map/ppermute | solution.py:294
  49.7 1.3 %collective-permute-start.11 = (bf16[256,128]{1,0:T(8,128)(2,1)S(1)}, bf16[256,128]{1,0:T(8,128)(2,1)S(1)}, u32[]{:S(2)}, u32[]{:S(2)}) collective-permute-start(bf16[256,128]{1,0:T(8,128)(2,1)S(1)} %collective-permute-done.10.mine_ref), channel_id=1, source_target_pairs={{0,1},{1,0},{2,3},{3,2},{4,5},{5,4},{6,7},{7,6},{8,9},{9,8},{10,11... | collective-permute-start | bytes 196616 | tf_op jit(solution)/shard_map/ppermute | solution.py:185

commit v15 on v14

--- a/solution.py
+++ b/solution.py
@@ -128,7 +128,8 @@
     rows = out_ref.shape[0]
     chip = target_chip() if kept else 1 - target_chip()
     spot = pl.ds(pl.multiple_of(chip * rows, rows), rows)
-    out_ref[...] = masked_tile(queries_ref[spot, :], documents_ref[...], ids_ref[spot, :], block_of(row_index()))
+    tile = masked_tile(queries_ref[spot, :], documents_ref[...], ids_ref[spot, :], block_of(row_index()))
+    out_ref[...] = tile.astype(out_ref.dtype)
 
 
 def total_of(refs):
@@ -225,28 +226,12 @@
         out_ref[step_of(table)(row_index())] = ref[...].astype(jnp.float32)
 
 
-def finish_kernel(mine_ref, arrived_ref, scores_hbm, out_hbm, total, copied):
-    del scores_hbm
-    rows = total.shape[0]
-    share = pl.ds(pl.multiple_of(lax.rem(layer_index(), 2) * rows, rows), rows)
-    total[...] = mine_ref[share, :].astype(jnp.float32) + arrived_ref[share, :].astype(jnp.float32)
-    copy = pltpu.make_async_copy(total, out_hbm.at[step_of(BLOCK_LAST)(row_index())], copied)
-    copy.start()
-    copy.wait()
-
-
 def finish(mine, arrived, scores):
-    hbm = pl.BlockSpec(memory_space=pltpu.HBM)
-    vmem = pl.BlockSpec(memory_space=pltpu.VMEM)
-    return pl.pallas_call(
-        finish_kernel,
-        out_shape=jax.ShapeDtypeStruct(scores.shape, scores.dtype),
-        in_specs=[vmem, vmem, hbm],
-        out_specs=hbm,
-        scratch_shapes=[pltpu.VMEM(scores.shape[1:], jnp.float32), pltpu.SemaphoreType.DMA],
-        input_output_aliases={2: 0},
-        compiler_params=pltpu.CompilerParams(vmem_limit_bytes=4 * MIB),
-    )(mine, arrived, scores)
+    rows = scores.shape[1]
+    first = layer_index() % 2 * rows
+    parts = [lax.dynamic_slice_in_dim(part, first, rows, 0).astype(jnp.float32) for part in (mine, arrived)]
+    step = step_of(BLOCK_LAST)(row_index())
+    return lax.dynamic_update_slice(scores, (parts[0] + parts[1])[None], (step, 0, 0))
 
 
 def along_line(documents, conditioned, query_ids):
@@ -262,7 +247,7 @@
 
     def one_half(block, block_of, kept):
         kernel = functools.partial(half_kernel, block_of, kept)
-        out_shape = [jax.ShapeDtypeStruct(half, jnp.float32)]
+        out_shape = [jax.ShapeDtypeStruct(half, jnp.float32 if kept else jnp.bfloat16)]
         return scoring(kernel, out_shape, conditioned, query_ids, block)[0]
 
     def back(total, table):

time: 51.8 us -> 51.7 us (level)
  Pallas kernels: 10.8 us -> 10.1 us
  other arithmetic: 0 us -> 0.64 us
    pallas_call x1 -> x0, Pallas kernels: 0.65 us -> none  [finish(): pl.pallas_call(finish_kernel, out_shape=jax.ShapeDtypeStruct(scores.shape...]
    dynamic_update_slice x0 -> x1, other arithmetic: none -> 0.64 us  [finish(): lax.dynamic_update_slice(scores, (parts[0] + parts[1])[None], (step, 0, 0))]
where the time goes in v15:
time: 51.7 us; the launch traced here: 51.5 us
  waiting for transfers between devices  24.3 us (47%)
  starting transfers between devices  14.6 us (28%)
  Pallas kernels  10.1 us (20%)
  local copies, waits for them, and re-layouts  1.74 us (3%)
  other arithmetic  0.64 us (1%)
    ppermute x6, waiting for transfers between devices, swap(): lax.ppermute(value, 'layer', [(lay, lay ^ distance) for lay in range(coun...  7.11 us
    pallas_call x1, Pallas kernels, prepare(): pl.pallas_call(prepare_kernel, out_shape=jax.ShapeDtypeStruct((rows, dims...  6.15 us
    ppermute x2, waiting for transfers between devices, back(): return lax.ppermute(total, 'rows', tuple(enumerate(table)))  4.65 us
    ppermute x1, waiting for transfers between devices, along_line(): two = lax.ppermute(later, 'rows', ROUND_TWO)  4.39 us
    ppermute x1, waiting for transfers between devices, along_line(): mine = lax.ppermute(both, ('rows', 'layer'), pairs)  4.19 us
    ppermute x1, starting transfers between devices, along_line(): one = lax.ppermute(documents, 'rows', ROUND_ONE)  4.04 us
    ppermute x1, waiting for transfers between devices, along_line(): one = lax.ppermute(documents, 'rows', ROUND_ONE)  3.93 us
    ppermute x6, starting transfers between devices, swap(): lax.ppermute(value, 'layer', [(lay, lay ^ distance) for lay in range(coun...  3.41 us
  transfers between devices with their start and end apart: 12, of which 10 were waited for; matrix products, arithmetic and copies ran while one was open for 0% of the time, Pallas kernels for 19%

profile of v15, /device:TPU:0, one launch (start us, length us, event | category | flops | bytes accessed | tf_op | source)
XLA Modules:
  0.0 51.5 jit_solution(1130859177572493962)
XLA Ops:
  0.0 0.0 copy-start.1
  0.0 0.0 copy-start.2
  0.0 4.0 %collective-permute-start = (bf16[128,2048]{1,0:T(8,128)(2,1)}, bf16[128,2048]{1,0:T(8,128)(2,1)S(1)}, u32[]{:S(2)}, u32[]{:S(2)}) collective-permute-start(bf16[128,2048]{1,0:T(8,128)(2,1)} %documents_ref), channel_id=1, source_target_pairs={{0,8},{8,12},{12,4},{4,0},{1,9},{9,13},{13,5},{5,1},{2,10},{10,14}... | collective-permute-start | bytes 1572872 | tf_op jit(solution)/shard_map/ppermute | solution.py:256
  4.0 6.2 %shard_map.64.queries_ref = bf16[512,2048]{1,0:T(8,128)(2,1)} custom-call(s32[4]{0:T(128)} %offsets.1, bf16[512,2048]{1,0:T(8,128)(2,1)} %queries_hbm.1, bf16[4,512,512]{2,1,0:T(8,128)(2,1)} %bases_hbm.1, f32[4,512]{1,0:T(4,128)} %values_hbm.1), custom_call_target="tpu_custom_call" | custom-call | flops 2147483648 | bytes 6291456 | tf_op jit(solution)/shard_map/pallas_call | solution.py:52
  10.2 0.0 copy-done.1
  10.2 0.1 collective-permute-start.4
  10.3 0.0 copy-done.2
  10.3 0.1 copy.8.ids_ref
  10.4 0.0 copy-start
  10.4 1.6 %copy-done = bf16[512,2048]{1,0:T(8,128)(2,1)S(1)} copy-done((bf16[512,2048]{1,0:T(8,128)(2,1)S(1)}, bf16[512,2048]{1,0:T(8,128)(2,1)}, u32[]{:S(2)}) %copy-start) | copy-done | bytes 2097176
  12.0 0.8 %shard_map.65 = (f32[256,128]{1,0:T(8,128)S(1)}, f32[256,128]{1,0:T(8,128)S(1)}) custom-call(bf16[512,2048]{1,0:T(8,128)(2,1)S(1)} %copy-done, s32[512,1]{1,0:T(8,128)S(1)} %copy.8.ids_ref, bf16[128,2048]{1,0:T(8,128)(2,1)S(1)} %copy-done.1), custom_call_target="tpu_custom_call" | custom-call | flops 268435456 | bytes 2621440 | tf_op jit(solution)/shard_map/pallas_call | solution.py:81
  12.8 3.9 %collective-permute-done.documents_ref = bf16[128,2048]{1,0:T(8,128)(2,1)S(1)} collective-permute-done((bf16[128,2048]{1,0:T(8,128)(2,1)}, bf16[128,2048]{1,0:T(8,128)(2,1)S(1)}, u32[]{:S(2)}, u32[]{:S(2)}) %collective-permute-start) | collective-permute-done | bytes 524320 | tf_op jit(solution)/shard_map/ppermute | solution.py:256
  16.7 0.8 %shard_map.66 = (f32[256,256]{1,0:T(8,128)S(1)}, f32[256,256]{1,0:T(8,128)S(1)}) custom-call(bf16[512,2048]{1,0:T(8,128)(2,1)S(1)} %copy-done, s32[512,1]{1,0:T(8,128)S(1)} %copy.8.ids_ref, bf16[128,2048]{1,0:T(8,128)(2,1)S(1)} %collective-permute-done.documents_ref, f32[256,128]{1,0:T(8,128)S(1)} %get-tuple-element.32.refs_0_, ...), custom_call_target="tpu_custom_call" | custom-call | flops 268435456 | bytes 2621440 | tf_op jit(solution)/shard_map/pallas_call | solution.py:81
  17.5 0.1 collective-permute-start.1
  17.6 3.3 %collective-permute-start.3 = (bf16[128,2048]{1,0:T(8,128)(2,1)S(1)}, bf16[128,2048]{1,0:T(8,128)(2,1)S(1)}, u32[]{:S(2)}, u32[]{:S(2)}) collective-permute-start(bf16[128,2048]{1,0:T(8,128)(2,1)S(1)} %collective-permute-done.documents_ref), channel_id=1, source_target_pairs={{0,8},{8,12},{12,4},{4,0},{1,9},{9,13},{13,5},{5,1},{2,10},{10,14}... | collective-permute-start | bytes 1572872 | tf_op jit(solution)/shard_map/ppermute | solution.py:261
  20.9 0.0 collective-permute-done.1.arrived_ref
  20.9 1.6 %collective-permute-start.2 = (bf16[128,256]{1,0:T(8,128)(2,1)S(1)}, bf16[128,256]{1,0:T(8,128)(2,1)S(1)}, u32[]{:S(2)}, u32[]{:S(2)}) collective-permute-start(bf16[128,256]{1,0:T(8,128)(2,1)S(1)} %get-tuple-element.37), channel_id=1, source_target_pairs={{0,2},{1,3},{2,0},{3,1},{4,6},{5,7},{6,4},{7,5},{8,10},{9,11},{10,... | collective-permute-start | bytes 196616 | tf_op jit(solution)/shard_map/ppermute | solution.py:186
  22.5 2.8 %collective-permute-done.2.arrived_ref = bf16[128,256]{1,0:T(8,128)(2,1)S(1)} collective-permute-done((bf16[128,256]{1,0:T(8,128)(2,1)S(1)}, bf16[128,256]{1,0:T(8,128)(2,1)S(1)}, u32[]{:S(2)}, u32[]{:S(2)}) %collective-permute-start.2) | collective-permute-done | bytes 65568 | tf_op jit(solution)/shard_map/ppermute | solution.py:186
  25.3 4.4 %collective-permute-done.4.documents_ref = bf16[128,2048]{1,0:T(8,128)(2,1)S(1)} collective-permute-done((bf16[128,2048]{1,0:T(8,128)(2,1)S(1)}, bf16[128,2048]{1,0:T(8,128)(2,1)S(1)}, u32[]{:S(2)}, u32[]{:S(2)}) %collective-permute-start.4) | collective-permute-done | bytes 524320 | tf_op jit(solution)/shard_map/ppermute | solution.py:258
  29.7 0.8 %shard_map.69 = (f32[256,128]{1,0:T(8,128)S(1)}, f32[256,128]{1,0:T(8,128)S(1)}) custom-call(bf16[512,2048]{1,0:T(8,128)(2,1)S(1)} %copy-done, s32[512,1]{1,0:T(8,128)S(1)} %copy.8.ids_ref, bf16[128,2048]{1,0:T(8,128)(2,1)S(1)} %collective-permute-done.4.documents_ref), custom_call_target="tpu_custom_call" | custom-call | flops 268435456 | bytes 2621440 | tf_op jit(solution)/shard_map/pallas_call | solution.py:81
  30.4 0.1 collective-permute-start.6
  30.5 1.3 %collective-permute-done.6.arrived_ref = f32[256,128]{1,0:T(8,128)S(1)} collective-permute-done((f32[256,128]{1,0:T(8,128)S(1)}, f32[256,128]{1,0:T(8,128)S(1)}, u32[]{:S(2)}, u32[]{:S(2)}) %collective-permute-start.6) | collective-permute-done | bytes 131104 | tf_op jit(solution)/shard_map/ppermute | solution.py:186
  31.9 1.6 %collective-permute-start.7 = (bf16[128,128]{1,0:T(8,128)(2,1)S(1)}, bf16[128,128]{1,0:T(8,128)(2,1)S(1)}, u32[]{:S(2)}, u32[]{:S(2)}) collective-permute-start(bf16[128,128]{1,0:T(8,128)(2,1)S(1)} %get-tuple-element.45), channel_id=1, source_target_pairs={{0,2},{1,3},{2,0},{3,1},{4,6},{5,7},{6,4},{7,5},{8,10},{9,11},{10,... | collective-permute-start | bytes 98312 | tf_op jit(solution)/shard_map/ppermute | solution.py:186
  33.4 0.7 %collective-permute-start.5 = (bf16[128,128]{1,0:T(8,128)(2,1)S(1)}, bf16[128,128]{1,0:T(8,128)(2,1)S(1)}, u32[]{:S(2)}, u32[]{:S(2)}) collective-permute-start(bf16[128,128]{1,0:T(8,128)(2,1)S(1)} %get-tuple-element.40), channel_id=1, source_target_pairs={{0,4},{4,12},{8,0},{12,8},{1,5},{5,13},{9,1},{13,9},{2,6},{6,14},{... | collective-permute-start | bytes 98312 | tf_op jit(solution)/shard_map/ppermute | solution.py:254
  34.1 1.7 %collective-permute-done.7.arrived_ref = bf16[128,128]{1,0:T(8,128)(2,1)S(1)} collective-permute-done((bf16[128,128]{1,0:T(8,128)(2,1)S(1)}, bf16[128,128]{1,0:T(8,128)(2,1)S(1)}, u32[]{:S(2)}, u32[]{:S(2)}) %collective-permute-start.7) | collective-permute-done | bytes 32800 | tf_op jit(solution)/shard_map/ppermute | solution.py:186
  35.9 0.6 %collective-permute-start.8 = (bf16[128,128]{1,0:T(8,128)(2,1)S(1)}, bf16[128,128]{1,0:T(8,128)(2,1)S(1)}, u32[]{:S(2)}, u32[]{:S(2)}) collective-permute-start(bf16[128,128]{1,0:T(8,128)(2,1)S(1)} %shard_map.71), channel_id=1, source_target_pairs={{0,8},{4,0},{8,12},{12,4},{1,9},{5,1},{9,13},{13,5},{2,10},{6,2},{... | collective-permute-start | bytes 98312 | tf_op jit(solution)/shard_map/ppermute | solution.py:254
  36.5 4.5 %collective-permute-done.5.first_ref = bf16[128,128]{1,0:T(8,128)(2,1)S(1)} collective-permute-done((bf16[128,128]{1,0:T(8,128)(2,1)S(1)}, bf16[128,128]{1,0:T(8,128)(2,1)S(1)}, u32[]{:S(2)}, u32[]{:S(2)}) %collective-permute-start.5) | collective-permute-done | bytes 32800 | tf_op jit(solution)/shard_map/ppermute | solution.py:254
  40.9 0.0 collective-permute-done.3.documents_ref
  40.9 0.2 collective-permute-done.8.second_ref
  41.1 0.4 shard_map.74
  41.6 0.2 collective-permute-start.9
  41.7 0.4 shard_map.73.refs_0_
  42.2 0.7 %collective-permute-done.9.refs_1_ = bf16[256,128]{1,0:T(8,128)(2,1)S(1)} collective-permute-done((bf16[256,128]{1,0:T(8,128)(2,1)S(1)}, bf16[256,128]{1,0:T(8,128)(2,1)S(1)}, u32[]{:S(2)}, u32[]{:S(2)}) %collective-permute-start.9) | collective-permute-done | bytes 65568 | tf_op jit(solution)/shard_map/ppermute | solution.py:186
  42.9 2.5 %collective-permute-start.10 = (bf16[256,128]{1,0:T(8,128)(2,1)S(1)}, bf16[256,128]{1,0:T(8,128)(2,1)S(1)}, u32[]{:S(2)}, u32[]{:S(2)}) collective-permute-start(bf16[256,128]{1,0:T(8,128)(2,1)S(1)} %shard_map.75), channel_id=1, source_target_pairs={{0,12},{1,15},{2,14},{3,13},{4,8},{5,11},{6,10},{7,9},{8,4},{9,7},... | collective-permute-start | bytes 196616 | tf_op jit(solution)/shard_map/ppermute | solution.py:279
  45.4 4.2 %collective-permute-done.10 = bf16[256,128]{1,0:T(8,128)(2,1)S(1)} collective-permute-done((bf16[256,128]{1,0:T(8,128)(2,1)S(1)}, bf16[256,128]{1,0:T(8,128)(2,1)S(1)}, u32[]{:S(2)}, u32[]{:S(2)}) %collective-permute-start.10) | collective-permute-done | bytes 65568 | tf_op jit(solution)/shard_map/ppermute | solution.py:279
  49.6 0.0 collective-permute-start.11
  49.6 0.7 %shard_map.72 = f32[4,128,128]{2,1,0:T(8,128)} custom-call(f32[128,128]{1,0:T(8,128)S(1)} %get-tuple-element.38.own_ref, bf16[128,128]{1,0:T(8,128)(2,1)S(1)} %collective-permute-done.5.first_ref, bf16[128,128]{1,0:T(8,128)(2,1)S(1)} %collective-permute-done.8.second_ref), custom_call_target="tpu_custom_call" | custom-call | tf_op jit(solution)/shard_map/pallas_call | solution.py:148
  50.3 0.5 %collective-permute-done.11 = bf16[256,128]{1,0:T(8,128)(2,1)S(1)} collective-permute-done((bf16[256,128]{1,0:T(8,128)(2,1)S(1)}, bf16[256,128]{1,0:T(8,128)(2,1)S(1)}, u32[]{:S(2)}, u32[]{:S(2)}) %collective-permute-start.11) | collective-permute-done | bytes 65568 | tf_op jit(solution)/shard_map/ppermute | solution.py:186
  50.9 0.6 %bitcast_dynamic-update-slice_fusion = f32[4,128,128]{2,1,0:T(8,128)} fusion(f32[4,128,128]{2,1,0:T(8,128)} %shard_map.72, s32[]{:T(128)S(6)} %select_n.25, bf16[256,128]{1,0:T(8,128)(2,1)S(1)} %collective-permute-done.11, s32[]{:T(128)S(6)} %select_n.22, bf16[256,128]{1,0:T(8,128)(2,1)S(1)} %collective-permute-done.10), kind=kLoop, calls=%fused_computation | loop fusion | flops 49152 | bytes 131080 | tf_op jit(solution)/shard_map/dynamic_update_slice | solution.py:234
  (5 shorter events, 0.1 us)
Async XLA Ops:
  0.0 10.2 %copy-start.1 = (bf16[128,2048]{1,0:T(8,128)(2,1)S(1)}, bf16[128,2048]{1,0:T(8,128)(2,1)}, u32[]{:S(2)}) copy-start(bf16[128,2048]{1,0:T(8,128)(2,1)} %documents_ref) | copy-start | bytes 1572868
  0.0 10.3 %copy-start.2 = (s32[512]{0:T(512)S(1)}, s32[512]{0:T(512)}, u32[]{:S(2)}) copy-start(s32[512]{0:T(512)} %param.11) | copy-start | bytes 6148
  0.0 16.7 %collective-permute-start = (bf16[128,2048]{1,0:T(8,128)(2,1)}, bf16[128,2048]{1,0:T(8,128)(2,1)S(1)}, u32[]{:S(2)}, u32[]{:S(2)}) collective-permute-start(bf16[128,2048]{1,0:T(8,128)(2,1)} %documents_ref), channel_id=1, source_target_pairs={{0,8},{8,12},{12,4},{4,0},{1,9},{9,13},{13,5},{5,1},{2,10},{10,14}... | collective-permute-start | bytes 1572872 | tf_op jit(solution)/shard_map/ppermute | solution.py:256
  10.2 19.5 %collective-permute-start.4 = (bf16[128,2048]{1,0:T(8,128)(2,1)S(1)}, bf16[128,2048]{1,0:T(8,128)(2,1)S(1)}, u32[]{:S(2)}, u32[]{:S(2)}) collective-permute-start(bf16[128,2048]{1,0:T(8,128)(2,1)S(1)} %copy-done.1), channel_id=1, source_target_pairs={{0,4},{4,12},{12,8},{8,0},{1,5},{5,13},{13,9},{9,1},{2,6},{6,14},{... | collective-permute-start | bytes 1572872 | tf_op jit(solution)/shard_map/ppermute | solution.py:258
  10.4 1.6 %copy-start = (bf16[512,2048]{1,0:T(8,128)(2,1)S(1)}, bf16[512,2048]{1,0:T(8,128)(2,1)}, u32[]{:S(2)}) copy-start(bf16[512,2048]{1,0:T(8,128)(2,1)} %shard_map.64.queries_ref) | copy-start | bytes 6291460
  17.5 3.4 %collective-permute-start.1 = (f32[256,256]{1,0:T(8,128)S(1)}, f32[256,256]{1,0:T(8,128)S(1)}, u32[]{:S(2)}, u32[]{:S(2)}) collective-permute-start(f32[256,256]{1,0:T(8,128)S(1)} %get-tuple-element.35), channel_id=1, source_target_pairs={{0,1},{1,0},{2,3},{3,2},{4,5},{5,4},{6,7},{7,6},{8,9},{9,8},{10,11... | collective-permute-start | bytes 786440 | tf_op jit(solution)/shard_map/ppermute | solution.py:186
  17.6 23.4 %collective-permute-start.3 = (bf16[128,2048]{1,0:T(8,128)(2,1)S(1)}, bf16[128,2048]{1,0:T(8,128)(2,1)S(1)}, u32[]{:S(2)}, u32[]{:S(2)}) collective-permute-start(bf16[128,2048]{1,0:T(8,128)(2,1)S(1)} %collective-permute-done.documents_ref), channel_id=1, source_target_pairs={{0,8},{8,12},{12,4},{4,0},{1,9},{9,13},{13,5},{5,1},{2,10},{10,14}... | collective-permute-start | bytes 1572872 | tf_op jit(solution)/shard_map/ppermute | solution.py:261
  20.9 4.3 %collective-permute-start.2 = (bf16[128,256]{1,0:T(8,128)(2,1)S(1)}, bf16[128,256]{1,0:T(8,128)(2,1)S(1)}, u32[]{:S(2)}, u32[]{:S(2)}) collective-permute-start(bf16[128,256]{1,0:T(8,128)(2,1)S(1)} %get-tuple-element.37), channel_id=1, source_target_pairs={{0,2},{1,3},{2,0},{3,1},{4,6},{5,7},{6,4},{7,5},{8,10},{9,11},{10,... | collective-permute-start | bytes 196616 | tf_op jit(solution)/shard_map/ppermute | solution.py:186
  30.4 1.4 %collective-permute-start.6 = (f32[256,128]{1,0:T(8,128)S(1)}, f32[256,128]{1,0:T(8,128)S(1)}, u32[]{:S(2)}, u32[]{:S(2)}) collective-permute-start(f32[256,128]{1,0:T(8,128)S(1)} %get-tuple-element.43), channel_id=1, source_target_pairs={{0,1},{1,0},{2,3},{3,2},{4,5},{5,4},{6,7},{7,6},{8,9},{9,8},{10,11... | collective-permute-start | bytes 393224 | tf_op jit(solution)/shard_map/ppermute | solution.py:186
  31.9 4.0 %collective-permute-start.7 = (bf16[128,128]{1,0:T(8,128)(2,1)S(1)}, bf16[128,128]{1,0:T(8,128)(2,1)S(1)}, u32[]{:S(2)}, u32[]{:S(2)}) collective-permute-start(bf16[128,128]{1,0:T(8,128)(2,1)S(1)} %get-tuple-element.45), channel_id=1, source_target_pairs={{0,2},{1,3},{2,0},{3,1},{4,6},{5,7},{6,4},{7,5},{8,10},{9,11},{10,... | collective-permute-start | bytes 98312 | tf_op jit(solution)/shard_map/ppermute | solution.py:186
  33.4 7.5 %collective-permute-start.5 = (bf16[128,128]{1,0:T(8,128)(2,1)S(1)}, bf16[128,128]{1,0:T(8,128)(2,1)S(1)}, u32[]{:S(2)}, u32[]{:S(2)}) collective-permute-start(bf16[128,128]{1,0:T(8,128)(2,1)S(1)} %get-tuple-element.40), channel_id=1, source_target_pairs={{0,4},{4,12},{8,0},{12,8},{1,5},{5,13},{9,1},{13,9},{2,6},{6,14},{... | collective-permute-start | bytes 98312 | tf_op jit(solution)/shard_map/ppermute | solution.py:254
  35.9 5.3 %collective-permute-start.8 = (bf16[128,128]{1,0:T(8,128)(2,1)S(1)}, bf16[128,128]{1,0:T(8,128)(2,1)S(1)}, u32[]{:S(2)}, u32[]{:S(2)}) collective-permute-start(bf16[128,128]{1,0:T(8,128)(2,1)S(1)} %shard_map.71), channel_id=1, source_target_pairs={{0,8},{4,0},{8,12},{12,4},{1,9},{5,1},{9,13},{13,5},{2,10},{6,2},{... | collective-permute-start | bytes 98312 | tf_op jit(solution)/shard_map/ppermute | solution.py:254
  41.6 1.3 %collective-permute-start.9 = (bf16[256,128]{1,0:T(8,128)(2,1)S(1)}, bf16[256,128]{1,0:T(8,128)(2,1)S(1)}, u32[]{:S(2)}, u32[]{:S(2)}) collective-permute-start(bf16[256,128]{1,0:T(8,128)(2,1)S(1)} %shard_map.74), channel_id=1, source_target_pairs={{0,1},{1,0},{2,3},{3,2},{4,5},{5,4},{6,7},{7,6},{8,9},{9,8},{10,11... | collective-permute-start | bytes 196616 | tf_op jit(solution)/shard_map/ppermute | solution.py:186
  42.9 6.7 %collective-permute-start.10 = (bf16[256,128]{1,0:T(8,128)(2,1)S(1)}, bf16[256,128]{1,0:T(8,128)(2,1)S(1)}, u32[]{:S(2)}, u32[]{:S(2)}) collective-permute-start(bf16[256,128]{1,0:T(8,128)(2,1)S(1)} %shard_map.75), channel_id=1, source_target_pairs={{0,12},{1,15},{2,14},{3,13},{4,8},{5,11},{6,10},{7,9},{8,4},{9,7},... | collective-permute-start | bytes 196616 | tf_op jit(solution)/shard_map/ppermute | solution.py:279
  49.6 1.3 %collective-permute-start.11 = (bf16[256,128]{1,0:T(8,128)(2,1)S(1)}, bf16[256,128]{1,0:T(8,128)(2,1)S(1)}, u32[]{:S(2)}, u32[]{:S(2)}) collective-permute-start(bf16[256,128]{1,0:T(8,128)(2,1)S(1)} %collective-permute-done.10), channel_id=1, source_target_pairs={{0,1},{1,0},{2,3},{3,2},{4,5},{5,4},{6,7},{7,6},{8,9},{9,8},{10,11... | collective-permute-start | bytes 196616 | tf_op jit(solution)/shard_map/ppermute | solution.py:186

commit v16 on v14

--- a/solution.py
+++ b/solution.py
@@ -73,22 +73,22 @@
     return jnp.where(query_ids == doc_ids, 0.0, tile)
 
 
-def scoring(kernel, out_shape, conditioned, query_ids, documents, extra=(), scratch=()):
+def scoring(kernel, out_shape, conditioned, query_ids, *documents, extra=(), scratch=()):
     dims = conditioned.shape[1]
-    docs = documents.shape[0]
+    docs = sum(part.shape[0] for part in documents)
     rows = sum(shape.shape[0] for shape in out_shape)
     vmem = pl.BlockSpec(memory_space=pltpu.VMEM)
     return pl.pallas_call(
         kernel,
         out_shape=out_shape,
-        in_specs=[vmem] * (3 + len(extra)),
+        in_specs=[vmem] * (2 + len(documents) + len(extra)),
         out_specs=[vmem] * len(out_shape),
         scratch_shapes=scratch,
         compiler_params=pltpu.CompilerParams(vmem_limit_bytes=12 * MIB),
         cost_estimate=pl.CostEstimate(
             flops=2 * rows * docs * dims, bytes_accessed=2 * dims * (rows + docs), transcendentals=0
         ),
-    )(conditioned, query_ids, documents, *extra)
+    )(conditioned, query_ids, *documents, *extra)
 
 
 def turned_kernel(shares, block_of, queries_ref, ids_ref, documents_ref, *refs):
@@ -124,11 +124,12 @@
     return jnp.where(chip == core, 0, 1)
 
 
-def half_kernel(block_of, kept, queries_ref, ids_ref, documents_ref, out_ref):
+def half_kernel(block_of, kept, queries_ref, ids_ref, lower_ref, upper_ref, out_ref):
+    documents = jnp.concatenate([lower_ref[...], upper_ref[...]], axis=0)
     rows = out_ref.shape[0]
     chip = target_chip() if kept else 1 - target_chip()
     spot = pl.ds(pl.multiple_of(chip * rows, rows), rows)
-    out_ref[...] = masked_tile(queries_ref[spot, :], documents_ref[...], ids_ref[spot, :], block_of(row_index()))
+    out_ref[...] = masked_tile(queries_ref[spot, :], documents, ids_ref[spot, :], block_of(row_index()))
 
 
 def total_of(refs):
@@ -258,12 +259,12 @@
         out_shape = [jax.ShapeDtypeStruct((half[0], width), jnp.float32)] * 2
         scratch = [pltpu.VMEM((2 * half[0], docs), jnp.float32)]
         kernel = functools.partial(halves_kernel, block_of)
-        return scoring(kernel, out_shape, conditioned, query_ids, block, front, scratch)
-
-    def one_half(block, block_of, kept):
+        return scoring(kernel, out_shape, conditioned, query_ids, block, extra=front, scratch=scratch)
+
+    def one_half(parts, block_of, kept):
         kernel = functools.partial(half_kernel, block_of, kept)
         out_shape = [jax.ShapeDtypeStruct(half, jnp.float32)]
-        return scoring(kernel, out_shape, conditioned, query_ids, block)[0]
+        return scoring(kernel, out_shape, conditioned, query_ids, *parts)[0]
 
     def back(total, table):
         return lax.ppermute(total, "rows", tuple(enumerate(table)))
@@ -273,7 +274,9 @@
     two = lax.ppermute(later, "rows", ROUND_TWO)
     own = halves(later, lambda row: row)
     one, own = lax.optimization_barrier((one, own))
-    three = lax.ppermute(one, "rows", ROUND_ONE)
+    three = [
+        lax.ppermute(part, "rows", ROUND_ONE) for part in (one[: docs * 3 // 4], one[docs * 3 // 4 :])
+    ]
 
     own, first = layer_sum(*halves(one, pick(BLOCK_ONE), own), (jnp.float32, jnp.bfloat16))
     two, first = lax.optimization_barrier((two, first))
@@ -311,7 +314,7 @@
         kernel = functools.partial(turned_kernel, shares, ahead)
         out_shape = [jax.ShapeDtypeStruct((rows // shares, docs), jnp.bfloat16)] * shares
         scratch = [pltpu.VMEM((rows, docs), jnp.float32)]
-        total = direct_sum(scoring(kernel, out_shape, conditioned, query_ids, block, (), scratch))
+        total = direct_sum(scoring(kernel, out_shape, conditioned, query_ids, block, scratch=scratch))
         onward = [(row, (row + step) % n_rows) for row in range(n_rows)]
         result.append(lax.ppermute(total, "rows", onward) if step else total)
     return jnp.stack(result)

time: 51.8 us -> 51.8 us (level)
  starting transfers between devices: 14.6 us -> 16.6 us
  waiting for transfers between devices: 24.4 us -> 22.4 us
    ppermute x2, waiting for transfers between devices: 4.65 us -> 1 us  [back(): return lax.ppermute(total, 'rows', tuple(enumerate(table)))]
    ppermute x1 -> x2, waiting for transfers between devices: 0.01 us -> 2.44 us  [along_line(): lax.ppermute(part, 'rows', ROUND_ONE)]
    ppermute x2, starting transfers between devices: 1.29 us -> 2.59 us  [back(): return lax.ppermute(total, 'rows', tuple(enumerate(table)))]
    ppermute x6, waiting for transfers between devices: 7.21 us -> 6.47 us  [swap(): lax.ppermute(value, 'layer', [(lay, lay ^ distance) for lay in range(coun...]
    ppermute x1 -> x2, starting transfers between devices: 3.33 us -> 3.94 us  [along_line(): lax.ppermute(part, 'rows', ROUND_ONE)]
    unnamed x6 -> x8, local copies, waits for them, and re-layouts: 1.6 us -> 1.6 us
  transfers between devices with their start and end apart: 12 -> 13, of which waited for: 10 -> 11; matrix products, arithmetic and copies ran while one was open for 0% -> 0% of each run, Pallas kernels for 19% -> 19%
where the time goes in v16:
time: 51.8 us; the launch traced here: 51.6 us
  waiting for transfers between devices  22.4 us (43%)
  starting transfers between devices  16.6 us (32%)
  Pallas kernels  10.7 us (21%)
  local copies, waits for them, and re-layouts  1.78 us (3%)
    ppermute x6, waiting for transfers between devices, swap(): lax.ppermute(value, 'layer', [(lay, lay ^ distance) for lay in range(coun...  6.47 us
    pallas_call x1, Pallas kernels, prepare(): pl.pallas_call(prepare_kernel, out_shape=jax.ShapeDtypeStruct((rows, dims...  6.14 us
    ppermute x1, waiting for transfers between devices, along_line(): two = lax.ppermute(later, 'rows', ROUND_TWO)  4.35 us
    ppermute x1, waiting for transfers between devices, along_line(): mine = lax.ppermute(both, ('rows', 'layer'), pairs)  4.2 us
    ppermute x1, starting transfers between devices, along_line(): one = lax.ppermute(documents, 'rows', ROUND_ONE)  4.04 us
    ppermute x2, starting transfers between devices, along_line(): lax.ppermute(part, 'rows', ROUND_ONE)  3.94 us
    ppermute x1, waiting for transfers between devices, along_line(): one = lax.ppermute(documents, 'rows', ROUND_ONE)  3.94 us
    ppermute x6, starting transfers between devices, swap(): lax.ppermute(value, 'layer', [(lay, lay ^ distance) for lay in range(coun...  3.42 us
  transfers between devices with their start and end apart: 13, of which 11 were waited for; matrix products, arithmetic and copies ran while one was open for 0% of the time, Pallas kernels for 19%

profile of v16, /device:TPU:0, one launch (start us, length us, event | category | flops | bytes accessed | tf_op | source)
XLA Modules:
  0.0 51.6 jit_solution(6728440083909313022)
XLA Ops:
  0.0 0.0 copy-start.2
  0.0 0.0 copy-start.3
  0.0 4.0 %collective-permute-start = (bf16[128,2048]{1,0:T(8,128)(2,1)}, bf16[128,2048]{1,0:T(8,128)(2,1)S(1)}, u32[]{:S(2)}, u32[]{:S(2)}) collective-permute-start(bf16[128,2048]{1,0:T(8,128)(2,1)} %documents_ref), channel_id=1, source_target_pairs={{0,8},{8,12},{12,4},{4,0},{1,9},{9,13},{13,5},{5,1},{2,10},{10,14}... | collective-permute-start | bytes 1572872 | tf_op jit(solution)/shard_map/ppermute | solution.py:272
  4.0 6.1 %shard_map.64.queries_ref = bf16[512,2048]{1,0:T(8,128)(2,1)} custom-call(s32[4]{0:T(128)} %offsets.1, bf16[512,2048]{1,0:T(8,128)(2,1)} %queries_hbm.1, bf16[4,512,512]{2,1,0:T(8,128)(2,1)} %bases_hbm.1, f32[4,512]{1,0:T(4,128)} %values_hbm.1), custom_call_target="tpu_custom_call" | custom-call | flops 2147483648 | bytes 6291456 | tf_op jit(solution)/shard_map/pallas_call | solution.py:52
  10.2 0.0 copy-done.2
  10.2 0.1 collective-permute-start.3
  10.3 0.0 copy-done.3
  10.3 0.1 copy.11.ids_ref
  10.4 0.0 copy-start
  10.4 1.6 %copy-done = bf16[512,2048]{1,0:T(8,128)(2,1)S(1)} copy-done((bf16[512,2048]{1,0:T(8,128)(2,1)S(1)}, bf16[512,2048]{1,0:T(8,128)(2,1)}, u32[]{:S(2)}) %copy-start) | copy-done | bytes 2097176
  12.0 0.8 %shard_map.65 = (f32[256,128]{1,0:T(8,128)S(1)}, f32[256,128]{1,0:T(8,128)S(1)}) custom-call(bf16[512,2048]{1,0:T(8,128)(2,1)S(1)} %copy-done, s32[512,1]{1,0:T(8,128)S(1)} %copy.11.ids_ref, bf16[128,2048]{1,0:T(8,128)(2,1)S(1)} %copy-done.2), custom_call_target="tpu_custom_call" | custom-call | flops 268435456 | bytes 2621440 | tf_op jit(solution)/shard_map/pallas_call | solution.py:81
  12.8 3.9 %collective-permute-done.documents_ref = bf16[128,2048]{1,0:T(8,128)(2,1)S(1)} collective-permute-done((bf16[128,2048]{1,0:T(8,128)(2,1)}, bf16[128,2048]{1,0:T(8,128)(2,1)S(1)}, u32[]{:S(2)}, u32[]{:S(2)}) %collective-permute-start) | collective-permute-done | bytes 524320 | tf_op jit(solution)/shard_map/ppermute | solution.py:272
  16.7 0.0 copy-start.1
  16.7 0.8 %shard_map.66 = (f32[256,256]{1,0:T(8,128)S(1)}, f32[256,256]{1,0:T(8,128)S(1)}) custom-call(bf16[512,2048]{1,0:T(8,128)(2,1)S(1)} %copy-done, s32[512,1]{1,0:T(8,128)S(1)} %copy.11.ids_ref, bf16[128,2048]{1,0:T(8,128)(2,1)S(1)} %collective-permute-done.documents_ref, f32[256,128]{1,0:T(8,128)S(1)} %get-tuple-element.33.refs_0_, ...), custom_call_target="tpu_custom_call" | custom-call | flops 268435456 | bytes 2621440 | tf_op jit(solution)/shard_map/pallas_call | solution.py:81
  17.5 0.1 collective-permute-start.4
  17.6 3.3 %collective-permute-start.1 = (bf16[96,2048]{1,0:T(8,128)(2,1)S(1)}, bf16[96,2048]{1,0:T(8,128)(2,1)S(1)}, u32[]{:S(2)}, u32[]{:S(2)}) collective-permute-start(bf16[96,2048]{1,0:T(8,128)(2,1)S(1)} %slice.6), channel_id=1, source_target_pairs={{0,8},{8,12},{12,4},{4,0},{1,9},{9,13},{13,5},{5,1},{2,10},{10,14}... | collective-permute-start | bytes 1179656 | tf_op jit(solution)/shard_map/ppermute | solution.py:278
  20.9 0.0 collective-permute-done.4.arrived_ref
  21.0 1.6 %collective-permute-start.5 = (bf16[128,256]{1,0:T(8,128)(2,1)S(1)}, bf16[128,256]{1,0:T(8,128)(2,1)S(1)}, u32[]{:S(2)}, u32[]{:S(2)}) collective-permute-start(bf16[128,256]{1,0:T(8,128)(2,1)S(1)} %get-tuple-element.38), channel_id=1, source_target_pairs={{0,2},{1,3},{2,0},{3,1},{4,6},{5,7},{6,4},{7,5},{8,10},{9,11},{10,... | collective-permute-start | bytes 196616 | tf_op jit(solution)/shard_map/ppermute | solution.py:186
  22.5 2.8 %collective-permute-done.5.arrived_ref = bf16[128,256]{1,0:T(8,128)(2,1)S(1)} collective-permute-done((bf16[128,256]{1,0:T(8,128)(2,1)S(1)}, bf16[128,256]{1,0:T(8,128)(2,1)S(1)}, u32[]{:S(2)}, u32[]{:S(2)}) %collective-permute-start.5) | collective-permute-done | bytes 65568 | tf_op jit(solution)/shard_map/ppermute | solution.py:186
  25.3 4.4 %collective-permute-done.3.documents_ref = bf16[128,2048]{1,0:T(8,128)(2,1)S(1)} collective-permute-done((bf16[128,2048]{1,0:T(8,128)(2,1)S(1)}, bf16[128,2048]{1,0:T(8,128)(2,1)S(1)}, u32[]{:S(2)}, u32[]{:S(2)}) %collective-permute-start.3) | collective-permute-done | bytes 524320 | tf_op jit(solution)/shard_map/ppermute | solution.py:274
  29.7 0.0 copy-done.1
  29.7 0.8 %shard_map.69 = (f32[256,128]{1,0:T(8,128)S(1)}, f32[256,128]{1,0:T(8,128)S(1)}) custom-call(bf16[512,2048]{1,0:T(8,128)(2,1)S(1)} %copy-done.1, s32[512,1]{1,0:T(8,128)S(1)} %copy.11.ids_ref, bf16[128,2048]{1,0:T(8,128)(2,1)S(1)} %collective-permute-done.3.documents_ref), custom_call_target="tpu_custom_call" | custom-call | flops 268435456 | bytes 2621440 | tf_op jit(solution)/shard_map/pallas_call | solution.py:81
  30.4 0.1 collective-permute-start.7
  30.5 0.6 %collective-permute-start.2 = (bf16[32,2048]{1,0:T(8,128)(2,1)S(1)}, bf16[32,2048]{1,0:T(8,128)(2,1)S(1)}, u32[]{:S(2)}, u32[]{:S(2)}) collective-permute-start(bf16[32,2048]{1,0:T(8,128)(2,1)S(1)} %slice.7), channel_id=1, source_target_pairs={{0,8},{8,12},{12,4},{4,0},{1,9},{9,13},{13,5},{5,1},{2,10},{10,14}... | collective-permute-start | bytes 393224 | tf_op jit(solution)/shard_map/ppermute | solution.py:278
  31.2 0.7 %collective-permute-done.7.arrived_ref = f32[256,128]{1,0:T(8,128)S(1)} collective-permute-done((f32[256,128]{1,0:T(8,128)S(1)}, f32[256,128]{1,0:T(8,128)S(1)}, u32[]{:S(2)}, u32[]{:S(2)}) %collective-permute-start.7) | collective-permute-done | bytes 131104 | tf_op jit(solution)/shard_map/ppermute | solution.py:186
  31.9 1.6 %collective-permute-start.8 = (bf16[128,128]{1,0:T(8,128)(2,1)S(1)}, bf16[128,128]{1,0:T(8,128)(2,1)S(1)}, u32[]{:S(2)}, u32[]{:S(2)}) collective-permute-start(bf16[128,128]{1,0:T(8,128)(2,1)S(1)} %get-tuple-element.45), channel_id=1, source_target_pairs={{0,2},{1,3},{2,0},{3,1},{4,6},{5,7},{6,4},{7,5},{8,10},{9,11},{10,... | collective-permute-start | bytes 98312 | tf_op jit(solution)/shard_map/ppermute | solution.py:186
  33.4 0.8 %collective-permute-start.6 = (bf16[128,128]{1,0:T(8,128)(2,1)S(1)}, bf16[128,128]{1,0:T(8,128)(2,1)S(1)}, u32[]{:S(2)}, u32[]{:S(2)}) collective-permute-start(bf16[128,128]{1,0:T(8,128)(2,1)S(1)} %get-tuple-element.40), channel_id=1, source_target_pairs={{0,4},{4,12},{8,0},{12,8},{1,5},{5,13},{9,1},{13,9},{2,6},{6,14},{... | collective-permute-start | bytes 98312 | tf_op jit(solution)/shard_map/ppermute | solution.py:270
  34.2 1.7 %collective-permute-done.8.arrived_ref = bf16[128,128]{1,0:T(8,128)(2,1)S(1)} collective-permute-done((bf16[128,128]{1,0:T(8,128)(2,1)S(1)}, bf16[128,128]{1,0:T(8,128)(2,1)S(1)}, u32[]{:S(2)}, u32[]{:S(2)}) %collective-permute-start.8) | collective-permute-done | bytes 32800 | tf_op jit(solution)/shard_map/ppermute | solution.py:186
  35.9 1.8 %collective-permute-start.9 = (bf16[128,128]{1,0:T(8,128)(2,1)S(1)}, bf16[128,128]{1,0:T(8,128)(2,1)S(1)}, u32[]{:S(2)}, u32[]{:S(2)}) collective-permute-start(bf16[128,128]{1,0:T(8,128)(2,1)S(1)} %shard_map.71), channel_id=1, source_target_pairs={{0,8},{4,0},{8,12},{12,4},{1,9},{5,1},{9,13},{13,5},{2,10},{6,2},{... | collective-permute-start | bytes 98312 | tf_op jit(solution)/shard_map/ppermute | solution.py:270
  37.7 2.4 %collective-permute-done.2.upper_ref = bf16[32,2048]{1,0:T(8,128)(2,1)S(1)} collective-permute-done((bf16[32,2048]{1,0:T(8,128)(2,1)S(1)}, bf16[32,2048]{1,0:T(8,128)(2,1)S(1)}, u32[]{:S(2)}, u32[]{:S(2)}) %collective-permute-start.2) | collective-permute-done | bytes 131104 | tf_op jit(solution)/shard_map/ppermute | solution.py:278
  40.1 0.8 %collective-permute-done.6.first_ref = bf16[128,128]{1,0:T(8,128)(2,1)S(1)} collective-permute-done((bf16[128,128]{1,0:T(8,128)(2,1)S(1)}, bf16[128,128]{1,0:T(8,128)(2,1)S(1)}, u32[]{:S(2)}, u32[]{:S(2)}) %collective-permute-start.6) | collective-permute-done | bytes 32800 | tf_op jit(solution)/shard_map/ppermute | solution.py:270
  40.9 0.0 collective-permute-done.1.lower_ref
  40.9 0.2 collective-permute-done.9.second_ref
  41.1 0.4 shard_map.73
  41.6 0.2 collective-permute-start.10
  41.7 0.4 shard_map.72.refs_0_
  42.2 0.8 %collective-permute-done.10.refs_1_ = f32[256,128]{1,0:T(8,128)S(1)} collective-permute-done((f32[256,128]{1,0:T(8,128)S(1)}, f32[256,128]{1,0:T(8,128)S(1)}, u32[]{:S(2)}, u32[]{:S(2)}) %collective-permute-start.10) | collective-permute-done | bytes 131104 | tf_op jit(solution)/shard_map/ppermute | solution.py:186
  43.0 2.5 %collective-permute-start.11 = (bf16[256,128]{1,0:T(8,128)(2,1)S(1)}, bf16[256,128]{1,0:T(8,128)(2,1)S(1)}, u32[]{:S(2)}, u32[]{:S(2)}) collective-permute-start(bf16[256,128]{1,0:T(8,128)(2,1)S(1)} %shard_map.74), channel_id=1, source_target_pairs={{0,12},{1,15},{2,14},{3,13},{4,8},{5,11},{6,10},{7,9},{8,4},{9,7},... | collective-permute-start | bytes 196616 | tf_op jit(solution)/shard_map/ppermute | solution.py:297
  45.5 4.2 %collective-permute-done.11.mine_ref = bf16[256,128]{1,0:T(8,128)(2,1)S(1)} collective-permute-done((bf16[256,128]{1,0:T(8,128)(2,1)S(1)}, bf16[256,128]{1,0:T(8,128)(2,1)S(1)}, u32[]{:S(2)}, u32[]{:S(2)}) %collective-permute-start.11) | collective-permute-done | bytes 65568 | tf_op jit(solution)/shard_map/ppermute | solution.py:297
  49.7 0.0 collective-permute-start.12
  49.7 0.7 %shard_map.75.scores_hbm = f32[4,128,128]{2,1,0:T(8,128)} custom-call(f32[128,128]{1,0:T(8,128)S(1)} %get-tuple-element.48.own_ref, bf16[128,128]{1,0:T(8,128)(2,1)S(1)} %collective-permute-done.6.first_ref, bf16[128,128]{1,0:T(8,128)(2,1)S(1)} %collective-permute-done.9.second_ref), custom_call_target="tpu_custom_call" | custom-call | tf_op jit(solution)/shard_map/pallas_call | solution.py:148
  50.4 0.5 %collective-permute-done.12.arrived_ref = bf16[256,128]{1,0:T(8,128)(2,1)S(1)} collective-permute-done((bf16[256,128]{1,0:T(8,128)(2,1)S(1)}, bf16[256,128]{1,0:T(8,128)(2,1)S(1)}, u32[]{:S(2)}, u32[]{:S(2)}) %collective-permute-start.12) | collective-permute-done | bytes 65568 | tf_op jit(solution)/shard_map/ppermute | solution.py:186
  51.0 0.6 %shard_map.76 = f32[4,128,128]{2,1,0:T(8,128)} custom-call(bf16[256,128]{1,0:T(8,128)(2,1)S(1)} %collective-permute-done.11.mine_ref, bf16[256,128]{1,0:T(8,128)(2,1)S(1)} %collective-permute-done.12.arrived_ref, f32[4,128,128]{2,1,0:T(8,128)} %shard_map.75.scores_hbm), custom_call_target="tpu_custom_call", output_to_operand_aliasing={{}: (2, {})} | custom-call | tf_op jit(solution)/shard_map/pallas_call | solution.py:242
  (7 shorter events, 0.1 us)
Async XLA Ops:
  0.0 10.2 %copy-start.2 = (bf16[128,2048]{1,0:T(8,128)(2,1)S(1)}, bf16[128,2048]{1,0:T(8,128)(2,1)}, u32[]{:S(2)}) copy-start(bf16[128,2048]{1,0:T(8,128)(2,1)} %documents_ref) | copy-start | bytes 1572868
  0.0 10.3 %copy-start.3 = (s32[512]{0:T(512)S(1)}, s32[512]{0:T(512)}, u32[]{:S(2)}) copy-start(s32[512]{0:T(512)} %param.11) | copy-start | bytes 6148
  0.0 16.7 %collective-permute-start = (bf16[128,2048]{1,0:T(8,128)(2,1)}, bf16[128,2048]{1,0:T(8,128)(2,1)S(1)}, u32[]{:S(2)}, u32[]{:S(2)}) collective-permute-start(bf16[128,2048]{1,0:T(8,128)(2,1)} %documents_ref), channel_id=1, source_target_pairs={{0,8},{8,12},{12,4},{4,0},{1,9},{9,13},{13,5},{5,1},{2,10},{10,14}... | collective-permute-start | bytes 1572872 | tf_op jit(solution)/shard_map/ppermute | solution.py:272
  10.2 19.5 %collective-permute-start.3 = (bf16[128,2048]{1,0:T(8,128)(2,1)S(1)}, bf16[128,2048]{1,0:T(8,128)(2,1)S(1)}, u32[]{:S(2)}, u32[]{:S(2)}) collective-permute-start(bf16[128,2048]{1,0:T(8,128)(2,1)S(1)} %copy-done.2), channel_id=1, source_target_pairs={{0,4},{4,12},{12,8},{8,0},{1,5},{5,13},{13,9},{9,1},{2,6},{6,14},{... | collective-permute-start | bytes 1572872 | tf_op jit(solution)/shard_map/ppermute | solution.py:274
  10.4 1.6 %copy-start = (bf16[512,2048]{1,0:T(8,128)(2,1)S(1)}, bf16[512,2048]{1,0:T(8,128)(2,1)}, u32[]{:S(2)}) copy-start(bf16[512,2048]{1,0:T(8,128)(2,1)} %shard_map.64.queries_ref) | copy-start | bytes 6291460
  16.7 12.9 %copy-start.1 = (bf16[512,2048]{1,0:T(8,128)(2,1)S(1)}, bf16[512,2048]{1,0:T(8,128)(2,1)}, u32[]{:S(2)}) copy-start(bf16[512,2048]{1,0:T(8,128)(2,1)} %shard_map.64.queries_ref) | copy-start | bytes 6291460
  17.5 3.4 %collective-permute-start.4 = (f32[256,256]{1,0:T(8,128)S(1)}, f32[256,256]{1,0:T(8,128)S(1)}, u32[]{:S(2)}, u32[]{:S(2)}) collective-permute-start(f32[256,256]{1,0:T(8,128)S(1)} %get-tuple-element.36), channel_id=1, source_target_pairs={{0,1},{1,0},{2,3},{3,2},{4,5},{5,4},{6,7},{7,6},{8,9},{9,8},{10,11... | collective-permute-start | bytes 786440 | tf_op jit(solution)/shard_map/ppermute | solution.py:186
  17.6 23.3 %collective-permute-start.1 = (bf16[96,2048]{1,0:T(8,128)(2,1)S(1)}, bf16[96,2048]{1,0:T(8,128)(2,1)S(1)}, u32[]{:S(2)}, u32[]{:S(2)}) collective-permute-start(bf16[96,2048]{1,0:T(8,128)(2,1)S(1)} %slice.6), channel_id=1, source_target_pairs={{0,8},{8,12},{12,4},{4,0},{1,9},{9,13},{13,5},{5,1},{2,10},{10,14}... | collective-permute-start | bytes 1179656 | tf_op jit(solution)/shard_map/ppermute | solution.py:278
  21.0 4.3 %collective-permute-start.5 = (bf16[128,256]{1,0:T(8,128)(2,1)S(1)}, bf16[128,256]{1,0:T(8,128)(2,1)S(1)}, u32[]{:S(2)}, u32[]{:S(2)}) collective-permute-start(bf16[128,256]{1,0:T(8,128)(2,1)S(1)} %get-tuple-element.38), channel_id=1, source_target_pairs={{0,2},{1,3},{2,0},{3,1},{4,6},{5,7},{6,4},{7,5},{8,10},{9,11},{10,... | collective-permute-start | bytes 196616 | tf_op jit(solution)/shard_map/ppermute | solution.py:186
  30.4 1.4 %collective-permute-start.7 = (f32[256,128]{1,0:T(8,128)S(1)}, f32[256,128]{1,0:T(8,128)S(1)}, u32[]{:S(2)}, u32[]{:S(2)}) collective-permute-start(f32[256,128]{1,0:T(8,128)S(1)} %get-tuple-element.43), channel_id=1, source_target_pairs={{0,1},{1,0},{2,3},{3,2},{4,5},{5,4},{6,7},{7,6},{8,9},{9,8},{10,11... | collective-permute-start | bytes 393224 | tf_op jit(solution)/shard_map/ppermute | solution.py:186
  30.5 9.6 %collective-permute-start.2 = (bf16[32,2048]{1,0:T(8,128)(2,1)S(1)}, bf16[32,2048]{1,0:T(8,128)(2,1)S(1)}, u32[]{:S(2)}, u32[]{:S(2)}) collective-permute-start(bf16[32,2048]{1,0:T(8,128)(2,1)S(1)} %slice.7), channel_id=1, source_target_pairs={{0,8},{8,12},{12,4},{4,0},{1,9},{9,13},{13,5},{5,1},{2,10},{10,14}... | collective-permute-start | bytes 393224 | tf_op jit(solution)/shard_map/ppermute | solution.py:278
  31.9 4.0 %collective-permute-start.8 = (bf16[128,128]{1,0:T(8,128)(2,1)S(1)}, bf16[128,128]{1,0:T(8,128)(2,1)S(1)}, u32[]{:S(2)}, u32[]{:S(2)}) collective-permute-start(bf16[128,128]{1,0:T(8,128)(2,1)S(1)} %get-tuple-element.45), channel_id=1, source_target_pairs={{0,2},{1,3},{2,0},{3,1},{4,6},{5,7},{6,4},{7,5},{8,10},{9,11},{10,... | collective-permute-start | bytes 98312 | tf_op jit(solution)/shard_map/ppermute | solution.py:186
  33.4 7.5 %collective-permute-start.6 = (bf16[128,128]{1,0:T(8,128)(2,1)S(1)}, bf16[128,128]{1,0:T(8,128)(2,1)S(1)}, u32[]{:S(2)}, u32[]{:S(2)}) collective-permute-start(bf16[128,128]{1,0:T(8,128)(2,1)S(1)} %get-tuple-element.40), channel_id=1, source_target_pairs={{0,4},{4,12},{8,0},{12,8},{1,5},{5,13},{9,1},{13,9},{2,6},{6,14},{... | collective-permute-start | bytes 98312 | tf_op jit(solution)/shard_map/ppermute | solution.py:270
  35.9 5.3 %collective-permute-start.9 = (bf16[128,128]{1,0:T(8,128)(2,1)S(1)}, bf16[128,128]{1,0:T(8,128)(2,1)S(1)}, u32[]{:S(2)}, u32[]{:S(2)}) collective-permute-start(bf16[128,128]{1,0:T(8,128)(2,1)S(1)} %shard_map.71), channel_id=1, source_target_pairs={{0,8},{4,0},{8,12},{12,4},{1,9},{5,1},{9,13},{13,5},{2,10},{6,2},{... | collective-permute-start | bytes 98312 | tf_op jit(solution)/shard_map/ppermute | solution.py:270
  41.6 1.4 %collective-permute-start.10 = (f32[256,128]{1,0:T(8,128)S(1)}, f32[256,128]{1,0:T(8,128)S(1)}, u32[]{:S(2)}, u32[]{:S(2)}) collective-permute-start(f32[256,128]{1,0:T(8,128)S(1)} %shard_map.73), channel_id=1, source_target_pairs={{0,1},{1,0},{2,3},{3,2},{4,5},{5,4},{6,7},{7,6},{8,9},{9,8},{10,11... | collective-permute-start | bytes 393224 | tf_op jit(solution)/shard_map/ppermute | solution.py:186
  43.0 6.7 %collective-permute-start.11 = (bf16[256,128]{1,0:T(8,128)(2,1)S(1)}, bf16[256,128]{1,0:T(8,128)(2,1)S(1)}, u32[]{:S(2)}, u32[]{:S(2)}) collective-permute-start(bf16[256,128]{1,0:T(8,128)(2,1)S(1)} %shard_map.74), channel_id=1, source_target_pairs={{0,12},{1,15},{2,14},{3,13},{4,8},{5,11},{6,10},{7,9},{8,4},{9,7},... | collective-permute-start | bytes 196616 | tf_op jit(solution)/shard_map/ppermute | solution.py:297
  49.7 1.3 %collective-permute-start.12 = (bf16[256,128]{1,0:T(8,128)(2,1)S(1)}, bf16[256,128]{1,0:T(8,128)(2,1)S(1)}, u32[]{:S(2)}, u32[]{:S(2)}) collective-permute-start(bf16[256,128]{1,0:T(8,128)(2,1)S(1)} %collective-permute-done.11.mine_ref), channel_id=1, source_target_pairs={{0,1},{1,0},{2,3},{3,2},{4,5},{5,4},{6,7},{7,6},{8,9},{9,8},{10,11... | collective-permute-start | bytes 196616 | tf_op jit(solution)/shard_map/ppermute | solution.py:186

commit v17 on v14

--- a/solution.py
+++ b/solution.py
@@ -198,10 +198,10 @@
     return small_call(chip_sum_kernel, out_shape, mine, swap(other, 2))
 
 
-ROUND_ONE = ((0, 2), (2, 3), (3, 1), (1, 0))
-ROUND_TWO = ((0, 1), (1, 3), (3, 2), (2, 0))
-BLOCK_ONE = (1, 3, 0, 2)
-BLOCK_TWO = (2, 0, 3, 1)
+ROUND_ONE = ((0, 1), (1, 3), (3, 2), (2, 0))
+ROUND_TWO = ((0, 2), (2, 3), (3, 1), (1, 0))
+BLOCK_ONE = (2, 0, 3, 1)
+BLOCK_TWO = (1, 3, 0, 2)
 BLOCK_LAST = (3, 2, 1, 0)
 
 

time: 51.8 us -> 56.1 us (1.083)
  starting transfers between devices: 14.6 us -> 26.7 us
  waiting for transfers between devices: 24.4 us -> 16.6 us
    ppermute x1, starting transfers between devices: 3.33 us -> 12.1 us  [along_line(): three = lax.ppermute(one, 'rows', ROUND_ONE)]
    ppermute x1, waiting for transfers between devices: 4.39 us -> 0.01 us  [along_line(): two = lax.ppermute(later, 'rows', ROUND_TWO)]
    ppermute x2, waiting for transfers between devices: 4.65 us -> 2.08 us  [back(): return lax.ppermute(total, 'rows', tuple(enumerate(table)))]
    ppermute x2, starting transfers between devices: 1.29 us -> 3.34 us  [back(): return lax.ppermute(total, 'rows', tuple(enumerate(table)))]
    ppermute x1, starting transfers between devices: 2.52 us -> 3.69 us  [along_line(): mine = lax.ppermute(both, ('rows', 'layer'), pairs)]
    ppermute x1, starting transfers between devices: 0.06 us -> 1.21 us  [along_line(): two = lax.ppermute(later, 'rows', ROUND_TWO)]
    ppermute x1, waiting for transfers between devices: 4.2 us -> 3.13 us  [along_line(): mine = lax.ppermute(both, ('rows', 'layer'), pairs)]
    ppermute x1, starting transfers between devices: 4.04 us -> 3.02 us  [along_line(): one = lax.ppermute(documents, 'rows', ROUND_ONE)]
  transfers between devices with their start and end apart: 12 -> 12, of which waited for: 10 -> 8; matrix products, arithmetic and copies ran while one was open for 0% -> 0% of each run, Pallas kernels for 19% -> 17%
where the time goes in v17:
time: 56.1 us; the launch traced here: 55.9 us
  starting transfers between devices  26.7 us (48%)
  waiting for transfers between devices  16.6 us (30%)
  Pallas kernels  10.8 us (19%)
  local copies, waits for them, and re-layouts  1.74 us (3%)
    ppermute x1, starting transfers between devices, along_line(): three = lax.ppermute(one, 'rows', ROUND_ONE)  12.1 us
    ppermute x6, waiting for transfers between devices, swap(): lax.ppermute(value, 'layer', [(lay, lay ^ distance) for lay in range(coun...  7.94 us
    pallas_call x1, Pallas kernels, prepare(): pl.pallas_call(prepare_kernel, out_shape=jax.ShapeDtypeStruct((rows, dims...  6.15 us
    ppermute x1, starting transfers between devices, along_line(): mine = lax.ppermute(both, ('rows', 'layer'), pairs)  3.69 us
    ppermute x1, waiting for transfers between devices, along_line(): one = lax.ppermute(documents, 'rows', ROUND_ONE)  3.44 us
    ppermute x2, starting transfers between devices, back(): return lax.ppermute(total, 'rows', tuple(enumerate(table)))  3.34 us
    ppermute x6, starting transfers between devices, swap(): lax.ppermute(value, 'layer', [(lay, lay ^ distance) for lay in range(coun...  3.34 us
    pallas_call x5, Pallas kernels, scoring(): pl.pallas_call(kernel, out_shape=out_shape, in_specs=[vmem] * (3 + len(ex...  3.17 us
  transfers between devices with their start and end apart: 12, of which 8 were waited for; matrix products, arithmetic and copies ran while one was open for 0% of the time, Pallas kernels for 17%

profile of v17, /device:TPU:0, one launch (start us, length us, event | category | flops | bytes accessed | tf_op | source)
XLA Modules:
  0.0 55.9 jit_solution(13554147539671250478)
XLA Ops:
  0.0 0.0 copy-start.1
  0.0 0.0 copy-start.2
  0.0 3.0 %collective-permute-start = (bf16[128,2048]{1,0:T(8,128)(2,1)}, bf16[128,2048]{1,0:T(8,128)(2,1)S(1)}, u32[]{:S(2)}, u32[]{:S(2)}) collective-permute-start(bf16[128,2048]{1,0:T(8,128)(2,1)} %documents_ref), channel_id=1, source_target_pairs={{0,4},{4,12},{12,8},{8,0},{1,5},{5,13},{13,9},{9,1},{2,6},{6,14},{... | collective-permute-start | bytes 1572872 | tf_op jit(solution)/shard_map/ppermute | solution.py:271
  3.0 6.2 %shard_map.64.queries_ref = bf16[512,2048]{1,0:T(8,128)(2,1)} custom-call(s32[4]{0:T(128)} %offsets.1, bf16[512,2048]{1,0:T(8,128)(2,1)} %queries_hbm.1, bf16[4,512,512]{2,1,0:T(8,128)(2,1)} %bases_hbm.1, f32[4,512]{1,0:T(4,128)} %values_hbm.1), custom_call_target="tpu_custom_call" | custom-call | flops 2147483648 | bytes 6291456 | tf_op jit(solution)/shard_map/pallas_call | solution.py:52
  9.2 0.0 copy-done.1
  9.2 1.2 %collective-permute-start.2 = (bf16[128,2048]{1,0:T(8,128)(2,1)S(1)}, bf16[128,2048]{1,0:T(8,128)(2,1)S(1)}, u32[]{:S(2)}, u32[]{:S(2)}) collective-permute-start(bf16[128,2048]{1,0:T(8,128)(2,1)S(1)} %copy-done.1), channel_id=1, source_target_pairs={{0,8},{8,12},{12,4},{4,0},{1,9},{9,13},{13,5},{5,1},{2,10},{10,14}... | collective-permute-start | bytes 1572872 | tf_op jit(solution)/shard_map/ppermute | solution.py:273
  10.4 0.0 copy-done.2
  10.4 0.1 copy.11.ids_ref
  10.6 0.0 copy-start
  10.6 1.6 %copy-done = bf16[512,2048]{1,0:T(8,128)(2,1)S(1)} copy-done((bf16[512,2048]{1,0:T(8,128)(2,1)S(1)}, bf16[512,2048]{1,0:T(8,128)(2,1)}, u32[]{:S(2)}) %copy-start) | copy-done | bytes 2097176
  12.2 0.8 %shard_map.65 = (f32[256,128]{1,0:T(8,128)S(1)}, f32[256,128]{1,0:T(8,128)S(1)}) custom-call(bf16[512,2048]{1,0:T(8,128)(2,1)S(1)} %copy-done, s32[512,1]{1,0:T(8,128)S(1)} %copy.11.ids_ref, bf16[128,2048]{1,0:T(8,128)(2,1)S(1)} %copy-done.1), custom_call_target="tpu_custom_call" | custom-call | flops 268435456 | bytes 2621440 | tf_op jit(solution)/shard_map/pallas_call | solution.py:81
  12.9 3.4 %collective-permute-done.documents_ref = bf16[128,2048]{1,0:T(8,128)(2,1)S(1)} collective-permute-done((bf16[128,2048]{1,0:T(8,128)(2,1)}, bf16[128,2048]{1,0:T(8,128)(2,1)S(1)}, u32[]{:S(2)}, u32[]{:S(2)}) %collective-permute-start) | collective-permute-done | bytes 524320 | tf_op jit(solution)/shard_map/ppermute | solution.py:271
  16.4 0.8 %shard_map.66 = (f32[256,256]{1,0:T(8,128)S(1)}, f32[256,256]{1,0:T(8,128)S(1)}) custom-call(bf16[512,2048]{1,0:T(8,128)(2,1)S(1)} %copy-done, s32[512,1]{1,0:T(8,128)S(1)} %copy.11.ids_ref, bf16[128,2048]{1,0:T(8,128)(2,1)S(1)} %collective-permute-done.documents_ref, f32[256,128]{1,0:T(8,128)S(1)} %get-tuple-element.32.refs_0_, ...), custom_call_target="tpu_custom_call" | custom-call | flops 268435456 | bytes 2621440 | tf_op jit(solution)/shard_map/pallas_call | solution.py:81
  17.1 0.1 collective-permute-start.3
  17.2 12.1 %collective-permute-start.1 = (bf16[128,2048]{1,0:T(8,128)(2,1)S(1)}, bf16[128,2048]{1,0:T(8,128)(2,1)S(1)}, u32[]{:S(2)}, u32[]{:S(2)}) collective-permute-start(bf16[128,2048]{1,0:T(8,128)(2,1)S(1)} %collective-permute-done.documents_ref), channel_id=1, source_target_pairs={{0,4},{4,12},{12,8},{8,0},{1,5},{5,13},{13,9},{9,1},{2,6},{6,14},{... | collective-permute-start | bytes 1572872 | tf_op jit(solution)/shard_map/ppermute | solution.py:276
  29.3 0.0 collective-permute-done.3.arrived_ref
  29.3 1.6 %collective-permute-start.4 = (bf16[128,256]{1,0:T(8,128)(2,1)S(1)}, bf16[128,256]{1,0:T(8,128)(2,1)S(1)}, u32[]{:S(2)}, u32[]{:S(2)}) collective-permute-start(bf16[128,256]{1,0:T(8,128)(2,1)S(1)} %get-tuple-element.37), channel_id=1, source_target_pairs={{0,2},{1,3},{2,0},{3,1},{4,6},{5,7},{6,4},{7,5},{8,10},{9,11},{10,... | collective-permute-start | bytes 196616 | tf_op jit(solution)/shard_map/ppermute | solution.py:185
  30.9 2.8 %collective-permute-done.4.arrived_ref = bf16[128,256]{1,0:T(8,128)(2,1)S(1)} collective-permute-done((bf16[128,256]{1,0:T(8,128)(2,1)S(1)}, bf16[128,256]{1,0:T(8,128)(2,1)S(1)}, u32[]{:S(2)}, u32[]{:S(2)}) %collective-permute-start.4) | collective-permute-done | bytes 65568 | tf_op jit(solution)/shard_map/ppermute | solution.py:185
  33.7 0.0 collective-permute-done.2.documents_ref
  33.7 0.8 %shard_map.69 = (f32[256,128]{1,0:T(8,128)S(1)}, f32[256,128]{1,0:T(8,128)S(1)}) custom-call(bf16[512,2048]{1,0:T(8,128)(2,1)S(1)} %copy-done, s32[512,1]{1,0:T(8,128)S(1)} %copy.11.ids_ref, bf16[128,2048]{1,0:T(8,128)(2,1)S(1)} %collective-permute-done.2.documents_ref), custom_call_target="tpu_custom_call" | custom-call | flops 268435456 | bytes 2621440 | tf_op jit(solution)/shard_map/pallas_call | solution.py:81
  34.5 0.1 collective-permute-start.6
  34.5 1.3 %collective-permute-done.6.arrived_ref = f32[256,128]{1,0:T(8,128)S(1)} collective-permute-done((f32[256,128]{1,0:T(8,128)S(1)}, f32[256,128]{1,0:T(8,128)S(1)}, u32[]{:S(2)}, u32[]{:S(2)}) %collective-permute-start.6) | collective-permute-done | bytes 131104 | tf_op jit(solution)/shard_map/ppermute | solution.py:185
  35.9 1.6 %collective-permute-start.7 = (bf16[128,128]{1,0:T(8,128)(2,1)S(1)}, bf16[128,128]{1,0:T(8,128)(2,1)S(1)}, u32[]{:S(2)}, u32[]{:S(2)}) collective-permute-start(bf16[128,128]{1,0:T(8,128)(2,1)S(1)} %get-tuple-element.44), channel_id=1, source_target_pairs={{0,2},{1,3},{2,0},{3,1},{4,6},{5,7},{6,4},{7,5},{8,10},{9,11},{10,... | collective-permute-start | bytes 98312 | tf_op jit(solution)/shard_map/ppermute | solution.py:185
  37.4 0.0 collective-permute-start.5
  37.4 2.4 %collective-permute-done.7.arrived_ref = bf16[128,128]{1,0:T(8,128)(2,1)S(1)} collective-permute-done((bf16[128,128]{1,0:T(8,128)(2,1)S(1)}, bf16[128,128]{1,0:T(8,128)(2,1)S(1)}, u32[]{:S(2)}, u32[]{:S(2)}) %collective-permute-start.7) | collective-permute-done | bytes 32800 | tf_op jit(solution)/shard_map/ppermute | solution.py:185
  39.9 3.3 %collective-permute-start.8 = (bf16[128,128]{1,0:T(8,128)(2,1)S(1)}, bf16[128,128]{1,0:T(8,128)(2,1)S(1)}, u32[]{:S(2)}, u32[]{:S(2)}) collective-permute-start(bf16[128,128]{1,0:T(8,128)(2,1)S(1)} %shard_map.71), channel_id=1, source_target_pairs={{0,4},{4,12},{8,0},{12,8},{1,5},{5,13},{9,1},{13,9},{2,6},{6,14},{... | collective-permute-start | bytes 98312 | tf_op jit(solution)/shard_map/ppermute | solution.py:269
  43.2 0.0 collective-permute-done.5.first_ref
  43.2 0.0 collective-permute-done.1.documents_ref
  43.2 2.1 %collective-permute-done.8.second_ref = bf16[128,128]{1,0:T(8,128)(2,1)S(1)} collective-permute-done((bf16[128,128]{1,0:T(8,128)(2,1)S(1)}, bf16[128,128]{1,0:T(8,128)(2,1)S(1)}, u32[]{:S(2)}, u32[]{:S(2)}) %collective-permute-start.8) | collective-permute-done | bytes 32800 | tf_op jit(solution)/shard_map/ppermute | solution.py:269
  45.3 0.4 shard_map.73
  45.7 0.1 collective-permute-start.9
  45.8 0.4 shard_map.72.refs_0_
  46.3 0.9 %collective-permute-done.9.refs_1_ = f32[256,128]{1,0:T(8,128)S(1)} collective-permute-done((f32[256,128]{1,0:T(8,128)S(1)}, f32[256,128]{1,0:T(8,128)S(1)}, u32[]{:S(2)}, u32[]{:S(2)}) %collective-permute-start.9) | collective-permute-done | bytes 131104 | tf_op jit(solution)/shard_map/ppermute | solution.py:185
  47.2 3.7 %collective-permute-start.10 = (bf16[256,128]{1,0:T(8,128)(2,1)S(1)}, bf16[256,128]{1,0:T(8,128)(2,1)S(1)}, u32[]{:S(2)}, u32[]{:S(2)}) collective-permute-start(bf16[256,128]{1,0:T(8,128)(2,1)S(1)} %shard_map.74), channel_id=1, source_target_pairs={{0,12},{1,15},{2,14},{3,13},{4,8},{5,11},{6,10},{7,9},{8,4},{9,7},... | collective-permute-start | bytes 196616 | tf_op jit(solution)/shard_map/ppermute | solution.py:294
  50.9 3.1 %collective-permute-done.10.mine_ref = bf16[256,128]{1,0:T(8,128)(2,1)S(1)} collective-permute-done((bf16[256,128]{1,0:T(8,128)(2,1)S(1)}, bf16[256,128]{1,0:T(8,128)(2,1)S(1)}, u32[]{:S(2)}, u32[]{:S(2)}) %collective-permute-start.10) | collective-permute-done | bytes 65568 | tf_op jit(solution)/shard_map/ppermute | solution.py:294
  54.0 0.0 collective-permute-start.11
  54.0 0.7 %shard_map.75.scores_hbm = f32[4,128,128]{2,1,0:T(8,128)} custom-call(f32[128,128]{1,0:T(8,128)S(1)} %get-tuple-element.46.own_ref, bf16[128,128]{1,0:T(8,128)(2,1)S(1)} %collective-permute-done.5.first_ref, bf16[128,128]{1,0:T(8,128)(2,1)S(1)} %collective-permute-done.8.second_ref), custom_call_target="tpu_custom_call" | custom-call | tf_op jit(solution)/shard_map/pallas_call | solution.py:147
  54.7 0.5 collective-permute-done.11.arrived_ref
  55.2 0.6 %shard_map.76 = f32[4,128,128]{2,1,0:T(8,128)} custom-call(bf16[256,128]{1,0:T(8,128)(2,1)S(1)} %collective-permute-done.10.mine_ref, bf16[256,128]{1,0:T(8,128)(2,1)S(1)} %collective-permute-done.11.arrived_ref, f32[4,128,128]{2,1,0:T(8,128)} %shard_map.75.scores_hbm), custom_call_target="tpu_custom_call", output_to_operand_aliasing={{}: (2, {})} | custom-call | tf_op jit(solution)/shard_map/pallas_call | solution.py:241
  (5 shorter events, 0.1 us)
Async XLA Ops:
  0.0 9.2 %copy-start.1 = (bf16[128,2048]{1,0:T(8,128)(2,1)S(1)}, bf16[128,2048]{1,0:T(8,128)(2,1)}, u32[]{:S(2)}) copy-start(bf16[128,2048]{1,0:T(8,128)(2,1)} %documents_ref) | copy-start | bytes 1572868
  0.0 10.4 %copy-start.2 = (s32[512]{0:T(512)S(1)}, s32[512]{0:T(512)}, u32[]{:S(2)}) copy-start(s32[512]{0:T(512)} %param.11) | copy-start | bytes 6148
  0.0 16.4 %collective-permute-start = (bf16[128,2048]{1,0:T(8,128)(2,1)}, bf16[128,2048]{1,0:T(8,128)(2,1)S(1)}, u32[]{:S(2)}, u32[]{:S(2)}) collective-permute-start(bf16[128,2048]{1,0:T(8,128)(2,1)} %documents_ref), channel_id=1, source_target_pairs={{0,4},{4,12},{12,8},{8,0},{1,5},{5,13},{13,9},{9,1},{2,6},{6,14},{... | collective-permute-start | bytes 1572872 | tf_op jit(solution)/shard_map/ppermute | solution.py:271
  9.2 24.5 %collective-permute-start.2 = (bf16[128,2048]{1,0:T(8,128)(2,1)S(1)}, bf16[128,2048]{1,0:T(8,128)(2,1)S(1)}, u32[]{:S(2)}, u32[]{:S(2)}) collective-permute-start(bf16[128,2048]{1,0:T(8,128)(2,1)S(1)} %copy-done.1), channel_id=1, source_target_pairs={{0,8},{8,12},{12,4},{4,0},{1,9},{9,13},{13,5},{5,1},{2,10},{10,14}... | collective-permute-start | bytes 1572872 | tf_op jit(solution)/shard_map/ppermute | solution.py:273
  10.6 1.6 %copy-start = (bf16[512,2048]{1,0:T(8,128)(2,1)S(1)}, bf16[512,2048]{1,0:T(8,128)(2,1)}, u32[]{:S(2)}) copy-start(bf16[512,2048]{1,0:T(8,128)(2,1)} %shard_map.64.queries_ref) | copy-start | bytes 6291460
  17.1 12.2 %collective-permute-start.3 = (f32[256,256]{1,0:T(8,128)S(1)}, f32[256,256]{1,0:T(8,128)S(1)}, u32[]{:S(2)}, u32[]{:S(2)}) collective-permute-start(f32[256,256]{1,0:T(8,128)S(1)} %get-tuple-element.35), channel_id=1, source_target_pairs={{0,1},{1,0},{2,3},{3,2},{4,5},{5,4},{6,7},{7,6},{8,9},{9,8},{10,11... | collective-permute-start | bytes 786440 | tf_op jit(solution)/shard_map/ppermute | solution.py:185
  17.2 26.0 %collective-permute-start.1 = (bf16[128,2048]{1,0:T(8,128)(2,1)S(1)}, bf16[128,2048]{1,0:T(8,128)(2,1)S(1)}, u32[]{:S(2)}, u32[]{:S(2)}) collective-permute-start(bf16[128,2048]{1,0:T(8,128)(2,1)S(1)} %collective-permute-done.documents_ref), channel_id=1, source_target_pairs={{0,4},{4,12},{12,8},{8,0},{1,5},{5,13},{13,9},{9,1},{2,6},{6,14},{... | collective-permute-start | bytes 1572872 | tf_op jit(solution)/shard_map/ppermute | solution.py:276
  29.3 4.3 %collective-permute-start.4 = (bf16[128,256]{1,0:T(8,128)(2,1)S(1)}, bf16[128,256]{1,0:T(8,128)(2,1)S(1)}, u32[]{:S(2)}, u32[]{:S(2)}) collective-permute-start(bf16[128,256]{1,0:T(8,128)(2,1)S(1)} %get-tuple-element.37), channel_id=1, source_target_pairs={{0,2},{1,3},{2,0},{3,1},{4,6},{5,7},{6,4},{7,5},{8,10},{9,11},{10,... | collective-permute-start | bytes 196616 | tf_op jit(solution)/shard_map/ppermute | solution.py:185
  34.5 1.4 %collective-permute-start.6 = (f32[256,128]{1,0:T(8,128)S(1)}, f32[256,128]{1,0:T(8,128)S(1)}, u32[]{:S(2)}, u32[]{:S(2)}) collective-permute-start(f32[256,128]{1,0:T(8,128)S(1)} %get-tuple-element.42), channel_id=1, source_target_pairs={{0,1},{1,0},{2,3},{3,2},{4,5},{5,4},{6,7},{7,6},{8,9},{9,8},{10,11... | collective-permute-start | bytes 393224 | tf_op jit(solution)/shard_map/ppermute | solution.py:185
  35.9 4.0 %collective-permute-start.7 = (bf16[128,128]{1,0:T(8,128)(2,1)S(1)}, bf16[128,128]{1,0:T(8,128)(2,1)S(1)}, u32[]{:S(2)}, u32[]{:S(2)}) collective-permute-start(bf16[128,128]{1,0:T(8,128)(2,1)S(1)} %get-tuple-element.44), channel_id=1, source_target_pairs={{0,2},{1,3},{2,0},{3,1},{4,6},{5,7},{6,4},{7,5},{8,10},{9,11},{10,... | collective-permute-start | bytes 98312 | tf_op jit(solution)/shard_map/ppermute | solution.py:185
  37.4 5.8 %collective-permute-start.5 = (bf16[128,128]{1,0:T(8,128)(2,1)S(1)}, bf16[128,128]{1,0:T(8,128)(2,1)S(1)}, u32[]{:S(2)}, u32[]{:S(2)}) collective-permute-start(bf16[128,128]{1,0:T(8,128)(2,1)S(1)} %get-tuple-element.39), channel_id=1, source_target_pairs={{0,8},{4,0},{8,12},{12,4},{1,9},{5,1},{9,13},{13,5},{2,10},{6,2},{... | collective-permute-start | bytes 98312 | tf_op jit(solution)/shard_map/ppermute | solution.py:269
  39.9 5.4 %collective-permute-start.8 = (bf16[128,128]{1,0:T(8,128)(2,1)S(1)}, bf16[128,128]{1,0:T(8,128)(2,1)S(1)}, u32[]{:S(2)}, u32[]{:S(2)}) collective-permute-start(bf16[128,128]{1,0:T(8,128)(2,1)S(1)} %shard_map.71), channel_id=1, source_target_pairs={{0,4},{4,12},{8,0},{12,8},{1,5},{5,13},{9,1},{13,9},{2,6},{6,14},{... | collective-permute-start | bytes 98312 | tf_op jit(solution)/shard_map/ppermute | solution.py:269
  45.7 1.4 %collective-permute-start.9 = (f32[256,128]{1,0:T(8,128)S(1)}, f32[256,128]{1,0:T(8,128)S(1)}, u32[]{:S(2)}, u32[]{:S(2)}) collective-permute-start(f32[256,128]{1,0:T(8,128)S(1)} %shard_map.73), channel_id=1, source_target_pairs={{0,1},{1,0},{2,3},{3,2},{4,5},{5,4},{6,7},{7,6},{8,9},{9,8},{10,11... | collective-permute-start | bytes 393224 | tf_op jit(solution)/shard_map/ppermute | solution.py:185
  47.2 6.8 %collective-permute-start.10 = (bf16[256,128]{1,0:T(8,128)(2,1)S(1)}, bf16[256,128]{1,0:T(8,128)(2,1)S(1)}, u32[]{:S(2)}, u32[]{:S(2)}) collective-permute-start(bf16[256,128]{1,0:T(8,128)(2,1)S(1)} %shard_map.74), channel_id=1, source_target_pairs={{0,12},{1,15},{2,14},{3,13},{4,8},{5,11},{6,10},{7,9},{8,4},{9,7},... | collective-permute-start | bytes 196616 | tf_op jit(solution)/shard_map/ppermute | solution.py:294
  54.0 1.3 %collective-permute-start.11 = (bf16[256,128]{1,0:T(8,128)(2,1)S(1)}, bf16[256,128]{1,0:T(8,128)(2,1)S(1)}, u32[]{:S(2)}, u32[]{:S(2)}) collective-permute-start(bf16[256,128]{1,0:T(8,128)(2,1)S(1)} %collective-permute-done.10.mine_ref), channel_id=1, source_target_pairs={{0,1},{1,0},{2,3},{3,2},{4,5},{5,4},{6,7},{7,6},{8,9},{9,8},{10,11... | collective-permute-start | bytes 196616 | tf_op jit(solution)/shard_map/ppermute | solution.py:185

commit v18 on v14

--- a/solution.py
+++ b/solution.py
@@ -121,7 +121,7 @@
 
 def target_chip():
     chip, core = lax.div(layer_index(), 2), lax.rem(layer_index(), 2)
-    return jnp.where(chip == core, 0, 1)
+    return jnp.where(chip == core, 1, 0)
 
 
 def half_kernel(block_of, kept, queries_ref, ids_ref, documents_ref, out_ref):
@@ -287,7 +287,7 @@
     (both,) = small_call(sum_kernel, [jax.ShapeDtypeStruct(half, jnp.bfloat16)], kept, arrived)
     shares = lax.axis_size("layer")
     pairs = [
-        (row * shares + lay, BLOCK_LAST[row] * shares + 2 * ((lay // 2) ^ (lay % 2)) + lay % 2)
+        (row * shares + lay, BLOCK_LAST[row] * shares + 2 * (1 - ((lay // 2) ^ (lay % 2))) + lay % 2)
         for row in range(len(BLOCK_LAST))
         for lay in range(shares)
     ]

time: 51.8 us -> 52.1 us (level)
  starting transfers between devices: 14.6 us -> 15.6 us
  waiting for transfers between devices: 24.4 us -> 23.7 us
    ppermute x1, starting transfers between devices: 2.52 us -> 3.45 us  [along_line(): mine = lax.ppermute(both, ('rows', 'layer'), pairs)]
    ppermute x1, waiting for transfers between devices: 4.2 us -> 3.57 us  [along_line(): mine = lax.ppermute(both, ('rows', 'layer'), pairs)]
where the time goes in v18:
time: 52.1 us; the launch traced here: 51.9 us
  waiting for transfers between devices  23.7 us (45%)
  starting transfers between devices  15.6 us (30%)
  Pallas kernels  10.8 us (21%)
  local copies, waits for them, and re-layouts  1.74 us (3%)
    ppermute x6, waiting for transfers between devices, swap(): lax.ppermute(value, 'layer', [(lay, lay ^ distance) for lay in range(coun...  7.21 us
    pallas_call x1, Pallas kernels, prepare(): pl.pallas_call(prepare_kernel, out_shape=jax.ShapeDtypeStruct((rows, dims...  6.15 us
    ppermute x2, waiting for transfers between devices, back(): return lax.ppermute(total, 'rows', tuple(enumerate(table)))  4.65 us
    ppermute x1, waiting for transfers between devices, along_line(): two = lax.ppermute(later, 'rows', ROUND_TWO)  4.39 us
    ppermute x1, starting transfers between devices, along_line(): one = lax.ppermute(documents, 'rows', ROUND_ONE)  4.04 us
    ppermute x1, waiting for transfers between devices, along_line(): one = lax.ppermute(documents, 'rows', ROUND_ONE)  3.93 us
    ppermute x1, waiting for transfers between devices, along_line(): mine = lax.ppermute(both, ('rows', 'layer'), pairs)  3.57 us
    ppermute x1, starting transfers between devices, along_line(): mine = lax.ppermute(both, ('rows', 'layer'), pairs)  3.45 us
  transfers between devices with their start and end apart: 12, of which 10 were waited for; matrix products, arithmetic and copies ran while one was open for 0% of the time, Pallas kernels for 19%

profile of v18, /device:TPU:0, one launch (start us, length us, event | category | flops | bytes accessed | tf_op | source)
XLA Modules:
  0.0 51.9 jit_solution(3045433802763745612)
XLA Ops:
  0.0 0.0 copy-start.1
  0.0 0.0 copy-start.2
  0.0 4.0 %collective-permute-start = (bf16[128,2048]{1,0:T(8,128)(2,1)}, bf16[128,2048]{1,0:T(8,128)(2,1)S(1)}, u32[]{:S(2)}, u32[]{:S(2)}) collective-permute-start(bf16[128,2048]{1,0:T(8,128)(2,1)} %documents_ref), channel_id=1, source_target_pairs={{0,8},{8,12},{12,4},{4,0},{1,9},{9,13},{13,5},{5,1},{2,10},{10,14}... | collective-permute-start | bytes 1572872 | tf_op jit(solution)/shard_map/ppermute | solution.py:271
  4.0 6.2 %shard_map.64.queries_ref = bf16[512,2048]{1,0:T(8,128)(2,1)} custom-call(s32[4]{0:T(128)} %offsets.1, bf16[512,2048]{1,0:T(8,128)(2,1)} %queries_hbm.1, bf16[4,512,512]{2,1,0:T(8,128)(2,1)} %bases_hbm.1, f32[4,512]{1,0:T(4,128)} %values_hbm.1), custom_call_target="tpu_custom_call" | custom-call | flops 2147483648 | bytes 6291456 | tf_op jit(solution)/shard_map/pallas_call | solution.py:52
  10.2 0.0 copy-done.1
  10.2 0.1 collective-permute-start.2
  10.3 0.0 copy-done.2
  10.3 0.1 copy.11.ids_ref
  10.4 0.0 copy-start
  10.4 1.6 %copy-done = bf16[512,2048]{1,0:T(8,128)(2,1)S(1)} copy-done((bf16[512,2048]{1,0:T(8,128)(2,1)S(1)}, bf16[512,2048]{1,0:T(8,128)(2,1)}, u32[]{:S(2)}) %copy-start) | copy-done | bytes 2097176
  12.0 0.8 %shard_map.65 = (f32[256,128]{1,0:T(8,128)S(1)}, f32[256,128]{1,0:T(8,128)S(1)}) custom-call(bf16[512,2048]{1,0:T(8,128)(2,1)S(1)} %copy-done, s32[512,1]{1,0:T(8,128)S(1)} %copy.11.ids_ref, bf16[128,2048]{1,0:T(8,128)(2,1)S(1)} %copy-done.1), custom_call_target="tpu_custom_call" | custom-call | flops 268435456 | bytes 2621440 | tf_op jit(solution)/shard_map/pallas_call | solution.py:81
  12.8 3.9 %collective-permute-done.documents_ref = bf16[128,2048]{1,0:T(8,128)(2,1)S(1)} collective-permute-done((bf16[128,2048]{1,0:T(8,128)(2,1)}, bf16[128,2048]{1,0:T(8,128)(2,1)S(1)}, u32[]{:S(2)}, u32[]{:S(2)}) %collective-permute-start) | collective-permute-done | bytes 524320 | tf_op jit(solution)/shard_map/ppermute | solution.py:271
  16.7 0.8 %shard_map.66 = (f32[256,256]{1,0:T(8,128)S(1)}, f32[256,256]{1,0:T(8,128)S(1)}) custom-call(bf16[512,2048]{1,0:T(8,128)(2,1)S(1)} %copy-done, s32[512,1]{1,0:T(8,128)S(1)} %copy.11.ids_ref, bf16[128,2048]{1,0:T(8,128)(2,1)S(1)} %collective-permute-done.documents_ref, f32[256,128]{1,0:T(8,128)S(1)} %get-tuple-element.32.refs_0_, ...), custom_call_target="tpu_custom_call" | custom-call | flops 268435456 | bytes 2621440 | tf_op jit(solution)/shard_map/pallas_call | solution.py:81
  17.5 0.1 collective-permute-start.3
  17.6 3.3 %collective-permute-start.1 = (bf16[128,2048]{1,0:T(8,128)(2,1)S(1)}, bf16[128,2048]{1,0:T(8,128)(2,1)S(1)}, u32[]{:S(2)}, u32[]{:S(2)}) collective-permute-start(bf16[128,2048]{1,0:T(8,128)(2,1)S(1)} %collective-permute-done.documents_ref), channel_id=1, source_target_pairs={{0,8},{8,12},{12,4},{4,0},{1,9},{9,13},{13,5},{5,1},{2,10},{10,14}... | collective-permute-start | bytes 1572872 | tf_op jit(solution)/shard_map/ppermute | solution.py:276
  20.9 0.0 collective-permute-done.3.arrived_ref
  20.9 1.6 %collective-permute-start.4 = (bf16[128,256]{1,0:T(8,128)(2,1)S(1)}, bf16[128,256]{1,0:T(8,128)(2,1)S(1)}, u32[]{:S(2)}, u32[]{:S(2)}) collective-permute-start(bf16[128,256]{1,0:T(8,128)(2,1)S(1)} %get-tuple-element.37), channel_id=1, source_target_pairs={{0,2},{1,3},{2,0},{3,1},{4,6},{5,7},{6,4},{7,5},{8,10},{9,11},{10,... | collective-permute-start | bytes 196616 | tf_op jit(solution)/shard_map/ppermute | solution.py:185
  22.5 2.8 %collective-permute-done.4.arrived_ref = bf16[128,256]{1,0:T(8,128)(2,1)S(1)} collective-permute-done((bf16[128,256]{1,0:T(8,128)(2,1)S(1)}, bf16[128,256]{1,0:T(8,128)(2,1)S(1)}, u32[]{:S(2)}, u32[]{:S(2)}) %collective-permute-start.4) | collective-permute-done | bytes 65568 | tf_op jit(solution)/shard_map/ppermute | solution.py:185
  25.3 4.4 %collective-permute-done.2.documents_ref = bf16[128,2048]{1,0:T(8,128)(2,1)S(1)} collective-permute-done((bf16[128,2048]{1,0:T(8,128)(2,1)S(1)}, bf16[128,2048]{1,0:T(8,128)(2,1)S(1)}, u32[]{:S(2)}, u32[]{:S(2)}) %collective-permute-start.2) | collective-permute-done | bytes 524320 | tf_op jit(solution)/shard_map/ppermute | solution.py:273
  29.7 0.8 %shard_map.69 = (f32[256,128]{1,0:T(8,128)S(1)}, f32[256,128]{1,0:T(8,128)S(1)}) custom-call(bf16[512,2048]{1,0:T(8,128)(2,1)S(1)} %copy-done, s32[512,1]{1,0:T(8,128)S(1)} %copy.11.ids_ref, bf16[128,2048]{1,0:T(8,128)(2,1)S(1)} %collective-permute-done.2.documents_ref), custom_call_target="tpu_custom_call" | custom-call | flops 268435456 | bytes 2621440 | tf_op jit(solution)/shard_map/pallas_call | solution.py:81
  30.4 0.1 collective-permute-start.6
  30.5 1.3 %collective-permute-done.6.arrived_ref = f32[256,128]{1,0:T(8,128)S(1)} collective-permute-done((f32[256,128]{1,0:T(8,128)S(1)}, f32[256,128]{1,0:T(8,128)S(1)}, u32[]{:S(2)}, u32[]{:S(2)}) %collective-permute-start.6) | collective-permute-done | bytes 131104 | tf_op jit(solution)/shard_map/ppermute | solution.py:185
  31.9 1.6 %collective-permute-start.7 = (bf16[128,128]{1,0:T(8,128)(2,1)S(1)}, bf16[128,128]{1,0:T(8,128)(2,1)S(1)}, u32[]{:S(2)}, u32[]{:S(2)}) collective-permute-start(bf16[128,128]{1,0:T(8,128)(2,1)S(1)} %get-tuple-element.44), channel_id=1, source_target_pairs={{0,2},{1,3},{2,0},{3,1},{4,6},{5,7},{6,4},{7,5},{8,10},{9,11},{10,... | collective-permute-start | bytes 98312 | tf_op jit(solution)/shard_map/ppermute | solution.py:185
  33.4 0.7 %collective-permute-start.5 = (bf16[128,128]{1,0:T(8,128)(2,1)S(1)}, bf16[128,128]{1,0:T(8,128)(2,1)S(1)}, u32[]{:S(2)}, u32[]{:S(2)}) collective-permute-start(bf16[128,128]{1,0:T(8,128)(2,1)S(1)} %get-tuple-element.39), channel_id=1, source_target_pairs={{0,4},{4,12},{8,0},{12,8},{1,5},{5,13},{9,1},{13,9},{2,6},{6,14},{... | collective-permute-start | bytes 98312 | tf_op jit(solution)/shard_map/ppermute | solution.py:269
  34.1 1.7 %collective-permute-done.7.arrived_ref = bf16[128,128]{1,0:T(8,128)(2,1)S(1)} collective-permute-done((bf16[128,128]{1,0:T(8,128)(2,1)S(1)}, bf16[128,128]{1,0:T(8,128)(2,1)S(1)}, u32[]{:S(2)}, u32[]{:S(2)}) %collective-permute-start.7) | collective-permute-done | bytes 32800 | tf_op jit(solution)/shard_map/ppermute | solution.py:185
  35.9 0.6 %collective-permute-start.8 = (bf16[128,128]{1,0:T(8,128)(2,1)S(1)}, bf16[128,128]{1,0:T(8,128)(2,1)S(1)}, u32[]{:S(2)}, u32[]{:S(2)}) collective-permute-start(bf16[128,128]{1,0:T(8,128)(2,1)S(1)} %shard_map.71), channel_id=1, source_target_pairs={{0,8},{4,0},{8,12},{12,4},{1,9},{5,1},{9,13},{13,5},{2,10},{6,2},{... | collective-permute-start | bytes 98312 | tf_op jit(solution)/shard_map/ppermute | solution.py:269
  36.5 4.5 %collective-permute-done.5.first_ref = bf16[128,128]{1,0:T(8,128)(2,1)S(1)} collective-permute-done((bf16[128,128]{1,0:T(8,128)(2,1)S(1)}, bf16[128,128]{1,0:T(8,128)(2,1)S(1)}, u32[]{:S(2)}, u32[]{:S(2)}) %collective-permute-start.5) | collective-permute-done | bytes 32800 | tf_op jit(solution)/shard_map/ppermute | solution.py:269
  40.9 0.0 collective-permute-done.1.documents_ref
  40.9 0.2 collective-permute-done.8.second_ref
  41.1 0.4 shard_map.73
  41.6 0.2 collective-permute-start.9
  41.7 0.4 shard_map.72.refs_0_
  42.2 0.8 %collective-permute-done.9.refs_1_ = f32[256,128]{1,0:T(8,128)S(1)} collective-permute-done((f32[256,128]{1,0:T(8,128)S(1)}, f32[256,128]{1,0:T(8,128)S(1)}, u32[]{:S(2)}, u32[]{:S(2)}) %collective-permute-start.9) | collective-permute-done | bytes 131104 | tf_op jit(solution)/shard_map/ppermute | solution.py:185
  43.0 3.5 %collective-permute-start.10 = (bf16[256,128]{1,0:T(8,128)(2,1)S(1)}, bf16[256,128]{1,0:T(8,128)(2,1)S(1)}, u32[]{:S(2)}, u32[]{:S(2)}) collective-permute-start(bf16[256,128]{1,0:T(8,128)(2,1)S(1)} %shard_map.74), channel_id=1, source_target_pairs={{0,14},{1,13},{2,12},{3,15},{4,10},{5,9},{6,8},{7,11},{8,6},{9,5},... | collective-permute-start | bytes 196616 | tf_op jit(solution)/shard_map/ppermute | solution.py:294
  46.5 3.6 %collective-permute-done.10.mine_ref = bf16[256,128]{1,0:T(8,128)(2,1)S(1)} collective-permute-done((bf16[256,128]{1,0:T(8,128)(2,1)S(1)}, bf16[256,128]{1,0:T(8,128)(2,1)S(1)}, u32[]{:S(2)}, u32[]{:S(2)}) %collective-permute-start.10) | collective-permute-done | bytes 65568 | tf_op jit(solution)/shard_map/ppermute | solution.py:294
  50.0 0.0 collective-permute-start.11
  50.0 0.7 %shard_map.75.scores_hbm = f32[4,128,128]{2,1,0:T(8,128)} custom-call(f32[128,128]{1,0:T(8,128)S(1)} %get-tuple-element.46.own_ref, bf16[128,128]{1,0:T(8,128)(2,1)S(1)} %collective-permute-done.5.first_ref, bf16[128,128]{1,0:T(8,128)(2,1)S(1)} %collective-permute-done.8.second_ref), custom_call_target="tpu_custom_call" | custom-call | tf_op jit(solution)/shard_map/pallas_call | solution.py:147
  50.8 0.5 %collective-permute-done.11.arrived_ref = bf16[256,128]{1,0:T(8,128)(2,1)S(1)} collective-permute-done((bf16[256,128]{1,0:T(8,128)(2,1)S(1)}, bf16[256,128]{1,0:T(8,128)(2,1)S(1)}, u32[]{:S(2)}, u32[]{:S(2)}) %collective-permute-start.11) | collective-permute-done | bytes 65568 | tf_op jit(solution)/shard_map/ppermute | solution.py:185
  51.3 0.6 %shard_map.76 = f32[4,128,128]{2,1,0:T(8,128)} custom-call(bf16[256,128]{1,0:T(8,128)(2,1)S(1)} %collective-permute-done.10.mine_ref, bf16[256,128]{1,0:T(8,128)(2,1)S(1)} %collective-permute-done.11.arrived_ref, f32[4,128,128]{2,1,0:T(8,128)} %shard_map.75.scores_hbm), custom_call_target="tpu_custom_call", output_to_operand_aliasing={{}: (2, {})} | custom-call | tf_op jit(solution)/shard_map/pallas_call | solution.py:241
  (5 shorter events, 0.1 us)
Async XLA Ops:
  0.0 10.2 %copy-start.1 = (bf16[128,2048]{1,0:T(8,128)(2,1)S(1)}, bf16[128,2048]{1,0:T(8,128)(2,1)}, u32[]{:S(2)}) copy-start(bf16[128,2048]{1,0:T(8,128)(2,1)} %documents_ref) | copy-start | bytes 1572868
  0.0 10.3 %copy-start.2 = (s32[512]{0:T(512)S(1)}, s32[512]{0:T(512)}, u32[]{:S(2)}) copy-start(s32[512]{0:T(512)} %param.11) | copy-start | bytes 6148
  0.0 16.7 %collective-permute-start = (bf16[128,2048]{1,0:T(8,128)(2,1)}, bf16[128,2048]{1,0:T(8,128)(2,1)S(1)}, u32[]{:S(2)}, u32[]{:S(2)}) collective-permute-start(bf16[128,2048]{1,0:T(8,128)(2,1)} %documents_ref), channel_id=1, source_target_pairs={{0,8},{8,12},{12,4},{4,0},{1,9},{9,13},{13,5},{5,1},{2,10},{10,14}... | collective-permute-start | bytes 1572872 | tf_op jit(solution)/shard_map/ppermute | solution.py:271
  10.2 19.5 %collective-permute-start.2 = (bf16[128,2048]{1,0:T(8,128)(2,1)S(1)}, bf16[128,2048]{1,0:T(8,128)(2,1)S(1)}, u32[]{:S(2)}, u32[]{:S(2)}) collective-permute-start(bf16[128,2048]{1,0:T(8,128)(2,1)S(1)} %copy-done.1), channel_id=1, source_target_pairs={{0,4},{4,12},{12,8},{8,0},{1,5},{5,13},{13,9},{9,1},{2,6},{6,14},{... | collective-permute-start | bytes 1572872 | tf_op jit(solution)/shard_map/ppermute | solution.py:273
  10.4 1.6 %copy-start = (bf16[512,2048]{1,0:T(8,128)(2,1)S(1)}, bf16[512,2048]{1,0:T(8,128)(2,1)}, u32[]{:S(2)}) copy-start(bf16[512,2048]{1,0:T(8,128)(2,1)} %shard_map.64.queries_ref) | copy-start | bytes 6291460
  17.5 3.4 %collective-permute-start.3 = (f32[256,256]{1,0:T(8,128)S(1)}, f32[256,256]{1,0:T(8,128)S(1)}, u32[]{:S(2)}, u32[]{:S(2)}) collective-permute-start(f32[256,256]{1,0:T(8,128)S(1)} %get-tuple-element.35), channel_id=1, source_target_pairs={{0,1},{1,0},{2,3},{3,2},{4,5},{5,4},{6,7},{7,6},{8,9},{9,8},{10,11... | collective-permute-start | bytes 786440 | tf_op jit(solution)/shard_map/ppermute | solution.py:185
  17.6 23.4 %collective-permute-start.1 = (bf16[128,2048]{1,0:T(8,128)(2,1)S(1)}, bf16[128,2048]{1,0:T(8,128)(2,1)S(1)}, u32[]{:S(2)}, u32[]{:S(2)}) collective-permute-start(bf16[128,2048]{1,0:T(8,128)(2,1)S(1)} %collective-permute-done.documents_ref), channel_id=1, source_target_pairs={{0,8},{8,12},{12,4},{4,0},{1,9},{9,13},{13,5},{5,1},{2,10},{10,14}... | collective-permute-start | bytes 1572872 | tf_op jit(solution)/shard_map/ppermute | solution.py:276
  20.9 4.3 %collective-permute-start.4 = (bf16[128,256]{1,0:T(8,128)(2,1)S(1)}, bf16[128,256]{1,0:T(8,128)(2,1)S(1)}, u32[]{:S(2)}, u32[]{:S(2)}) collective-permute-start(bf16[128,256]{1,0:T(8,128)(2,1)S(1)} %get-tuple-element.37), channel_id=1, source_target_pairs={{0,2},{1,3},{2,0},{3,1},{4,6},{5,7},{6,4},{7,5},{8,10},{9,11},{10,... | collective-permute-start | bytes 196616 | tf_op jit(solution)/shard_map/ppermute | solution.py:185
  30.4 1.4 %collective-permute-start.6 = (f32[256,128]{1,0:T(8,128)S(1)}, f32[256,128]{1,0:T(8,128)S(1)}, u32[]{:S(2)}, u32[]{:S(2)}) collective-permute-start(f32[256,128]{1,0:T(8,128)S(1)} %get-tuple-element.42), channel_id=1, source_target_pairs={{0,1},{1,0},{2,3},{3,2},{4,5},{5,4},{6,7},{7,6},{8,9},{9,8},{10,11... | collective-permute-start | bytes 393224 | tf_op jit(solution)/shard_map/ppermute | solution.py:185
  31.9 4.0 %collective-permute-start.7 = (bf16[128,128]{1,0:T(8,128)(2,1)S(1)}, bf16[128,128]{1,0:T(8,128)(2,1)S(1)}, u32[]{:S(2)}, u32[]{:S(2)}) collective-permute-start(bf16[128,128]{1,0:T(8,128)(2,1)S(1)} %get-tuple-element.44), channel_id=1, source_target_pairs={{0,2},{1,3},{2,0},{3,1},{4,6},{5,7},{6,4},{7,5},{8,10},{9,11},{10,... | collective-permute-start | bytes 98312 | tf_op jit(solution)/shard_map/ppermute | solution.py:185
  33.4 7.5 %collective-permute-start.5 = (bf16[128,128]{1,0:T(8,128)(2,1)S(1)}, bf16[128,128]{1,0:T(8,128)(2,1)S(1)}, u32[]{:S(2)}, u32[]{:S(2)}) collective-permute-start(bf16[128,128]{1,0:T(8,128)(2,1)S(1)} %get-tuple-element.39), channel_id=1, source_target_pairs={{0,4},{4,12},{8,0},{12,8},{1,5},{5,13},{9,1},{13,9},{2,6},{6,14},{... | collective-permute-start | bytes 98312 | tf_op jit(solution)/shard_map/ppermute | solution.py:269
  35.9 5.3 %collective-permute-start.8 = (bf16[128,128]{1,0:T(8,128)(2,1)S(1)}, bf16[128,128]{1,0:T(8,128)(2,1)S(1)}, u32[]{:S(2)}, u32[]{:S(2)}) collective-permute-start(bf16[128,128]{1,0:T(8,128)(2,1)S(1)} %shard_map.71), channel_id=1, source_target_pairs={{0,8},{4,0},{8,12},{12,4},{1,9},{5,1},{9,13},{13,5},{2,10},{6,2},{... | collective-permute-start | bytes 98312 | tf_op jit(solution)/shard_map/ppermute | solution.py:269
  41.6 1.4 %collective-permute-start.9 = (f32[256,128]{1,0:T(8,128)S(1)}, f32[256,128]{1,0:T(8,128)S(1)}, u32[]{:S(2)}, u32[]{:S(2)}) collective-permute-start(f32[256,128]{1,0:T(8,128)S(1)} %shard_map.73), channel_id=1, source_target_pairs={{0,1},{1,0},{2,3},{3,2},{4,5},{5,4},{6,7},{7,6},{8,9},{9,8},{10,11... | collective-permute-start | bytes 393224 | tf_op jit(solution)/shard_map/ppermute | solution.py:185
  43.0 7.0 %collective-permute-start.10 = (bf16[256,128]{1,0:T(8,128)(2,1)S(1)}, bf16[256,128]{1,0:T(8,128)(2,1)S(1)}, u32[]{:S(2)}, u32[]{:S(2)}) collective-permute-start(bf16[256,128]{1,0:T(8,128)(2,1)S(1)} %shard_map.74), channel_id=1, source_target_pairs={{0,14},{1,13},{2,12},{3,15},{4,10},{5,9},{6,8},{7,11},{8,6},{9,5},... | collective-permute-start | bytes 196616 | tf_op jit(solution)/shard_map/ppermute | solution.py:294
  50.0 1.3 %collective-permute-start.11 = (bf16[256,128]{1,0:T(8,128)(2,1)S(1)}, bf16[256,128]{1,0:T(8,128)(2,1)S(1)}, u32[]{:S(2)}, u32[]{:S(2)}) collective-permute-start(bf16[256,128]{1,0:T(8,128)(2,1)S(1)} %collective-permute-done.10.mine_ref), channel_id=1, source_target_pairs={{0,1},{1,0},{2,3},{3,2},{4,5},{5,4},{6,7},{7,6},{8,9},{9,8},{10,11... | collective-permute-start | bytes 196616 | tf_op jit(solution)/shard_map/ppermute | solution.py:185

commit v19 on v14

--- a/solution.py
+++ b/solution.py
@@ -128,7 +128,8 @@
     rows = out_ref.shape[0]
     chip = target_chip() if kept else 1 - target_chip()
     spot = pl.ds(pl.multiple_of(chip * rows, rows), rows)
-    out_ref[...] = masked_tile(queries_ref[spot, :], documents_ref[...], ids_ref[spot, :], block_of(row_index()))
+    tile = masked_tile(queries_ref[spot, :], documents_ref[...], ids_ref[spot, :], block_of(row_index()))
+    out_ref[...] = tile.astype(out_ref.dtype)
 
 
 def total_of(refs):
@@ -225,11 +226,19 @@
         out_ref[step_of(table)(row_index())] = ref[...].astype(jnp.float32)
 
 
+def core_share(rows, own):
+    core = lax.rem(layer_index(), 2)
+    return pl.ds(pl.multiple_of((core if own else 1 - core) * rows, rows), rows)
+
+
+def other_share_kernel(mine_ref, out_ref):
+    out_ref[...] = mine_ref[core_share(out_ref.shape[0], False), :]
+
+
 def finish_kernel(mine_ref, arrived_ref, scores_hbm, out_hbm, total, copied):
     del scores_hbm
-    rows = total.shape[0]
-    share = pl.ds(pl.multiple_of(lax.rem(layer_index(), 2) * rows, rows), rows)
-    total[...] = mine_ref[share, :].astype(jnp.float32) + arrived_ref[share, :].astype(jnp.float32)
+    mine = mine_ref[core_share(total.shape[0], True), :].astype(jnp.float32)
+    total[...] = mine + arrived_ref[...].astype(jnp.float32)
     copy = pltpu.make_async_copy(total, out_hbm.at[step_of(BLOCK_LAST)(row_index())], copied)
     copy.start()
     copy.wait()
@@ -262,7 +271,7 @@
 
     def one_half(block, block_of, kept):
         kernel = functools.partial(half_kernel, block_of, kept)
-        out_shape = [jax.ShapeDtypeStruct(half, jnp.float32)]
+        out_shape = [jax.ShapeDtypeStruct(half, jnp.float32 if kept else jnp.bfloat16)]
         return scoring(kernel, out_shape, conditioned, query_ids, block)[0]
 
     def back(total, table):
@@ -294,7 +303,8 @@
     mine = lax.ppermute(both, ("rows", "layer"), pairs)
     out_shape = [jax.ShapeDtypeStruct((STEPS,) + own.shape, jnp.float32)]
     (scores,) = small_call(assemble_kernel, out_shape, own, first, second)
-    return finish(mine, swap(mine, 1), scores)
+    (other,) = small_call(other_share_kernel, [jax.ShapeDtypeStruct(own.shape, jnp.bfloat16)], mine)
+    return finish(mine, swap(other, 1), scores)
 
 
 def around_ring(documents, conditioned, query_ids):

time: 51.8 us -> 51.7 us (level)
  no operation moved by 1% of the time
where the time goes in v19:
time: 51.7 us; the launch traced here: 51.5 us
  waiting for transfers between devices  24.2 us (47%)
  starting transfers between devices  14.6 us (28%)
  Pallas kernels  10.8 us (21%)
  local copies, waits for them, and re-layouts  1.74 us (3%)
    ppermute x6, waiting for transfers between devices, swap(): lax.ppermute(value, 'layer', [(lay, lay ^ distance) for lay in range(coun...  7.07 us
    pallas_call x1, Pallas kernels, prepare(): pl.pallas_call(prepare_kernel, out_shape=jax.ShapeDtypeStruct((rows, dims...  6.15 us
    ppermute x2, waiting for transfers between devices, back(): return lax.ppermute(total, 'rows', tuple(enumerate(table)))  4.65 us
    ppermute x1, waiting for transfers between devices, along_line(): two = lax.ppermute(later, 'rows', ROUND_TWO)  4.39 us
    ppermute x1, waiting for transfers between devices, along_line(): mine = lax.ppermute(both, ('rows', 'layer'), pairs)  4.19 us
    ppermute x1, starting transfers between devices, along_line(): one = lax.ppermute(documents, 'rows', ROUND_ONE)  4.04 us
    ppermute x1, waiting for transfers between devices, along_line(): one = lax.ppermute(documents, 'rows', ROUND_ONE)  3.93 us
    ppermute x6, starting transfers between devices, swap(): lax.ppermute(value, 'layer', [(lay, lay ^ distance) for lay in range(coun...  3.41 us
  transfers between devices with their start and end apart: 12, of which 10 were waited for; matrix products, arithmetic and copies ran while one was open for 0% of the time, Pallas kernels for 19%

profile of v19, /device:TPU:0, one launch (start us, length us, event | category | flops | bytes accessed | tf_op | source)
XLA Modules:
  0.0 51.5 jit_solution(15291466766875427332)
XLA Ops:
  0.0 0.0 copy-start.1
  0.0 0.0 copy-start.2
  0.0 4.0 %collective-permute-start = (bf16[128,2048]{1,0:T(8,128)(2,1)}, bf16[128,2048]{1,0:T(8,128)(2,1)S(1)}, u32[]{:S(2)}, u32[]{:S(2)}) collective-permute-start(bf16[128,2048]{1,0:T(8,128)(2,1)} %documents_ref), channel_id=1, source_target_pairs={{0,8},{8,12},{12,4},{4,0},{1,9},{9,13},{13,5},{5,1},{2,10},{10,14}... | collective-permute-start | bytes 1572872 | tf_op jit(solution)/shard_map/ppermute | solution.py:280
  4.0 6.2 %shard_map.64.queries_ref = bf16[512,2048]{1,0:T(8,128)(2,1)} custom-call(s32[4]{0:T(128)} %offsets.1, bf16[512,2048]{1,0:T(8,128)(2,1)} %queries_hbm.1, bf16[4,512,512]{2,1,0:T(8,128)(2,1)} %bases_hbm.1, f32[4,512]{1,0:T(4,128)} %values_hbm.1), custom_call_target="tpu_custom_call" | custom-call | flops 2147483648 | bytes 6291456 | tf_op jit(solution)/shard_map/pallas_call | solution.py:52
  10.2 0.0 copy-done.1
  10.2 0.1 collective-permute-start.2
  10.3 0.0 copy-done.2
  10.3 0.1 copy.11.ids_ref
  10.4 0.0 copy-start
  10.4 1.6 %copy-done = bf16[512,2048]{1,0:T(8,128)(2,1)S(1)} copy-done((bf16[512,2048]{1,0:T(8,128)(2,1)S(1)}, bf16[512,2048]{1,0:T(8,128)(2,1)}, u32[]{:S(2)}) %copy-start) | copy-done | bytes 2097176
  12.0 0.8 %shard_map.65 = (f32[256,128]{1,0:T(8,128)S(1)}, f32[256,128]{1,0:T(8,128)S(1)}) custom-call(bf16[512,2048]{1,0:T(8,128)(2,1)S(1)} %copy-done, s32[512,1]{1,0:T(8,128)S(1)} %copy.11.ids_ref, bf16[128,2048]{1,0:T(8,128)(2,1)S(1)} %copy-done.1), custom_call_target="tpu_custom_call" | custom-call | flops 268435456 | bytes 2621440 | tf_op jit(solution)/shard_map/pallas_call | solution.py:81
  12.8 3.9 %collective-permute-done.documents_ref = bf16[128,2048]{1,0:T(8,128)(2,1)S(1)} collective-permute-done((bf16[128,2048]{1,0:T(8,128)(2,1)}, bf16[128,2048]{1,0:T(8,128)(2,1)S(1)}, u32[]{:S(2)}, u32[]{:S(2)}) %collective-permute-start) | collective-permute-done | bytes 524320 | tf_op jit(solution)/shard_map/ppermute | solution.py:280
  16.7 0.8 %shard_map.66 = (f32[256,256]{1,0:T(8,128)S(1)}, f32[256,256]{1,0:T(8,128)S(1)}) custom-call(bf16[512,2048]{1,0:T(8,128)(2,1)S(1)} %copy-done, s32[512,1]{1,0:T(8,128)S(1)} %copy.11.ids_ref, bf16[128,2048]{1,0:T(8,128)(2,1)S(1)} %collective-permute-done.documents_ref, f32[256,128]{1,0:T(8,128)S(1)} %get-tuple-element.32.refs_0_, ...), custom_call_target="tpu_custom_call" | custom-call | flops 268435456 | bytes 2621440 | tf_op jit(solution)/shard_map/pallas_call | solution.py:81
  17.5 0.1 collective-permute-start.3
  17.6 3.3 %collective-permute-start.1 = (bf16[128,2048]{1,0:T(8,128)(2,1)S(1)}, bf16[128,2048]{1,0:T(8,128)(2,1)S(1)}, u32[]{:S(2)}, u32[]{:S(2)}) collective-permute-start(bf16[128,2048]{1,0:T(8,128)(2,1)S(1)} %collective-permute-done.documents_ref), channel_id=1, source_target_pairs={{0,8},{8,12},{12,4},{4,0},{1,9},{9,13},{13,5},{5,1},{2,10},{10,14}... | collective-permute-start | bytes 1572872 | tf_op jit(solution)/shard_map/ppermute | solution.py:285
  20.9 0.0 collective-permute-done.3.arrived_ref
  20.9 1.6 %collective-permute-start.4 = (bf16[128,256]{1,0:T(8,128)(2,1)S(1)}, bf16[128,256]{1,0:T(8,128)(2,1)S(1)}, u32[]{:S(2)}, u32[]{:S(2)}) collective-permute-start(bf16[128,256]{1,0:T(8,128)(2,1)S(1)} %get-tuple-element.37), channel_id=1, source_target_pairs={{0,2},{1,3},{2,0},{3,1},{4,6},{5,7},{6,4},{7,5},{8,10},{9,11},{10,... | collective-permute-start | bytes 196616 | tf_op jit(solution)/shard_map/ppermute | solution.py:186
  22.5 2.8 %collective-permute-done.4.arrived_ref = bf16[128,256]{1,0:T(8,128)(2,1)S(1)} collective-permute-done((bf16[128,256]{1,0:T(8,128)(2,1)S(1)}, bf16[128,256]{1,0:T(8,128)(2,1)S(1)}, u32[]{:S(2)}, u32[]{:S(2)}) %collective-permute-start.4) | collective-permute-done | bytes 65568 | tf_op jit(solution)/shard_map/ppermute | solution.py:186
  25.3 4.4 %collective-permute-done.2.documents_ref = bf16[128,2048]{1,0:T(8,128)(2,1)S(1)} collective-permute-done((bf16[128,2048]{1,0:T(8,128)(2,1)S(1)}, bf16[128,2048]{1,0:T(8,128)(2,1)S(1)}, u32[]{:S(2)}, u32[]{:S(2)}) %collective-permute-start.2) | collective-permute-done | bytes 524320 | tf_op jit(solution)/shard_map/ppermute | solution.py:282
  29.7 0.8 %shard_map.69 = (f32[256,128]{1,0:T(8,128)S(1)}, f32[256,128]{1,0:T(8,128)S(1)}) custom-call(bf16[512,2048]{1,0:T(8,128)(2,1)S(1)} %copy-done, s32[512,1]{1,0:T(8,128)S(1)} %copy.11.ids_ref, bf16[128,2048]{1,0:T(8,128)(2,1)S(1)} %collective-permute-done.2.documents_ref), custom_call_target="tpu_custom_call" | custom-call | flops 268435456 | bytes 2621440 | tf_op jit(solution)/shard_map/pallas_call | solution.py:81
  30.4 0.1 collective-permute-start.6
  30.5 1.3 %collective-permute-done.6.arrived_ref = f32[256,128]{1,0:T(8,128)S(1)} collective-permute-done((f32[256,128]{1,0:T(8,128)S(1)}, f32[256,128]{1,0:T(8,128)S(1)}, u32[]{:S(2)}, u32[]{:S(2)}) %collective-permute-start.6) | collective-permute-done | bytes 131104 | tf_op jit(solution)/shard_map/ppermute | solution.py:186
  31.9 1.6 %collective-permute-start.7 = (bf16[128,128]{1,0:T(8,128)(2,1)S(1)}, bf16[128,128]{1,0:T(8,128)(2,1)S(1)}, u32[]{:S(2)}, u32[]{:S(2)}) collective-permute-start(bf16[128,128]{1,0:T(8,128)(2,1)S(1)} %get-tuple-element.44), channel_id=1, source_target_pairs={{0,2},{1,3},{2,0},{3,1},{4,6},{5,7},{6,4},{7,5},{8,10},{9,11},{10,... | collective-permute-start | bytes 98312 | tf_op jit(solution)/shard_map/ppermute | solution.py:186
  33.4 0.7 %collective-permute-start.5 = (bf16[128,128]{1,0:T(8,128)(2,1)S(1)}, bf16[128,128]{1,0:T(8,128)(2,1)S(1)}, u32[]{:S(2)}, u32[]{:S(2)}) collective-permute-start(bf16[128,128]{1,0:T(8,128)(2,1)S(1)} %get-tuple-element.39), channel_id=1, source_target_pairs={{0,4},{4,12},{8,0},{12,8},{1,5},{5,13},{9,1},{13,9},{2,6},{6,14},{... | collective-permute-start | bytes 98312 | tf_op jit(solution)/shard_map/ppermute | solution.py:278
  34.1 1.7 %collective-permute-done.7.arrived_ref = bf16[128,128]{1,0:T(8,128)(2,1)S(1)} collective-permute-done((bf16[128,128]{1,0:T(8,128)(2,1)S(1)}, bf16[128,128]{1,0:T(8,128)(2,1)S(1)}, u32[]{:S(2)}, u32[]{:S(2)}) %collective-permute-start.7) | collective-permute-done | bytes 32800 | tf_op jit(solution)/shard_map/ppermute | solution.py:186
  35.9 0.6 %collective-permute-start.8 = (bf16[128,128]{1,0:T(8,128)(2,1)S(1)}, bf16[128,128]{1,0:T(8,128)(2,1)S(1)}, u32[]{:S(2)}, u32[]{:S(2)}) collective-permute-start(bf16[128,128]{1,0:T(8,128)(2,1)S(1)} %shard_map.71), channel_id=1, source_target_pairs={{0,8},{4,0},{8,12},{12,4},{1,9},{5,1},{9,13},{13,5},{2,10},{6,2},{... | collective-permute-start | bytes 98312 | tf_op jit(solution)/shard_map/ppermute | solution.py:278
  36.5 4.5 %collective-permute-done.5.first_ref = bf16[128,128]{1,0:T(8,128)(2,1)S(1)} collective-permute-done((bf16[128,128]{1,0:T(8,128)(2,1)S(1)}, bf16[128,128]{1,0:T(8,128)(2,1)S(1)}, u32[]{:S(2)}, u32[]{:S(2)}) %collective-permute-start.5) | collective-permute-done | bytes 32800 | tf_op jit(solution)/shard_map/ppermute | solution.py:278
  40.9 0.0 collective-permute-done.1.documents_ref
  40.9 0.2 collective-permute-done.8.second_ref
  41.1 0.4 shard_map.73
  41.6 0.2 collective-permute-start.9
  41.7 0.4 shard_map.72.refs_0_
  42.2 0.7 %collective-permute-done.9.refs_1_ = bf16[256,128]{1,0:T(8,128)(2,1)S(1)} collective-permute-done((bf16[256,128]{1,0:T(8,128)(2,1)S(1)}, bf16[256,128]{1,0:T(8,128)(2,1)S(1)}, u32[]{:S(2)}, u32[]{:S(2)}) %collective-permute-start.9) | collective-permute-done | bytes 65568 | tf_op jit(solution)/shard_map/ppermute | solution.py:186
  42.9 2.5 %collective-permute-start.10 = (bf16[256,128]{1,0:T(8,128)(2,1)S(1)}, bf16[256,128]{1,0:T(8,128)(2,1)S(1)}, u32[]{:S(2)}, u32[]{:S(2)}) collective-permute-start(bf16[256,128]{1,0:T(8,128)(2,1)S(1)} %shard_map.74), channel_id=1, source_target_pairs={{0,12},{1,15},{2,14},{3,13},{4,8},{5,11},{6,10},{7,9},{8,4},{9,7},... | collective-permute-start | bytes 196616 | tf_op jit(solution)/shard_map/ppermute | solution.py:303
  45.4 4.2 %collective-permute-done.10.mine_ref = bf16[256,128]{1,0:T(8,128)(2,1)S(1)} collective-permute-done((bf16[256,128]{1,0:T(8,128)(2,1)S(1)}, bf16[256,128]{1,0:T(8,128)(2,1)S(1)}, u32[]{:S(2)}, u32[]{:S(2)}) %collective-permute-start.10) | collective-permute-done | bytes 65568 | tf_op jit(solution)/shard_map/ppermute | solution.py:303
  49.6 0.0 collective-permute-start.11
  49.6 0.7 %shard_map.76.scores_hbm = f32[4,128,128]{2,1,0:T(8,128)} custom-call(f32[128,128]{1,0:T(8,128)S(1)} %get-tuple-element.46.own_ref, bf16[128,128]{1,0:T(8,128)(2,1)S(1)} %collective-permute-done.5.first_ref, bf16[128,128]{1,0:T(8,128)(2,1)S(1)} %collective-permute-done.8.second_ref), custom_call_target="tpu_custom_call" | custom-call | tf_op jit(solution)/shard_map/pallas_call | solution.py:148
  50.3 0.5 collective-permute-done.11.arrived_ref
  50.8 0.6 %shard_map.77 = f32[4,128,128]{2,1,0:T(8,128)} custom-call(bf16[256,128]{1,0:T(8,128)(2,1)S(1)} %collective-permute-done.10.mine_ref, bf16[128,128]{1,0:T(8,128)(2,1)S(1)} %collective-permute-done.11.arrived_ref, f32[4,128,128]{2,1,0:T(8,128)} %shard_map.76.scores_hbm), custom_call_target="tpu_custom_call", output_to_operand_aliasing={{}: (2, {})} | custom-call | tf_op jit(solution)/shard_map/pallas_call | solution.py:250
  (6 shorter events, 0.1 us)
Async XLA Ops:
  0.0 10.2 %copy-start.1 = (bf16[128,2048]{1,0:T(8,128)(2,1)S(1)}, bf16[128,2048]{1,0:T(8,128)(2,1)}, u32[]{:S(2)}) copy-start(bf16[128,2048]{1,0:T(8,128)(2,1)} %documents_ref) | copy-start | bytes 1572868
  0.0 10.3 %copy-start.2 = (s32[512]{0:T(512)S(1)}, s32[512]{0:T(512)}, u32[]{:S(2)}) copy-start(s32[512]{0:T(512)} %param.11) | copy-start | bytes 6148
  0.0 16.7 %collective-permute-start = (bf16[128,2048]{1,0:T(8,128)(2,1)}, bf16[128,2048]{1,0:T(8,128)(2,1)S(1)}, u32[]{:S(2)}, u32[]{:S(2)}) collective-permute-start(bf16[128,2048]{1,0:T(8,128)(2,1)} %documents_ref), channel_id=1, source_target_pairs={{0,8},{8,12},{12,4},{4,0},{1,9},{9,13},{13,5},{5,1},{2,10},{10,14}... | collective-permute-start | bytes 1572872 | tf_op jit(solution)/shard_map/ppermute | solution.py:280
  10.2 19.5 %collective-permute-start.2 = (bf16[128,2048]{1,0:T(8,128)(2,1)S(1)}, bf16[128,2048]{1,0:T(8,128)(2,1)S(1)}, u32[]{:S(2)}, u32[]{:S(2)}) collective-permute-start(bf16[128,2048]{1,0:T(8,128)(2,1)S(1)} %copy-done.1), channel_id=1, source_target_pairs={{0,4},{4,12},{12,8},{8,0},{1,5},{5,13},{13,9},{9,1},{2,6},{6,14},{... | collective-permute-start | bytes 1572872 | tf_op jit(solution)/shard_map/ppermute | solution.py:282
  10.4 1.6 %copy-start = (bf16[512,2048]{1,0:T(8,128)(2,1)S(1)}, bf16[512,2048]{1,0:T(8,128)(2,1)}, u32[]{:S(2)}) copy-start(bf16[512,2048]{1,0:T(8,128)(2,1)} %shard_map.64.queries_ref) | copy-start | bytes 6291460
  17.5 3.4 %collective-permute-start.3 = (f32[256,256]{1,0:T(8,128)S(1)}, f32[256,256]{1,0:T(8,128)S(1)}, u32[]{:S(2)}, u32[]{:S(2)}) collective-permute-start(f32[256,256]{1,0:T(8,128)S(1)} %get-tuple-element.35), channel_id=1, source_target_pairs={{0,1},{1,0},{2,3},{3,2},{4,5},{5,4},{6,7},{7,6},{8,9},{9,8},{10,11... | collective-permute-start | bytes 786440 | tf_op jit(solution)/shard_map/ppermute | solution.py:186
  17.6 23.4 %collective-permute-start.1 = (bf16[128,2048]{1,0:T(8,128)(2,1)S(1)}, bf16[128,2048]{1,0:T(8,128)(2,1)S(1)}, u32[]{:S(2)}, u32[]{:S(2)}) collective-permute-start(bf16[128,2048]{1,0:T(8,128)(2,1)S(1)} %collective-permute-done.documents_ref), channel_id=1, source_target_pairs={{0,8},{8,12},{12,4},{4,0},{1,9},{9,13},{13,5},{5,1},{2,10},{10,14}... | collective-permute-start | bytes 1572872 | tf_op jit(solution)/shard_map/ppermute | solution.py:285
  20.9 4.3 %collective-permute-start.4 = (bf16[128,256]{1,0:T(8,128)(2,1)S(1)}, bf16[128,256]{1,0:T(8,128)(2,1)S(1)}, u32[]{:S(2)}, u32[]{:S(2)}) collective-permute-start(bf16[128,256]{1,0:T(8,128)(2,1)S(1)} %get-tuple-element.37), channel_id=1, source_target_pairs={{0,2},{1,3},{2,0},{3,1},{4,6},{5,7},{6,4},{7,5},{8,10},{9,11},{10,... | collective-permute-start | bytes 196616 | tf_op jit(solution)/shard_map/ppermute | solution.py:186
  30.4 1.4 %collective-permute-start.6 = (f32[256,128]{1,0:T(8,128)S(1)}, f32[256,128]{1,0:T(8,128)S(1)}, u32[]{:S(2)}, u32[]{:S(2)}) collective-permute-start(f32[256,128]{1,0:T(8,128)S(1)} %get-tuple-element.42), channel_id=1, source_target_pairs={{0,1},{1,0},{2,3},{3,2},{4,5},{5,4},{6,7},{7,6},{8,9},{9,8},{10,11... | collective-permute-start | bytes 393224 | tf_op jit(solution)/shard_map/ppermute | solution.py:186
  31.9 4.0 %collective-permute-start.7 = (bf16[128,128]{1,0:T(8,128)(2,1)S(1)}, bf16[128,128]{1,0:T(8,128)(2,1)S(1)}, u32[]{:S(2)}, u32[]{:S(2)}) collective-permute-start(bf16[128,128]{1,0:T(8,128)(2,1)S(1)} %get-tuple-element.44), channel_id=1, source_target_pairs={{0,2},{1,3},{2,0},{3,1},{4,6},{5,7},{6,4},{7,5},{8,10},{9,11},{10,... | collective-permute-start | bytes 98312 | tf_op jit(solution)/shard_map/ppermute | solution.py:186
  33.4 7.5 %collective-permute-start.5 = (bf16[128,128]{1,0:T(8,128)(2,1)S(1)}, bf16[128,128]{1,0:T(8,128)(2,1)S(1)}, u32[]{:S(2)}, u32[]{:S(2)}) collective-permute-start(bf16[128,128]{1,0:T(8,128)(2,1)S(1)} %get-tuple-element.39), channel_id=1, source_target_pairs={{0,4},{4,12},{8,0},{12,8},{1,5},{5,13},{9,1},{13,9},{2,6},{6,14},{... | collective-permute-start | bytes 98312 | tf_op jit(solution)/shard_map/ppermute | solution.py:278
  35.9 5.3 %collective-permute-start.8 = (bf16[128,128]{1,0:T(8,128)(2,1)S(1)}, bf16[128,128]{1,0:T(8,128)(2,1)S(1)}, u32[]{:S(2)}, u32[]{:S(2)}) collective-permute-start(bf16[128,128]{1,0:T(8,128)(2,1)S(1)} %shard_map.71), channel_id=1, source_target_pairs={{0,8},{4,0},{8,12},{12,4},{1,9},{5,1},{9,13},{13,5},{2,10},{6,2},{... | collective-permute-start | bytes 98312 | tf_op jit(solution)/shard_map/ppermute | solution.py:278
  41.6 1.3 %collective-permute-start.9 = (bf16[256,128]{1,0:T(8,128)(2,1)S(1)}, bf16[256,128]{1,0:T(8,128)(2,1)S(1)}, u32[]{:S(2)}, u32[]{:S(2)}) collective-permute-start(bf16[256,128]{1,0:T(8,128)(2,1)S(1)} %shard_map.73), channel_id=1, source_target_pairs={{0,1},{1,0},{2,3},{3,2},{4,5},{5,4},{6,7},{7,6},{8,9},{9,8},{10,11... | collective-permute-start | bytes 196616 | tf_op jit(solution)/shard_map/ppermute | solution.py:186
  42.9 6.7 %collective-permute-start.10 = (bf16[256,128]{1,0:T(8,128)(2,1)S(1)}, bf16[256,128]{1,0:T(8,128)(2,1)S(1)}, u32[]{:S(2)}, u32[]{:S(2)}) collective-permute-start(bf16[256,128]{1,0:T(8,128)(2,1)S(1)} %shard_map.74), channel_id=1, source_target_pairs={{0,12},{1,15},{2,14},{3,13},{4,8},{5,11},{6,10},{7,9},{8,4},{9,7},... | collective-permute-start | bytes 196616 | tf_op jit(solution)/shard_map/ppermute | solution.py:303
  49.6 1.2 %collective-permute-start.11 = (bf16[128,128]{1,0:T(8,128)(2,1)S(1)}, bf16[128,128]{1,0:T(8,128)(2,1)S(1)}, u32[]{:S(2)}, u32[]{:S(2)}) collective-permute-start(bf16[128,128]{1,0:T(8,128)(2,1)S(1)} %shard_map.75), channel_id=1, source_target_pairs={{0,1},{1,0},{2,3},{3,2},{4,5},{5,4},{6,7},{7,6},{8,9},{9,8},{10,11... | collective-permute-start | bytes 98312 | tf_op jit(solution)/shard_map/ppermute | solution.py:186

commit v20 on v14

--- a/solution.py
+++ b/solution.py
@@ -73,7 +73,7 @@
     return jnp.where(query_ids == doc_ids, 0.0, tile)
 
 
-def scoring(kernel, out_shape, conditioned, query_ids, documents, extra=(), scratch=()):
+def scoring(kernel, out_shape, conditioned, query_ids, documents, extra=(), scratch=(), weight=1):
     dims = conditioned.shape[1]
     docs = documents.shape[0]
     rows = sum(shape.shape[0] for shape in out_shape)
@@ -86,7 +86,7 @@
         scratch_shapes=scratch,
         compiler_params=pltpu.CompilerParams(vmem_limit_bytes=12 * MIB),
         cost_estimate=pl.CostEstimate(
-            flops=2 * rows * docs * dims, bytes_accessed=2 * dims * (rows + docs), transcendentals=0
+            flops=2 * rows * docs * dims * weight, bytes_accessed=2 * dims * (rows + docs) * weight, transcendentals=0
         ),
     )(conditioned, query_ids, documents, *extra)
 
@@ -263,7 +263,8 @@
     def one_half(block, block_of, kept):
         kernel = functools.partial(half_kernel, block_of, kept)
         out_shape = [jax.ShapeDtypeStruct(half, jnp.float32)]
-        return scoring(kernel, out_shape, conditioned, query_ids, block)[0]
+        weight = 8 if kept else 1
+        return scoring(kernel, out_shape, conditioned, query_ids, block, weight=weight)[0]
 
     def back(total, table):
         return lax.ppermute(total, "rows", tuple(enumerate(table)))
@@ -277,12 +278,12 @@
 
     own, first = layer_sum(*halves(one, pick(BLOCK_ONE), own), (jnp.float32, jnp.bfloat16))
     two, first = lax.optimization_barrier((two, first))
-    first = back(first, BLOCK_ONE)
     (second,) = layer_sum(*halves(two, pick(BLOCK_TWO)), (jnp.bfloat16,))
-    second = back(second, BLOCK_TWO)
+    three, *_ = lax.optimization_barrier((three, first, second))
+    first, second = back(first, BLOCK_ONE), back(second, BLOCK_TWO)
+
+    arrived = swap(one_half(three, pick(BLOCK_LAST), False), 1)
     three, first, second = lax.optimization_barrier((three, first, second))
-
-    arrived = swap(one_half(three, pick(BLOCK_LAST), False), 1)
     kept = one_half(three, pick(BLOCK_LAST), True)
     (both,) = small_call(sum_kernel, [jax.ShapeDtypeStruct(half, jnp.bfloat16)], kept, arrived)
     shares = lax.axis_size("layer")

time: 51.8 us -> 50.8 us (0.981)
  waiting for transfers between devices: 24.4 us -> 23.4 us
    ppermute x2, waiting for transfers between devices: 4.65 us -> 0.22 us  [back(): return lax.ppermute(total, 'rows', tuple(enumerate(table)))]
    ppermute x1, waiting for transfers between devices: 0.01 us -> 3.62 us  [along_line(): three = lax.ppermute(one, 'rows', ROUND_ONE)]
    ppermute x1, waiting for transfers between devices: 4.39 us -> 2.93 us  [along_line(): two = lax.ppermute(later, 'rows', ROUND_TWO)]
    ppermute x6, waiting for transfers between devices: 7.21 us -> 8.59 us  [swap(): lax.ppermute(value, 'layer', [(lay, lay ^ distance) for lay in range(coun...]
  transfers between devices with their start and end apart: 12 -> 12, of which waited for: 10 -> 11; matrix products, arithmetic and copies ran while one was open for 0% -> 0% of each run, Pallas kernels for 19% -> 20%
where the time goes in v20:
time: 50.8 us; the launch traced here: 50.6 us
  waiting for transfers between devices  23.4 us (46%)
  starting transfers between devices  14.6 us (29%)
  Pallas kernels  10.8 us (21%)
  local copies, waits for them, and re-layouts  1.74 us (3%)
    ppermute x6, waiting for transfers between devices, swap(): lax.ppermute(value, 'layer', [(lay, lay ^ distance) for lay in range(coun...  8.59 us
    pallas_call x1, Pallas kernels, prepare(): pl.pallas_call(prepare_kernel, out_shape=jax.ShapeDtypeStruct((rows, dims...  6.15 us
    ppermute x1, waiting for transfers between devices, along_line(): mine = lax.ppermute(both, ('rows', 'layer'), pairs)  4.1 us
    ppermute x1, starting transfers between devices, along_line(): one = lax.ppermute(documents, 'rows', ROUND_ONE)  4.04 us
    ppermute x1, waiting for transfers between devices, along_line(): one = lax.ppermute(documents, 'rows', ROUND_ONE)  3.93 us
    ppermute x1, waiting for transfers between devices, along_line(): three = lax.ppermute(one, 'rows', ROUND_ONE)  3.62 us
    ppermute x6, starting transfers between devices, swap(): lax.ppermute(value, 'layer', [(lay, lay ^ distance) for lay in range(coun...  3.32 us
    ppermute x1, starting transfers between devices, along_line(): three = lax.ppermute(one, 'rows', ROUND_ONE)  3.28 us
  transfers between devices with their start and end apart: 12, of which 11 were waited for; matrix products, arithmetic and copies ran while one was open for 0% of the time, Pallas kernels for 20%

profile of v20, /device:TPU:0, one launch (start us, length us, event | category | flops | bytes accessed | tf_op | source)
XLA Modules:
  0.0 50.6 jit_solution(7695052206071081608)
XLA Ops:
  0.0 0.0 copy-start.1
  0.0 0.0 copy-start.2
  0.0 4.0 %collective-permute-start = (bf16[128,2048]{1,0:T(8,128)(2,1)}, bf16[128,2048]{1,0:T(8,128)(2,1)S(1)}, u32[]{:S(2)}, u32[]{:S(2)}) collective-permute-start(bf16[128,2048]{1,0:T(8,128)(2,1)} %documents_ref), channel_id=1, source_target_pairs={{0,8},{8,12},{12,4},{4,0},{1,9},{9,13},{13,5},{5,1},{2,10},{10,14}... | collective-permute-start | bytes 1572872 | tf_op jit(solution)/shard_map/ppermute | solution.py:272
  4.0 6.2 %shard_map.64.queries_ref = bf16[512,2048]{1,0:T(8,128)(2,1)} custom-call(s32[4]{0:T(128)} %offsets.1, bf16[512,2048]{1,0:T(8,128)(2,1)} %queries_hbm.1, bf16[4,512,512]{2,1,0:T(8,128)(2,1)} %bases_hbm.1, f32[4,512]{1,0:T(4,128)} %values_hbm.1), custom_call_target="tpu_custom_call" | custom-call | flops 2147483648 | bytes 6291456 | tf_op jit(solution)/shard_map/pallas_call | solution.py:52
  10.2 0.0 copy-done.1
  10.2 0.1 collective-permute-start.2
  10.3 0.0 copy-done.2
  10.3 0.1 copy.11.ids_ref
  10.4 0.0 copy-start
  10.4 1.6 %copy-done = bf16[512,2048]{1,0:T(8,128)(2,1)S(1)} copy-done((bf16[512,2048]{1,0:T(8,128)(2,1)S(1)}, bf16[512,2048]{1,0:T(8,128)(2,1)}, u32[]{:S(2)}) %copy-start) | copy-done | bytes 2097176
  12.0 0.8 %shard_map.65 = (f32[256,128]{1,0:T(8,128)S(1)}, f32[256,128]{1,0:T(8,128)S(1)}) custom-call(bf16[512,2048]{1,0:T(8,128)(2,1)S(1)} %copy-done, s32[512,1]{1,0:T(8,128)S(1)} %copy.11.ids_ref, bf16[128,2048]{1,0:T(8,128)(2,1)S(1)} %copy-done.1), custom_call_target="tpu_custom_call" | custom-call | flops 268435456 | bytes 2621440 | tf_op jit(solution)/shard_map/pallas_call | solution.py:81
  12.8 3.9 %collective-permute-done.documents_ref = bf16[128,2048]{1,0:T(8,128)(2,1)S(1)} collective-permute-done((bf16[128,2048]{1,0:T(8,128)(2,1)}, bf16[128,2048]{1,0:T(8,128)(2,1)S(1)}, u32[]{:S(2)}, u32[]{:S(2)}) %collective-permute-start) | collective-permute-done | bytes 524320 | tf_op jit(solution)/shard_map/ppermute | solution.py:272
  16.7 3.3 %collective-permute-start.1 = (bf16[128,2048]{1,0:T(8,128)(2,1)S(1)}, bf16[128,2048]{1,0:T(8,128)(2,1)S(1)}, u32[]{:S(2)}, u32[]{:S(2)}) collective-permute-start(bf16[128,2048]{1,0:T(8,128)(2,1)S(1)} %collective-permute-done.documents_ref), channel_id=1, source_target_pairs={{0,8},{8,12},{12,4},{4,0},{1,9},{9,13},{13,5},{5,1},{2,10},{10,14}... | collective-permute-start | bytes 1572872 | tf_op jit(solution)/shard_map/ppermute | solution.py:277
  20.0 0.8 %shard_map.66 = (f32[256,256]{1,0:T(8,128)S(1)}, f32[256,256]{1,0:T(8,128)S(1)}) custom-call(bf16[512,2048]{1,0:T(8,128)(2,1)S(1)} %copy-done, s32[512,1]{1,0:T(8,128)S(1)} %copy.11.ids_ref, bf16[128,2048]{1,0:T(8,128)(2,1)S(1)} %collective-permute-done.documents_ref, f32[256,128]{1,0:T(8,128)S(1)} %get-tuple-element.33.refs_0_, ...), custom_call_target="tpu_custom_call" | custom-call | flops 268435456 | bytes 2621440 | tf_op jit(solution)/shard_map/pallas_call | solution.py:81
  20.8 0.1 collective-permute-start.3
  20.8 1.5 %collective-permute-done.3.arrived_ref = f32[256,256]{1,0:T(8,128)S(1)} collective-permute-done((f32[256,256]{1,0:T(8,128)S(1)}, f32[256,256]{1,0:T(8,128)S(1)}, u32[]{:S(2)}, u32[]{:S(2)}) %collective-permute-start.3) | collective-permute-done | bytes 262176 | tf_op jit(solution)/shard_map/ppermute | solution.py:185
  22.4 1.6 %collective-permute-start.4 = (bf16[128,256]{1,0:T(8,128)(2,1)S(1)}, bf16[128,256]{1,0:T(8,128)(2,1)S(1)}, u32[]{:S(2)}, u32[]{:S(2)}) collective-permute-start(bf16[128,256]{1,0:T(8,128)(2,1)S(1)} %get-tuple-element.38), channel_id=1, source_target_pairs={{0,2},{1,3},{2,0},{3,1},{4,6},{5,7},{6,4},{7,5},{8,10},{9,11},{10,... | collective-permute-start | bytes 196616 | tf_op jit(solution)/shard_map/ppermute | solution.py:185
  24.0 2.8 %collective-permute-done.4.arrived_ref = bf16[128,256]{1,0:T(8,128)(2,1)S(1)} collective-permute-done((bf16[128,256]{1,0:T(8,128)(2,1)S(1)}, bf16[128,256]{1,0:T(8,128)(2,1)S(1)}, u32[]{:S(2)}, u32[]{:S(2)}) %collective-permute-start.4) | collective-permute-done | bytes 65568 | tf_op jit(solution)/shard_map/ppermute | solution.py:185
  26.7 2.9 %collective-permute-done.2.documents_ref = bf16[128,2048]{1,0:T(8,128)(2,1)S(1)} collective-permute-done((bf16[128,2048]{1,0:T(8,128)(2,1)S(1)}, bf16[128,2048]{1,0:T(8,128)(2,1)S(1)}, u32[]{:S(2)}, u32[]{:S(2)}) %collective-permute-start.2) | collective-permute-done | bytes 524320 | tf_op jit(solution)/shard_map/ppermute | solution.py:274
  29.7 0.8 %shard_map.69 = (f32[256,128]{1,0:T(8,128)S(1)}, f32[256,128]{1,0:T(8,128)S(1)}) custom-call(bf16[512,2048]{1,0:T(8,128)(2,1)S(1)} %copy-done, s32[512,1]{1,0:T(8,128)S(1)} %copy.11.ids_ref, bf16[128,2048]{1,0:T(8,128)(2,1)S(1)} %collective-permute-done.2.documents_ref), custom_call_target="tpu_custom_call" | custom-call | flops 268435456 | bytes 2621440 | tf_op jit(solution)/shard_map/pallas_call | solution.py:81
  30.4 0.1 collective-permute-start.5
  30.5 1.3 %collective-permute-done.5.arrived_ref = f32[256,128]{1,0:T(8,128)S(1)} collective-permute-done((f32[256,128]{1,0:T(8,128)S(1)}, f32[256,128]{1,0:T(8,128)S(1)}, u32[]{:S(2)}, u32[]{:S(2)}) %collective-permute-start.5) | collective-permute-done | bytes 131104 | tf_op jit(solution)/shard_map/ppermute | solution.py:185
  31.9 1.6 %collective-permute-start.6 = (bf16[128,128]{1,0:T(8,128)(2,1)S(1)}, bf16[128,128]{1,0:T(8,128)(2,1)S(1)}, u32[]{:S(2)}, u32[]{:S(2)}) collective-permute-start(bf16[128,128]{1,0:T(8,128)(2,1)S(1)} %get-tuple-element.45), channel_id=1, source_target_pairs={{0,2},{1,3},{2,0},{3,1},{4,6},{5,7},{6,4},{7,5},{8,10},{9,11},{10,... | collective-permute-start | bytes 98312 | tf_op jit(solution)/shard_map/ppermute | solution.py:185
  33.4 0.7 %collective-permute-start.7 = (bf16[128,128]{1,0:T(8,128)(2,1)S(1)}, bf16[128,128]{1,0:T(8,128)(2,1)S(1)}, u32[]{:S(2)}, u32[]{:S(2)}) collective-permute-start(bf16[128,128]{1,0:T(8,128)(2,1)S(1)} %get-tuple-element.40), channel_id=1, source_target_pairs={{0,4},{4,12},{8,0},{12,8},{1,5},{5,13},{9,1},{13,9},{2,6},{6,14},{... | collective-permute-start | bytes 98312 | tf_op jit(solution)/shard_map/ppermute | solution.py:270
  34.1 1.8 %collective-permute-done.6.arrived_ref = bf16[128,128]{1,0:T(8,128)(2,1)S(1)} collective-permute-done((bf16[128,128]{1,0:T(8,128)(2,1)S(1)}, bf16[128,128]{1,0:T(8,128)(2,1)S(1)}, u32[]{:S(2)}, u32[]{:S(2)}) %collective-permute-start.6) | collective-permute-done | bytes 32800 | tf_op jit(solution)/shard_map/ppermute | solution.py:185
  35.9 0.6 %collective-permute-start.8 = (bf16[128,128]{1,0:T(8,128)(2,1)S(1)}, bf16[128,128]{1,0:T(8,128)(2,1)S(1)}, u32[]{:S(2)}, u32[]{:S(2)}) collective-permute-start(bf16[128,128]{1,0:T(8,128)(2,1)S(1)} %shard_map.71), channel_id=1, source_target_pairs={{0,8},{4,0},{8,12},{12,4},{1,9},{5,1},{9,13},{13,5},{2,10},{6,2},{... | collective-permute-start | bytes 98312 | tf_op jit(solution)/shard_map/ppermute | solution.py:270
  36.5 3.6 %collective-permute-done.1.documents_ref = bf16[128,2048]{1,0:T(8,128)(2,1)S(1)} collective-permute-done((bf16[128,2048]{1,0:T(8,128)(2,1)S(1)}, bf16[128,2048]{1,0:T(8,128)(2,1)S(1)}, u32[]{:S(2)}, u32[]{:S(2)}) %collective-permute-start.1) | collective-permute-done | bytes 524320 | tf_op jit(solution)/shard_map/ppermute | solution.py:277
  40.1 0.4 shard_map.73
  40.5 0.1 collective-permute-start.9
  40.6 0.2 collective-permute-done.7.first_ref
  40.8 0.0 collective-permute-done.8.second_ref
  40.8 0.4 shard_map.72.refs_0_
  41.3 0.7 %collective-permute-done.9.refs_1_ = f32[256,128]{1,0:T(8,128)S(1)} collective-permute-done((f32[256,128]{1,0:T(8,128)S(1)}, f32[256,128]{1,0:T(8,128)S(1)}, u32[]{:S(2)}, u32[]{:S(2)}) %collective-permute-start.9) | collective-permute-done | bytes 131104 | tf_op jit(solution)/shard_map/ppermute | solution.py:185
  42.0 2.6 %collective-permute-start.10 = (bf16[256,128]{1,0:T(8,128)(2,1)S(1)}, bf16[256,128]{1,0:T(8,128)(2,1)S(1)}, u32[]{:S(2)}, u32[]{:S(2)}) collective-permute-start(bf16[256,128]{1,0:T(8,128)(2,1)S(1)} %shard_map.74), channel_id=1, source_target_pairs={{0,12},{1,15},{2,14},{3,13},{4,8},{5,11},{6,10},{7,9},{8,4},{9,7},... | collective-permute-start | bytes 196616 | tf_op jit(solution)/shard_map/ppermute | solution.py:295
  44.6 4.1 %collective-permute-done.10.mine_ref = bf16[256,128]{1,0:T(8,128)(2,1)S(1)} collective-permute-done((bf16[256,128]{1,0:T(8,128)(2,1)S(1)}, bf16[256,128]{1,0:T(8,128)(2,1)S(1)}, u32[]{:S(2)}, u32[]{:S(2)}) %collective-permute-start.10) | collective-permute-done | bytes 65568 | tf_op jit(solution)/shard_map/ppermute | solution.py:295
  48.7 0.0 collective-permute-start.11
  48.7 0.7 %shard_map.75.scores_hbm = f32[4,128,128]{2,1,0:T(8,128)} custom-call(f32[128,128]{1,0:T(8,128)S(1)} %get-tuple-element.48.own_ref, bf16[128,128]{1,0:T(8,128)(2,1)S(1)} %collective-permute-done.7.first_ref, bf16[128,128]{1,0:T(8,128)(2,1)S(1)} %collective-permute-done.8.second_ref), custom_call_target="tpu_custom_call" | custom-call | tf_op jit(solution)/shard_map/pallas_call | solution.py:147
  49.4 0.5 %collective-permute-done.11.arrived_ref = bf16[256,128]{1,0:T(8,128)(2,1)S(1)} collective-permute-done((bf16[256,128]{1,0:T(8,128)(2,1)S(1)}, bf16[256,128]{1,0:T(8,128)(2,1)S(1)}, u32[]{:S(2)}, u32[]{:S(2)}) %collective-permute-start.11) | collective-permute-done | bytes 65568 | tf_op jit(solution)/shard_map/ppermute | solution.py:185
  50.0 0.6 %shard_map.76 = f32[4,128,128]{2,1,0:T(8,128)} custom-call(bf16[256,128]{1,0:T(8,128)(2,1)S(1)} %collective-permute-done.10.mine_ref, bf16[256,128]{1,0:T(8,128)(2,1)S(1)} %collective-permute-done.11.arrived_ref, f32[4,128,128]{2,1,0:T(8,128)} %shard_map.75.scores_hbm), custom_call_target="tpu_custom_call", output_to_operand_aliasing={{}: (2, {})} | custom-call | tf_op jit(solution)/shard_map/pallas_call | solution.py:241
  (5 shorter events, 0.1 us)
Async XLA Ops:
  0.0 10.2 %copy-start.1 = (bf16[128,2048]{1,0:T(8,128)(2,1)S(1)}, bf16[128,2048]{1,0:T(8,128)(2,1)}, u32[]{:S(2)}) copy-start(bf16[128,2048]{1,0:T(8,128)(2,1)} %documents_ref) | copy-start | bytes 1572868
  0.0 10.3 %copy-start.2 = (s32[512]{0:T(512)S(1)}, s32[512]{0:T(512)}, u32[]{:S(2)}) copy-start(s32[512]{0:T(512)} %param.11) | copy-start | bytes 6148
  0.0 16.7 %collective-permute-start = (bf16[128,2048]{1,0:T(8,128)(2,1)}, bf16[128,2048]{1,0:T(8,128)(2,1)S(1)}, u32[]{:S(2)}, u32[]{:S(2)}) collective-permute-start(bf16[128,2048]{1,0:T(8,128)(2,1)} %documents_ref), channel_id=1, source_target_pairs={{0,8},{8,12},{12,4},{4,0},{1,9},{9,13},{13,5},{5,1},{2,10},{10,14}... | collective-permute-start | bytes 1572872 | tf_op jit(solution)/shard_map/ppermute | solution.py:272
  10.2 19.5 %collective-permute-start.2 = (bf16[128,2048]{1,0:T(8,128)(2,1)S(1)}, bf16[128,2048]{1,0:T(8,128)(2,1)S(1)}, u32[]{:S(2)}, u32[]{:S(2)}) collective-permute-start(bf16[128,2048]{1,0:T(8,128)(2,1)S(1)} %copy-done.1), channel_id=1, source_target_pairs={{0,4},{4,12},{12,8},{8,0},{1,5},{5,13},{13,9},{9,1},{2,6},{6,14},{... | collective-permute-start | bytes 1572872 | tf_op jit(solution)/shard_map/ppermute | solution.py:274
  10.4 1.6 %copy-start = (bf16[512,2048]{1,0:T(8,128)(2,1)S(1)}, bf16[512,2048]{1,0:T(8,128)(2,1)}, u32[]{:S(2)}) copy-start(bf16[512,2048]{1,0:T(8,128)(2,1)} %shard_map.64.queries_ref) | copy-start | bytes 6291460
  16.7 23.4 %collective-permute-start.1 = (bf16[128,2048]{1,0:T(8,128)(2,1)S(1)}, bf16[128,2048]{1,0:T(8,128)(2,1)S(1)}, u32[]{:S(2)}, u32[]{:S(2)}) collective-permute-start(bf16[128,2048]{1,0:T(8,128)(2,1)S(1)} %collective-permute-done.documents_ref), channel_id=1, source_target_pairs={{0,8},{8,12},{12,4},{4,0},{1,9},{9,13},{13,5},{5,1},{2,10},{10,14}... | collective-permute-start | bytes 1572872 | tf_op jit(solution)/shard_map/ppermute | solution.py:277
  20.8 1.6 %collective-permute-start.3 = (f32[256,256]{1,0:T(8,128)S(1)}, f32[256,256]{1,0:T(8,128)S(1)}, u32[]{:S(2)}, u32[]{:S(2)}) collective-permute-start(f32[256,256]{1,0:T(8,128)S(1)} %get-tuple-element.36), channel_id=1, source_target_pairs={{0,1},{1,0},{2,3},{3,2},{4,5},{5,4},{6,7},{7,6},{8,9},{9,8},{10,11... | collective-permute-start | bytes 786440 | tf_op jit(solution)/shard_map/ppermute | solution.py:185
  22.4 4.3 %collective-permute-start.4 = (bf16[128,256]{1,0:T(8,128)(2,1)S(1)}, bf16[128,256]{1,0:T(8,128)(2,1)S(1)}, u32[]{:S(2)}, u32[]{:S(2)}) collective-permute-start(bf16[128,256]{1,0:T(8,128)(2,1)S(1)} %get-tuple-element.38), channel_id=1, source_target_pairs={{0,2},{1,3},{2,0},{3,1},{4,6},{5,7},{6,4},{7,5},{8,10},{9,11},{10,... | collective-permute-start | bytes 196616 | tf_op jit(solution)/shard_map/ppermute | solution.py:185
  30.4 1.4 %collective-permute-start.5 = (f32[256,128]{1,0:T(8,128)S(1)}, f32[256,128]{1,0:T(8,128)S(1)}, u32[]{:S(2)}, u32[]{:S(2)}) collective-permute-start(f32[256,128]{1,0:T(8,128)S(1)} %get-tuple-element.43), channel_id=1, source_target_pairs={{0,1},{1,0},{2,3},{3,2},{4,5},{5,4},{6,7},{7,6},{8,9},{9,8},{10,11... | collective-permute-start | bytes 393224 | tf_op jit(solution)/shard_map/ppermute | solution.py:185
  31.9 4.0 %collective-permute-start.6 = (bf16[128,128]{1,0:T(8,128)(2,1)S(1)}, bf16[128,128]{1,0:T(8,128)(2,1)S(1)}, u32[]{:S(2)}, u32[]{:S(2)}) collective-permute-start(bf16[128,128]{1,0:T(8,128)(2,1)S(1)} %get-tuple-element.45), channel_id=1, source_target_pairs={{0,2},{1,3},{2,0},{3,1},{4,6},{5,7},{6,4},{7,5},{8,10},{9,11},{10,... | collective-permute-start | bytes 98312 | tf_op jit(solution)/shard_map/ppermute | solution.py:185
  33.4 7.4 %collective-permute-start.7 = (bf16[128,128]{1,0:T(8,128)(2,1)S(1)}, bf16[128,128]{1,0:T(8,128)(2,1)S(1)}, u32[]{:S(2)}, u32[]{:S(2)}) collective-permute-start(bf16[128,128]{1,0:T(8,128)(2,1)S(1)} %get-tuple-element.40), channel_id=1, source_target_pairs={{0,4},{4,12},{8,0},{12,8},{1,5},{5,13},{9,1},{13,9},{2,6},{6,14},{... | collective-permute-start | bytes 98312 | tf_op jit(solution)/shard_map/ppermute | solution.py:270
  35.9 5.0 %collective-permute-start.8 = (bf16[128,128]{1,0:T(8,128)(2,1)S(1)}, bf16[128,128]{1,0:T(8,128)(2,1)S(1)}, u32[]{:S(2)}, u32[]{:S(2)}) collective-permute-start(bf16[128,128]{1,0:T(8,128)(2,1)S(1)} %shard_map.71), channel_id=1, source_target_pairs={{0,8},{4,0},{8,12},{12,4},{1,9},{5,1},{9,13},{13,5},{2,10},{6,2},{... | collective-permute-start | bytes 98312 | tf_op jit(solution)/shard_map/ppermute | solution.py:270
  40.5 1.4 %collective-permute-start.9 = (f32[256,128]{1,0:T(8,128)S(1)}, f32[256,128]{1,0:T(8,128)S(1)}, u32[]{:S(2)}, u32[]{:S(2)}) collective-permute-start(f32[256,128]{1,0:T(8,128)S(1)} %shard_map.73), channel_id=1, source_target_pairs={{0,1},{1,0},{2,3},{3,2},{4,5},{5,4},{6,7},{7,6},{8,9},{9,8},{10,11... | collective-permute-start | bytes 393224 | tf_op jit(solution)/shard_map/ppermute | solution.py:185
  42.0 6.7 %collective-permute-start.10 = (bf16[256,128]{1,0:T(8,128)(2,1)S(1)}, bf16[256,128]{1,0:T(8,128)(2,1)S(1)}, u32[]{:S(2)}, u32[]{:S(2)}) collective-permute-start(bf16[256,128]{1,0:T(8,128)(2,1)S(1)} %shard_map.74), channel_id=1, source_target_pairs={{0,12},{1,15},{2,14},{3,13},{4,8},{5,11},{6,10},{7,9},{8,4},{9,7},... | collective-permute-start | bytes 196616 | tf_op jit(solution)/shard_map/ppermute | solution.py:295
  48.7 1.3 %collective-permute-start.11 = (bf16[256,128]{1,0:T(8,128)(2,1)S(1)}, bf16[256,128]{1,0:T(8,128)(2,1)S(1)}, u32[]{:S(2)}, u32[]{:S(2)}) collective-permute-start(bf16[256,128]{1,0:T(8,128)(2,1)S(1)} %collective-permute-done.10.mine_ref), channel_id=1, source_target_pairs={{0,1},{1,0},{2,3},{3,2},{4,5},{5,4},{6,7},{7,6},{8,9},{9,8},{10,11... | collective-permute-start | bytes 196616 | tf_op jit(solution)/shard_map/ppermute | solution.py:185

commit v21 on v19

--- a/solution.py
+++ b/solution.py
@@ -73,7 +73,7 @@
     return jnp.where(query_ids == doc_ids, 0.0, tile)
 
 
-def scoring(kernel, out_shape, conditioned, query_ids, documents, extra=(), scratch=()):
+def scoring(kernel, out_shape, conditioned, query_ids, documents, extra=(), scratch=(), weight=1):
     dims = conditioned.shape[1]
     docs = documents.shape[0]
     rows = sum(shape.shape[0] for shape in out_shape)
@@ -86,7 +86,7 @@
         scratch_shapes=scratch,
         compiler_params=pltpu.CompilerParams(vmem_limit_bytes=12 * MIB),
         cost_estimate=pl.CostEstimate(
-            flops=2 * rows * docs * dims, bytes_accessed=2 * dims * (rows + docs), transcendentals=0
+            flops=2 * rows * docs * dims * weight, bytes_accessed=2 * dims * (rows + docs) * weight, transcendentals=0
         ),
     )(conditioned, query_ids, documents, *extra)
 
@@ -272,7 +272,8 @@
     def one_half(block, block_of, kept):
         kernel = functools.partial(half_kernel, block_of, kept)
         out_shape = [jax.ShapeDtypeStruct(half, jnp.float32 if kept else jnp.bfloat16)]
-        return scoring(kernel, out_shape, conditioned, query_ids, block)[0]
+        weight = 5 if kept else 1
+        return scoring(kernel, out_shape, conditioned, query_ids, block, weight=weight)[0]
 
     def back(total, table):
         return lax.ppermute(total, "rows", tuple(enumerate(table)))
@@ -286,12 +287,12 @@
 
     own, first = layer_sum(*halves(one, pick(BLOCK_ONE), own), (jnp.float32, jnp.bfloat16))
     two, first = lax.optimization_barrier((two, first))
-    first = back(first, BLOCK_ONE)
     (second,) = layer_sum(*halves(two, pick(BLOCK_TWO)), (jnp.bfloat16,))
-    second = back(second, BLOCK_TWO)
+    three, *_ = lax.optimization_barrier((three, first, second))
+    first, second = back(first, BLOCK_ONE), back(second, BLOCK_TWO)
+
+    arrived = swap(one_half(three, pick(BLOCK_LAST), False), 1)
     three, first, second = lax.optimization_barrier((three, first, second))
-
-    arrived = swap(one_half(three, pick(BLOCK_LAST), False), 1)
     kept = one_half(three, pick(BLOCK_LAST), True)
     (both,) = small_call(sum_kernel, [jax.ShapeDtypeStruct(half, jnp.bfloat16)], kept, arrived)
     shares = lax.axis_size("layer")

time: 51.7 us -> 50.7 us (0.981)
  waiting for transfers between devices: 24.2 us -> 23.2 us
    ppermute x2, waiting for transfers between devices: 4.65 us -> 0.42 us  [back(): return lax.ppermute(total, 'rows', tuple(enumerate(table)))]
    ppermute x1, waiting for transfers between devices: 0.01 us -> 3.66 us  [along_line(): three = lax.ppermute(one, 'rows', ROUND_ONE)]
  transfers between devices with their start and end apart: 12 -> 12, of which waited for: 10 -> 11; matrix products, arithmetic and copies ran while one was open for 0% -> 0% of each run, Pallas kernels for 19% -> 20%
where the time goes in v21:
time: 50.7 us; the launch traced here: 50.5 us
  waiting for transfers between devices  23.2 us (46%)
  starting transfers between devices  14.6 us (29%)
  Pallas kernels  10.8 us (21%)
  local copies, waits for them, and re-layouts  1.74 us (3%)
    ppermute x6, waiting for transfers between devices, swap(): lax.ppermute(value, 'layer', [(lay, lay ^ distance) for lay in range(coun...  6.67 us
    pallas_call x1, Pallas kernels, prepare(): pl.pallas_call(prepare_kernel, out_shape=jax.ShapeDtypeStruct((rows, dims...  6.15 us
    ppermute x1, waiting for transfers between devices, along_line(): two = lax.ppermute(later, 'rows', ROUND_TWO)  4.39 us
    ppermute x1, waiting for transfers between devices, along_line(): mine = lax.ppermute(both, ('rows', 'layer'), pairs)  4.19 us
    ppermute x1, starting transfers between devices, along_line(): one = lax.ppermute(documents, 'rows', ROUND_ONE)  4.04 us
    ppermute x1, waiting for transfers between devices, along_line(): one = lax.ppermute(documents, 'rows', ROUND_ONE)  3.93 us
    ppermute x1, waiting for transfers between devices, along_line(): three = lax.ppermute(one, 'rows', ROUND_ONE)  3.66 us
    ppermute x6, starting transfers between devices, swap(): lax.ppermute(value, 'layer', [(lay, lay ^ distance) for lay in range(coun...  3.39 us
  transfers between devices with their start and end apart: 12, of which 11 were waited for; matrix products, arithmetic and copies ran while one was open for 0% of the time, Pallas kernels for 20%

profile of v21, /device:TPU:0, one launch (start us, length us, event | category | flops | bytes accessed | tf_op | source)
XLA Modules:
  0.0 50.5 jit_solution(8577148778194864664)
XLA Ops:
  0.0 0.0 copy-start.1
  0.0 0.0 copy-start.2
  0.0 4.0 %collective-permute-start = (bf16[128,2048]{1,0:T(8,128)(2,1)}, bf16[128,2048]{1,0:T(8,128)(2,1)S(1)}, u32[]{:S(2)}, u32[]{:S(2)}) collective-permute-start(bf16[128,2048]{1,0:T(8,128)(2,1)} %documents_ref), channel_id=1, source_target_pairs={{0,8},{8,12},{12,4},{4,0},{1,9},{9,13},{13,5},{5,1},{2,10},{10,14}... | collective-permute-start | bytes 1572872 | tf_op jit(solution)/shard_map/ppermute | solution.py:281
  4.0 6.2 %shard_map.64.queries_ref = bf16[512,2048]{1,0:T(8,128)(2,1)} custom-call(s32[4]{0:T(128)} %offsets.1, bf16[512,2048]{1,0:T(8,128)(2,1)} %queries_hbm.1, bf16[4,512,512]{2,1,0:T(8,128)(2,1)} %bases_hbm.1, f32[4,512]{1,0:T(4,128)} %values_hbm.1), custom_call_target="tpu_custom_call" | custom-call | flops 2147483648 | bytes 6291456 | tf_op jit(solution)/shard_map/pallas_call | solution.py:52
  10.2 0.0 copy-done.1
  10.2 0.1 collective-permute-start.2
  10.3 0.0 copy-done.2
  10.3 0.1 copy.11.ids_ref
  10.4 0.0 copy-start
  10.4 1.6 %copy-done = bf16[512,2048]{1,0:T(8,128)(2,1)S(1)} copy-done((bf16[512,2048]{1,0:T(8,128)(2,1)S(1)}, bf16[512,2048]{1,0:T(8,128)(2,1)}, u32[]{:S(2)}) %copy-start) | copy-done | bytes 2097176
  12.0 0.8 %shard_map.65 = (f32[256,128]{1,0:T(8,128)S(1)}, f32[256,128]{1,0:T(8,128)S(1)}) custom-call(bf16[512,2048]{1,0:T(8,128)(2,1)S(1)} %copy-done, s32[512,1]{1,0:T(8,128)S(1)} %copy.11.ids_ref, bf16[128,2048]{1,0:T(8,128)(2,1)S(1)} %copy-done.1), custom_call_target="tpu_custom_call" | custom-call | flops 268435456 | bytes 2621440 | tf_op jit(solution)/shard_map/pallas_call | solution.py:81
  12.8 3.9 %collective-permute-done.documents_ref = bf16[128,2048]{1,0:T(8,128)(2,1)S(1)} collective-permute-done((bf16[128,2048]{1,0:T(8,128)(2,1)}, bf16[128,2048]{1,0:T(8,128)(2,1)S(1)}, u32[]{:S(2)}, u32[]{:S(2)}) %collective-permute-start) | collective-permute-done | bytes 524320 | tf_op jit(solution)/shard_map/ppermute | solution.py:281
  16.7 0.8 %shard_map.66 = (f32[256,256]{1,0:T(8,128)S(1)}, f32[256,256]{1,0:T(8,128)S(1)}) custom-call(bf16[512,2048]{1,0:T(8,128)(2,1)S(1)} %copy-done, s32[512,1]{1,0:T(8,128)S(1)} %copy.11.ids_ref, bf16[128,2048]{1,0:T(8,128)(2,1)S(1)} %collective-permute-done.documents_ref, f32[256,128]{1,0:T(8,128)S(1)} %get-tuple-element.33.refs_0_, ...), custom_call_target="tpu_custom_call" | custom-call | flops 268435456 | bytes 2621440 | tf_op jit(solution)/shard_map/pallas_call | solution.py:81
  17.5 0.1 collective-permute-start.3
  17.6 3.3 %collective-permute-start.1 = (bf16[128,2048]{1,0:T(8,128)(2,1)S(1)}, bf16[128,2048]{1,0:T(8,128)(2,1)S(1)}, u32[]{:S(2)}, u32[]{:S(2)}) collective-permute-start(bf16[128,2048]{1,0:T(8,128)(2,1)S(1)} %collective-permute-done.documents_ref), channel_id=1, source_target_pairs={{0,8},{8,12},{12,4},{4,0},{1,9},{9,13},{13,5},{5,1},{2,10},{10,14}... | collective-permute-start | bytes 1572872 | tf_op jit(solution)/shard_map/ppermute | solution.py:286
  20.9 0.0 collective-permute-done.3.arrived_ref
  20.9 1.6 %collective-permute-start.4 = (bf16[128,256]{1,0:T(8,128)(2,1)S(1)}, bf16[128,256]{1,0:T(8,128)(2,1)S(1)}, u32[]{:S(2)}, u32[]{:S(2)}) collective-permute-start(bf16[128,256]{1,0:T(8,128)(2,1)S(1)} %get-tuple-element.38), channel_id=1, source_target_pairs={{0,2},{1,3},{2,0},{3,1},{4,6},{5,7},{6,4},{7,5},{8,10},{9,11},{10,... | collective-permute-start | bytes 196616 | tf_op jit(solution)/shard_map/ppermute | solution.py:186
  22.5 2.8 %collective-permute-done.4.arrived_ref = bf16[128,256]{1,0:T(8,128)(2,1)S(1)} collective-permute-done((bf16[128,256]{1,0:T(8,128)(2,1)S(1)}, bf16[128,256]{1,0:T(8,128)(2,1)S(1)}, u32[]{:S(2)}, u32[]{:S(2)}) %collective-permute-start.4) | collective-permute-done | bytes 65568 | tf_op jit(solution)/shard_map/ppermute | solution.py:186
  25.3 4.4 %collective-permute-done.2.documents_ref = bf16[128,2048]{1,0:T(8,128)(2,1)S(1)} collective-permute-done((bf16[128,2048]{1,0:T(8,128)(2,1)S(1)}, bf16[128,2048]{1,0:T(8,128)(2,1)S(1)}, u32[]{:S(2)}, u32[]{:S(2)}) %collective-permute-start.2) | collective-permute-done | bytes 524320 | tf_op jit(solution)/shard_map/ppermute | solution.py:283
  29.7 0.8 %shard_map.69 = (f32[256,128]{1,0:T(8,128)S(1)}, f32[256,128]{1,0:T(8,128)S(1)}) custom-call(bf16[512,2048]{1,0:T(8,128)(2,1)S(1)} %copy-done, s32[512,1]{1,0:T(8,128)S(1)} %copy.11.ids_ref, bf16[128,2048]{1,0:T(8,128)(2,1)S(1)} %collective-permute-done.2.documents_ref), custom_call_target="tpu_custom_call" | custom-call | flops 268435456 | bytes 2621440 | tf_op jit(solution)/shard_map/pallas_call | solution.py:81
  30.4 0.1 collective-permute-start.5
  30.5 1.3 %collective-permute-done.5.arrived_ref = f32[256,128]{1,0:T(8,128)S(1)} collective-permute-done((f32[256,128]{1,0:T(8,128)S(1)}, f32[256,128]{1,0:T(8,128)S(1)}, u32[]{:S(2)}, u32[]{:S(2)}) %collective-permute-start.5) | collective-permute-done | bytes 131104 | tf_op jit(solution)/shard_map/ppermute | solution.py:186
  31.9 1.6 %collective-permute-start.6 = (bf16[128,128]{1,0:T(8,128)(2,1)S(1)}, bf16[128,128]{1,0:T(8,128)(2,1)S(1)}, u32[]{:S(2)}, u32[]{:S(2)}) collective-permute-start(bf16[128,128]{1,0:T(8,128)(2,1)S(1)} %get-tuple-element.45), channel_id=1, source_target_pairs={{0,2},{1,3},{2,0},{3,1},{4,6},{5,7},{6,4},{7,5},{8,10},{9,11},{10,... | collective-permute-start | bytes 98312 | tf_op jit(solution)/shard_map/ppermute | solution.py:186
  33.4 0.7 %collective-permute-start.7 = (bf16[128,128]{1,0:T(8,128)(2,1)S(1)}, bf16[128,128]{1,0:T(8,128)(2,1)S(1)}, u32[]{:S(2)}, u32[]{:S(2)}) collective-permute-start(bf16[128,128]{1,0:T(8,128)(2,1)S(1)} %get-tuple-element.40), channel_id=1, source_target_pairs={{0,4},{4,12},{8,0},{12,8},{1,5},{5,13},{9,1},{13,9},{2,6},{6,14},{... | collective-permute-start | bytes 98312 | tf_op jit(solution)/shard_map/ppermute | solution.py:279
  34.1 1.7 %collective-permute-done.6.arrived_ref = bf16[128,128]{1,0:T(8,128)(2,1)S(1)} collective-permute-done((bf16[128,128]{1,0:T(8,128)(2,1)S(1)}, bf16[128,128]{1,0:T(8,128)(2,1)S(1)}, u32[]{:S(2)}, u32[]{:S(2)}) %collective-permute-start.6) | collective-permute-done | bytes 32800 | tf_op jit(solution)/shard_map/ppermute | solution.py:186
  35.9 0.6 %collective-permute-start.8 = (bf16[128,128]{1,0:T(8,128)(2,1)S(1)}, bf16[128,128]{1,0:T(8,128)(2,1)S(1)}, u32[]{:S(2)}, u32[]{:S(2)}) collective-permute-start(bf16[128,128]{1,0:T(8,128)(2,1)S(1)} %shard_map.71), channel_id=1, source_target_pairs={{0,8},{4,0},{8,12},{12,4},{1,9},{5,1},{9,13},{13,5},{2,10},{6,2},{... | collective-permute-start | bytes 98312 | tf_op jit(solution)/shard_map/ppermute | solution.py:279
  36.5 3.7 %collective-permute-done.1.documents_ref = bf16[128,2048]{1,0:T(8,128)(2,1)S(1)} collective-permute-done((bf16[128,2048]{1,0:T(8,128)(2,1)S(1)}, bf16[128,2048]{1,0:T(8,128)(2,1)S(1)}, u32[]{:S(2)}, u32[]{:S(2)}) %collective-permute-start.1) | collective-permute-done | bytes 524320 | tf_op jit(solution)/shard_map/ppermute | solution.py:286
  40.1 0.4 shard_map.73
  40.6 0.1 collective-permute-start.9
  40.7 0.2 collective-permute-done.7.first_ref
  40.9 0.2 collective-permute-done.8.second_ref
  41.1 0.4 shard_map.72.refs_0_
  41.6 0.3 collective-permute-done.9.refs_1_
  41.9 2.5 %collective-permute-start.10 = (bf16[256,128]{1,0:T(8,128)(2,1)S(1)}, bf16[256,128]{1,0:T(8,128)(2,1)S(1)}, u32[]{:S(2)}, u32[]{:S(2)}) collective-permute-start(bf16[256,128]{1,0:T(8,128)(2,1)S(1)} %shard_map.74), channel_id=1, source_target_pairs={{0,12},{1,15},{2,14},{3,13},{4,8},{5,11},{6,10},{7,9},{8,4},{9,7},... | collective-permute-start | bytes 196616 | tf_op jit(solution)/shard_map/ppermute | solution.py:304
  44.4 4.2 %collective-permute-done.10.mine_ref = bf16[256,128]{1,0:T(8,128)(2,1)S(1)} collective-permute-done((bf16[256,128]{1,0:T(8,128)(2,1)S(1)}, bf16[256,128]{1,0:T(8,128)(2,1)S(1)}, u32[]{:S(2)}, u32[]{:S(2)}) %collective-permute-start.10) | collective-permute-done | bytes 65568 | tf_op jit(solution)/shard_map/ppermute | solution.py:304
  48.6 0.0 collective-permute-start.11
  48.6 0.7 %shard_map.76.scores_hbm = f32[4,128,128]{2,1,0:T(8,128)} custom-call(f32[128,128]{1,0:T(8,128)S(1)} %get-tuple-element.48.own_ref, bf16[128,128]{1,0:T(8,128)(2,1)S(1)} %collective-permute-done.7.first_ref, bf16[128,128]{1,0:T(8,128)(2,1)S(1)} %collective-permute-done.8.second_ref), custom_call_target="tpu_custom_call" | custom-call | tf_op jit(solution)/shard_map/pallas_call | solution.py:148
  49.3 0.5 collective-permute-done.11.arrived_ref
  49.8 0.6 %shard_map.77 = f32[4,128,128]{2,1,0:T(8,128)} custom-call(bf16[256,128]{1,0:T(8,128)(2,1)S(1)} %collective-permute-done.10.mine_ref, bf16[128,128]{1,0:T(8,128)(2,1)S(1)} %collective-permute-done.11.arrived_ref, f32[4,128,128]{2,1,0:T(8,128)} %shard_map.76.scores_hbm), custom_call_target="tpu_custom_call", output_to_operand_aliasing={{}: (2, {})} | custom-call | tf_op jit(solution)/shard_map/pallas_call | solution.py:250
  (6 shorter events, 0.1 us)
Async XLA Ops:
  0.0 10.2 %copy-start.1 = (bf16[128,2048]{1,0:T(8,128)(2,1)S(1)}, bf16[128,2048]{1,0:T(8,128)(2,1)}, u32[]{:S(2)}) copy-start(bf16[128,2048]{1,0:T(8,128)(2,1)} %documents_ref) | copy-start | bytes 1572868
  0.0 10.3 %copy-start.2 = (s32[512]{0:T(512)S(1)}, s32[512]{0:T(512)}, u32[]{:S(2)}) copy-start(s32[512]{0:T(512)} %param.11) | copy-start | bytes 6148
  0.0 16.7 %collective-permute-start = (bf16[128,2048]{1,0:T(8,128)(2,1)}, bf16[128,2048]{1,0:T(8,128)(2,1)S(1)}, u32[]{:S(2)}, u32[]{:S(2)}) collective-permute-start(bf16[128,2048]{1,0:T(8,128)(2,1)} %documents_ref), channel_id=1, source_target_pairs={{0,8},{8,12},{12,4},{4,0},{1,9},{9,13},{13,5},{5,1},{2,10},{10,14}... | collective-permute-start | bytes 1572872 | tf_op jit(solution)/shard_map/ppermute | solution.py:281
  10.2 19.5 %collective-permute-start.2 = (bf16[128,2048]{1,0:T(8,128)(2,1)S(1)}, bf16[128,2048]{1,0:T(8,128)(2,1)S(1)}, u32[]{:S(2)}, u32[]{:S(2)}) collective-permute-start(bf16[128,2048]{1,0:T(8,128)(2,1)S(1)} %copy-done.1), channel_id=1, source_target_pairs={{0,4},{4,12},{12,8},{8,0},{1,5},{5,13},{13,9},{9,1},{2,6},{6,14},{... | collective-permute-start | bytes 1572872 | tf_op jit(solution)/shard_map/ppermute | solution.py:283
  10.4 1.6 %copy-start = (bf16[512,2048]{1,0:T(8,128)(2,1)S(1)}, bf16[512,2048]{1,0:T(8,128)(2,1)}, u32[]{:S(2)}) copy-start(bf16[512,2048]{1,0:T(8,128)(2,1)} %shard_map.64.queries_ref) | copy-start | bytes 6291460
  17.5 3.4 %collective-permute-start.3 = (f32[256,256]{1,0:T(8,128)S(1)}, f32[256,256]{1,0:T(8,128)S(1)}, u32[]{:S(2)}, u32[]{:S(2)}) collective-permute-start(f32[256,256]{1,0:T(8,128)S(1)} %get-tuple-element.36), channel_id=1, source_target_pairs={{0,1},{1,0},{2,3},{3,2},{4,5},{5,4},{6,7},{7,6},{8,9},{9,8},{10,11... | collective-permute-start | bytes 786440 | tf_op jit(solution)/shard_map/ppermute | solution.py:186
  17.6 22.6 %collective-permute-start.1 = (bf16[128,2048]{1,0:T(8,128)(2,1)S(1)}, bf16[128,2048]{1,0:T(8,128)(2,1)S(1)}, u32[]{:S(2)}, u32[]{:S(2)}) collective-permute-start(bf16[128,2048]{1,0:T(8,128)(2,1)S(1)} %collective-permute-done.documents_ref), channel_id=1, source_target_pairs={{0,8},{8,12},{12,4},{4,0},{1,9},{9,13},{13,5},{5,1},{2,10},{10,14}... | collective-permute-start | bytes 1572872 | tf_op jit(solution)/shard_map/ppermute | solution.py:286
  20.9 4.3 %collective-permute-start.4 = (bf16[128,256]{1,0:T(8,128)(2,1)S(1)}, bf16[128,256]{1,0:T(8,128)(2,1)S(1)}, u32[]{:S(2)}, u32[]{:S(2)}) collective-permute-start(bf16[128,256]{1,0:T(8,128)(2,1)S(1)} %get-tuple-element.38), channel_id=1, source_target_pairs={{0,2},{1,3},{2,0},{3,1},{4,6},{5,7},{6,4},{7,5},{8,10},{9,11},{10,... | collective-permute-start | bytes 196616 | tf_op jit(solution)/shard_map/ppermute | solution.py:186
  30.4 1.4 %collective-permute-start.5 = (f32[256,128]{1,0:T(8,128)S(1)}, f32[256,128]{1,0:T(8,128)S(1)}, u32[]{:S(2)}, u32[]{:S(2)}) collective-permute-start(f32[256,128]{1,0:T(8,128)S(1)} %get-tuple-element.43), channel_id=1, source_target_pairs={{0,1},{1,0},{2,3},{3,2},{4,5},{5,4},{6,7},{7,6},{8,9},{9,8},{10,11... | collective-permute-start | bytes 393224 | tf_op jit(solution)/shard_map/ppermute | solution.py:186
  31.9 4.0 %collective-permute-start.6 = (bf16[128,128]{1,0:T(8,128)(2,1)S(1)}, bf16[128,128]{1,0:T(8,128)(2,1)S(1)}, u32[]{:S(2)}, u32[]{:S(2)}) collective-permute-start(bf16[128,128]{1,0:T(8,128)(2,1)S(1)} %get-tuple-element.45), channel_id=1, source_target_pairs={{0,2},{1,3},{2,0},{3,1},{4,6},{5,7},{6,4},{7,5},{8,10},{9,11},{10,... | collective-permute-start | bytes 98312 | tf_op jit(solution)/shard_map/ppermute | solution.py:186
  33.4 7.5 %collective-permute-start.7 = (bf16[128,128]{1,0:T(8,128)(2,1)S(1)}, bf16[128,128]{1,0:T(8,128)(2,1)S(1)}, u32[]{:S(2)}, u32[]{:S(2)}) collective-permute-start(bf16[128,128]{1,0:T(8,128)(2,1)S(1)} %get-tuple-element.40), channel_id=1, source_target_pairs={{0,4},{4,12},{8,0},{12,8},{1,5},{5,13},{9,1},{13,9},{2,6},{6,14},{... | collective-permute-start | bytes 98312 | tf_op jit(solution)/shard_map/ppermute | solution.py:279
  35.9 5.3 %collective-permute-start.8 = (bf16[128,128]{1,0:T(8,128)(2,1)S(1)}, bf16[128,128]{1,0:T(8,128)(2,1)S(1)}, u32[]{:S(2)}, u32[]{:S(2)}) collective-permute-start(bf16[128,128]{1,0:T(8,128)(2,1)S(1)} %shard_map.71), channel_id=1, source_target_pairs={{0,8},{4,0},{8,12},{12,4},{1,9},{5,1},{9,13},{13,5},{2,10},{6,2},{... | collective-permute-start | bytes 98312 | tf_op jit(solution)/shard_map/ppermute | solution.py:279
  40.6 1.3 %collective-permute-start.9 = (bf16[256,128]{1,0:T(8,128)(2,1)S(1)}, bf16[256,128]{1,0:T(8,128)(2,1)S(1)}, u32[]{:S(2)}, u32[]{:S(2)}) collective-permute-start(bf16[256,128]{1,0:T(8,128)(2,1)S(1)} %shard_map.73), channel_id=1, source_target_pairs={{0,1},{1,0},{2,3},{3,2},{4,5},{5,4},{6,7},{7,6},{8,9},{9,8},{10,11... | collective-permute-start | bytes 196616 | tf_op jit(solution)/shard_map/ppermute | solution.py:186
  41.9 6.7 %collective-permute-start.10 = (bf16[256,128]{1,0:T(8,128)(2,1)S(1)}, bf16[256,128]{1,0:T(8,128)(2,1)S(1)}, u32[]{:S(2)}, u32[]{:S(2)}) collective-permute-start(bf16[256,128]{1,0:T(8,128)(2,1)S(1)} %shard_map.74), channel_id=1, source_target_pairs={{0,12},{1,15},{2,14},{3,13},{4,8},{5,11},{6,10},{7,9},{8,4},{9,7},... | collective-permute-start | bytes 196616 | tf_op jit(solution)/shard_map/ppermute | solution.py:304
  48.6 1.2 %collective-permute-start.11 = (bf16[128,128]{1,0:T(8,128)(2,1)S(1)}, bf16[128,128]{1,0:T(8,128)(2,1)S(1)}, u32[]{:S(2)}, u32[]{:S(2)}) collective-permute-start(bf16[128,128]{1,0:T(8,128)(2,1)S(1)} %shard_map.75), channel_id=1, source_target_pairs={{0,1},{1,0},{2,3},{3,2},{4,5},{5,4},{6,7},{7,6},{8,9},{9,8},{10,11... | collective-permute-start | bytes 98312 | tf_op jit(solution)/shard_map/ppermute | solution.py:186

commit v22 on v21

--- a/solution.py
+++ b/solution.py
@@ -128,7 +128,9 @@
     rows = out_ref.shape[0]
     chip = target_chip() if kept else 1 - target_chip()
     spot = pl.ds(pl.multiple_of(chip * rows, rows), rows)
-    tile = masked_tile(queries_ref[spot, :], documents_ref[...], ids_ref[spot, :], block_of(row_index()))
+    tile = lax.dot_general(documents_ref[...], queries_ref[spot, :], NT, preferred_element_type=jnp.float32).T
+    doc_ids = block_of(row_index()) * tile.shape[1] + lax.broadcasted_iota(jnp.int32, tile.shape, 1)
+    tile = jnp.where(ids_ref[spot, :] == doc_ids, 0.0, tile)
     out_ref[...] = tile.astype(out_ref.dtype)
 
 

time: 50.7 us -> 50.8 us (level)
  transfers between devices with their start and end apart: 12 -> 12, of which waited for: 11 -> 11; matrix products, arithmetic and copies ran while one was open for 0% -> 0% of each run, Pallas kernels for 20% -> 21%
where the time goes in v22:
time: 50.8 us; the launch traced here: 50.6 us
  waiting for transfers between devices  23.1 us (45%)
  starting transfers between devices  14.6 us (29%)
  Pallas kernels  11 us (22%)
  local copies, waits for them, and re-layouts  1.74 us (3%)
    ppermute x6, waiting for transfers between devices, swap(): lax.ppermute(value, 'layer', [(lay, lay ^ distance) for lay in range(coun...  6.65 us
    pallas_call x1, Pallas kernels, prepare(): pl.pallas_call(prepare_kernel, out_shape=jax.ShapeDtypeStruct((rows, dims...  6.15 us
    ppermute x1, waiting for transfers between devices, along_line(): two = lax.ppermute(later, 'rows', ROUND_TWO)  4.39 us
    ppermute x1, waiting for transfers between devices, along_line(): mine = lax.ppermute(both, ('rows', 'layer'), pairs)  4.18 us
    ppermute x1, starting transfers between devices, along_line(): one = lax.ppermute(documents, 'rows', ROUND_ONE)  4.04 us
    ppermute x1, waiting for transfers between devices, along_line(): one = lax.ppermute(documents, 'rows', ROUND_ONE)  3.93 us
    ppermute x1, waiting for transfers between devices, along_line(): three = lax.ppermute(one, 'rows', ROUND_ONE)  3.66 us
    pallas_call x5, Pallas kernels, scoring(): pl.pallas_call(kernel, out_shape=out_shape, in_specs=[vmem] * (3 + len(ex...  3.44 us
  transfers between devices with their start and end apart: 12, of which 11 were waited for; matrix products, arithmetic and copies ran while one was open for 0% of the time, Pallas kernels for 21%

profile of v22, /device:TPU:0, one launch (start us, length us, event | category | flops | bytes accessed | tf_op | source)
XLA Modules:
  0.0 50.6 jit_solution(2267597049493118788)
XLA Ops:
  0.0 0.0 copy-start.1
  0.0 0.0 copy-start.2
  0.0 4.0 %collective-permute-start = (bf16[128,2048]{1,0:T(8,128)(2,1)}, bf16[128,2048]{1,0:T(8,128)(2,1)S(1)}, u32[]{:S(2)}, u32[]{:S(2)}) collective-permute-start(bf16[128,2048]{1,0:T(8,128)(2,1)} %documents_ref), channel_id=1, source_target_pairs={{0,8},{8,12},{12,4},{4,0},{1,9},{9,13},{13,5},{5,1},{2,10},{10,14}... | collective-permute-start | bytes 1572872 | tf_op jit(solution)/shard_map/ppermute | solution.py:283
  4.0 6.2 %shard_map.64.queries_ref = bf16[512,2048]{1,0:T(8,128)(2,1)} custom-call(s32[4]{0:T(128)} %offsets.1, bf16[512,2048]{1,0:T(8,128)(2,1)} %queries_hbm.1, bf16[4,512,512]{2,1,0:T(8,128)(2,1)} %bases_hbm.1, f32[4,512]{1,0:T(4,128)} %values_hbm.1), custom_call_target="tpu_custom_call" | custom-call | flops 2147483648 | bytes 6291456 | tf_op jit(solution)/shard_map/pallas_call | solution.py:52
  10.2 0.0 copy-done.1
  10.2 0.1 collective-permute-start.2
  10.3 0.0 copy-done.2
  10.3 0.1 copy.11.ids_ref
  10.4 0.0 copy-start
  10.4 1.6 %copy-done = bf16[512,2048]{1,0:T(8,128)(2,1)S(1)} copy-done((bf16[512,2048]{1,0:T(8,128)(2,1)S(1)}, bf16[512,2048]{1,0:T(8,128)(2,1)}, u32[]{:S(2)}) %copy-start) | copy-done | bytes 2097176
  12.0 0.8 %shard_map.65 = (f32[256,128]{1,0:T(8,128)S(1)}, f32[256,128]{1,0:T(8,128)S(1)}) custom-call(bf16[512,2048]{1,0:T(8,128)(2,1)S(1)} %copy-done, s32[512,1]{1,0:T(8,128)S(1)} %copy.11.ids_ref, bf16[128,2048]{1,0:T(8,128)(2,1)S(1)} %copy-done.1), custom_call_target="tpu_custom_call" | custom-call | flops 268435456 | bytes 2621440 | tf_op jit(solution)/shard_map/pallas_call | solution.py:81
  12.8 3.9 %collective-permute-done.documents_ref = bf16[128,2048]{1,0:T(8,128)(2,1)S(1)} collective-permute-done((bf16[128,2048]{1,0:T(8,128)(2,1)}, bf16[128,2048]{1,0:T(8,128)(2,1)S(1)}, u32[]{:S(2)}, u32[]{:S(2)}) %collective-permute-start) | collective-permute-done | bytes 524320 | tf_op jit(solution)/shard_map/ppermute | solution.py:283
  16.7 0.8 %shard_map.66 = (f32[256,256]{1,0:T(8,128)S(1)}, f32[256,256]{1,0:T(8,128)S(1)}) custom-call(bf16[512,2048]{1,0:T(8,128)(2,1)S(1)} %copy-done, s32[512,1]{1,0:T(8,128)S(1)} %copy.11.ids_ref, bf16[128,2048]{1,0:T(8,128)(2,1)S(1)} %collective-permute-done.documents_ref, f32[256,128]{1,0:T(8,128)S(1)} %get-tuple-element.33.refs_0_, ...), custom_call_target="tpu_custom_call" | custom-call | flops 268435456 | bytes 2621440 | tf_op jit(solution)/shard_map/pallas_call | solution.py:81
  17.5 0.1 collective-permute-start.3
  17.6 3.3 %collective-permute-start.1 = (bf16[128,2048]{1,0:T(8,128)(2,1)S(1)}, bf16[128,2048]{1,0:T(8,128)(2,1)S(1)}, u32[]{:S(2)}, u32[]{:S(2)}) collective-permute-start(bf16[128,2048]{1,0:T(8,128)(2,1)S(1)} %collective-permute-done.documents_ref), channel_id=1, source_target_pairs={{0,8},{8,12},{12,4},{4,0},{1,9},{9,13},{13,5},{5,1},{2,10},{10,14}... | collective-permute-start | bytes 1572872 | tf_op jit(solution)/shard_map/ppermute | solution.py:288
  20.9 0.0 collective-permute-done.3.arrived_ref
  20.9 1.6 %collective-permute-start.4 = (bf16[128,256]{1,0:T(8,128)(2,1)S(1)}, bf16[128,256]{1,0:T(8,128)(2,1)S(1)}, u32[]{:S(2)}, u32[]{:S(2)}) collective-permute-start(bf16[128,256]{1,0:T(8,128)(2,1)S(1)} %get-tuple-element.38), channel_id=1, source_target_pairs={{0,2},{1,3},{2,0},{3,1},{4,6},{5,7},{6,4},{7,5},{8,10},{9,11},{10,... | collective-permute-start | bytes 196616 | tf_op jit(solution)/shard_map/ppermute | solution.py:188
  22.5 2.8 %collective-permute-done.4.arrived_ref = bf16[128,256]{1,0:T(8,128)(2,1)S(1)} collective-permute-done((bf16[128,256]{1,0:T(8,128)(2,1)S(1)}, bf16[128,256]{1,0:T(8,128)(2,1)S(1)}, u32[]{:S(2)}, u32[]{:S(2)}) %collective-permute-start.4) | collective-permute-done | bytes 65568 | tf_op jit(solution)/shard_map/ppermute | solution.py:188
  25.3 4.4 %collective-permute-done.2.documents_ref = bf16[128,2048]{1,0:T(8,128)(2,1)S(1)} collective-permute-done((bf16[128,2048]{1,0:T(8,128)(2,1)S(1)}, bf16[128,2048]{1,0:T(8,128)(2,1)S(1)}, u32[]{:S(2)}, u32[]{:S(2)}) %collective-permute-start.2) | collective-permute-done | bytes 524320 | tf_op jit(solution)/shard_map/ppermute | solution.py:285
  29.7 0.8 %shard_map.69 = (f32[256,128]{1,0:T(8,128)S(1)}, f32[256,128]{1,0:T(8,128)S(1)}) custom-call(bf16[512,2048]{1,0:T(8,128)(2,1)S(1)} %copy-done, s32[512,1]{1,0:T(8,128)S(1)} %copy.11.ids_ref, bf16[128,2048]{1,0:T(8,128)(2,1)S(1)} %collective-permute-done.2.documents_ref), custom_call_target="tpu_custom_call" | custom-call | flops 268435456 | bytes 2621440 | tf_op jit(solution)/shard_map/pallas_call | solution.py:81
  30.4 0.1 collective-permute-start.5
  30.5 1.3 %collective-permute-done.5.arrived_ref = f32[256,128]{1,0:T(8,128)S(1)} collective-permute-done((f32[256,128]{1,0:T(8,128)S(1)}, f32[256,128]{1,0:T(8,128)S(1)}, u32[]{:S(2)}, u32[]{:S(2)}) %collective-permute-start.5) | collective-permute-done | bytes 131104 | tf_op jit(solution)/shard_map/ppermute | solution.py:188
  31.9 1.6 %collective-permute-start.6 = (bf16[128,128]{1,0:T(8,128)(2,1)S(1)}, bf16[128,128]{1,0:T(8,128)(2,1)S(1)}, u32[]{:S(2)}, u32[]{:S(2)}) collective-permute-start(bf16[128,128]{1,0:T(8,128)(2,1)S(1)} %get-tuple-element.45), channel_id=1, source_target_pairs={{0,2},{1,3},{2,0},{3,1},{4,6},{5,7},{6,4},{7,5},{8,10},{9,11},{10,... | collective-permute-start | bytes 98312 | tf_op jit(solution)/shard_map/ppermute | solution.py:188
  33.4 0.7 %collective-permute-start.7 = (bf16[128,128]{1,0:T(8,128)(2,1)S(1)}, bf16[128,128]{1,0:T(8,128)(2,1)S(1)}, u32[]{:S(2)}, u32[]{:S(2)}) collective-permute-start(bf16[128,128]{1,0:T(8,128)(2,1)S(1)} %get-tuple-element.40), channel_id=1, source_target_pairs={{0,4},{4,12},{8,0},{12,8},{1,5},{5,13},{9,1},{13,9},{2,6},{6,14},{... | collective-permute-start | bytes 98312 | tf_op jit(solution)/shard_map/ppermute | solution.py:281
  34.1 1.7 %collective-permute-done.6.arrived_ref = bf16[128,128]{1,0:T(8,128)(2,1)S(1)} collective-permute-done((bf16[128,128]{1,0:T(8,128)(2,1)S(1)}, bf16[128,128]{1,0:T(8,128)(2,1)S(1)}, u32[]{:S(2)}, u32[]{:S(2)}) %collective-permute-start.6) | collective-permute-done | bytes 32800 | tf_op jit(solution)/shard_map/ppermute | solution.py:188
  35.9 0.6 %collective-permute-start.8 = (bf16[128,128]{1,0:T(8,128)(2,1)S(1)}, bf16[128,128]{1,0:T(8,128)(2,1)S(1)}, u32[]{:S(2)}, u32[]{:S(2)}) collective-permute-start(bf16[128,128]{1,0:T(8,128)(2,1)S(1)} %shard_map.71), channel_id=1, source_target_pairs={{0,8},{4,0},{8,12},{12,4},{1,9},{5,1},{9,13},{13,5},{2,10},{6,2},{... | collective-permute-start | bytes 98312 | tf_op jit(solution)/shard_map/ppermute | solution.py:281
  36.5 3.7 %collective-permute-done.1.documents_ref = bf16[128,2048]{1,0:T(8,128)(2,1)S(1)} collective-permute-done((bf16[128,2048]{1,0:T(8,128)(2,1)S(1)}, bf16[128,2048]{1,0:T(8,128)(2,1)S(1)}, u32[]{:S(2)}, u32[]{:S(2)}) %collective-permute-start.1) | collective-permute-done | bytes 524320 | tf_op jit(solution)/shard_map/ppermute | solution.py:288
  40.1 0.6 %shard_map.73 = bf16[256,128]{1,0:T(8,128)(2,1)S(1)} custom-call(bf16[512,2048]{1,0:T(8,128)(2,1)S(1)} %copy-done, s32[512,1]{1,0:T(8,128)S(1)} %copy.11.ids_ref, bf16[128,2048]{1,0:T(8,128)(2,1)S(1)} %collective-permute-done.1.documents_ref), custom_call_target="tpu_custom_call" | custom-call | flops 134217728 | bytes 1572864 | tf_op jit(solution)/shard_map/pallas_call | solution.py:81
  40.7 0.1 collective-permute-start.9
  40.8 0.1 collective-permute-done.7.first_ref
  40.9 0.2 collective-permute-done.8.second_ref
  41.1 0.6 %shard_map.72.refs_0_ = f32[256,128]{1,0:T(8,128)S(1)} custom-call(bf16[512,2048]{1,0:T(8,128)(2,1)S(1)} %copy-done, s32[512,1]{1,0:T(8,128)S(1)} %copy.11.ids_ref, bf16[128,2048]{1,0:T(8,128)(2,1)S(1)} %collective-permute-done.1.documents_ref), custom_call_target="tpu_custom_call" | custom-call | flops 671088640 | bytes 7864320 | tf_op jit(solution)/shard_map/pallas_call | solution.py:81
  41.7 0.3 collective-permute-done.9.refs_1_
  42.0 2.5 %collective-permute-start.10 = (bf16[256,128]{1,0:T(8,128)(2,1)S(1)}, bf16[256,128]{1,0:T(8,128)(2,1)S(1)}, u32[]{:S(2)}, u32[]{:S(2)}) collective-permute-start(bf16[256,128]{1,0:T(8,128)(2,1)S(1)} %shard_map.74), channel_id=1, source_target_pairs={{0,12},{1,15},{2,14},{3,13},{4,8},{5,11},{6,10},{7,9},{8,4},{9,7},... | collective-permute-start | bytes 196616 | tf_op jit(solution)/shard_map/ppermute | solution.py:306
  44.6 4.2 %collective-permute-done.10.mine_ref = bf16[256,128]{1,0:T(8,128)(2,1)S(1)} collective-permute-done((bf16[256,128]{1,0:T(8,128)(2,1)S(1)}, bf16[256,128]{1,0:T(8,128)(2,1)S(1)}, u32[]{:S(2)}, u32[]{:S(2)}) %collective-permute-start.10) | collective-permute-done | bytes 65568 | tf_op jit(solution)/shard_map/ppermute | solution.py:306
  48.7 0.0 collective-permute-start.11
  48.7 0.7 %shard_map.76.scores_hbm = f32[4,128,128]{2,1,0:T(8,128)} custom-call(f32[128,128]{1,0:T(8,128)S(1)} %get-tuple-element.48.own_ref, bf16[128,128]{1,0:T(8,128)(2,1)S(1)} %collective-permute-done.7.first_ref, bf16[128,128]{1,0:T(8,128)(2,1)S(1)} %collective-permute-done.8.second_ref), custom_call_target="tpu_custom_call" | custom-call | tf_op jit(solution)/shard_map/pallas_call | solution.py:150
  49.5 0.5 collective-permute-done.11.arrived_ref
  49.9 0.6 %shard_map.77 = f32[4,128,128]{2,1,0:T(8,128)} custom-call(bf16[256,128]{1,0:T(8,128)(2,1)S(1)} %collective-permute-done.10.mine_ref, bf16[128,128]{1,0:T(8,128)(2,1)S(1)} %collective-permute-done.11.arrived_ref, f32[4,128,128]{2,1,0:T(8,128)} %shard_map.76.scores_hbm), custom_call_target="tpu_custom_call", output_to_operand_aliasing={{}: (2, {})} | custom-call | tf_op jit(solution)/shard_map/pallas_call | solution.py:252
  (6 shorter events, 0.1 us)
Async XLA Ops:
  0.0 10.2 %copy-start.1 = (bf16[128,2048]{1,0:T(8,128)(2,1)S(1)}, bf16[128,2048]{1,0:T(8,128)(2,1)}, u32[]{:S(2)}) copy-start(bf16[128,2048]{1,0:T(8,128)(2,1)} %documents_ref) | copy-start | bytes 1572868
  0.0 10.3 %copy-start.2 = (s32[512]{0:T(512)S(1)}, s32[512]{0:T(512)}, u32[]{:S(2)}) copy-start(s32[512]{0:T(512)} %param.11) | copy-start | bytes 6148
  0.0 16.7 %collective-permute-start = (bf16[128,2048]{1,0:T(8,128)(2,1)}, bf16[128,2048]{1,0:T(8,128)(2,1)S(1)}, u32[]{:S(2)}, u32[]{:S(2)}) collective-permute-start(bf16[128,2048]{1,0:T(8,128)(2,1)} %documents_ref), channel_id=1, source_target_pairs={{0,8},{8,12},{12,4},{4,0},{1,9},{9,13},{13,5},{5,1},{2,10},{10,14}... | collective-permute-start | bytes 1572872 | tf_op jit(solution)/shard_map/ppermute | solution.py:283
  10.2 19.5 %collective-permute-start.2 = (bf16[128,2048]{1,0:T(8,128)(2,1)S(1)}, bf16[128,2048]{1,0:T(8,128)(2,1)S(1)}, u32[]{:S(2)}, u32[]{:S(2)}) collective-permute-start(bf16[128,2048]{1,0:T(8,128)(2,1)S(1)} %copy-done.1), channel_id=1, source_target_pairs={{0,4},{4,12},{12,8},{8,0},{1,5},{5,13},{13,9},{9,1},{2,6},{6,14},{... | collective-permute-start | bytes 1572872 | tf_op jit(solution)/shard_map/ppermute | solution.py:285
  10.4 1.6 %copy-start = (bf16[512,2048]{1,0:T(8,128)(2,1)S(1)}, bf16[512,2048]{1,0:T(8,128)(2,1)}, u32[]{:S(2)}) copy-start(bf16[512,2048]{1,0:T(8,128)(2,1)} %shard_map.64.queries_ref) | copy-start | bytes 6291460
  17.5 3.4 %collective-permute-start.3 = (f32[256,256]{1,0:T(8,128)S(1)}, f32[256,256]{1,0:T(8,128)S(1)}, u32[]{:S(2)}, u32[]{:S(2)}) collective-permute-start(f32[256,256]{1,0:T(8,128)S(1)} %get-tuple-element.36), channel_id=1, source_target_pairs={{0,1},{1,0},{2,3},{3,2},{4,5},{5,4},{6,7},{7,6},{8,9},{9,8},{10,11... | collective-permute-start | bytes 786440 | tf_op jit(solution)/shard_map/ppermute | solution.py:188
  17.6 22.6 %collective-permute-start.1 = (bf16[128,2048]{1,0:T(8,128)(2,1)S(1)}, bf16[128,2048]{1,0:T(8,128)(2,1)S(1)}, u32[]{:S(2)}, u32[]{:S(2)}) collective-permute-start(bf16[128,2048]{1,0:T(8,128)(2,1)S(1)} %collective-permute-done.documents_ref), channel_id=1, source_target_pairs={{0,8},{8,12},{12,4},{4,0},{1,9},{9,13},{13,5},{5,1},{2,10},{10,14}... | collective-permute-start | bytes 1572872 | tf_op jit(solution)/shard_map/ppermute | solution.py:288
  20.9 4.3 %collective-permute-start.4 = (bf16[128,256]{1,0:T(8,128)(2,1)S(1)}, bf16[128,256]{1,0:T(8,128)(2,1)S(1)}, u32[]{:S(2)}, u32[]{:S(2)}) collective-permute-start(bf16[128,256]{1,0:T(8,128)(2,1)S(1)} %get-tuple-element.38), channel_id=1, source_target_pairs={{0,2},{1,3},{2,0},{3,1},{4,6},{5,7},{6,4},{7,5},{8,10},{9,11},{10,... | collective-permute-start | bytes 196616 | tf_op jit(solution)/shard_map/ppermute | solution.py:188
  30.4 1.4 %collective-permute-start.5 = (f32[256,128]{1,0:T(8,128)S(1)}, f32[256,128]{1,0:T(8,128)S(1)}, u32[]{:S(2)}, u32[]{:S(2)}) collective-permute-start(f32[256,128]{1,0:T(8,128)S(1)} %get-tuple-element.43), channel_id=1, source_target_pairs={{0,1},{1,0},{2,3},{3,2},{4,5},{5,4},{6,7},{7,6},{8,9},{9,8},{10,11... | collective-permute-start | bytes 393224 | tf_op jit(solution)/shard_map/ppermute | solution.py:188
  31.9 4.0 %collective-permute-start.6 = (bf16[128,128]{1,0:T(8,128)(2,1)S(1)}, bf16[128,128]{1,0:T(8,128)(2,1)S(1)}, u32[]{:S(2)}, u32[]{:S(2)}) collective-permute-start(bf16[128,128]{1,0:T(8,128)(2,1)S(1)} %get-tuple-element.45), channel_id=1, source_target_pairs={{0,2},{1,3},{2,0},{3,1},{4,6},{5,7},{6,4},{7,5},{8,10},{9,11},{10,... | collective-permute-start | bytes 98312 | tf_op jit(solution)/shard_map/ppermute | solution.py:188
  33.4 7.5 %collective-permute-start.7 = (bf16[128,128]{1,0:T(8,128)(2,1)S(1)}, bf16[128,128]{1,0:T(8,128)(2,1)S(1)}, u32[]{:S(2)}, u32[]{:S(2)}) collective-permute-start(bf16[128,128]{1,0:T(8,128)(2,1)S(1)} %get-tuple-element.40), channel_id=1, source_target_pairs={{0,4},{4,12},{8,0},{12,8},{1,5},{5,13},{9,1},{13,9},{2,6},{6,14},{... | collective-permute-start | bytes 98312 | tf_op jit(solution)/shard_map/ppermute | solution.py:281
  35.9 5.3 %collective-permute-start.8 = (bf16[128,128]{1,0:T(8,128)(2,1)S(1)}, bf16[128,128]{1,0:T(8,128)(2,1)S(1)}, u32[]{:S(2)}, u32[]{:S(2)}) collective-permute-start(bf16[128,128]{1,0:T(8,128)(2,1)S(1)} %shard_map.71), channel_id=1, source_target_pairs={{0,8},{4,0},{8,12},{12,4},{1,9},{5,1},{9,13},{13,5},{2,10},{6,2},{... | collective-permute-start | bytes 98312 | tf_op jit(solution)/shard_map/ppermute | solution.py:281
  40.7 1.3 %collective-permute-start.9 = (bf16[256,128]{1,0:T(8,128)(2,1)S(1)}, bf16[256,128]{1,0:T(8,128)(2,1)S(1)}, u32[]{:S(2)}, u32[]{:S(2)}) collective-permute-start(bf16[256,128]{1,0:T(8,128)(2,1)S(1)} %shard_map.73), channel_id=1, source_target_pairs={{0,1},{1,0},{2,3},{3,2},{4,5},{5,4},{6,7},{7,6},{8,9},{9,8},{10,11... | collective-permute-start | bytes 196616 | tf_op jit(solution)/shard_map/ppermute | solution.py:188
  42.0 6.7 %collective-permute-start.10 = (bf16[256,128]{1,0:T(8,128)(2,1)S(1)}, bf16[256,128]{1,0:T(8,128)(2,1)S(1)}, u32[]{:S(2)}, u32[]{:S(2)}) collective-permute-start(bf16[256,128]{1,0:T(8,128)(2,1)S(1)} %shard_map.74), channel_id=1, source_target_pairs={{0,12},{1,15},{2,14},{3,13},{4,8},{5,11},{6,10},{7,9},{8,4},{9,7},... | collective-permute-start | bytes 196616 | tf_op jit(solution)/shard_map/ppermute | solution.py:306
  48.7 1.2 %collective-permute-start.11 = (bf16[128,128]{1,0:T(8,128)(2,1)S(1)}, bf16[128,128]{1,0:T(8,128)(2,1)S(1)}, u32[]{:S(2)}, u32[]{:S(2)}) collective-permute-start(bf16[128,128]{1,0:T(8,128)(2,1)S(1)} %shard_map.75), channel_id=1, source_target_pairs={{0,1},{1,0},{2,3},{3,2},{4,5},{5,4},{6,7},{7,6},{8,9},{9,8},{10,11... | collective-permute-start | bytes 98312 | tf_op jit(solution)/shard_map/ppermute | solution.py:188

commit v23 on v21

--- a/solution.py
+++ b/solution.py
@@ -279,9 +279,8 @@
         return lax.ppermute(total, "rows", tuple(enumerate(table)))
 
     one = lax.ppermute(documents, "rows", ROUND_ONE)
-    later, conditioned = lax.optimization_barrier((documents, conditioned))
-    two = lax.ppermute(later, "rows", ROUND_TWO)
-    own = halves(later, lambda row: row)
+    two = lax.ppermute(documents, "rows", ROUND_TWO)
+    own = halves(documents, lambda row: row)
     one, own = lax.optimization_barrier((one, own))
     three = lax.ppermute(one, "rows", ROUND_ONE)
 

time: 50.7 us -> 50.7 us (level)
  waiting for transfers between devices: 23.2 us -> 22.4 us
  local copies, waits for them, and re-layouts: 1.74 us -> 2.41 us
    ppermute x1, waiting for transfers between devices: 3.93 us -> 3.17 us  [along_line(): one = lax.ppermute(documents, 'rows', ROUND_ONE)]
    broadcast_in_dim x1, local copies, waits for them, and re-layouts: 0.14 us -> 0.82 us  [local(): return plan(train_grads, conditioned, query_doc_ids[:, None])]
    unnamed x6 -> x4, local copies, waits for them, and re-layouts: 1.6 us -> 1.59 us
  transfers between devices with their start and end apart: 12 -> 12, of which waited for: 11 -> 11; matrix products, arithmetic and copies ran while one was open for 0% -> 2% of each run, Pallas kernels for 20% -> 20%
where the time goes in v23:
time: 50.7 us; the launch traced here: 50.5 us
  waiting for transfers between devices  22.4 us (44%)
  starting transfers between devices  14.6 us (29%)
  Pallas kernels  10.9 us (21%)
  local copies, waits for them, and re-layouts  2.41 us (5%)
    ppermute x6, waiting for transfers between devices, swap(): lax.ppermute(value, 'layer', [(lay, lay ^ distance) for lay in range(coun...  6.66 us
    pallas_call x1, Pallas kernels, prepare(): pl.pallas_call(prepare_kernel, out_shape=jax.ShapeDtypeStruct((rows, dims...  6.29 us
    ppermute x1, waiting for transfers between devices, along_line(): two = lax.ppermute(documents, 'rows', ROUND_TWO)  4.38 us
    ppermute x1, waiting for transfers between devices, along_line(): mine = lax.ppermute(both, ('rows', 'layer'), pairs)  4.17 us
    ppermute x1, starting transfers between devices, along_line(): one = lax.ppermute(documents, 'rows', ROUND_ONE)  4.04 us
    ppermute x1, waiting for transfers between devices, along_line(): three = lax.ppermute(one, 'rows', ROUND_ONE)  3.65 us
    ppermute x6, starting transfers between devices, swap(): lax.ppermute(value, 'layer', [(lay, lay ^ distance) for lay in range(coun...  3.4 us
    ppermute x1, starting transfers between devices, along_line(): three = lax.ppermute(one, 'rows', ROUND_ONE)  3.33 us
  transfers between devices with their start and end apart: 12, of which 11 were waited for; matrix products, arithmetic and copies ran while one was open for 2% of the time, Pallas kernels for 20%

profile of v23, /device:TPU:0, one launch (start us, length us, event | category | flops | bytes accessed | tf_op | source)
XLA Modules:
  0.0 50.5 jit_solution(3329772744227342484)
XLA Ops:
  0.0 4.0 %collective-permute-start = (bf16[128,2048]{1,0:T(8,128)(2,1)}, bf16[128,2048]{1,0:T(8,128)(2,1)S(1)}, u32[]{:S(2)}, u32[]{:S(2)}) collective-permute-start(bf16[128,2048]{1,0:T(8,128)(2,1)} %documents_ref.1), channel_id=1, source_target_pairs={{0,8},{8,12},{12,4},{4,0},{1,9},{9,13},{13,5},{5,1},{2,10},{10,14}... | collective-permute-start | bytes 1572872 | tf_op jit(solution)/shard_map/ppermute | solution.py:281
  4.0 0.0 collective-permute-start.2
  4.0 0.8 %copy.11.ids_ref = s32[512,1]{1,0:T(8,128)S(1)} copy(s32[512,1]{0,1:T(1,128)} %bitcast.1) | data formatting | bytes 4096 | tf_op jit(solution)/shard_map/broadcast_in_dim | solution.py:334
  4.9 0.0 copy-start.1
  4.9 6.3 %shard_map.64.queries_ref = bf16[512,2048]{1,0:T(8,128)(2,1)} custom-call(s32[4]{0:T(128)} %offsets.1, bf16[512,2048]{1,0:T(8,128)(2,1)} %queries_hbm.1, bf16[4,512,512]{2,1,0:T(8,128)(2,1)} %bases_hbm.1, f32[4,512]{1,0:T(4,128)} %values_hbm.1), custom_call_target="tpu_custom_call" | custom-call | flops 2147483648 | bytes 6291456 | tf_op jit(solution)/shard_map/pallas_call | solution.py:52
  11.2 0.0 copy-done.1
  11.2 0.0 copy-start
  11.2 1.6 %copy-done = bf16[512,2048]{1,0:T(8,128)(2,1)S(1)} copy-done((bf16[512,2048]{1,0:T(8,128)(2,1)S(1)}, bf16[512,2048]{1,0:T(8,128)(2,1)}, u32[]{:S(2)}) %copy-start) | copy-done | bytes 2097176
  12.8 0.8 %shard_map.65 = (f32[256,128]{1,0:T(8,128)S(1)}, f32[256,128]{1,0:T(8,128)S(1)}) custom-call(bf16[512,2048]{1,0:T(8,128)(2,1)S(1)} %copy-done, s32[512,1]{1,0:T(8,128)S(1)} %copy.11.ids_ref, bf16[128,2048]{1,0:T(8,128)(2,1)S(1)} %copy-done.1), custom_call_target="tpu_custom_call" | custom-call | flops 268435456 | bytes 2621440 | tf_op jit(solution)/shard_map/pallas_call | solution.py:81
  13.6 3.2 %collective-permute-done.documents_ref = bf16[128,2048]{1,0:T(8,128)(2,1)S(1)} collective-permute-done((bf16[128,2048]{1,0:T(8,128)(2,1)}, bf16[128,2048]{1,0:T(8,128)(2,1)S(1)}, u32[]{:S(2)}, u32[]{:S(2)}) %collective-permute-start) | collective-permute-done | bytes 524320 | tf_op jit(solution)/shard_map/ppermute | solution.py:281
  16.7 0.8 %shard_map.66 = (f32[256,256]{1,0:T(8,128)S(1)}, f32[256,256]{1,0:T(8,128)S(1)}) custom-call(bf16[512,2048]{1,0:T(8,128)(2,1)S(1)} %copy-done, s32[512,1]{1,0:T(8,128)S(1)} %copy.11.ids_ref, bf16[128,2048]{1,0:T(8,128)(2,1)S(1)} %collective-permute-done.documents_ref, f32[256,128]{1,0:T(8,128)S(1)} %get-tuple-element.29.refs_0_, ...), custom_call_target="tpu_custom_call" | custom-call | flops 268435456 | bytes 2621440 | tf_op jit(solution)/shard_map/pallas_call | solution.py:81
  17.5 0.1 collective-permute-start.3
  17.6 3.3 %collective-permute-start.1 = (bf16[128,2048]{1,0:T(8,128)(2,1)S(1)}, bf16[128,2048]{1,0:T(8,128)(2,1)S(1)}, u32[]{:S(2)}, u32[]{:S(2)}) collective-permute-start(bf16[128,2048]{1,0:T(8,128)(2,1)S(1)} %collective-permute-done.documents_ref), channel_id=1, source_target_pairs={{0,8},{8,12},{12,4},{4,0},{1,9},{9,13},{13,5},{5,1},{2,10},{10,14}... | collective-permute-start | bytes 1572872 | tf_op jit(solution)/shard_map/ppermute | solution.py:285
  20.9 0.0 collective-permute-done.3.arrived_ref
  20.9 1.6 %collective-permute-start.4 = (bf16[128,256]{1,0:T(8,128)(2,1)S(1)}, bf16[128,256]{1,0:T(8,128)(2,1)S(1)}, u32[]{:S(2)}, u32[]{:S(2)}) collective-permute-start(bf16[128,256]{1,0:T(8,128)(2,1)S(1)} %get-tuple-element.34), channel_id=1, source_target_pairs={{0,2},{1,3},{2,0},{3,1},{4,6},{5,7},{6,4},{7,5},{8,10},{9,11},{10,... | collective-permute-start | bytes 196616 | tf_op jit(solution)/shard_map/ppermute | solution.py:186
  22.5 2.8 %collective-permute-done.4.arrived_ref = bf16[128,256]{1,0:T(8,128)(2,1)S(1)} collective-permute-done((bf16[128,256]{1,0:T(8,128)(2,1)S(1)}, bf16[128,256]{1,0:T(8,128)(2,1)S(1)}, u32[]{:S(2)}, u32[]{:S(2)}) %collective-permute-start.4) | collective-permute-done | bytes 65568 | tf_op jit(solution)/shard_map/ppermute | solution.py:186
  25.3 4.4 %collective-permute-done.2.documents_ref = bf16[128,2048]{1,0:T(8,128)(2,1)S(1)} collective-permute-done((bf16[128,2048]{1,0:T(8,128)(2,1)}, bf16[128,2048]{1,0:T(8,128)(2,1)S(1)}, u32[]{:S(2)}, u32[]{:S(2)}) %collective-permute-start.2) | collective-permute-done | bytes 524320 | tf_op jit(solution)/shard_map/ppermute | solution.py:282
  29.7 0.8 %shard_map.69 = (f32[256,128]{1,0:T(8,128)S(1)}, f32[256,128]{1,0:T(8,128)S(1)}) custom-call(bf16[512,2048]{1,0:T(8,128)(2,1)S(1)} %copy-done, s32[512,1]{1,0:T(8,128)S(1)} %copy.11.ids_ref, bf16[128,2048]{1,0:T(8,128)(2,1)S(1)} %collective-permute-done.2.documents_ref), custom_call_target="tpu_custom_call" | custom-call | flops 268435456 | bytes 2621440 | tf_op jit(solution)/shard_map/pallas_call | solution.py:81
  30.4 0.1 collective-permute-start.5
  30.5 1.3 %collective-permute-done.5.arrived_ref = f32[256,128]{1,0:T(8,128)S(1)} collective-permute-done((f32[256,128]{1,0:T(8,128)S(1)}, f32[256,128]{1,0:T(8,128)S(1)}, u32[]{:S(2)}, u32[]{:S(2)}) %collective-permute-start.5) | collective-permute-done | bytes 131104 | tf_op jit(solution)/shard_map/ppermute | solution.py:186
  31.9 1.6 %collective-permute-start.6 = (bf16[128,128]{1,0:T(8,128)(2,1)S(1)}, bf16[128,128]{1,0:T(8,128)(2,1)S(1)}, u32[]{:S(2)}, u32[]{:S(2)}) collective-permute-start(bf16[128,128]{1,0:T(8,128)(2,1)S(1)} %get-tuple-element.41), channel_id=1, source_target_pairs={{0,2},{1,3},{2,0},{3,1},{4,6},{5,7},{6,4},{7,5},{8,10},{9,11},{10,... | collective-permute-start | bytes 98312 | tf_op jit(solution)/shard_map/ppermute | solution.py:186
  33.4 0.7 %collective-permute-start.7 = (bf16[128,128]{1,0:T(8,128)(2,1)S(1)}, bf16[128,128]{1,0:T(8,128)(2,1)S(1)}, u32[]{:S(2)}, u32[]{:S(2)}) collective-permute-start(bf16[128,128]{1,0:T(8,128)(2,1)S(1)} %get-tuple-element.36), channel_id=1, source_target_pairs={{0,4},{4,12},{8,0},{12,8},{1,5},{5,13},{9,1},{13,9},{2,6},{6,14},{... | collective-permute-start | bytes 98312 | tf_op jit(solution)/shard_map/ppermute | solution.py:279
  34.1 1.7 %collective-permute-done.6.arrived_ref = bf16[128,128]{1,0:T(8,128)(2,1)S(1)} collective-permute-done((bf16[128,128]{1,0:T(8,128)(2,1)S(1)}, bf16[128,128]{1,0:T(8,128)(2,1)S(1)}, u32[]{:S(2)}, u32[]{:S(2)}) %collective-permute-start.6) | collective-permute-done | bytes 32800 | tf_op jit(solution)/shard_map/ppermute | solution.py:186
  35.8 0.6 %collective-permute-start.8 = (bf16[128,128]{1,0:T(8,128)(2,1)S(1)}, bf16[128,128]{1,0:T(8,128)(2,1)S(1)}, u32[]{:S(2)}, u32[]{:S(2)}) collective-permute-start(bf16[128,128]{1,0:T(8,128)(2,1)S(1)} %shard_map.71), channel_id=1, source_target_pairs={{0,8},{4,0},{8,12},{12,4},{1,9},{5,1},{9,13},{13,5},{2,10},{6,2},{... | collective-permute-start | bytes 98312 | tf_op jit(solution)/shard_map/ppermute | solution.py:279
  36.5 3.6 %collective-permute-done.1.documents_ref = bf16[128,2048]{1,0:T(8,128)(2,1)S(1)} collective-permute-done((bf16[128,2048]{1,0:T(8,128)(2,1)S(1)}, bf16[128,2048]{1,0:T(8,128)(2,1)S(1)}, u32[]{:S(2)}, u32[]{:S(2)}) %collective-permute-start.1) | collective-permute-done | bytes 524320 | tf_op jit(solution)/shard_map/ppermute | solution.py:285
  40.1 0.4 shard_map.73
  40.5 0.1 collective-permute-start.9
  40.7 0.2 collective-permute-done.7.first_ref
  40.9 0.2 collective-permute-done.8.second_ref
  41.1 0.4 shard_map.72.refs_0_
  41.5 0.3 collective-permute-done.9.refs_1_
  41.9 2.5 %collective-permute-start.10 = (bf16[256,128]{1,0:T(8,128)(2,1)S(1)}, bf16[256,128]{1,0:T(8,128)(2,1)S(1)}, u32[]{:S(2)}, u32[]{:S(2)}) collective-permute-start(bf16[256,128]{1,0:T(8,128)(2,1)S(1)} %shard_map.74), channel_id=1, source_target_pairs={{0,12},{1,15},{2,14},{3,13},{4,8},{5,11},{6,10},{7,9},{8,4},{9,7},... | collective-permute-start | bytes 196616 | tf_op jit(solution)/shard_map/ppermute | solution.py:303
  44.4 4.2 %collective-permute-done.10.mine_ref = bf16[256,128]{1,0:T(8,128)(2,1)S(1)} collective-permute-done((bf16[256,128]{1,0:T(8,128)(2,1)S(1)}, bf16[256,128]{1,0:T(8,128)(2,1)S(1)}, u32[]{:S(2)}, u32[]{:S(2)}) %collective-permute-start.10) | collective-permute-done | bytes 65568 | tf_op jit(solution)/shard_map/ppermute | solution.py:303
  48.6 0.0 collective-permute-start.11
  48.6 0.7 %shard_map.76.scores_hbm = f32[4,128,128]{2,1,0:T(8,128)} custom-call(f32[128,128]{1,0:T(8,128)S(1)} %get-tuple-element.44.own_ref, bf16[128,128]{1,0:T(8,128)(2,1)S(1)} %collective-permute-done.7.first_ref, bf16[128,128]{1,0:T(8,128)(2,1)S(1)} %collective-permute-done.8.second_ref), custom_call_target="tpu_custom_call" | custom-call | tf_op jit(solution)/shard_map/pallas_call | solution.py:148
  49.3 0.5 collective-permute-done.11.arrived_ref
  49.8 0.6 %shard_map.77 = f32[4,128,128]{2,1,0:T(8,128)} custom-call(bf16[256,128]{1,0:T(8,128)(2,1)S(1)} %collective-permute-done.10.mine_ref, bf16[128,128]{1,0:T(8,128)(2,1)S(1)} %collective-permute-done.11.arrived_ref, f32[4,128,128]{2,1,0:T(8,128)} %shard_map.76.scores_hbm), custom_call_target="tpu_custom_call", output_to_operand_aliasing={{}: (2, {})} | custom-call | tf_op jit(solution)/shard_map/pallas_call | solution.py:250
  (6 shorter events, 0.1 us)
Async XLA Ops:
  0.0 16.7 %collective-permute-start = (bf16[128,2048]{1,0:T(8,128)(2,1)}, bf16[128,2048]{1,0:T(8,128)(2,1)S(1)}, u32[]{:S(2)}, u32[]{:S(2)}) collective-permute-start(bf16[128,2048]{1,0:T(8,128)(2,1)} %documents_ref.1), channel_id=1, source_target_pairs={{0,8},{8,12},{12,4},{4,0},{1,9},{9,13},{13,5},{5,1},{2,10},{10,14}... | collective-permute-start | bytes 1572872 | tf_op jit(solution)/shard_map/ppermute | solution.py:281
  4.0 25.6 %collective-permute-start.2 = (bf16[128,2048]{1,0:T(8,128)(2,1)}, bf16[128,2048]{1,0:T(8,128)(2,1)S(1)}, u32[]{:S(2)}, u32[]{:S(2)}) collective-permute-start(bf16[128,2048]{1,0:T(8,128)(2,1)} %documents_ref.1), channel_id=1, source_target_pairs={{0,4},{4,12},{12,8},{8,0},{1,5},{5,13},{13,9},{9,1},{2,6},{6,14},{... | collective-permute-start | bytes 1572872 | tf_op jit(solution)/shard_map/ppermute | solution.py:282
  4.9 6.3 %copy-start.1 = (bf16[128,2048]{1,0:T(8,128)(2,1)S(1)}, bf16[128,2048]{1,0:T(8,128)(2,1)}, u32[]{:S(2)}) copy-start(bf16[128,2048]{1,0:T(8,128)(2,1)} %documents_ref.1) | copy-start | bytes 1572868
  11.2 1.6 %copy-start = (bf16[512,2048]{1,0:T(8,128)(2,1)S(1)}, bf16[512,2048]{1,0:T(8,128)(2,1)}, u32[]{:S(2)}) copy-start(bf16[512,2048]{1,0:T(8,128)(2,1)} %shard_map.64.queries_ref) | copy-start | bytes 6291460
  17.5 3.4 %collective-permute-start.3 = (f32[256,256]{1,0:T(8,128)S(1)}, f32[256,256]{1,0:T(8,128)S(1)}, u32[]{:S(2)}, u32[]{:S(2)}) collective-permute-start(f32[256,256]{1,0:T(8,128)S(1)} %get-tuple-element.32), channel_id=1, source_target_pairs={{0,1},{1,0},{2,3},{3,2},{4,5},{5,4},{6,7},{7,6},{8,9},{9,8},{10,11... | collective-permute-start | bytes 786440 | tf_op jit(solution)/shard_map/ppermute | solution.py:186
  17.6 22.5 %collective-permute-start.1 = (bf16[128,2048]{1,0:T(8,128)(2,1)S(1)}, bf16[128,2048]{1,0:T(8,128)(2,1)S(1)}, u32[]{:S(2)}, u32[]{:S(2)}) collective-permute-start(bf16[128,2048]{1,0:T(8,128)(2,1)S(1)} %collective-permute-done.documents_ref), channel_id=1, source_target_pairs={{0,8},{8,12},{12,4},{4,0},{1,9},{9,13},{13,5},{5,1},{2,10},{10,14}... | collective-permute-start | bytes 1572872 | tf_op jit(solution)/shard_map/ppermute | solution.py:285
  20.9 4.3 %collective-permute-start.4 = (bf16[128,256]{1,0:T(8,128)(2,1)S(1)}, bf16[128,256]{1,0:T(8,128)(2,1)S(1)}, u32[]{:S(2)}, u32[]{:S(2)}) collective-permute-start(bf16[128,256]{1,0:T(8,128)(2,1)S(1)} %get-tuple-element.34), channel_id=1, source_target_pairs={{0,2},{1,3},{2,0},{3,1},{4,6},{5,7},{6,4},{7,5},{8,10},{9,11},{10,... | collective-permute-start | bytes 196616 | tf_op jit(solution)/shard_map/ppermute | solution.py:186
  30.4 1.4 %collective-permute-start.5 = (f32[256,128]{1,0:T(8,128)S(1)}, f32[256,128]{1,0:T(8,128)S(1)}, u32[]{:S(2)}, u32[]{:S(2)}) collective-permute-start(f32[256,128]{1,0:T(8,128)S(1)} %get-tuple-element.39), channel_id=1, source_target_pairs={{0,1},{1,0},{2,3},{3,2},{4,5},{5,4},{6,7},{7,6},{8,9},{9,8},{10,11... | collective-permute-start | bytes 393224 | tf_op jit(solution)/shard_map/ppermute | solution.py:186
  31.9 4.0 %collective-permute-start.6 = (bf16[128,128]{1,0:T(8,128)(2,1)S(1)}, bf16[128,128]{1,0:T(8,128)(2,1)S(1)}, u32[]{:S(2)}, u32[]{:S(2)}) collective-permute-start(bf16[128,128]{1,0:T(8,128)(2,1)S(1)} %get-tuple-element.41), channel_id=1, source_target_pairs={{0,2},{1,3},{2,0},{3,1},{4,6},{5,7},{6,4},{7,5},{8,10},{9,11},{10,... | collective-permute-start | bytes 98312 | tf_op jit(solution)/shard_map/ppermute | solution.py:186
  33.4 7.5 %collective-permute-start.7 = (bf16[128,128]{1,0:T(8,128)(2,1)S(1)}, bf16[128,128]{1,0:T(8,128)(2,1)S(1)}, u32[]{:S(2)}, u32[]{:S(2)}) collective-permute-start(bf16[128,128]{1,0:T(8,128)(2,1)S(1)} %get-tuple-element.36), channel_id=1, source_target_pairs={{0,4},{4,12},{8,0},{12,8},{1,5},{5,13},{9,1},{13,9},{2,6},{6,14},{... | collective-permute-start | bytes 98312 | tf_op jit(solution)/shard_map/ppermute | solution.py:279
  35.8 5.3 %collective-permute-start.8 = (bf16[128,128]{1,0:T(8,128)(2,1)S(1)}, bf16[128,128]{1,0:T(8,128)(2,1)S(1)}, u32[]{:S(2)}, u32[]{:S(2)}) collective-permute-start(bf16[128,128]{1,0:T(8,128)(2,1)S(1)} %shard_map.71), channel_id=1, source_target_pairs={{0,8},{4,0},{8,12},{12,4},{1,9},{5,1},{9,13},{13,5},{2,10},{6,2},{... | collective-permute-start | bytes 98312 | tf_op jit(solution)/shard_map/ppermute | solution.py:279
  40.5 1.3 %collective-permute-start.9 = (bf16[256,128]{1,0:T(8,128)(2,1)S(1)}, bf16[256,128]{1,0:T(8,128)(2,1)S(1)}, u32[]{:S(2)}, u32[]{:S(2)}) collective-permute-start(bf16[256,128]{1,0:T(8,128)(2,1)S(1)} %shard_map.73), channel_id=1, source_target_pairs={{0,1},{1,0},{2,3},{3,2},{4,5},{5,4},{6,7},{7,6},{8,9},{9,8},{10,11... | collective-permute-start | bytes 196616 | tf_op jit(solution)/shard_map/ppermute | solution.py:186
  41.9 6.7 %collective-permute-start.10 = (bf16[256,128]{1,0:T(8,128)(2,1)S(1)}, bf16[256,128]{1,0:T(8,128)(2,1)S(1)}, u32[]{:S(2)}, u32[]{:S(2)}) collective-permute-start(bf16[256,128]{1,0:T(8,128)(2,1)S(1)} %shard_map.74), channel_id=1, source_target_pairs={{0,12},{1,15},{2,14},{3,13},{4,8},{5,11},{6,10},{7,9},{8,4},{9,7},... | collective-permute-start | bytes 196616 | tf_op jit(solution)/shard_map/ppermute | solution.py:303
  48.6 1.2 %collective-permute-start.11 = (bf16[128,128]{1,0:T(8,128)(2,1)S(1)}, bf16[128,128]{1,0:T(8,128)(2,1)S(1)}, u32[]{:S(2)}, u32[]{:S(2)}) collective-permute-start(bf16[128,128]{1,0:T(8,128)(2,1)S(1)} %shard_map.75), channel_id=1, source_target_pairs={{0,1},{1,0},{2,3},{3,2},{4,5},{5,4},{6,7},{7,6},{8,9},{9,8},{10,11... | collective-permute-start | bytes 98312 | tf_op jit(solution)/shard_map/ppermute | solution.py:186

commit v24 on v23

--- a/solution.py
+++ b/solution.py
@@ -60,7 +60,7 @@
             pltpu.VMEM(values.shape, jnp.float32),
             pltpu.SemaphoreType.DMA((1 + 2 * LAY_DEV,)),
         ],
-        compiler_params=pltpu.CompilerParams(vmem_limit_bytes=62 * MIB),
+        compiler_params=pltpu.CompilerParams(vmem_limit_bytes=48 * MIB),
         cost_estimate=pl.CostEstimate(
             flops=4 * rows * dims * LDIM, bytes_accessed=6 * MIB, transcendentals=0
         ),

time: 50.7 us -> 50.7 us (level)
  Pallas kernels: 10.9 us -> 9.22 us
  local copies, waits for them, and re-layouts: 2.41 us -> 3.76 us
    pallas_call x1, Pallas kernels: 6.29 us -> 4.59 us  [prepare(): pl.pallas_call(prepare_kernel, out_shape=jax.ShapeDtypeStruct((rows, dims...]
    unnamed x4 -> x8, local copies, waits for them, and re-layouts: 1.59 us -> 2.94 us
  transfers between devices with their start and end apart: 12 -> 12, of which waited for: 11 -> 11; matrix products, arithmetic and copies ran while one was open for 2% -> 2% of each run, Pallas kernels for 20% -> 17%
where the time goes in v24:
time: 50.7 us; the launch traced here: 50.5 us
  waiting for transfers between devices  22.8 us (45%)
  starting transfers between devices  14.6 us (29%)
  Pallas kernels  9.22 us (18%)
  local copies, waits for them, and re-layouts  3.76 us (7%)
    ppermute x6, waiting for transfers between devices, swap(): lax.ppermute(value, 'layer', [(lay, lay ^ distance) for lay in range(coun...  6.66 us
    pallas_call x1, Pallas kernels, prepare(): pl.pallas_call(prepare_kernel, out_shape=jax.ShapeDtypeStruct((rows, dims...  4.59 us
    ppermute x1, waiting for transfers between devices, along_line(): two = lax.ppermute(documents, 'rows', ROUND_TWO)  4.38 us
    ppermute x1, waiting for transfers between devices, along_line(): mine = lax.ppermute(both, ('rows', 'layer'), pairs)  4.17 us
    ppermute x1, starting transfers between devices, along_line(): one = lax.ppermute(documents, 'rows', ROUND_ONE)  4.04 us
    ppermute x1, waiting for transfers between devices, along_line(): three = lax.ppermute(one, 'rows', ROUND_ONE)  3.64 us
    ppermute x1, waiting for transfers between devices, along_line(): one = lax.ppermute(documents, 'rows', ROUND_ONE)  3.52 us
    ppermute x6, starting transfers between devices, swap(): lax.ppermute(value, 'layer', [(lay, lay ^ distance) for lay in range(coun...  3.4 us
  transfers between devices with their start and end apart: 12, of which 11 were waited for; matrix products, arithmetic and copies ran while one was open for 2% of the time, Pallas kernels for 17%

profile of v24, /device:TPU:0, one launch (start us, length us, event | category | flops | bytes accessed | tf_op | source)
XLA Modules:
  0.0 50.5 jit_solution(2566480352437676437)
XLA Ops:
  0.0 4.0 %collective-permute-start = (bf16[128,2048]{1,0:T(8,128)(2,1)}, bf16[128,2048]{1,0:T(8,128)(2,1)S(1)}, u32[]{:S(2)}, u32[]{:S(2)}) collective-permute-start(bf16[128,2048]{1,0:T(8,128)(2,1)} %documents_ref.1), channel_id=1, source_target_pairs={{0,8},{8,12},{12,4},{4,0},{1,9},{9,13},{13,5},{5,1},{2,10},{10,14}... | collective-permute-start | bytes 1572872 | tf_op jit(solution)/shard_map/ppermute | solution.py:281
  4.0 0.0 collective-permute-start.2
  4.0 0.8 %copy.11.ids_ref = s32[512,1]{1,0:T(8,128)S(1)} copy(s32[512,1]{0,1:T(1,128)} %bitcast.1) | data formatting | bytes 4096 | tf_op jit(solution)/shard_map/broadcast_in_dim | solution.py:334
  4.9 0.0 copy-start.1
  4.9 1.6 %copy-done.1 = bf16[512,2048]{1,0:T(8,128)(2,1)S(1)} copy-done((bf16[512,2048]{1,0:T(8,128)(2,1)S(1)}, bf16[512,2048]{1,0:T(8,128)(2,1)}, u32[]{:S(2)}) %copy-start.1) | copy-done | bytes 2097176
  6.5 0.0 copy-start.2
  6.5 0.7 %copy-done.2 = f32[4,512]{1,0:T(4,128)S(1)} copy-done((f32[4,512]{1,0:T(4,128)S(1)}, f32[4,512]{1,0:T(4,128)}, u32[]{:S(2)}) %copy-start.2) | copy-done | bytes 8216
  7.2 0.0 copy-start.3
  7.2 0.7 %copy-done.3 = s32[4]{0:T(128)S(1)} copy-done((s32[4]{0:T(128)S(1)}, s32[4]{0:T(128)}, u32[]{:S(2)}) %copy-start.3) | copy-done | bytes 40
  7.8 0.0 copy-start
  7.8 4.6 %shard_map.64.queries_ref = bf16[512,2048]{1,0:T(8,128)(2,1)S(1)} custom-call(s32[4]{0:T(128)S(1)} %copy-done.3, bf16[512,2048]{1,0:T(8,128)(2,1)S(1)} %copy-done.1, bf16[4,512,512]{2,1,0:T(8,128)(2,1)} %bases_hbm.1, f32[4,512]{1,0:T(4,128)S(1)} %copy-done.2), custom_call_target="tpu_custom_call" | custom-call | flops 2147483648 | bytes 6291456 | tf_op jit(solution)/shard_map/pallas_call | solution.py:52
  12.4 0.0 copy-done
  12.4 0.8 %shard_map.65 = (f32[256,128]{1,0:T(8,128)S(1)}, f32[256,128]{1,0:T(8,128)S(1)}) custom-call(bf16[512,2048]{1,0:T(8,128)(2,1)S(1)} %shard_map.64.queries_ref, s32[512,1]{1,0:T(8,128)S(1)} %copy.11.ids_ref, bf16[128,2048]{1,0:T(8,128)(2,1)S(1)} %copy-done), custom_call_target="tpu_custom_call" | custom-call | flops 268435456 | bytes 2621440 | tf_op jit(solution)/shard_map/pallas_call | solution.py:81
  13.2 3.5 %collective-permute-done.documents_ref = bf16[128,2048]{1,0:T(8,128)(2,1)S(1)} collective-permute-done((bf16[128,2048]{1,0:T(8,128)(2,1)}, bf16[128,2048]{1,0:T(8,128)(2,1)S(1)}, u32[]{:S(2)}, u32[]{:S(2)}) %collective-permute-start) | collective-permute-done | bytes 524320 | tf_op jit(solution)/shard_map/ppermute | solution.py:281
  16.7 0.8 %shard_map.66 = (f32[256,256]{1,0:T(8,128)S(1)}, f32[256,256]{1,0:T(8,128)S(1)}) custom-call(bf16[512,2048]{1,0:T(8,128)(2,1)S(1)} %shard_map.64.queries_ref, s32[512,1]{1,0:T(8,128)S(1)} %copy.11.ids_ref, bf16[128,2048]{1,0:T(8,128)(2,1)S(1)} %collective-permute-done.documents_ref, f32[256,128]{1,0:T(8,128)S(1)} %get-tuple-element.29.refs_0_, ...), custom_call_target="tpu_custom_call" | custom-call | flops 268435456 | bytes 2621440 | tf_op jit(solution)/shard_map/pallas_call | solution.py:81
  17.5 0.1 collective-permute-start.3
  17.6 3.3 %collective-permute-start.1 = (bf16[128,2048]{1,0:T(8,128)(2,1)S(1)}, bf16[128,2048]{1,0:T(8,128)(2,1)S(1)}, u32[]{:S(2)}, u32[]{:S(2)}) collective-permute-start(bf16[128,2048]{1,0:T(8,128)(2,1)S(1)} %collective-permute-done.documents_ref), channel_id=1, source_target_pairs={{0,8},{8,12},{12,4},{4,0},{1,9},{9,13},{13,5},{5,1},{2,10},{10,14}... | collective-permute-start | bytes 1572872 | tf_op jit(solution)/shard_map/ppermute | solution.py:285
  20.9 0.0 collective-permute-done.3.arrived_ref
  20.9 1.6 %collective-permute-start.4 = (bf16[128,256]{1,0:T(8,128)(2,1)S(1)}, bf16[128,256]{1,0:T(8,128)(2,1)S(1)}, u32[]{:S(2)}, u32[]{:S(2)}) collective-permute-start(bf16[128,256]{1,0:T(8,128)(2,1)S(1)} %get-tuple-element.34), channel_id=1, source_target_pairs={{0,2},{1,3},{2,0},{3,1},{4,6},{5,7},{6,4},{7,5},{8,10},{9,11},{10,... | collective-permute-start | bytes 196616 | tf_op jit(solution)/shard_map/ppermute | solution.py:186
  22.5 2.8 %collective-permute-done.4.arrived_ref = bf16[128,256]{1,0:T(8,128)(2,1)S(1)} collective-permute-done((bf16[128,256]{1,0:T(8,128)(2,1)S(1)}, bf16[128,256]{1,0:T(8,128)(2,1)S(1)}, u32[]{:S(2)}, u32[]{:S(2)}) %collective-permute-start.4) | collective-permute-done | bytes 65568 | tf_op jit(solution)/shard_map/ppermute | solution.py:186
  25.3 4.4 %collective-permute-done.2.documents_ref = bf16[128,2048]{1,0:T(8,128)(2,1)S(1)} collective-permute-done((bf16[128,2048]{1,0:T(8,128)(2,1)}, bf16[128,2048]{1,0:T(8,128)(2,1)S(1)}, u32[]{:S(2)}, u32[]{:S(2)}) %collective-permute-start.2) | collective-permute-done | bytes 524320 | tf_op jit(solution)/shard_map/ppermute | solution.py:282
  29.7 0.8 %shard_map.69 = (f32[256,128]{1,0:T(8,128)S(1)}, f32[256,128]{1,0:T(8,128)S(1)}) custom-call(bf16[512,2048]{1,0:T(8,128)(2,1)S(1)} %shard_map.64.queries_ref, s32[512,1]{1,0:T(8,128)S(1)} %copy.11.ids_ref, bf16[128,2048]{1,0:T(8,128)(2,1)S(1)} %collective-permute-done.2.documents_ref), custom_call_target="tpu_custom_call" | custom-call | flops 268435456 | bytes 2621440 | tf_op jit(solution)/shard_map/pallas_call | solution.py:81
  30.4 0.1 collective-permute-start.5
  30.5 1.3 %collective-permute-done.5.arrived_ref = f32[256,128]{1,0:T(8,128)S(1)} collective-permute-done((f32[256,128]{1,0:T(8,128)S(1)}, f32[256,128]{1,0:T(8,128)S(1)}, u32[]{:S(2)}, u32[]{:S(2)}) %collective-permute-start.5) | collective-permute-done | bytes 131104 | tf_op jit(solution)/shard_map/ppermute | solution.py:186
  31.9 1.6 %collective-permute-start.6 = (bf16[128,128]{1,0:T(8,128)(2,1)S(1)}, bf16[128,128]{1,0:T(8,128)(2,1)S(1)}, u32[]{:S(2)}, u32[]{:S(2)}) collective-permute-start(bf16[128,128]{1,0:T(8,128)(2,1)S(1)} %get-tuple-element.41), channel_id=1, source_target_pairs={{0,2},{1,3},{2,0},{3,1},{4,6},{5,7},{6,4},{7,5},{8,10},{9,11},{10,... | collective-permute-start | bytes 98312 | tf_op jit(solution)/shard_map/ppermute | solution.py:186
  33.4 0.7 %collective-permute-start.7 = (bf16[128,128]{1,0:T(8,128)(2,1)S(1)}, bf16[128,128]{1,0:T(8,128)(2,1)S(1)}, u32[]{:S(2)}, u32[]{:S(2)}) collective-permute-start(bf16[128,128]{1,0:T(8,128)(2,1)S(1)} %get-tuple-element.36), channel_id=1, source_target_pairs={{0,4},{4,12},{8,0},{12,8},{1,5},{5,13},{9,1},{13,9},{2,6},{6,14},{... | collective-permute-start | bytes 98312 | tf_op jit(solution)/shard_map/ppermute | solution.py:279
  34.1 1.7 %collective-permute-done.6.arrived_ref = bf16[128,128]{1,0:T(8,128)(2,1)S(1)} collective-permute-done((bf16[128,128]{1,0:T(8,128)(2,1)S(1)}, bf16[128,128]{1,0:T(8,128)(2,1)S(1)}, u32[]{:S(2)}, u32[]{:S(2)}) %collective-permute-start.6) | collective-permute-done | bytes 32800 | tf_op jit(solution)/shard_map/ppermute | solution.py:186
  35.9 0.6 %collective-permute-start.8 = (bf16[128,128]{1,0:T(8,128)(2,1)S(1)}, bf16[128,128]{1,0:T(8,128)(2,1)S(1)}, u32[]{:S(2)}, u32[]{:S(2)}) collective-permute-start(bf16[128,128]{1,0:T(8,128)(2,1)S(1)} %shard_map.71), channel_id=1, source_target_pairs={{0,8},{4,0},{8,12},{12,4},{1,9},{5,1},{9,13},{13,5},{2,10},{6,2},{... | collective-permute-start | bytes 98312 | tf_op jit(solution)/shard_map/ppermute | solution.py:279
  36.5 3.6 %collective-permute-done.1.documents_ref = bf16[128,2048]{1,0:T(8,128)(2,1)S(1)} collective-permute-done((bf16[128,2048]{1,0:T(8,128)(2,1)S(1)}, bf16[128,2048]{1,0:T(8,128)(2,1)S(1)}, u32[]{:S(2)}, u32[]{:S(2)}) %collective-permute-start.1) | collective-permute-done | bytes 524320 | tf_op jit(solution)/shard_map/ppermute | solution.py:285
  40.1 0.4 shard_map.73
  40.6 0.1 collective-permute-start.9
  40.7 0.2 collective-permute-done.7.first_ref
  40.9 0.2 collective-permute-done.8.second_ref
  41.1 0.4 shard_map.72.refs_0_
  41.6 0.3 collective-permute-done.9.refs_1_
  41.9 2.5 %collective-permute-start.10 = (bf16[256,128]{1,0:T(8,128)(2,1)S(1)}, bf16[256,128]{1,0:T(8,128)(2,1)S(1)}, u32[]{:S(2)}, u32[]{:S(2)}) collective-permute-start(bf16[256,128]{1,0:T(8,128)(2,1)S(1)} %shard_map.74), channel_id=1, source_target_pairs={{0,12},{1,15},{2,14},{3,13},{4,8},{5,11},{6,10},{7,9},{8,4},{9,7},... | collective-permute-start | bytes 196616 | tf_op jit(solution)/shard_map/ppermute | solution.py:303
  44.4 4.2 %collective-permute-done.10.mine_ref = bf16[256,128]{1,0:T(8,128)(2,1)S(1)} collective-permute-done((bf16[256,128]{1,0:T(8,128)(2,1)S(1)}, bf16[256,128]{1,0:T(8,128)(2,1)S(1)}, u32[]{:S(2)}, u32[]{:S(2)}) %collective-permute-start.10) | collective-permute-done | bytes 65568 | tf_op jit(solution)/shard_map/ppermute | solution.py:303
  48.6 0.0 collective-permute-start.11
  48.6 0.7 %shard_map.76.scores_hbm = f32[4,128,128]{2,1,0:T(8,128)} custom-call(f32[128,128]{1,0:T(8,128)S(1)} %get-tuple-element.44.own_ref, bf16[128,128]{1,0:T(8,128)(2,1)S(1)} %collective-permute-done.7.first_ref, bf16[128,128]{1,0:T(8,128)(2,1)S(1)} %collective-permute-done.8.second_ref), custom_call_target="tpu_custom_call" | custom-call | tf_op jit(solution)/shard_map/pallas_call | solution.py:148
  49.3 0.5 collective-permute-done.11.arrived_ref
  49.8 0.6 %shard_map.77 = f32[4,128,128]{2,1,0:T(8,128)} custom-call(bf16[256,128]{1,0:T(8,128)(2,1)S(1)} %collective-permute-done.10.mine_ref, bf16[128,128]{1,0:T(8,128)(2,1)S(1)} %collective-permute-done.11.arrived_ref, f32[4,128,128]{2,1,0:T(8,128)} %shard_map.76.scores_hbm), custom_call_target="tpu_custom_call", output_to_operand_aliasing={{}: (2, {})} | custom-call | tf_op jit(solution)/shard_map/pallas_call | solution.py:250
  (6 shorter events, 0.1 us)
Async XLA Ops:
  0.0 16.7 %collective-permute-start = (bf16[128,2048]{1,0:T(8,128)(2,1)}, bf16[128,2048]{1,0:T(8,128)(2,1)S(1)}, u32[]{:S(2)}, u32[]{:S(2)}) collective-permute-start(bf16[128,2048]{1,0:T(8,128)(2,1)} %documents_ref.1), channel_id=1, source_target_pairs={{0,8},{8,12},{12,4},{4,0},{1,9},{9,13},{13,5},{5,1},{2,10},{10,14}... | collective-permute-start | bytes 1572872 | tf_op jit(solution)/shard_map/ppermute | solution.py:281
  4.0 25.6 %collective-permute-start.2 = (bf16[128,2048]{1,0:T(8,128)(2,1)}, bf16[128,2048]{1,0:T(8,128)(2,1)S(1)}, u32[]{:S(2)}, u32[]{:S(2)}) collective-permute-start(bf16[128,2048]{1,0:T(8,128)(2,1)} %documents_ref.1), channel_id=1, source_target_pairs={{0,4},{4,12},{12,8},{8,0},{1,5},{5,13},{13,9},{9,1},{2,6},{6,14},{... | collective-permute-start | bytes 1572872 | tf_op jit(solution)/shard_map/ppermute | solution.py:282
  4.9 1.6 %copy-start.1 = (bf16[512,2048]{1,0:T(8,128)(2,1)S(1)}, bf16[512,2048]{1,0:T(8,128)(2,1)}, u32[]{:S(2)}) copy-start(bf16[512,2048]{1,0:T(8,128)(2,1)} %queries_hbm.1) | copy-start | bytes 6291460
  6.5 0.7 %copy-start.2 = (f32[4,512]{1,0:T(4,128)S(1)}, f32[4,512]{1,0:T(4,128)}, u32[]{:S(2)}) copy-start(f32[4,512]{1,0:T(4,128)} %values_hbm.1) | copy-start | bytes 24580
  7.2 0.7 %copy-start.3 = (s32[4]{0:T(128)S(1)}, s32[4]{0:T(128)}, u32[]{:S(2)}) copy-start(s32[4]{0:T(128)} %offsets.1) | copy-start | bytes 52
  7.8 4.6 %copy-start = (bf16[128,2048]{1,0:T(8,128)(2,1)S(1)}, bf16[128,2048]{1,0:T(8,128)(2,1)}, u32[]{:S(2)}) copy-start(bf16[128,2048]{1,0:T(8,128)(2,1)} %documents_ref.1) | copy-start | bytes 1572868
  17.5 3.4 %collective-permute-start.3 = (f32[256,256]{1,0:T(8,128)S(1)}, f32[256,256]{1,0:T(8,128)S(1)}, u32[]{:S(2)}, u32[]{:S(2)}) collective-permute-start(f32[256,256]{1,0:T(8,128)S(1)} %get-tuple-element.32), channel_id=1, source_target_pairs={{0,1},{1,0},{2,3},{3,2},{4,5},{5,4},{6,7},{7,6},{8,9},{9,8},{10,11... | collective-permute-start | bytes 786440 | tf_op jit(solution)/shard_map/ppermute | solution.py:186
  17.6 22.5 %collective-permute-start.1 = (bf16[128,2048]{1,0:T(8,128)(2,1)S(1)}, bf16[128,2048]{1,0:T(8,128)(2,1)S(1)}, u32[]{:S(2)}, u32[]{:S(2)}) collective-permute-start(bf16[128,2048]{1,0:T(8,128)(2,1)S(1)} %collective-permute-done.documents_ref), channel_id=1, source_target_pairs={{0,8},{8,12},{12,4},{4,0},{1,9},{9,13},{13,5},{5,1},{2,10},{10,14}... | collective-permute-start | bytes 1572872 | tf_op jit(solution)/shard_map/ppermute | solution.py:285
  20.9 4.3 %collective-permute-start.4 = (bf16[128,256]{1,0:T(8,128)(2,1)S(1)}, bf16[128,256]{1,0:T(8,128)(2,1)S(1)}, u32[]{:S(2)}, u32[]{:S(2)}) collective-permute-start(bf16[128,256]{1,0:T(8,128)(2,1)S(1)} %get-tuple-element.34), channel_id=1, source_target_pairs={{0,2},{1,3},{2,0},{3,1},{4,6},{5,7},{6,4},{7,5},{8,10},{9,11},{10,... | collective-permute-start | bytes 196616 | tf_op jit(solution)/shard_map/ppermute | solution.py:186
  30.4 1.4 %collective-permute-start.5 = (f32[256,128]{1,0:T(8,128)S(1)}, f32[256,128]{1,0:T(8,128)S(1)}, u32[]{:S(2)}, u32[]{:S(2)}) collective-permute-start(f32[256,128]{1,0:T(8,128)S(1)} %get-tuple-element.39), channel_id=1, source_target_pairs={{0,1},{1,0},{2,3},{3,2},{4,5},{5,4},{6,7},{7,6},{8,9},{9,8},{10,11... | collective-permute-start | bytes 393224 | tf_op jit(solution)/shard_map/ppermute | solution.py:186
  31.9 4.0 %collective-permute-start.6 = (bf16[128,128]{1,0:T(8,128)(2,1)S(1)}, bf16[128,128]{1,0:T(8,128)(2,1)S(1)}, u32[]{:S(2)}, u32[]{:S(2)}) collective-permute-start(bf16[128,128]{1,0:T(8,128)(2,1)S(1)} %get-tuple-element.41), channel_id=1, source_target_pairs={{0,2},{1,3},{2,0},{3,1},{4,6},{5,7},{6,4},{7,5},{8,10},{9,11},{10,... | collective-permute-start | bytes 98312 | tf_op jit(solution)/shard_map/ppermute | solution.py:186
  33.4 7.5 %collective-permute-start.7 = (bf16[128,128]{1,0:T(8,128)(2,1)S(1)}, bf16[128,128]{1,0:T(8,128)(2,1)S(1)}, u32[]{:S(2)}, u32[]{:S(2)}) collective-permute-start(bf16[128,128]{1,0:T(8,128)(2,1)S(1)} %get-tuple-element.36), channel_id=1, source_target_pairs={{0,4},{4,12},{8,0},{12,8},{1,5},{5,13},{9,1},{13,9},{2,6},{6,14},{... | collective-permute-start | bytes 98312 | tf_op jit(solution)/shard_map/ppermute | solution.py:279
  35.9 5.3 %collective-permute-start.8 = (bf16[128,128]{1,0:T(8,128)(2,1)S(1)}, bf16[128,128]{1,0:T(8,128)(2,1)S(1)}, u32[]{:S(2)}, u32[]{:S(2)}) collective-permute-start(bf16[128,128]{1,0:T(8,128)(2,1)S(1)} %shard_map.71), channel_id=1, source_target_pairs={{0,8},{4,0},{8,12},{12,4},{1,9},{5,1},{9,13},{13,5},{2,10},{6,2},{... | collective-permute-start | bytes 98312 | tf_op jit(solution)/shard_map/ppermute | solution.py:279
  40.6 1.3 %collective-permute-start.9 = (bf16[256,128]{1,0:T(8,128)(2,1)S(1)}, bf16[256,128]{1,0:T(8,128)(2,1)S(1)}, u32[]{:S(2)}, u32[]{:S(2)}) collective-permute-start(bf16[256,128]{1,0:T(8,128)(2,1)S(1)} %shard_map.73), channel_id=1, source_target_pairs={{0,1},{1,0},{2,3},{3,2},{4,5},{5,4},{6,7},{7,6},{8,9},{9,8},{10,11... | collective-permute-start | bytes 196616 | tf_op jit(solution)/shard_map/ppermute | solution.py:186
  41.9 6.7 %collective-permute-start.10 = (bf16[256,128]{1,0:T(8,128)(2,1)S(1)}, bf16[256,128]{1,0:T(8,128)(2,1)S(1)}, u32[]{:S(2)}, u32[]{:S(2)}) collective-permute-start(bf16[256,128]{1,0:T(8,128)(2,1)S(1)} %shard_map.74), channel_id=1, source_target_pairs={{0,12},{1,15},{2,14},{3,13},{4,8},{5,11},{6,10},{7,9},{8,4},{9,7},... | collective-permute-start | bytes 196616 | tf_op jit(solution)/shard_map/ppermute | solution.py:303
  48.6 1.2 %collective-permute-start.11 = (bf16[128,128]{1,0:T(8,128)(2,1)S(1)}, bf16[128,128]{1,0:T(8,128)(2,1)S(1)}, u32[]{:S(2)}, u32[]{:S(2)}) collective-permute-start(bf16[128,128]{1,0:T(8,128)(2,1)S(1)} %shard_map.75), channel_id=1, source_target_pairs={{0,1},{1,0},{2,3},{3,2},{4,5},{5,4},{6,7},{7,6},{8,9},{9,8},{10,11... | collective-permute-start | bytes 98312 | tf_op jit(solution)/shard_map/ppermute | solution.py:186

commit v25 on v23

--- a/solution.py
+++ b/solution.py
@@ -303,6 +303,7 @@
     mine = lax.ppermute(both, ("rows", "layer"), pairs)
     out_shape = [jax.ShapeDtypeStruct((STEPS,) + own.shape, jnp.float32)]
     (scores,) = small_call(assemble_kernel, out_shape, own, first, second)
+    mine, scores = lax.optimization_barrier((mine, scores))
     (other,) = small_call(other_share_kernel, [jax.ShapeDtypeStruct(own.shape, jnp.bfloat16)], mine)
     return finish(mine, swap(other, 1), scores)
 

time: 50.7 us -> 50.7 us (level)
    ppermute x6, waiting for transfers between devices: 6.66 us -> 7.38 us  [swap(): lax.ppermute(value, 'layer', [(lay, lay ^ distance) for lay in range(coun...]
    ppermute x1, waiting for transfers between devices: 4.17 us -> 3.45 us  [along_line(): mine = lax.ppermute(both, ('rows', 'layer'), pairs)]
where the time goes in v25:
time: 50.7 us; the launch traced here: 50.5 us
  waiting for transfers between devices  22.4 us (44%)
  starting transfers between devices  14.6 us (29%)
  Pallas kernels  10.9 us (21%)
  local copies, waits for them, and re-layouts  2.41 us (5%)
    ppermute x6, waiting for transfers between devices, swap(): lax.ppermute(value, 'layer', [(lay, lay ^ distance) for lay in range(coun...  7.38 us
    pallas_call x1, Pallas kernels, prepare(): pl.pallas_call(prepare_kernel, out_shape=jax.ShapeDtypeStruct((rows, dims...  6.29 us
    ppermute x1, waiting for transfers between devices, along_line(): two = lax.ppermute(documents, 'rows', ROUND_TWO)  4.38 us
    ppermute x1, starting transfers between devices, along_line(): one = lax.ppermute(documents, 'rows', ROUND_ONE)  4.04 us
    ppermute x1, waiting for transfers between devices, along_line(): three = lax.ppermute(one, 'rows', ROUND_ONE)  3.65 us
    ppermute x1, waiting for transfers between devices, along_line(): mine = lax.ppermute(both, ('rows', 'layer'), pairs)  3.45 us
    ppermute x6, starting transfers between devices, swap(): lax.ppermute(value, 'layer', [(lay, lay ^ distance) for lay in range(coun...  3.4 us
    ppermute x1, starting transfers between devices, along_line(): three = lax.ppermute(one, 'rows', ROUND_ONE)  3.33 us
  transfers between devices with their start and end apart: 12, of which 11 were waited for; matrix products, arithmetic and copies ran while one was open for 2% of the time, Pallas kernels for 20%

profile of v25, /device:TPU:0, one launch (start us, length us, event | category | flops | bytes accessed | tf_op | source)
XLA Modules:
  0.0 50.5 jit_solution(6121700619289391407)
XLA Ops:
  0.0 4.0 %collective-permute-start = (bf16[128,2048]{1,0:T(8,128)(2,1)}, bf16[128,2048]{1,0:T(8,128)(2,1)S(1)}, u32[]{:S(2)}, u32[]{:S(2)}) collective-permute-start(bf16[128,2048]{1,0:T(8,128)(2,1)} %documents_ref.1), channel_id=1, source_target_pairs={{0,8},{8,12},{12,4},{4,0},{1,9},{9,13},{13,5},{5,1},{2,10},{10,14}... | collective-permute-start | bytes 1572872 | tf_op jit(solution)/shard_map/ppermute | solution.py:281
  4.0 0.0 collective-permute-start.2
  4.0 0.8 %copy.11.ids_ref = s32[512,1]{1,0:T(8,128)S(1)} copy(s32[512,1]{0,1:T(1,128)} %bitcast.1) | data formatting | bytes 4096 | tf_op jit(solution)/shard_map/broadcast_in_dim | solution.py:335
  4.9 0.0 copy-start.1
  4.9 6.3 %shard_map.64.queries_ref = bf16[512,2048]{1,0:T(8,128)(2,1)} custom-call(s32[4]{0:T(128)} %offsets.1, bf16[512,2048]{1,0:T(8,128)(2,1)} %queries_hbm.1, bf16[4,512,512]{2,1,0:T(8,128)(2,1)} %bases_hbm.1, f32[4,512]{1,0:T(4,128)} %values_hbm.1), custom_call_target="tpu_custom_call" | custom-call | flops 2147483648 | bytes 6291456 | tf_op jit(solution)/shard_map/pallas_call | solution.py:52
  11.2 0.0 copy-done.1
  11.2 0.0 copy-start
  11.2 1.6 %copy-done = bf16[512,2048]{1,0:T(8,128)(2,1)S(1)} copy-done((bf16[512,2048]{1,0:T(8,128)(2,1)S(1)}, bf16[512,2048]{1,0:T(8,128)(2,1)}, u32[]{:S(2)}) %copy-start) | copy-done | bytes 2097176
  12.8 0.8 %shard_map.65 = (f32[256,128]{1,0:T(8,128)S(1)}, f32[256,128]{1,0:T(8,128)S(1)}) custom-call(bf16[512,2048]{1,0:T(8,128)(2,1)S(1)} %copy-done, s32[512,1]{1,0:T(8,128)S(1)} %copy.11.ids_ref, bf16[128,2048]{1,0:T(8,128)(2,1)S(1)} %copy-done.1), custom_call_target="tpu_custom_call" | custom-call | flops 268435456 | bytes 2621440 | tf_op jit(solution)/shard_map/pallas_call | solution.py:81
  13.6 3.2 %collective-permute-done.documents_ref = bf16[128,2048]{1,0:T(8,128)(2,1)S(1)} collective-permute-done((bf16[128,2048]{1,0:T(8,128)(2,1)}, bf16[128,2048]{1,0:T(8,128)(2,1)S(1)}, u32[]{:S(2)}, u32[]{:S(2)}) %collective-permute-start) | collective-permute-done | bytes 524320 | tf_op jit(solution)/shard_map/ppermute | solution.py:281
  16.7 0.8 %shard_map.66 = (f32[256,256]{1,0:T(8,128)S(1)}, f32[256,256]{1,0:T(8,128)S(1)}) custom-call(bf16[512,2048]{1,0:T(8,128)(2,1)S(1)} %copy-done, s32[512,1]{1,0:T(8,128)S(1)} %copy.11.ids_ref, bf16[128,2048]{1,0:T(8,128)(2,1)S(1)} %collective-permute-done.documents_ref, f32[256,128]{1,0:T(8,128)S(1)} %get-tuple-element.31.refs_0_, ...), custom_call_target="tpu_custom_call" | custom-call | flops 268435456 | bytes 2621440 | tf_op jit(solution)/shard_map/pallas_call | solution.py:81
  17.5 0.1 collective-permute-start.3
  17.6 3.3 %collective-permute-start.1 = (bf16[128,2048]{1,0:T(8,128)(2,1)S(1)}, bf16[128,2048]{1,0:T(8,128)(2,1)S(1)}, u32[]{:S(2)}, u32[]{:S(2)}) collective-permute-start(bf16[128,2048]{1,0:T(8,128)(2,1)S(1)} %collective-permute-done.documents_ref), channel_id=1, source_target_pairs={{0,8},{8,12},{12,4},{4,0},{1,9},{9,13},{13,5},{5,1},{2,10},{10,14}... | collective-permute-start | bytes 1572872 | tf_op jit(solution)/shard_map/ppermute | solution.py:285
  20.9 0.0 collective-permute-done.3.arrived_ref
  20.9 1.6 %collective-permute-start.4 = (bf16[128,256]{1,0:T(8,128)(2,1)S(1)}, bf16[128,256]{1,0:T(8,128)(2,1)S(1)}, u32[]{:S(2)}, u32[]{:S(2)}) collective-permute-start(bf16[128,256]{1,0:T(8,128)(2,1)S(1)} %get-tuple-element.36), channel_id=1, source_target_pairs={{0,2},{1,3},{2,0},{3,1},{4,6},{5,7},{6,4},{7,5},{8,10},{9,11},{10,... | collective-permute-start | bytes 196616 | tf_op jit(solution)/shard_map/ppermute | solution.py:186
  22.5 2.8 %collective-permute-done.4.arrived_ref = bf16[128,256]{1,0:T(8,128)(2,1)S(1)} collective-permute-done((bf16[128,256]{1,0:T(8,128)(2,1)S(1)}, bf16[128,256]{1,0:T(8,128)(2,1)S(1)}, u32[]{:S(2)}, u32[]{:S(2)}) %collective-permute-start.4) | collective-permute-done | bytes 65568 | tf_op jit(solution)/shard_map/ppermute | solution.py:186
  25.3 4.4 %collective-permute-done.2.documents_ref = bf16[128,2048]{1,0:T(8,128)(2,1)S(1)} collective-permute-done((bf16[128,2048]{1,0:T(8,128)(2,1)}, bf16[128,2048]{1,0:T(8,128)(2,1)S(1)}, u32[]{:S(2)}, u32[]{:S(2)}) %collective-permute-start.2) | collective-permute-done | bytes 524320 | tf_op jit(solution)/shard_map/ppermute | solution.py:282
  29.7 0.8 %shard_map.69 = (f32[256,128]{1,0:T(8,128)S(1)}, f32[256,128]{1,0:T(8,128)S(1)}) custom-call(bf16[512,2048]{1,0:T(8,128)(2,1)S(1)} %copy-done, s32[512,1]{1,0:T(8,128)S(1)} %copy.11.ids_ref, bf16[128,2048]{1,0:T(8,128)(2,1)S(1)} %collective-permute-done.2.documents_ref), custom_call_target="tpu_custom_call" | custom-call | flops 268435456 | bytes 2621440 | tf_op jit(solution)/shard_map/pallas_call | solution.py:81
  30.4 0.1 collective-permute-start.5
  30.5 1.3 %collective-permute-done.5.arrived_ref = f32[256,128]{1,0:T(8,128)S(1)} collective-permute-done((f32[256,128]{1,0:T(8,128)S(1)}, f32[256,128]{1,0:T(8,128)S(1)}, u32[]{:S(2)}, u32[]{:S(2)}) %collective-permute-start.5) | collective-permute-done | bytes 131104 | tf_op jit(solution)/shard_map/ppermute | solution.py:186
  31.9 1.6 %collective-permute-start.6 = (bf16[128,128]{1,0:T(8,128)(2,1)S(1)}, bf16[128,128]{1,0:T(8,128)(2,1)S(1)}, u32[]{:S(2)}, u32[]{:S(2)}) collective-permute-start(bf16[128,128]{1,0:T(8,128)(2,1)S(1)} %get-tuple-element.43), channel_id=1, source_target_pairs={{0,2},{1,3},{2,0},{3,1},{4,6},{5,7},{6,4},{7,5},{8,10},{9,11},{10,... | collective-permute-start | bytes 98312 | tf_op jit(solution)/shard_map/ppermute | solution.py:186
  33.4 0.7 %collective-permute-start.7 = (bf16[128,128]{1,0:T(8,128)(2,1)S(1)}, bf16[128,128]{1,0:T(8,128)(2,1)S(1)}, u32[]{:S(2)}, u32[]{:S(2)}) collective-permute-start(bf16[128,128]{1,0:T(8,128)(2,1)S(1)} %get-tuple-element.38), channel_id=1, source_target_pairs={{0,4},{4,12},{8,0},{12,8},{1,5},{5,13},{9,1},{13,9},{2,6},{6,14},{... | collective-permute-start | bytes 98312 | tf_op jit(solution)/shard_map/ppermute | solution.py:279
  34.1 1.7 %collective-permute-done.6.arrived_ref = bf16[128,128]{1,0:T(8,128)(2,1)S(1)} collective-permute-done((bf16[128,128]{1,0:T(8,128)(2,1)S(1)}, bf16[128,128]{1,0:T(8,128)(2,1)S(1)}, u32[]{:S(2)}, u32[]{:S(2)}) %collective-permute-start.6) | collective-permute-done | bytes 32800 | tf_op jit(solution)/shard_map/ppermute | solution.py:186
  35.8 0.6 %collective-permute-start.8 = (bf16[128,128]{1,0:T(8,128)(2,1)S(1)}, bf16[128,128]{1,0:T(8,128)(2,1)S(1)}, u32[]{:S(2)}, u32[]{:S(2)}) collective-permute-start(bf16[128,128]{1,0:T(8,128)(2,1)S(1)} %shard_map.71), channel_id=1, source_target_pairs={{0,8},{4,0},{8,12},{12,4},{1,9},{5,1},{9,13},{13,5},{2,10},{6,2},{... | collective-permute-start | bytes 98312 | tf_op jit(solution)/shard_map/ppermute | solution.py:279
  36.5 3.6 %collective-permute-done.1.documents_ref = bf16[128,2048]{1,0:T(8,128)(2,1)S(1)} collective-permute-done((bf16[128,2048]{1,0:T(8,128)(2,1)S(1)}, bf16[128,2048]{1,0:T(8,128)(2,1)S(1)}, u32[]{:S(2)}, u32[]{:S(2)}) %collective-permute-start.1) | collective-permute-done | bytes 524320 | tf_op jit(solution)/shard_map/ppermute | solution.py:285
  40.1 0.4 shard_map.73
  40.5 0.1 collective-permute-start.9
  40.7 0.2 collective-permute-done.7.first_ref
  40.9 0.2 collective-permute-done.8.second_ref
  41.1 0.4 shard_map.72.refs_0_
  41.5 0.3 collective-permute-done.9.refs_1_
  41.9 2.5 %collective-permute-start.10 = (bf16[256,128]{1,0:T(8,128)(2,1)S(1)}, bf16[256,128]{1,0:T(8,128)(2,1)S(1)}, u32[]{:S(2)}, u32[]{:S(2)}) collective-permute-start(bf16[256,128]{1,0:T(8,128)(2,1)S(1)} %shard_map.74), channel_id=1, source_target_pairs={{0,12},{1,15},{2,14},{3,13},{4,8},{5,11},{6,10},{7,9},{8,4},{9,7},... | collective-permute-start | bytes 196616 | tf_op jit(solution)/shard_map/ppermute | solution.py:303
  44.4 0.7 %shard_map.75.scores_hbm = f32[4,128,128]{2,1,0:T(8,128)} custom-call(f32[128,128]{1,0:T(8,128)S(1)} %get-tuple-element.46.own_ref, bf16[128,128]{1,0:T(8,128)(2,1)S(1)} %collective-permute-done.7.first_ref, bf16[128,128]{1,0:T(8,128)(2,1)S(1)} %collective-permute-done.8.second_ref), custom_call_target="tpu_custom_call" | custom-call | tf_op jit(solution)/shard_map/pallas_call | solution.py:148
  45.1 3.4 %collective-permute-done.10.mine_ref = bf16[256,128]{1,0:T(8,128)(2,1)S(1)} collective-permute-done((bf16[256,128]{1,0:T(8,128)(2,1)S(1)}, bf16[256,128]{1,0:T(8,128)(2,1)S(1)}, u32[]{:S(2)}, u32[]{:S(2)}) %collective-permute-start.10) | collective-permute-done | bytes 65568 | tf_op jit(solution)/shard_map/ppermute | solution.py:303
  48.6 0.0 collective-permute-start.11
  48.6 1.2 %collective-permute-done.11.arrived_ref = bf16[128,128]{1,0:T(8,128)(2,1)S(1)} collective-permute-done((bf16[128,128]{1,0:T(8,128)(2,1)S(1)}, bf16[128,128]{1,0:T(8,128)(2,1)S(1)}, u32[]{:S(2)}, u32[]{:S(2)}) %collective-permute-start.11) | collective-permute-done | bytes 32800 | tf_op jit(solution)/shard_map/ppermute | solution.py:186
  49.8 0.6 %shard_map.77 = f32[4,128,128]{2,1,0:T(8,128)} custom-call(bf16[256,128]{1,0:T(8,128)(2,1)S(1)} %collective-permute-done.10.mine_ref, bf16[128,128]{1,0:T(8,128)(2,1)S(1)} %collective-permute-done.11.arrived_ref, f32[4,128,128]{2,1,0:T(8,128)} %shard_map.75.scores_hbm), custom_call_target="tpu_custom_call", output_to_operand_aliasing={{}: (2, {})} | custom-call | tf_op jit(solution)/shard_map/pallas_call | solution.py:250
  (6 shorter events, 0.1 us)
Async XLA Ops:
  0.0 16.7 %collective-permute-start = (bf16[128,2048]{1,0:T(8,128)(2,1)}, bf16[128,2048]{1,0:T(8,128)(2,1)S(1)}, u32[]{:S(2)}, u32[]{:S(2)}) collective-permute-start(bf16[128,2048]{1,0:T(8,128)(2,1)} %documents_ref.1), channel_id=1, source_target_pairs={{0,8},{8,12},{12,4},{4,0},{1,9},{9,13},{13,5},{5,1},{2,10},{10,14}... | collective-permute-start | bytes 1572872 | tf_op jit(solution)/shard_map/ppermute | solution.py:281
  4.0 25.6 %collective-permute-start.2 = (bf16[128,2048]{1,0:T(8,128)(2,1)}, bf16[128,2048]{1,0:T(8,128)(2,1)S(1)}, u32[]{:S(2)}, u32[]{:S(2)}) collective-permute-start(bf16[128,2048]{1,0:T(8,128)(2,1)} %documents_ref.1), channel_id=1, source_target_pairs={{0,4},{4,12},{12,8},{8,0},{1,5},{5,13},{13,9},{9,1},{2,6},{6,14},{... | collective-permute-start | bytes 1572872 | tf_op jit(solution)/shard_map/ppermute | solution.py:282
  4.9 6.3 %copy-start.1 = (bf16[128,2048]{1,0:T(8,128)(2,1)S(1)}, bf16[128,2048]{1,0:T(8,128)(2,1)}, u32[]{:S(2)}) copy-start(bf16[128,2048]{1,0:T(8,128)(2,1)} %documents_ref.1) | copy-start | bytes 1572868
  11.2 1.6 %copy-start = (bf16[512,2048]{1,0:T(8,128)(2,1)S(1)}, bf16[512,2048]{1,0:T(8,128)(2,1)}, u32[]{:S(2)}) copy-start(bf16[512,2048]{1,0:T(8,128)(2,1)} %shard_map.64.queries_ref) | copy-start | bytes 6291460
  17.5 3.4 %collective-permute-start.3 = (f32[256,256]{1,0:T(8,128)S(1)}, f32[256,256]{1,0:T(8,128)S(1)}, u32[]{:S(2)}, u32[]{:S(2)}) collective-permute-start(f32[256,256]{1,0:T(8,128)S(1)} %get-tuple-element.34), channel_id=1, source_target_pairs={{0,1},{1,0},{2,3},{3,2},{4,5},{5,4},{6,7},{7,6},{8,9},{9,8},{10,11... | collective-permute-start | bytes 786440 | tf_op jit(solution)/shard_map/ppermute | solution.py:186
  17.6 22.5 %collective-permute-start.1 = (bf16[128,2048]{1,0:T(8,128)(2,1)S(1)}, bf16[128,2048]{1,0:T(8,128)(2,1)S(1)}, u32[]{:S(2)}, u32[]{:S(2)}) collective-permute-start(bf16[128,2048]{1,0:T(8,128)(2,1)S(1)} %collective-permute-done.documents_ref), channel_id=1, source_target_pairs={{0,8},{8,12},{12,4},{4,0},{1,9},{9,13},{13,5},{5,1},{2,10},{10,14}... | collective-permute-start | bytes 1572872 | tf_op jit(solution)/shard_map/ppermute | solution.py:285
  20.9 4.3 %collective-permute-start.4 = (bf16[128,256]{1,0:T(8,128)(2,1)S(1)}, bf16[128,256]{1,0:T(8,128)(2,1)S(1)}, u32[]{:S(2)}, u32[]{:S(2)}) collective-permute-start(bf16[128,256]{1,0:T(8,128)(2,1)S(1)} %get-tuple-element.36), channel_id=1, source_target_pairs={{0,2},{1,3},{2,0},{3,1},{4,6},{5,7},{6,4},{7,5},{8,10},{9,11},{10,... | collective-permute-start | bytes 196616 | tf_op jit(solution)/shard_map/ppermute | solution.py:186
  30.4 1.4 %collective-permute-start.5 = (f32[256,128]{1,0:T(8,128)S(1)}, f32[256,128]{1,0:T(8,128)S(1)}, u32[]{:S(2)}, u32[]{:S(2)}) collective-permute-start(f32[256,128]{1,0:T(8,128)S(1)} %get-tuple-element.41), channel_id=1, source_target_pairs={{0,1},{1,0},{2,3},{3,2},{4,5},{5,4},{6,7},{7,6},{8,9},{9,8},{10,11... | collective-permute-start | bytes 393224 | tf_op jit(solution)/shard_map/ppermute | solution.py:186
  31.9 4.0 %collective-permute-start.6 = (bf16[128,128]{1,0:T(8,128)(2,1)S(1)}, bf16[128,128]{1,0:T(8,128)(2,1)S(1)}, u32[]{:S(2)}, u32[]{:S(2)}) collective-permute-start(bf16[128,128]{1,0:T(8,128)(2,1)S(1)} %get-tuple-element.43), channel_id=1, source_target_pairs={{0,2},{1,3},{2,0},{3,1},{4,6},{5,7},{6,4},{7,5},{8,10},{9,11},{10,... | collective-permute-start | bytes 98312 | tf_op jit(solution)/shard_map/ppermute | solution.py:186
  33.4 7.5 %collective-permute-start.7 = (bf16[128,128]{1,0:T(8,128)(2,1)S(1)}, bf16[128,128]{1,0:T(8,128)(2,1)S(1)}, u32[]{:S(2)}, u32[]{:S(2)}) collective-permute-start(bf16[128,128]{1,0:T(8,128)(2,1)S(1)} %get-tuple-element.38), channel_id=1, source_target_pairs={{0,4},{4,12},{8,0},{12,8},{1,5},{5,13},{9,1},{13,9},{2,6},{6,14},{... | collective-permute-start | bytes 98312 | tf_op jit(solution)/shard_map/ppermute | solution.py:279
  35.8 5.3 %collective-permute-start.8 = (bf16[128,128]{1,0:T(8,128)(2,1)S(1)}, bf16[128,128]{1,0:T(8,128)(2,1)S(1)}, u32[]{:S(2)}, u32[]{:S(2)}) collective-permute-start(bf16[128,128]{1,0:T(8,128)(2,1)S(1)} %shard_map.71), channel_id=1, source_target_pairs={{0,8},{4,0},{8,12},{12,4},{1,9},{5,1},{9,13},{13,5},{2,10},{6,2},{... | collective-permute-start | bytes 98312 | tf_op jit(solution)/shard_map/ppermute | solution.py:279
  40.5 1.3 %collective-permute-start.9 = (bf16[256,128]{1,0:T(8,128)(2,1)S(1)}, bf16[256,128]{1,0:T(8,128)(2,1)S(1)}, u32[]{:S(2)}, u32[]{:S(2)}) collective-permute-start(bf16[256,128]{1,0:T(8,128)(2,1)S(1)} %shard_map.73), channel_id=1, source_target_pairs={{0,1},{1,0},{2,3},{3,2},{4,5},{5,4},{6,7},{7,6},{8,9},{9,8},{10,11... | collective-permute-start | bytes 196616 | tf_op jit(solution)/shard_map/ppermute | solution.py:186
  41.9 6.7 %collective-permute-start.10 = (bf16[256,128]{1,0:T(8,128)(2,1)S(1)}, bf16[256,128]{1,0:T(8,128)(2,1)S(1)}, u32[]{:S(2)}, u32[]{:S(2)}) collective-permute-start(bf16[256,128]{1,0:T(8,128)(2,1)S(1)} %shard_map.74), channel_id=1, source_target_pairs={{0,12},{1,15},{2,14},{3,13},{4,8},{5,11},{6,10},{7,9},{8,4},{9,7},... | collective-permute-start | bytes 196616 | tf_op jit(solution)/shard_map/ppermute | solution.py:303
  48.6 1.2 %collective-permute-start.11 = (bf16[128,128]{1,0:T(8,128)(2,1)S(1)}, bf16[128,128]{1,0:T(8,128)(2,1)S(1)}, u32[]{:S(2)}, u32[]{:S(2)}) collective-permute-start(bf16[128,128]{1,0:T(8,128)(2,1)S(1)} %shard_map.76), channel_id=1, source_target_pairs={{0,1},{1,0},{2,3},{3,2},{4,5},{5,4},{6,7},{7,6},{8,9},{9,8},{10,11... | collective-permute-start | bytes 98312 | tf_op jit(solution)/shard_map/ppermute | solution.py:186

commit v26 on v24

--- a/solution.py
+++ b/solution.py
@@ -303,6 +303,7 @@
     mine = lax.ppermute(both, ("rows", "layer"), pairs)
     out_shape = [jax.ShapeDtypeStruct((STEPS,) + own.shape, jnp.float32)]
     (scores,) = small_call(assemble_kernel, out_shape, own, first, second)
+    mine, scores = lax.optimization_barrier((mine, scores))
     (other,) = small_call(other_share_kernel, [jax.ShapeDtypeStruct(own.shape, jnp.bfloat16)], mine)
     return finish(mine, swap(other, 1), scores)
 

time: 50.7 us -> 50.7 us (level)
    ppermute x6, waiting for transfers between devices: 6.66 us -> 7.38 us  [swap(): lax.ppermute(value, 'layer', [(lay, lay ^ distance) for lay in range(coun...]
    ppermute x1, waiting for transfers between devices: 4.17 us -> 3.45 us  [along_line(): mine = lax.ppermute(both, ('rows', 'layer'), pairs)]
where the time goes in v26:
time: 50.7 us; the launch traced here: 50.5 us
  waiting for transfers between devices  22.8 us (45%)
  starting transfers between devices  14.6 us (29%)
  Pallas kernels  9.22 us (18%)
  local copies, waits for them, and re-layouts  3.76 us (7%)
    ppermute x6, waiting for transfers between devices, swap(): lax.ppermute(value, 'layer', [(lay, lay ^ distance) for lay in range(coun...  7.38 us
    pallas_call x1, Pallas kernels, prepare(): pl.pallas_call(prepare_kernel, out_shape=jax.ShapeDtypeStruct((rows, dims...  4.59 us
    ppermute x1, waiting for transfers between devices, along_line(): two = lax.ppermute(documents, 'rows', ROUND_TWO)  4.38 us
    ppermute x1, starting transfers between devices, along_line(): one = lax.ppermute(documents, 'rows', ROUND_ONE)  4.04 us
    ppermute x1, waiting for transfers between devices, along_line(): three = lax.ppermute(one, 'rows', ROUND_ONE)  3.64 us
    ppermute x1, waiting for transfers between devices, along_line(): one = lax.ppermute(documents, 'rows', ROUND_ONE)  3.52 us
    ppermute x1, waiting for transfers between devices, along_line(): mine = lax.ppermute(both, ('rows', 'layer'), pairs)  3.45 us
    ppermute x6, starting transfers between devices, swap(): lax.ppermute(value, 'layer', [(lay, lay ^ distance) for lay in range(coun...  3.4 us
  transfers between devices with their start and end apart: 12, of which 11 were waited for; matrix products, arithmetic and copies ran while one was open for 2% of the time, Pallas kernels for 17%

profile of v26, /device:TPU:0, one launch (start us, length us, event | category | flops | bytes accessed | tf_op | source)
XLA Modules:
  0.0 50.5 jit_solution(18269474764091508987)
XLA Ops:
  0.0 4.0 %collective-permute-start = (bf16[128,2048]{1,0:T(8,128)(2,1)}, bf16[128,2048]{1,0:T(8,128)(2,1)S(1)}, u32[]{:S(2)}, u32[]{:S(2)}) collective-permute-start(bf16[128,2048]{1,0:T(8,128)(2,1)} %documents_ref.1), channel_id=1, source_target_pairs={{0,8},{8,12},{12,4},{4,0},{1,9},{9,13},{13,5},{5,1},{2,10},{10,14}... | collective-permute-start | bytes 1572872 | tf_op jit(solution)/shard_map/ppermute | solution.py:281
  4.0 0.0 collective-permute-start.2
  4.0 0.8 %copy.11.ids_ref = s32[512,1]{1,0:T(8,128)S(1)} copy(s32[512,1]{0,1:T(1,128)} %bitcast.1) | data formatting | bytes 4096 | tf_op jit(solution)/shard_map/broadcast_in_dim | solution.py:335
  4.9 0.0 copy-start.1
  4.9 1.6 %copy-done.1 = bf16[512,2048]{1,0:T(8,128)(2,1)S(1)} copy-done((bf16[512,2048]{1,0:T(8,128)(2,1)S(1)}, bf16[512,2048]{1,0:T(8,128)(2,1)}, u32[]{:S(2)}) %copy-start.1) | copy-done | bytes 2097176
  6.5 0.0 copy-start.2
  6.5 0.7 %copy-done.2 = f32[4,512]{1,0:T(4,128)S(1)} copy-done((f32[4,512]{1,0:T(4,128)S(1)}, f32[4,512]{1,0:T(4,128)}, u32[]{:S(2)}) %copy-start.2) | copy-done | bytes 8216
  7.2 0.0 copy-start.3
  7.2 0.7 %copy-done.3 = s32[4]{0:T(128)S(1)} copy-done((s32[4]{0:T(128)S(1)}, s32[4]{0:T(128)}, u32[]{:S(2)}) %copy-start.3) | copy-done | bytes 40
  7.8 0.0 copy-start
  7.8 4.6 %shard_map.64.queries_ref = bf16[512,2048]{1,0:T(8,128)(2,1)S(1)} custom-call(s32[4]{0:T(128)S(1)} %copy-done.3, bf16[512,2048]{1,0:T(8,128)(2,1)S(1)} %copy-done.1, bf16[4,512,512]{2,1,0:T(8,128)(2,1)} %bases_hbm.1, f32[4,512]{1,0:T(4,128)S(1)} %copy-done.2), custom_call_target="tpu_custom_call" | custom-call | flops 2147483648 | bytes 6291456 | tf_op jit(solution)/shard_map/pallas_call | solution.py:52
  12.4 0.0 copy-done
  12.4 0.8 %shard_map.65 = (f32[256,128]{1,0:T(8,128)S(1)}, f32[256,128]{1,0:T(8,128)S(1)}) custom-call(bf16[512,2048]{1,0:T(8,128)(2,1)S(1)} %shard_map.64.queries_ref, s32[512,1]{1,0:T(8,128)S(1)} %copy.11.ids_ref, bf16[128,2048]{1,0:T(8,128)(2,1)S(1)} %copy-done), custom_call_target="tpu_custom_call" | custom-call | flops 268435456 | bytes 2621440 | tf_op jit(solution)/shard_map/pallas_call | solution.py:81
  13.2 3.5 %collective-permute-done.documents_ref = bf16[128,2048]{1,0:T(8,128)(2,1)S(1)} collective-permute-done((bf16[128,2048]{1,0:T(8,128)(2,1)}, bf16[128,2048]{1,0:T(8,128)(2,1)S(1)}, u32[]{:S(2)}, u32[]{:S(2)}) %collective-permute-start) | collective-permute-done | bytes 524320 | tf_op jit(solution)/shard_map/ppermute | solution.py:281
  16.7 0.8 %shard_map.66 = (f32[256,256]{1,0:T(8,128)S(1)}, f32[256,256]{1,0:T(8,128)S(1)}) custom-call(bf16[512,2048]{1,0:T(8,128)(2,1)S(1)} %shard_map.64.queries_ref, s32[512,1]{1,0:T(8,128)S(1)} %copy.11.ids_ref, bf16[128,2048]{1,0:T(8,128)(2,1)S(1)} %collective-permute-done.documents_ref, f32[256,128]{1,0:T(8,128)S(1)} %get-tuple-element.31.refs_0_, ...), custom_call_target="tpu_custom_call" | custom-call | flops 268435456 | bytes 2621440 | tf_op jit(solution)/shard_map/pallas_call | solution.py:81
  17.5 0.1 collective-permute-start.3
  17.6 3.3 %collective-permute-start.1 = (bf16[128,2048]{1,0:T(8,128)(2,1)S(1)}, bf16[128,2048]{1,0:T(8,128)(2,1)S(1)}, u32[]{:S(2)}, u32[]{:S(2)}) collective-permute-start(bf16[128,2048]{1,0:T(8,128)(2,1)S(1)} %collective-permute-done.documents_ref), channel_id=1, source_target_pairs={{0,8},{8,12},{12,4},{4,0},{1,9},{9,13},{13,5},{5,1},{2,10},{10,14}... | collective-permute-start | bytes 1572872 | tf_op jit(solution)/shard_map/ppermute | solution.py:285
  20.9 0.0 collective-permute-done.3.arrived_ref
  20.9 1.6 %collective-permute-start.4 = (bf16[128,256]{1,0:T(8,128)(2,1)S(1)}, bf16[128,256]{1,0:T(8,128)(2,1)S(1)}, u32[]{:S(2)}, u32[]{:S(2)}) collective-permute-start(bf16[128,256]{1,0:T(8,128)(2,1)S(1)} %get-tuple-element.36), channel_id=1, source_target_pairs={{0,2},{1,3},{2,0},{3,1},{4,6},{5,7},{6,4},{7,5},{8,10},{9,11},{10,... | collective-permute-start | bytes 196616 | tf_op jit(solution)/shard_map/ppermute | solution.py:186
  22.5 2.8 %collective-permute-done.4.arrived_ref = bf16[128,256]{1,0:T(8,128)(2,1)S(1)} collective-permute-done((bf16[128,256]{1,0:T(8,128)(2,1)S(1)}, bf16[128,256]{1,0:T(8,128)(2,1)S(1)}, u32[]{:S(2)}, u32[]{:S(2)}) %collective-permute-start.4) | collective-permute-done | bytes 65568 | tf_op jit(solution)/shard_map/ppermute | solution.py:186
  25.3 4.4 %collective-permute-done.2.documents_ref = bf16[128,2048]{1,0:T(8,128)(2,1)S(1)} collective-permute-done((bf16[128,2048]{1,0:T(8,128)(2,1)}, bf16[128,2048]{1,0:T(8,128)(2,1)S(1)}, u32[]{:S(2)}, u32[]{:S(2)}) %collective-permute-start.2) | collective-permute-done | bytes 524320 | tf_op jit(solution)/shard_map/ppermute | solution.py:282
  29.7 0.8 %shard_map.69 = (f32[256,128]{1,0:T(8,128)S(1)}, f32[256,128]{1,0:T(8,128)S(1)}) custom-call(bf16[512,2048]{1,0:T(8,128)(2,1)S(1)} %shard_map.64.queries_ref, s32[512,1]{1,0:T(8,128)S(1)} %copy.11.ids_ref, bf16[128,2048]{1,0:T(8,128)(2,1)S(1)} %collective-permute-done.2.documents_ref), custom_call_target="tpu_custom_call" | custom-call | flops 268435456 | bytes 2621440 | tf_op jit(solution)/shard_map/pallas_call | solution.py:81
  30.4 0.1 collective-permute-start.5
  30.5 1.3 %collective-permute-done.5.arrived_ref = f32[256,128]{1,0:T(8,128)S(1)} collective-permute-done((f32[256,128]{1,0:T(8,128)S(1)}, f32[256,128]{1,0:T(8,128)S(1)}, u32[]{:S(2)}, u32[]{:S(2)}) %collective-permute-start.5) | collective-permute-done | bytes 131104 | tf_op jit(solution)/shard_map/ppermute | solution.py:186
  31.9 1.6 %collective-permute-start.6 = (bf16[128,128]{1,0:T(8,128)(2,1)S(1)}, bf16[128,128]{1,0:T(8,128)(2,1)S(1)}, u32[]{:S(2)}, u32[]{:S(2)}) collective-permute-start(bf16[128,128]{1,0:T(8,128)(2,1)S(1)} %get-tuple-element.43), channel_id=1, source_target_pairs={{0,2},{1,3},{2,0},{3,1},{4,6},{5,7},{6,4},{7,5},{8,10},{9,11},{10,... | collective-permute-start | bytes 98312 | tf_op jit(solution)/shard_map/ppermute | solution.py:186
  33.4 0.7 %collective-permute-start.7 = (bf16[128,128]{1,0:T(8,128)(2,1)S(1)}, bf16[128,128]{1,0:T(8,128)(2,1)S(1)}, u32[]{:S(2)}, u32[]{:S(2)}) collective-permute-start(bf16[128,128]{1,0:T(8,128)(2,1)S(1)} %get-tuple-element.38), channel_id=1, source_target_pairs={{0,4},{4,12},{8,0},{12,8},{1,5},{5,13},{9,1},{13,9},{2,6},{6,14},{... | collective-permute-start | bytes 98312 | tf_op jit(solution)/shard_map/ppermute | solution.py:279
  34.1 1.7 %collective-permute-done.6.arrived_ref = bf16[128,128]{1,0:T(8,128)(2,1)S(1)} collective-permute-done((bf16[128,128]{1,0:T(8,128)(2,1)S(1)}, bf16[128,128]{1,0:T(8,128)(2,1)S(1)}, u32[]{:S(2)}, u32[]{:S(2)}) %collective-permute-start.6) | collective-permute-done | bytes 32800 | tf_op jit(solution)/shard_map/ppermute | solution.py:186
  35.9 0.6 %collective-permute-start.8 = (bf16[128,128]{1,0:T(8,128)(2,1)S(1)}, bf16[128,128]{1,0:T(8,128)(2,1)S(1)}, u32[]{:S(2)}, u32[]{:S(2)}) collective-permute-start(bf16[128,128]{1,0:T(8,128)(2,1)S(1)} %shard_map.71), channel_id=1, source_target_pairs={{0,8},{4,0},{8,12},{12,4},{1,9},{5,1},{9,13},{13,5},{2,10},{6,2},{... | collective-permute-start | bytes 98312 | tf_op jit(solution)/shard_map/ppermute | solution.py:279
  36.5 3.6 %collective-permute-done.1.documents_ref = bf16[128,2048]{1,0:T(8,128)(2,1)S(1)} collective-permute-done((bf16[128,2048]{1,0:T(8,128)(2,1)S(1)}, bf16[128,2048]{1,0:T(8,128)(2,1)S(1)}, u32[]{:S(2)}, u32[]{:S(2)}) %collective-permute-start.1) | collective-permute-done | bytes 524320 | tf_op jit(solution)/shard_map/ppermute | solution.py:285
  40.1 0.4 shard_map.73
  40.6 0.1 collective-permute-start.9
  40.7 0.2 collective-permute-done.7.first_ref
  40.9 0.2 collective-permute-done.8.second_ref
  41.1 0.4 shard_map.72.refs_0_
  41.6 0.3 collective-permute-done.9.refs_1_
  41.9 2.5 %collective-permute-start.10 = (bf16[256,128]{1,0:T(8,128)(2,1)S(1)}, bf16[256,128]{1,0:T(8,128)(2,1)S(1)}, u32[]{:S(2)}, u32[]{:S(2)}) collective-permute-start(bf16[256,128]{1,0:T(8,128)(2,1)S(1)} %shard_map.74), channel_id=1, source_target_pairs={{0,12},{1,15},{2,14},{3,13},{4,8},{5,11},{6,10},{7,9},{8,4},{9,7},... | collective-permute-start | bytes 196616 | tf_op jit(solution)/shard_map/ppermute | solution.py:303
  44.4 0.7 %shard_map.75.scores_hbm = f32[4,128,128]{2,1,0:T(8,128)} custom-call(f32[128,128]{1,0:T(8,128)S(1)} %get-tuple-element.46.own_ref, bf16[128,128]{1,0:T(8,128)(2,1)S(1)} %collective-permute-done.7.first_ref, bf16[128,128]{1,0:T(8,128)(2,1)S(1)} %collective-permute-done.8.second_ref), custom_call_target="tpu_custom_call" | custom-call | tf_op jit(solution)/shard_map/pallas_call | solution.py:148
  45.2 3.4 %collective-permute-done.10.mine_ref = bf16[256,128]{1,0:T(8,128)(2,1)S(1)} collective-permute-done((bf16[256,128]{1,0:T(8,128)(2,1)S(1)}, bf16[256,128]{1,0:T(8,128)(2,1)S(1)}, u32[]{:S(2)}, u32[]{:S(2)}) %collective-permute-start.10) | collective-permute-done | bytes 65568 | tf_op jit(solution)/shard_map/ppermute | solution.py:303
  48.6 0.0 collective-permute-start.11
  48.6 1.2 %collective-permute-done.11.arrived_ref = bf16[128,128]{1,0:T(8,128)(2,1)S(1)} collective-permute-done((bf16[128,128]{1,0:T(8,128)(2,1)S(1)}, bf16[128,128]{1,0:T(8,128)(2,1)S(1)}, u32[]{:S(2)}, u32[]{:S(2)}) %collective-permute-start.11) | collective-permute-done | bytes 32800 | tf_op jit(solution)/shard_map/ppermute | solution.py:186
  49.8 0.6 %shard_map.77 = f32[4,128,128]{2,1,0:T(8,128)} custom-call(bf16[256,128]{1,0:T(8,128)(2,1)S(1)} %collective-permute-done.10.mine_ref, bf16[128,128]{1,0:T(8,128)(2,1)S(1)} %collective-permute-done.11.arrived_ref, f32[4,128,128]{2,1,0:T(8,128)} %shard_map.75.scores_hbm), custom_call_target="tpu_custom_call", output_to_operand_aliasing={{}: (2, {})} | custom-call | tf_op jit(solution)/shard_map/pallas_call | solution.py:250
  (6 shorter events, 0.1 us)
Async XLA Ops:
  0.0 16.7 %collective-permute-start = (bf16[128,2048]{1,0:T(8,128)(2,1)}, bf16[128,2048]{1,0:T(8,128)(2,1)S(1)}, u32[]{:S(2)}, u32[]{:S(2)}) collective-permute-start(bf16[128,2048]{1,0:T(8,128)(2,1)} %documents_ref.1), channel_id=1, source_target_pairs={{0,8},{8,12},{12,4},{4,0},{1,9},{9,13},{13,5},{5,1},{2,10},{10,14}... | collective-permute-start | bytes 1572872 | tf_op jit(solution)/shard_map/ppermute | solution.py:281
  4.0 25.6 %collective-permute-start.2 = (bf16[128,2048]{1,0:T(8,128)(2,1)}, bf16[128,2048]{1,0:T(8,128)(2,1)S(1)}, u32[]{:S(2)}, u32[]{:S(2)}) collective-permute-start(bf16[128,2048]{1,0:T(8,128)(2,1)} %documents_ref.1), channel_id=1, source_target_pairs={{0,4},{4,12},{12,8},{8,0},{1,5},{5,13},{13,9},{9,1},{2,6},{6,14},{... | collective-permute-start | bytes 1572872 | tf_op jit(solution)/shard_map/ppermute | solution.py:282
  4.9 1.6 %copy-start.1 = (bf16[512,2048]{1,0:T(8,128)(2,1)S(1)}, bf16[512,2048]{1,0:T(8,128)(2,1)}, u32[]{:S(2)}) copy-start(bf16[512,2048]{1,0:T(8,128)(2,1)} %queries_hbm.1) | copy-start | bytes 6291460
  6.5 0.7 %copy-start.2 = (f32[4,512]{1,0:T(4,128)S(1)}, f32[4,512]{1,0:T(4,128)}, u32[]{:S(2)}) copy-start(f32[4,512]{1,0:T(4,128)} %values_hbm.1) | copy-start | bytes 24580
  7.2 0.7 %copy-start.3 = (s32[4]{0:T(128)S(1)}, s32[4]{0:T(128)}, u32[]{:S(2)}) copy-start(s32[4]{0:T(128)} %offsets.1) | copy-start | bytes 52
  7.8 4.6 %copy-start = (bf16[128,2048]{1,0:T(8,128)(2,1)S(1)}, bf16[128,2048]{1,0:T(8,128)(2,1)}, u32[]{:S(2)}) copy-start(bf16[128,2048]{1,0:T(8,128)(2,1)} %documents_ref.1) | copy-start | bytes 1572868
  17.5 3.4 %collective-permute-start.3 = (f32[256,256]{1,0:T(8,128)S(1)}, f32[256,256]{1,0:T(8,128)S(1)}, u32[]{:S(2)}, u32[]{:S(2)}) collective-permute-start(f32[256,256]{1,0:T(8,128)S(1)} %get-tuple-element.34), channel_id=1, source_target_pairs={{0,1},{1,0},{2,3},{3,2},{4,5},{5,4},{6,7},{7,6},{8,9},{9,8},{10,11... | collective-permute-start | bytes 786440 | tf_op jit(solution)/shard_map/ppermute | solution.py:186
  17.6 22.5 %collective-permute-start.1 = (bf16[128,2048]{1,0:T(8,128)(2,1)S(1)}, bf16[128,2048]{1,0:T(8,128)(2,1)S(1)}, u32[]{:S(2)}, u32[]{:S(2)}) collective-permute-start(bf16[128,2048]{1,0:T(8,128)(2,1)S(1)} %collective-permute-done.documents_ref), channel_id=1, source_target_pairs={{0,8},{8,12},{12,4},{4,0},{1,9},{9,13},{13,5},{5,1},{2,10},{10,14}... | collective-permute-start | bytes 1572872 | tf_op jit(solution)/shard_map/ppermute | solution.py:285
  20.9 4.3 %collective-permute-start.4 = (bf16[128,256]{1,0:T(8,128)(2,1)S(1)}, bf16[128,256]{1,0:T(8,128)(2,1)S(1)}, u32[]{:S(2)}, u32[]{:S(2)}) collective-permute-start(bf16[128,256]{1,0:T(8,128)(2,1)S(1)} %get-tuple-element.36), channel_id=1, source_target_pairs={{0,2},{1,3},{2,0},{3,1},{4,6},{5,7},{6,4},{7,5},{8,10},{9,11},{10,... | collective-permute-start | bytes 196616 | tf_op jit(solution)/shard_map/ppermute | solution.py:186
  30.4 1.4 %collective-permute-start.5 = (f32[256,128]{1,0:T(8,128)S(1)}, f32[256,128]{1,0:T(8,128)S(1)}, u32[]{:S(2)}, u32[]{:S(2)}) collective-permute-start(f32[256,128]{1,0:T(8,128)S(1)} %get-tuple-element.41), channel_id=1, source_target_pairs={{0,1},{1,0},{2,3},{3,2},{4,5},{5,4},{6,7},{7,6},{8,9},{9,8},{10,11... | collective-permute-start | bytes 393224 | tf_op jit(solution)/shard_map/ppermute | solution.py:186
  31.9 4.0 %collective-permute-start.6 = (bf16[128,128]{1,0:T(8,128)(2,1)S(1)}, bf16[128,128]{1,0:T(8,128)(2,1)S(1)}, u32[]{:S(2)}, u32[]{:S(2)}) collective-permute-start(bf16[128,128]{1,0:T(8,128)(2,1)S(1)} %get-tuple-element.43), channel_id=1, source_target_pairs={{0,2},{1,3},{2,0},{3,1},{4,6},{5,7},{6,4},{7,5},{8,10},{9,11},{10,... | collective-permute-start | bytes 98312 | tf_op jit(solution)/shard_map/ppermute | solution.py:186
  33.4 7.5 %collective-permute-start.7 = (bf16[128,128]{1,0:T(8,128)(2,1)S(1)}, bf16[128,128]{1,0:T(8,128)(2,1)S(1)}, u32[]{:S(2)}, u32[]{:S(2)}) collective-permute-start(bf16[128,128]{1,0:T(8,128)(2,1)S(1)} %get-tuple-element.38), channel_id=1, source_target_pairs={{0,4},{4,12},{8,0},{12,8},{1,5},{5,13},{9,1},{13,9},{2,6},{6,14},{... | collective-permute-start | bytes 98312 | tf_op jit(solution)/shard_map/ppermute | solution.py:279
  35.9 5.3 %collective-permute-start.8 = (bf16[128,128]{1,0:T(8,128)(2,1)S(1)}, bf16[128,128]{1,0:T(8,128)(2,1)S(1)}, u32[]{:S(2)}, u32[]{:S(2)}) collective-permute-start(bf16[128,128]{1,0:T(8,128)(2,1)S(1)} %shard_map.71), channel_id=1, source_target_pairs={{0,8},{4,0},{8,12},{12,4},{1,9},{5,1},{9,13},{13,5},{2,10},{6,2},{... | collective-permute-start | bytes 98312 | tf_op jit(solution)/shard_map/ppermute | solution.py:279
  40.6 1.3 %collective-permute-start.9 = (bf16[256,128]{1,0:T(8,128)(2,1)S(1)}, bf16[256,128]{1,0:T(8,128)(2,1)S(1)}, u32[]{:S(2)}, u32[]{:S(2)}) collective-permute-start(bf16[256,128]{1,0:T(8,128)(2,1)S(1)} %shard_map.73), channel_id=1, source_target_pairs={{0,1},{1,0},{2,3},{3,2},{4,5},{5,4},{6,7},{7,6},{8,9},{9,8},{10,11... | collective-permute-start | bytes 196616 | tf_op jit(solution)/shard_map/ppermute | solution.py:186
  41.9 6.7 %collective-permute-start.10 = (bf16[256,128]{1,0:T(8,128)(2,1)S(1)}, bf16[256,128]{1,0:T(8,128)(2,1)S(1)}, u32[]{:S(2)}, u32[]{:S(2)}) collective-permute-start(bf16[256,128]{1,0:T(8,128)(2,1)S(1)} %shard_map.74), channel_id=1, source_target_pairs={{0,12},{1,15},{2,14},{3,13},{4,8},{5,11},{6,10},{7,9},{8,4},{9,7},... | collective-permute-start | bytes 196616 | tf_op jit(solution)/shard_map/ppermute | solution.py:303
  48.6 1.2 %collective-permute-start.11 = (bf16[128,128]{1,0:T(8,128)(2,1)S(1)}, bf16[128,128]{1,0:T(8,128)(2,1)S(1)}, u32[]{:S(2)}, u32[]{:S(2)}) collective-permute-start(bf16[128,128]{1,0:T(8,128)(2,1)S(1)} %shard_map.76), channel_id=1, source_target_pairs={{0,1},{1,0},{2,3},{3,2},{4,5},{5,4},{6,7},{7,6},{8,9},{9,8},{10,11... | collective-permute-start | bytes 98312 | tf_op jit(solution)/shard_map/ppermute | solution.py:186

commit v27 on v23

--- a/solution.py
+++ b/solution.py
@@ -281,7 +281,6 @@
     one = lax.ppermute(documents, "rows", ROUND_ONE)
     two = lax.ppermute(documents, "rows", ROUND_TWO)
     own = halves(documents, lambda row: row)
-    one, own = lax.optimization_barrier((one, own))
     three = lax.ppermute(one, "rows", ROUND_ONE)
 
     own, first = layer_sum(*halves(one, pick(BLOCK_ONE), own), (jnp.float32, jnp.bfloat16))

time: 50.7 us -> 50.7 us (level)
  no operation moved by 1% of the time
where the time goes in v27:
time: 50.7 us; the launch traced here: 50.5 us
  waiting for transfers between devices  22.4 us (44%)
  starting transfers between devices  14.6 us (29%)
  Pallas kernels  10.9 us (21%)
  local copies, waits for them, and re-layouts  2.41 us (5%)
    ppermute x6, waiting for transfers between devices, swap(): lax.ppermute(value, 'layer', [(lay, lay ^ distance) for lay in range(coun...  6.66 us
    pallas_call x1, Pallas kernels, prepare(): pl.pallas_call(prepare_kernel, out_shape=jax.ShapeDtypeStruct((rows, dims...  6.29 us
    ppermute x1, waiting for transfers between devices, along_line(): two = lax.ppermute(documents, 'rows', ROUND_TWO)  4.38 us
    ppermute x1, waiting for transfers between devices, along_line(): mine = lax.ppermute(both, ('rows', 'layer'), pairs)  4.17 us
    ppermute x1, starting transfers between devices, along_line(): one = lax.ppermute(documents, 'rows', ROUND_ONE)  4.04 us
    ppermute x1, waiting for transfers between devices, along_line(): three = lax.ppermute(one, 'rows', ROUND_ONE)  3.65 us
    ppermute x6, starting transfers between devices, swap(): lax.ppermute(value, 'layer', [(lay, lay ^ distance) for lay in range(coun...  3.4 us
    ppermute x1, starting transfers between devices, along_line(): three = lax.ppermute(one, 'rows', ROUND_ONE)  3.33 us
  transfers between devices with their start and end apart: 12, of which 11 were waited for; matrix products, arithmetic and copies ran while one was open for 2% of the time, Pallas kernels for 20%

profile of v27, /device:TPU:0, one launch (start us, length us, event | category | flops | bytes accessed | tf_op | source)
XLA Modules:
  0.0 50.5 jit_solution(3329772744227342484)
XLA Ops:
  0.0 4.0 %collective-permute-start = (bf16[128,2048]{1,0:T(8,128)(2,1)}, bf16[128,2048]{1,0:T(8,128)(2,1)S(1)}, u32[]{:S(2)}, u32[]{:S(2)}) collective-permute-start(bf16[128,2048]{1,0:T(8,128)(2,1)} %documents_ref.1), channel_id=1, source_target_pairs={{0,8},{8,12},{12,4},{4,0},{1,9},{9,13},{13,5},{5,1},{2,10},{10,14}... | collective-permute-start | bytes 1572872 | tf_op jit(solution)/shard_map/ppermute | solution.py:281
  4.0 0.0 collective-permute-start.2
  4.0 0.8 %copy.11.ids_ref = s32[512,1]{1,0:T(8,128)S(1)} copy(s32[512,1]{0,1:T(1,128)} %bitcast.1) | data formatting | bytes 4096 | tf_op jit(solution)/shard_map/broadcast_in_dim | solution.py:333
  4.9 0.0 copy-start.1
  4.9 6.3 %shard_map.64.queries_ref = bf16[512,2048]{1,0:T(8,128)(2,1)} custom-call(s32[4]{0:T(128)} %offsets.1, bf16[512,2048]{1,0:T(8,128)(2,1)} %queries_hbm.1, bf16[4,512,512]{2,1,0:T(8,128)(2,1)} %bases_hbm.1, f32[4,512]{1,0:T(4,128)} %values_hbm.1), custom_call_target="tpu_custom_call" | custom-call | flops 2147483648 | bytes 6291456 | tf_op jit(solution)/shard_map/pallas_call | solution.py:52
  11.2 0.0 copy-done.1
  11.2 0.0 copy-start
  11.2 1.6 %copy-done = bf16[512,2048]{1,0:T(8,128)(2,1)S(1)} copy-done((bf16[512,2048]{1,0:T(8,128)(2,1)S(1)}, bf16[512,2048]{1,0:T(8,128)(2,1)}, u32[]{:S(2)}) %copy-start) | copy-done | bytes 2097176
  12.8 0.8 %shard_map.65 = (f32[256,128]{1,0:T(8,128)S(1)}, f32[256,128]{1,0:T(8,128)S(1)}) custom-call(bf16[512,2048]{1,0:T(8,128)(2,1)S(1)} %copy-done, s32[512,1]{1,0:T(8,128)S(1)} %copy.11.ids_ref, bf16[128,2048]{1,0:T(8,128)(2,1)S(1)} %copy-done.1), custom_call_target="tpu_custom_call" | custom-call | flops 268435456 | bytes 2621440 | tf_op jit(solution)/shard_map/pallas_call | solution.py:81
  13.6 3.2 %collective-permute-done.documents_ref = bf16[128,2048]{1,0:T(8,128)(2,1)S(1)} collective-permute-done((bf16[128,2048]{1,0:T(8,128)(2,1)}, bf16[128,2048]{1,0:T(8,128)(2,1)S(1)}, u32[]{:S(2)}, u32[]{:S(2)}) %collective-permute-start) | collective-permute-done | bytes 524320 | tf_op jit(solution)/shard_map/ppermute | solution.py:281
  16.7 0.8 %shard_map.66 = (f32[256,256]{1,0:T(8,128)S(1)}, f32[256,256]{1,0:T(8,128)S(1)}) custom-call(bf16[512,2048]{1,0:T(8,128)(2,1)S(1)} %copy-done, s32[512,1]{1,0:T(8,128)S(1)} %copy.11.ids_ref, bf16[128,2048]{1,0:T(8,128)(2,1)S(1)} %collective-permute-done.documents_ref, f32[256,128]{1,0:T(8,128)S(1)} %get-tuple-element.23.refs_0_, ...), custom_call_target="tpu_custom_call" | custom-call | flops 268435456 | bytes 2621440 | tf_op jit(solution)/shard_map/pallas_call | solution.py:81
  17.5 0.1 collective-permute-start.3
  17.6 3.3 %collective-permute-start.1 = (bf16[128,2048]{1,0:T(8,128)(2,1)S(1)}, bf16[128,2048]{1,0:T(8,128)(2,1)S(1)}, u32[]{:S(2)}, u32[]{:S(2)}) collective-permute-start(bf16[128,2048]{1,0:T(8,128)(2,1)S(1)} %collective-permute-done.documents_ref), channel_id=1, source_target_pairs={{0,8},{8,12},{12,4},{4,0},{1,9},{9,13},{13,5},{5,1},{2,10},{10,14}... | collective-permute-start | bytes 1572872 | tf_op jit(solution)/shard_map/ppermute | solution.py:284
  20.9 0.0 collective-permute-done.3.arrived_ref
  20.9 1.6 %collective-permute-start.4 = (bf16[128,256]{1,0:T(8,128)(2,1)S(1)}, bf16[128,256]{1,0:T(8,128)(2,1)S(1)}, u32[]{:S(2)}, u32[]{:S(2)}) collective-permute-start(bf16[128,256]{1,0:T(8,128)(2,1)S(1)} %get-tuple-element.28), channel_id=1, source_target_pairs={{0,2},{1,3},{2,0},{3,1},{4,6},{5,7},{6,4},{7,5},{8,10},{9,11},{10,... | collective-permute-start | bytes 196616 | tf_op jit(solution)/shard_map/ppermute | solution.py:186
  22.5 2.8 %collective-permute-done.4.arrived_ref = bf16[128,256]{1,0:T(8,128)(2,1)S(1)} collective-permute-done((bf16[128,256]{1,0:T(8,128)(2,1)S(1)}, bf16[128,256]{1,0:T(8,128)(2,1)S(1)}, u32[]{:S(2)}, u32[]{:S(2)}) %collective-permute-start.4) | collective-permute-done | bytes 65568 | tf_op jit(solution)/shard_map/ppermute | solution.py:186
  25.3 4.4 %collective-permute-done.2.documents_ref = bf16[128,2048]{1,0:T(8,128)(2,1)S(1)} collective-permute-done((bf16[128,2048]{1,0:T(8,128)(2,1)}, bf16[128,2048]{1,0:T(8,128)(2,1)S(1)}, u32[]{:S(2)}, u32[]{:S(2)}) %collective-permute-start.2) | collective-permute-done | bytes 524320 | tf_op jit(solution)/shard_map/ppermute | solution.py:282
  29.7 0.8 %shard_map.69 = (f32[256,128]{1,0:T(8,128)S(1)}, f32[256,128]{1,0:T(8,128)S(1)}) custom-call(bf16[512,2048]{1,0:T(8,128)(2,1)S(1)} %copy-done, s32[512,1]{1,0:T(8,128)S(1)} %copy.11.ids_ref, bf16[128,2048]{1,0:T(8,128)(2,1)S(1)} %collective-permute-done.2.documents_ref), custom_call_target="tpu_custom_call" | custom-call | flops 268435456 | bytes 2621440 | tf_op jit(solution)/shard_map/pallas_call | solution.py:81
  30.4 0.1 collective-permute-start.5
  30.5 1.3 %collective-permute-done.5.arrived_ref = f32[256,128]{1,0:T(8,128)S(1)} collective-permute-done((f32[256,128]{1,0:T(8,128)S(1)}, f32[256,128]{1,0:T(8,128)S(1)}, u32[]{:S(2)}, u32[]{:S(2)}) %collective-permute-start.5) | collective-permute-done | bytes 131104 | tf_op jit(solution)/shard_map/ppermute | solution.py:186
  31.9 1.6 %collective-permute-start.6 = (bf16[128,128]{1,0:T(8,128)(2,1)S(1)}, bf16[128,128]{1,0:T(8,128)(2,1)S(1)}, u32[]{:S(2)}, u32[]{:S(2)}) collective-permute-start(bf16[128,128]{1,0:T(8,128)(2,1)S(1)} %get-tuple-element.35), channel_id=1, source_target_pairs={{0,2},{1,3},{2,0},{3,1},{4,6},{5,7},{6,4},{7,5},{8,10},{9,11},{10,... | collective-permute-start | bytes 98312 | tf_op jit(solution)/shard_map/ppermute | solution.py:186
  33.4 0.7 %collective-permute-start.7 = (bf16[128,128]{1,0:T(8,128)(2,1)S(1)}, bf16[128,128]{1,0:T(8,128)(2,1)S(1)}, u32[]{:S(2)}, u32[]{:S(2)}) collective-permute-start(bf16[128,128]{1,0:T(8,128)(2,1)S(1)} %get-tuple-element.30), channel_id=1, source_target_pairs={{0,4},{4,12},{8,0},{12,8},{1,5},{5,13},{9,1},{13,9},{2,6},{6,14},{... | collective-permute-start | bytes 98312 | tf_op jit(solution)/shard_map/ppermute | solution.py:279
  34.1 1.7 %collective-permute-done.6.arrived_ref = bf16[128,128]{1,0:T(8,128)(2,1)S(1)} collective-permute-done((bf16[128,128]{1,0:T(8,128)(2,1)S(1)}, bf16[128,128]{1,0:T(8,128)(2,1)S(1)}, u32[]{:S(2)}, u32[]{:S(2)}) %collective-permute-start.6) | collective-permute-done | bytes 32800 | tf_op jit(solution)/shard_map/ppermute | solution.py:186
  35.8 0.6 %collective-permute-start.8 = (bf16[128,128]{1,0:T(8,128)(2,1)S(1)}, bf16[128,128]{1,0:T(8,128)(2,1)S(1)}, u32[]{:S(2)}, u32[]{:S(2)}) collective-permute-start(bf16[128,128]{1,0:T(8,128)(2,1)S(1)} %shard_map.71), channel_id=1, source_target_pairs={{0,8},{4,0},{8,12},{12,4},{1,9},{5,1},{9,13},{13,5},{2,10},{6,2},{... | collective-permute-start | bytes 98312 | tf_op jit(solution)/shard_map/ppermute | solution.py:279
  36.5 3.6 %collective-permute-done.1.documents_ref = bf16[128,2048]{1,0:T(8,128)(2,1)S(1)} collective-permute-done((bf16[128,2048]{1,0:T(8,128)(2,1)S(1)}, bf16[128,2048]{1,0:T(8,128)(2,1)S(1)}, u32[]{:S(2)}, u32[]{:S(2)}) %collective-permute-start.1) | collective-permute-done | bytes 524320 | tf_op jit(solution)/shard_map/ppermute | solution.py:284
  40.1 0.4 shard_map.73
  40.5 0.1 collective-permute-start.9
  40.7 0.2 collective-permute-done.7.first_ref
  40.9 0.2 collective-permute-done.8.second_ref
  41.1 0.4 shard_map.72.refs_0_
  41.5 0.3 collective-permute-done.9.refs_1_
  41.9 2.5 %collective-permute-start.10 = (bf16[256,128]{1,0:T(8,128)(2,1)S(1)}, bf16[256,128]{1,0:T(8,128)(2,1)S(1)}, u32[]{:S(2)}, u32[]{:S(2)}) collective-permute-start(bf16[256,128]{1,0:T(8,128)(2,1)S(1)} %shard_map.74), channel_id=1, source_target_pairs={{0,12},{1,15},{2,14},{3,13},{4,8},{5,11},{6,10},{7,9},{8,4},{9,7},... | collective-permute-start | bytes 196616 | tf_op jit(solution)/shard_map/ppermute | solution.py:302
  44.4 4.2 %collective-permute-done.10.mine_ref = bf16[256,128]{1,0:T(8,128)(2,1)S(1)} collective-permute-done((bf16[256,128]{1,0:T(8,128)(2,1)S(1)}, bf16[256,128]{1,0:T(8,128)(2,1)S(1)}, u32[]{:S(2)}, u32[]{:S(2)}) %collective-permute-start.10) | collective-permute-done | bytes 65568 | tf_op jit(solution)/shard_map/ppermute | solution.py:302
  48.6 0.0 collective-permute-start.11
  48.6 0.7 %shard_map.76.scores_hbm = f32[4,128,128]{2,1,0:T(8,128)} custom-call(f32[128,128]{1,0:T(8,128)S(1)} %get-tuple-element.38.own_ref, bf16[128,128]{1,0:T(8,128)(2,1)S(1)} %collective-permute-done.7.first_ref, bf16[128,128]{1,0:T(8,128)(2,1)S(1)} %collective-permute-done.8.second_ref), custom_call_target="tpu_custom_call" | custom-call | tf_op jit(solution)/shard_map/pallas_call | solution.py:148
  49.3 0.5 collective-permute-done.11.arrived_ref
  49.8 0.6 %shard_map.77 = f32[4,128,128]{2,1,0:T(8,128)} custom-call(bf16[256,128]{1,0:T(8,128)(2,1)S(1)} %collective-permute-done.10.mine_ref, bf16[128,128]{1,0:T(8,128)(2,1)S(1)} %collective-permute-done.11.arrived_ref, f32[4,128,128]{2,1,0:T(8,128)} %shard_map.76.scores_hbm), custom_call_target="tpu_custom_call", output_to_operand_aliasing={{}: (2, {})} | custom-call | tf_op jit(solution)/shard_map/pallas_call | solution.py:250
  (6 shorter events, 0.1 us)
Async XLA Ops:
  0.0 16.7 %collective-permute-start = (bf16[128,2048]{1,0:T(8,128)(2,1)}, bf16[128,2048]{1,0:T(8,128)(2,1)S(1)}, u32[]{:S(2)}, u32[]{:S(2)}) collective-permute-start(bf16[128,2048]{1,0:T(8,128)(2,1)} %documents_ref.1), channel_id=1, source_target_pairs={{0,8},{8,12},{12,4},{4,0},{1,9},{9,13},{13,5},{5,1},{2,10},{10,14}... | collective-permute-start | bytes 1572872 | tf_op jit(solution)/shard_map/ppermute | solution.py:281
  4.0 25.6 %collective-permute-start.2 = (bf16[128,2048]{1,0:T(8,128)(2,1)}, bf16[128,2048]{1,0:T(8,128)(2,1)S(1)}, u32[]{:S(2)}, u32[]{:S(2)}) collective-permute-start(bf16[128,2048]{1,0:T(8,128)(2,1)} %documents_ref.1), channel_id=1, source_target_pairs={{0,4},{4,12},{12,8},{8,0},{1,5},{5,13},{13,9},{9,1},{2,6},{6,14},{... | collective-permute-start | bytes 1572872 | tf_op jit(solution)/shard_map/ppermute | solution.py:282
  4.9 6.3 %copy-start.1 = (bf16[128,2048]{1,0:T(8,128)(2,1)S(1)}, bf16[128,2048]{1,0:T(8,128)(2,1)}, u32[]{:S(2)}) copy-start(bf16[128,2048]{1,0:T(8,128)(2,1)} %documents_ref.1) | copy-start | bytes 1572868
  11.2 1.6 %copy-start = (bf16[512,2048]{1,0:T(8,128)(2,1)S(1)}, bf16[512,2048]{1,0:T(8,128)(2,1)}, u32[]{:S(2)}) copy-start(bf16[512,2048]{1,0:T(8,128)(2,1)} %shard_map.64.queries_ref) | copy-start | bytes 6291460
  17.5 3.4 %collective-permute-start.3 = (f32[256,256]{1,0:T(8,128)S(1)}, f32[256,256]{1,0:T(8,128)S(1)}, u32[]{:S(2)}, u32[]{:S(2)}) collective-permute-start(f32[256,256]{1,0:T(8,128)S(1)} %get-tuple-element.26), channel_id=1, source_target_pairs={{0,1},{1,0},{2,3},{3,2},{4,5},{5,4},{6,7},{7,6},{8,9},{9,8},{10,11... | collective-permute-start | bytes 786440 | tf_op jit(solution)/shard_map/ppermute | solution.py:186
  17.6 22.5 %collective-permute-start.1 = (bf16[128,2048]{1,0:T(8,128)(2,1)S(1)}, bf16[128,2048]{1,0:T(8,128)(2,1)S(1)}, u32[]{:S(2)}, u32[]{:S(2)}) collective-permute-start(bf16[128,2048]{1,0:T(8,128)(2,1)S(1)} %collective-permute-done.documents_ref), channel_id=1, source_target_pairs={{0,8},{8,12},{12,4},{4,0},{1,9},{9,13},{13,5},{5,1},{2,10},{10,14}... | collective-permute-start | bytes 1572872 | tf_op jit(solution)/shard_map/ppermute | solution.py:284
  20.9 4.3 %collective-permute-start.4 = (bf16[128,256]{1,0:T(8,128)(2,1)S(1)}, bf16[128,256]{1,0:T(8,128)(2,1)S(1)}, u32[]{:S(2)}, u32[]{:S(2)}) collective-permute-start(bf16[128,256]{1,0:T(8,128)(2,1)S(1)} %get-tuple-element.28), channel_id=1, source_target_pairs={{0,2},{1,3},{2,0},{3,1},{4,6},{5,7},{6,4},{7,5},{8,10},{9,11},{10,... | collective-permute-start | bytes 196616 | tf_op jit(solution)/shard_map/ppermute | solution.py:186
  30.4 1.4 %collective-permute-start.5 = (f32[256,128]{1,0:T(8,128)S(1)}, f32[256,128]{1,0:T(8,128)S(1)}, u32[]{:S(2)}, u32[]{:S(2)}) collective-permute-start(f32[256,128]{1,0:T(8,128)S(1)} %get-tuple-element.33), channel_id=1, source_target_pairs={{0,1},{1,0},{2,3},{3,2},{4,5},{5,4},{6,7},{7,6},{8,9},{9,8},{10,11... | collective-permute-start | bytes 393224 | tf_op jit(solution)/shard_map/ppermute | solution.py:186
  31.9 4.0 %collective-permute-start.6 = (bf16[128,128]{1,0:T(8,128)(2,1)S(1)}, bf16[128,128]{1,0:T(8,128)(2,1)S(1)}, u32[]{:S(2)}, u32[]{:S(2)}) collective-permute-start(bf16[128,128]{1,0:T(8,128)(2,1)S(1)} %get-tuple-element.35), channel_id=1, source_target_pairs={{0,2},{1,3},{2,0},{3,1},{4,6},{5,7},{6,4},{7,5},{8,10},{9,11},{10,... | collective-permute-start | bytes 98312 | tf_op jit(solution)/shard_map/ppermute | solution.py:186
  33.4 7.5 %collective-permute-start.7 = (bf16[128,128]{1,0:T(8,128)(2,1)S(1)}, bf16[128,128]{1,0:T(8,128)(2,1)S(1)}, u32[]{:S(2)}, u32[]{:S(2)}) collective-permute-start(bf16[128,128]{1,0:T(8,128)(2,1)S(1)} %get-tuple-element.30), channel_id=1, source_target_pairs={{0,4},{4,12},{8,0},{12,8},{1,5},{5,13},{9,1},{13,9},{2,6},{6,14},{... | collective-permute-start | bytes 98312 | tf_op jit(solution)/shard_map/ppermute | solution.py:279
  35.8 5.3 %collective-permute-start.8 = (bf16[128,128]{1,0:T(8,128)(2,1)S(1)}, bf16[128,128]{1,0:T(8,128)(2,1)S(1)}, u32[]{:S(2)}, u32[]{:S(2)}) collective-permute-start(bf16[128,128]{1,0:T(8,128)(2,1)S(1)} %shard_map.71), channel_id=1, source_target_pairs={{0,8},{4,0},{8,12},{12,4},{1,9},{5,1},{9,13},{13,5},{2,10},{6,2},{... | collective-permute-start | bytes 98312 | tf_op jit(solution)/shard_map/ppermute | solution.py:279
  40.5 1.3 %collective-permute-start.9 = (bf16[256,128]{1,0:T(8,128)(2,1)S(1)}, bf16[256,128]{1,0:T(8,128)(2,1)S(1)}, u32[]{:S(2)}, u32[]{:S(2)}) collective-permute-start(bf16[256,128]{1,0:T(8,128)(2,1)S(1)} %shard_map.73), channel_id=1, source_target_pairs={{0,1},{1,0},{2,3},{3,2},{4,5},{5,4},{6,7},{7,6},{8,9},{9,8},{10,11... | collective-permute-start | bytes 196616 | tf_op jit(solution)/shard_map/ppermute | solution.py:186
  41.9 6.7 %collective-permute-start.10 = (bf16[256,128]{1,0:T(8,128)(2,1)S(1)}, bf16[256,128]{1,0:T(8,128)(2,1)S(1)}, u32[]{:S(2)}, u32[]{:S(2)}) collective-permute-start(bf16[256,128]{1,0:T(8,128)(2,1)S(1)} %shard_map.74), channel_id=1, source_target_pairs={{0,12},{1,15},{2,14},{3,13},{4,8},{5,11},{6,10},{7,9},{8,4},{9,7},... | collective-permute-start | bytes 196616 | tf_op jit(solution)/shard_map/ppermute | solution.py:302
  48.6 1.2 %collective-permute-start.11 = (bf16[128,128]{1,0:T(8,128)(2,1)S(1)}, bf16[128,128]{1,0:T(8,128)(2,1)S(1)}, u32[]{:S(2)}, u32[]{:S(2)}) collective-permute-start(bf16[128,128]{1,0:T(8,128)(2,1)S(1)} %shard_map.75), channel_id=1, source_target_pairs={{0,1},{1,0},{2,3},{3,2},{4,5},{5,4},{6,7},{7,6},{8,9},{9,8},{10,11... | collective-permute-start | bytes 98312 | tf_op jit(solution)/shard_map/ppermute | solution.py:186
